TPU v7x, 32 devices: a whole 2x2x4 slice. The times are simulated.
32 devices in a mesh: dp: 4 (over y, x), tensor: 8 (over z, core).
Axes of the slice: x: 2, y: 2, z: 4, core: 2. Of those that a mesh axis runs over, the one named last changes fastest.
Arguments:
- hidden_states: bfloat16 [1024, 2048], P(('dp', 'tensor')), may hold values from -36 to 36
- attention_gain: float32 [2048], replicated, may hold values from 0.4 to 2.5
- feedforward_gain: float32 [2048], replicated, may hold values from 0.4 to 2.5
- heads_weight: bfloat16 [2048, 6144], P(None, 'tensor'), may hold values from -1.9887378 to 1.9887378
- output_weight: bfloat16 [2048, 2048], P('tensor'), may hold values from -0.125 to 0.125
- upward_weight: bfloat16 [2048, 8192], P(None, 'tensor'), may hold values from -0.125 to 0.125
- downward_weight: bfloat16 [8192, 2048], P('tensor'), may hold values from -0.0625 to 0.0625
- segments: int32 [4, 256], P('dp'), may hold values from 0 to 7, never falling along the last dimension, each value on 1 to 128 neighbouring positions
- page_targets: int32 [64, 1], P('dp'), may hold values from 0 to 3; in each aligned block of 16 rows (0 to 15, 16 to 31, ...) at most 8 rows name the same one
Outputs:
- layer_output: float32 [1024, 2048], P(('dp', 'tensor'))
- cache_pages: bfloat16 [4, 4, 8, 16, 4096], P('dp', None, None, None, 'tensor')
Inputs may be any that keep to these rules, and one draw needn't show every extreme that they name: `segments`: in each group's row the numbers never fall, every number below 8 occurs, no prompt has more than 128 tokens, and one has exactly 128. `page_targets`: among the 16 pages of one request group no target is named more than 8 times, a bound that some block reaches.
All inputs are finite; a program needn't handle non-finite values.
Results may differ from a plain program's by a relative error of at most 0.011.
Values may be sent and summed in bfloat16 or wider, within the bound.
No kernel may reach another device: no remote copies, remote signals or barrier semaphores. Data moves between devices by JAX's collectives and lax.ppermute only.
A program may use at most 64 MiB of HBM per device.

v0:
```python
import math

import jax
import jax.numpy as jnp
from jax import lax
from jax.sharding import PartitionSpec as P

H = 8
HD = 256
ROT = 64
PAGE = 16


epsilon = 1e-05
rotary_base = 10000.0
key_block = 256


def shortened(array):

    def short(part):
        return part.astype(jnp.bfloat16) if part.dtype == jnp.float32 else part

    return jax.tree.map(short, array)


def swapped(block, axis, apart):
    count = lax.axis_size(axis)
    route = []
    for low in range(count):
        high = low | 1 << apart
        if high != low and high < count:
            route += [(low, high), (high, low)]
    return lax.ppermute(block, axis, route)


def layer_norm(values, gain):
    floats = values.astype(jnp.float32)
    center = jnp.mean(floats, axis=-1, keepdims=True)
    shifted = floats - center
    spread = jnp.mean(shifted * shifted, axis=-1, keepdims=True)
    return (shifted * lax.rsqrt(spread + epsilon) * gain).astype(jnp.bfloat16)


def positions_of(stream):
    indices = jnp.arange(stream.shape[0], dtype=jnp.int32)
    boundary = jnp.concatenate([jnp.ones((1,), dtype=bool), stream[1:] != stream[:-1]])
    starting = lax.cummax(jnp.where(boundary, indices, jnp.zeros_like(indices)), axis=0)
    return (indices, starting)


def rotate_heads(vectors, offsets, rotary_dims):
    half_dims = rotary_dims // 2
    frequency = jnp.exp(
        jnp.arange(half_dims, dtype=jnp.float32) * (-2.0 * math.log(rotary_base) / rotary_dims)
    )
    angles = offsets.astype(jnp.float32)[:, None] * frequency[None, :]
    cosine = jnp.cos(angles)
    sine = jnp.sin(angles)
    floats = vectors.astype(jnp.float32)
    leading = floats[..., :half_dims]
    trailing = floats[..., half_dims:rotary_dims]
    rotated = jnp.concatenate(
        [
            leading * cosine - trailing * sine,
            trailing * cosine + leading * sine,
            floats[..., rotary_dims:],
        ],
        axis=-1,
    )
    return rotated.astype(jnp.bfloat16)


def shards(
    hidden_states,
    attention_gain,
    feedforward_gain,
    heads_weight,
    output_weight,
    upward_weight,
    downward_weight,
    segments,
    page_targets,
):
    tensor_count = lax.axis_size("tensor")
    replica_count = lax.axis_size("dp")
    tensor_index = lax.axis_index("tensor")
    quarters = tensor_count // H
    quarter_width = HD // quarters
    quarter_index = tensor_index % quarters
    stream = segments[0]
    tokens_total = stream.shape[0]
    level_count = quarters.bit_length() - 1
    normed_attention = layer_norm(hidden_states, attention_gain)
    normed_feedforward = layer_norm(hidden_states, feedforward_gain)
    shard_rows = lax.all_gather(
        (normed_attention, normed_feedforward), "tensor", axis=0, tiled=True
    )
    joined_rows = jnp.dot(shard_rows[0], heads_weight, preferred_element_type=jnp.float32).astype(
        jnp.bfloat16
    )
    upward = jnp.dot(shard_rows[1], upward_weight, preferred_element_type=jnp.float32)
    hidden_rows = jax.nn.gelu(upward, approximate=False).astype(jnp.bfloat16)
    hidden = hidden_rows
    pieces = (
        joined_rows.reshape(tokens_total, 3, quarter_width)
        .transpose(1, 0, 2)
        .reshape(1, 3, tokens_total * quarter_width)
    )
    for bit_number in range(level_count):
        partner = swapped(shortened(pieces), "tensor", bit_number).astype(pieces.dtype)
        lower = tensor_index >> bit_number & 1 == 0
        pieces = jnp.where(
            lower, jnp.concatenate([pieces, partner], 0), jnp.concatenate([partner, pieces], 0)
        )
    whole_head = (
        pieces.reshape(quarters, 3, tokens_total, quarter_width)
        .transpose(1, 2, 0, 3)
        .reshape(3, tokens_total, HD)
    )
    indices, starting = positions_of(stream)
    offsets = indices - starting
    queries = rotate_heads(whole_head[0], offsets, ROT)
    keys = rotate_heads(whole_head[1], offsets, ROT)
    values = whole_head[2]
    block_rows = tokens_total // (2 * quarters)
    score_scale = HD ** (-0.5)

    def attend_block(block_number):
        first_row = block_number * block_rows
        block_queries = lax.dynamic_slice_in_dim(queries, first_row, block_rows, 0)
        query_segments = lax.dynamic_slice_in_dim(stream, first_row, block_rows, 0)
        query_indices = first_row + jnp.arange(block_rows, dtype=jnp.int32)
        lowest = lax.dynamic_index_in_dim(starting, first_row, 0, keepdims=False) // key_block
        highest = (first_row + block_rows + key_block - 1) // key_block

        def scores_of(key_number):
            key_first = key_number * key_block
            key_indices = key_first + jnp.arange(key_block, dtype=jnp.int32)
            scores = (
                jnp.dot(block_queries, keys.T, preferred_element_type=jnp.float32) * score_scale
            )
            allowed = (stream[None, :] == query_segments[:, None]) & (
                key_indices[None, :] <= query_indices[:, None]
            )
            return (scores, allowed)

        def find_peak(key_number, peak):
            scores, allowed = scores_of(key_number)
            return jnp.maximum(peak, jnp.max(jnp.where(allowed, scores, -jnp.inf), axis=1))

        peak = lax.fori_loop(
            lowest, highest, find_peak, jnp.full((block_rows,), -jnp.inf, jnp.float32)
        )

        def accumulate(key_number, state):
            weight_sum, mixed_sum = state
            scores, allowed = scores_of(key_number)
            weights = jnp.where(allowed, jnp.exp(scores - peak[:, None]), 0.0)
            mixed_next = mixed_sum + jnp.dot(
                weights.astype(jnp.bfloat16), values, preferred_element_type=jnp.float32
            )
            return (weight_sum + jnp.sum(weights, axis=1), mixed_next)

        start_state = (
            jnp.zeros((block_rows,), jnp.float32),
            jnp.zeros((block_rows, HD), jnp.float32),
        )
        weight_sum, mixed_sum = lax.fori_loop(lowest, highest, accumulate, start_state)
        return (mixed_sum / weight_sum[:, None]).astype(jnp.bfloat16)

    own_blocks = (2 * quarter_index, 2 * quarter_index + 1)
    own_rows = jnp.concatenate([attend_block(own_blocks[0]), attend_block(own_blocks[1])], 0)[None]
    for bit_number in range(level_count):
        partner = swapped(own_rows, "tensor", bit_number)
        lower = tensor_index >> bit_number & 1 == 0
        own_rows = jnp.where(
            lower, jnp.concatenate([own_rows, partner], 0), jnp.concatenate([partner, own_rows], 0)
        )
    attended = own_rows.reshape(tokens_total, HD)
    attended_quarter = lax.dynamic_slice_in_dim(
        attended, quarter_index * quarter_width, quarter_width, 1
    )
    hidden_rows = hidden
    summed = lax.psum_scatter(
        (
            jnp.dot(attended_quarter, output_weight, preferred_element_type=jnp.float32)
            + jnp.dot(hidden_rows, downward_weight, preferred_element_type=jnp.float32)
        ).astype(jnp.bfloat16),
        "tensor",
        scatter_dimension=0,
        tiled=True,
    ).astype(jnp.float32)
    layer_output = hidden_states.astype(jnp.float32) + summed
    key_quarter = lax.dynamic_slice_in_dim(keys, quarter_index * quarter_width, quarter_width, 1)
    value_quarter = joined_rows[:, 2 * quarter_width :]
    page_count = tokens_total // PAGE
    page_rows = jnp.concatenate([key_quarter, value_quarter], 1).reshape(
        page_count, PAGE * 2 * quarter_width
    )
    targets = page_targets[:, 0]
    page_numbers = jnp.arange(page_count, dtype=jnp.int32)
    earlier = jnp.sum(
        (
            (targets[None, :] == targets[:, None]) & (page_numbers[None, :] < page_numbers[:, None])
        ).astype(jnp.int32),
        axis=1,
    )
    capacity = 2 * page_count // replica_count
    slot_numbers = targets * capacity + earlier
    placing = (
        jnp.arange(replica_count * capacity, dtype=jnp.int32)[:, None] == slot_numbers[None, :]
    ).astype(jnp.bfloat16)
    outgoing = jnp.dot(placing, page_rows, preferred_element_type=jnp.float32).astype(jnp.bfloat16)
    outgoing = outgoing.reshape(replica_count, capacity, PAGE * 2 * quarter_width)
    incoming = lax.all_to_all(outgoing, "dp", split_axis=0, concat_axis=0, tiled=True)
    cache_pages = incoming.reshape(1, replica_count, capacity, PAGE, 2 * quarter_width)
    return (layer_output, cache_pages)


def solution(mesh):
    in_specs = (
        P(("dp", "tensor"), None),
        P(),
        P(),
        P(None, "tensor"),
        P("tensor", None),
        P(None, "tensor"),
        P("tensor", None),
        P("dp", None),
        P("dp", None),
    )
    out_specs = (P(("dp", "tensor"), None), P("dp", None, None, None, "tensor"))
    return jax.shard_map(shards, mesh=mesh, in_specs=in_specs, out_specs=out_specs, check_vma=False)
```

profile of v0, /device:TPU:0, one launch (start us, length us, event | category | flops | bytes accessed | tf_op | source)
XLA Modules:
  0.0 113.1 jit_solution(12335606101138286126)
XLA Ops:
  7.2 1.2 %convert_reduce_fusion = f32[32]{0:T(128)S(1)} fusion(bf16[32,2048]{1,0:T(8,128)(2,1)} %param.17), kind=kLoop, calls=%fused_computation.99 | loop fusion | flops 131040 | bytes 131200 | tf_op jit(solution)/shard_map/reduce_sum | solution.py:39
  8.4 1.1 fusion.83
  9.5 1.7 %fusion.81 = (bf16[32,2048]{1,0:T(8,128)(2,1)}, bf16[32,2048]{1,0:T(8,128)(2,1)}) fusion(bf16[32,2048]{1,0:T(8,128)(2,1)} %param.17, f32[2048]{0:T(1024)} %param.18, f32[32]{0:T(128)S(1)} %add_rsqrt_fusion, f32[32]{0:T(128)S(1)} %broadcast_multiply_fusion, f32[2048]{0:T(1024)} %param.19), kind=kLoop, calls=%fused_computation.104 | loop fusion | flops 458752 | bytes 409856 | tf_op jit(solution)/shard_map/convert_element_type | solution.py:42
  11.4 0.7 all-gather.5.cloned.1.call-update
  12.6 0.8 compare_reduce_fusion
  20.1 16.1 %all-gather.3.cloned.1.call-done = bf16[256,2048]{1,0:T(8,128)(2,1)} async-done(((bf16[32,2048]{1,0:T(8,128)(2,1)}), bf16[256,2048]{1,0:T(8,128)(2,1)}) %all-gather.3.cloned.1.call-update) | async-done | bytes 1048592 | tf_op jit(solution)/shard_map/all_gather | solution.py:96
  36.3 3.0 %convolution_convert_fusion.1 = bf16[256,768]{1,0:T(8,128)(2,1)} fusion(bf16[256,2048]{1,0:T(8,128)(2,1)} %all-gather.3.cloned.1.call-done, bf16[2048,768]{1,0:T(8,128)(2,1)S(1)} %copy-done), kind=kOutput, calls=%fused_computation.46 | convolution fusion | flops 805502976 | bytes 4587520 | tf_op jit(solution)/shard_map/dot_general | solution.py:99
  39.2 1.2 %copy.15 = bf16[256,768]{0,1:T(8,128)(2,1)S(1)} copy(bf16[256,768]{1,0:T(8,128)(2,1)} %convolution_convert_fusion.1) | data formatting | bytes 786432 | tf_op jit(solution)/shard_map/convert_element_type | solution.py:99
  40.4 0.7 slice_bitcast_fusion
  41.1 0.8 fusion.104
  42.6 1.0 copy.16
  45.8 3.2 %while.63 = (s32[]{:T(128)}, f32[128]{0:T(128)}, f32[128,256]{1,0:T(8,128)}, s32[1,256]{1,0:T(1,128)S(1)}, s32[128]{0:T(128)S(1)}, /*index=5*/f32[128,256]{1,0:T...) while((s32[]{:T(128)}, f32[128]{0:T(128)}, ...), condition=%wide.region_15.16_spmd.clone, body=%wide.region_13.15_spmd.clone.sunk | while | flops 17269124 | bytes 666229 | solution.py:169
  46.0 1.2 %add.278 = f32[128]{0:T(128)} add(f32[128]{0:T(128)} %get-tuple-element.853, f32[128]{0:T(128)S(1)} %fusion.168) | non-fusion elementwise | flops 128 | bytes 1536 | tf_op jit(solution)/shard_map/while/body/add | solution.py:163
  47.3 1.8 %convolution_add_fusion.6 = f32[128,256]{1,0:T(8,128)} fusion(f32[128,256]{1,0:T(8,128)} %get-tuple-element.854, bf16[256,256]{1,0:T(8,128)(2,1)S(1)} %get-tuple-element.869, f32[128,256]{1,0:T(8,128)S(1)} %get-tuple-element.867, f32[128]{0:T(128)S(1)} %get-tuple-element.868, s32[256]{0:T(256)S(1)} %iota_add_fusion.16, s32[256]{0:T(256)S(1)} %bitcast.66, ...), kind=kOutput, calls=%fused_computation.26.clone.1 | convolution fusion | flops 17039360 | bytes 527872 | tf_op jit(solution)/shard_map/while/body/dot_general | solution.py:160
  49.1 1.7 %while.61 = (s32[]{:T(128)}, f32[128]{0:T(128)S(1)}, f32[128,256]{1,0:T(8,128)S(1)}, s32[1,256]{1,0:T(1,128)S(1)}, s32[128]{0:T(128)S(1)}, /*index=5*/f32[128,25...) while((s32[]{:T(128)}, f32[128]{0:T(128)S(1)}, ...), condition=%wide.region_9.10_spmd.clone, body=%wide.region_7.9_spmd.clone.sunk | while | flops 17268996 | bytes 664693 | solution.py:169
  49.1 0.8 fusion.165
  49.9 0.8 convolution_add_fusion.5
  50.8 1.7 %divide_convert_fusion = (bf16[128,256]{1,0:T(8,128)(2,1)}, bf16[128,256]{1,0:T(8,128)(2,1)}) fusion(f32[128,256]{1,0:T(8,128)} %get-tuple-element.510, f32[128]{0:T(128)} %get-tuple-element.511, f32[128,256]{1,0:T(8,128)S(1)} %get-tuple-element.507, f32[128]{0:T(128)S(1)} %get-tuple-element.508), kind=kLoop, calls=%fused_computation.116 | loop fusion | flops 131072 | bytes 394240 | tf_op jit(solution)/shard_map/convert_element_type | solution.py:170
  52.4 7.2 %all-gather.5.cloned.1.call-done = bf16[256,2048]{1,0:T(8,128)(2,1)} async-done(((bf16[32,2048]{1,0:T(8,128)(2,1)}), bf16[256,2048]{1,0:T(8,128)(2,1)}) %all-gather.5.cloned.1.call-update) | async-done | bytes 1048592 | tf_op jit(solution)/shard_map/all_gather | solution.py:96
  59.6 9.7 %fusion.45 = f32[256,2048]{1,0:T(8,128)} fusion(bf16[1024,2048]{1,0:T(8,128)(2,1)} %param.23, bf16[256,2048]{1,0:T(8,128)(2,1)} %all-gather.5.cloned.1.call-done, bf16[2048,1024]{1,0:T(8,128)(2,1)} %param.22), kind=kOutput, calls=%fused_computation.65 | convolution fusion | flops 2164523008 | bytes 11534336 | tf_op jit(solution)/shard_map/dot_general | solution.py:188
  69.3 3.4 %fusion.34 = bf16[256,2048]{1,0:T(8,128)(2,1)} fusion(f32[256,2048]{1,0:T(8,128)} %fusion.45, bf16[256,2048]{1,0:T(8,128)(2,1)} %param.21, bf16[128,256]{1,0:T(8,128)(2,1)S(1)} %copy-done.5, bf16[128,256]{1,0:T(8,128)(2,1)S(1)} %copy-done.6), kind=kOutput, calls=%fused_computation.44 | convolution fusion | flops 269746176 | bytes 4325376 | tf_op jit(solution)/shard_map/dot_general | solution.py:187
  73.0 1.6 %slice.76 = bf16[256,256]{1,0:T(8,128)(2,1)} slice(bf16[256,768]{1,0:T(8,128)(2,1)} %convolution_convert_fusion.1), slice={[0:256], [512:768]} | slice | bytes 262144 | tf_op jit(solution)/shard_map/slice | solution.py:196
  74.5 0.7 copy.18
  75.3 0.7 copy.19
  76.0 0.8 copy.20
  76.7 1.2 %pad_maximum_fusion = bf16[256,512]{1,0:T(8,128)(2,1)S(1)} fusion(bf16[256,256]{1,0:T(8,128)(2,1)} %slice.76, bf16[256,192]{1,0:T(8,128)(2,1)} %copy.20, bf16[256,32]{1,0:T(8,128)(2,1)} %copy.19, bf16[256,32]{1,0:T(8,128)(2,1)} %copy.18), kind=kLoop, calls=%fused_computation.107 | loop fusion | flops 1048576 | bytes 524288 | tf_op jit(solution)/shard_map/concatenate | solution.py:198
  77.9 0.8 reshape.112
  78.7 1.2 %fusion.33 = bf16[4,8,8192]{2,1,0:T(8,128)(2,1)S(1)} fusion(bf16[16,8192]{1,0:T(8,128)(2,1)} %reshape.112, s32[16]{0:T(128)S(1)} %multiply_add_fusion), kind=kOutput, calls=%fused_computation.42 | convolution fusion | flops 8651264 | bytes 786496 | tf_op jit(solution)/shard_map/dot_general | solution.py:214
  80.0 12.3 %all_to_all.5 = bf16[4,8,8192]{2,1,0:T(8,128)(2,1)S(1)} all-to-all(bf16[4,8,8192]{2,1,0:T(8,128)(2,1)S(1)} %fusion.33), channel_id=1, replica_groups=mesh['dp'=4,'tensor'=8] {'dp'}, dimensions={0} | all-to-all | bytes 1048576 | tf_op jit(solution)/shard_map/all_to_all | solution.py:216
  92.3 1.0 copy.23
  93.3 11.7 %reduce-scatter.2.cloned.1.call-done = bf16[32,2048]{1,0:T(8,128)(2,1)} async-done(((bf16[256,2048]{1,0:T(8,128)(2,1)}), bf16[32,2048]{1,0:T(8,128)(2,1)}) %reduce-scatter.2.cloned.1.call-update) | async-done | bytes 131088 | tf_op jit(solution)/shard_map/reduce_scatter | solution.py:185
  105.0 1.6 %convert_add_fusion = f32[32,2048]{1,0:T(8,128)} fusion(bf16[32,2048]{1,0:T(8,128)(2,1)S(1)} %copy-done.1, bf16[32,2048]{1,0:T(8,128)(2,1)} %reduce-scatter.2.cloned.1.call-done), kind=kLoop, calls=%fused_computation.97 | loop fusion | flops 196608 | bytes 524288 | tf_op jit(solution)/shard_map/add | solution.py:194
  (69 shorter events, 6.2 us)
Async XLA Ops:
  7.2 29.1 %copy-start = (bf16[2048,768]{1,0:T(8,128)(2,1)S(1)}, bf16[2048,768]{1,0:T(8,128)(2,1)}, u32[]{:S(2)}) copy-start(bf16[2048,768]{1,0:T(8,128)(2,1)} %param.20) | copy-start | bytes 9437188
  7.2 29.1 %all-gather.3.cloned.1.call-start = ((), (), s32[]{:S(2)}) async-start(), calls=%async_computation.2 | async-start | bytes 1179648 | tf_op jit(solution)/shard_map/all_gather | solution.py:96
  11.3 48.3 %all-gather.5.cloned.1.call-start = ((), (), s32[]{:S(2)}) async-start(), calls=%async_computation.3 | async-start | bytes 1179648 | tf_op jit(solution)/shard_map/all_gather | solution.py:96
  12.1 92.9 %reduce-scatter.2.cloned.1.call-start = ((), (), s32[]{:S(2)}) async-start(), calls=%async_computation.4 | async-start | bytes 1179648 | tf_op jit(solution)/shard_map/reduce_scatter | solution.py:185
  20.1 23.5 %copy-start.2 = (s32[1,256]{1,0:T(1,128)S(1)}, s32[1,256]{1,0:T(1,128)}, u32[]{:S(2)}) copy-start(s32[1,256]{1,0:T(1,128)} %param.24) | copy-start | bytes 3076
  41.1 1.3 %copy-start.3 = (bf16[256,192]{0,1:T(8,128)(2,1)}, bf16[256,192]{0,1:T(8,128)(2,1)S(1)}, u32[]{:S(2)}) copy-start(bf16[256,192]{0,1:T(8,128)(2,1)S(1)} %slice.74) | copy-start | bytes 294916
  42.0 0.6 copy-start.7
  42.0 0.6 copy-start.9
  43.8 0.5 copy-start.11
  52.4 16.9 %copy-start.5 = (bf16[128,256]{1,0:T(8,128)(2,1)S(1)}, bf16[128,256]{1,0:T(8,128)(2,1)}, u32[]{:S(2)}) copy-start(bf16[128,256]{1,0:T(8,128)(2,1)} %get-tuple-element.659) | copy-start | bytes 196612
  52.4 16.9 %copy-start.6 = (bf16[128,256]{1,0:T(8,128)(2,1)S(1)}, bf16[128,256]{1,0:T(8,128)(2,1)}, u32[]{:S(2)}) copy-start(bf16[128,256]{1,0:T(8,128)(2,1)} %get-tuple-element.660) | copy-start | bytes 196612
  69.3 3.5 %copy-start.12 = (s32[16,1]{0,1:T(1,128)S(1)}, s32[16,1]{0,1:T(1,128)}, u32[]{:S(2)}) copy-start(s32[16,1]{0,1:T(1,128)} %param.25) | copy-start | bytes 196
  69.3 5.3 %copy-start.10 = (bf16[256,32]{0,1:T(8,128)(2,1)S(1)}, bf16[256,32]{0,1:T(8,128)(2,1)}, u32[]{:S(2)}) copy-start(bf16[256,32]{0,1:T(8,128)(2,1)} %copy-done.9) | copy-start | bytes 49156
  69.3 6.0 %copy-start.8 = (bf16[256,32]{0,1:T(8,128)(2,1)S(1)}, bf16[256,32]{0,1:T(8,128)(2,1)}, u32[]{:S(2)}) copy-start(bf16[256,32]{0,1:T(8,128)(2,1)} %copy-done.7) | copy-start | bytes 49156
  69.3 6.7 %copy-start.4 = (bf16[256,192]{0,1:T(8,128)(2,1)S(1)}, bf16[256,192]{0,1:T(8,128)(2,1)}, u32[]{:S(2)}) copy-start(bf16[256,192]{0,1:T(8,128)(2,1)} %copy-done.3) | copy-start | bytes 294916
  69.3 35.7 %copy-start.1 = (bf16[32,2048]{1,0:T(8,128)(2,1)S(1)}, bf16[32,2048]{1,0:T(8,128)(2,1)}, u32[]{:S(2)}) copy-start(bf16[32,2048]{1,0:T(8,128)(2,1)} %param.17) | copy-start | bytes 393220
Sparse Core Ops, SparseCore 0:
  11.4 24.7 all-gather.2
  37.9 21.7 all-gather.4
  72.9 32.0 reduce-scatter.1
where the time goes:
time: 114 us; the launch traced here: 113 us
  waiting for transfers between devices  35.8 us (31%)
  matrix products  20.3 us (18%)
  between operations  18.7 us (16%)
  other arithmetic  14.8 us (13%)
  blocking collectives  12.3 us (11%)
  local copies, waits for them, and re-layouts  11.1 us (10%)
    all_gather x2, waiting for transfers between devices, shards(): lax.all_gather((normed_attention, normed_feedforward), 'tensor', axis=0,...  23.3 us
    all_to_all x1, blocking collectives, shards(): lax.all_to_all(outgoing, 'dp', split_axis=0, concat_axis=0, tiled=True)  12.3 us
    reduce_scatter x1, waiting for transfers between devices, shards(): lax.psum_scatter((jnp.dot(attended_quarter, output_weight, preferred_elem...  11.7 us
    dot_general x1, matrix products, shards(): jnp.dot(hidden_rows, downward_weight, preferred_element_type=jnp.float32)  9.65 us
    dot_general x1, matrix products, shards(): jnp.dot(attended_quarter, output_weight, preferred_element_type=jnp.float32)  3.41 us
    dot_general x1, matrix products, shards(): jnp.dot(shard_rows[0], heads_weight, preferred_element_type=jnp.float32)  2.95 us
    another operation x9, local copies, waits for them, and re-layouts  2.81 us
    unnamed x28, local copies, waits for them, and re-layouts  2.68 us
  transfers between devices with their start and end apart: 3, of which 3 were waited for; matrix products, arithmetic and copies ran while one was open for 24% of the time, Pallas kernels for 0%

commit v1 on v0

--- a/solution.py
+++ b/solution.py
@@ -1,8 +1,11 @@
+import functools
 import math
 
 import jax
 import jax.numpy as jnp
 from jax import lax
+from jax.experimental import pallas as pl
+from jax.experimental.pallas import tpu as pltpu
 from jax.sharding import PartitionSpec as P
 
 H = 8
@@ -71,7 +74,7 @@
     return rotated.astype(jnp.bfloat16)
 
 
-def shards(
+def shards_split_heads(
     hidden_states,
     attention_gain,
     feedforward_gain,
@@ -218,7 +221,329 @@
     return (layer_output, cache_pages)
 
 
+CORES = 2
+MIB = 1 << 20
+
+
+def in_vmem(array):
+    return pltpu.with_memory_space_constraint(array, pltpu.VMEM)
+
+
+def exchanged(block, axis, mask):
+    count = lax.axis_size(axis)
+    return lax.ppermute(block, axis, [(member, member ^ mask) for member in range(count)])
+
+
+def vmem_specs(count):
+    return [pl.BlockSpec(memory_space=pltpu.VMEM)] * count
+
+
+def prepare_kernel(segments_ref, offsets_ref, cosine_ref, sine_down_ref, sine_up_ref):
+    tokens = segments_ref.shape[1]
+    shape = (tokens, tokens)
+    rows = lax.broadcasted_iota(jnp.int32, shape, 0)
+    columns = lax.broadcasted_iota(jnp.int32, shape, 1)
+    across = jnp.broadcast_to(segments_ref[...], shape).astype(jnp.float32)
+    down = jnp.sum(jnp.where(rows == columns, across, 0.0), axis=1, keepdims=True)
+    earlier = (across == down) & (columns < rows)
+    offsets = jnp.sum(jnp.where(earlier, 1.0, 0.0), axis=1, keepdims=True)
+    offsets_ref[...] = jnp.broadcast_to(offsets, offsets_ref.shape)
+    half = ROT // 2
+    lane = lax.broadcasted_iota(jnp.int32, (tokens, 128), 1)
+    step = (lane & (half - 1)).astype(jnp.float32)
+    frequency = jnp.exp(step * (-2.0 * math.log(rotary_base) / ROT))
+    angles = offsets * frequency
+    sine = jnp.sin(angles)
+    cosine_ref[...] = jnp.where(lane < ROT, jnp.cos(angles), 1.0)
+    sine_down_ref[...] = jnp.where(lane < half, -sine, 0.0)
+    sine_up_ref[...] = jnp.where((lane >= half) & (lane < ROT), sine, 0.0)
+
+
+def prepare(segments):
+    tokens = segments.shape[1]
+    table = jax.ShapeDtypeStruct((tokens, 128), jnp.float32)
+    return pl.pallas_call(
+        prepare_kernel,
+        out_shape=[table] * 4,
+        in_specs=vmem_specs(1),
+        out_specs=vmem_specs(4),
+        compiler_params=pltpu.CompilerParams(vmem_limit_bytes=8 * MIB),
+        name="prepare",
+    )(segments)
+
+
+def layer_kernel(
+    chips,
+    *refs,
+):
+    blocks = refs[: CORES * chips]
+    (
+        attention_gain_ref,
+        feedforward_gain_ref,
+        heads_ref,
+        output_ref,
+        upward_ref,
+        downward_ref,
+        offsets_ref,
+        cosine_ref,
+        sine_down_ref,
+        sine_up_ref,
+        targets_ref,
+        sibling_ref,
+        own_ref,
+        *pages_refs,
+    ) = refs[CORES * chips : -6]
+    attention_scr, feedforward_scr, joined_scr, hidden_scr, attended_scr, counts_ref = refs[-6:]
+    member = lax.axis_index("tensor")
+    chip = member // CORES
+    core = member % CORES
+    group = lax.axis_index("dp")
+    block_rows = blocks[0].shape[0]
+    tokens = block_rows * CORES * chips
+    piece = 16
+
+    gain_a = attention_gain_ref[...]
+    gain_f = feedforward_gain_ref[...]
+    for mask in range(chips):
+        for away in range(CORES):
+            block_ref = blocks[mask * CORES + away]
+            first = ((chip ^ mask) * CORES + (core ^ away)) * block_rows
+            for part in range(block_rows // piece):
+                floats = block_ref[part * piece : (part + 1) * piece, :].astype(jnp.float32)
+                center = jnp.mean(floats, axis=-1, keepdims=True)
+                shifted = floats - center
+                spread = jnp.mean(shifted * shifted, axis=-1, keepdims=True)
+                scaled = shifted * lax.rsqrt(spread + epsilon)
+                place = pl.ds(pl.multiple_of(first + part * piece, piece), piece)
+                attention_scr[place, :] = (scaled * gain_a).astype(jnp.bfloat16)
+                feedforward_scr[place, :] = (scaled * gain_f).astype(jnp.bfloat16)
+
+    normed = attention_scr[...]
+    cosine = cosine_ref[...]
+    sine_down = sine_down_ref[...]
+    sine_up = sine_up_ref[...]
+    for component in range(3):
+        columns = slice(component * HD, (component + 1) * HD)
+        joined = jnp.dot(
+            normed, heads_ref[:, columns], preferred_element_type=jnp.float32
+        ).astype(jnp.bfloat16)
+        joined_scr[:, columns] = joined
+        if component < 2:
+            turning = joined[:, :128].astype(jnp.float32)
+            turned = (
+                turning * cosine
+                + pltpu.roll(turning, 128 - ROT // 2, 1) * sine_down
+                + pltpu.roll(turning, ROT // 2, 1) * sine_up
+            )
+            joined_scr[:, component * HD : component * HD + 128] = turned.astype(jnp.bfloat16)
+
+    for page_ref in pages_refs:
+        page_ref[...] = jnp.zeros(page_ref.shape, page_ref.dtype)
+    capacity = pages_refs[0].shape[0]
+    for target in range(len(pages_refs)):
+        counts_ref[target] = 0
+    for page in range(tokens // PAGE):
+        target = targets_ref[page]
+        slot = counts_ref[target]
+        counts_ref[target] = slot + 1
+        slot = jnp.minimum(slot, capacity - 1)
+        rows = joined_scr[page * PAGE : (page + 1) * PAGE, HD:]
+        for mask, page_ref in enumerate(pages_refs):
+
+            @pl.when(target == (group ^ mask))
+            def _():
+                page_ref[pl.ds(slot, 1)] = rows[None]
+
+    shape = (tokens, tokens)
+    row = lax.broadcasted_iota(jnp.int32, shape, 0)
+    column = lax.broadcasted_iota(jnp.int32, shape, 1)
+    reach = offsets_ref[:, :1].astype(jnp.int32)
+    allowed = (column <= row) & (column >= row - reach)
+    scores = lax.dot_general(
+        joined_scr[:, :HD],
+        joined_scr[:, HD : 2 * HD],
+        (((1,), (1,)), ((), ())),
+        preferred_element_type=jnp.float32,
+    ) * (HD ** (-0.5))
+    peak = jnp.max(jnp.where(allowed, scores, -jnp.inf), axis=1, keepdims=True)
+    weights = jnp.where(allowed, jnp.exp(scores - peak), 0.0)
+    weight_sum = jnp.sum(weights, axis=1, keepdims=True)
+    mixed = jnp.dot(
+        weights.astype(jnp.bfloat16), joined_scr[:, 2 * HD :], preferred_element_type=jnp.float32
+    )
+    attended_scr[...] = (mixed / weight_sum).astype(jnp.bfloat16)
+
+    normed = feedforward_scr[...]
+    chunk = 256
+    for first in range(0, upward_ref.shape[1], chunk):
+        columns = slice(first, first + chunk)
+        upward = jnp.dot(normed, upward_ref[:, columns], preferred_element_type=jnp.float32)
+        hidden = 0.5 * upward * (1.0 + lax.erf(upward * (0.5**0.5)))
+        hidden_scr[:, columns] = hidden.astype(jnp.bfloat16)
+
+    hidden = hidden_scr[...]
+    attended = attended_scr[...]
+    for first in range(0, downward_ref.shape[1], chunk):
+        columns = slice(first, first + chunk)
+        partial = jnp.dot(
+            attended, output_ref[:, columns], preferred_element_type=jnp.float32
+        ) + jnp.dot(hidden, downward_ref[:, columns], preferred_element_type=jnp.float32)
+        partial = partial.reshape(chips, CORES, block_rows, chunk)
+        even, odd = partial[:, 0], partial[:, 1]
+        own = jnp.where(core == 0, even, odd)
+        sibling = jnp.where(core == 0, odd, even)
+        own_ref[:, :, columns] = own
+        sibling_ref[:, :, columns] = sibling.astype(jnp.bfloat16)
+
+
+def layer(blocks, gains, weights, tables, targets, replica_count):
+    count = len(blocks)
+    chips = count // CORES
+    block_rows, width = blocks[0].shape
+    tokens = block_rows * count
+    capacity = 2 * (tokens // PAGE) // replica_count
+    hidden_width = weights[2].shape[1]
+    out_shape = [
+        jax.ShapeDtypeStruct((chips, block_rows, width), jnp.bfloat16),
+        jax.ShapeDtypeStruct((chips, block_rows, width), jnp.float32),
+    ] + [jax.ShapeDtypeStruct((capacity, PAGE, 2 * HD), jnp.bfloat16)] * replica_count
+    return pl.pallas_call(
+        functools.partial(layer_kernel, chips),
+        out_shape=out_shape,
+        in_specs=vmem_specs(count + 2 + 4 + 4) + [pl.BlockSpec(memory_space=pltpu.SMEM)],
+        out_specs=vmem_specs(len(out_shape)),
+        scratch_shapes=[
+            pltpu.VMEM((tokens, width), jnp.bfloat16),
+            pltpu.VMEM((tokens, width), jnp.bfloat16),
+            pltpu.VMEM((tokens, 3 * HD), jnp.bfloat16),
+            pltpu.VMEM((tokens, hidden_width), jnp.bfloat16),
+            pltpu.VMEM((tokens, HD), jnp.bfloat16),
+            pltpu.SMEM((replica_count,), jnp.int32),
+        ],
+        compiler_params=pltpu.CompilerParams(vmem_limit_bytes=32 * MIB),
+        cost_estimate=pl.CostEstimate(
+            flops=2 * tokens * width * (3 * HD + HD + 2 * hidden_width),
+            bytes_accessed=16 * MIB,
+            transcendentals=tokens * (hidden_width + tokens),
+        ),
+        name="layer",
+    )(*blocks, *gains, *weights, *tables, targets)
+
+
+def reduce_kernel(chips, own_ref, sibling_ref, hidden_ref, base_ref, *out_refs):
+    chip = lax.axis_index("tensor") // CORES
+    base_ref[...] = (
+        hidden_ref[...].astype(jnp.float32)
+        + own_ref[chip]
+        + sibling_ref[chip].astype(jnp.float32)
+    )
+    for mask in range(1, chips):
+        other = chip ^ mask
+        out_refs[mask - 1][...] = (
+            own_ref[other] + sibling_ref[other].astype(jnp.float32)
+        ).astype(jnp.bfloat16)
+
+
+def reduced(own, sibling, hidden_states):
+    chips, block_rows, width = own.shape
+    return pl.pallas_call(
+        functools.partial(reduce_kernel, chips),
+        out_shape=[jax.ShapeDtypeStruct((block_rows, width), jnp.float32)]
+        + [jax.ShapeDtypeStruct((block_rows, width), jnp.bfloat16)] * (chips - 1),
+        in_specs=vmem_specs(3),
+        out_specs=vmem_specs(chips),
+        compiler_params=pltpu.CompilerParams(vmem_limit_bytes=16 * MIB),
+        name="reduced",
+    )(own, sibling, hidden_states)
+
+
+def finish_kernel(base_ref, *refs):
+    total = base_ref[...]
+    for ref in refs[:-1]:
+        total = total + ref[...].astype(jnp.float32)
+    refs[-1][...] = total
+
+
+def finished(base, parts):
+    return pl.pallas_call(
+        finish_kernel,
+        out_shape=jax.ShapeDtypeStruct(base.shape, base.dtype),
+        in_specs=vmem_specs(1 + len(parts)),
+        out_specs=pl.BlockSpec(memory_space=pltpu.VMEM),
+        compiler_params=pltpu.CompilerParams(vmem_limit_bytes=8 * MIB),
+        name="finished",
+    )(base, *parts)
+
+
+def place_kernel(*refs):
+    group = lax.axis_index("dp")
+    page_refs, cache_ref, sems = refs[:-2], refs[-2], refs[-1]
+    copies = [
+        pltpu.make_async_copy(page_ref, cache_ref.at[0, group ^ mask], sems.at[mask])
+        for mask, page_ref in enumerate(page_refs)
+    ]
+    for copy in copies:
+        copy.start()
+    for copy in copies:
+        copy.wait()
+
+
+def placed(pages):
+    count = len(pages)
+    return pl.pallas_call(
+        place_kernel,
+        out_shape=jax.ShapeDtypeStruct((1, count) + pages[0].shape, pages[0].dtype),
+        in_specs=[pl.BlockSpec(memory_space=pl.ANY)] * count,
+        out_specs=pl.BlockSpec(memory_space=pl.ANY),
+        scratch_shapes=[pltpu.SemaphoreType.DMA((count,))],
+        compiler_params=pltpu.CompilerParams(vmem_limit_bytes=8 * MIB),
+        name="placed",
+    )(*pages)
+
+
+def shards_whole_heads(
+    hidden_states,
+    attention_gain,
+    feedforward_gain,
+    heads_weight,
+    output_weight,
+    upward_weight,
+    downward_weight,
+    segments,
+    page_targets,
+):
+    chips = lax.axis_size("tensor") // CORES
+    replica_count = lax.axis_size("dp")
+    near = [hidden_states] + [
+        exchanged(hidden_states, "tensor", mask * CORES) for mask in range(1, chips)
+    ]
+    blocks = []
+    for block in near:
+        blocks += [block, exchanged(block, "tensor", 1)]
+    tables = prepare(segments)
+    weights = (heads_weight, output_weight, upward_weight, downward_weight)
+    sibling, own, *pages = layer(
+        blocks,
+        (attention_gain[None], feedforward_gain[None]),
+        [in_vmem(weight) for weight in weights],
+        tables,
+        page_targets[:, 0],
+        replica_count,
+    )
+    received = exchanged(sibling, "tensor", 1)
+    base, *outgoing = reduced(own, received, hidden_states)
+    incoming = [
+        exchanged(block, "tensor", (mask + 1) * CORES) for mask, block in enumerate(outgoing)
+    ]
+    cache_pages = placed(
+        [pages[0]] + [exchanged(pages[mask], "dp", mask) for mask in range(1, replica_count)]
+    )
+    return (finished(base, incoming), cache_pages)
+
+
 def solution(mesh):
+    whole_heads = mesh.shape["tensor"] == H and mesh.shape["dp"] == 4
+    shards = shards_whole_heads if whole_heads else shards_split_heads
     in_specs = (
         P(("dp", "tensor"), None),
         P(),

time: 114 us -> 54 us (0.47)
  matrix products: 20.3 us -> 0 us
  between operations: 18.7 us -> 0.73 us
  waiting for transfers between devices: 35.8 us -> 17.9 us
  other arithmetic: 14.8 us -> 0 us
  starting transfers between devices: 0.12 us -> 14.9 us
  blocking collectives: 12.3 us -> 0 us
  Pallas kernels: 0 us -> 8.89 us
    all_gather x2 -> x0, waiting for transfers between devices: 23.3 us -> none  [shards(): lax.all_gather((normed_attention, normed_feedforward), 'tensor', axis=0,...]
    dot_general x8 -> x0, matrix products: 20.3 us -> none  [the longest x1 9.65 us: shards(): jnp.dot(hidden_rows, downward_weight, preferred_element_type=jnp.float32)]
    ppermute x0 -> x14, waiting for transfers between devices: none -> 17.9 us  [exchanged(): lax.ppermute(block, axis, [(member, member ^ mask) for member in range(co...]
    ppermute x0 -> x14, starting transfers between devices: none -> 14.9 us  [exchanged(): lax.ppermute(block, axis, [(member, member ^ mask) for member in range(co...]
    all_to_all x1 -> x0, blocking collectives: 12.3 us -> none  [shards(): lax.all_to_all(outgoing, 'dp', split_axis=0, concat_axis=0, tiled=True)]
    reduce_scatter x1 -> x0, waiting for transfers between devices: 11.7 us -> none  [shards(): lax.psum_scatter((jnp.dot(attended_quarter, output_weight, preferred_elem...]
    pallas_call x0 -> x5, Pallas kernels: none -> 8.89 us  [the longest x1 6.54 us: layer(): pl.pallas_call(functools.partial(layer_kernel, chips), out_shape=out_shap...]
    unnamed x28 -> x18, local copies, waits for them, and re-layouts: 2.68 us -> 11.1 us
  transfers between devices with their start and end apart: 3 -> 14, of which waited for: 3 -> 4; matrix products, arithmetic and copies ran while one was open for 24% -> 0% of each run, Pallas kernels for 0% -> 3%
where the time goes in v1:
time: 54 us; the launch traced here: 53.6 us
  waiting for transfers between devices  17.9 us (33%)
  starting transfers between devices  14.9 us (28%)
  local copies, waits for them, and re-layouts  11.1 us (21%)
  Pallas kernels  8.89 us (16%)
  between operations  0.73 us (1%)
    ppermute x14, waiting for transfers between devices, exchanged(): lax.ppermute(block, axis, [(member, member ^ mask) for member in range(co...  17.9 us
    ppermute x14, starting transfers between devices, exchanged(): lax.ppermute(block, axis, [(member, member ^ mask) for member in range(co...  14.9 us
    unnamed x18, local copies, waits for them, and re-layouts  11.1 us
    pallas_call x1, Pallas kernels, layer(): pl.pallas_call(functools.partial(layer_kernel, chips), out_shape=out_shap...  6.54 us
  transfers between devices with their start and end apart: 14, of which 4 were waited for; matrix products, arithmetic and copies ran while one was open for 0% of the time, Pallas kernels for 3%

profile of v1, /device:TPU:0, one launch (start us, length us, event | category | flops | bytes accessed | tf_op | source)
XLA Modules:
  0.0 53.6 jit_solution(8941175927489152320)
XLA Ops:
  0.6 5.1 %collective-permute-start.5 = (bf16[32,2048]{1,0:T(8,128)(2,1)}, bf16[32,2048]{1,0:T(8,128)(2,1)S(1)}, u32[]{:S(2)}, u32[]{:S(2)}) collective-permute-start(bf16[32,2048]{1,0:T(8,128)(2,1)} %hidden_ref.1), channel_id=1, source_target_pairs={{0,6},{1,7},{2,4},{3,5},{4,2},{5,3},{6,0},{7,1},{8,14},{9,15},{10,... | collective-permute-start | bytes 393224 | tf_op jit(solution)/shard_map/ppermute | solution.py:234
  5.7 0.6 %collective-permute-start.1 = (bf16[32,2048]{1,0:T(8,128)(2,1)}, bf16[32,2048]{1,0:T(8,128)(2,1)S(1)}, u32[]{:S(2)}, u32[]{:S(2)}) collective-permute-start(bf16[32,2048]{1,0:T(8,128)(2,1)} %hidden_ref.1), channel_id=1, source_target_pairs={{0,2},{1,3},{2,0},{3,1},{4,6},{5,7},{6,4},{7,5},{8,10},{9,11},{10,... | collective-permute-start | bytes 393224 | tf_op jit(solution)/shard_map/ppermute | solution.py:234
  6.4 0.0 collective-permute-start
  6.4 4.0 %collective-permute-done.5.refs_6_ = bf16[32,2048]{1,0:T(8,128)(2,1)S(1)} collective-permute-done((bf16[32,2048]{1,0:T(8,128)(2,1)}, bf16[32,2048]{1,0:T(8,128)(2,1)S(1)}, u32[]{:S(2)}, u32[]{:S(2)}) %collective-permute-start.5) | collective-permute-done | bytes 131104 | tf_op jit(solution)/shard_map/ppermute | solution.py:234
  10.4 6.6 %collective-permute-done.3.refs_4_ = bf16[32,2048]{1,0:T(8,128)(2,1)S(1)} collective-permute-done((bf16[32,2048]{1,0:T(8,128)(2,1)}, bf16[32,2048]{1,0:T(8,128)(2,1)S(1)}, u32[]{:S(2)}, u32[]{:S(2)}) %collective-permute-start.3) | collective-permute-done | bytes 131104 | tf_op jit(solution)/shard_map/ppermute | solution.py:234
  17.0 0.0 collective-permute-start.4
  17.0 0.5 collective-permute-start.2
  17.5 0.7 %copy-done.8 = s32[1,256]{1,0:T(1,128)S(1)} copy-done((s32[1,256]{1,0:T(1,128)S(1)}, s32[1,256]{1,0:T(1,128)}, u32[]{:S(2)}) %copy-start.8) | copy-done | bytes 1048
  18.2 0.7 %prepare.1 = (f32[256,128]{1,0:T(8,128)S(1)}, f32[256,128]{1,0:T(8,128)S(1)}, f32[256,128]{1,0:T(8,128)S(1)}, f32[256,128]{1,0:T(8,128)S(1)}) custom-call(s32[1,256]{1,0:T(1,128)S(1)} %copy-done.8), custom_call_target="tpu_custom_call" | custom-call | tf_op jit(solution)/shard_map/prepare/pallas_call | solution.py:265
  18.9 0.0 copy-start
  18.9 2.2 %copy-done = bf16[2048,1024]{1,0:T(8,128)(2,1)S(1)} copy-done((bf16[2048,1024]{1,0:T(8,128)(2,1)S(1)}, bf16[2048,1024]{1,0:T(8,128)(2,1)}, u32[]{:S(2)}) %copy-start) | copy-done | bytes 4194328
  21.1 2.2 %copy-done.1 = bf16[1024,2048]{1,0:T(8,128)(2,1)S(1)} copy-done((bf16[1024,2048]{1,0:T(8,128)(2,1)S(1)}, bf16[1024,2048]{1,0:T(8,128)(2,1)}, u32[]{:S(2)}) %copy-start.1) | copy-done | bytes 4194328
  23.3 1.9 %copy-done.2 = bf16[2048,768]{1,0:T(8,128)(2,1)S(1)} copy-done((bf16[2048,768]{1,0:T(8,128)(2,1)S(1)}, bf16[2048,768]{1,0:T(8,128)(2,1)}, u32[]{:S(2)}) %copy-start.2) | copy-done | bytes 3145752
  25.2 1.2 %copy-done.3 = bf16[256,2048]{1,0:T(8,128)(2,1)S(1)} copy-done((bf16[256,2048]{1,0:T(8,128)(2,1)S(1)}, bf16[256,2048]{1,0:T(8,128)(2,1)}, u32[]{:S(2)}) %copy-start.3) | copy-done | bytes 1048600
  26.4 0.9 %copy-done.4 = bf16[32,2048]{1,0:T(8,128)(2,1)S(1)} copy-done((bf16[32,2048]{1,0:T(8,128)(2,1)S(1)}, bf16[32,2048]{1,0:T(8,128)(2,1)}, u32[]{:S(2)}) %copy-start.4) | copy-done | bytes 131096
  27.3 0.7 %copy-done.5 = f32[2048]{0:T(1024)S(1)} copy-done((f32[2048]{0:T(1024)S(1)}, f32[2048]{0:T(1024)}, u32[]{:S(2)}) %copy-start.5) | copy-done | bytes 8216
  28.0 0.7 %copy-done.6 = f32[2048]{0:T(1024)S(1)} copy-done((f32[2048]{0:T(1024)S(1)}, f32[2048]{0:T(1024)}, u32[]{:S(2)}) %copy-start.6) | copy-done | bytes 8216
  28.7 0.7 %copy-done.7 = s32[16,1]{0,1:T(1,128)S(1)} copy-done((s32[16,1]{0,1:T(1,128)S(1)}, s32[16,1]{0,1:T(1,128)}, u32[]{:S(2)}) %copy-start.7) | copy-done | bytes 88
  29.4 6.5 %layer.1 = (bf16[4,32,2048]{2,1,0:T(8,128)(2,1)S(1)}, f32[4,32,2048]{2,1,0:T(8,128)S(1)}, bf16[8,16,512]{2,1,0:T(8,128)(2,1)S(1)}, bf16[8,16,512]{2,1,0:T(8,128)...) custom-call(bf16[32,2048]{1,0:T(8,128)(2,1)S(1)} %copy-done.4, ...), custom_call_target="tpu_custom_call" | custom-call | flops 3221225472 | bytes 16777216 | tf_op jit(solution)/shard_map/layer/pallas_call | solution.py:410
  35.9 0.1 collective-permute-start.7
  36.0 1.5 %collective-permute-start.11 = (bf16[8,16,512]{2,1,0:T(8,128)(2,1)S(1)}, bf16[8,16,512]{2,1,0:T(8,128)(2,1)S(1)}, u32[]{:S(2)}, u32[]{:S(2)}) collective-permute-start(bf16[8,16,512]{2,1,0:T(8,128)(2,1)S(1)} %get-tuple-element.27), channel_id=1, source_target_pairs={{0,8},{8,0},{16,24},{24,16},{1,9},{9,1},{17,25},{25,17},{2,10},{10... | collective-permute-start | bytes 393224 | tf_op jit(solution)/shard_map/ppermute | solution.py:234
  37.5 1.5 %collective-permute-start.12 = (bf16[8,16,512]{2,1,0:T(8,128)(2,1)S(1)}, bf16[8,16,512]{2,1,0:T(8,128)(2,1)S(1)}, u32[]{:S(2)}, u32[]{:S(2)}) collective-permute-start(bf16[8,16,512]{2,1,0:T(8,128)(2,1)S(1)} %get-tuple-element.28), channel_id=1, source_target_pairs={{0,16},{8,24},{16,0},{24,8},{1,17},{9,25},{17,1},{25,9},{2,18},{10... | collective-permute-start | bytes 393224 | tf_op jit(solution)/shard_map/ppermute | solution.py:234
  39.1 0.5 collective-permute-start.13
  39.6 0.1 reduced.1
  39.7 0.1 collective-permute-start.8
  39.8 3.0 %collective-permute-start.9 = (bf16[32,2048]{1,0:T(8,128)(2,1)S(1)}, bf16[32,2048]{1,0:T(8,128)(2,1)S(1)}, u32[]{:S(2)}, u32[]{:S(2)}) collective-permute-start(bf16[32,2048]{1,0:T(8,128)(2,1)S(1)} %get-tuple-element.24), channel_id=1, source_target_pairs={{0,4},{1,5},{2,6},{3,7},{4,0},{5,1},{6,2},{7,3},{8,12},{9,13},{10,... | collective-permute-start | bytes 393224 | tf_op jit(solution)/shard_map/ppermute | solution.py:234
  42.8 1.9 %collective-permute-start.10 = (bf16[32,2048]{1,0:T(8,128)(2,1)S(1)}, bf16[32,2048]{1,0:T(8,128)(2,1)S(1)}, u32[]{:S(2)}, u32[]{:S(2)}) collective-permute-start(bf16[32,2048]{1,0:T(8,128)(2,1)S(1)} %get-tuple-element.25), channel_id=1, source_target_pairs={{0,6},{1,7},{2,4},{3,5},{4,2},{5,3},{6,0},{7,1},{8,14},{9,15},{10,... | collective-permute-start | bytes 393224 | tf_op jit(solution)/shard_map/ppermute | solution.py:234
  44.7 1.2 %collective-permute-done.12.refs_2_ = bf16[8,16,512]{2,1,0:T(8,128)(2,1)S(1)} collective-permute-done((bf16[8,16,512]{2,1,0:T(8,128)(2,1)S(1)}, bf16[8,16,512]{2,1,0:T(8,128)(2,1)S(1)}, u32[]{:S(2)}, u32[]{:S(2)}) %collective-permute-start.12) | collective-permute-done | bytes 131104 | tf_op jit(solution)/shard_map/ppermute | solution.py:234
  45.9 0.8 %placed.1 = bf16[1,4,8,16,512]{4,3,2,1,0:T(8,128)(2,1)} custom-call(bf16[8,16,512]{2,1,0:T(8,128)(2,1)S(1)} %get-tuple-element.26.refs_0_, bf16[8,16,512]{2,1,0:T(8,128)(2,1)S(1)} %collective-permute-done.11.refs_1_, bf16[8,16,512]{2,1,0:T(8,128)(2,1)S(1)} %collective-permute-done.12.refs_2_, bf16[8,16,512]{2,1,0:T(8,128)(2,1)S(1)} %collective-permute-done.13.refs_3_), custom_call_target="tpu_custom_call" | custom-call | tf_op jit(solution)/shard_map/placed/pallas_call | solution.py:493
  46.8 0.0 collective-permute-done.8.refs_0_
  46.8 6.0 %collective-permute-done.9.refs_1_ = bf16[32,2048]{1,0:T(8,128)(2,1)S(1)} collective-permute-done((bf16[32,2048]{1,0:T(8,128)(2,1)S(1)}, bf16[32,2048]{1,0:T(8,128)(2,1)S(1)}, u32[]{:S(2)}, u32[]{:S(2)}) %collective-permute-start.9) | collective-permute-done | bytes 131104 | tf_op jit(solution)/shard_map/ppermute | solution.py:234
  52.8 0.8 %finished.1 = f32[32,2048]{1,0:T(8,128)} custom-call(f32[32,2048]{1,0:T(8,128)S(1)} %get-tuple-element.22.base_ref, bf16[32,2048]{1,0:T(8,128)(2,1)S(1)} %collective-permute-done.8.refs_0_, bf16[32,2048]{1,0:T(8,128)(2,1)S(1)} %collective-permute-done.9.refs_1_, bf16[32,2048]{1,0:T(8,128)(2,1)S(1)} %collective-permute-done.10.refs_2_), custom_call_target="tpu_custom_call" | custom-call | tf_op jit(solution)/shard_map/finished/pallas_call | solution.py:468
  (19 shorter events, 0.0 us)
Async XLA Ops:
  0.6 9.8 %collective-permute-start.5 = (bf16[32,2048]{1,0:T(8,128)(2,1)}, bf16[32,2048]{1,0:T(8,128)(2,1)S(1)}, u32[]{:S(2)}, u32[]{:S(2)}) collective-permute-start(bf16[32,2048]{1,0:T(8,128)(2,1)} %hidden_ref.1), channel_id=1, source_target_pairs={{0,6},{1,7},{2,4},{3,5},{4,2},{5,3},{6,0},{7,1},{8,14},{9,15},{10,... | collective-permute-start | bytes 393224 | tf_op jit(solution)/shard_map/ppermute | solution.py:234
  5.7 11.3 %collective-permute-start.3 = (bf16[32,2048]{1,0:T(8,128)(2,1)}, bf16[32,2048]{1,0:T(8,128)(2,1)S(1)}, u32[]{:S(2)}, u32[]{:S(2)}) collective-permute-start(bf16[32,2048]{1,0:T(8,128)(2,1)} %hidden_ref.1), channel_id=1, source_target_pairs={{0,4},{1,5},{2,6},{3,7},{4,0},{5,1},{6,2},{7,3},{8,12},{9,13},{10,... | collective-permute-start | bytes 393224 | tf_op jit(solution)/shard_map/ppermute | solution.py:234
  5.7 11.3 %collective-permute-start.1 = (bf16[32,2048]{1,0:T(8,128)(2,1)}, bf16[32,2048]{1,0:T(8,128)(2,1)S(1)}, u32[]{:S(2)}, u32[]{:S(2)}) collective-permute-start(bf16[32,2048]{1,0:T(8,128)(2,1)} %hidden_ref.1), channel_id=1, source_target_pairs={{0,2},{1,3},{2,0},{3,1},{4,6},{5,7},{6,4},{7,5},{8,10},{9,11},{10,... | collective-permute-start | bytes 393224 | tf_op jit(solution)/shard_map/ppermute | solution.py:234
  6.4 12.5 %collective-permute-start = (bf16[32,2048]{1,0:T(8,128)(2,1)}, bf16[32,2048]{1,0:T(8,128)(2,1)S(1)}, u32[]{:S(2)}, u32[]{:S(2)}) collective-permute-start(bf16[32,2048]{1,0:T(8,128)(2,1)} %hidden_ref.1), channel_id=1, source_target_pairs={{0,1},{1,0},{2,3},{3,2},{4,5},{5,4},{6,7},{7,6},{8,9},{9,8},{10,11... | collective-permute-start | bytes 393224 | tf_op jit(solution)/shard_map/ppermute | solution.py:234
  10.4 8.5 %collective-permute-start.6 = (bf16[32,2048]{1,0:T(8,128)(2,1)S(1)}, bf16[32,2048]{1,0:T(8,128)(2,1)S(1)}, u32[]{:S(2)}, u32[]{:S(2)}) collective-permute-start(bf16[32,2048]{1,0:T(8,128)(2,1)S(1)} %collective-permute-done.5.refs_6_), channel_id=1, source_target_pairs={{0,1},{1,0},{2,3},{3,2},{4,5},{5,4},{6,7},{7,6},{8,9},{9,8},{10,11... | collective-permute-start | bytes 393224 | tf_op jit(solution)/shard_map/ppermute | solution.py:234
  17.0 1.9 %collective-permute-start.4 = (bf16[32,2048]{1,0:T(8,128)(2,1)S(1)}, bf16[32,2048]{1,0:T(8,128)(2,1)S(1)}, u32[]{:S(2)}, u32[]{:S(2)}) collective-permute-start(bf16[32,2048]{1,0:T(8,128)(2,1)S(1)} %collective-permute-done.3.refs_4_), channel_id=1, source_target_pairs={{0,1},{1,0},{2,3},{3,2},{4,5},{5,4},{6,7},{7,6},{8,9},{9,8},{10,11... | collective-permute-start | bytes 393224 | tf_op jit(solution)/shard_map/ppermute | solution.py:234
  17.0 1.9 %collective-permute-start.2 = (bf16[32,2048]{1,0:T(8,128)(2,1)S(1)}, bf16[32,2048]{1,0:T(8,128)(2,1)S(1)}, u32[]{:S(2)}, u32[]{:S(2)}) collective-permute-start(bf16[32,2048]{1,0:T(8,128)(2,1)S(1)} %collective-permute-done.1.refs_2_), channel_id=1, source_target_pairs={{0,1},{1,0},{2,3},{3,2},{4,5},{5,4},{6,7},{7,6},{8,9},{9,8},{10,11... | collective-permute-start | bytes 393224 | tf_op jit(solution)/shard_map/ppermute | solution.py:234
  17.5 0.7 %copy-start.8 = (s32[1,256]{1,0:T(1,128)S(1)}, s32[1,256]{1,0:T(1,128)}, u32[]{:S(2)}) copy-start(s32[1,256]{1,0:T(1,128)} %segments_ref.1) | copy-start | bytes 3076
  18.9 2.2 %copy-start = (bf16[2048,1024]{1,0:T(8,128)(2,1)S(1)}, bf16[2048,1024]{1,0:T(8,128)(2,1)}, u32[]{:S(2)}) copy-start(bf16[2048,1024]{1,0:T(8,128)(2,1)} %refs_12_.1) | copy-start | bytes 12582916
  21.1 2.2 %copy-start.1 = (bf16[1024,2048]{1,0:T(8,128)(2,1)S(1)}, bf16[1024,2048]{1,0:T(8,128)(2,1)}, u32[]{:S(2)}) copy-start(bf16[1024,2048]{1,0:T(8,128)(2,1)} %refs_13_.1) | copy-start | bytes 12582916
  23.3 1.9 %copy-start.2 = (bf16[2048,768]{1,0:T(8,128)(2,1)S(1)}, bf16[2048,768]{1,0:T(8,128)(2,1)}, u32[]{:S(2)}) copy-start(bf16[2048,768]{1,0:T(8,128)(2,1)} %refs_10_.1) | copy-start | bytes 9437188
  25.2 1.2 %copy-start.3 = (bf16[256,2048]{1,0:T(8,128)(2,1)S(1)}, bf16[256,2048]{1,0:T(8,128)(2,1)}, u32[]{:S(2)}) copy-start(bf16[256,2048]{1,0:T(8,128)(2,1)} %refs_11_.1) | copy-start | bytes 3145732
  26.4 0.9 %copy-start.4 = (bf16[32,2048]{1,0:T(8,128)(2,1)S(1)}, bf16[32,2048]{1,0:T(8,128)(2,1)}, u32[]{:S(2)}) copy-start(bf16[32,2048]{1,0:T(8,128)(2,1)} %hidden_ref.1) | copy-start | bytes 393220
  27.3 0.7 %copy-start.5 = (f32[2048]{0:T(1024)S(1)}, f32[2048]{0:T(1024)}, u32[]{:S(2)}) copy-start(f32[2048]{0:T(1024)} %param.10) | copy-start | bytes 24580
  28.0 0.7 %copy-start.6 = (f32[2048]{0:T(1024)S(1)}, f32[2048]{0:T(1024)}, u32[]{:S(2)}) copy-start(f32[2048]{0:T(1024)} %param.11) | copy-start | bytes 24580
  28.7 0.7 %copy-start.7 = (s32[16,1]{0,1:T(1,128)S(1)}, s32[16,1]{0,1:T(1,128)}, u32[]{:S(2)}) copy-start(s32[16,1]{0,1:T(1,128)} %param.17) | copy-start | bytes 196
  35.9 3.6 %collective-permute-start.7 = (bf16[4,32,2048]{2,1,0:T(8,128)(2,1)S(1)}, bf16[4,32,2048]{2,1,0:T(8,128)(2,1)S(1)}, u32[]{:S(2)}, u32[]{:S(2)}) collective-permute-start(bf16[4,32,2048]{2,1,0:T(8,128)(2,1)S(1)} %get-tuple-element.21), channel_id=1, source_target_pairs={{0,1},{1,0},{2,3},{3,2},{4,5},{5,4},{6,7},{7,6},{8,9},{9,8},{10,11... | collective-permute-start | bytes 1572872 | tf_op jit(solution)/shard_map/ppermute | solution.py:234
  36.0 6.8 %collective-permute-start.11 = (bf16[8,16,512]{2,1,0:T(8,128)(2,1)S(1)}, bf16[8,16,512]{2,1,0:T(8,128)(2,1)S(1)}, u32[]{:S(2)}, u32[]{:S(2)}) collective-permute-start(bf16[8,16,512]{2,1,0:T(8,128)(2,1)S(1)} %get-tuple-element.27), channel_id=1, source_target_pairs={{0,8},{8,0},{16,24},{24,16},{1,9},{9,1},{17,25},{25,17},{2,10},{10... | collective-permute-start | bytes 393224 | tf_op jit(solution)/shard_map/ppermute | solution.py:234
  37.5 8.4 %collective-permute-start.12 = (bf16[8,16,512]{2,1,0:T(8,128)(2,1)S(1)}, bf16[8,16,512]{2,1,0:T(8,128)(2,1)S(1)}, u32[]{:S(2)}, u32[]{:S(2)}) collective-permute-start(bf16[8,16,512]{2,1,0:T(8,128)(2,1)S(1)} %get-tuple-element.28), channel_id=1, source_target_pairs={{0,16},{8,24},{16,0},{24,8},{1,17},{9,25},{17,1},{25,9},{2,18},{10... | collective-permute-start | bytes 393224 | tf_op jit(solution)/shard_map/ppermute | solution.py:234
  39.1 6.9 %collective-permute-start.13 = (bf16[8,16,512]{2,1,0:T(8,128)(2,1)S(1)}, bf16[8,16,512]{2,1,0:T(8,128)(2,1)S(1)}, u32[]{:S(2)}, u32[]{:S(2)}) collective-permute-start(bf16[8,16,512]{2,1,0:T(8,128)(2,1)S(1)} %get-tuple-element.29), channel_id=1, source_target_pairs={{0,24},{8,16},{16,8},{24,0},{1,25},{9,17},{17,9},{25,1},{2,26},{10... | collective-permute-start | bytes 393224 | tf_op jit(solution)/shard_map/ppermute | solution.py:234
  39.7 7.1 %collective-permute-start.8 = (bf16[32,2048]{1,0:T(8,128)(2,1)S(1)}, bf16[32,2048]{1,0:T(8,128)(2,1)S(1)}, u32[]{:S(2)}, u32[]{:S(2)}) collective-permute-start(bf16[32,2048]{1,0:T(8,128)(2,1)S(1)} %get-tuple-element.23), channel_id=1, source_target_pairs={{0,2},{1,3},{2,0},{3,1},{4,6},{5,7},{6,4},{7,5},{8,10},{9,11},{10,... | collective-permute-start | bytes 393224 | tf_op jit(solution)/shard_map/ppermute | solution.py:234
  39.8 13.0 %collective-permute-start.9 = (bf16[32,2048]{1,0:T(8,128)(2,1)S(1)}, bf16[32,2048]{1,0:T(8,128)(2,1)S(1)}, u32[]{:S(2)}, u32[]{:S(2)}) collective-permute-start(bf16[32,2048]{1,0:T(8,128)(2,1)S(1)} %get-tuple-element.24), channel_id=1, source_target_pairs={{0,4},{1,5},{2,6},{3,7},{4,0},{5,1},{6,2},{7,3},{8,12},{9,13},{10,... | collective-permute-start | bytes 393224 | tf_op jit(solution)/shard_map/ppermute | solution.py:234
  42.8 10.0 %collective-permute-start.10 = (bf16[32,2048]{1,0:T(8,128)(2,1)S(1)}, bf16[32,2048]{1,0:T(8,128)(2,1)S(1)}, u32[]{:S(2)}, u32[]{:S(2)}) collective-permute-start(bf16[32,2048]{1,0:T(8,128)(2,1)S(1)} %get-tuple-element.25), channel_id=1, source_target_pairs={{0,6},{1,7},{2,4},{3,5},{4,2},{5,3},{6,0},{7,1},{8,14},{9,15},{10,... | collective-permute-start | bytes 393224 | tf_op jit(solution)/shard_map/ppermute | solution.py:234

commit v2 on v1

--- a/solution.py
+++ b/solution.py
@@ -225,8 +225,8 @@
 MIB = 1 << 20
 
 
-def in_vmem(array):
-    return pltpu.with_memory_space_constraint(array, pltpu.VMEM)
+def in_hbm(array):
+    return pltpu.with_memory_space_constraint(array, pltpu.HBM)
 
 
 def exchanged(block, axis, mask):
@@ -238,7 +238,20 @@
     return [pl.BlockSpec(memory_space=pltpu.VMEM)] * count
 
 
-def prepare_kernel(segments_ref, offsets_ref, cosine_ref, sine_down_ref, sine_up_ref):
+def prepare_kernel(count, segments_ref, *refs):
+    sources, targets = refs[:count], refs[count : 2 * count]
+    offsets_ref, cosine_ref, sine_down_ref, sine_up_ref, sems = refs[2 * count :]
+    copies = []
+    for number, (source, target) in enumerate(zip(sources, targets)):
+        parts = 4 if source.shape[0] >= 256 else 1
+        rows = source.shape[0] // parts
+        for part in range(parts):
+            place = pl.ds(part * rows, rows)
+            copies.append(
+                pltpu.make_async_copy(source.at[place], target.at[place], sems.at[number, part])
+            )
+    for copy in copies:
+        copy.start()
     tokens = segments_ref.shape[1]
     shape = (tokens, tokens)
     rows = lax.broadcasted_iota(jnp.int32, shape, 0)
@@ -257,19 +270,27 @@
     cosine_ref[...] = jnp.where(lane < ROT, jnp.cos(angles), 1.0)
     sine_down_ref[...] = jnp.where(lane < half, -sine, 0.0)
     sine_up_ref[...] = jnp.where((lane >= half) & (lane < ROT), sine, 0.0)
-
-
-def prepare(segments):
+    for copy in copies:
+        copy.wait()
+
+
+def prepare(segments, staged):
     tokens = segments.shape[1]
-    table = jax.ShapeDtypeStruct((tokens, 128), jnp.float32)
+    shapes = [pltpu.VMEM(array.shape, array.dtype) for array in staged]
+    shapes += [pltpu.VMEM((tokens, 128), jnp.float32)] * 4
+    count = len(staged)
     return pl.pallas_call(
-        prepare_kernel,
-        out_shape=[table] * 4,
-        in_specs=vmem_specs(1),
-        out_specs=vmem_specs(4),
+        functools.partial(prepare_kernel, count),
+        out_shape=shapes,
+        in_specs=vmem_specs(1) + [pl.BlockSpec(memory_space=pltpu.HBM)] * count,
+        out_specs=vmem_specs(len(shapes)),
+        scratch_shapes=[pltpu.SemaphoreType.DMA((count, 4))],
         compiler_params=pltpu.CompilerParams(vmem_limit_bytes=8 * MIB),
+        cost_estimate=pl.CostEstimate(
+            flops=0, bytes_accessed=sum(array.nbytes for array in staged), transcendentals=0
+        ),
         name="prepare",
-    )(segments)
+    )(segments, *[in_hbm(array) for array in staged])
 
 
 def layer_kernel(
@@ -292,8 +313,11 @@
         sibling_ref,
         own_ref,
         *pages_refs,
-    ) = refs[CORES * chips : -6]
-    attention_scr, feedforward_scr, joined_scr, hidden_scr, attended_scr, counts_ref = refs[-6:]
+    ) = refs[CORES * chips : -8]
+    attention_scr, feedforward_scr, joined_scr, hidden_scr, attended_scr = refs[-8:-3]
+    named_ref, counts_ref, sem = refs[-3:]
+    naming = pltpu.make_async_copy(targets_ref, named_ref, sem)
+    naming.start()
     member = lax.axis_index("tensor")
     chip = member // CORES
     core = member % CORES
@@ -342,8 +366,9 @@
     capacity = pages_refs[0].shape[0]
     for target in range(len(pages_refs)):
         counts_ref[target] = 0
+    naming.wait()
     for page in range(tokens // PAGE):
-        target = targets_ref[page]
+        target = named_ref[page]
         slot = counts_ref[target]
         counts_ref[target] = slot + 1
         slot = jnp.minimum(slot, capacity - 1)
@@ -410,7 +435,7 @@
     return pl.pallas_call(
         functools.partial(layer_kernel, chips),
         out_shape=out_shape,
-        in_specs=vmem_specs(count + 2 + 4 + 4) + [pl.BlockSpec(memory_space=pltpu.SMEM)],
+        in_specs=vmem_specs(count + 2 + 4 + 4) + [pl.BlockSpec(memory_space=pltpu.HBM)],
         out_specs=vmem_specs(len(out_shape)),
         scratch_shapes=[
             pltpu.VMEM((tokens, width), jnp.bfloat16),
@@ -418,7 +443,9 @@
             pltpu.VMEM((tokens, 3 * HD), jnp.bfloat16),
             pltpu.VMEM((tokens, hidden_width), jnp.bfloat16),
             pltpu.VMEM((tokens, HD), jnp.bfloat16),
+            pltpu.SMEM(targets.shape, jnp.int32),
             pltpu.SMEM((replica_count,), jnp.int32),
+            pltpu.SemaphoreType.DMA(()),
         ],
         compiler_params=pltpu.CompilerParams(vmem_limit_bytes=32 * MIB),
         cost_estimate=pl.CostEstimate(
@@ -427,7 +454,7 @@
             transcendentals=tokens * (hidden_width + tokens),
         ),
         name="layer",
-    )(*blocks, *gains, *weights, *tables, targets)
+    )(*blocks, *gains, *weights, *tables, in_hbm(targets))
 
 
 def reduce_kernel(chips, own_ref, sibling_ref, hidden_ref, base_ref, *out_refs):
@@ -457,48 +484,38 @@
     )(own, sibling, hidden_states)
 
 
-def finish_kernel(base_ref, *refs):
-    total = base_ref[...]
-    for ref in refs[:-1]:
-        total = total + ref[...].astype(jnp.float32)
-    refs[-1][...] = total
-
-
-def finished(base, parts):
-    return pl.pallas_call(
-        finish_kernel,
-        out_shape=jax.ShapeDtypeStruct(base.shape, base.dtype),
-        in_specs=vmem_specs(1 + len(parts)),
-        out_specs=pl.BlockSpec(memory_space=pltpu.VMEM),
-        compiler_params=pltpu.CompilerParams(vmem_limit_bytes=8 * MIB),
-        name="finished",
-    )(base, *parts)
-
-
-def place_kernel(*refs):
+def finish_kernel(chips, base_ref, *refs):
     group = lax.axis_index("dp")
-    page_refs, cache_ref, sems = refs[:-2], refs[-2], refs[-1]
+    parts, pages = refs[: chips - 1], refs[chips - 1 : -3]
+    output_ref, cache_ref, sems = refs[-3:]
     copies = [
         pltpu.make_async_copy(page_ref, cache_ref.at[0, group ^ mask], sems.at[mask])
-        for mask, page_ref in enumerate(page_refs)
+        for mask, page_ref in enumerate(pages)
     ]
     for copy in copies:
         copy.start()
+    total = base_ref[...]
+    for part_ref in parts:
+        total = total + part_ref[...].astype(jnp.float32)
+    output_ref[...] = total
     for copy in copies:
         copy.wait()
 
 
-def placed(pages):
+def finished(base, parts, pages):
     count = len(pages)
     return pl.pallas_call(
-        place_kernel,
-        out_shape=jax.ShapeDtypeStruct((1, count) + pages[0].shape, pages[0].dtype),
-        in_specs=[pl.BlockSpec(memory_space=pl.ANY)] * count,
-        out_specs=pl.BlockSpec(memory_space=pl.ANY),
+        functools.partial(finish_kernel, len(parts) + 1),
+        out_shape=[
+            jax.ShapeDtypeStruct(base.shape, base.dtype),
+            jax.ShapeDtypeStruct((1, count) + pages[0].shape, pages[0].dtype),
+        ],
+        in_specs=vmem_specs(1 + len(parts)) + [pl.BlockSpec(memory_space=pl.ANY)] * count,
+        out_specs=vmem_specs(1) + [pl.BlockSpec(memory_space=pltpu.HBM)],
         scratch_shapes=[pltpu.SemaphoreType.DMA((count,))],
         compiler_params=pltpu.CompilerParams(vmem_limit_bytes=8 * MIB),
-        name="placed",
-    )(*pages)
+        name="finished",
+    )(base, *parts, *pages)
 
 
 def shards_whole_heads(
@@ -514,31 +531,37 @@
 ):
     chips = lax.axis_size("tensor") // CORES
     replica_count = lax.axis_size("dp")
-    near = [hidden_states] + [
-        exchanged(hidden_states, "tensor", mask * CORES) for mask in range(1, chips)
+    near = {mask: exchanged(hidden_states, "tensor", mask * CORES) for mask in (2, 3, 1)}
+    beside = exchanged(hidden_states, "tensor", 1)
+    (*staged,) = prepare(
+        segments,
+        (
+            heads_weight,
+            output_weight,
+            upward_weight,
+            downward_weight,
+            attention_gain[None],
+            feedforward_gain[None],
+            hidden_states,
+        ),
+    )
+    blocks = [staged[6], beside]
+    for mask in range(1, chips):
+        near[mask], staged[7] = lax.optimization_barrier((near[mask], staged[7]))
+        blocks += [near[mask], exchanged(near[mask], "tensor", 1)]
+    sibling, own, *pages = layer(
+        blocks, staged[4:6], staged[:4], staged[7:], page_targets[:, 0], replica_count
+    )
+    received = exchanged(sibling, "tensor", 1)
+    base, *outgoing = reduced(own, received, staged[6])
+    outgoing, pages = lax.optimization_barrier((outgoing, pages))
+    incoming = [
+        exchanged(outgoing[mask - 1], "tensor", mask * CORES) for mask in (2, 3, 1)
     ]
-    blocks = []
-    for block in near:
-        blocks += [block, exchanged(block, "tensor", 1)]
-    tables = prepare(segments)
-    weights = (heads_weight, output_weight, upward_weight, downward_weight)
-    sibling, own, *pages = layer(
-        blocks,
-        (attention_gain[None], feedforward_gain[None]),
-        [in_vmem(weight) for weight in weights],
-        tables,
-        page_targets[:, 0],
-        replica_count,
-    )
-    received = exchanged(sibling, "tensor", 1)
-    base, *outgoing = reduced(own, received, hidden_states)
-    incoming = [
-        exchanged(block, "tensor", (mask + 1) * CORES) for mask, block in enumerate(outgoing)
+    arriving = [pages[0]] + [
+        exchanged(pages[mask], "dp", mask) for mask in range(1, replica_count)
     ]
-    cache_pages = placed(
-        [pages[0]] + [exchanged(pages[mask], "dp", mask) for mask in range(1, replica_count)]
-    )
-    return (finished(base, incoming), cache_pages)
+    return tuple(finished(base, incoming, arriving))
 
 
 def solution(mesh):

time: 54 us -> 47.7 us (0.88)
  local copies, waits for them, and re-layouts: 11.1 us -> 0.68 us
  Pallas kernels: 8.89 us -> 12.9 us
  starting transfers between devices: 14.9 us -> 16.3 us
  waiting for transfers between devices: 17.9 us -> 17 us
    unnamed x18 -> x2, local copies, waits for them, and re-layouts: 11.1 us -> 0.68 us
    pallas_call x3 -> x2, Pallas kernels: 2.23 us -> 6.38 us  [the longest x1 4.85 us: prepare(): pl.pallas_call(functools.partial(prepare_kernel, count), out_shape=shapes...]
    ppermute x14, starting transfers between devices: 14.9 us -> 16.3 us  [exchanged(): lax.ppermute(block, axis, [(member, member ^ mask) for member in range(co...]
    ppermute x14, waiting for transfers between devices: 17.9 us -> 17 us  [exchanged(): lax.ppermute(block, axis, [(member, member ^ mask) for member in range(co...]
  transfers between devices with their start and end apart: 14 -> 14, of which waited for: 4 -> 7; matrix products, arithmetic and copies ran while one was open for 0% -> 0% of each run, Pallas kernels for 3% -> 10%
where the time goes in v2:
time: 47.7 us; the launch traced here: 47.6 us
  waiting for transfers between devices  17 us (36%)
  starting transfers between devices  16.3 us (34%)
  Pallas kernels  12.9 us (27%)
  between operations  0.69 us (1%)
  local copies, waits for them, and re-layouts  0.68 us (1%)
    ppermute x14, waiting for transfers between devices, exchanged(): lax.ppermute(block, axis, [(member, member ^ mask) for member in range(co...  17 us
    ppermute x14, starting transfers between devices, exchanged(): lax.ppermute(block, axis, [(member, member ^ mask) for member in range(co...  16.3 us
    pallas_call x1, Pallas kernels, layer(): pl.pallas_call(functools.partial(layer_kernel, chips), out_shape=out_shap...  6.39 us
    pallas_call x1, Pallas kernels, prepare(): pl.pallas_call(functools.partial(prepare_kernel, count), out_shape=shapes...  4.85 us
    pallas_call x1, Pallas kernels, finished(): pl.pallas_call(functools.partial(finish_kernel, len(parts) + 1), out_shap...  1.53 us
  transfers between devices with their start and end apart: 14, of which 7 were waited for; matrix products, arithmetic and copies ran while one was open for 0% of the time, Pallas kernels for 10%

profile of v2, /device:TPU:0, one launch (start us, length us, event | category | flops | bytes accessed | tf_op | source)
XLA Modules:
  0.0 47.6 jit_solution(9035640371942436094)
XLA Ops:
  0.6 3.1 %collective-permute-start.1 = (bf16[32,2048]{1,0:T(8,128)(2,1)}, bf16[32,2048]{1,0:T(8,128)(2,1)S(1)}, u32[]{:S(2)}, u32[]{:S(2)}) collective-permute-start(bf16[32,2048]{1,0:T(8,128)(2,1)} %refs_6_.1), channel_id=1, source_target_pairs={{0,2},{1,3},{2,0},{3,1},{4,6},{5,7},{6,4},{7,5},{8,10},{9,11},{10,... | collective-permute-start | bytes 393224 | tf_op jit(solution)/shard_map/ppermute | solution.py:234
  3.7 2.6 %collective-permute-start.3 = (bf16[32,2048]{1,0:T(8,128)(2,1)}, bf16[32,2048]{1,0:T(8,128)(2,1)S(1)}, u32[]{:S(2)}, u32[]{:S(2)}) collective-permute-start(bf16[32,2048]{1,0:T(8,128)(2,1)} %refs_6_.1), channel_id=1, source_target_pairs={{0,4},{1,5},{2,6},{3,7},{4,0},{5,1},{6,2},{7,3},{8,12},{9,13},{10,... | collective-permute-start | bytes 393224 | tf_op jit(solution)/shard_map/ppermute | solution.py:234
  6.3 0.0 collective-permute-start.5
  6.3 0.0 collective-permute-start
  6.3 0.7 %copy-done = s32[1,256]{1,0:T(1,128)S(1)} copy-done((s32[1,256]{1,0:T(1,128)S(1)}, s32[1,256]{1,0:T(1,128)}, u32[]{:S(2)}) %copy-start) | copy-done | bytes 1048
  7.0 4.9 %prepare.1 = (bf16[2048,768]{1,0:T(8,128)(2,1)S(1)}, bf16[256,2048]{1,0:T(8,128)(2,1)S(1)}, bf16[2048,1024]{1,0:T(8,128)(2,1)S(1)}, bf16[1024,2048]{1,0:T(8,128)...) custom-call(s32[1,256]{1,0:T(1,128)S(1)} %copy-done, ...), custom_call_target="tpu_custom_call" | custom-call | bytes 12730368 | tf_op jit(solution)/shard_map/prepare/pallas_call | solution.py:282
  11.9 0.0 collective-permute-done.1.refs_2_
  11.9 5.0 %collective-permute-done.3.refs_4_ = bf16[32,2048]{1,0:T(8,128)(2,1)S(1)} collective-permute-done((bf16[32,2048]{1,0:T(8,128)(2,1)}, bf16[32,2048]{1,0:T(8,128)(2,1)S(1)}, u32[]{:S(2)}, u32[]{:S(2)}) %collective-permute-start.3) | collective-permute-done | bytes 131104 | tf_op jit(solution)/shard_map/ppermute | solution.py:234
  16.9 0.0 collective-permute-done.5.refs_6_
  16.9 0.0 collective-permute-start.6
  16.9 0.5 %collective-permute-start.4 = (bf16[32,2048]{1,0:T(8,128)(2,1)S(1)}, bf16[32,2048]{1,0:T(8,128)(2,1)S(1)}, u32[]{:S(2)}, u32[]{:S(2)}) collective-permute-start(bf16[32,2048]{1,0:T(8,128)(2,1)S(1)} %collective-permute-done.3.refs_4_), channel_id=1, source_target_pairs={{0,1},{1,0},{2,3},{3,2},{4,5},{5,4},{6,7},{7,6},{8,9},{9,8},{10,11... | collective-permute-start | bytes 393224 | tf_op jit(solution)/shard_map/ppermute | solution.py:234
  17.4 0.0 collective-permute-start.2
  17.4 0.0 collective-permute-done.refs_1_
  17.4 0.8 %collective-permute-done.6.refs_7_ = bf16[32,2048]{1,0:T(8,128)(2,1)S(1)} collective-permute-done((bf16[32,2048]{1,0:T(8,128)(2,1)S(1)}, bf16[32,2048]{1,0:T(8,128)(2,1)S(1)}, u32[]{:S(2)}, u32[]{:S(2)}) %collective-permute-start.6) | collective-permute-done | bytes 131104 | tf_op jit(solution)/shard_map/ppermute | solution.py:234
  18.2 0.2 collective-permute-done.4.refs_5_
  18.4 0.3 collective-permute-done.2.refs_3_
  18.7 6.4 %layer.1 = (bf16[4,32,2048]{2,1,0:T(8,128)(2,1)S(1)}, f32[4,32,2048]{2,1,0:T(8,128)S(1)}, bf16[8,16,512]{2,1,0:T(8,128)(2,1)S(1)}, bf16[8,16,512]{2,1,0:T(8,128)...) custom-call(bf16[32,2048]{1,0:T(8,128)(2,1)S(1)} %get-tuple-element.36.refs_0_.hidden_ref, ...), custom_call_target="tpu_custom_call" | custom-call | flops 3221225472 | bytes 16777216 | tf_op jit(solution)/shard_map/layer/pallas_call | solution.py:435
  25.1 0.3 collective-permute-start.7
  25.4 1.7 %collective-permute-done.7.sibling_ref = bf16[4,32,2048]{2,1,0:T(8,128)(2,1)S(1)} collective-permute-done((bf16[4,32,2048]{2,1,0:T(8,128)(2,1)S(1)}, bf16[4,32,2048]{2,1,0:T(8,128)(2,1)S(1)}, u32[]{:S(2)}, u32[]{:S(2)}) %collective-permute-start.7) | collective-permute-done | bytes 524320 | tf_op jit(solution)/shard_map/ppermute | solution.py:234
  27.1 0.1 reduced.1
  27.2 3.0 %collective-permute-start.8 = (bf16[32,2048]{1,0:T(8,128)(2,1)S(1)}, bf16[32,2048]{1,0:T(8,128)(2,1)S(1)}, u32[]{:S(2)}, u32[]{:S(2)}) collective-permute-start(bf16[32,2048]{1,0:T(8,128)(2,1)S(1)} %get-tuple-element.63), channel_id=1, source_target_pairs={{0,4},{1,5},{2,6},{3,7},{4,0},{5,1},{6,2},{7,3},{8,12},{9,13},{10,... | collective-permute-start | bytes 393224 | tf_op jit(solution)/shard_map/ppermute | solution.py:234
  30.2 1.4 %collective-permute-start.9 = (bf16[32,2048]{1,0:T(8,128)(2,1)S(1)}, bf16[32,2048]{1,0:T(8,128)(2,1)S(1)}, u32[]{:S(2)}, u32[]{:S(2)}) collective-permute-start(bf16[32,2048]{1,0:T(8,128)(2,1)S(1)} %get-tuple-element.64), channel_id=1, source_target_pairs={{0,6},{1,7},{2,4},{3,5},{4,2},{5,3},{6,0},{7,1},{8,14},{9,15},{10,... | collective-permute-start | bytes 393224 | tf_op jit(solution)/shard_map/ppermute | solution.py:234
  31.6 0.0 collective-permute-start.10
  31.6 1.5 %collective-permute-start.11 = (bf16[8,16,512]{2,1,0:T(8,128)(2,1)S(1)}, bf16[8,16,512]{2,1,0:T(8,128)(2,1)S(1)}, u32[]{:S(2)}, u32[]{:S(2)}) collective-permute-start(bf16[8,16,512]{2,1,0:T(8,128)(2,1)S(1)} %get-tuple-element.67), channel_id=1, source_target_pairs={{0,8},{8,0},{16,24},{24,16},{1,9},{9,1},{17,25},{25,17},{2,10},{10... | collective-permute-start | bytes 393224 | tf_op jit(solution)/shard_map/ppermute | solution.py:234
  33.1 1.5 %collective-permute-start.12 = (bf16[8,16,512]{2,1,0:T(8,128)(2,1)S(1)}, bf16[8,16,512]{2,1,0:T(8,128)(2,1)S(1)}, u32[]{:S(2)}, u32[]{:S(2)}) collective-permute-start(bf16[8,16,512]{2,1,0:T(8,128)(2,1)S(1)} %get-tuple-element.68), channel_id=1, source_target_pairs={{0,16},{8,24},{16,0},{24,8},{1,17},{9,25},{17,1},{25,9},{2,18},{10... | collective-permute-start | bytes 393224 | tf_op jit(solution)/shard_map/ppermute | solution.py:234
  34.6 5.5 %collective-permute-done.8.refs_0_ = bf16[32,2048]{1,0:T(8,128)(2,1)S(1)} collective-permute-done((bf16[32,2048]{1,0:T(8,128)(2,1)S(1)}, bf16[32,2048]{1,0:T(8,128)(2,1)S(1)}, u32[]{:S(2)}, u32[]{:S(2)}) %collective-permute-start.8) | collective-permute-done | bytes 131104 | tf_op jit(solution)/shard_map/ppermute | solution.py:234
  40.2 2.5 %collective-permute-start.13 = (bf16[8,16,512]{2,1,0:T(8,128)(2,1)S(1)}, bf16[8,16,512]{2,1,0:T(8,128)(2,1)S(1)}, u32[]{:S(2)}, u32[]{:S(2)}) collective-permute-start(bf16[8,16,512]{2,1,0:T(8,128)(2,1)S(1)} %get-tuple-element.69), channel_id=1, source_target_pairs={{0,24},{8,16},{16,8},{24,0},{1,25},{9,17},{17,9},{25,1},{2,26},{10... | collective-permute-start | bytes 393224 | tf_op jit(solution)/shard_map/ppermute | solution.py:234
  42.6 0.0 collective-permute-done.9.refs_1_
  42.6 0.0 collective-permute-done.10.refs_2_
  42.6 0.0 collective-permute-done.12.refs_5_
  42.7 3.4 %collective-permute-done.13.refs_6_ = bf16[8,16,512]{2,1,0:T(8,128)(2,1)S(1)} collective-permute-done((bf16[8,16,512]{2,1,0:T(8,128)(2,1)S(1)}, bf16[8,16,512]{2,1,0:T(8,128)(2,1)S(1)}, u32[]{:S(2)}, u32[]{:S(2)}) %collective-permute-start.13) | collective-permute-done | bytes 131104 | tf_op jit(solution)/shard_map/ppermute | solution.py:234
  46.0 1.5 %finished.1 = (f32[32,2048]{1,0:T(8,128)}, bf16[1,4,8,16,512]{4,3,2,1,0:T(8,128)(2,1)}) custom-call(f32[32,2048]{1,0:T(8,128)S(1)} %get-tuple-element.55.base_ref, bf16[32,2048]{1,0:T(8,128)(2,1)S(1)} %collective-permute-done.8.refs_0_, bf16[32,2048]{1,0:T(8,128)(2,1)S(1)} %collective-permute-done.9.refs_1_, ...), custom_call_target="tpu_custom_call" | custom-call | tf_op jit(solution)/shard_map/finished/pallas_call | solution.py:507
  (2 shorter events, 0.0 us)
Async XLA Ops:
  0.6 11.2 %collective-permute-start.1 = (bf16[32,2048]{1,0:T(8,128)(2,1)}, bf16[32,2048]{1,0:T(8,128)(2,1)S(1)}, u32[]{:S(2)}, u32[]{:S(2)}) collective-permute-start(bf16[32,2048]{1,0:T(8,128)(2,1)} %refs_6_.1), channel_id=1, source_target_pairs={{0,2},{1,3},{2,0},{3,1},{4,6},{5,7},{6,4},{7,5},{8,10},{9,11},{10,... | collective-permute-start | bytes 393224 | tf_op jit(solution)/shard_map/ppermute | solution.py:234
  3.7 13.2 %collective-permute-start.3 = (bf16[32,2048]{1,0:T(8,128)(2,1)}, bf16[32,2048]{1,0:T(8,128)(2,1)S(1)}, u32[]{:S(2)}, u32[]{:S(2)}) collective-permute-start(bf16[32,2048]{1,0:T(8,128)(2,1)} %refs_6_.1), channel_id=1, source_target_pairs={{0,4},{1,5},{2,6},{3,7},{4,0},{5,1},{6,2},{7,3},{8,12},{9,13},{10,... | collective-permute-start | bytes 393224 | tf_op jit(solution)/shard_map/ppermute | solution.py:234
  6.3 10.6 %collective-permute-start.5 = (bf16[32,2048]{1,0:T(8,128)(2,1)}, bf16[32,2048]{1,0:T(8,128)(2,1)S(1)}, u32[]{:S(2)}, u32[]{:S(2)}) collective-permute-start(bf16[32,2048]{1,0:T(8,128)(2,1)} %refs_6_.1), channel_id=1, source_target_pairs={{0,6},{1,7},{2,4},{3,5},{4,2},{5,3},{6,0},{7,1},{8,14},{9,15},{10,... | collective-permute-start | bytes 393224 | tf_op jit(solution)/shard_map/ppermute | solution.py:234
  6.3 11.1 %collective-permute-start = (bf16[32,2048]{1,0:T(8,128)(2,1)}, bf16[32,2048]{1,0:T(8,128)(2,1)S(1)}, u32[]{:S(2)}, u32[]{:S(2)}) collective-permute-start(bf16[32,2048]{1,0:T(8,128)(2,1)} %refs_6_.1), channel_id=1, source_target_pairs={{0,1},{1,0},{2,3},{3,2},{4,5},{5,4},{6,7},{7,6},{8,9},{9,8},{10,11... | collective-permute-start | bytes 393224 | tf_op jit(solution)/shard_map/ppermute | solution.py:234
  6.3 0.7 %copy-start = (s32[1,256]{1,0:T(1,128)S(1)}, s32[1,256]{1,0:T(1,128)}, u32[]{:S(2)}) copy-start(s32[1,256]{1,0:T(1,128)} %segments_ref.1) | copy-start | bytes 3076
  16.9 1.3 %collective-permute-start.6 = (bf16[32,2048]{1,0:T(8,128)(2,1)S(1)}, bf16[32,2048]{1,0:T(8,128)(2,1)S(1)}, u32[]{:S(2)}, u32[]{:S(2)}) collective-permute-start(bf16[32,2048]{1,0:T(8,128)(2,1)S(1)} %collective-permute-done.5.refs_6_), channel_id=1, source_target_pairs={{0,1},{1,0},{2,3},{3,2},{4,5},{5,4},{6,7},{7,6},{8,9},{9,8},{10,11... | collective-permute-start | bytes 393224 | tf_op jit(solution)/shard_map/ppermute | solution.py:234
  16.9 1.5 %collective-permute-start.4 = (bf16[32,2048]{1,0:T(8,128)(2,1)S(1)}, bf16[32,2048]{1,0:T(8,128)(2,1)S(1)}, u32[]{:S(2)}, u32[]{:S(2)}) collective-permute-start(bf16[32,2048]{1,0:T(8,128)(2,1)S(1)} %collective-permute-done.3.refs_4_), channel_id=1, source_target_pairs={{0,1},{1,0},{2,3},{3,2},{4,5},{5,4},{6,7},{7,6},{8,9},{9,8},{10,11... | collective-permute-start | bytes 393224 | tf_op jit(solution)/shard_map/ppermute | solution.py:234
  17.4 1.3 %collective-permute-start.2 = (bf16[32,2048]{1,0:T(8,128)(2,1)S(1)}, bf16[32,2048]{1,0:T(8,128)(2,1)S(1)}, u32[]{:S(2)}, u32[]{:S(2)}) collective-permute-start(bf16[32,2048]{1,0:T(8,128)(2,1)S(1)} %collective-permute-done.1.refs_2_), channel_id=1, source_target_pairs={{0,1},{1,0},{2,3},{3,2},{4,5},{5,4},{6,7},{7,6},{8,9},{9,8},{10,11... | collective-permute-start | bytes 393224 | tf_op jit(solution)/shard_map/ppermute | solution.py:234
  25.1 2.0 %collective-permute-start.7 = (bf16[4,32,2048]{2,1,0:T(8,128)(2,1)S(1)}, bf16[4,32,2048]{2,1,0:T(8,128)(2,1)S(1)}, u32[]{:S(2)}, u32[]{:S(2)}) collective-permute-start(bf16[4,32,2048]{2,1,0:T(8,128)(2,1)S(1)} %get-tuple-element.54), channel_id=1, source_target_pairs={{0,1},{1,0},{2,3},{3,2},{4,5},{5,4},{6,7},{7,6},{8,9},{9,8},{10,11... | collective-permute-start | bytes 1572872 | tf_op jit(solution)/shard_map/ppermute | solution.py:234
  27.2 13.0 %collective-permute-start.8 = (bf16[32,2048]{1,0:T(8,128)(2,1)S(1)}, bf16[32,2048]{1,0:T(8,128)(2,1)S(1)}, u32[]{:S(2)}, u32[]{:S(2)}) collective-permute-start(bf16[32,2048]{1,0:T(8,128)(2,1)S(1)} %get-tuple-element.63), channel_id=1, source_target_pairs={{0,4},{1,5},{2,6},{3,7},{4,0},{5,1},{6,2},{7,3},{8,12},{9,13},{10,... | collective-permute-start | bytes 393224 | tf_op jit(solution)/shard_map/ppermute | solution.py:234
  30.2 12.4 %collective-permute-start.9 = (bf16[32,2048]{1,0:T(8,128)(2,1)S(1)}, bf16[32,2048]{1,0:T(8,128)(2,1)S(1)}, u32[]{:S(2)}, u32[]{:S(2)}) collective-permute-start(bf16[32,2048]{1,0:T(8,128)(2,1)S(1)} %get-tuple-element.64), channel_id=1, source_target_pairs={{0,6},{1,7},{2,4},{3,5},{4,2},{5,3},{6,0},{7,1},{8,14},{9,15},{10,... | collective-permute-start | bytes 393224 | tf_op jit(solution)/shard_map/ppermute | solution.py:234
  31.6 11.0 %collective-permute-start.10 = (bf16[32,2048]{1,0:T(8,128)(2,1)S(1)}, bf16[32,2048]{1,0:T(8,128)(2,1)S(1)}, u32[]{:S(2)}, u32[]{:S(2)}) collective-permute-start(bf16[32,2048]{1,0:T(8,128)(2,1)S(1)} %get-tuple-element.65), channel_id=1, source_target_pairs={{0,2},{1,3},{2,0},{3,1},{4,6},{5,7},{6,4},{7,5},{8,10},{9,11},{10,... | collective-permute-start | bytes 393224 | tf_op jit(solution)/shard_map/ppermute | solution.py:234
  31.6 11.0 %collective-permute-start.11 = (bf16[8,16,512]{2,1,0:T(8,128)(2,1)S(1)}, bf16[8,16,512]{2,1,0:T(8,128)(2,1)S(1)}, u32[]{:S(2)}, u32[]{:S(2)}) collective-permute-start(bf16[8,16,512]{2,1,0:T(8,128)(2,1)S(1)} %get-tuple-element.67), channel_id=1, source_target_pairs={{0,8},{8,0},{16,24},{24,16},{1,9},{9,1},{17,25},{25,17},{2,10},{10... | collective-permute-start | bytes 393224 | tf_op jit(solution)/shard_map/ppermute | solution.py:234
  33.1 9.6 %collective-permute-start.12 = (bf16[8,16,512]{2,1,0:T(8,128)(2,1)S(1)}, bf16[8,16,512]{2,1,0:T(8,128)(2,1)S(1)}, u32[]{:S(2)}, u32[]{:S(2)}) collective-permute-start(bf16[8,16,512]{2,1,0:T(8,128)(2,1)S(1)} %get-tuple-element.68), channel_id=1, source_target_pairs={{0,16},{8,24},{16,0},{24,8},{1,17},{9,25},{17,1},{25,9},{2,18},{10... | collective-permute-start | bytes 393224 | tf_op jit(solution)/shard_map/ppermute | solution.py:234
  40.2 5.9 %collective-permute-start.13 = (bf16[8,16,512]{2,1,0:T(8,128)(2,1)S(1)}, bf16[8,16,512]{2,1,0:T(8,128)(2,1)S(1)}, u32[]{:S(2)}, u32[]{:S(2)}) collective-permute-start(bf16[8,16,512]{2,1,0:T(8,128)(2,1)S(1)} %get-tuple-element.69), channel_id=1, source_target_pairs={{0,24},{8,16},{16,8},{24,0},{1,25},{9,17},{17,9},{25,1},{2,26},{10... | collective-permute-start | bytes 393224 | tf_op jit(solution)/shard_map/ppermute | solution.py:234

commit v3 on v0

--- a/solution.py
+++ b/solution.py
@@ -1,8 +1,11 @@
+import functools
 import math
 
 import jax
 import jax.numpy as jnp
 from jax import lax
+from jax.experimental import pallas as pl
+from jax.experimental.pallas import tpu as pltpu
 from jax.sharding import PartitionSpec as P
 
 H = 8
@@ -71,7 +74,7 @@
     return rotated.astype(jnp.bfloat16)
 
 
-def shards(
+def shards_split_heads(
     hidden_states,
     attention_gain,
     feedforward_gain,
@@ -218,7 +221,547 @@
     return (layer_output, cache_pages)
 
 
+CORES = 2
+CHIPS = 4
+MIB = 1 << 20
+
+
+def in_hbm(array):
+    return pltpu.with_memory_space_constraint(array, pltpu.HBM)
+
+
+def exchanged(block, axis, mask):
+    count = lax.axis_size(axis)
+    return lax.ppermute(block, axis, [(member, member ^ mask) for member in range(count)])
+
+
+def vmem_specs(count):
+    return [pl.BlockSpec(memory_space=pltpu.VMEM)] * count
+
+
+def parameters(mebibytes):
+    return pltpu.CompilerParams(vmem_limit_bytes=mebibytes * MIB)
+
+
+def whereabouts():
+    member = lax.axis_index("tensor")
+    return member // CORES, member % CORES
+
+
+def position_of(kind, half, block_rows):
+    chip, core = whereabouts()
+    return ((chip ^ kind) * CORES + (core ^ half)) * block_rows
+
+
+def positions_along(first, shape, axis, block_rows):
+    chip, core = whereabouts()
+    bits = block_rows.bit_length() - 1
+    place = first + lax.broadcasted_iota(jnp.int32, shape, axis)
+    kind = place >> (bits + 1)
+    half = (place >> bits) & 1
+    return ((((chip ^ kind) << 1) | (core ^ half)) << bits) | (place & (block_rows - 1))
+
+
+def normalize(blocks, gain_refs, normed_refs):
+    piece = 16
+    gains = [gain_ref[...] for gain_ref in gain_refs]
+    for number, block_ref in enumerate(blocks):
+        block_rows = block_ref.shape[0]
+        for part in range(0, block_rows, piece):
+            floats = block_ref[part : part + piece, :].astype(jnp.float32)
+            center = jnp.mean(floats, axis=-1, keepdims=True)
+            shifted = floats - center
+            spread = jnp.mean(shifted * shifted, axis=-1, keepdims=True)
+            scaled = shifted * lax.rsqrt(spread + epsilon)
+            first = number * block_rows + part
+            for gain, normed_ref in zip(gains, normed_refs):
+                normed_ref[first : first + piece, :] = (scaled * gain).astype(jnp.bfloat16)
+
+
+def project(normed_ref, heads_ref, table_refs, places, joined_ref, first):
+    rows = normed_ref.shape[0]
+    block_rows = rows // len(places)
+    for component in range(3):
+        columns = slice(component * HD, (component + 1) * HD)
+        joined = jnp.dot(
+            normed_ref[...], heads_ref[:, columns], preferred_element_type=jnp.float32
+        ).astype(jnp.bfloat16)
+        joined_ref[first : first + rows, columns] = joined
+        if component < 2:
+            cosine, sine_down, sine_up = [
+                jnp.concatenate(
+                    [
+                        table_ref[pl.ds(pl.multiple_of(place, block_rows), block_rows), :]
+                        for place in places
+                    ],
+                    0,
+                )
+                for table_ref in table_refs
+            ]
+            turning = joined[:, :128].astype(jnp.float32)
+            turned = (
+                turning * cosine
+                + pltpu.roll(turning, 128 - ROT // 2, 1) * sine_down
+                + pltpu.roll(turning, ROT // 2, 1) * sine_up
+            )
+            joined_ref[first : first + rows, component * HD : component * HD + 128] = turned.astype(
+                jnp.bfloat16
+            )
+
+
+def hide(normed_ref, upward_ref, hidden_ref):
+    chunk = 256
+    for first in range(0, upward_ref.shape[1], chunk):
+        columns = slice(first, first + chunk)
+        upward = jnp.dot(
+            normed_ref[...], upward_ref[:, columns], preferred_element_type=jnp.float32
+        )
+        hidden = 0.5 * upward * (1.0 + lax.erf(upward * (0.5**0.5)))
+        hidden_ref[:, columns] = hidden.astype(jnp.bfloat16)
+
+
+def attend(joined_ref, offsets_ref, first, rows, block_rows):
+    tokens = joined_ref.shape[0]
+    starts = [
+        position_of(place // (2 * block_rows), (place // block_rows) % 2, block_rows)
+        for place in range(first, first + rows, block_rows)
+    ]
+    reach = jnp.concatenate(
+        [
+            offsets_ref[pl.ds(pl.multiple_of(start, block_rows), block_rows), :]
+            for start in starts
+        ],
+        0,
+    )[:, :1].astype(jnp.int32)
+    row = positions_along(first, (rows, 1), 0, block_rows)
+    column = positions_along(0, (1, tokens), 1, block_rows)
+    allowed = (column <= row) & (column >= row - reach)
+    scores = lax.dot_general(
+        joined_ref[first : first + rows, :HD],
+        joined_ref[:, HD : 2 * HD],
+        (((1,), (1,)), ((), ())),
+        preferred_element_type=jnp.float32,
+    ) * (HD ** (-0.5))
+    peak = jnp.max(jnp.where(allowed, scores, -jnp.inf), axis=1, keepdims=True)
+    weights = jnp.where(allowed, jnp.exp(scores - peak), 0.0)
+    weight_sum = jnp.sum(weights, axis=1, keepdims=True)
+    mixed = jnp.dot(
+        weights.astype(jnp.bfloat16), joined_ref[:, 2 * HD :], preferred_element_type=jnp.float32
+    )
+    return (mixed / weight_sum).astype(jnp.bfloat16)
+
+
+def make_tables(segments_ref, offsets_ref, cosine_ref, sine_down_ref, sine_up_ref):
+    tokens = segments_ref.shape[1]
+    shape = (tokens, tokens)
+    rows = lax.broadcasted_iota(jnp.int32, shape, 0)
+    columns = lax.broadcasted_iota(jnp.int32, shape, 1)
+    across = jnp.broadcast_to(segments_ref[...], shape).astype(jnp.float32)
+    down = jnp.sum(jnp.where(rows == columns, across, 0.0), axis=1, keepdims=True)
+    earlier = (across == down) & (columns < rows)
+    offsets = jnp.sum(jnp.where(earlier, 1.0, 0.0), axis=1, keepdims=True)
+    offsets_ref[...] = jnp.broadcast_to(offsets, offsets_ref.shape)
+    half = ROT // 2
+    lane = lax.broadcasted_iota(jnp.int32, (tokens, 128), 1)
+    step = (lane & (half - 1)).astype(jnp.float32)
+    frequency = jnp.exp(step * (-2.0 * math.log(rotary_base) / ROT))
+    angles = offsets * frequency
+    sine = jnp.sin(angles)
+    cosine_ref[...] = jnp.where(lane < ROT, jnp.cos(angles), 1.0)
+    sine_down_ref[...] = jnp.where(lane < half, -sine, 0.0)
+    sine_up_ref[...] = jnp.where((lane >= half) & (lane < ROT), sine, 0.0)
+
+
+def own_kernel(count, segments_ref, beside_ref, *refs):
+    sources, targets = refs[:count], refs[count : 2 * count]
+    offsets_ref, *table_refs, joined_ref, fed_ref = refs[2 * count : 2 * count + 6]
+    attention_scr, feedforward_scr, hidden_scr, sems = refs[2 * count + 6 :]
+    copies = []
+    for number, (source, target) in enumerate(zip(sources, targets)):
+        parts = 4 if source.shape[0] >= 256 else 1
+        rows = source.shape[0] // parts
+        places = [pl.ds(part * rows, rows) for part in range(parts)]
+        copies.append(
+            [
+                pltpu.make_async_copy(source.at[place], target.at[place], sems.at[number, part])
+                for part, place in enumerate(places)
+            ]
+        )
+    for copy in sum(copies, []):
+        copy.start()
+
+    def wait_for(*numbers):
+        for number in numbers:
+            for copy in copies[number]:
+                copy.wait()
+
+    hidden_ref, *gain_refs, heads_ref, upward_ref, downward_ref, _ = targets
+    block_rows = hidden_ref.shape[0]
+    make_tables(segments_ref, offsets_ref, *table_refs)
+    wait_for(0, 1, 2)
+    normalize([hidden_ref, beside_ref], gain_refs, [attention_scr, feedforward_scr])
+    wait_for(3)
+    places = [position_of(0, half, block_rows) for half in range(CORES)]
+    project(attention_scr, heads_ref, table_refs, places, joined_ref, 0)
+    wait_for(4)
+    hide(feedforward_scr, upward_ref, hidden_scr)
+    wait_for(5)
+    fed_ref[...] = jnp.dot(
+        hidden_scr[...], downward_ref[...], preferred_element_type=jnp.float32
+    )
+    wait_for(6)
+
+
+def own_rows(segments, beside, staged):
+    tokens = segments.shape[1]
+    block_rows, width = beside.shape
+    rows = CORES * block_rows
+    hidden_width = staged[4].shape[1]
+    shapes = [pltpu.VMEM(array.shape, array.dtype) for array in staged]
+    shapes += [pltpu.VMEM((tokens, 128), jnp.float32)] * 4
+    shapes += [pltpu.VMEM((rows, 3 * HD), jnp.bfloat16), pltpu.VMEM((rows, width), jnp.float32)]
+    count = len(staged)
+    return pl.pallas_call(
+        functools.partial(own_kernel, count),
+        out_shape=shapes,
+        in_specs=vmem_specs(2) + [pl.BlockSpec(memory_space=pltpu.HBM)] * count,
+        out_specs=vmem_specs(len(shapes)),
+        scratch_shapes=[
+            pltpu.VMEM((rows, width), jnp.bfloat16),
+            pltpu.VMEM((rows, width), jnp.bfloat16),
+            pltpu.VMEM((rows, hidden_width), jnp.bfloat16),
+            pltpu.SemaphoreType.DMA((count, 4)),
+        ],
+        compiler_params=parameters(12),
+        cost_estimate=pl.CostEstimate(
+            flops=2 * rows * width * (3 * HD + 2 * hidden_width),
+            bytes_accessed=sum(array.nbytes for array in staged),
+            transcendentals=rows * hidden_width,
+        ),
+        name="own_rows",
+    )(segments, beside, *[in_hbm(array) for array in staged])
+
+
+def middle_kernel(*refs):
+    blocks, (gain_a, gain_f, heads_ref, upward_ref, downward_ref) = refs[:4], refs[4:9]
+    table_refs = refs[9:12]
+    joined_ref, fed_ref, attention_scr, feedforward_scr, hidden_scr = refs[12:]
+    block_rows = blocks[0].shape[0]
+    normalize(blocks, [gain_a, gain_f], [attention_scr, feedforward_scr])
+    places = [position_of(kind, half, block_rows) for kind in (1, 2) for half in range(CORES)]
+    project(attention_scr, heads_ref, table_refs, places, joined_ref, 0)
+    hide(feedforward_scr, upward_ref, hidden_scr)
+    chunk = 512
+    for first in range(0, downward_ref.shape[1], chunk):
+        columns = slice(first, first + chunk)
+        fed_ref[:, columns] = jnp.dot(
+            hidden_scr[...], downward_ref[:, columns], preferred_element_type=jnp.float32
+        )
+
+
+def middle_rows(blocks, gains, weights, tables):
+    block_rows, width = blocks[0].shape
+    rows = len(blocks) * block_rows
+    hidden_width = weights[1].shape[1]
+    return pl.pallas_call(
+        middle_kernel,
+        out_shape=[
+            pltpu.VMEM((rows, 3 * HD), jnp.bfloat16),
+            pltpu.VMEM((rows, width), jnp.float32),
+        ],
+        in_specs=vmem_specs(len(blocks) + 2 + 3 + 3),
+        out_specs=vmem_specs(2),
+        scratch_shapes=[
+            pltpu.VMEM((rows, width), jnp.bfloat16),
+            pltpu.VMEM((rows, width), jnp.bfloat16),
+            pltpu.VMEM((rows, hidden_width), jnp.bfloat16),
+        ],
+        compiler_params=parameters(12),
+        cost_estimate=pl.CostEstimate(
+            flops=2 * rows * width * (3 * HD + 2 * hidden_width),
+            bytes_accessed=MIB,
+            transcendentals=rows * hidden_width,
+        ),
+        name="middle_rows",
+    )(*blocks, *gains, *weights, *tables)
+
+
+def last_kernel(*refs):
+    blocks, (gain_a, gain_f, heads_ref, upward_ref, downward_ref, output_ref) = refs[:2], refs[2:8]
+    offsets_ref, *table_refs = refs[8:12]
+    joined_own_ref, joined_middle_ref = refs[12:14]
+    joined_ref, sibling_ref, own_ref, attention_scr, feedforward_scr, hidden_scr = refs[14:]
+    block_rows = blocks[0].shape[0]
+    tokens = joined_ref.shape[0]
+    first = tokens - CORES * block_rows
+    normalize(blocks, [gain_a, gain_f], [attention_scr, feedforward_scr])
+    own_count = joined_own_ref.shape[0]
+    joined_ref[:own_count, :] = joined_own_ref[...]
+    joined_ref[own_count:first, :] = joined_middle_ref[...]
+    places = [position_of(CHIPS - 1, half, block_rows) for half in range(CORES)]
+    project(attention_scr, heads_ref, table_refs, places, joined_ref, first)
+    hide(feedforward_scr, upward_ref, hidden_scr)
+    attended = attend(joined_ref, offsets_ref, first, CORES * block_rows, block_rows)
+    chunk = 512
+    for begin in range(0, downward_ref.shape[1], chunk):
+        columns = slice(begin, begin + chunk)
+        partial = jnp.dot(
+            hidden_scr[...], downward_ref[:, columns], preferred_element_type=jnp.float32
+        ) + jnp.dot(attended, output_ref[:, columns], preferred_element_type=jnp.float32)
+        own_ref[:, columns] = partial[:block_rows]
+        sibling_ref[:, columns] = partial[block_rows:].astype(jnp.bfloat16)
+
+
+def last_rows(blocks, gains, weights, tables, joined_own, joined_middle):
+    block_rows, width = blocks[0].shape
+    rows = len(blocks) * block_rows
+    hidden_width = weights[1].shape[1]
+    tokens = joined_own.shape[0] + joined_middle.shape[0] + rows
+    return pl.pallas_call(
+        last_kernel,
+        out_shape=[
+            pltpu.VMEM((tokens, 3 * HD), jnp.bfloat16),
+            pltpu.VMEM((block_rows, width), jnp.bfloat16),
+            pltpu.VMEM((block_rows, width), jnp.float32),
+        ],
+        in_specs=vmem_specs(len(blocks) + 2 + 4 + 4 + 2),
+        out_specs=vmem_specs(3),
+        scratch_shapes=[
+            pltpu.VMEM((rows, width), jnp.bfloat16),
+            pltpu.VMEM((rows, width), jnp.bfloat16),
+            pltpu.VMEM((rows, hidden_width), jnp.bfloat16),
+        ],
+        compiler_params=parameters(12),
+        cost_estimate=pl.CostEstimate(
+            flops=2 * rows * width * (3 * HD + HD + 2 * hidden_width),
+            bytes_accessed=MIB,
+            transcendentals=rows * hidden_width,
+        ),
+        name="last_rows",
+    )(*blocks, *gains, *weights, *tables, joined_own, joined_middle)
+
+
+def tail_kernel(block_rows, joined_ref, offsets_ref, output_ref, fed_own_ref, fed_middle_ref, *refs):
+    targets_ref, *sibling_refs = refs[:4]
+    own_refs = refs[4:7]
+    pages_refs, (named_ref, counts_ref, slots_ref, sem) = refs[7:-4], refs[-4:]
+    naming = pltpu.make_async_copy(targets_ref, named_ref, sem)
+    naming.start()
+    tokens = joined_ref.shape[0]
+    kind_rows = CORES * block_rows
+    rows = tokens - kind_rows
+    attended = attend(joined_ref, offsets_ref, 0, rows, block_rows)
+    chunk = 512
+    for begin in range(0, output_ref.shape[1], chunk):
+        columns = slice(begin, begin + chunk)
+        product = jnp.dot(attended, output_ref[:, columns], preferred_element_type=jnp.float32)
+        near = product[:kind_rows] + fed_own_ref[:, columns]
+        middle = product[kind_rows:] + fed_middle_ref[:, columns]
+        for kind, partial in enumerate((near, middle[:kind_rows], middle[kind_rows:])):
+            own_refs[kind][:, columns] = partial[:block_rows]
+            sibling_refs[kind][:, columns] = partial[block_rows:].astype(jnp.bfloat16)
+
+    chip, core = whereabouts()
+    group = lax.axis_index("dp")
+    naming.wait()
+    for target in range(len(pages_refs)):
+        counts_ref[target] = 0
+    for page in range(tokens // PAGE):
+        target = named_ref[page]
+        slot = counts_ref[target]
+        counts_ref[target] = slot + 1
+        slots_ref[page] = slot
+    for page_ref in pages_refs:
+        page_ref[...] = jnp.zeros(page_ref.shape, page_ref.dtype)
+    capacity = pages_refs[0].shape[0]
+    for place in range(0, tokens, PAGE):
+        kind, half = place // kind_rows, (place // block_rows) % CORES
+        start = ((chip ^ kind) * CORES + (core ^ half)) * block_rows + place % block_rows
+        page = start // PAGE
+        target = named_ref[page]
+        slot = jnp.minimum(slots_ref[page], capacity - 1)
+        for mask, page_ref in enumerate(pages_refs):
+
+            @pl.when(target == (group ^ mask))
+            def _():
+                page_ref[pl.ds(slot, 1)] = joined_ref[place : place + PAGE, HD:][None]
+
+
+def tail_rows(joined, offsets, output_weight, fed_own, fed_middle, targets, replica_count):
+    tokens = joined.shape[0]
+    width = fed_own.shape[1]
+    block_rows = fed_own.shape[0] // CORES
+    page_count = tokens // PAGE
+    capacity = 2 * page_count // replica_count
+    shapes = [
+        pltpu.VMEM((block_rows, width), dtype) for dtype in [jnp.bfloat16] * 3 + [jnp.float32] * 3
+    ] + [pltpu.VMEM((capacity, PAGE, 2 * HD), jnp.bfloat16)] * replica_count
+    return pl.pallas_call(
+        functools.partial(tail_kernel, block_rows),
+        out_shape=shapes,
+        in_specs=vmem_specs(5) + [pl.BlockSpec(memory_space=pltpu.HBM)],
+        out_specs=vmem_specs(len(shapes)),
+        scratch_shapes=[
+            pltpu.SMEM(targets.shape, jnp.int32),
+            pltpu.SMEM((replica_count,), jnp.int32),
+            pltpu.SMEM((page_count,), jnp.int32),
+            pltpu.SemaphoreType.DMA(()),
+        ],
+        compiler_params=parameters(12),
+        cost_estimate=pl.CostEstimate(
+            flops=2 * tokens * width * HD, bytes_accessed=MIB, transcendentals=tokens * tokens
+        ),
+        name="tail_rows",
+    )(joined, offsets, output_weight, fed_own, fed_middle, in_hbm(targets))
+
+
+def add_kernel(*refs):
+    total = refs[0][...].astype(jnp.float32)
+    for ref in refs[1:-1]:
+        total = total + ref[...].astype(jnp.float32)
+    refs[-1][...] = total.astype(refs[-1].dtype)
+
+
+def added(name, *parts):
+    return pl.pallas_call(
+        add_kernel,
+        out_shape=pltpu.VMEM(parts[0].shape, jnp.bfloat16),
+        in_specs=vmem_specs(len(parts)),
+        out_specs=pl.BlockSpec(memory_space=pltpu.VMEM),
+        compiler_params=parameters(4),
+        name=name,
+    )(*parts)
+
+
+def sums_kernel(passing_ref, *refs):
+    twos, ones, zeros = refs[0:2], refs[2:4], refs[4:7]
+    second_ref, first_ref, base_ref = refs[7:]
+
+    def total(parts):
+        return sum([part[...].astype(jnp.float32) for part in parts[1:]], parts[0][...])
+
+    second_ref[...] = total((twos[1], twos[0], passing_ref)).astype(jnp.bfloat16)
+    first_ref[...] = total((ones[1], ones[0])).astype(jnp.bfloat16)
+    base_ref[...] = total((zeros[1], zeros[0], zeros[2]))
+
+
+def remaining_sums(passing, twos, ones, zeros, hidden):
+    return pl.pallas_call(
+        sums_kernel,
+        out_shape=[
+            pltpu.VMEM(hidden.shape, jnp.bfloat16),
+            pltpu.VMEM(hidden.shape, jnp.bfloat16),
+            pltpu.VMEM(hidden.shape, jnp.float32),
+        ],
+        in_specs=vmem_specs(8),
+        out_specs=vmem_specs(3),
+        compiler_params=parameters(4),
+        name="remaining_sums",
+    )(passing, *twos, *ones, *zeros, hidden)
+
+
+def finish_kernel(part_count, base_ref, *refs):
+    group = lax.axis_index("dp")
+    parts, pages = refs[:part_count], refs[part_count:-3]
+    output_ref, cache_ref, sems = refs[-3:]
+    copies = [
+        pltpu.make_async_copy(page_ref, cache_ref.at[0, group ^ mask], sems.at[mask])
+        for mask, page_ref in enumerate(pages)
+    ]
+    for copy in copies:
+        copy.start()
+    total = base_ref[...]
+    for part_ref in parts:
+        total = total + part_ref[...].astype(jnp.float32)
+    output_ref[...] = total
+    for copy in copies:
+        copy.wait()
+
+
+def finished(base, parts, pages):
+    count = len(pages)
+    return pl.pallas_call(
+        functools.partial(finish_kernel, len(parts)),
+        out_shape=[
+            jax.ShapeDtypeStruct(base.shape, base.dtype),
+            jax.ShapeDtypeStruct((1, count) + pages[0].shape, pages[0].dtype),
+        ],
+        in_specs=vmem_specs(1 + len(parts)) + [pl.BlockSpec(memory_space=pl.ANY)] * count,
+        out_specs=vmem_specs(1) + [pl.BlockSpec(memory_space=pltpu.HBM)],
+        scratch_shapes=[pltpu.SemaphoreType.DMA((count,))],
+        compiler_params=parameters(4),
+        name="finished",
+    )(base, *parts, *pages)
+
+
+def shards_whole_heads(
+    hidden_states,
+    attention_gain,
+    feedforward_gain,
+    heads_weight,
+    output_weight,
+    upward_weight,
+    downward_weight,
+    segments,
+    page_targets,
+):
+    replica_count = lax.axis_size("dp")
+    to_chip = [mask * CORES for mask in range(CHIPS)]
+    second = exchanged(hidden_states, "tensor", to_chip[2])
+    first = exchanged(hidden_states, "tensor", to_chip[1])
+    beside = exchanged(hidden_states, "tensor", 1)
+    staged = (
+        hidden_states,
+        attention_gain[None],
+        feedforward_gain[None],
+        heads_weight,
+        upward_weight,
+        downward_weight,
+        output_weight,
+    )
+    hidden, *rest = own_rows(segments, beside, staged)
+    gains, (heads, upward, downward, output), tables = rest[:2], rest[2:6], rest[6:10]
+    joined_own, fed_own = rest[10:]
+
+    second, first, joined_own = lax.optimization_barrier((second, first, joined_own))
+    third = exchanged(second, "tensor", to_chip[1])
+    second_beside = exchanged(second, "tensor", 1)
+    first_beside = exchanged(first, "tensor", 1)
+    third_beside = exchanged(third, "tensor", 1)
+    joined_middle, fed_middle = middle_rows(
+        (first, first_beside, second, second_beside), gains, (heads, upward, downward), tables[1:]
+    )
+    joined, sibling, own = last_rows(
+        (third, third_beside),
+        gains,
+        (heads, upward, downward, output),
+        tables,
+        joined_own,
+        joined_middle,
+    )
+
+    received = exchanged(sibling, "tensor", 1)
+    parts = tail_rows(
+        joined, tables[0], output, fed_own, fed_middle, page_targets[:, 0], replica_count
+    )
+    third_sum = added("third_added", own, received)
+    siblings, owns, pages = parts[:3], parts[3:6], parts[6:]
+    third_sum, siblings = lax.optimization_barrier((third_sum, siblings))
+    passing = exchanged(third_sum, "tensor", to_chip[1])
+    pairs = [(exchanged(siblings[kind], "tensor", 1), owns[kind]) for kind in (2, 1, 0)]
+    second_sum, first_sum, base = remaining_sums(passing, *pairs, hidden)
+    second_sum, first_sum, pages = lax.optimization_barrier((second_sum, first_sum, pages))
+    from_second = exchanged(second_sum, "tensor", to_chip[2])
+    from_first = exchanged(first_sum, "tensor", to_chip[1])
+    arriving = [pages[0]] + [
+        exchanged(pages[mask], "dp", mask) for mask in range(1, replica_count)
+    ]
+    return tuple(finished(base, (from_second, from_first), arriving))
+
+
 def solution(mesh):
+    whole_heads = mesh.shape["tensor"] == H and mesh.shape["dp"] == 4
+    shards = shards_whole_heads if whole_heads else shards_split_heads
     in_specs = (
         P(("dp", "tensor"), None),
         P(),

time: 114 us -> 44.8 us (0.39)
  waiting for transfers between devices: 35.8 us -> 14.6 us
  matrix products: 20.3 us -> 0 us
  between operations: 18.7 us -> 0.72 us
  other arithmetic: 14.8 us -> 0 us
  starting transfers between devices: 0.12 us -> 14.9 us
  Pallas kernels: 0 us -> 13.7 us
  blocking collectives: 12.3 us -> 0 us
  local copies, waits for them, and re-layouts: 11.1 us -> 0.68 us
    all_gather x2 -> x0, waiting for transfers between devices: 23.3 us -> none  [shards(): lax.all_gather((normed_attention, normed_feedforward), 'tensor', axis=0,...]
    dot_general x8 -> x0, matrix products: 20.3 us -> none  [the longest x1 9.65 us: shards(): jnp.dot(hidden_rows, downward_weight, preferred_element_type=jnp.float32)]
    ppermute x0 -> x17, starting transfers between devices: none -> 14.9 us  [exchanged(): lax.ppermute(block, axis, [(member, member ^ mask) for member in range(co...]
    ppermute x0 -> x17, waiting for transfers between devices: none -> 14.6 us  [exchanged(): lax.ppermute(block, axis, [(member, member ^ mask) for member in range(co...]
    pallas_call x0 -> x7, Pallas kernels: none -> 13.7 us  [the longest x1 5.62 us: own_rows(): pl.pallas_call(functools.partial(own_kernel, count), out_shape=shapes, in...]
    all_to_all x1 -> x0, blocking collectives: 12.3 us -> none  [shards(): lax.all_to_all(outgoing, 'dp', split_axis=0, concat_axis=0, tiled=True)]
    reduce_scatter x1 -> x0, waiting for transfers between devices: 11.7 us -> none  [shards(): lax.psum_scatter((jnp.dot(attended_quarter, output_weight, preferred_elem...]
    convert_element_type x3 -> x0, other arithmetic: 3.5 us -> none  [the longest x1 1.74 us: layer_norm(): return (shifted * lax.rsqrt(spread + epsilon) * gain).astype(jnp.bfloat16)]
  transfers between devices with their start and end apart: 3 -> 17, of which waited for: 3 -> 7; matrix products, arithmetic and copies ran while one was open for 24% -> 0% of each run, Pallas kernels for 0% -> 21%
where the time goes in v3:
time: 44.8 us; the launch traced here: 44.6 us
  starting transfers between devices  14.9 us (33%)
  waiting for transfers between devices  14.6 us (33%)
  Pallas kernels  13.7 us (31%)
  between operations  0.72 us (2%)
  local copies, waits for them, and re-layouts  0.68 us (2%)
    ppermute x17, starting transfers between devices, exchanged(): lax.ppermute(block, axis, [(member, member ^ mask) for member in range(co...  14.9 us
    ppermute x17, waiting for transfers between devices, exchanged(): lax.ppermute(block, axis, [(member, member ^ mask) for member in range(co...  14.6 us
    pallas_call x1, Pallas kernels, own_rows(): pl.pallas_call(functools.partial(own_kernel, count), out_shape=shapes, in...  5.62 us
    pallas_call x1, Pallas kernels, last_rows(): pl.pallas_call(last_kernel, out_shape=[pltpu.VMEM((tokens, 3 * HD), jnp.b...  2.84 us
    pallas_call x1, Pallas kernels, middle_rows(): pl.pallas_call(middle_kernel, out_shape=[pltpu.VMEM((rows, 3 * HD), jnp.b...  2.23 us
    pallas_call x1, Pallas kernels, finished(): pl.pallas_call(functools.partial(finish_kernel, len(parts)), out_shape=[j...  1.53 us
    pallas_call x1, Pallas kernels, tail_rows(): pl.pallas_call(functools.partial(tail_kernel, block_rows), out_shape=shap...  1.35 us
  transfers between devices with their start and end apart: 17, of which 7 were waited for; matrix products, arithmetic and copies ran while one was open for 0% of the time, Pallas kernels for 21%

profile of v3, /device:TPU:0, one launch (start us, length us, event | category | flops | bytes accessed | tf_op | source)
XLA Modules:
  0.0 44.6 jit_solution(7937892376430730516)
XLA Ops:
  0.6 0.5 %collective-permute-start.2 = (bf16[32,2048]{1,0:T(8,128)(2,1)}, bf16[32,2048]{1,0:T(8,128)(2,1)S(1)}, u32[]{:S(2)}, u32[]{:S(2)}) collective-permute-start(bf16[32,2048]{1,0:T(8,128)(2,1)} %refs_0_.1), channel_id=1, source_target_pairs={{0,1},{1,0},{2,3},{3,2},{4,5},{5,4},{6,7},{7,6},{8,9},{9,8},{10,11... | collective-permute-start | bytes 393224 | tf_op jit(solution)/shard_map/ppermute | solution.py:235
  1.2 2.6 %collective-permute-start.1 = (bf16[32,2048]{1,0:T(8,128)(2,1)}, bf16[32,2048]{1,0:T(8,128)(2,1)S(1)}, u32[]{:S(2)}, u32[]{:S(2)}) collective-permute-start(bf16[32,2048]{1,0:T(8,128)(2,1)} %refs_0_.1), channel_id=1, source_target_pairs={{0,2},{1,3},{2,0},{3,1},{4,6},{5,7},{6,4},{7,5},{8,10},{9,11},{10,... | collective-permute-start | bytes 393224 | tf_op jit(solution)/shard_map/ppermute | solution.py:235
  3.8 2.6 %collective-permute-start = (bf16[32,2048]{1,0:T(8,128)(2,1)}, bf16[32,2048]{1,0:T(8,128)(2,1)S(1)}, u32[]{:S(2)}, u32[]{:S(2)}) collective-permute-start(bf16[32,2048]{1,0:T(8,128)(2,1)} %refs_0_.1), channel_id=1, source_target_pairs={{0,4},{1,5},{2,6},{3,7},{4,0},{5,1},{6,2},{7,3},{8,12},{9,13},{10,... | collective-permute-start | bytes 393224 | tf_op jit(solution)/shard_map/ppermute | solution.py:235
  6.4 0.7 %copy-done = s32[1,256]{1,0:T(1,128)S(1)} copy-done((s32[1,256]{1,0:T(1,128)S(1)}, s32[1,256]{1,0:T(1,128)}, u32[]{:S(2)}) %copy-start) | copy-done | bytes 1048
  7.1 5.6 %own_rows.1 = (bf16[32,2048]{1,0:T(8,128)(2,1)S(1)}, f32[1,2048]{1,0:T(1,128)S(1)}, f32[1,2048]{1,0:T(1,128)S(1)}, bf16[2048,768]{1,0:T(8,128)(2,1)S(1)}, bf16[2...) custom-call(s32[1,256]{1,0:T(1,128)S(1)} %copy-done, ...), custom_call_target="tpu_custom_call" | custom-call | flops 738197504 | bytes 12730368 | tf_op jit(solution)/shard_map/own_rows/pallas_call | solution.py:424
  12.7 0.0 collective-permute-done.1.refs_0_
  12.7 0.6 %collective-permute-done.refs_2_ = bf16[32,2048]{1,0:T(8,128)(2,1)S(1)} collective-permute-done((bf16[32,2048]{1,0:T(8,128)(2,1)}, bf16[32,2048]{1,0:T(8,128)(2,1)S(1)}, u32[]{:S(2)}, u32[]{:S(2)}) %collective-permute-start) | collective-permute-done | bytes 131104 | tf_op jit(solution)/shard_map/ppermute | solution.py:235
  13.4 0.4 collective-permute-start.3
  13.8 0.0 collective-permute-start.5
  13.8 0.5 %collective-permute-start.6 = (bf16[32,2048]{1,0:T(8,128)(2,1)S(1)}, bf16[32,2048]{1,0:T(8,128)(2,1)S(1)}, u32[]{:S(2)}, u32[]{:S(2)}) collective-permute-start(bf16[32,2048]{1,0:T(8,128)(2,1)S(1)} %collective-permute-done.refs_2_), channel_id=1, source_target_pairs={{0,1},{1,0},{2,3},{3,2},{4,5},{5,4},{6,7},{7,6},{8,9},{9,8},{10,11... | collective-permute-start | bytes 393224 | tf_op jit(solution)/shard_map/ppermute | solution.py:235
  14.3 4.0 %collective-permute-done.3.refs_0_ = bf16[32,2048]{1,0:T(8,128)(2,1)S(1)} collective-permute-done((bf16[32,2048]{1,0:T(8,128)(2,1)S(1)}, bf16[32,2048]{1,0:T(8,128)(2,1)S(1)}, u32[]{:S(2)}, u32[]{:S(2)}) %collective-permute-start.3) | collective-permute-done | bytes 131104 | tf_op jit(solution)/shard_map/ppermute | solution.py:235
  18.3 0.0 collective-permute-done.5.refs_1_
  18.3 0.0 collective-permute-done.6.refs_3_
  18.3 2.2 %middle_rows.1 = (bf16[128,768]{1,0:T(8,128)(2,1)S(1)}, f32[128,2048]{1,0:T(8,128)S(1)}) custom-call(bf16[32,2048]{1,0:T(8,128)(2,1)S(1)} %collective-permute-done.1.refs_0_, bf16[32,2048]{1,0:T(8,128)(2,1)S(1)} %collective-permute-done.5.refs_1_, bf16[32,2048]{1,0:T(8,128)(2,1)S(1)} %collective-permute-done.refs_2_, ...), custom_call_target="tpu_custom_call" | custom-call | flops 1476395008 | bytes 1048576 | tf_op jit(solution)/shard_map/middle_rows/pallas_call | solution.py:466
  20.6 0.0 collective-permute-done.4.refs_1_
  20.6 2.8 %last_rows.1 = (bf16[256,768]{1,0:T(8,128)(2,1)S(1)}, bf16[32,2048]{1,0:T(8,128)(2,1)S(1)}, f32[32,2048]{1,0:T(8,128)S(1)}) custom-call(bf16[32,2048]{1,0:T(8,128)(2,1)S(1)} %collective-permute-done.3.refs_0_, bf16[32,2048]{1,0:T(8,128)(2,1)S(1)} %collective-permute-done.4.refs_1_, f32[1,2048]{1,0:T(1,128)S(1)} %get-tuple-element.48.refs_4_.refs_2_, ...), custom_call_target="tpu_custom_call" | custom-call | flops 805306368 | bytes 1048576 | tf_op jit(solution)/shard_map/last_rows/pallas_call | solution.py:520
  23.4 0.6 %collective-permute-start.7 = (bf16[32,2048]{1,0:T(8,128)(2,1)S(1)}, bf16[32,2048]{1,0:T(8,128)(2,1)S(1)}, u32[]{:S(2)}, u32[]{:S(2)}) collective-permute-start(bf16[32,2048]{1,0:T(8,128)(2,1)S(1)} %get-tuple-element.62), channel_id=1, source_target_pairs={{0,1},{1,0},{2,3},{3,2},{4,5},{5,4},{6,7},{7,6},{8,9},{9,8},{10,11... | collective-permute-start | bytes 393224 | tf_op jit(solution)/shard_map/ppermute | solution.py:235
  24.0 1.4 %tail_rows.1 = (bf16[32,2048]{1,0:T(8,128)(2,1)S(1)}, bf16[32,2048]{1,0:T(8,128)(2,1)S(1)}, bf16[32,2048]{1,0:T(8,128)(2,1)S(1)}, f32[32,2048]{1,0:T(8,128)S(1)}...) custom-call(bf16[256,768]{1,0:T(8,128)(2,1)S(1)} %get-tuple-element., ...), custom_call_target="tpu_custom_call" | custom-call | flops 268435456 | bytes 1048576 | tf_op jit(solution)/shard_map/tail_rows/pallas_call | solution.py:599
  25.4 0.5 %collective-permute-start.8 = (bf16[32,2048]{1,0:T(8,128)(2,1)S(1)}, bf16[32,2048]{1,0:T(8,128)(2,1)S(1)}, u32[]{:S(2)}, u32[]{:S(2)}) collective-permute-start(bf16[32,2048]{1,0:T(8,128)(2,1)S(1)} %third_added.1), channel_id=1, source_target_pairs={{0,2},{1,3},{2,0},{3,1},{4,6},{5,7},{6,4},{7,5},{8,10},{9,11},{10,... | collective-permute-start | bytes 393224 | tf_op jit(solution)/shard_map/ppermute | solution.py:235
  25.9 0.5 %collective-permute-start.10 = (bf16[32,2048]{1,0:T(8,128)(2,1)S(1)}, bf16[32,2048]{1,0:T(8,128)(2,1)S(1)}, u32[]{:S(2)}, u32[]{:S(2)}) collective-permute-start(bf16[32,2048]{1,0:T(8,128)(2,1)S(1)} %get-tuple-element.72), channel_id=1, source_target_pairs={{0,1},{1,0},{2,3},{3,2},{4,5},{5,4},{6,7},{7,6},{8,9},{9,8},{10,11... | collective-permute-start | bytes 393224 | tf_op jit(solution)/shard_map/ppermute | solution.py:235
  26.4 4.4 %collective-permute-done.8.passing_ref = bf16[32,2048]{1,0:T(8,128)(2,1)S(1)} collective-permute-done((bf16[32,2048]{1,0:T(8,128)(2,1)S(1)}, bf16[32,2048]{1,0:T(8,128)(2,1)S(1)}, u32[]{:S(2)}, u32[]{:S(2)}) %collective-permute-start.8) | collective-permute-done | bytes 131104 | tf_op jit(solution)/shard_map/ppermute | solution.py:235
  30.9 0.1 remaining_sums.1
  31.0 1.3 %collective-permute-start.12 = (bf16[32,2048]{1,0:T(8,128)(2,1)S(1)}, bf16[32,2048]{1,0:T(8,128)(2,1)S(1)}, u32[]{:S(2)}, u32[]{:S(2)}) collective-permute-start(bf16[32,2048]{1,0:T(8,128)(2,1)S(1)} %get-tuple-element.84), channel_id=1, source_target_pairs={{0,4},{1,5},{2,6},{3,7},{4,0},{5,1},{6,2},{7,3},{8,12},{9,13},{10,... | collective-permute-start | bytes 393224 | tf_op jit(solution)/shard_map/ppermute | solution.py:235
  32.3 1.7 %collective-permute-start.13 = (bf16[32,2048]{1,0:T(8,128)(2,1)S(1)}, bf16[32,2048]{1,0:T(8,128)(2,1)S(1)}, u32[]{:S(2)}, u32[]{:S(2)}) collective-permute-start(bf16[32,2048]{1,0:T(8,128)(2,1)S(1)} %get-tuple-element.85), channel_id=1, source_target_pairs={{0,2},{1,3},{2,0},{3,1},{4,6},{5,7},{6,4},{7,5},{8,10},{9,11},{10,... | collective-permute-start | bytes 393224 | tf_op jit(solution)/shard_map/ppermute | solution.py:235
  34.1 1.5 %collective-permute-start.14 = (bf16[8,16,512]{2,1,0:T(8,128)(2,1)S(1)}, bf16[8,16,512]{2,1,0:T(8,128)(2,1)S(1)}, u32[]{:S(2)}, u32[]{:S(2)}) collective-permute-start(bf16[8,16,512]{2,1,0:T(8,128)(2,1)S(1)} %get-tuple-element.87), channel_id=1, source_target_pairs={{0,8},{8,0},{16,24},{24,16},{1,9},{9,1},{17,25},{25,17},{2,10},{10... | collective-permute-start | bytes 393224 | tf_op jit(solution)/shard_map/ppermute | solution.py:235
  35.6 1.5 %collective-permute-start.15 = (bf16[8,16,512]{2,1,0:T(8,128)(2,1)S(1)}, bf16[8,16,512]{2,1,0:T(8,128)(2,1)S(1)}, u32[]{:S(2)}, u32[]{:S(2)}) collective-permute-start(bf16[8,16,512]{2,1,0:T(8,128)(2,1)S(1)} %get-tuple-element.88), channel_id=1, source_target_pairs={{0,16},{8,24},{16,0},{24,8},{1,17},{9,25},{17,1},{25,9},{2,18},{10... | collective-permute-start | bytes 393224 | tf_op jit(solution)/shard_map/ppermute | solution.py:235
  37.1 0.5 %collective-permute-start.16 = (bf16[8,16,512]{2,1,0:T(8,128)(2,1)S(1)}, bf16[8,16,512]{2,1,0:T(8,128)(2,1)S(1)}, u32[]{:S(2)}, u32[]{:S(2)}) collective-permute-start(bf16[8,16,512]{2,1,0:T(8,128)(2,1)S(1)} %get-tuple-element.89), channel_id=1, source_target_pairs={{0,24},{8,16},{16,8},{24,0},{1,25},{9,17},{17,9},{25,1},{2,26},{10... | collective-permute-start | bytes 393224 | tf_op jit(solution)/shard_map/ppermute | solution.py:235
  37.6 1.8 %collective-permute-done.12.refs_0_ = bf16[32,2048]{1,0:T(8,128)(2,1)S(1)} collective-permute-done((bf16[32,2048]{1,0:T(8,128)(2,1)S(1)}, bf16[32,2048]{1,0:T(8,128)(2,1)S(1)}, u32[]{:S(2)}, u32[]{:S(2)}) %collective-permute-start.12) | collective-permute-done | bytes 131104 | tf_op jit(solution)/shard_map/ppermute | solution.py:235
  39.3 0.3 collective-permute-done.13.refs_1_
  39.7 0.7 %collective-permute-done.14.refs_3_ = bf16[8,16,512]{2,1,0:T(8,128)(2,1)S(1)} collective-permute-done((bf16[8,16,512]{2,1,0:T(8,128)(2,1)S(1)}, bf16[8,16,512]{2,1,0:T(8,128)(2,1)S(1)}, u32[]{:S(2)}, u32[]{:S(2)}) %collective-permute-start.14) | collective-permute-done | bytes 131104 | tf_op jit(solution)/shard_map/ppermute | solution.py:235
  40.4 2.7 %collective-permute-done.15.refs_4_ = bf16[8,16,512]{2,1,0:T(8,128)(2,1)S(1)} collective-permute-done((bf16[8,16,512]{2,1,0:T(8,128)(2,1)S(1)}, bf16[8,16,512]{2,1,0:T(8,128)(2,1)S(1)}, u32[]{:S(2)}, u32[]{:S(2)}) %collective-permute-start.15) | collective-permute-done | bytes 131104 | tf_op jit(solution)/shard_map/ppermute | solution.py:235
  43.1 1.5 %finished.1 = (f32[32,2048]{1,0:T(8,128)}, bf16[1,4,8,16,512]{4,3,2,1,0:T(8,128)(2,1)}) custom-call(f32[32,2048]{1,0:T(8,128)S(1)} %get-tuple-element.77.base_ref, bf16[32,2048]{1,0:T(8,128)(2,1)S(1)} %collective-permute-done.12.refs_0_, bf16[32,2048]{1,0:T(8,128)(2,1)S(1)} %collective-permute-done.13.refs_1_, ...), custom_call_target="tpu_custom_call" | custom-call | tf_op jit(solution)/shard_map/finished/pallas_call | solution.py:683
  (11 shorter events, 0.1 us)
Async XLA Ops:
  0.6 5.8 %collective-permute-start.2 = (bf16[32,2048]{1,0:T(8,128)(2,1)}, bf16[32,2048]{1,0:T(8,128)(2,1)S(1)}, u32[]{:S(2)}, u32[]{:S(2)}) collective-permute-start(bf16[32,2048]{1,0:T(8,128)(2,1)} %refs_0_.1), channel_id=1, source_target_pairs={{0,1},{1,0},{2,3},{3,2},{4,5},{5,4},{6,7},{7,6},{8,9},{9,8},{10,11... | collective-permute-start | bytes 393224 | tf_op jit(solution)/shard_map/ppermute | solution.py:235
  1.2 11.6 %collective-permute-start.1 = (bf16[32,2048]{1,0:T(8,128)(2,1)}, bf16[32,2048]{1,0:T(8,128)(2,1)S(1)}, u32[]{:S(2)}, u32[]{:S(2)}) collective-permute-start(bf16[32,2048]{1,0:T(8,128)(2,1)} %refs_0_.1), channel_id=1, source_target_pairs={{0,2},{1,3},{2,0},{3,1},{4,6},{5,7},{6,4},{7,5},{8,10},{9,11},{10,... | collective-permute-start | bytes 393224 | tf_op jit(solution)/shard_map/ppermute | solution.py:235
  3.8 9.6 %collective-permute-start = (bf16[32,2048]{1,0:T(8,128)(2,1)}, bf16[32,2048]{1,0:T(8,128)(2,1)S(1)}, u32[]{:S(2)}, u32[]{:S(2)}) collective-permute-start(bf16[32,2048]{1,0:T(8,128)(2,1)} %refs_0_.1), channel_id=1, source_target_pairs={{0,4},{1,5},{2,6},{3,7},{4,0},{5,1},{6,2},{7,3},{8,12},{9,13},{10,... | collective-permute-start | bytes 393224 | tf_op jit(solution)/shard_map/ppermute | solution.py:235
  6.4 0.7 %copy-start = (s32[1,256]{1,0:T(1,128)S(1)}, s32[1,256]{1,0:T(1,128)}, u32[]{:S(2)}) copy-start(s32[1,256]{1,0:T(1,128)} %segments_ref.1) | copy-start | bytes 3076
  13.4 5.0 %collective-permute-start.3 = (bf16[32,2048]{1,0:T(8,128)(2,1)S(1)}, bf16[32,2048]{1,0:T(8,128)(2,1)S(1)}, u32[]{:S(2)}, u32[]{:S(2)}) collective-permute-start(bf16[32,2048]{1,0:T(8,128)(2,1)S(1)} %collective-permute-done.refs_2_), channel_id=1, source_target_pairs={{0,2},{1,3},{2,0},{3,1},{4,6},{5,7},{6,4},{7,5},{8,10},{9,11},{10,... | collective-permute-start | bytes 393224 | tf_op jit(solution)/shard_map/ppermute | solution.py:235
  13.8 4.5 %collective-permute-start.5 = (bf16[32,2048]{1,0:T(8,128)(2,1)S(1)}, bf16[32,2048]{1,0:T(8,128)(2,1)S(1)}, u32[]{:S(2)}, u32[]{:S(2)}) collective-permute-start(bf16[32,2048]{1,0:T(8,128)(2,1)S(1)} %collective-permute-done.1.refs_0_), channel_id=1, source_target_pairs={{0,1},{1,0},{2,3},{3,2},{4,5},{5,4},{6,7},{7,6},{8,9},{9,8},{10,11... | collective-permute-start | bytes 393224 | tf_op jit(solution)/shard_map/ppermute | solution.py:235
  13.8 4.5 %collective-permute-start.6 = (bf16[32,2048]{1,0:T(8,128)(2,1)S(1)}, bf16[32,2048]{1,0:T(8,128)(2,1)S(1)}, u32[]{:S(2)}, u32[]{:S(2)}) collective-permute-start(bf16[32,2048]{1,0:T(8,128)(2,1)S(1)} %collective-permute-done.refs_2_), channel_id=1, source_target_pairs={{0,1},{1,0},{2,3},{3,2},{4,5},{5,4},{6,7},{7,6},{8,9},{9,8},{10,11... | collective-permute-start | bytes 393224 | tf_op jit(solution)/shard_map/ppermute | solution.py:235
  18.3 2.3 %collective-permute-start.4 = (bf16[32,2048]{1,0:T(8,128)(2,1)S(1)}, bf16[32,2048]{1,0:T(8,128)(2,1)S(1)}, u32[]{:S(2)}, u32[]{:S(2)}) collective-permute-start(bf16[32,2048]{1,0:T(8,128)(2,1)S(1)} %collective-permute-done.3.refs_0_), channel_id=1, source_target_pairs={{0,1},{1,0},{2,3},{3,2},{4,5},{5,4},{6,7},{7,6},{8,9},{9,8},{10,11... | collective-permute-start | bytes 393224 | tf_op jit(solution)/shard_map/ppermute | solution.py:235
  23.4 1.9 %collective-permute-start.7 = (bf16[32,2048]{1,0:T(8,128)(2,1)S(1)}, bf16[32,2048]{1,0:T(8,128)(2,1)S(1)}, u32[]{:S(2)}, u32[]{:S(2)}) collective-permute-start(bf16[32,2048]{1,0:T(8,128)(2,1)S(1)} %get-tuple-element.62), channel_id=1, source_target_pairs={{0,1},{1,0},{2,3},{3,2},{4,5},{5,4},{6,7},{7,6},{8,9},{9,8},{10,11... | collective-permute-start | bytes 393224 | tf_op jit(solution)/shard_map/ppermute | solution.py:235
  25.4 5.5 %collective-permute-start.8 = (bf16[32,2048]{1,0:T(8,128)(2,1)S(1)}, bf16[32,2048]{1,0:T(8,128)(2,1)S(1)}, u32[]{:S(2)}, u32[]{:S(2)}) collective-permute-start(bf16[32,2048]{1,0:T(8,128)(2,1)S(1)} %third_added.1), channel_id=1, source_target_pairs={{0,2},{1,3},{2,0},{3,1},{4,6},{5,7},{6,4},{7,5},{8,10},{9,11},{10,... | collective-permute-start | bytes 393224 | tf_op jit(solution)/shard_map/ppermute | solution.py:235
  25.9 4.9 %collective-permute-start.9 = (bf16[32,2048]{1,0:T(8,128)(2,1)S(1)}, bf16[32,2048]{1,0:T(8,128)(2,1)S(1)}, u32[]{:S(2)}, u32[]{:S(2)}) collective-permute-start(bf16[32,2048]{1,0:T(8,128)(2,1)S(1)} %get-tuple-element.70), channel_id=1, source_target_pairs={{0,1},{1,0},{2,3},{3,2},{4,5},{5,4},{6,7},{7,6},{8,9},{9,8},{10,11... | collective-permute-start | bytes 393224 | tf_op jit(solution)/shard_map/ppermute | solution.py:235
  25.9 4.9 %collective-permute-start.10 = (bf16[32,2048]{1,0:T(8,128)(2,1)S(1)}, bf16[32,2048]{1,0:T(8,128)(2,1)S(1)}, u32[]{:S(2)}, u32[]{:S(2)}) collective-permute-start(bf16[32,2048]{1,0:T(8,128)(2,1)S(1)} %get-tuple-element.72), channel_id=1, source_target_pairs={{0,1},{1,0},{2,3},{3,2},{4,5},{5,4},{6,7},{7,6},{8,9},{9,8},{10,11... | collective-permute-start | bytes 393224 | tf_op jit(solution)/shard_map/ppermute | solution.py:235
  26.4 4.4 %collective-permute-start.11 = (bf16[32,2048]{1,0:T(8,128)(2,1)S(1)}, bf16[32,2048]{1,0:T(8,128)(2,1)S(1)}, u32[]{:S(2)}, u32[]{:S(2)}) collective-permute-start(bf16[32,2048]{1,0:T(8,128)(2,1)S(1)} %get-tuple-element.74), channel_id=1, source_target_pairs={{0,1},{1,0},{2,3},{3,2},{4,5},{5,4},{6,7},{7,6},{8,9},{9,8},{10,11... | collective-permute-start | bytes 393224 | tf_op jit(solution)/shard_map/ppermute | solution.py:235
  31.0 8.4 %collective-permute-start.12 = (bf16[32,2048]{1,0:T(8,128)(2,1)S(1)}, bf16[32,2048]{1,0:T(8,128)(2,1)S(1)}, u32[]{:S(2)}, u32[]{:S(2)}) collective-permute-start(bf16[32,2048]{1,0:T(8,128)(2,1)S(1)} %get-tuple-element.84), channel_id=1, source_target_pairs={{0,4},{1,5},{2,6},{3,7},{4,0},{5,1},{6,2},{7,3},{8,12},{9,13},{10,... | collective-permute-start | bytes 393224 | tf_op jit(solution)/shard_map/ppermute | solution.py:235
  32.3 7.3 %collective-permute-start.13 = (bf16[32,2048]{1,0:T(8,128)(2,1)S(1)}, bf16[32,2048]{1,0:T(8,128)(2,1)S(1)}, u32[]{:S(2)}, u32[]{:S(2)}) collective-permute-start(bf16[32,2048]{1,0:T(8,128)(2,1)S(1)} %get-tuple-element.85), channel_id=1, source_target_pairs={{0,2},{1,3},{2,0},{3,1},{4,6},{5,7},{6,4},{7,5},{8,10},{9,11},{10,... | collective-permute-start | bytes 393224 | tf_op jit(solution)/shard_map/ppermute | solution.py:235
  34.1 6.3 %collective-permute-start.14 = (bf16[8,16,512]{2,1,0:T(8,128)(2,1)S(1)}, bf16[8,16,512]{2,1,0:T(8,128)(2,1)S(1)}, u32[]{:S(2)}, u32[]{:S(2)}) collective-permute-start(bf16[8,16,512]{2,1,0:T(8,128)(2,1)S(1)} %get-tuple-element.87), channel_id=1, source_target_pairs={{0,8},{8,0},{16,24},{24,16},{1,9},{9,1},{17,25},{25,17},{2,10},{10... | collective-permute-start | bytes 393224 | tf_op jit(solution)/shard_map/ppermute | solution.py:235
  35.6 7.5 %collective-permute-start.15 = (bf16[8,16,512]{2,1,0:T(8,128)(2,1)S(1)}, bf16[8,16,512]{2,1,0:T(8,128)(2,1)S(1)}, u32[]{:S(2)}, u32[]{:S(2)}) collective-permute-start(bf16[8,16,512]{2,1,0:T(8,128)(2,1)S(1)} %get-tuple-element.88), channel_id=1, source_target_pairs={{0,16},{8,24},{16,0},{24,8},{1,17},{9,25},{17,1},{25,9},{2,18},{10... | collective-permute-start | bytes 393224 | tf_op jit(solution)/shard_map/ppermute | solution.py:235
  37.1 6.0 %collective-permute-start.16 = (bf16[8,16,512]{2,1,0:T(8,128)(2,1)S(1)}, bf16[8,16,512]{2,1,0:T(8,128)(2,1)S(1)}, u32[]{:S(2)}, u32[]{:S(2)}) collective-permute-start(bf16[8,16,512]{2,1,0:T(8,128)(2,1)S(1)} %get-tuple-element.89), channel_id=1, source_target_pairs={{0,24},{8,16},{16,8},{24,0},{1,25},{9,17},{17,9},{25,1},{2,26},{10... | collective-permute-start | bytes 393224 | tf_op jit(solution)/shard_map/ppermute | solution.py:235

commit v4 on v3

--- a/solution.py
+++ b/solution.py
@@ -309,15 +309,16 @@
             )
 
 
-def hide(normed_ref, upward_ref, hidden_ref):
+def hide(normed_ref, upward_ref, hidden_ref, place):
     chunk = 256
+    rows = slice(place, place + normed_ref.shape[0])
     for first in range(0, upward_ref.shape[1], chunk):
         columns = slice(first, first + chunk)
         upward = jnp.dot(
             normed_ref[...], upward_ref[:, columns], preferred_element_type=jnp.float32
         )
         hidden = 0.5 * upward * (1.0 + lax.erf(upward * (0.5**0.5)))
-        hidden_ref[:, columns] = hidden.astype(jnp.bfloat16)
+        hidden_ref[rows, columns] = hidden.astype(jnp.bfloat16)
 
 
 def attend(joined_ref, offsets_ref, first, rows, block_rows):
@@ -372,10 +373,7 @@
     sine_up_ref[...] = jnp.where((lane >= half) & (lane < ROT), sine, 0.0)
 
 
-def own_kernel(count, segments_ref, beside_ref, *refs):
-    sources, targets = refs[:count], refs[count : 2 * count]
-    offsets_ref, *table_refs, joined_ref, fed_ref = refs[2 * count : 2 * count + 6]
-    attention_scr, feedforward_scr, hidden_scr, sems = refs[2 * count + 6 :]
+def copies_in(sources, targets, sems):
     copies = []
     for number, (source, target) in enumerate(zip(sources, targets)):
         parts = 4 if source.shape[0] >= 256 else 1
@@ -389,134 +387,153 @@
         )
     for copy in sum(copies, []):
         copy.start()
-
-    def wait_for(*numbers):
-        for number in numbers:
-            for copy in copies[number]:
-                copy.wait()
-
-    hidden_ref, *gain_refs, heads_ref, upward_ref, downward_ref, _ = targets
-    block_rows = hidden_ref.shape[0]
+    return copies
+
+
+def wait_for(copies):
+    for copy in copies:
+        copy.wait()
+
+
+def own_kernel(count, *refs):
+    sources, targets = refs[:count], refs[count : 2 * count]
+    offsets_ref, *table_refs, joined_ref, hidden_ref = refs[2 * count : 2 * count + 6]
+    attention_scr, feedforward_scr, sems = refs[2 * count + 6 :]
+    copies = copies_in(sources, targets, sems)
+    segments_ref, states_ref, *gain_refs, heads_ref, upward_ref = targets
+    block_rows = states_ref.shape[0]
+    wait_for(copies[0])
     make_tables(segments_ref, offsets_ref, *table_refs)
-    wait_for(0, 1, 2)
-    normalize([hidden_ref, beside_ref], gain_refs, [attention_scr, feedforward_scr])
-    wait_for(3)
-    places = [position_of(0, half, block_rows) for half in range(CORES)]
+    for number in (1, 2, 3):
+        wait_for(copies[number])
+    normalize([states_ref], gain_refs, [attention_scr, feedforward_scr])
+    wait_for(copies[4])
+    places = [position_of(0, 0, block_rows)]
     project(attention_scr, heads_ref, table_refs, places, joined_ref, 0)
-    wait_for(4)
-    hide(feedforward_scr, upward_ref, hidden_scr)
-    wait_for(5)
-    fed_ref[...] = jnp.dot(
-        hidden_scr[...], downward_ref[...], preferred_element_type=jnp.float32
-    )
-    wait_for(6)
-
-
-def own_rows(segments, beside, staged):
-    tokens = segments.shape[1]
-    block_rows, width = beside.shape
-    rows = CORES * block_rows
-    hidden_width = staged[4].shape[1]
+    wait_for(copies[5])
+    hide(feedforward_scr, upward_ref, hidden_ref, 0)
+
+
+def own_rows(staged):
+    tokens = staged[0].shape[1]
+    rows, width = staged[1].shape
+    hidden_width = staged[5].shape[1]
     shapes = [pltpu.VMEM(array.shape, array.dtype) for array in staged]
     shapes += [pltpu.VMEM((tokens, 128), jnp.float32)] * 4
-    shapes += [pltpu.VMEM((rows, 3 * HD), jnp.bfloat16), pltpu.VMEM((rows, width), jnp.float32)]
+    shapes += [
+        pltpu.VMEM((rows, 3 * HD), jnp.bfloat16),
+        pltpu.VMEM((rows, hidden_width), jnp.bfloat16),
+    ]
     count = len(staged)
     return pl.pallas_call(
         functools.partial(own_kernel, count),
         out_shape=shapes,
-        in_specs=vmem_specs(2) + [pl.BlockSpec(memory_space=pltpu.HBM)] * count,
+        in_specs=[pl.BlockSpec(memory_space=pltpu.HBM)] * count,
         out_specs=vmem_specs(len(shapes)),
         scratch_shapes=[
             pltpu.VMEM((rows, width), jnp.bfloat16),
             pltpu.VMEM((rows, width), jnp.bfloat16),
-            pltpu.VMEM((rows, hidden_width), jnp.bfloat16),
             pltpu.SemaphoreType.DMA((count, 4)),
         ],
         compiler_params=parameters(12),
         cost_estimate=pl.CostEstimate(
-            flops=2 * rows * width * (3 * HD + 2 * hidden_width),
+            flops=2 * rows * width * (3 * HD + hidden_width),
             bytes_accessed=sum(array.nbytes for array in staged),
             transcendentals=rows * hidden_width,
         ),
         name="own_rows",
-    )(segments, beside, *[in_hbm(array) for array in staged])
-
-
-def middle_kernel(*refs):
-    blocks, (gain_a, gain_f, heads_ref, upward_ref, downward_ref) = refs[:4], refs[4:9]
-    table_refs = refs[9:12]
-    joined_ref, fed_ref, attention_scr, feedforward_scr, hidden_scr = refs[12:]
+    )(*[in_hbm(array) for array in staged])
+
+
+def middle_kernel(origins, *refs):
+    count = len(origins)
+    blocks, (gain_a, gain_f, heads_ref, upward_ref) = refs[:count], refs[count : count + 4]
+    table_refs, source_ref = refs[count + 4 : count + 7], refs[count + 7]
+    joined_ref, hidden_ref, target_ref = refs[count + 8 : count + 11]
+    attention_scr, feedforward_scr, sems = refs[count + 11 :]
+    (copies,) = copies_in([source_ref], [target_ref], sems)
     block_rows = blocks[0].shape[0]
     normalize(blocks, [gain_a, gain_f], [attention_scr, feedforward_scr])
-    places = [position_of(kind, half, block_rows) for kind in (1, 2) for half in range(CORES)]
+    places = [position_of(kind, half, block_rows) for kind, half in origins]
     project(attention_scr, heads_ref, table_refs, places, joined_ref, 0)
-    hide(feedforward_scr, upward_ref, hidden_scr)
-    chunk = 512
-    for first in range(0, downward_ref.shape[1], chunk):
-        columns = slice(first, first + chunk)
-        fed_ref[:, columns] = jnp.dot(
-            hidden_scr[...], downward_ref[:, columns], preferred_element_type=jnp.float32
-        )
-
-
-def middle_rows(blocks, gains, weights, tables):
+    hide(feedforward_scr, upward_ref, hidden_ref, 0)
+    wait_for(copies)
+
+
+def middle_rows(name, origins, blocks, gains, weights, tables, staged):
     block_rows, width = blocks[0].shape
     rows = len(blocks) * block_rows
     hidden_width = weights[1].shape[1]
     return pl.pallas_call(
-        middle_kernel,
+        functools.partial(middle_kernel, origins),
         out_shape=[
             pltpu.VMEM((rows, 3 * HD), jnp.bfloat16),
-            pltpu.VMEM((rows, width), jnp.float32),
+            pltpu.VMEM((rows, hidden_width), jnp.bfloat16),
+            pltpu.VMEM(staged.shape, staged.dtype),
         ],
-        in_specs=vmem_specs(len(blocks) + 2 + 3 + 3),
-        out_specs=vmem_specs(2),
+        in_specs=vmem_specs(len(blocks) + 2 + 2 + 3) + [pl.BlockSpec(memory_space=pltpu.HBM)],
+        out_specs=vmem_specs(3),
         scratch_shapes=[
             pltpu.VMEM((rows, width), jnp.bfloat16),
             pltpu.VMEM((rows, width), jnp.bfloat16),
-            pltpu.VMEM((rows, hidden_width), jnp.bfloat16),
+            pltpu.SemaphoreType.DMA((1, 4)),
         ],
         compiler_params=parameters(12),
         cost_estimate=pl.CostEstimate(
-            flops=2 * rows * width * (3 * HD + 2 * hidden_width),
-            bytes_accessed=MIB,
+            flops=2 * rows * width * (3 * HD + hidden_width),
+            bytes_accessed=staged.nbytes,
             transcendentals=rows * hidden_width,
         ),
-        name="middle_rows",
-    )(*blocks, *gains, *weights, *tables)
+        name=name,
+    )(*blocks, *gains, *weights, *tables, in_hbm(staged))
 
 
 def last_kernel(*refs):
     blocks, (gain_a, gain_f, heads_ref, upward_ref, downward_ref, output_ref) = refs[:2], refs[2:8]
     offsets_ref, *table_refs = refs[8:12]
-    joined_own_ref, joined_middle_ref = refs[12:14]
-    joined_ref, sibling_ref, own_ref, attention_scr, feedforward_scr, hidden_scr = refs[14:]
+    pieces = refs[12:15]
+    joined_ref, sibling_ref, own_ref, attention_scr, feedforward_scr, hidden_scr = refs[15:]
     block_rows = blocks[0].shape[0]
     tokens = joined_ref.shape[0]
     first = tokens - CORES * block_rows
     normalize(blocks, [gain_a, gain_f], [attention_scr, feedforward_scr])
-    own_count = joined_own_ref.shape[0]
-    joined_ref[:own_count, :] = joined_own_ref[...]
-    joined_ref[own_count:first, :] = joined_middle_ref[...]
+    for kind in range(CHIPS - 1):
+        for half in range(CORES):
+            place = (kind * CORES + half) * block_rows
+            joined_ref[place : place + block_rows, :] = piece_of(pieces, kind, half, block_rows)
     places = [position_of(CHIPS - 1, half, block_rows) for half in range(CORES)]
     project(attention_scr, heads_ref, table_refs, places, joined_ref, first)
-    hide(feedforward_scr, upward_ref, hidden_scr)
+    hide(feedforward_scr, upward_ref, hidden_scr, 0)
     attended = attend(joined_ref, offsets_ref, first, CORES * block_rows, block_rows)
+    partial_sums(attended, hidden_scr[...], output_ref, downward_ref, [own_ref], [sibling_ref])
+
+
+def piece_of(pieces, kind, half, block_rows):
+    piece = 2 if half else min(kind, 1)
+    place = (kind if half else (0, 1, 0)[kind]) * block_rows
+    return pieces[piece][place : place + block_rows, :]
+
+
+def partial_sums(attended, hidden, output_ref, downward_ref, own_refs, sibling_refs):
+    rows = attended.shape[0] // (2 * len(own_refs))
     chunk = 512
     for begin in range(0, downward_ref.shape[1], chunk):
         columns = slice(begin, begin + chunk)
         partial = jnp.dot(
-            hidden_scr[...], downward_ref[:, columns], preferred_element_type=jnp.float32
+            hidden, downward_ref[:, columns], preferred_element_type=jnp.float32
         ) + jnp.dot(attended, output_ref[:, columns], preferred_element_type=jnp.float32)
-        own_ref[:, columns] = partial[:block_rows]
-        sibling_ref[:, columns] = partial[block_rows:].astype(jnp.bfloat16)
-
-
-def last_rows(blocks, gains, weights, tables, joined_own, joined_middle):
+        for number, (own_ref, sibling_ref) in enumerate(zip(own_refs, sibling_refs)):
+            first = 2 * number * rows
+            middle = first + rows
+            own_ref[:, columns] = partial[first:middle]
+            sibling_ref[:, columns] = partial[middle : middle + rows].astype(jnp.bfloat16)
+
+
+def last_rows(blocks, gains, weights, tables, pieces):
     block_rows, width = blocks[0].shape
     rows = len(blocks) * block_rows
     hidden_width = weights[1].shape[1]
-    tokens = joined_own.shape[0] + joined_middle.shape[0] + rows
+    tokens = CHIPS * CORES * block_rows
     return pl.pallas_call(
         last_kernel,
         out_shape=[
@@ -524,7 +541,7 @@
             pltpu.VMEM((block_rows, width), jnp.bfloat16),
             pltpu.VMEM((block_rows, width), jnp.float32),
         ],
-        in_specs=vmem_specs(len(blocks) + 2 + 4 + 4 + 2),
+        in_specs=vmem_specs(len(blocks) + 2 + 4 + 4 + 3),
         out_specs=vmem_specs(3),
         scratch_shapes=[
             pltpu.VMEM((rows, width), jnp.bfloat16),
@@ -538,29 +555,51 @@
             transcendentals=rows * hidden_width,
         ),
         name="last_rows",
-    )(*blocks, *gains, *weights, *tables, joined_own, joined_middle)
-
-
-def tail_kernel(block_rows, joined_ref, offsets_ref, output_ref, fed_own_ref, fed_middle_ref, *refs):
-    targets_ref, *sibling_refs = refs[:4]
-    own_refs = refs[4:7]
-    pages_refs, (named_ref, counts_ref, slots_ref, sem) = refs[7:-4], refs[-4:]
+    )(*blocks, *gains, *weights, *tables, *pieces)
+
+
+def kind_kernel(kinds, joined_ref, offsets_ref, output_ref, downward_ref, *refs):
+    pieces, refs = refs[:3], refs[3:]
+    count = len(kinds)
+    siblings, owns = refs[:count], refs[count : 2 * count]
+    block_rows = owns[0].shape[0]
+    rows = CORES * block_rows * count
+    attended = attend(joined_ref, offsets_ref, kinds[0] * CORES * block_rows, rows, block_rows)
+    hidden = jnp.concatenate(
+        [piece_of(pieces, kind, half, block_rows) for kind in kinds for half in range(CORES)], 0
+    )
+    partial_sums(attended, hidden, output_ref, downward_ref, owns, siblings)
+
+
+def kind_rows(name, kinds, joined, offsets, weights, pieces):
+    block_rows = pieces[0].shape[0]
+    output_weight, downward_weight = weights
+    width = output_weight.shape[1]
+    shape = (block_rows, width)
+    count = len(kinds)
+    tokens = joined.shape[0]
+    return pl.pallas_call(
+        functools.partial(kind_kernel, kinds),
+        out_shape=[pltpu.VMEM(shape, jnp.bfloat16)] * count + [pltpu.VMEM(shape, jnp.float32)] * count,
+        in_specs=vmem_specs(7),
+        out_specs=vmem_specs(2 * count),
+        compiler_params=parameters(12),
+        cost_estimate=pl.CostEstimate(
+            flops=4 * block_rows * count * width * (HD + downward_weight.shape[0]),
+            bytes_accessed=MIB,
+            transcendentals=2 * block_rows * count * tokens,
+        ),
+        name=name,
+    )(joined, offsets, output_weight, downward_weight, *pieces)
+
+
+def pages_kernel(block_rows, joined_ref, targets_ref, *refs):
+    pages_refs, (named_ref, counts_ref, slots_ref, sem) = refs[:-4], refs[-4:]
     naming = pltpu.make_async_copy(targets_ref, named_ref, sem)
     naming.start()
     tokens = joined_ref.shape[0]
-    kind_rows = CORES * block_rows
-    rows = tokens - kind_rows
-    attended = attend(joined_ref, offsets_ref, 0, rows, block_rows)
-    chunk = 512
-    for begin in range(0, output_ref.shape[1], chunk):
-        columns = slice(begin, begin + chunk)
-        product = jnp.dot(attended, output_ref[:, columns], preferred_element_type=jnp.float32)
-        near = product[:kind_rows] + fed_own_ref[:, columns]
-        middle = product[kind_rows:] + fed_middle_ref[:, columns]
-        for kind, partial in enumerate((near, middle[:kind_rows], middle[kind_rows:])):
-            own_refs[kind][:, columns] = partial[:block_rows]
-            sibling_refs[kind][:, columns] = partial[block_rows:].astype(jnp.bfloat16)
-
+    for page_ref in pages_refs:
+        page_ref[...] = jnp.zeros(page_ref.shape, page_ref.dtype)
     chip, core = whereabouts()
     group = lax.axis_index("dp")
     naming.wait()
@@ -571,11 +610,9 @@
         slot = counts_ref[target]
         counts_ref[target] = slot + 1
         slots_ref[page] = slot
-    for page_ref in pages_refs:
-        page_ref[...] = jnp.zeros(page_ref.shape, page_ref.dtype)
     capacity = pages_refs[0].shape[0]
     for place in range(0, tokens, PAGE):
-        kind, half = place // kind_rows, (place // block_rows) % CORES
+        kind, half = place // (CORES * block_rows), (place // block_rows) % CORES
         start = ((chip ^ kind) * CORES + (core ^ half)) * block_rows + place % block_rows
         page = start // PAGE
         target = named_ref[page]
@@ -587,19 +624,15 @@
                 page_ref[pl.ds(slot, 1)] = joined_ref[place : place + PAGE, HD:][None]
 
 
-def tail_rows(joined, offsets, output_weight, fed_own, fed_middle, targets, replica_count):
+def cached_pages(joined, targets, replica_count):
     tokens = joined.shape[0]
-    width = fed_own.shape[1]
-    block_rows = fed_own.shape[0] // CORES
     page_count = tokens // PAGE
     capacity = 2 * page_count // replica_count
-    shapes = [
-        pltpu.VMEM((block_rows, width), dtype) for dtype in [jnp.bfloat16] * 3 + [jnp.float32] * 3
-    ] + [pltpu.VMEM((capacity, PAGE, 2 * HD), jnp.bfloat16)] * replica_count
+    shapes = [pltpu.VMEM((capacity, PAGE, 2 * HD), jnp.bfloat16)] * replica_count
     return pl.pallas_call(
-        functools.partial(tail_kernel, block_rows),
+        functools.partial(pages_kernel, tokens // (CHIPS * CORES)),
         out_shape=shapes,
-        in_specs=vmem_specs(5) + [pl.BlockSpec(memory_space=pltpu.HBM)],
+        in_specs=vmem_specs(1) + [pl.BlockSpec(memory_space=pltpu.HBM)],
         out_specs=vmem_specs(len(shapes)),
         scratch_shapes=[
             pltpu.SMEM(targets.shape, jnp.int32),
@@ -607,12 +640,10 @@
             pltpu.SMEM((page_count,), jnp.int32),
             pltpu.SemaphoreType.DMA(()),
         ],
-        compiler_params=parameters(12),
-        cost_estimate=pl.CostEstimate(
-            flops=2 * tokens * width * HD, bytes_accessed=MIB, transcendentals=tokens * tokens
-        ),
-        name="tail_rows",
-    )(joined, offsets, output_weight, fed_own, fed_middle, in_hbm(targets))
+        compiler_params=parameters(8),
+        cost_estimate=pl.CostEstimate(flops=0, bytes_accessed=MIB, transcendentals=0),
+        name="cached_pages",
+    )(joined, in_hbm(targets))
 
 
 def add_kernel(*refs):
@@ -633,65 +664,68 @@
     )(*parts)
 
 
-def sums_kernel(passing_ref, *refs):
-    twos, ones, zeros = refs[0:2], refs[2:4], refs[4:7]
-    second_ref, first_ref, base_ref = refs[7:]
-
-    def total(parts):
-        return sum([part[...].astype(jnp.float32) for part in parts[1:]], parts[0][...])
-
-    second_ref[...] = total((twos[1], twos[0], passing_ref)).astype(jnp.bfloat16)
-    first_ref[...] = total((ones[1], ones[0])).astype(jnp.bfloat16)
-    base_ref[...] = total((zeros[1], zeros[0], zeros[2]))
-
-
-def remaining_sums(passing, twos, ones, zeros, hidden):
+def near_kernel(*refs):
+    ones, zeros, (first_ref, base_ref) = refs[:2], refs[2:5], refs[5:]
+    first = ones[0][...] + ones[1][...].astype(jnp.float32)
+    first_ref[...] = first.astype(jnp.bfloat16)
+    base = zeros[0][...] + zeros[1][...].astype(jnp.float32)
+    base_ref[...] = zeros[2][...].astype(jnp.float32) + base
+
+
+def near_sums(ones, zeros):
+    shape = ones[0].shape
     return pl.pallas_call(
-        sums_kernel,
-        out_shape=[
-            pltpu.VMEM(hidden.shape, jnp.bfloat16),
-            pltpu.VMEM(hidden.shape, jnp.bfloat16),
-            pltpu.VMEM(hidden.shape, jnp.float32),
-        ],
-        in_specs=vmem_specs(8),
-        out_specs=vmem_specs(3),
+        near_kernel,
+        out_shape=[pltpu.VMEM(shape, jnp.bfloat16), pltpu.VMEM(shape, jnp.float32)],
+        in_specs=vmem_specs(5),
+        out_specs=vmem_specs(2),
         compiler_params=parameters(4),
-        name="remaining_sums",
-    )(passing, *twos, *ones, *zeros, hidden)
-
-
-def finish_kernel(part_count, base_ref, *refs):
+        name="near_sums",
+    )(*ones, *zeros)
+
+
+def place_kernel(*refs):
     group = lax.axis_index("dp")
-    parts, pages = refs[:part_count], refs[part_count:-3]
-    output_ref, cache_ref, sems = refs[-3:]
+    pages, (cache_ref, sems) = refs[:-2], refs[-2:]
     copies = [
         pltpu.make_async_copy(page_ref, cache_ref.at[0, group ^ mask], sems.at[mask])
         for mask, page_ref in enumerate(pages)
     ]
     for copy in copies:
         copy.start()
-    total = base_ref[...]
-    for part_ref in parts:
-        total = total + part_ref[...].astype(jnp.float32)
-    output_ref[...] = total
     for copy in copies:
         copy.wait()
 
 
-def finished(base, parts, pages):
+def placed(pages):
     count = len(pages)
     return pl.pallas_call(
-        functools.partial(finish_kernel, len(parts)),
-        out_shape=[
-            jax.ShapeDtypeStruct(base.shape, base.dtype),
-            jax.ShapeDtypeStruct((1, count) + pages[0].shape, pages[0].dtype),
-        ],
-        in_specs=vmem_specs(1 + len(parts)) + [pl.BlockSpec(memory_space=pl.ANY)] * count,
-        out_specs=vmem_specs(1) + [pl.BlockSpec(memory_space=pltpu.HBM)],
+        place_kernel,
+        out_shape=jax.ShapeDtypeStruct((1, count) + pages[0].shape, pages[0].dtype),
+        in_specs=[pl.BlockSpec(memory_space=pl.ANY)] * count,
+        out_specs=pl.BlockSpec(memory_space=pltpu.HBM),
         scratch_shapes=[pltpu.SemaphoreType.DMA((count,))],
         compiler_params=parameters(4),
+        name="placed",
+    )(*pages)
+
+
+def finish_kernel(base_ref, *refs):
+    total = base_ref[...]
+    for part_ref in refs[:-1]:
+        total = total + part_ref[...].astype(jnp.float32)
+    refs[-1][...] = total
+
+
+def finished(base, parts):
+    return pl.pallas_call(
+        finish_kernel,
+        out_shape=jax.ShapeDtypeStruct(base.shape, base.dtype),
+        in_specs=vmem_specs(1 + len(parts)),
+        out_specs=pl.BlockSpec(memory_space=pltpu.VMEM),
+        compiler_params=parameters(4),
         name="finished",
-    )(base, *parts, *pages)
+    )(base, *parts)
 
 
 def shards_whole_heads(
@@ -711,52 +745,76 @@
     first = exchanged(hidden_states, "tensor", to_chip[1])
     beside = exchanged(hidden_states, "tensor", 1)
     staged = (
+        segments,
         hidden_states,
         attention_gain[None],
         feedforward_gain[None],
         heads_weight,
         upward_weight,
-        downward_weight,
-        output_weight,
-    )
-    hidden, *rest = own_rows(segments, beside, staged)
-    gains, (heads, upward, downward, output), tables = rest[:2], rest[2:6], rest[6:10]
-    joined_own, fed_own = rest[10:]
-
-    second, first, joined_own = lax.optimization_barrier((second, first, joined_own))
+    )
+    staged = own_rows(staged)
+    hidden, gains, (heads, upward), tables = staged[1], staged[2:4], staged[4:6], staged[6:10]
+    own_joined, own_hidden = staged[10:]
+
+    second, first, own_joined = lax.optimization_barrier((second, first, own_joined))
     third = exchanged(second, "tensor", to_chip[1])
     second_beside = exchanged(second, "tensor", 1)
     first_beside = exchanged(first, "tensor", 1)
+    there_joined, there_hidden, downward = middle_rows(
+        "there_rows",
+        ((2, 0), (1, 0)),
+        (second, first),
+        gains,
+        (heads, upward),
+        tables[1:],
+        downward_weight,
+    )
+    third, there_joined = lax.optimization_barrier((third, there_joined))
     third_beside = exchanged(third, "tensor", 1)
-    joined_middle, fed_middle = middle_rows(
-        (first, first_beside, second, second_beside), gains, (heads, upward, downward), tables[1:]
+    beside_joined, beside_hidden, output = middle_rows(
+        "beside_rows",
+        ((0, 1), (1, 1), (2, 1)),
+        (beside, first_beside, second_beside),
+        gains,
+        (heads, upward),
+        tables[1:],
+        output_weight,
     )
     joined, sibling, own = last_rows(
         (third, third_beside),
         gains,
         (heads, upward, downward, output),
         tables,
-        joined_own,
-        joined_middle,
-    )
-
+        (own_joined, there_joined, beside_joined),
+    )
+
+    pieces = (own_hidden, there_hidden, beside_hidden)
     received = exchanged(sibling, "tensor", 1)
-    parts = tail_rows(
-        joined, tables[0], output, fed_own, fed_middle, page_targets[:, 0], replica_count
+    second_sibling, second_own = kind_rows(
+        "second_rows", (2,), joined, tables[0], (output, downward), pieces
     )
     third_sum = added("third_added", own, received)
-    siblings, owns, pages = parts[:3], parts[3:6], parts[6:]
-    third_sum, siblings = lax.optimization_barrier((third_sum, siblings))
+    third_sum, second_sibling, joined = lax.optimization_barrier(
+        (third_sum, second_sibling, joined)
+    )
     passing = exchanged(third_sum, "tensor", to_chip[1])
-    pairs = [(exchanged(siblings[kind], "tensor", 1), owns[kind]) for kind in (2, 1, 0)]
-    second_sum, first_sum, base = remaining_sums(passing, *pairs, hidden)
-    second_sum, first_sum, pages = lax.optimization_barrier((second_sum, first_sum, pages))
-    from_second = exchanged(second_sum, "tensor", to_chip[2])
-    from_first = exchanged(first_sum, "tensor", to_chip[1])
+    second_received = exchanged(second_sibling, "tensor", 1)
+    zero_sibling, first_sibling, zero_own, first_own = kind_rows(
+        "near_rows", (0, 1), joined, tables[0], (output, downward), pieces
+    )
+    first_received = exchanged(first_sibling, "tensor", 1)
+    zero_received = exchanged(zero_sibling, "tensor", 1)
+    pages = cached_pages(joined, page_targets[:, 0], replica_count)
     arriving = [pages[0]] + [
         exchanged(pages[mask], "dp", mask) for mask in range(1, replica_count)
     ]
-    return tuple(finished(base, (from_second, from_first), arriving))
+    second_sum = added("second_added", second_own, passing, second_received)
+    from_second = exchanged(second_sum, "tensor", to_chip[2])
+    first_sum, base = near_sums((first_own, first_received), (zero_own, zero_received, hidden))
+    from_first = exchanged(first_sum, "tensor", to_chip[1])
+    cache_pages = placed(arriving)
+    base, cache_pages = lax.optimization_barrier((base, cache_pages))
+    return (finished(base, (from_second, from_first)), cache_pages)
 
 
 def solution(mesh):

time: 44.8 us -> 42.3 us (0.944)
  waiting for transfers between devices: 14.6 us -> 7.26 us
  Pallas kernels: 13.7 us -> 17.8 us
  starting transfers between devices: 14.9 us -> 16.3 us
  local copies, waits for them, and re-layouts: 0.68 us -> 0.01 us
    ppermute x17, waiting for transfers between devices: 14.6 us -> 7.26 us  [exchanged(): lax.ppermute(block, axis, [(member, member ^ mask) for member in range(co...]
    pallas_call x4 -> x8, Pallas kernels: 5.21 us -> 10.6 us  [the longest x2 5.17 us: middle_rows(): pl.pallas_call(functools.partial(middle_kernel, origins), out_shape=[pltp...]
    ppermute x17, starting transfers between devices: 14.9 us -> 16.3 us  [exchanged(): lax.ppermute(block, axis, [(member, member ^ mask) for member in range(co...]
    pallas_call x1, Pallas kernels: 5.62 us -> 4.28 us  [own_rows(): pl.pallas_call(functools.partial(own_kernel, count), out_shape=shapes, in...]
    unnamed x2, local copies, waits for them, and re-layouts: 0.68 us -> 0.01 us
  transfers between devices with their start and end apart: 17 -> 17, of which waited for: 7 -> 5; matrix products, arithmetic and copies ran while one was open for 0% -> 0% of each run, Pallas kernels for 21% -> 34%
where the time goes in v4:
time: 42.3 us; the launch traced here: 42.1 us
  Pallas kernels  17.8 us (42%)
  starting transfers between devices  16.3 us (39%)
  waiting for transfers between devices  7.26 us (17%)
  between operations  0.76 us (2%)
    ppermute x17, starting transfers between devices, exchanged(): lax.ppermute(block, axis, [(member, member ^ mask) for member in range(co...  16.3 us
    ppermute x17, waiting for transfers between devices, exchanged(): lax.ppermute(block, axis, [(member, member ^ mask) for member in range(co...  7.26 us
    pallas_call x2, Pallas kernels, middle_rows(): pl.pallas_call(functools.partial(middle_kernel, origins), out_shape=[pltp...  5.17 us
    pallas_call x1, Pallas kernels, own_rows(): pl.pallas_call(functools.partial(own_kernel, count), out_shape=shapes, in...  4.28 us
    pallas_call x1, Pallas kernels, last_rows(): pl.pallas_call(last_kernel, out_shape=[pltpu.VMEM((tokens, 3 * HD), jnp.b...  2.83 us
    pallas_call x2, Pallas kernels, kind_rows(): pl.pallas_call(functools.partial(kind_kernel, kinds), out_shape=[pltpu.VM...  2.63 us
    pallas_call x1, Pallas kernels, cached_pages(): pl.pallas_call(functools.partial(pages_kernel, tokens // (CHIPS * CORES))...  1.2 us
  transfers between devices with their start and end apart: 17, of which 5 were waited for; matrix products, arithmetic and copies ran while one was open for 0% of the time, Pallas kernels for 34%

profile of v4, /device:TPU:0, one launch (start us, length us, event | category | flops | bytes accessed | tf_op | source)
XLA Modules:
  0.0 42.1 jit_solution(6204851951368162850)
XLA Ops:
  0.6 3.1 %collective-permute-start.1 = (bf16[32,2048]{1,0:T(8,128)(2,1)}, bf16[32,2048]{1,0:T(8,128)(2,1)S(1)}, u32[]{:S(2)}, u32[]{:S(2)}) collective-permute-start(bf16[32,2048]{1,0:T(8,128)(2,1)} %refs_1_.1), channel_id=1, source_target_pairs={{0,2},{1,3},{2,0},{3,1},{4,6},{5,7},{6,4},{7,5},{8,10},{9,11},{10,... | collective-permute-start | bytes 393224 | tf_op jit(solution)/shard_map/ppermute | solution.py:235
  3.7 2.6 %collective-permute-start = (bf16[32,2048]{1,0:T(8,128)(2,1)}, bf16[32,2048]{1,0:T(8,128)(2,1)S(1)}, u32[]{:S(2)}, u32[]{:S(2)}) collective-permute-start(bf16[32,2048]{1,0:T(8,128)(2,1)} %refs_1_.1), channel_id=1, source_target_pairs={{0,4},{1,5},{2,6},{3,7},{4,0},{5,1},{6,2},{7,3},{8,12},{9,13},{10,... | collective-permute-start | bytes 393224 | tf_op jit(solution)/shard_map/ppermute | solution.py:235
  6.3 4.3 %own_rows.1 = (s32[1,256]{1,0:T(1,128)}, bf16[32,2048]{1,0:T(8,128)(2,1)S(1)}, f32[1,2048]{1,0:T(1,128)S(1)}, f32[1,2048]{1,0:T(1,128)S(1)}, bf16[2048,768]{1,0:...) custom-call(s32[1,256]{1,0:T(1,128)} %refs_0_.1, ...), custom_call_target="tpu_custom_call" | custom-call | flops 234881024 | bytes 7488512 | tf_op jit(solution)/shard_map/own_rows/pallas_call | solution.py:428
  10.6 0.0 collective-permute-done.1.refs_1_
  10.6 2.1 %collective-permute-done.refs_0_ = bf16[32,2048]{1,0:T(8,128)(2,1)S(1)} collective-permute-done((bf16[32,2048]{1,0:T(8,128)(2,1)}, bf16[32,2048]{1,0:T(8,128)(2,1)S(1)}, u32[]{:S(2)}, u32[]{:S(2)}) %collective-permute-start) | collective-permute-done | bytes 131104 | tf_op jit(solution)/shard_map/ppermute | solution.py:235
  12.7 0.4 %collective-permute-start.2 = (bf16[32,2048]{1,0:T(8,128)(2,1)S(1)}, bf16[32,2048]{1,0:T(8,128)(2,1)S(1)}, u32[]{:S(2)}, u32[]{:S(2)}) collective-permute-start(bf16[32,2048]{1,0:T(8,128)(2,1)S(1)} %collective-permute-done.refs_0_), channel_id=1, source_target_pairs={{0,2},{1,3},{2,0},{3,1},{4,6},{5,7},{6,4},{7,5},{8,10},{9,11},{10,... | collective-permute-start | bytes 393224 | tf_op jit(solution)/shard_map/ppermute | solution.py:235
  13.1 0.0 collective-permute-start.4
  13.1 0.5 %collective-permute-start.5 = (bf16[32,2048]{1,0:T(8,128)(2,1)S(1)}, bf16[32,2048]{1,0:T(8,128)(2,1)S(1)}, u32[]{:S(2)}, u32[]{:S(2)}) collective-permute-start(bf16[32,2048]{1,0:T(8,128)(2,1)S(1)} %collective-permute-done.1.refs_1_), channel_id=1, source_target_pairs={{0,1},{1,0},{2,3},{3,2},{4,5},{5,4},{6,7},{7,6},{8,9},{9,8},{10,11... | collective-permute-start | bytes 393224 | tf_op jit(solution)/shard_map/ppermute | solution.py:235
  13.6 0.0 collective-permute-start.6
  13.6 3.0 %there_rows.1 = (bf16[64,768]{1,0:T(8,128)(2,1)S(1)}, bf16[64,1024]{1,0:T(8,128)(2,1)S(1)}, bf16[1024,2048]{1,0:T(8,128)(2,1)S(1)}) custom-call(bf16[32,2048]{1,0:T(8,128)(2,1)S(1)} %collective-permute-done.refs_0_, bf16[32,2048]{1,0:T(8,128)(2,1)S(1)} %collective-permute-done.1.refs_1_, f32[1,2048]{1,0:T(1,128)S(1)} %get-tuple-element.47.refs_2_.refs_3_, ...), custom_call_target="tpu_custom_call" | custom-call | flops 469762048 | bytes 4194304 | tf_op jit(solution)/shard_map/there_rows/pallas_call | solution.py:467
  16.6 1.0 %collective-permute-done.2.refs_0_ = bf16[32,2048]{1,0:T(8,128)(2,1)S(1)} collective-permute-done((bf16[32,2048]{1,0:T(8,128)(2,1)S(1)}, bf16[32,2048]{1,0:T(8,128)(2,1)S(1)}, u32[]{:S(2)}, u32[]{:S(2)}) %collective-permute-start.2) | collective-permute-done | bytes 131104 | tf_op jit(solution)/shard_map/ppermute | solution.py:235
  17.7 2.1 %beside_rows.1 = (bf16[96,768]{1,0:T(8,128)(2,1)S(1)}, bf16[96,1024]{1,0:T(8,128)(2,1)S(1)}, bf16[256,2048]{1,0:T(8,128)(2,1)S(1)}) custom-call(bf16[32,2048]{1,0:T(8,128)(2,1)S(1)} %collective-permute-done.4.refs_0_, bf16[32,2048]{1,0:T(8,128)(2,1)S(1)} %collective-permute-done.5.refs_1_, bf16[32,2048]{1,0:T(8,128)(2,1)S(1)} %collective-permute-done.6.refs_2_, ...), custom_call_target="tpu_custom_call" | custom-call | flops 704643072 | bytes 1048576 | tf_op jit(solution)/shard_map/beside_rows/pallas_call | solution.py:467
  19.8 2.8 %last_rows.1 = (bf16[256,768]{1,0:T(8,128)(2,1)S(1)}, bf16[32,2048]{1,0:T(8,128)(2,1)S(1)}, f32[32,2048]{1,0:T(8,128)S(1)}) custom-call(bf16[32,2048]{1,0:T(8,128)(2,1)S(1)} %collective-permute-done.2.refs_0_, bf16[32,2048]{1,0:T(8,128)(2,1)S(1)} %collective-permute-done.3.refs_1_, f32[1,2048]{1,0:T(1,128)S(1)} %get-tuple-element.47.refs_2_.refs_3_, ...), custom_call_target="tpu_custom_call" | custom-call | flops 805306368 | bytes 1048576 | tf_op jit(solution)/shard_map/last_rows/pallas_call | solution.py:537
  22.7 0.6 %collective-permute-start.7 = (bf16[32,2048]{1,0:T(8,128)(2,1)S(1)}, bf16[32,2048]{1,0:T(8,128)(2,1)S(1)}, u32[]{:S(2)}, u32[]{:S(2)}) collective-permute-start(bf16[32,2048]{1,0:T(8,128)(2,1)S(1)} %get-tuple-element.63), channel_id=1, source_target_pairs={{0,1},{1,0},{2,3},{3,2},{4,5},{5,4},{6,7},{7,6},{8,9},{9,8},{10,11... | collective-permute-start | bytes 393224 | tf_op jit(solution)/shard_map/ppermute | solution.py:235
  23.2 1.4 %second_rows.1 = (bf16[32,2048]{1,0:T(8,128)(2,1)S(1)}, f32[32,2048]{1,0:T(8,128)S(1)}) custom-call(bf16[256,768]{1,0:T(8,128)(2,1)S(1)} %get-tuple-element.69.joined_ref, f32[256,128]{1,0:T(8,128)S(1)} %get-tuple-element.58.refs_8_.offsets_ref, bf16[256,2048]{1,0:T(8,128)(2,1)S(1)} %get-tuple-element.57.refs_7_.output_ref, ...), custom_call_target="tpu_custom_call" | custom-call | flops 335544320 | bytes 1048576 | tf_op jit(solution)/shard_map/second_rows/pallas_call | solution.py:581
  24.7 0.8 %collective-permute-start.13 = (bf16[32,2048]{1,0:T(8,128)(2,1)S(1)}, bf16[32,2048]{1,0:T(8,128)(2,1)S(1)}, u32[]{:S(2)}, u32[]{:S(2)}) collective-permute-start(bf16[32,2048]{1,0:T(8,128)(2,1)S(1)} %third_added.1), channel_id=1, source_target_pairs={{0,2},{1,3},{2,0},{3,1},{4,6},{5,7},{6,4},{7,5},{8,10},{9,11},{10,... | collective-permute-start | bytes 393224 | tf_op jit(solution)/shard_map/ppermute | solution.py:235
  25.4 0.2 collective-permute-start.14
  25.6 1.2 %near_rows.1 = (bf16[32,2048]{1,0:T(8,128)(2,1)S(1)}, bf16[32,2048]{1,0:T(8,128)(2,1)S(1)}, f32[32,2048]{1,0:T(8,128)S(1)}, f32[32,2048]{1,0:T(8,128)S(1)}) custom-call(bf16[256,768]{1,0:T(8,128)(2,1)S(1)} %get-tuple-element.69.joined_ref, f32[256,128]{1,0:T(8,128)S(1)} %get-tuple-element.58.refs_8_.offsets_ref, ...), custom_call_target="tpu_custom_call" | custom-call | flops 671088640 | bytes 1048576 | tf_op jit(solution)/shard_map/near_rows/pallas_call | solution.py:581
  26.9 0.4 collective-permute-start.8
  27.2 0.2 collective-permute-start.9
  27.4 1.2 %cached_pages.1 = (bf16[8,16,512]{2,1,0:T(8,128)(2,1)S(1)}, bf16[8,16,512]{2,1,0:T(8,128)(2,1)S(1)}, bf16[8,16,512]{2,1,0:T(8,128)(2,1)S(1)}, bf16[8,16,512]{2,1,0:T(8,128)(2,1)S(1)}) custom-call(bf16[256,768]{1,0:T(8,128)(2,1)S(1)} %get-tuple-element.69.joined_ref, s32[16]{0:T(128)} %bitcast.5), custom_call_target="tpu_custom_call" | custom-call | bytes 1048576 | tf_op jit(solution)/shard_map/cached_pages/pallas_call | solution.py:632
  28.7 1.6 %collective-permute-start.10 = (bf16[8,16,512]{2,1,0:T(8,128)(2,1)S(1)}, bf16[8,16,512]{2,1,0:T(8,128)(2,1)S(1)}, u32[]{:S(2)}, u32[]{:S(2)}) collective-permute-start(bf16[8,16,512]{2,1,0:T(8,128)(2,1)S(1)} %get-tuple-element.77), channel_id=1, source_target_pairs={{0,8},{8,0},{16,24},{24,16},{1,9},{9,1},{17,25},{25,17},{2,10},{10... | collective-permute-start | bytes 393224 | tf_op jit(solution)/shard_map/ppermute | solution.py:235
  30.2 1.5 %collective-permute-start.11 = (bf16[8,16,512]{2,1,0:T(8,128)(2,1)S(1)}, bf16[8,16,512]{2,1,0:T(8,128)(2,1)S(1)}, u32[]{:S(2)}, u32[]{:S(2)}) collective-permute-start(bf16[8,16,512]{2,1,0:T(8,128)(2,1)S(1)} %get-tuple-element.78), channel_id=1, source_target_pairs={{0,16},{8,24},{16,0},{24,8},{1,17},{9,25},{17,1},{25,9},{2,18},{10... | collective-permute-start | bytes 393224 | tf_op jit(solution)/shard_map/ppermute | solution.py:235
  31.7 1.4 %collective-permute-start.12 = (bf16[8,16,512]{2,1,0:T(8,128)(2,1)S(1)}, bf16[8,16,512]{2,1,0:T(8,128)(2,1)S(1)}, u32[]{:S(2)}, u32[]{:S(2)}) collective-permute-start(bf16[8,16,512]{2,1,0:T(8,128)(2,1)S(1)} %get-tuple-element.79), channel_id=1, source_target_pairs={{0,24},{8,16},{16,8},{24,0},{1,25},{9,17},{17,9},{25,1},{2,26},{10... | collective-permute-start | bytes 393224 | tf_op jit(solution)/shard_map/ppermute | solution.py:235
  33.2 2.2 %collective-permute-start.15 = (bf16[32,2048]{1,0:T(8,128)(2,1)S(1)}, bf16[32,2048]{1,0:T(8,128)(2,1)S(1)}, u32[]{:S(2)}, u32[]{:S(2)}) collective-permute-start(bf16[32,2048]{1,0:T(8,128)(2,1)S(1)} %second_added.1), channel_id=1, source_target_pairs={{0,4},{1,5},{2,6},{3,7},{4,0},{5,1},{6,2},{7,3},{8,12},{9,13},{10,... | collective-permute-start | bytes 393224 | tf_op jit(solution)/shard_map/ppermute | solution.py:235
  35.4 0.1 near_sums.1
  35.5 0.9 %collective-permute-start.16 = (bf16[32,2048]{1,0:T(8,128)(2,1)S(1)}, bf16[32,2048]{1,0:T(8,128)(2,1)S(1)}, u32[]{:S(2)}, u32[]{:S(2)}) collective-permute-start(bf16[32,2048]{1,0:T(8,128)(2,1)S(1)} %get-tuple-element.84), channel_id=1, source_target_pairs={{0,2},{1,3},{2,0},{3,1},{4,6},{5,7},{6,4},{7,5},{8,10},{9,11},{10,... | collective-permute-start | bytes 393224 | tf_op jit(solution)/shard_map/ppermute | solution.py:235
  36.4 2.1 %collective-permute-done.11.refs_2_ = bf16[8,16,512]{2,1,0:T(8,128)(2,1)S(1)} collective-permute-done((bf16[8,16,512]{2,1,0:T(8,128)(2,1)S(1)}, bf16[8,16,512]{2,1,0:T(8,128)(2,1)S(1)}, u32[]{:S(2)}, u32[]{:S(2)}) %collective-permute-start.11) | collective-permute-done | bytes 131104 | tf_op jit(solution)/shard_map/ppermute | solution.py:235
  38.5 0.8 %placed.1 = bf16[1,4,8,16,512]{4,3,2,1,0:T(8,128)(2,1)} custom-call(bf16[8,16,512]{2,1,0:T(8,128)(2,1)S(1)} %get-tuple-element.76.refs_0_, bf16[8,16,512]{2,1,0:T(8,128)(2,1)S(1)} %collective-permute-done.10.refs_1_, bf16[8,16,512]{2,1,0:T(8,128)(2,1)S(1)} %collective-permute-done.11.refs_2_, bf16[8,16,512]{2,1,0:T(8,128)(2,1)S(1)} %collective-permute-done.12.refs_3_), custom_call_target="tpu_custom_call" | custom-call | tf_op jit(solution)/shard_map/placed/pallas_call | solution.py:702
  39.3 1.8 %collective-permute-done.15.refs_0_ = bf16[32,2048]{1,0:T(8,128)(2,1)S(1)} collective-permute-done((bf16[32,2048]{1,0:T(8,128)(2,1)S(1)}, bf16[32,2048]{1,0:T(8,128)(2,1)S(1)}, u32[]{:S(2)}, u32[]{:S(2)}) %collective-permute-start.15) | collective-permute-done | bytes 131104 | tf_op jit(solution)/shard_map/ppermute | solution.py:235
  41.1 0.3 collective-permute-done.16.refs_1_
  41.4 0.7 %finished.1 = f32[32,2048]{1,0:T(8,128)} custom-call(f32[32,2048]{1,0:T(8,128)S(1)} %get-tuple-element.80.base_ref, bf16[32,2048]{1,0:T(8,128)(2,1)S(1)} %collective-permute-done.15.refs_0_, bf16[32,2048]{1,0:T(8,128)(2,1)S(1)} %collective-permute-done.16.refs_1_), custom_call_target="tpu_custom_call" | custom-call | tf_op jit(solution)/shard_map/finished/pallas_call | solution.py:721
  (16 shorter events, 0.1 us)
Async XLA Ops:
  0.6 12.5 %copy-start = (bf16[32,2048]{1,0:T(8,128)(2,1)S(1)}, bf16[32,2048]{1,0:T(8,128)(2,1)}, u32[]{:S(2)}) copy-start(bf16[32,2048]{1,0:T(8,128)(2,1)} %refs_1_.1) | copy-start | bytes 393220
  0.6 10.0 %collective-permute-start.1 = (bf16[32,2048]{1,0:T(8,128)(2,1)}, bf16[32,2048]{1,0:T(8,128)(2,1)S(1)}, u32[]{:S(2)}, u32[]{:S(2)}) collective-permute-start(bf16[32,2048]{1,0:T(8,128)(2,1)} %refs_1_.1), channel_id=1, source_target_pairs={{0,2},{1,3},{2,0},{3,1},{4,6},{5,7},{6,4},{7,5},{8,10},{9,11},{10,... | collective-permute-start | bytes 393224 | tf_op jit(solution)/shard_map/ppermute | solution.py:235
  3.7 8.9 %collective-permute-start = (bf16[32,2048]{1,0:T(8,128)(2,1)}, bf16[32,2048]{1,0:T(8,128)(2,1)S(1)}, u32[]{:S(2)}, u32[]{:S(2)}) collective-permute-start(bf16[32,2048]{1,0:T(8,128)(2,1)} %refs_1_.1), channel_id=1, source_target_pairs={{0,4},{1,5},{2,6},{3,7},{4,0},{5,1},{6,2},{7,3},{8,12},{9,13},{10,... | collective-permute-start | bytes 393224 | tf_op jit(solution)/shard_map/ppermute | solution.py:235
  12.7 5.0 %collective-permute-start.2 = (bf16[32,2048]{1,0:T(8,128)(2,1)S(1)}, bf16[32,2048]{1,0:T(8,128)(2,1)S(1)}, u32[]{:S(2)}, u32[]{:S(2)}) collective-permute-start(bf16[32,2048]{1,0:T(8,128)(2,1)S(1)} %collective-permute-done.refs_0_), channel_id=1, source_target_pairs={{0,2},{1,3},{2,0},{3,1},{4,6},{5,7},{6,4},{7,5},{8,10},{9,11},{10,... | collective-permute-start | bytes 393224 | tf_op jit(solution)/shard_map/ppermute | solution.py:235
  13.1 4.5 %collective-permute-start.4 = (bf16[32,2048]{1,0:T(8,128)(2,1)S(1)}, bf16[32,2048]{1,0:T(8,128)(2,1)S(1)}, u32[]{:S(2)}, u32[]{:S(2)}) collective-permute-start(bf16[32,2048]{1,0:T(8,128)(2,1)S(1)} %copy-done), channel_id=1, source_target_pairs={{0,1},{1,0},{2,3},{3,2},{4,5},{5,4},{6,7},{7,6},{8,9},{9,8},{10,11... | collective-permute-start | bytes 393224 | tf_op jit(solution)/shard_map/ppermute | solution.py:235
  13.1 4.5 %collective-permute-start.5 = (bf16[32,2048]{1,0:T(8,128)(2,1)S(1)}, bf16[32,2048]{1,0:T(8,128)(2,1)S(1)}, u32[]{:S(2)}, u32[]{:S(2)}) collective-permute-start(bf16[32,2048]{1,0:T(8,128)(2,1)S(1)} %collective-permute-done.1.refs_1_), channel_id=1, source_target_pairs={{0,1},{1,0},{2,3},{3,2},{4,5},{5,4},{6,7},{7,6},{8,9},{9,8},{10,11... | collective-permute-start | bytes 393224 | tf_op jit(solution)/shard_map/ppermute | solution.py:235
  13.6 4.0 %collective-permute-start.6 = (bf16[32,2048]{1,0:T(8,128)(2,1)S(1)}, bf16[32,2048]{1,0:T(8,128)(2,1)S(1)}, u32[]{:S(2)}, u32[]{:S(2)}) collective-permute-start(bf16[32,2048]{1,0:T(8,128)(2,1)S(1)} %collective-permute-done.refs_0_), channel_id=1, source_target_pairs={{0,1},{1,0},{2,3},{3,2},{4,5},{5,4},{6,7},{7,6},{8,9},{9,8},{10,11... | collective-permute-start | bytes 393224 | tf_op jit(solution)/shard_map/ppermute | solution.py:235
  17.6 2.2 %collective-permute-start.3 = (bf16[32,2048]{1,0:T(8,128)(2,1)S(1)}, bf16[32,2048]{1,0:T(8,128)(2,1)S(1)}, u32[]{:S(2)}, u32[]{:S(2)}) collective-permute-start(bf16[32,2048]{1,0:T(8,128)(2,1)S(1)} %collective-permute-done.2.refs_0_), channel_id=1, source_target_pairs={{0,1},{1,0},{2,3},{3,2},{4,5},{5,4},{6,7},{7,6},{8,9},{9,8},{10,11... | collective-permute-start | bytes 393224 | tf_op jit(solution)/shard_map/ppermute | solution.py:235
  22.7 2.0 %collective-permute-start.7 = (bf16[32,2048]{1,0:T(8,128)(2,1)S(1)}, bf16[32,2048]{1,0:T(8,128)(2,1)S(1)}, u32[]{:S(2)}, u32[]{:S(2)}) collective-permute-start(bf16[32,2048]{1,0:T(8,128)(2,1)S(1)} %get-tuple-element.63), channel_id=1, source_target_pairs={{0,1},{1,0},{2,3},{3,2},{4,5},{5,4},{6,7},{7,6},{8,9},{9,8},{10,11... | collective-permute-start | bytes 393224 | tf_op jit(solution)/shard_map/ppermute | solution.py:235
  24.7 5.6 %collective-permute-start.13 = (bf16[32,2048]{1,0:T(8,128)(2,1)S(1)}, bf16[32,2048]{1,0:T(8,128)(2,1)S(1)}, u32[]{:S(2)}, u32[]{:S(2)}) collective-permute-start(bf16[32,2048]{1,0:T(8,128)(2,1)S(1)} %third_added.1), channel_id=1, source_target_pairs={{0,2},{1,3},{2,0},{3,1},{4,6},{5,7},{6,4},{7,5},{8,10},{9,11},{10,... | collective-permute-start | bytes 393224 | tf_op jit(solution)/shard_map/ppermute | solution.py:235
  25.4 6.3 %collective-permute-start.14 = (bf16[32,2048]{1,0:T(8,128)(2,1)S(1)}, bf16[32,2048]{1,0:T(8,128)(2,1)S(1)}, u32[]{:S(2)}, u32[]{:S(2)}) collective-permute-start(bf16[32,2048]{1,0:T(8,128)(2,1)S(1)} %get-tuple-element.83), channel_id=1, source_target_pairs={{0,1},{1,0},{2,3},{3,2},{4,5},{5,4},{6,7},{7,6},{8,9},{9,8},{10,11... | collective-permute-start | bytes 393224 | tf_op jit(solution)/shard_map/ppermute | solution.py:235
  26.9 6.3 %collective-permute-start.8 = (bf16[32,2048]{1,0:T(8,128)(2,1)S(1)}, bf16[32,2048]{1,0:T(8,128)(2,1)S(1)}, u32[]{:S(2)}, u32[]{:S(2)}) collective-permute-start(bf16[32,2048]{1,0:T(8,128)(2,1)S(1)} %get-tuple-element.71), channel_id=1, source_target_pairs={{0,1},{1,0},{2,3},{3,2},{4,5},{5,4},{6,7},{7,6},{8,9},{9,8},{10,11... | collective-permute-start | bytes 393224 | tf_op jit(solution)/shard_map/ppermute | solution.py:235
  27.2 8.1 %collective-permute-start.9 = (bf16[32,2048]{1,0:T(8,128)(2,1)S(1)}, bf16[32,2048]{1,0:T(8,128)(2,1)S(1)}, u32[]{:S(2)}, u32[]{:S(2)}) collective-permute-start(bf16[32,2048]{1,0:T(8,128)(2,1)S(1)} %get-tuple-element.73), channel_id=1, source_target_pairs={{0,1},{1,0},{2,3},{3,2},{4,5},{5,4},{6,7},{7,6},{8,9},{9,8},{10,11... | collective-permute-start | bytes 393224 | tf_op jit(solution)/shard_map/ppermute | solution.py:235
  28.7 7.7 %collective-permute-start.10 = (bf16[8,16,512]{2,1,0:T(8,128)(2,1)S(1)}, bf16[8,16,512]{2,1,0:T(8,128)(2,1)S(1)}, u32[]{:S(2)}, u32[]{:S(2)}) collective-permute-start(bf16[8,16,512]{2,1,0:T(8,128)(2,1)S(1)} %get-tuple-element.77), channel_id=1, source_target_pairs={{0,8},{8,0},{16,24},{24,16},{1,9},{9,1},{17,25},{25,17},{2,10},{10... | collective-permute-start | bytes 393224 | tf_op jit(solution)/shard_map/ppermute | solution.py:235
  30.2 8.2 %collective-permute-start.11 = (bf16[8,16,512]{2,1,0:T(8,128)(2,1)S(1)}, bf16[8,16,512]{2,1,0:T(8,128)(2,1)S(1)}, u32[]{:S(2)}, u32[]{:S(2)}) collective-permute-start(bf16[8,16,512]{2,1,0:T(8,128)(2,1)S(1)} %get-tuple-element.78), channel_id=1, source_target_pairs={{0,16},{8,24},{16,0},{24,8},{1,17},{9,25},{17,1},{25,9},{2,18},{10... | collective-permute-start | bytes 393224 | tf_op jit(solution)/shard_map/ppermute | solution.py:235
  31.7 6.7 %collective-permute-start.12 = (bf16[8,16,512]{2,1,0:T(8,128)(2,1)S(1)}, bf16[8,16,512]{2,1,0:T(8,128)(2,1)S(1)}, u32[]{:S(2)}, u32[]{:S(2)}) collective-permute-start(bf16[8,16,512]{2,1,0:T(8,128)(2,1)S(1)} %get-tuple-element.79), channel_id=1, source_target_pairs={{0,24},{8,16},{16,8},{24,0},{1,25},{9,17},{17,9},{25,1},{2,26},{10... | collective-permute-start | bytes 393224 | tf_op jit(solution)/shard_map/ppermute | solution.py:235
  33.2 7.9 %collective-permute-start.15 = (bf16[32,2048]{1,0:T(8,128)(2,1)S(1)}, bf16[32,2048]{1,0:T(8,128)(2,1)S(1)}, u32[]{:S(2)}, u32[]{:S(2)}) collective-permute-start(bf16[32,2048]{1,0:T(8,128)(2,1)S(1)} %second_added.1), channel_id=1, source_target_pairs={{0,4},{1,5},{2,6},{3,7},{4,0},{5,1},{6,2},{7,3},{8,12},{9,13},{10,... | collective-permute-start | bytes 393224 | tf_op jit(solution)/shard_map/ppermute | solution.py:235
  35.5 5.9 %collective-permute-start.16 = (bf16[32,2048]{1,0:T(8,128)(2,1)S(1)}, bf16[32,2048]{1,0:T(8,128)(2,1)S(1)}, u32[]{:S(2)}, u32[]{:S(2)}) collective-permute-start(bf16[32,2048]{1,0:T(8,128)(2,1)S(1)} %get-tuple-element.84), channel_id=1, source_target_pairs={{0,2},{1,3},{2,0},{3,1},{4,6},{5,7},{6,4},{7,5},{8,10},{9,11},{10,... | collective-permute-start | bytes 393224 | tf_op jit(solution)/shard_map/ppermute | solution.py:235

commit v5 on v4

--- a/solution.py
+++ b/solution.py
@@ -373,6 +373,26 @@
     sine_up_ref[...] = jnp.where((lane >= half) & (lane < ROT), sine, 0.0)
 
 
+def make_destinations(targets_ref, destinations_ref, replica_count, block_rows):
+    page_count = targets_ref.shape[1]
+    tokens = destinations_ref.shape[1]
+    capacity = 2 * page_count // replica_count
+    square = (page_count, page_count)
+    rows = lax.broadcasted_iota(jnp.int32, square, 0)
+    columns = lax.broadcasted_iota(jnp.int32, square, 1)
+    across = jnp.broadcast_to(targets_ref[...], square).astype(jnp.float32)
+    down = jnp.sum(jnp.where(rows == columns, across, 0.0), axis=1, keepdims=True)
+    earlier = jnp.where((across == down) & (columns < rows), 1.0, 0.0)
+    slots = jnp.sum(earlier, axis=1, keepdims=True).astype(jnp.int32)
+    slots = (down.astype(jnp.int32) ^ lax.axis_index("dp")) * capacity + slots
+    positions = positions_along(0, (1, tokens), 1, block_rows)
+    bits = PAGE.bit_length() - 1
+    pages = lax.broadcasted_iota(jnp.int32, (page_count, tokens), 0)
+    chosen = jnp.where(pages == positions >> bits, slots.astype(jnp.float32), 0.0)
+    slot = jnp.sum(chosen, axis=0, keepdims=True).astype(jnp.int32)
+    destinations_ref[...] = slot * PAGE + (positions & (PAGE - 1))
+
+
 def copies_in(sources, targets, sems):
     copies = []
     for number, (source, target) in enumerate(zip(sources, targets)):
@@ -395,38 +415,42 @@
         copy.wait()
 
 
-def own_kernel(count, *refs):
+def own_kernel(count, replica_count, *refs):
     sources, targets = refs[:count], refs[count : 2 * count]
-    offsets_ref, *table_refs, joined_ref, hidden_ref = refs[2 * count : 2 * count + 6]
-    attention_scr, feedforward_scr, sems = refs[2 * count + 6 :]
+    offsets_ref, *table_refs, destinations_ref, joined_ref, hidden_ref = refs[2 * count : -3]
+    attention_scr, feedforward_scr, sems = refs[-3:]
     copies = copies_in(sources, targets, sems)
-    segments_ref, states_ref, *gain_refs, heads_ref, upward_ref = targets
+    segments_ref, targets_ref, states_ref, *gain_refs, heads_ref, upward_ref, _ = targets
     block_rows = states_ref.shape[0]
     wait_for(copies[0])
     make_tables(segments_ref, offsets_ref, *table_refs)
-    for number in (1, 2, 3):
+    wait_for(copies[1])
+    make_destinations(targets_ref, destinations_ref, replica_count, block_rows)
+    for number in (2, 3, 4):
         wait_for(copies[number])
     normalize([states_ref], gain_refs, [attention_scr, feedforward_scr])
-    wait_for(copies[4])
+    wait_for(copies[5])
     places = [position_of(0, 0, block_rows)]
     project(attention_scr, heads_ref, table_refs, places, joined_ref, 0)
-    wait_for(copies[5])
+    wait_for(copies[6])
     hide(feedforward_scr, upward_ref, hidden_ref, 0)
-
-
-def own_rows(staged):
+    wait_for(copies[7])
+
+
+def own_rows(staged, replica_count):
     tokens = staged[0].shape[1]
-    rows, width = staged[1].shape
-    hidden_width = staged[5].shape[1]
+    rows, width = staged[2].shape
+    hidden_width = staged[6].shape[1]
     shapes = [pltpu.VMEM(array.shape, array.dtype) for array in staged]
     shapes += [pltpu.VMEM((tokens, 128), jnp.float32)] * 4
     shapes += [
+        pltpu.VMEM((1, tokens), jnp.int32),
         pltpu.VMEM((rows, 3 * HD), jnp.bfloat16),
         pltpu.VMEM((rows, hidden_width), jnp.bfloat16),
     ]
     count = len(staged)
     return pl.pallas_call(
-        functools.partial(own_kernel, count),
+        functools.partial(own_kernel, count, replica_count),
         out_shape=shapes,
         in_specs=[pl.BlockSpec(memory_space=pltpu.HBM)] * count,
         out_specs=vmem_specs(len(shapes)),
@@ -448,19 +472,20 @@
 def middle_kernel(origins, *refs):
     count = len(origins)
     blocks, (gain_a, gain_f, heads_ref, upward_ref) = refs[:count], refs[count : count + 4]
-    table_refs, source_ref = refs[count + 4 : count + 7], refs[count + 7]
-    joined_ref, hidden_ref, target_ref = refs[count + 8 : count + 11]
-    attention_scr, feedforward_scr, sems = refs[count + 11 :]
-    (copies,) = copies_in([source_ref], [target_ref], sems)
+    table_refs, refs = refs[count + 4 : count + 7], refs[count + 7 :]
+    staged = (len(refs) - 5) // 2
+    sources, (joined_ref, hidden_ref), refs = refs[:staged], refs[staged:][:2], refs[staged + 2 :]
+    targets, (attention_scr, feedforward_scr, sems) = refs[:staged], refs[staged:]
+    copies = copies_in(sources, targets, sems)
     block_rows = blocks[0].shape[0]
     normalize(blocks, [gain_a, gain_f], [attention_scr, feedforward_scr])
     places = [position_of(kind, half, block_rows) for kind, half in origins]
     project(attention_scr, heads_ref, table_refs, places, joined_ref, 0)
     hide(feedforward_scr, upward_ref, hidden_ref, 0)
-    wait_for(copies)
-
-
-def middle_rows(name, origins, blocks, gains, weights, tables, staged):
+    wait_for(sum(copies, []))
+
+
+def middle_rows(name, origins, blocks, gains, weights, tables, *staged):
     block_rows, width = blocks[0].shape
     rows = len(blocks) * block_rows
     hidden_width = weights[1].shape[1]
@@ -469,23 +494,24 @@
         out_shape=[
             pltpu.VMEM((rows, 3 * HD), jnp.bfloat16),
             pltpu.VMEM((rows, hidden_width), jnp.bfloat16),
-            pltpu.VMEM(staged.shape, staged.dtype),
-        ],
-        in_specs=vmem_specs(len(blocks) + 2 + 2 + 3) + [pl.BlockSpec(memory_space=pltpu.HBM)],
-        out_specs=vmem_specs(3),
+        ]
+        + [pltpu.VMEM(array.shape, array.dtype) for array in staged],
+        in_specs=vmem_specs(len(blocks) + 2 + 2 + 3)
+        + [pl.BlockSpec(memory_space=pltpu.HBM)] * len(staged),
+        out_specs=vmem_specs(2 + len(staged)),
         scratch_shapes=[
             pltpu.VMEM((rows, width), jnp.bfloat16),
             pltpu.VMEM((rows, width), jnp.bfloat16),
-            pltpu.SemaphoreType.DMA((1, 4)),
+            pltpu.SemaphoreType.DMA((max(len(staged), 1), 4)),
         ],
         compiler_params=parameters(12),
         cost_estimate=pl.CostEstimate(
             flops=2 * rows * width * (3 * HD + hidden_width),
-            bytes_accessed=staged.nbytes,
+            bytes_accessed=MIB,
             transcendentals=rows * hidden_width,
         ),
         name=name,
-    )(*blocks, *gains, *weights, *tables, in_hbm(staged))
+    )(*blocks, *gains, *weights, *tables, *[in_hbm(array) for array in staged])
 
 
 def last_kernel(*refs):
@@ -509,8 +535,9 @@
 
 
 def piece_of(pieces, kind, half, block_rows):
-    piece = 2 if half else min(kind, 1)
-    place = (kind if half else (0, 1, 0)[kind]) * block_rows
+    piece, place = (0, 2, 1)[kind], 0
+    if half:
+        piece, place = 2, (kind + 1) * block_rows
     return pieces[piece][place : place + block_rows, :]
 
 
@@ -593,57 +620,30 @@
     )(joined, offsets, output_weight, downward_weight, *pieces)
 
 
-def pages_kernel(block_rows, joined_ref, targets_ref, *refs):
-    pages_refs, (named_ref, counts_ref, slots_ref, sem) = refs[:-4], refs[-4:]
-    naming = pltpu.make_async_copy(targets_ref, named_ref, sem)
-    naming.start()
+def pages_kernel(joined_ref, destinations_ref, *page_refs):
     tokens = joined_ref.shape[0]
-    for page_ref in pages_refs:
-        page_ref[...] = jnp.zeros(page_ref.shape, page_ref.dtype)
-    chip, core = whereabouts()
-    group = lax.axis_index("dp")
-    naming.wait()
-    for target in range(len(pages_refs)):
-        counts_ref[target] = 0
-    for page in range(tokens // PAGE):
-        target = named_ref[page]
-        slot = counts_ref[target]
-        counts_ref[target] = slot + 1
-        slots_ref[page] = slot
-    capacity = pages_refs[0].shape[0]
-    for place in range(0, tokens, PAGE):
-        kind, half = place // (CORES * block_rows), (place // block_rows) % CORES
-        start = ((chip ^ kind) * CORES + (core ^ half)) * block_rows + place % block_rows
-        page = start // PAGE
-        target = named_ref[page]
-        slot = jnp.minimum(slots_ref[page], capacity - 1)
-        for mask, page_ref in enumerate(pages_refs):
-
-            @pl.when(target == (group ^ mask))
-            def _():
-                page_ref[pl.ds(slot, 1)] = joined_ref[place : place + PAGE, HD:][None]
-
-
-def cached_pages(joined, targets, replica_count):
+    slot_rows = page_refs[0].shape[0] * PAGE
+    for number, page_ref in enumerate(page_refs):
+        shape = (slot_rows, tokens)
+        row = number * slot_rows + lax.broadcasted_iota(jnp.int32, shape, 0)
+        placing = jnp.where(row == destinations_ref[...], 1.0, 0.0).astype(jnp.bfloat16)
+        rows = jnp.dot(placing, joined_ref[:, HD:], preferred_element_type=jnp.float32)
+        page_ref[...] = rows.astype(jnp.bfloat16).reshape(page_ref.shape)
+
+
+def cached_pages(joined, destinations, replica_count):
     tokens = joined.shape[0]
-    page_count = tokens // PAGE
-    capacity = 2 * page_count // replica_count
+    capacity = 2 * (tokens // PAGE) // replica_count
     shapes = [pltpu.VMEM((capacity, PAGE, 2 * HD), jnp.bfloat16)] * replica_count
     return pl.pallas_call(
-        functools.partial(pages_kernel, tokens // (CHIPS * CORES)),
+        pages_kernel,
         out_shape=shapes,
-        in_specs=vmem_specs(1) + [pl.BlockSpec(memory_space=pltpu.HBM)],
+        in_specs=vmem_specs(2),
         out_specs=vmem_specs(len(shapes)),
-        scratch_shapes=[
-            pltpu.SMEM(targets.shape, jnp.int32),
-            pltpu.SMEM((replica_count,), jnp.int32),
-            pltpu.SMEM((page_count,), jnp.int32),
-            pltpu.SemaphoreType.DMA(()),
-        ],
         compiler_params=parameters(8),
         cost_estimate=pl.CostEstimate(flops=0, bytes_accessed=MIB, transcendentals=0),
         name="cached_pages",
-    )(joined, in_hbm(targets))
+    )(joined, destinations)
 
 
 def add_kernel(*refs):
@@ -746,35 +746,32 @@
     beside = exchanged(hidden_states, "tensor", 1)
     staged = (
         segments,
+        page_targets.reshape(1, -1),
         hidden_states,
         attention_gain[None],
         feedforward_gain[None],
         heads_weight,
         upward_weight,
-    )
-    staged = own_rows(staged)
-    hidden, gains, (heads, upward), tables = staged[1], staged[2:4], staged[4:6], staged[6:10]
-    own_joined, own_hidden = staged[10:]
-
-    second, first, own_joined = lax.optimization_barrier((second, first, own_joined))
+        downward_weight,
+    )
+    staged = own_rows(staged, replica_count)
+    hidden, gains, weights, tables = staged[2], staged[3:5], staged[5:8], staged[8:12]
+    heads, upward, downward = weights
+    destinations, own_joined, own_hidden = staged[12:]
+
+    second, own_joined = lax.optimization_barrier((second, own_joined))
     third = exchanged(second, "tensor", to_chip[1])
     second_beside = exchanged(second, "tensor", 1)
     first_beside = exchanged(first, "tensor", 1)
-    there_joined, there_hidden, downward = middle_rows(
-        "there_rows",
-        ((2, 0), (1, 0)),
-        (second, first),
-        gains,
-        (heads, upward),
-        tables[1:],
-        downward_weight,
+    there_joined, there_hidden = middle_rows(
+        "there_rows", ((2, 0),), (second,), gains, (heads, upward), tables[1:]
     )
     third, there_joined = lax.optimization_barrier((third, there_joined))
     third_beside = exchanged(third, "tensor", 1)
     beside_joined, beside_hidden, output = middle_rows(
         "beside_rows",
-        ((0, 1), (1, 1), (2, 1)),
-        (beside, first_beside, second_beside),
+        ((1, 0), (0, 1), (1, 1), (2, 1)),
+        (first, beside, first_beside, second_beside),
         gains,
         (heads, upward),
         tables[1:],
@@ -804,14 +801,19 @@
     )
     first_received = exchanged(first_sibling, "tensor", 1)
     zero_received = exchanged(zero_sibling, "tensor", 1)
-    pages = cached_pages(joined, page_targets[:, 0], replica_count)
+    pages = cached_pages(joined, destinations, replica_count)
+    second_sum = added("second_added", second_own, passing, second_received)
+    second_sum, first_received = lax.optimization_barrier((second_sum, first_received))
+    from_second = exchanged(second_sum, "tensor", to_chip[2])
+    first_sum, base = near_sums((first_own, first_received), (zero_own, zero_received, hidden))
+    first_sum, pages = lax.optimization_barrier((first_sum, pages))
+    from_first = exchanged(first_sum, "tensor", to_chip[1])
     arriving = [pages[0]] + [
         exchanged(pages[mask], "dp", mask) for mask in range(1, replica_count)
     ]
-    second_sum = added("second_added", second_own, passing, second_received)
-    from_second = exchanged(second_sum, "tensor", to_chip[2])
-    first_sum, base = near_sums((first_own, first_received), (zero_own, zero_received, hidden))
-    from_first = exchanged(first_sum, "tensor", to_chip[1])
+    from_second, from_first, arriving = lax.optimization_barrier(
+        (from_second, from_first, arriving)
+    )
     cache_pages = placed(arriving)
     base, cache_pages = lax.optimization_barrier((base, cache_pages))
     return (finished(base, (from_second, from_first)), cache_pages)

time: 42.3 us -> 44.2 us (1.045)
  waiting for transfers between devices: 7.26 us -> 10.2 us
  Pallas kernels: 17.8 us -> 16.5 us
    ppermute x17, waiting for transfers between devices: 7.26 us -> 10.2 us  [exchanged(): lax.ppermute(block, axis, [(member, member ^ mask) for member in range(co...]
    pallas_call x2, Pallas kernels: 5.17 us -> 3.7 us  [middle_rows(): pl.pallas_call(functools.partial(middle_kernel, origins), out_shape=[pltp...]
  transfers between devices with their start and end apart: 17 -> 17, of which waited for: 5 -> 6; matrix products, arithmetic and copies ran while one was open for 0% -> 0% of each run, Pallas kernels for 34% -> 27%
where the time goes in v5:
time: 44.2 us; the launch traced here: 44.1 us
  starting transfers between devices  16.6 us (38%)
  Pallas kernels  16.5 us (37%)
  waiting for transfers between devices  10.2 us (23%)
  between operations  0.76 us (2%)
    ppermute x17, starting transfers between devices, exchanged(): lax.ppermute(block, axis, [(member, member ^ mask) for member in range(co...  16.6 us
    ppermute x17, waiting for transfers between devices, exchanged(): lax.ppermute(block, axis, [(member, member ^ mask) for member in range(co...  10.2 us
    pallas_call x1, Pallas kernels, own_rows(): pl.pallas_call(functools.partial(own_kernel, count, replica_count), out_s...  5.3 us
    pallas_call x2, Pallas kernels, middle_rows(): pl.pallas_call(functools.partial(middle_kernel, origins), out_shape=[pltp...  3.7 us
    pallas_call x1, Pallas kernels, last_rows(): pl.pallas_call(last_kernel, out_shape=[pltpu.VMEM((tokens, 3 * HD), jnp.b...  2.84 us
    pallas_call x2, Pallas kernels, kind_rows(): pl.pallas_call(functools.partial(kind_kernel, kinds), out_shape=[pltpu.VM...  2.64 us
  transfers between devices with their start and end apart: 17, of which 6 were waited for; matrix products, arithmetic and copies ran while one was open for 0% of the time, Pallas kernels for 27%

profile of v5, /device:TPU:0, one launch (start us, length us, event | category | flops | bytes accessed | tf_op | source)
XLA Modules:
  0.0 44.1 jit_solution(8772024386862365830)
XLA Ops:
  0.6 4.1 %collective-permute-start = (bf16[32,2048]{1,0:T(8,128)(2,1)}, bf16[32,2048]{1,0:T(8,128)(2,1)S(1)}, u32[]{:S(2)}, u32[]{:S(2)}) collective-permute-start(bf16[32,2048]{1,0:T(8,128)(2,1)} %refs_2_.1), channel_id=1, source_target_pairs={{0,4},{1,5},{2,6},{3,7},{4,0},{5,1},{6,2},{7,3},{8,12},{9,13},{10,... | collective-permute-start | bytes 393224 | tf_op jit(solution)/shard_map/ppermute | solution.py:235
  4.7 1.6 %collective-permute-start.3 = (bf16[32,2048]{1,0:T(8,128)(2,1)}, bf16[32,2048]{1,0:T(8,128)(2,1)S(1)}, u32[]{:S(2)}, u32[]{:S(2)}) collective-permute-start(bf16[32,2048]{1,0:T(8,128)(2,1)} %refs_2_.1), channel_id=1, source_target_pairs={{0,2},{1,3},{2,0},{3,1},{4,6},{5,7},{6,4},{7,5},{8,10},{9,11},{10,... | collective-permute-start | bytes 393224 | tf_op jit(solution)/shard_map/ppermute | solution.py:235
  6.3 5.3 %own_rows.1 = (s32[1,256]{1,0:T(1,128)}, s32[1,16]{1,0:T(1,128)}, bf16[32,2048]{1,0:T(8,128)(2,1)S(1)}, f32[1,2048]{1,0:T(1,128)S(1)}, f32[1,2048]{1,0:T(1,128)S...) custom-call(s32[1,256]{1,0:T(1,128)} %refs_0_.1, ...), custom_call_target="tpu_custom_call" | custom-call | flops 234881024 | bytes 11682880 | tf_op jit(solution)/shard_map/own_rows/pallas_call | solution.py:452
  11.6 0.5 %collective-permute-start.1 = (bf16[32,2048]{1,0:T(8,128)(2,1)S(1)}, bf16[32,2048]{1,0:T(8,128)(2,1)S(1)}, u32[]{:S(2)}, u32[]{:S(2)}) collective-permute-start(bf16[32,2048]{1,0:T(8,128)(2,1)S(1)} %collective-permute-done.refs_0_), channel_id=1, source_target_pairs={{0,2},{1,3},{2,0},{3,1},{4,6},{5,7},{6,4},{7,5},{8,10},{9,11},{10,... | collective-permute-start | bytes 393224 | tf_op jit(solution)/shard_map/ppermute | solution.py:235
  12.2 0.5 %collective-permute-start.5 = (bf16[32,2048]{1,0:T(8,128)(2,1)S(1)}, bf16[32,2048]{1,0:T(8,128)(2,1)S(1)}, u32[]{:S(2)}, u32[]{:S(2)}) collective-permute-start(bf16[32,2048]{1,0:T(8,128)(2,1)S(1)} %collective-permute-done.3.refs_0_), channel_id=1, source_target_pairs={{0,1},{1,0},{2,3},{3,2},{4,5},{5,4},{6,7},{7,6},{8,9},{9,8},{10,11... | collective-permute-start | bytes 393224 | tf_op jit(solution)/shard_map/ppermute | solution.py:235
  12.7 0.1 collective-permute-start.6
  12.7 1.6 %there_rows.1 = (bf16[32,768]{1,0:T(8,128)(2,1)S(1)}, bf16[32,1024]{1,0:T(8,128)(2,1)S(1)}) custom-call(bf16[32,2048]{1,0:T(8,128)(2,1)S(1)} %collective-permute-done.refs_0_, f32[1,2048]{1,0:T(1,128)S(1)} %get-tuple-element.59.refs_1_.refs_4_.refs_2_, f32[1,2048]{1,0:T(1,128)S(1)} %get-tuple-element.60.refs_2_.refs_5_.refs_3_, ...), custom_call_target="tpu_custom_call" | custom-call | flops 234881024 | bytes 1048576 | tf_op jit(solution)/shard_map/there_rows/pallas_call | solution.py:492
  14.3 2.3 %collective-permute-done.1.refs_0_ = bf16[32,2048]{1,0:T(8,128)(2,1)S(1)} collective-permute-done((bf16[32,2048]{1,0:T(8,128)(2,1)S(1)}, bf16[32,2048]{1,0:T(8,128)(2,1)S(1)}, u32[]{:S(2)}, u32[]{:S(2)}) %collective-permute-start.1) | collective-permute-done | bytes 131104 | tf_op jit(solution)/shard_map/ppermute | solution.py:235
  16.7 0.0 collective-permute-start.2
  16.7 0.0 collective-permute-done.4.refs_1_
  16.7 2.1 %beside_rows.1 = (bf16[128,768]{1,0:T(8,128)(2,1)S(1)}, bf16[128,1024]{1,0:T(8,128)(2,1)S(1)}, bf16[256,2048]{1,0:T(8,128)(2,1)S(1)}) custom-call(bf16[32,2048]{1,0:T(8,128)(2,1)S(1)} %collective-permute-done.3.refs_0_, bf16[32,2048]{1,0:T(8,128)(2,1)S(1)} %collective-permute-done.4.refs_1_, bf16[32,2048]{1,0:T(8,128)(2,1)S(1)} %collective-permute-done.5.refs_2_, ...), custom_call_target="tpu_custom_call" | custom-call | flops 939524096 | bytes 1048576 | tf_op jit(solution)/shard_map/beside_rows/pallas_call | solution.py:492
  18.8 2.8 %last_rows.1 = (bf16[256,768]{1,0:T(8,128)(2,1)S(1)}, bf16[32,2048]{1,0:T(8,128)(2,1)S(1)}, f32[32,2048]{1,0:T(8,128)S(1)}) custom-call(bf16[32,2048]{1,0:T(8,128)(2,1)S(1)} %collective-permute-done.1.refs_0_, bf16[32,2048]{1,0:T(8,128)(2,1)S(1)} %collective-permute-done.2.refs_1_, f32[1,2048]{1,0:T(1,128)S(1)} %get-tuple-element.59.refs_1_.refs_4_.refs_2_, ...), custom_call_target="tpu_custom_call" | custom-call | flops 805306368 | bytes 1048576 | tf_op jit(solution)/shard_map/last_rows/pallas_call | solution.py:564
  21.6 0.5 %collective-permute-start.7 = (bf16[32,2048]{1,0:T(8,128)(2,1)S(1)}, bf16[32,2048]{1,0:T(8,128)(2,1)S(1)}, u32[]{:S(2)}, u32[]{:S(2)}) collective-permute-start(bf16[32,2048]{1,0:T(8,128)(2,1)S(1)} %get-tuple-element.75), channel_id=1, source_target_pairs={{0,1},{1,0},{2,3},{3,2},{4,5},{5,4},{6,7},{7,6},{8,9},{9,8},{10,11... | collective-permute-start | bytes 393224 | tf_op jit(solution)/shard_map/ppermute | solution.py:235
  22.2 1.4 %second_rows.1 = (bf16[32,2048]{1,0:T(8,128)(2,1)S(1)}, f32[32,2048]{1,0:T(8,128)S(1)}) custom-call(bf16[256,768]{1,0:T(8,128)(2,1)S(1)} %get-tuple-element.81.joined_ref, f32[256,128]{1,0:T(8,128)S(1)} %get-tuple-element.70.refs_8_.offsets_ref, bf16[256,2048]{1,0:T(8,128)(2,1)S(1)} %get-tuple-element.69.refs_7_.output_ref, ...), custom_call_target="tpu_custom_call" | custom-call | flops 335544320 | bytes 1048576 | tf_op jit(solution)/shard_map/second_rows/pallas_call | solution.py:608
  23.6 0.9 %collective-permute-start.8 = (bf16[32,2048]{1,0:T(8,128)(2,1)S(1)}, bf16[32,2048]{1,0:T(8,128)(2,1)S(1)}, u32[]{:S(2)}, u32[]{:S(2)}) collective-permute-start(bf16[32,2048]{1,0:T(8,128)(2,1)S(1)} %third_added.1), channel_id=1, source_target_pairs={{0,2},{1,3},{2,0},{3,1},{4,6},{5,7},{6,4},{7,5},{8,10},{9,11},{10,... | collective-permute-start | bytes 393224 | tf_op jit(solution)/shard_map/ppermute | solution.py:235
  24.5 1.2 %near_rows.1 = (bf16[32,2048]{1,0:T(8,128)(2,1)S(1)}, bf16[32,2048]{1,0:T(8,128)(2,1)S(1)}, f32[32,2048]{1,0:T(8,128)S(1)}, f32[32,2048]{1,0:T(8,128)S(1)}) custom-call(bf16[256,768]{1,0:T(8,128)(2,1)S(1)} %get-tuple-element.81.joined_ref, f32[256,128]{1,0:T(8,128)S(1)} %get-tuple-element.70.refs_8_.offsets_ref, ...), custom_call_target="tpu_custom_call" | custom-call | flops 671088640 | bytes 1048576 | tf_op jit(solution)/shard_map/near_rows/pallas_call | solution.py:608
  25.8 0.6 %collective-permute-start.10 = (bf16[32,2048]{1,0:T(8,128)(2,1)S(1)}, bf16[32,2048]{1,0:T(8,128)(2,1)S(1)}, u32[]{:S(2)}, u32[]{:S(2)}) collective-permute-start(bf16[32,2048]{1,0:T(8,128)(2,1)S(1)} %get-tuple-element.86), channel_id=1, source_target_pairs={{0,1},{1,0},{2,3},{3,2},{4,5},{5,4},{6,7},{7,6},{8,9},{9,8},{10,11... | collective-permute-start | bytes 393224 | tf_op jit(solution)/shard_map/ppermute | solution.py:235
  26.3 0.1 collective-permute-start.11
  26.4 0.3 cached_pages.1
  26.7 2.4 %collective-permute-done.8.refs_1_ = bf16[32,2048]{1,0:T(8,128)(2,1)S(1)} collective-permute-done((bf16[32,2048]{1,0:T(8,128)(2,1)S(1)}, bf16[32,2048]{1,0:T(8,128)(2,1)S(1)}, u32[]{:S(2)}, u32[]{:S(2)}) %collective-permute-start.8) | collective-permute-done | bytes 131104 | tf_op jit(solution)/shard_map/ppermute | solution.py:235
  29.2 2.4 %collective-permute-start.12 = (bf16[32,2048]{1,0:T(8,128)(2,1)S(1)}, bf16[32,2048]{1,0:T(8,128)(2,1)S(1)}, u32[]{:S(2)}, u32[]{:S(2)}) collective-permute-start(bf16[32,2048]{1,0:T(8,128)(2,1)S(1)} %second_added.1), channel_id=1, source_target_pairs={{0,4},{1,5},{2,6},{3,7},{4,0},{5,1},{6,2},{7,3},{8,12},{9,13},{10,... | collective-permute-start | bytes 393224 | tf_op jit(solution)/shard_map/ppermute | solution.py:235
  31.6 0.1 near_sums.1
  31.7 1.8 %collective-permute-start.13 = (bf16[32,2048]{1,0:T(8,128)(2,1)S(1)}, bf16[32,2048]{1,0:T(8,128)(2,1)S(1)}, u32[]{:S(2)}, u32[]{:S(2)}) collective-permute-start(bf16[32,2048]{1,0:T(8,128)(2,1)S(1)} %get-tuple-element.99), channel_id=1, source_target_pairs={{0,2},{1,3},{2,0},{3,1},{4,6},{5,7},{6,4},{7,5},{8,10},{9,11},{10,... | collective-permute-start | bytes 393224 | tf_op jit(solution)/shard_map/ppermute | solution.py:235
  33.5 1.5 %collective-permute-start.14 = (bf16[8,16,512]{2,1,0:T(8,128)(2,1)S(1)}, bf16[8,16,512]{2,1,0:T(8,128)(2,1)S(1)}, u32[]{:S(2)}, u32[]{:S(2)}) collective-permute-start(bf16[8,16,512]{2,1,0:T(8,128)(2,1)S(1)} %get-tuple-element.101), channel_id=1, source_target_pairs={{0,8},{8,0},{16,24},{24,16},{1,9},{9,1},{17,25},{25,17},{2,10},{10... | collective-permute-start | bytes 393224 | tf_op jit(solution)/shard_map/ppermute | solution.py:235
  35.0 1.5 %collective-permute-start.15 = (bf16[8,16,512]{2,1,0:T(8,128)(2,1)S(1)}, bf16[8,16,512]{2,1,0:T(8,128)(2,1)S(1)}, u32[]{:S(2)}, u32[]{:S(2)}) collective-permute-start(bf16[8,16,512]{2,1,0:T(8,128)(2,1)S(1)} %get-tuple-element.102), channel_id=1, source_target_pairs={{0,16},{8,24},{16,0},{24,8},{1,17},{9,25},{17,1},{25,9},{2,18},{10... | collective-permute-start | bytes 393224 | tf_op jit(solution)/shard_map/ppermute | solution.py:235
  36.5 0.5 %collective-permute-start.16 = (bf16[8,16,512]{2,1,0:T(8,128)(2,1)S(1)}, bf16[8,16,512]{2,1,0:T(8,128)(2,1)S(1)}, u32[]{:S(2)}, u32[]{:S(2)}) collective-permute-start(bf16[8,16,512]{2,1,0:T(8,128)(2,1)S(1)} %get-tuple-element.103), channel_id=1, source_target_pairs={{0,24},{8,16},{16,8},{24,0},{1,25},{9,17},{17,9},{25,1},{2,26},{10... | collective-permute-start | bytes 393224 | tf_op jit(solution)/shard_map/ppermute | solution.py:235
  37.0 0.6 %collective-permute-done.12.refs_0_ = bf16[32,2048]{1,0:T(8,128)(2,1)S(1)} collective-permute-done((bf16[32,2048]{1,0:T(8,128)(2,1)S(1)}, bf16[32,2048]{1,0:T(8,128)(2,1)S(1)}, u32[]{:S(2)}, u32[]{:S(2)}) %collective-permute-start.12) | collective-permute-done | bytes 131104 | tf_op jit(solution)/shard_map/ppermute | solution.py:235
  37.6 0.5 %collective-permute-done.13.refs_1_ = bf16[32,2048]{1,0:T(8,128)(2,1)S(1)} collective-permute-done((bf16[32,2048]{1,0:T(8,128)(2,1)S(1)}, bf16[32,2048]{1,0:T(8,128)(2,1)S(1)}, u32[]{:S(2)}, u32[]{:S(2)}) %collective-permute-start.13) | collective-permute-done | bytes 131104 | tf_op jit(solution)/shard_map/ppermute | solution.py:235
  38.0 1.8 %collective-permute-done.14.refs_1_ = bf16[8,16,512]{2,1,0:T(8,128)(2,1)S(1)} collective-permute-done((bf16[8,16,512]{2,1,0:T(8,128)(2,1)S(1)}, bf16[8,16,512]{2,1,0:T(8,128)(2,1)S(1)}, u32[]{:S(2)}, u32[]{:S(2)}) %collective-permute-start.14) | collective-permute-done | bytes 131104 | tf_op jit(solution)/shard_map/ppermute | solution.py:235
  39.8 2.7 %collective-permute-done.15.refs_2_ = bf16[8,16,512]{2,1,0:T(8,128)(2,1)S(1)} collective-permute-done((bf16[8,16,512]{2,1,0:T(8,128)(2,1)S(1)}, bf16[8,16,512]{2,1,0:T(8,128)(2,1)S(1)}, u32[]{:S(2)}, u32[]{:S(2)}) %collective-permute-start.15) | collective-permute-done | bytes 131104 | tf_op jit(solution)/shard_map/ppermute | solution.py:235
  42.5 0.8 %placed.1 = bf16[1,4,8,16,512]{4,3,2,1,0:T(8,128)(2,1)} custom-call(bf16[8,16,512]{2,1,0:T(8,128)(2,1)S(1)} %get-tuple-element.104.refs_0_, bf16[8,16,512]{2,1,0:T(8,128)(2,1)S(1)} %collective-permute-done.14.refs_1_, bf16[8,16,512]{2,1,0:T(8,128)(2,1)S(1)} %collective-permute-done.15.refs_2_, bf16[8,16,512]{2,1,0:T(8,128)(2,1)S(1)} %collective-permute-done.16.refs_3_), custom_call_target="tpu_custom_call" | custom-call | tf_op jit(solution)/shard_map/placed/pallas_call | solution.py:702
  43.3 0.7 %finished.1 = f32[32,2048]{1,0:T(8,128)} custom-call(f32[32,2048]{1,0:T(8,128)S(1)} %get-tuple-element.108.base_ref, bf16[32,2048]{1,0:T(8,128)(2,1)S(1)} %collective-permute-done.12.refs_0_, bf16[32,2048]{1,0:T(8,128)(2,1)S(1)} %collective-permute-done.13.refs_1_), custom_call_target="tpu_custom_call" | custom-call | tf_op jit(solution)/shard_map/finished/pallas_call | solution.py:721
  (16 shorter events, 0.1 us)
Async XLA Ops:
  0.6 11.0 %collective-permute-start = (bf16[32,2048]{1,0:T(8,128)(2,1)}, bf16[32,2048]{1,0:T(8,128)(2,1)S(1)}, u32[]{:S(2)}, u32[]{:S(2)}) collective-permute-start(bf16[32,2048]{1,0:T(8,128)(2,1)} %refs_2_.1), channel_id=1, source_target_pairs={{0,4},{1,5},{2,6},{3,7},{4,0},{5,1},{6,2},{7,3},{8,12},{9,13},{10,... | collective-permute-start | bytes 393224 | tf_op jit(solution)/shard_map/ppermute | solution.py:235
  4.7 7.4 %collective-permute-start.3 = (bf16[32,2048]{1,0:T(8,128)(2,1)}, bf16[32,2048]{1,0:T(8,128)(2,1)S(1)}, u32[]{:S(2)}, u32[]{:S(2)}) collective-permute-start(bf16[32,2048]{1,0:T(8,128)(2,1)} %refs_2_.1), channel_id=1, source_target_pairs={{0,2},{1,3},{2,0},{3,1},{4,6},{5,7},{6,4},{7,5},{8,10},{9,11},{10,... | collective-permute-start | bytes 393224 | tf_op jit(solution)/shard_map/ppermute | solution.py:235
  6.3 5.8 %copy-start = (bf16[32,2048]{1,0:T(8,128)(2,1)S(1)}, bf16[32,2048]{1,0:T(8,128)(2,1)}, u32[]{:S(2)}) copy-start(bf16[32,2048]{1,0:T(8,128)(2,1)} %refs_2_.1) | copy-start | bytes 393220
  11.6 5.0 %collective-permute-start.1 = (bf16[32,2048]{1,0:T(8,128)(2,1)S(1)}, bf16[32,2048]{1,0:T(8,128)(2,1)S(1)}, u32[]{:S(2)}, u32[]{:S(2)}) collective-permute-start(bf16[32,2048]{1,0:T(8,128)(2,1)S(1)} %collective-permute-done.refs_0_), channel_id=1, source_target_pairs={{0,2},{1,3},{2,0},{3,1},{4,6},{5,7},{6,4},{7,5},{8,10},{9,11},{10,... | collective-permute-start | bytes 393224 | tf_op jit(solution)/shard_map/ppermute | solution.py:235
  12.1 4.5 %collective-permute-start.4 = (bf16[32,2048]{1,0:T(8,128)(2,1)S(1)}, bf16[32,2048]{1,0:T(8,128)(2,1)S(1)}, u32[]{:S(2)}, u32[]{:S(2)}) collective-permute-start(bf16[32,2048]{1,0:T(8,128)(2,1)S(1)} %copy-done), channel_id=1, source_target_pairs={{0,1},{1,0},{2,3},{3,2},{4,5},{5,4},{6,7},{7,6},{8,9},{9,8},{10,11... | collective-permute-start | bytes 393224 | tf_op jit(solution)/shard_map/ppermute | solution.py:235
  12.2 4.5 %collective-permute-start.5 = (bf16[32,2048]{1,0:T(8,128)(2,1)S(1)}, bf16[32,2048]{1,0:T(8,128)(2,1)S(1)}, u32[]{:S(2)}, u32[]{:S(2)}) collective-permute-start(bf16[32,2048]{1,0:T(8,128)(2,1)S(1)} %collective-permute-done.3.refs_0_), channel_id=1, source_target_pairs={{0,1},{1,0},{2,3},{3,2},{4,5},{5,4},{6,7},{7,6},{8,9},{9,8},{10,11... | collective-permute-start | bytes 393224 | tf_op jit(solution)/shard_map/ppermute | solution.py:235
  12.7 4.0 %collective-permute-start.6 = (bf16[32,2048]{1,0:T(8,128)(2,1)S(1)}, bf16[32,2048]{1,0:T(8,128)(2,1)S(1)}, u32[]{:S(2)}, u32[]{:S(2)}) collective-permute-start(bf16[32,2048]{1,0:T(8,128)(2,1)S(1)} %collective-permute-done.refs_0_), channel_id=1, source_target_pairs={{0,1},{1,0},{2,3},{3,2},{4,5},{5,4},{6,7},{7,6},{8,9},{9,8},{10,11... | collective-permute-start | bytes 393224 | tf_op jit(solution)/shard_map/ppermute | solution.py:235
  16.7 2.1 %collective-permute-start.2 = (bf16[32,2048]{1,0:T(8,128)(2,1)S(1)}, bf16[32,2048]{1,0:T(8,128)(2,1)S(1)}, u32[]{:S(2)}, u32[]{:S(2)}) collective-permute-start(bf16[32,2048]{1,0:T(8,128)(2,1)S(1)} %collective-permute-done.1.refs_0_), channel_id=1, source_target_pairs={{0,1},{1,0},{2,3},{3,2},{4,5},{5,4},{6,7},{7,6},{8,9},{9,8},{10,11... | collective-permute-start | bytes 393224 | tf_op jit(solution)/shard_map/ppermute | solution.py:235
  21.6 1.9 %collective-permute-start.7 = (bf16[32,2048]{1,0:T(8,128)(2,1)S(1)}, bf16[32,2048]{1,0:T(8,128)(2,1)S(1)}, u32[]{:S(2)}, u32[]{:S(2)}) collective-permute-start(bf16[32,2048]{1,0:T(8,128)(2,1)S(1)} %get-tuple-element.75), channel_id=1, source_target_pairs={{0,1},{1,0},{2,3},{3,2},{4,5},{5,4},{6,7},{7,6},{8,9},{9,8},{10,11... | collective-permute-start | bytes 393224 | tf_op jit(solution)/shard_map/ppermute | solution.py:235
  23.6 5.5 %collective-permute-start.8 = (bf16[32,2048]{1,0:T(8,128)(2,1)S(1)}, bf16[32,2048]{1,0:T(8,128)(2,1)S(1)}, u32[]{:S(2)}, u32[]{:S(2)}) collective-permute-start(bf16[32,2048]{1,0:T(8,128)(2,1)S(1)} %third_added.1), channel_id=1, source_target_pairs={{0,2},{1,3},{2,0},{3,1},{4,6},{5,7},{6,4},{7,5},{8,10},{9,11},{10,... | collective-permute-start | bytes 393224 | tf_op jit(solution)/shard_map/ppermute | solution.py:235
  24.5 4.6 %collective-permute-start.9 = (bf16[32,2048]{1,0:T(8,128)(2,1)S(1)}, bf16[32,2048]{1,0:T(8,128)(2,1)S(1)}, u32[]{:S(2)}, u32[]{:S(2)}) collective-permute-start(bf16[32,2048]{1,0:T(8,128)(2,1)S(1)} %get-tuple-element.85), channel_id=1, source_target_pairs={{0,1},{1,0},{2,3},{3,2},{4,5},{5,4},{6,7},{7,6},{8,9},{9,8},{10,11... | collective-permute-start | bytes 393224 | tf_op jit(solution)/shard_map/ppermute | solution.py:235
  25.8 3.4 %collective-permute-start.10 = (bf16[32,2048]{1,0:T(8,128)(2,1)S(1)}, bf16[32,2048]{1,0:T(8,128)(2,1)S(1)}, u32[]{:S(2)}, u32[]{:S(2)}) collective-permute-start(bf16[32,2048]{1,0:T(8,128)(2,1)S(1)} %get-tuple-element.86), channel_id=1, source_target_pairs={{0,1},{1,0},{2,3},{3,2},{4,5},{5,4},{6,7},{7,6},{8,9},{9,8},{10,11... | collective-permute-start | bytes 393224 | tf_op jit(solution)/shard_map/ppermute | solution.py:235
  26.3 5.3 %collective-permute-start.11 = (bf16[32,2048]{1,0:T(8,128)(2,1)S(1)}, bf16[32,2048]{1,0:T(8,128)(2,1)S(1)}, u32[]{:S(2)}, u32[]{:S(2)}) collective-permute-start(bf16[32,2048]{1,0:T(8,128)(2,1)S(1)} %get-tuple-element.89), channel_id=1, source_target_pairs={{0,1},{1,0},{2,3},{3,2},{4,5},{5,4},{6,7},{7,6},{8,9},{9,8},{10,11... | collective-permute-start | bytes 393224 | tf_op jit(solution)/shard_map/ppermute | solution.py:235
  29.2 8.4 %collective-permute-start.12 = (bf16[32,2048]{1,0:T(8,128)(2,1)S(1)}, bf16[32,2048]{1,0:T(8,128)(2,1)S(1)}, u32[]{:S(2)}, u32[]{:S(2)}) collective-permute-start(bf16[32,2048]{1,0:T(8,128)(2,1)S(1)} %second_added.1), channel_id=1, source_target_pairs={{0,4},{1,5},{2,6},{3,7},{4,0},{5,1},{6,2},{7,3},{8,12},{9,13},{10,... | collective-permute-start | bytes 393224 | tf_op jit(solution)/shard_map/ppermute | solution.py:235
  31.7 6.3 %collective-permute-start.13 = (bf16[32,2048]{1,0:T(8,128)(2,1)S(1)}, bf16[32,2048]{1,0:T(8,128)(2,1)S(1)}, u32[]{:S(2)}, u32[]{:S(2)}) collective-permute-start(bf16[32,2048]{1,0:T(8,128)(2,1)S(1)} %get-tuple-element.99), channel_id=1, source_target_pairs={{0,2},{1,3},{2,0},{3,1},{4,6},{5,7},{6,4},{7,5},{8,10},{9,11},{10,... | collective-permute-start | bytes 393224 | tf_op jit(solution)/shard_map/ppermute | solution.py:235
  33.5 6.3 %collective-permute-start.14 = (bf16[8,16,512]{2,1,0:T(8,128)(2,1)S(1)}, bf16[8,16,512]{2,1,0:T(8,128)(2,1)S(1)}, u32[]{:S(2)}, u32[]{:S(2)}) collective-permute-start(bf16[8,16,512]{2,1,0:T(8,128)(2,1)S(1)} %get-tuple-element.101), channel_id=1, source_target_pairs={{0,8},{8,0},{16,24},{24,16},{1,9},{9,1},{17,25},{25,17},{2,10},{10... | collective-permute-start | bytes 393224 | tf_op jit(solution)/shard_map/ppermute | solution.py:235
  35.0 7.5 %collective-permute-start.15 = (bf16[8,16,512]{2,1,0:T(8,128)(2,1)S(1)}, bf16[8,16,512]{2,1,0:T(8,128)(2,1)S(1)}, u32[]{:S(2)}, u32[]{:S(2)}) collective-permute-start(bf16[8,16,512]{2,1,0:T(8,128)(2,1)S(1)} %get-tuple-element.102), channel_id=1, source_target_pairs={{0,16},{8,24},{16,0},{24,8},{1,17},{9,25},{17,1},{25,9},{2,18},{10... | collective-permute-start | bytes 393224 | tf_op jit(solution)/shard_map/ppermute | solution.py:235
  36.5 6.0 %collective-permute-start.16 = (bf16[8,16,512]{2,1,0:T(8,128)(2,1)S(1)}, bf16[8,16,512]{2,1,0:T(8,128)(2,1)S(1)}, u32[]{:S(2)}, u32[]{:S(2)}) collective-permute-start(bf16[8,16,512]{2,1,0:T(8,128)(2,1)S(1)} %get-tuple-element.103), channel_id=1, source_target_pairs={{0,24},{8,16},{16,8},{24,0},{1,25},{9,17},{17,9},{25,1},{2,26},{10... | collective-permute-start | bytes 393224 | tf_op jit(solution)/shard_map/ppermute | solution.py:235

commit v6 on v5

--- a/solution.py
+++ b/solution.py
@@ -664,32 +664,42 @@
     )(*parts)
 
 
-def near_kernel(*refs):
-    ones, zeros, (first_ref, base_ref) = refs[:2], refs[2:5], refs[5:]
-    first = ones[0][...] + ones[1][...].astype(jnp.float32)
-    first_ref[...] = first.astype(jnp.bfloat16)
-    base = zeros[0][...] + zeros[1][...].astype(jnp.float32)
-    base_ref[...] = zeros[2][...].astype(jnp.float32) + base
-
-
-def near_sums(ones, zeros):
-    shape = ones[0].shape
+def sums_kernel(passing_ref, *refs):
+    zeros, ones, twos = refs[0:2], refs[2:4], refs[4:6]
+    hidden_ref, second_ref, first_ref, base_ref = refs[6:]
+
+    def total(pair, extra=None):
+        received_ref, own_ref = pair
+        value = own_ref[...] + received_ref[...].astype(jnp.float32)
+        return value if extra is None else value + extra[...].astype(jnp.float32)
+
+    second_ref[...] = total(twos, passing_ref).astype(jnp.bfloat16)
+    first_ref[...] = total(ones).astype(jnp.bfloat16)
+    base_ref[...] = total(zeros, hidden_ref)
+
+
+def remaining_sums(passing, pairs, hidden):
+    shape = hidden.shape
     return pl.pallas_call(
-        near_kernel,
-        out_shape=[pltpu.VMEM(shape, jnp.bfloat16), pltpu.VMEM(shape, jnp.float32)],
-        in_specs=vmem_specs(5),
-        out_specs=vmem_specs(2),
+        sums_kernel,
+        out_shape=[
+            pltpu.VMEM(shape, jnp.bfloat16),
+            pltpu.VMEM(shape, jnp.bfloat16),
+            pltpu.VMEM(shape, jnp.float32),
+        ],
+        in_specs=vmem_specs(8),
+        out_specs=vmem_specs(3),
         compiler_params=parameters(4),
-        name="near_sums",
-    )(*ones, *zeros)
-
-
-def place_kernel(*refs):
+        name="remaining_sums",
+    )(passing, *[array for pair in pairs for array in pair], hidden)
+
+
+def place_kernel(masks, *refs):
     group = lax.axis_index("dp")
     pages, (cache_ref, sems) = refs[:-2], refs[-2:]
     copies = [
-        pltpu.make_async_copy(page_ref, cache_ref.at[0, group ^ mask], sems.at[mask])
-        for mask, page_ref in enumerate(pages)
+        pltpu.make_async_copy(page_ref, cache_ref.at[0, group ^ mask], sems.at[number])
+        for number, (mask, page_ref) in enumerate(zip(masks, pages))
     ]
     for copy in copies:
         copy.start()
@@ -697,11 +707,11 @@
         copy.wait()
 
 
-def placed(pages):
+def placed(masks, pages, replica_count):
     count = len(pages)
     return pl.pallas_call(
-        place_kernel,
-        out_shape=jax.ShapeDtypeStruct((1, count) + pages[0].shape, pages[0].dtype),
+        functools.partial(place_kernel, masks),
+        out_shape=jax.ShapeDtypeStruct((1, replica_count) + pages[0].shape, pages[0].dtype),
         in_specs=[pl.BlockSpec(memory_space=pl.ANY)] * count,
         out_specs=pl.BlockSpec(memory_space=pltpu.HBM),
         scratch_shapes=[pltpu.SemaphoreType.DMA((count,))],
@@ -710,22 +720,34 @@
     )(*pages)
 
 
-def finish_kernel(base_ref, *refs):
+def finish_kernel(mask, base_ref, *refs):
+    *parts, page_ref, _, output_ref, cache_ref, sem = refs
+    target = cache_ref.at[0, lax.axis_index("dp") ^ mask]
+    copy = pltpu.make_async_copy(page_ref, target, sem)
+    copy.start()
     total = base_ref[...]
-    for part_ref in refs[:-1]:
+    for part_ref in parts:
         total = total + part_ref[...].astype(jnp.float32)
-    refs[-1][...] = total
-
-
-def finished(base, parts):
+    output_ref[...] = total
+    copy.wait()
+
+
+def finished(base, parts, mask, page, cache):
+    count = len(parts)
     return pl.pallas_call(
-        finish_kernel,
-        out_shape=jax.ShapeDtypeStruct(base.shape, base.dtype),
-        in_specs=vmem_specs(1 + len(parts)),
-        out_specs=pl.BlockSpec(memory_space=pltpu.VMEM),
+        functools.partial(finish_kernel, mask),
+        out_shape=[
+            jax.ShapeDtypeStruct(base.shape, base.dtype),
+            jax.ShapeDtypeStruct(cache.shape, cache.dtype),
+        ],
+        in_specs=vmem_specs(1 + count)
+        + [pl.BlockSpec(memory_space=pl.ANY), pl.BlockSpec(memory_space=pltpu.HBM)],
+        out_specs=vmem_specs(1) + [pl.BlockSpec(memory_space=pltpu.HBM)],
+        scratch_shapes=[pltpu.SemaphoreType.DMA(())],
+        input_output_aliases={count + 2: 1},
         compiler_params=parameters(4),
         name="finished",
-    )(base, *parts)
+    )(base, *parts, page, cache)
 
 
 def shards_whole_heads(
@@ -787,36 +809,22 @@
 
     pieces = (own_hidden, there_hidden, beside_hidden)
     received = exchanged(sibling, "tensor", 1)
-    second_sibling, second_own = kind_rows(
-        "second_rows", (2,), joined, tables[0], (output, downward), pieces
-    )
+    partials = kind_rows("rest_rows", (0, 1, 2), joined, tables[0], (output, downward), pieces)
+    siblings, owns = partials[: CHIPS - 1], partials[CHIPS - 1 :]
     third_sum = added("third_added", own, received)
-    third_sum, second_sibling, joined = lax.optimization_barrier(
-        (third_sum, second_sibling, joined)
-    )
+    third_sum, siblings, joined = lax.optimization_barrier((third_sum, siblings, joined))
     passing = exchanged(third_sum, "tensor", to_chip[1])
-    second_received = exchanged(second_sibling, "tensor", 1)
-    zero_sibling, first_sibling, zero_own, first_own = kind_rows(
-        "near_rows", (0, 1), joined, tables[0], (output, downward), pieces
-    )
-    first_received = exchanged(first_sibling, "tensor", 1)
-    zero_received = exchanged(zero_sibling, "tensor", 1)
+    pairs = [(exchanged(sibling, "tensor", 1), own) for sibling, own in zip(siblings, owns)]
     pages = cached_pages(joined, destinations, replica_count)
-    second_sum = added("second_added", second_own, passing, second_received)
-    second_sum, first_received = lax.optimization_barrier((second_sum, first_received))
+    early, late = (3, 1), 2
+    arriving = [exchanged(pages[mask], "dp", mask) for mask in early]
+    second_sum, first_sum, base = remaining_sums(passing, pairs, hidden)
     from_second = exchanged(second_sum, "tensor", to_chip[2])
-    first_sum, base = near_sums((first_own, first_received), (zero_own, zero_received, hidden))
-    first_sum, pages = lax.optimization_barrier((first_sum, pages))
     from_first = exchanged(first_sum, "tensor", to_chip[1])
-    arriving = [pages[0]] + [
-        exchanged(pages[mask], "dp", mask) for mask in range(1, replica_count)
-    ]
-    from_second, from_first, arriving = lax.optimization_barrier(
-        (from_second, from_first, arriving)
-    )
-    cache_pages = placed(arriving)
-    base, cache_pages = lax.optimization_barrier((base, cache_pages))
-    return (finished(base, (from_second, from_first)), cache_pages)
+    base, late_page = lax.optimization_barrier((base, pages[late]))
+    late_page = exchanged(late_page, "dp", late)
+    cache_pages = placed((0,) + early, [pages[0]] + arriving, replica_count)
+    return tuple(finished(base, (from_second, from_first), late, late_page, cache_pages))
 
 
 def solution(mesh):

time: 44.2 us -> 41.6 us (0.941)
  waiting for transfers between devices: 10.2 us -> 6.25 us
  starting transfers between devices: 16.6 us -> 18.4 us
  Pallas kernels: 16.5 us -> 16 us
    ppermute x17, waiting for transfers between devices: 10.2 us -> 6.25 us  [exchanged(): lax.ppermute(block, axis, [(member, member ^ mask) for member in range(co...]
    ppermute x17, starting transfers between devices: 16.6 us -> 18.4 us  [exchanged(): lax.ppermute(block, axis, [(member, member ^ mask) for member in range(co...]
    pallas_call x2 -> x1, Pallas kernels: 2.64 us -> 1.6 us  [kind_rows(): pl.pallas_call(functools.partial(kind_kernel, kinds), out_shape=[pltpu.VM...]
    pallas_call x3, Pallas kernels: 1.63 us -> 2.26 us  [the longest x1 1.37 us: finished(): pl.pallas_call(functools.partial(finish_kernel, mask), out_shape=[jax.Sha...]
  transfers between devices with their start and end apart: 17 -> 17, of which waited for: 6 -> 5; matrix products, arithmetic and copies ran while one was open for 0% -> 0% of each run, Pallas kernels for 27% -> 28%
where the time goes in v6:
time: 41.6 us; the launch traced here: 41.5 us
  starting transfers between devices  18.4 us (44%)
  Pallas kernels  16 us (38%)
  waiting for transfers between devices  6.25 us (15%)
  between operations  0.75 us (2%)
    ppermute x17, starting transfers between devices, exchanged(): lax.ppermute(block, axis, [(member, member ^ mask) for member in range(co...  18.4 us
    ppermute x17, waiting for transfers between devices, exchanged(): lax.ppermute(block, axis, [(member, member ^ mask) for member in range(co...  6.25 us
    pallas_call x1, Pallas kernels, own_rows(): pl.pallas_call(functools.partial(own_kernel, count, replica_count), out_s...  5.3 us
    pallas_call x2, Pallas kernels, middle_rows(): pl.pallas_call(functools.partial(middle_kernel, origins), out_shape=[pltp...  3.7 us
    pallas_call x1, Pallas kernels, last_rows(): pl.pallas_call(last_kernel, out_shape=[pltpu.VMEM((tokens, 3 * HD), jnp.b...  2.84 us
    pallas_call x1, Pallas kernels, kind_rows(): pl.pallas_call(functools.partial(kind_kernel, kinds), out_shape=[pltpu.VM...  1.6 us
    pallas_call x1, Pallas kernels, finished(): pl.pallas_call(functools.partial(finish_kernel, mask), out_shape=[jax.Sha...  1.37 us
  transfers between devices with their start and end apart: 17, of which 5 were waited for; matrix products, arithmetic and copies ran while one was open for 0% of the time, Pallas kernels for 28%

profile of v6, /device:TPU:0, one launch (start us, length us, event | category | flops | bytes accessed | tf_op | source)
XLA Modules:
  0.0 41.5 jit_solution(5191620589691176786)
XLA Ops:
  0.6 4.1 %collective-permute-start = (bf16[32,2048]{1,0:T(8,128)(2,1)}, bf16[32,2048]{1,0:T(8,128)(2,1)S(1)}, u32[]{:S(2)}, u32[]{:S(2)}) collective-permute-start(bf16[32,2048]{1,0:T(8,128)(2,1)} %refs_2_.1), channel_id=1, source_target_pairs={{0,4},{1,5},{2,6},{3,7},{4,0},{5,1},{6,2},{7,3},{8,12},{9,13},{10,... | collective-permute-start | bytes 393224 | tf_op jit(solution)/shard_map/ppermute | solution.py:235
  4.7 1.6 %collective-permute-start.3 = (bf16[32,2048]{1,0:T(8,128)(2,1)}, bf16[32,2048]{1,0:T(8,128)(2,1)S(1)}, u32[]{:S(2)}, u32[]{:S(2)}) collective-permute-start(bf16[32,2048]{1,0:T(8,128)(2,1)} %refs_2_.1), channel_id=1, source_target_pairs={{0,2},{1,3},{2,0},{3,1},{4,6},{5,7},{6,4},{7,5},{8,10},{9,11},{10,... | collective-permute-start | bytes 393224 | tf_op jit(solution)/shard_map/ppermute | solution.py:235
  6.3 5.3 %own_rows.1 = (s32[1,256]{1,0:T(1,128)}, s32[1,16]{1,0:T(1,128)}, bf16[32,2048]{1,0:T(8,128)(2,1)S(1)}, f32[1,2048]{1,0:T(1,128)S(1)}, f32[1,2048]{1,0:T(1,128)S...) custom-call(s32[1,256]{1,0:T(1,128)} %refs_0_.1, ...), custom_call_target="tpu_custom_call" | custom-call | flops 234881024 | bytes 11682880 | tf_op jit(solution)/shard_map/own_rows/pallas_call | solution.py:452
  11.6 0.0 collective-permute-done.refs_0_
  11.6 0.5 %collective-permute-start.1 = (bf16[32,2048]{1,0:T(8,128)(2,1)S(1)}, bf16[32,2048]{1,0:T(8,128)(2,1)S(1)}, u32[]{:S(2)}, u32[]{:S(2)}) collective-permute-start(bf16[32,2048]{1,0:T(8,128)(2,1)S(1)} %collective-permute-done.refs_0_), channel_id=1, source_target_pairs={{0,2},{1,3},{2,0},{3,1},{4,6},{5,7},{6,4},{7,5},{8,10},{9,11},{10,... | collective-permute-start | bytes 393224 | tf_op jit(solution)/shard_map/ppermute | solution.py:235
  12.1 0.0 collective-permute-start.4
  12.2 0.0 collective-permute-done.3.refs_0_
  12.2 0.5 %collective-permute-start.5 = (bf16[32,2048]{1,0:T(8,128)(2,1)S(1)}, bf16[32,2048]{1,0:T(8,128)(2,1)S(1)}, u32[]{:S(2)}, u32[]{:S(2)}) collective-permute-start(bf16[32,2048]{1,0:T(8,128)(2,1)S(1)} %collective-permute-done.3.refs_0_), channel_id=1, source_target_pairs={{0,1},{1,0},{2,3},{3,2},{4,5},{5,4},{6,7},{7,6},{8,9},{9,8},{10,11... | collective-permute-start | bytes 393224 | tf_op jit(solution)/shard_map/ppermute | solution.py:235
  12.7 0.1 collective-permute-start.6
  12.7 1.6 %there_rows.1 = (bf16[32,768]{1,0:T(8,128)(2,1)S(1)}, bf16[32,1024]{1,0:T(8,128)(2,1)S(1)}) custom-call(bf16[32,2048]{1,0:T(8,128)(2,1)S(1)} %collective-permute-done.refs_0_, f32[1,2048]{1,0:T(1,128)S(1)} %get-tuple-element.49.refs_1_.refs_4_.refs_2_, f32[1,2048]{1,0:T(1,128)S(1)} %get-tuple-element.50.refs_2_.refs_5_.refs_3_, ...), custom_call_target="tpu_custom_call" | custom-call | flops 234881024 | bytes 1048576 | tf_op jit(solution)/shard_map/there_rows/pallas_call | solution.py:492
  14.3 2.3 %collective-permute-done.1.refs_0_ = bf16[32,2048]{1,0:T(8,128)(2,1)S(1)} collective-permute-done((bf16[32,2048]{1,0:T(8,128)(2,1)S(1)}, bf16[32,2048]{1,0:T(8,128)(2,1)S(1)}, u32[]{:S(2)}, u32[]{:S(2)}) %collective-permute-start.1) | collective-permute-done | bytes 131104 | tf_op jit(solution)/shard_map/ppermute | solution.py:235
  16.7 0.0 collective-permute-done.4.refs_1_
  16.7 0.0 collective-permute-done.5.refs_2_
  16.7 2.1 %beside_rows.1 = (bf16[128,768]{1,0:T(8,128)(2,1)S(1)}, bf16[128,1024]{1,0:T(8,128)(2,1)S(1)}, bf16[256,2048]{1,0:T(8,128)(2,1)S(1)}) custom-call(bf16[32,2048]{1,0:T(8,128)(2,1)S(1)} %collective-permute-done.3.refs_0_, bf16[32,2048]{1,0:T(8,128)(2,1)S(1)} %collective-permute-done.4.refs_1_, bf16[32,2048]{1,0:T(8,128)(2,1)S(1)} %collective-permute-done.5.refs_2_, ...), custom_call_target="tpu_custom_call" | custom-call | flops 939524096 | bytes 1048576 | tf_op jit(solution)/shard_map/beside_rows/pallas_call | solution.py:492
  18.8 2.8 %last_rows.1 = (bf16[256,768]{1,0:T(8,128)(2,1)S(1)}, bf16[32,2048]{1,0:T(8,128)(2,1)S(1)}, f32[32,2048]{1,0:T(8,128)S(1)}) custom-call(bf16[32,2048]{1,0:T(8,128)(2,1)S(1)} %collective-permute-done.1.refs_0_, bf16[32,2048]{1,0:T(8,128)(2,1)S(1)} %collective-permute-done.2.refs_1_, f32[1,2048]{1,0:T(1,128)S(1)} %get-tuple-element.49.refs_1_.refs_4_.refs_2_, ...), custom_call_target="tpu_custom_call" | custom-call | flops 805306368 | bytes 1048576 | tf_op jit(solution)/shard_map/last_rows/pallas_call | solution.py:564
  21.6 0.5 %collective-permute-start.7 = (bf16[32,2048]{1,0:T(8,128)(2,1)S(1)}, bf16[32,2048]{1,0:T(8,128)(2,1)S(1)}, u32[]{:S(2)}, u32[]{:S(2)}) collective-permute-start(bf16[32,2048]{1,0:T(8,128)(2,1)S(1)} %get-tuple-element.65), channel_id=1, source_target_pairs={{0,1},{1,0},{2,3},{3,2},{4,5},{5,4},{6,7},{7,6},{8,9},{9,8},{10,11... | collective-permute-start | bytes 393224 | tf_op jit(solution)/shard_map/ppermute | solution.py:235
  22.2 1.6 %rest_rows.1 = (bf16[32,2048]{1,0:T(8,128)(2,1)S(1)}, bf16[32,2048]{1,0:T(8,128)(2,1)S(1)}, bf16[32,2048]{1,0:T(8,128)(2,1)S(1)}, f32[32,2048]{1,0:T(8,128)S(1)}...) custom-call(bf16[256,768]{1,0:T(8,128)(2,1)S(1)} %get-tuple-element.82.joined_ref, ...), custom_call_target="tpu_custom_call" | custom-call | flops 1006632960 | bytes 1048576 | tf_op jit(solution)/shard_map/rest_rows/pallas_call | solution.py:608
  23.8 0.9 %collective-permute-start.8 = (bf16[32,2048]{1,0:T(8,128)(2,1)S(1)}, bf16[32,2048]{1,0:T(8,128)(2,1)S(1)}, u32[]{:S(2)}, u32[]{:S(2)}) collective-permute-start(bf16[32,2048]{1,0:T(8,128)(2,1)S(1)} %third_added.1), channel_id=1, source_target_pairs={{0,2},{1,3},{2,0},{3,1},{4,6},{5,7},{6,4},{7,5},{8,10},{9,11},{10,... | collective-permute-start | bytes 393224 | tf_op jit(solution)/shard_map/ppermute | solution.py:235
  24.7 0.5 %collective-permute-start.10 = (bf16[32,2048]{1,0:T(8,128)(2,1)S(1)}, bf16[32,2048]{1,0:T(8,128)(2,1)S(1)}, u32[]{:S(2)}, u32[]{:S(2)}) collective-permute-start(bf16[32,2048]{1,0:T(8,128)(2,1)S(1)} %get-tuple-element.76), channel_id=1, source_target_pairs={{0,1},{1,0},{2,3},{3,2},{4,5},{5,4},{6,7},{7,6},{8,9},{9,8},{10,11... | collective-permute-start | bytes 393224 | tf_op jit(solution)/shard_map/ppermute | solution.py:235
  25.3 0.3 cached_pages.1
  25.6 2.5 %collective-permute-start.15 = (bf16[8,16,512]{2,1,0:T(8,128)(2,1)S(1)}, bf16[8,16,512]{2,1,0:T(8,128)(2,1)S(1)}, u32[]{:S(2)}, u32[]{:S(2)}) collective-permute-start(bf16[8,16,512]{2,1,0:T(8,128)(2,1)S(1)} %get-tuple-element.90), channel_id=1, source_target_pairs={{0,24},{8,16},{16,8},{24,0},{1,25},{9,17},{17,9},{25,1},{2,26},{10... | collective-permute-start | bytes 393224 | tf_op jit(solution)/shard_map/ppermute | solution.py:235
  28.1 1.2 %collective-permute-done.8.passing_ref = bf16[32,2048]{1,0:T(8,128)(2,1)S(1)} collective-permute-done((bf16[32,2048]{1,0:T(8,128)(2,1)S(1)}, bf16[32,2048]{1,0:T(8,128)(2,1)S(1)}, u32[]{:S(2)}, u32[]{:S(2)}) %collective-permute-start.8) | collective-permute-done | bytes 131104 | tf_op jit(solution)/shard_map/ppermute | solution.py:235
  29.3 1.5 %collective-permute-start.16 = (bf16[8,16,512]{2,1,0:T(8,128)(2,1)S(1)}, bf16[8,16,512]{2,1,0:T(8,128)(2,1)S(1)}, u32[]{:S(2)}, u32[]{:S(2)}) collective-permute-start(bf16[8,16,512]{2,1,0:T(8,128)(2,1)S(1)} %get-tuple-element.91), channel_id=1, source_target_pairs={{0,8},{8,0},{16,24},{24,16},{1,9},{9,1},{17,25},{25,17},{2,10},{10... | collective-permute-start | bytes 393224 | tf_op jit(solution)/shard_map/ppermute | solution.py:235
  30.8 0.1 remaining_sums.1
  31.0 2.4 %collective-permute-start.12 = (bf16[32,2048]{1,0:T(8,128)(2,1)S(1)}, bf16[32,2048]{1,0:T(8,128)(2,1)S(1)}, u32[]{:S(2)}, u32[]{:S(2)}) collective-permute-start(bf16[32,2048]{1,0:T(8,128)(2,1)S(1)} %get-tuple-element.86), channel_id=1, source_target_pairs={{0,4},{1,5},{2,6},{3,7},{4,0},{5,1},{6,2},{7,3},{8,12},{9,13},{10,... | collective-permute-start | bytes 393224 | tf_op jit(solution)/shard_map/ppermute | solution.py:235
  33.4 1.7 %collective-permute-start.13 = (bf16[32,2048]{1,0:T(8,128)(2,1)S(1)}, bf16[32,2048]{1,0:T(8,128)(2,1)S(1)}, u32[]{:S(2)}, u32[]{:S(2)}) collective-permute-start(bf16[32,2048]{1,0:T(8,128)(2,1)S(1)} %get-tuple-element.87), channel_id=1, source_target_pairs={{0,2},{1,3},{2,0},{3,1},{4,6},{5,7},{6,4},{7,5},{8,10},{9,11},{10,... | collective-permute-start | bytes 393224 | tf_op jit(solution)/shard_map/ppermute | solution.py:235
  35.1 1.5 %collective-permute-start.14 = (bf16[8,16,512]{2,1,0:T(8,128)(2,1)S(1)}, bf16[8,16,512]{2,1,0:T(8,128)(2,1)S(1)}, u32[]{:S(2)}, u32[]{:S(2)}) collective-permute-start(bf16[8,16,512]{2,1,0:T(8,128)(2,1)S(1)} %get-tuple-element.88), channel_id=1, source_target_pairs={{0,16},{8,24},{16,0},{24,8},{1,17},{9,25},{17,1},{25,9},{2,18},{10... | collective-permute-start | bytes 393224 | tf_op jit(solution)/shard_map/ppermute | solution.py:235
  36.6 0.8 %placed.1.refs_3_ = bf16[1,4,8,16,512]{4,3,2,1,0:T(8,128)(2,1)} custom-call(bf16[8,16,512]{2,1,0:T(8,128)(2,1)S(1)} %get-tuple-element.89.refs_0_, bf16[8,16,512]{2,1,0:T(8,128)(2,1)S(1)} %collective-permute-done.15.refs_1_, bf16[8,16,512]{2,1,0:T(8,128)(2,1)S(1)} %collective-permute-done.16.refs_2_), custom_call_target="tpu_custom_call" | custom-call | tf_op jit(solution)/shard_map/placed/pallas_call | solution.py:712
  37.4 1.6 %collective-permute-done.12.refs_0_ = bf16[32,2048]{1,0:T(8,128)(2,1)S(1)} collective-permute-done((bf16[32,2048]{1,0:T(8,128)(2,1)S(1)}, bf16[32,2048]{1,0:T(8,128)(2,1)S(1)}, u32[]{:S(2)}, u32[]{:S(2)}) %collective-permute-start.12) | collective-permute-done | bytes 131104 | tf_op jit(solution)/shard_map/ppermute | solution.py:235
  39.1 0.3 collective-permute-done.13.refs_1_
  39.4 0.7 %collective-permute-done.14.refs_2_ = bf16[8,16,512]{2,1,0:T(8,128)(2,1)S(1)} collective-permute-done((bf16[8,16,512]{2,1,0:T(8,128)(2,1)S(1)}, bf16[8,16,512]{2,1,0:T(8,128)(2,1)S(1)}, u32[]{:S(2)}, u32[]{:S(2)}) %collective-permute-start.14) | collective-permute-done | bytes 131104 | tf_op jit(solution)/shard_map/ppermute | solution.py:235
  40.1 1.4 %finished.1 = (f32[32,2048]{1,0:T(8,128)}, bf16[1,4,8,16,512]{4,3,2,1,0:T(8,128)(2,1)}) custom-call(f32[32,2048]{1,0:T(8,128)S(1)} %get-tuple-element.85.base_ref, bf16[32,2048]{1,0:T(8,128)(2,1)S(1)} %collective-permute-done.12.refs_0_, bf16[32,2048]{1,0:T(8,128)(2,1)S(1)} %collective-permute-done.13.refs_1_, ...), custom_call_target="tpu_custom_call", output_to_operand_aliasing={{1}: (4, {})} | custom-call | tf_op jit(solution)/shard_map/finished/pallas_call | solution.py:737
  (14 shorter events, 0.1 us)
Async XLA Ops:
  0.6 11.0 %collective-permute-start = (bf16[32,2048]{1,0:T(8,128)(2,1)}, bf16[32,2048]{1,0:T(8,128)(2,1)S(1)}, u32[]{:S(2)}, u32[]{:S(2)}) collective-permute-start(bf16[32,2048]{1,0:T(8,128)(2,1)} %refs_2_.1), channel_id=1, source_target_pairs={{0,4},{1,5},{2,6},{3,7},{4,0},{5,1},{6,2},{7,3},{8,12},{9,13},{10,... | collective-permute-start | bytes 393224 | tf_op jit(solution)/shard_map/ppermute | solution.py:235
  4.7 7.4 %collective-permute-start.3 = (bf16[32,2048]{1,0:T(8,128)(2,1)}, bf16[32,2048]{1,0:T(8,128)(2,1)S(1)}, u32[]{:S(2)}, u32[]{:S(2)}) collective-permute-start(bf16[32,2048]{1,0:T(8,128)(2,1)} %refs_2_.1), channel_id=1, source_target_pairs={{0,2},{1,3},{2,0},{3,1},{4,6},{5,7},{6,4},{7,5},{8,10},{9,11},{10,... | collective-permute-start | bytes 393224 | tf_op jit(solution)/shard_map/ppermute | solution.py:235
  6.3 5.8 %copy-start = (bf16[32,2048]{1,0:T(8,128)(2,1)S(1)}, bf16[32,2048]{1,0:T(8,128)(2,1)}, u32[]{:S(2)}) copy-start(bf16[32,2048]{1,0:T(8,128)(2,1)} %refs_2_.1) | copy-start | bytes 393220
  11.6 5.0 %collective-permute-start.1 = (bf16[32,2048]{1,0:T(8,128)(2,1)S(1)}, bf16[32,2048]{1,0:T(8,128)(2,1)S(1)}, u32[]{:S(2)}, u32[]{:S(2)}) collective-permute-start(bf16[32,2048]{1,0:T(8,128)(2,1)S(1)} %collective-permute-done.refs_0_), channel_id=1, source_target_pairs={{0,2},{1,3},{2,0},{3,1},{4,6},{5,7},{6,4},{7,5},{8,10},{9,11},{10,... | collective-permute-start | bytes 393224 | tf_op jit(solution)/shard_map/ppermute | solution.py:235
  12.1 4.5 %collective-permute-start.4 = (bf16[32,2048]{1,0:T(8,128)(2,1)S(1)}, bf16[32,2048]{1,0:T(8,128)(2,1)S(1)}, u32[]{:S(2)}, u32[]{:S(2)}) collective-permute-start(bf16[32,2048]{1,0:T(8,128)(2,1)S(1)} %copy-done), channel_id=1, source_target_pairs={{0,1},{1,0},{2,3},{3,2},{4,5},{5,4},{6,7},{7,6},{8,9},{9,8},{10,11... | collective-permute-start | bytes 393224 | tf_op jit(solution)/shard_map/ppermute | solution.py:235
  12.2 4.5 %collective-permute-start.5 = (bf16[32,2048]{1,0:T(8,128)(2,1)S(1)}, bf16[32,2048]{1,0:T(8,128)(2,1)S(1)}, u32[]{:S(2)}, u32[]{:S(2)}) collective-permute-start(bf16[32,2048]{1,0:T(8,128)(2,1)S(1)} %collective-permute-done.3.refs_0_), channel_id=1, source_target_pairs={{0,1},{1,0},{2,3},{3,2},{4,5},{5,4},{6,7},{7,6},{8,9},{9,8},{10,11... | collective-permute-start | bytes 393224 | tf_op jit(solution)/shard_map/ppermute | solution.py:235
  12.7 4.0 %collective-permute-start.6 = (bf16[32,2048]{1,0:T(8,128)(2,1)S(1)}, bf16[32,2048]{1,0:T(8,128)(2,1)S(1)}, u32[]{:S(2)}, u32[]{:S(2)}) collective-permute-start(bf16[32,2048]{1,0:T(8,128)(2,1)S(1)} %collective-permute-done.refs_0_), channel_id=1, source_target_pairs={{0,1},{1,0},{2,3},{3,2},{4,5},{5,4},{6,7},{7,6},{8,9},{9,8},{10,11... | collective-permute-start | bytes 393224 | tf_op jit(solution)/shard_map/ppermute | solution.py:235
  16.7 2.1 %collective-permute-start.2 = (bf16[32,2048]{1,0:T(8,128)(2,1)S(1)}, bf16[32,2048]{1,0:T(8,128)(2,1)S(1)}, u32[]{:S(2)}, u32[]{:S(2)}) collective-permute-start(bf16[32,2048]{1,0:T(8,128)(2,1)S(1)} %collective-permute-done.1.refs_0_), channel_id=1, source_target_pairs={{0,1},{1,0},{2,3},{3,2},{4,5},{5,4},{6,7},{7,6},{8,9},{9,8},{10,11... | collective-permute-start | bytes 393224 | tf_op jit(solution)/shard_map/ppermute | solution.py:235
  21.6 2.2 %collective-permute-start.7 = (bf16[32,2048]{1,0:T(8,128)(2,1)S(1)}, bf16[32,2048]{1,0:T(8,128)(2,1)S(1)}, u32[]{:S(2)}, u32[]{:S(2)}) collective-permute-start(bf16[32,2048]{1,0:T(8,128)(2,1)S(1)} %get-tuple-element.65), channel_id=1, source_target_pairs={{0,1},{1,0},{2,3},{3,2},{4,5},{5,4},{6,7},{7,6},{8,9},{9,8},{10,11... | collective-permute-start | bytes 393224 | tf_op jit(solution)/shard_map/ppermute | solution.py:235
  23.8 5.5 %collective-permute-start.8 = (bf16[32,2048]{1,0:T(8,128)(2,1)S(1)}, bf16[32,2048]{1,0:T(8,128)(2,1)S(1)}, u32[]{:S(2)}, u32[]{:S(2)}) collective-permute-start(bf16[32,2048]{1,0:T(8,128)(2,1)S(1)} %third_added.1), channel_id=1, source_target_pairs={{0,2},{1,3},{2,0},{3,1},{4,6},{5,7},{6,4},{7,5},{8,10},{9,11},{10,... | collective-permute-start | bytes 393224 | tf_op jit(solution)/shard_map/ppermute | solution.py:235
  24.7 6.1 %collective-permute-start.9 = (bf16[32,2048]{1,0:T(8,128)(2,1)S(1)}, bf16[32,2048]{1,0:T(8,128)(2,1)S(1)}, u32[]{:S(2)}, u32[]{:S(2)}) collective-permute-start(bf16[32,2048]{1,0:T(8,128)(2,1)S(1)} %get-tuple-element.74), channel_id=1, source_target_pairs={{0,1},{1,0},{2,3},{3,2},{4,5},{5,4},{6,7},{7,6},{8,9},{9,8},{10,11... | collective-permute-start | bytes 393224 | tf_op jit(solution)/shard_map/ppermute | solution.py:235
  24.7 6.1 %collective-permute-start.10 = (bf16[32,2048]{1,0:T(8,128)(2,1)S(1)}, bf16[32,2048]{1,0:T(8,128)(2,1)S(1)}, u32[]{:S(2)}, u32[]{:S(2)}) collective-permute-start(bf16[32,2048]{1,0:T(8,128)(2,1)S(1)} %get-tuple-element.76), channel_id=1, source_target_pairs={{0,1},{1,0},{2,3},{3,2},{4,5},{5,4},{6,7},{7,6},{8,9},{9,8},{10,11... | collective-permute-start | bytes 393224 | tf_op jit(solution)/shard_map/ppermute | solution.py:235
  25.3 5.6 %collective-permute-start.11 = (bf16[32,2048]{1,0:T(8,128)(2,1)S(1)}, bf16[32,2048]{1,0:T(8,128)(2,1)S(1)}, u32[]{:S(2)}, u32[]{:S(2)}) collective-permute-start(bf16[32,2048]{1,0:T(8,128)(2,1)S(1)} %get-tuple-element.78), channel_id=1, source_target_pairs={{0,1},{1,0},{2,3},{3,2},{4,5},{5,4},{6,7},{7,6},{8,9},{9,8},{10,11... | collective-permute-start | bytes 393224 | tf_op jit(solution)/shard_map/ppermute | solution.py:235
  25.6 11.1 %collective-permute-start.15 = (bf16[8,16,512]{2,1,0:T(8,128)(2,1)S(1)}, bf16[8,16,512]{2,1,0:T(8,128)(2,1)S(1)}, u32[]{:S(2)}, u32[]{:S(2)}) collective-permute-start(bf16[8,16,512]{2,1,0:T(8,128)(2,1)S(1)} %get-tuple-element.90), channel_id=1, source_target_pairs={{0,24},{8,16},{16,8},{24,0},{1,25},{9,17},{17,9},{25,1},{2,26},{10... | collective-permute-start | bytes 393224 | tf_op jit(solution)/shard_map/ppermute | solution.py:235
  29.3 7.3 %collective-permute-start.16 = (bf16[8,16,512]{2,1,0:T(8,128)(2,1)S(1)}, bf16[8,16,512]{2,1,0:T(8,128)(2,1)S(1)}, u32[]{:S(2)}, u32[]{:S(2)}) collective-permute-start(bf16[8,16,512]{2,1,0:T(8,128)(2,1)S(1)} %get-tuple-element.91), channel_id=1, source_target_pairs={{0,8},{8,0},{16,24},{24,16},{1,9},{9,1},{17,25},{25,17},{2,10},{10... | collective-permute-start | bytes 393224 | tf_op jit(solution)/shard_map/ppermute | solution.py:235
  31.0 8.1 %collective-permute-start.12 = (bf16[32,2048]{1,0:T(8,128)(2,1)S(1)}, bf16[32,2048]{1,0:T(8,128)(2,1)S(1)}, u32[]{:S(2)}, u32[]{:S(2)}) collective-permute-start(bf16[32,2048]{1,0:T(8,128)(2,1)S(1)} %get-tuple-element.86), channel_id=1, source_target_pairs={{0,4},{1,5},{2,6},{3,7},{4,0},{5,1},{6,2},{7,3},{8,12},{9,13},{10,... | collective-permute-start | bytes 393224 | tf_op jit(solution)/shard_map/ppermute | solution.py:235
  33.4 6.0 %collective-permute-start.13 = (bf16[32,2048]{1,0:T(8,128)(2,1)S(1)}, bf16[32,2048]{1,0:T(8,128)(2,1)S(1)}, u32[]{:S(2)}, u32[]{:S(2)}) collective-permute-start(bf16[32,2048]{1,0:T(8,128)(2,1)S(1)} %get-tuple-element.87), channel_id=1, source_target_pairs={{0,2},{1,3},{2,0},{3,1},{4,6},{5,7},{6,4},{7,5},{8,10},{9,11},{10,... | collective-permute-start | bytes 393224 | tf_op jit(solution)/shard_map/ppermute | solution.py:235
  35.1 5.0 %collective-permute-start.14 = (bf16[8,16,512]{2,1,0:T(8,128)(2,1)S(1)}, bf16[8,16,512]{2,1,0:T(8,128)(2,1)S(1)}, u32[]{:S(2)}, u32[]{:S(2)}) collective-permute-start(bf16[8,16,512]{2,1,0:T(8,128)(2,1)S(1)} %get-tuple-element.88), channel_id=1, source_target_pairs={{0,16},{8,24},{16,0},{24,8},{1,17},{9,25},{17,1},{25,9},{2,18},{10... | collective-permute-start | bytes 393224 | tf_op jit(solution)/shard_map/ppermute | solution.py:235

commit v7 on v6

--- a/solution.py
+++ b/solution.py
@@ -720,34 +720,47 @@
     )(*pages)
 
 
-def finish_kernel(mask, base_ref, *refs):
-    *parts, page_ref, _, output_ref, cache_ref, sem = refs
-    target = cache_ref.at[0, lax.axis_index("dp") ^ mask]
-    copy = pltpu.make_async_copy(page_ref, target, sem)
-    copy.start()
+def finish_kernel(masks, base_ref, *refs):
+    count = len(masks)
+    *parts, _, output_ref, cache_ref, total_scr, sems = refs
+    parts, pages = parts[:-count], parts[-count:]
+    group = lax.axis_index("dp")
+    copies = [
+        pltpu.make_async_copy(page_ref, cache_ref.at[0, group ^ mask], sems.at[number])
+        for number, (mask, page_ref) in enumerate(zip(masks, pages))
+    ]
+    for copy in copies:
+        copy.start()
     total = base_ref[...]
     for part_ref in parts:
         total = total + part_ref[...].astype(jnp.float32)
-    output_ref[...] = total
-    copy.wait()
-
-
-def finished(base, parts, mask, page, cache):
-    count = len(parts)
+    total_scr[...] = total
+    copies.append(pltpu.make_async_copy(total_scr, output_ref, sems.at[count]))
+    copies[-1].start()
+    for copy in copies:
+        copy.wait()
+
+
+def finished(base, parts, masks, pages, cache):
+    count = len(pages)
     return pl.pallas_call(
-        functools.partial(finish_kernel, mask),
+        functools.partial(finish_kernel, masks),
         out_shape=[
             jax.ShapeDtypeStruct(base.shape, base.dtype),
             jax.ShapeDtypeStruct(cache.shape, cache.dtype),
         ],
-        in_specs=vmem_specs(1 + count)
-        + [pl.BlockSpec(memory_space=pl.ANY), pl.BlockSpec(memory_space=pltpu.HBM)],
-        out_specs=vmem_specs(1) + [pl.BlockSpec(memory_space=pltpu.HBM)],
-        scratch_shapes=[pltpu.SemaphoreType.DMA(())],
-        input_output_aliases={count + 2: 1},
+        in_specs=vmem_specs(1 + len(parts))
+        + [pl.BlockSpec(memory_space=pl.ANY)] * count
+        + [pl.BlockSpec(memory_space=pltpu.HBM)],
+        out_specs=[pl.BlockSpec(memory_space=pltpu.HBM)] * 2,
+        scratch_shapes=[
+            pltpu.VMEM(base.shape, base.dtype),
+            pltpu.SemaphoreType.DMA((count + 1,)),
+        ],
+        input_output_aliases={1 + len(parts) + count: 1},
         compiler_params=parameters(4),
         name="finished",
-    )(base, *parts, page, cache)
+    )(base, *parts, *pages, cache)
 
 
 def shards_whole_heads(
@@ -764,8 +777,6 @@
     replica_count = lax.axis_size("dp")
     to_chip = [mask * CORES for mask in range(CHIPS)]
     second = exchanged(hidden_states, "tensor", to_chip[2])
-    first = exchanged(hidden_states, "tensor", to_chip[1])
-    beside = exchanged(hidden_states, "tensor", 1)
     staged = (
         segments,
         page_targets.reshape(1, -1),
@@ -781,6 +792,8 @@
     heads, upward, downward = weights
     destinations, own_joined, own_hidden = staged[12:]
 
+    first = exchanged(hidden, "tensor", to_chip[1])
+    beside = exchanged(hidden, "tensor", 1)
     second, own_joined = lax.optimization_barrier((second, own_joined))
     third = exchanged(second, "tensor", to_chip[1])
     second_beside = exchanged(second, "tensor", 1)
@@ -816,15 +829,15 @@
     passing = exchanged(third_sum, "tensor", to_chip[1])
     pairs = [(exchanged(sibling, "tensor", 1), own) for sibling, own in zip(siblings, owns)]
     pages = cached_pages(joined, destinations, replica_count)
-    early, late = (3, 1), 2
+    early, late = (3,), (1, 2)
     arriving = [exchanged(pages[mask], "dp", mask) for mask in early]
     second_sum, first_sum, base = remaining_sums(passing, pairs, hidden)
     from_second = exchanged(second_sum, "tensor", to_chip[2])
     from_first = exchanged(first_sum, "tensor", to_chip[1])
-    base, late_page = lax.optimization_barrier((base, pages[late]))
-    late_page = exchanged(late_page, "dp", late)
+    base, late_pages = lax.optimization_barrier((base, [pages[mask] for mask in late]))
+    late_pages = [exchanged(page, "dp", mask) for mask, page in zip(late, late_pages)]
     cache_pages = placed((0,) + early, [pages[0]] + arriving, replica_count)
-    return tuple(finished(base, (from_second, from_first), late, late_page, cache_pages))
+    return tuple(finished(base, (from_second, from_first), late, late_pages, cache_pages))
 
 
 def solution(mesh):

time: 41.6 us -> 41.3 us (level)
  waiting for transfers between devices: 6.25 us -> 7.37 us
  starting transfers between devices: 18.4 us -> 17.6 us
  Pallas kernels: 16 us -> 15.4 us
    ppermute x17, waiting for transfers between devices: 6.25 us -> 7.37 us  [exchanged(): lax.ppermute(block, axis, [(member, member ^ mask) for member in range(co...]
    ppermute x17, starting transfers between devices: 18.4 us -> 17.6 us  [exchanged(): lax.ppermute(block, axis, [(member, member ^ mask) for member in range(co...]
    pallas_call x1, Pallas kernels: 1.37 us -> 0.83 us  [finished(): pl.pallas_call(functools.partial(finish_kernel, masks), out_shape=[jax.Sh...]
  transfers between devices with their start and end apart: 17 -> 17, of which waited for: 5 -> 3; matrix products, arithmetic and copies ran while one was open for 0% -> 0% of each run, Pallas kernels for 28% -> 28%
where the time goes in v7:
time: 41.3 us; the launch traced here: 41.2 us
  starting transfers between devices  17.6 us (43%)
  Pallas kernels  15.4 us (37%)
  waiting for transfers between devices  7.37 us (18%)
  between operations  0.74 us (2%)
    ppermute x17, starting transfers between devices, exchanged(): lax.ppermute(block, axis, [(member, member ^ mask) for member in range(co...  17.6 us
    ppermute x17, waiting for transfers between devices, exchanged(): lax.ppermute(block, axis, [(member, member ^ mask) for member in range(co...  7.37 us
    pallas_call x1, Pallas kernels, own_rows(): pl.pallas_call(functools.partial(own_kernel, count, replica_count), out_s...  5.28 us
    pallas_call x2, Pallas kernels, middle_rows(): pl.pallas_call(functools.partial(middle_kernel, origins), out_shape=[pltp...  3.7 us
    pallas_call x1, Pallas kernels, last_rows(): pl.pallas_call(last_kernel, out_shape=[pltpu.VMEM((tokens, 3 * HD), jnp.b...  2.83 us
    pallas_call x1, Pallas kernels, kind_rows(): pl.pallas_call(functools.partial(kind_kernel, kinds), out_shape=[pltpu.VM...  1.6 us
    pallas_call x1, Pallas kernels, finished(): pl.pallas_call(functools.partial(finish_kernel, masks), out_shape=[jax.Sh...  0.83 us
  transfers between devices with their start and end apart: 17, of which 3 were waited for; matrix products, arithmetic and copies ran while one was open for 0% of the time, Pallas kernels for 28%

profile of v7, /device:TPU:0, one launch (start us, length us, event | category | flops | bytes accessed | tf_op | source)
XLA Modules:
  0.0 41.2 jit_solution(16897635064584615600)
XLA Ops:
  0.6 4.1 %collective-permute-start = (bf16[32,2048]{1,0:T(8,128)(2,1)}, bf16[32,2048]{1,0:T(8,128)(2,1)S(1)}, u32[]{:S(2)}, u32[]{:S(2)}) collective-permute-start(bf16[32,2048]{1,0:T(8,128)(2,1)} %refs_2_.1), channel_id=1, source_target_pairs={{0,4},{1,5},{2,6},{3,7},{4,0},{5,1},{6,2},{7,3},{8,12},{9,13},{10,... | collective-permute-start | bytes 393224 | tf_op jit(solution)/shard_map/ppermute | solution.py:235
  4.7 5.3 %own_rows.1 = (s32[1,256]{1,0:T(1,128)}, s32[1,16]{1,0:T(1,128)}, bf16[32,2048]{1,0:T(8,128)(2,1)S(1)}, f32[1,2048]{1,0:T(1,128)S(1)}, f32[1,2048]{1,0:T(1,128)S...) custom-call(s32[1,256]{1,0:T(1,128)} %refs_0_.1, ...), custom_call_target="tpu_custom_call" | custom-call | flops 234881024 | bytes 11682880 | tf_op jit(solution)/shard_map/own_rows/pallas_call | solution.py:452
  10.0 1.6 %collective-permute-start.3 = (bf16[32,2048]{1,0:T(8,128)(2,1)S(1)}, bf16[32,2048]{1,0:T(8,128)(2,1)S(1)}, u32[]{:S(2)}, u32[]{:S(2)}) collective-permute-start(bf16[32,2048]{1,0:T(8,128)(2,1)S(1)} %get-tuple-element.60.refs_6_), channel_id=1, source_target_pairs={{0,2},{1,3},{2,0},{3,1},{4,6},{5,7},{6,4},{7,5},{8,10},{9,11},{10,... | collective-permute-start | bytes 393224 | tf_op jit(solution)/shard_map/ppermute | solution.py:235
  11.7 0.0 collective-permute-done.refs_0_
  11.7 0.5 %collective-permute-start.1 = (bf16[32,2048]{1,0:T(8,128)(2,1)S(1)}, bf16[32,2048]{1,0:T(8,128)(2,1)S(1)}, u32[]{:S(2)}, u32[]{:S(2)}) collective-permute-start(bf16[32,2048]{1,0:T(8,128)(2,1)S(1)} %collective-permute-done.refs_0_), channel_id=1, source_target_pairs={{0,2},{1,3},{2,0},{3,1},{4,6},{5,7},{6,4},{7,5},{8,10},{9,11},{10,... | collective-permute-start | bytes 393224 | tf_op jit(solution)/shard_map/ppermute | solution.py:235
  12.1 0.0 collective-permute-start.4
  12.1 0.5 %collective-permute-start.6 = (bf16[32,2048]{1,0:T(8,128)(2,1)S(1)}, bf16[32,2048]{1,0:T(8,128)(2,1)S(1)}, u32[]{:S(2)}, u32[]{:S(2)}) collective-permute-start(bf16[32,2048]{1,0:T(8,128)(2,1)S(1)} %collective-permute-done.refs_0_), channel_id=1, source_target_pairs={{0,1},{1,0},{2,3},{3,2},{4,5},{5,4},{6,7},{7,6},{8,9},{9,8},{10,11... | collective-permute-start | bytes 393224 | tf_op jit(solution)/shard_map/ppermute | solution.py:235
  12.6 3.8 %collective-permute-done.3.refs_0_ = bf16[32,2048]{1,0:T(8,128)(2,1)S(1)} collective-permute-done((bf16[32,2048]{1,0:T(8,128)(2,1)S(1)}, bf16[32,2048]{1,0:T(8,128)(2,1)S(1)}, u32[]{:S(2)}, u32[]{:S(2)}) %collective-permute-start.3) | collective-permute-done | bytes 131104 | tf_op jit(solution)/shard_map/ppermute | solution.py:235
  16.4 0.0 collective-permute-start.5
  16.4 1.6 %there_rows.1 = (bf16[32,768]{1,0:T(8,128)(2,1)S(1)}, bf16[32,1024]{1,0:T(8,128)(2,1)S(1)}) custom-call(bf16[32,2048]{1,0:T(8,128)(2,1)S(1)} %collective-permute-done.refs_0_, f32[1,2048]{1,0:T(1,128)S(1)} %get-tuple-element.50.refs_1_.refs_4_.refs_2_, f32[1,2048]{1,0:T(1,128)S(1)} %get-tuple-element.51.refs_2_.refs_5_.refs_3_, ...), custom_call_target="tpu_custom_call" | custom-call | flops 234881024 | bytes 1048576 | tf_op jit(solution)/shard_map/there_rows/pallas_call | solution.py:492
  18.1 0.6 %collective-permute-start.2 = (bf16[32,2048]{1,0:T(8,128)(2,1)S(1)}, bf16[32,2048]{1,0:T(8,128)(2,1)S(1)}, u32[]{:S(2)}, u32[]{:S(2)}) collective-permute-start(bf16[32,2048]{1,0:T(8,128)(2,1)S(1)} %collective-permute-done.1.refs_0_), channel_id=1, source_target_pairs={{0,1},{1,0},{2,3},{3,2},{4,5},{5,4},{6,7},{7,6},{8,9},{9,8},{10,11... | collective-permute-start | bytes 393224 | tf_op jit(solution)/shard_map/ppermute | solution.py:235
  18.6 0.0 collective-permute-done.4.refs_1_
  18.6 0.0 collective-permute-done.6.refs_3_
  18.7 2.1 %beside_rows.1 = (bf16[128,768]{1,0:T(8,128)(2,1)S(1)}, bf16[128,1024]{1,0:T(8,128)(2,1)S(1)}, bf16[256,2048]{1,0:T(8,128)(2,1)S(1)}) custom-call(bf16[32,2048]{1,0:T(8,128)(2,1)S(1)} %collective-permute-done.3.refs_0_, bf16[32,2048]{1,0:T(8,128)(2,1)S(1)} %collective-permute-done.4.refs_1_, bf16[32,2048]{1,0:T(8,128)(2,1)S(1)} %collective-permute-done.5.refs_2_, ...), custom_call_target="tpu_custom_call" | custom-call | flops 939524096 | bytes 1048576 | tf_op jit(solution)/shard_map/beside_rows/pallas_call | solution.py:492
  20.8 2.8 %last_rows.1 = (bf16[256,768]{1,0:T(8,128)(2,1)S(1)}, bf16[32,2048]{1,0:T(8,128)(2,1)S(1)}, f32[32,2048]{1,0:T(8,128)S(1)}) custom-call(bf16[32,2048]{1,0:T(8,128)(2,1)S(1)} %collective-permute-done.1.refs_0_, bf16[32,2048]{1,0:T(8,128)(2,1)S(1)} %collective-permute-done.2.refs_1_, f32[1,2048]{1,0:T(1,128)S(1)} %get-tuple-element.50.refs_1_.refs_4_.refs_2_, ...), custom_call_target="tpu_custom_call" | custom-call | flops 805306368 | bytes 1048576 | tf_op jit(solution)/shard_map/last_rows/pallas_call | solution.py:564
  23.6 0.1 collective-permute-start.7
  23.7 1.6 %rest_rows.1 = (bf16[32,2048]{1,0:T(8,128)(2,1)S(1)}, bf16[32,2048]{1,0:T(8,128)(2,1)S(1)}, bf16[32,2048]{1,0:T(8,128)(2,1)S(1)}, f32[32,2048]{1,0:T(8,128)S(1)}...) custom-call(bf16[256,768]{1,0:T(8,128)(2,1)S(1)} %get-tuple-element.83.joined_ref, ...), custom_call_target="tpu_custom_call" | custom-call | flops 1006632960 | bytes 1048576 | tf_op jit(solution)/shard_map/rest_rows/pallas_call | solution.py:608
  25.3 1.6 %collective-permute-start.8 = (bf16[32,2048]{1,0:T(8,128)(2,1)S(1)}, bf16[32,2048]{1,0:T(8,128)(2,1)S(1)}, u32[]{:S(2)}, u32[]{:S(2)}) collective-permute-start(bf16[32,2048]{1,0:T(8,128)(2,1)S(1)} %third_added.1), channel_id=1, source_target_pairs={{0,2},{1,3},{2,0},{3,1},{4,6},{5,7},{6,4},{7,5},{8,10},{9,11},{10,... | collective-permute-start | bytes 393224 | tf_op jit(solution)/shard_map/ppermute | solution.py:235
  27.0 0.2 collective-permute-start.9
  27.2 0.3 collective-permute-start.10
  27.5 0.2 collective-permute-start.11
  27.7 0.3 cached_pages.1
  28.0 2.5 %collective-permute-start.16 = (bf16[8,16,512]{2,1,0:T(8,128)(2,1)S(1)}, bf16[8,16,512]{2,1,0:T(8,128)(2,1)S(1)}, u32[]{:S(2)}, u32[]{:S(2)}) collective-permute-start(bf16[8,16,512]{2,1,0:T(8,128)(2,1)S(1)} %get-tuple-element.93), channel_id=1, source_target_pairs={{0,24},{8,16},{16,8},{24,0},{1,25},{9,17},{17,9},{25,1},{2,26},{10... | collective-permute-start | bytes 393224 | tf_op jit(solution)/shard_map/ppermute | solution.py:235
  30.5 0.8 %collective-permute-done.8.passing_ref = bf16[32,2048]{1,0:T(8,128)(2,1)S(1)} collective-permute-done((bf16[32,2048]{1,0:T(8,128)(2,1)S(1)}, bf16[32,2048]{1,0:T(8,128)(2,1)S(1)}, u32[]{:S(2)}, u32[]{:S(2)}) %collective-permute-start.8) | collective-permute-done | bytes 131104 | tf_op jit(solution)/shard_map/ppermute | solution.py:235
  31.3 0.1 remaining_sums.1
  31.4 0.7 %collective-permute-start.12 = (bf16[32,2048]{1,0:T(8,128)(2,1)S(1)}, bf16[32,2048]{1,0:T(8,128)(2,1)S(1)}, u32[]{:S(2)}, u32[]{:S(2)}) collective-permute-start(bf16[32,2048]{1,0:T(8,128)(2,1)S(1)} %get-tuple-element.88), channel_id=1, source_target_pairs={{0,4},{1,5},{2,6},{3,7},{4,0},{5,1},{6,2},{7,3},{8,12},{9,13},{10,... | collective-permute-start | bytes 393224 | tf_op jit(solution)/shard_map/ppermute | solution.py:235
  32.1 1.7 %collective-permute-start.13 = (bf16[32,2048]{1,0:T(8,128)(2,1)S(1)}, bf16[32,2048]{1,0:T(8,128)(2,1)S(1)}, u32[]{:S(2)}, u32[]{:S(2)}) collective-permute-start(bf16[32,2048]{1,0:T(8,128)(2,1)S(1)} %get-tuple-element.89), channel_id=1, source_target_pairs={{0,2},{1,3},{2,0},{3,1},{4,6},{5,7},{6,4},{7,5},{8,10},{9,11},{10,... | collective-permute-start | bytes 393224 | tf_op jit(solution)/shard_map/ppermute | solution.py:235
  33.8 1.5 %collective-permute-start.14 = (bf16[8,16,512]{2,1,0:T(8,128)(2,1)S(1)}, bf16[8,16,512]{2,1,0:T(8,128)(2,1)S(1)}, u32[]{:S(2)}, u32[]{:S(2)}) collective-permute-start(bf16[8,16,512]{2,1,0:T(8,128)(2,1)S(1)} %get-tuple-element.90), channel_id=1, source_target_pairs={{0,8},{8,0},{16,24},{24,16},{1,9},{9,1},{17,25},{25,17},{2,10},{10... | collective-permute-start | bytes 393224 | tf_op jit(solution)/shard_map/ppermute | solution.py:235
  35.3 1.5 %collective-permute-start.15 = (bf16[8,16,512]{2,1,0:T(8,128)(2,1)S(1)}, bf16[8,16,512]{2,1,0:T(8,128)(2,1)S(1)}, u32[]{:S(2)}, u32[]{:S(2)}) collective-permute-start(bf16[8,16,512]{2,1,0:T(8,128)(2,1)S(1)} %get-tuple-element.91), channel_id=1, source_target_pairs={{0,16},{8,24},{16,0},{24,8},{1,17},{9,25},{17,1},{25,9},{2,18},{10... | collective-permute-start | bytes 393224 | tf_op jit(solution)/shard_map/ppermute | solution.py:235
  36.8 0.7 %placed.1.refs_4_ = bf16[1,4,8,16,512]{4,3,2,1,0:T(8,128)(2,1)} custom-call(bf16[8,16,512]{2,1,0:T(8,128)(2,1)S(1)} %get-tuple-element.92.refs_0_, bf16[8,16,512]{2,1,0:T(8,128)(2,1)S(1)} %collective-permute-done.16.refs_1_), custom_call_target="tpu_custom_call" | custom-call | tf_op jit(solution)/shard_map/placed/pallas_call | solution.py:712
  37.6 2.8 %collective-permute-done.12.refs_0_ = bf16[32,2048]{1,0:T(8,128)(2,1)S(1)} collective-permute-done((bf16[32,2048]{1,0:T(8,128)(2,1)S(1)}, bf16[32,2048]{1,0:T(8,128)(2,1)S(1)}, u32[]{:S(2)}, u32[]{:S(2)}) %collective-permute-start.12) | collective-permute-done | bytes 131104 | tf_op jit(solution)/shard_map/ppermute | solution.py:235
  40.3 0.8 %finished.1 = (f32[32,2048]{1,0:T(8,128)}, bf16[1,4,8,16,512]{4,3,2,1,0:T(8,128)(2,1)}) custom-call(f32[32,2048]{1,0:T(8,128)S(1)} %get-tuple-element.87.base_ref, bf16[32,2048]{1,0:T(8,128)(2,1)S(1)} %collective-permute-done.12.refs_0_, bf16[32,2048]{1,0:T(8,128)(2,1)S(1)} %collective-permute-done.13.refs_1_, ...), custom_call_target="tpu_custom_call", output_to_operand_aliasing={{1}: (5, {})} | custom-call | tf_op jit(solution)/shard_map/finished/pallas_call | solution.py:746
  (12 shorter events, 0.1 us)
Async XLA Ops:
  0.6 11.0 %collective-permute-start = (bf16[32,2048]{1,0:T(8,128)(2,1)}, bf16[32,2048]{1,0:T(8,128)(2,1)S(1)}, u32[]{:S(2)}, u32[]{:S(2)}) collective-permute-start(bf16[32,2048]{1,0:T(8,128)(2,1)} %refs_2_.1), channel_id=1, source_target_pairs={{0,4},{1,5},{2,6},{3,7},{4,0},{5,1},{6,2},{7,3},{8,12},{9,13},{10,... | collective-permute-start | bytes 393224 | tf_op jit(solution)/shard_map/ppermute | solution.py:235
  10.0 6.4 %collective-permute-start.3 = (bf16[32,2048]{1,0:T(8,128)(2,1)S(1)}, bf16[32,2048]{1,0:T(8,128)(2,1)S(1)}, u32[]{:S(2)}, u32[]{:S(2)}) collective-permute-start(bf16[32,2048]{1,0:T(8,128)(2,1)S(1)} %get-tuple-element.60.refs_6_), channel_id=1, source_target_pairs={{0,2},{1,3},{2,0},{3,1},{4,6},{5,7},{6,4},{7,5},{8,10},{9,11},{10,... | collective-permute-start | bytes 393224 | tf_op jit(solution)/shard_map/ppermute | solution.py:235
  11.7 6.4 %collective-permute-start.1 = (bf16[32,2048]{1,0:T(8,128)(2,1)S(1)}, bf16[32,2048]{1,0:T(8,128)(2,1)S(1)}, u32[]{:S(2)}, u32[]{:S(2)}) collective-permute-start(bf16[32,2048]{1,0:T(8,128)(2,1)S(1)} %collective-permute-done.refs_0_), channel_id=1, source_target_pairs={{0,2},{1,3},{2,0},{3,1},{4,6},{5,7},{6,4},{7,5},{8,10},{9,11},{10,... | collective-permute-start | bytes 393224 | tf_op jit(solution)/shard_map/ppermute | solution.py:235
  12.1 6.5 %collective-permute-start.4 = (bf16[32,2048]{1,0:T(8,128)(2,1)S(1)}, bf16[32,2048]{1,0:T(8,128)(2,1)S(1)}, u32[]{:S(2)}, u32[]{:S(2)}) collective-permute-start(bf16[32,2048]{1,0:T(8,128)(2,1)S(1)} %get-tuple-element.60.refs_6_), channel_id=1, source_target_pairs={{0,1},{1,0},{2,3},{3,2},{4,5},{5,4},{6,7},{7,6},{8,9},{9,8},{10,11... | collective-permute-start | bytes 393224 | tf_op jit(solution)/shard_map/ppermute | solution.py:235
  12.1 6.5 %collective-permute-start.6 = (bf16[32,2048]{1,0:T(8,128)(2,1)S(1)}, bf16[32,2048]{1,0:T(8,128)(2,1)S(1)}, u32[]{:S(2)}, u32[]{:S(2)}) collective-permute-start(bf16[32,2048]{1,0:T(8,128)(2,1)S(1)} %collective-permute-done.refs_0_), channel_id=1, source_target_pairs={{0,1},{1,0},{2,3},{3,2},{4,5},{5,4},{6,7},{7,6},{8,9},{9,8},{10,11... | collective-permute-start | bytes 393224 | tf_op jit(solution)/shard_map/ppermute | solution.py:235
  16.4 2.2 %collective-permute-start.5 = (bf16[32,2048]{1,0:T(8,128)(2,1)S(1)}, bf16[32,2048]{1,0:T(8,128)(2,1)S(1)}, u32[]{:S(2)}, u32[]{:S(2)}) collective-permute-start(bf16[32,2048]{1,0:T(8,128)(2,1)S(1)} %collective-permute-done.3.refs_0_), channel_id=1, source_target_pairs={{0,1},{1,0},{2,3},{3,2},{4,5},{5,4},{6,7},{7,6},{8,9},{9,8},{10,11... | collective-permute-start | bytes 393224 | tf_op jit(solution)/shard_map/ppermute | solution.py:235
  18.1 2.7 %collective-permute-start.2 = (bf16[32,2048]{1,0:T(8,128)(2,1)S(1)}, bf16[32,2048]{1,0:T(8,128)(2,1)S(1)}, u32[]{:S(2)}, u32[]{:S(2)}) collective-permute-start(bf16[32,2048]{1,0:T(8,128)(2,1)S(1)} %collective-permute-done.1.refs_0_), channel_id=1, source_target_pairs={{0,1},{1,0},{2,3},{3,2},{4,5},{5,4},{6,7},{7,6},{8,9},{9,8},{10,11... | collective-permute-start | bytes 393224 | tf_op jit(solution)/shard_map/ppermute | solution.py:235
  23.6 1.7 %collective-permute-start.7 = (bf16[32,2048]{1,0:T(8,128)(2,1)S(1)}, bf16[32,2048]{1,0:T(8,128)(2,1)S(1)}, u32[]{:S(2)}, u32[]{:S(2)}) collective-permute-start(bf16[32,2048]{1,0:T(8,128)(2,1)S(1)} %get-tuple-element.67), channel_id=1, source_target_pairs={{0,1},{1,0},{2,3},{3,2},{4,5},{5,4},{6,7},{7,6},{8,9},{9,8},{10,11... | collective-permute-start | bytes 393224 | tf_op jit(solution)/shard_map/ppermute | solution.py:235
  25.3 5.9 %collective-permute-start.8 = (bf16[32,2048]{1,0:T(8,128)(2,1)S(1)}, bf16[32,2048]{1,0:T(8,128)(2,1)S(1)}, u32[]{:S(2)}, u32[]{:S(2)}) collective-permute-start(bf16[32,2048]{1,0:T(8,128)(2,1)S(1)} %third_added.1), channel_id=1, source_target_pairs={{0,2},{1,3},{2,0},{3,1},{4,6},{5,7},{6,4},{7,5},{8,10},{9,11},{10,... | collective-permute-start | bytes 393224 | tf_op jit(solution)/shard_map/ppermute | solution.py:235
  27.0 4.3 %collective-permute-start.9 = (bf16[32,2048]{1,0:T(8,128)(2,1)S(1)}, bf16[32,2048]{1,0:T(8,128)(2,1)S(1)}, u32[]{:S(2)}, u32[]{:S(2)}) collective-permute-start(bf16[32,2048]{1,0:T(8,128)(2,1)S(1)} %get-tuple-element.76), channel_id=1, source_target_pairs={{0,1},{1,0},{2,3},{3,2},{4,5},{5,4},{6,7},{7,6},{8,9},{9,8},{10,11... | collective-permute-start | bytes 393224 | tf_op jit(solution)/shard_map/ppermute | solution.py:235
  27.2 4.1 %collective-permute-start.10 = (bf16[32,2048]{1,0:T(8,128)(2,1)S(1)}, bf16[32,2048]{1,0:T(8,128)(2,1)S(1)}, u32[]{:S(2)}, u32[]{:S(2)}) collective-permute-start(bf16[32,2048]{1,0:T(8,128)(2,1)S(1)} %get-tuple-element.78), channel_id=1, source_target_pairs={{0,1},{1,0},{2,3},{3,2},{4,5},{5,4},{6,7},{7,6},{8,9},{9,8},{10,11... | collective-permute-start | bytes 393224 | tf_op jit(solution)/shard_map/ppermute | solution.py:235
  27.5 3.8 %collective-permute-start.11 = (bf16[32,2048]{1,0:T(8,128)(2,1)S(1)}, bf16[32,2048]{1,0:T(8,128)(2,1)S(1)}, u32[]{:S(2)}, u32[]{:S(2)}) collective-permute-start(bf16[32,2048]{1,0:T(8,128)(2,1)S(1)} %get-tuple-element.80), channel_id=1, source_target_pairs={{0,1},{1,0},{2,3},{3,2},{4,5},{5,4},{6,7},{7,6},{8,9},{9,8},{10,11... | collective-permute-start | bytes 393224 | tf_op jit(solution)/shard_map/ppermute | solution.py:235
  28.0 8.8 %collective-permute-start.16 = (bf16[8,16,512]{2,1,0:T(8,128)(2,1)S(1)}, bf16[8,16,512]{2,1,0:T(8,128)(2,1)S(1)}, u32[]{:S(2)}, u32[]{:S(2)}) collective-permute-start(bf16[8,16,512]{2,1,0:T(8,128)(2,1)S(1)} %get-tuple-element.93), channel_id=1, source_target_pairs={{0,24},{8,16},{16,8},{24,0},{1,25},{9,17},{17,9},{25,1},{2,26},{10... | collective-permute-start | bytes 393224 | tf_op jit(solution)/shard_map/ppermute | solution.py:235
  31.4 8.9 %collective-permute-start.12 = (bf16[32,2048]{1,0:T(8,128)(2,1)S(1)}, bf16[32,2048]{1,0:T(8,128)(2,1)S(1)}, u32[]{:S(2)}, u32[]{:S(2)}) collective-permute-start(bf16[32,2048]{1,0:T(8,128)(2,1)S(1)} %get-tuple-element.88), channel_id=1, source_target_pairs={{0,4},{1,5},{2,6},{3,7},{4,0},{5,1},{6,2},{7,3},{8,12},{9,13},{10,... | collective-permute-start | bytes 393224 | tf_op jit(solution)/shard_map/ppermute | solution.py:235
  32.1 8.2 %collective-permute-start.13 = (bf16[32,2048]{1,0:T(8,128)(2,1)S(1)}, bf16[32,2048]{1,0:T(8,128)(2,1)S(1)}, u32[]{:S(2)}, u32[]{:S(2)}) collective-permute-start(bf16[32,2048]{1,0:T(8,128)(2,1)S(1)} %get-tuple-element.89), channel_id=1, source_target_pairs={{0,2},{1,3},{2,0},{3,1},{4,6},{5,7},{6,4},{7,5},{8,10},{9,11},{10,... | collective-permute-start | bytes 393224 | tf_op jit(solution)/shard_map/ppermute | solution.py:235
  33.8 6.5 %collective-permute-start.14 = (bf16[8,16,512]{2,1,0:T(8,128)(2,1)S(1)}, bf16[8,16,512]{2,1,0:T(8,128)(2,1)S(1)}, u32[]{:S(2)}, u32[]{:S(2)}) collective-permute-start(bf16[8,16,512]{2,1,0:T(8,128)(2,1)S(1)} %get-tuple-element.90), channel_id=1, source_target_pairs={{0,8},{8,0},{16,24},{24,16},{1,9},{9,1},{17,25},{25,17},{2,10},{10... | collective-permute-start | bytes 393224 | tf_op jit(solution)/shard_map/ppermute | solution.py:235
  35.3 5.0 %collective-permute-start.15 = (bf16[8,16,512]{2,1,0:T(8,128)(2,1)S(1)}, bf16[8,16,512]{2,1,0:T(8,128)(2,1)S(1)}, u32[]{:S(2)}, u32[]{:S(2)}) collective-permute-start(bf16[8,16,512]{2,1,0:T(8,128)(2,1)S(1)} %get-tuple-element.91), channel_id=1, source_target_pairs={{0,16},{8,24},{16,0},{24,8},{1,17},{9,25},{17,1},{25,9},{2,18},{10... | collective-permute-start | bytes 393224 | tf_op jit(solution)/shard_map/ppermute | solution.py:235

commit v8 on v7

--- a/solution.py
+++ b/solution.py
@@ -515,48 +515,36 @@
 
 
 def last_kernel(*refs):
-    blocks, (gain_a, gain_f, heads_ref, upward_ref, downward_ref, output_ref) = refs[:2], refs[2:8]
-    offsets_ref, *table_refs = refs[8:12]
-    pieces = refs[12:15]
-    joined_ref, sibling_ref, own_ref, attention_scr, feedforward_scr, hidden_scr = refs[15:]
+    blocks, (gain_a, gain_f, heads_ref, upward_ref, downward_ref, output_ref) = refs[:3], refs[3:9]
+    offsets_ref, *table_refs = refs[9:13]
+    own_joined_ref, middle_joined_ref = refs[13:15]
+    joined_ref, fed_ref, sibling_ref, own_ref = refs[15:19]
+    attention_scr, feedforward_scr, hidden_scr = refs[19:]
     block_rows = blocks[0].shape[0]
     tokens = joined_ref.shape[0]
-    first = tokens - CORES * block_rows
+    first = tokens - len(blocks) * block_rows
     normalize(blocks, [gain_a, gain_f], [attention_scr, feedforward_scr])
-    for kind in range(CHIPS - 1):
-        for half in range(CORES):
-            place = (kind * CORES + half) * block_rows
-            joined_ref[place : place + block_rows, :] = piece_of(pieces, kind, half, block_rows)
-    places = [position_of(CHIPS - 1, half, block_rows) for half in range(CORES)]
+    joined_ref[:block_rows, :] = own_joined_ref[...]
+    joined_ref[block_rows:first, :] = middle_joined_ref[...]
+    origins = ((CHIPS - 2, 1), (CHIPS - 1, 0), (CHIPS - 1, 1))
+    places = [position_of(kind, half, block_rows) for kind, half in origins]
     project(attention_scr, heads_ref, table_refs, places, joined_ref, first)
     hide(feedforward_scr, upward_ref, hidden_scr, 0)
-    attended = attend(joined_ref, offsets_ref, first, CORES * block_rows, block_rows)
-    partial_sums(attended, hidden_scr[...], output_ref, downward_ref, [own_ref], [sibling_ref])
-
-
-def piece_of(pieces, kind, half, block_rows):
-    piece, place = (0, 2, 1)[kind], 0
-    if half:
-        piece, place = 2, (kind + 1) * block_rows
-    return pieces[piece][place : place + block_rows, :]
-
-
-def partial_sums(attended, hidden, output_ref, downward_ref, own_refs, sibling_refs):
-    rows = attended.shape[0] // (2 * len(own_refs))
+    rows = CORES * block_rows
+    attended = attend(joined_ref, offsets_ref, tokens - rows, rows, block_rows)
     chunk = 512
     for begin in range(0, downward_ref.shape[1], chunk):
         columns = slice(begin, begin + chunk)
-        partial = jnp.dot(
-            hidden, downward_ref[:, columns], preferred_element_type=jnp.float32
-        ) + jnp.dot(attended, output_ref[:, columns], preferred_element_type=jnp.float32)
-        for number, (own_ref, sibling_ref) in enumerate(zip(own_refs, sibling_refs)):
-            first = 2 * number * rows
-            middle = first + rows
-            own_ref[:, columns] = partial[first:middle]
-            sibling_ref[:, columns] = partial[middle : middle + rows].astype(jnp.bfloat16)
-
-
-def last_rows(blocks, gains, weights, tables, pieces):
+        fed = jnp.dot(hidden_scr[...], downward_ref[:, columns], preferred_element_type=jnp.float32)
+        fed_ref[:, columns] = fed[:block_rows]
+        partial = fed[block_rows:] + jnp.dot(
+            attended, output_ref[:, columns], preferred_element_type=jnp.float32
+        )
+        own_ref[:, columns] = partial[:block_rows]
+        sibling_ref[:, columns] = partial[block_rows:].astype(jnp.bfloat16)
+
+
+def last_rows(blocks, gains, weights, tables, own_joined, middle_joined):
     block_rows, width = blocks[0].shape
     rows = len(blocks) * block_rows
     hidden_width = weights[1].shape[1]
@@ -565,11 +553,12 @@
         last_kernel,
         out_shape=[
             pltpu.VMEM((tokens, 3 * HD), jnp.bfloat16),
+            pltpu.VMEM((block_rows, width), jnp.float32),
             pltpu.VMEM((block_rows, width), jnp.bfloat16),
             pltpu.VMEM((block_rows, width), jnp.float32),
         ],
-        in_specs=vmem_specs(len(blocks) + 2 + 4 + 4 + 3),
-        out_specs=vmem_specs(3),
+        in_specs=vmem_specs(len(blocks) + 2 + 4 + 4 + 2),
+        out_specs=vmem_specs(4),
         scratch_shapes=[
             pltpu.VMEM((rows, width), jnp.bfloat16),
             pltpu.VMEM((rows, width), jnp.bfloat16),
@@ -582,42 +571,74 @@
             transcendentals=rows * hidden_width,
         ),
         name="last_rows",
-    )(*blocks, *gains, *weights, *tables, *pieces)
-
-
-def kind_kernel(kinds, joined_ref, offsets_ref, output_ref, downward_ref, *refs):
-    pieces, refs = refs[:3], refs[3:]
-    count = len(kinds)
-    siblings, owns = refs[:count], refs[count : 2 * count]
+    )(*blocks, *gains, *weights, *tables, own_joined, middle_joined)
+
+
+def fed_kernel(own_hidden_ref, middle_hidden_ref, downward_ref, fed_ref):
+    hidden = jnp.concatenate([own_hidden_ref[...], middle_hidden_ref[...]], 0)
+    chunk = 512
+    for begin in range(0, downward_ref.shape[1], chunk):
+        columns = slice(begin, begin + chunk)
+        fed_ref[:, columns] = jnp.dot(
+            hidden, downward_ref[:, columns], preferred_element_type=jnp.float32
+        )
+
+
+def fed_rows(own_hidden, middle_hidden, downward_weight):
+    rows = own_hidden.shape[0] + middle_hidden.shape[0]
+    depth, width = downward_weight.shape
+    return pl.pallas_call(
+        fed_kernel,
+        out_shape=pltpu.VMEM((rows, width), jnp.float32),
+        in_specs=vmem_specs(3),
+        out_specs=pl.BlockSpec(memory_space=pltpu.VMEM),
+        compiler_params=parameters(12),
+        cost_estimate=pl.CostEstimate(
+            flops=2 * rows * depth * width, bytes_accessed=MIB, transcendentals=0
+        ),
+        name="fed_rows",
+    )(own_hidden, middle_hidden, downward_weight)
+
+
+def rest_kernel(joined_ref, offsets_ref, output_ref, fed_ref, fed_beside_ref, *refs):
+    count = len(refs) // 2
+    siblings, owns = refs[:count], refs[count:]
     block_rows = owns[0].shape[0]
-    rows = CORES * block_rows * count
-    attended = attend(joined_ref, offsets_ref, kinds[0] * CORES * block_rows, rows, block_rows)
-    hidden = jnp.concatenate(
-        [piece_of(pieces, kind, half, block_rows) for kind in kinds for half in range(CORES)], 0
-    )
-    partial_sums(attended, hidden, output_ref, downward_ref, owns, siblings)
-
-
-def kind_rows(name, kinds, joined, offsets, weights, pieces):
-    block_rows = pieces[0].shape[0]
-    output_weight, downward_weight = weights
-    width = output_weight.shape[1]
-    shape = (block_rows, width)
-    count = len(kinds)
-    tokens = joined.shape[0]
-    return pl.pallas_call(
-        functools.partial(kind_kernel, kinds),
-        out_shape=[pltpu.VMEM(shape, jnp.bfloat16)] * count + [pltpu.VMEM(shape, jnp.float32)] * count,
-        in_specs=vmem_specs(7),
+    rows = fed_ref.shape[0] + fed_beside_ref.shape[0]
+    attended = attend(joined_ref, offsets_ref, 0, rows, block_rows)
+    chunk = 512
+    for begin in range(0, output_ref.shape[1], chunk):
+        columns = slice(begin, begin + chunk)
+        fed = jnp.concatenate([fed_ref[:, columns], fed_beside_ref[:, columns]], 0)
+        partial = fed + jnp.dot(
+            attended, output_ref[:, columns], preferred_element_type=jnp.float32
+        )
+        for number, (sibling_ref, own_ref) in enumerate(zip(siblings, owns)):
+            first = CORES * number * block_rows
+            middle = first + block_rows
+            own_ref[:, columns] = partial[first:middle]
+            sibling_ref[:, columns] = partial[middle : middle + block_rows].astype(jnp.bfloat16)
+
+
+def rest_rows(joined, offsets, output_weight, fed, fed_beside):
+    width = fed.shape[1]
+    rows = fed.shape[0] + fed_beside.shape[0]
+    count = CHIPS - 1
+    shape = (rows // (CORES * count), width)
+    shapes = [pltpu.VMEM(shape, dtype) for dtype in [jnp.bfloat16] * count + [jnp.float32] * count]
+    return pl.pallas_call(
+        rest_kernel,
+        out_shape=shapes,
+        in_specs=vmem_specs(5),
         out_specs=vmem_specs(2 * count),
         compiler_params=parameters(12),
         cost_estimate=pl.CostEstimate(
-            flops=4 * block_rows * count * width * (HD + downward_weight.shape[0]),
+            flops=2 * rows * width * HD,
             bytes_accessed=MIB,
-            transcendentals=2 * block_rows * count * tokens,
+            transcendentals=rows * joined.shape[0],
         ),
-        name=name,
-    )(joined, offsets, output_weight, downward_weight, *pieces)
+        name="rest_rows",
+    )(joined, offsets, output_weight, fed, fed_beside)
 
 
 def pages_kernel(joined_ref, destinations_ref, *page_refs):
@@ -777,6 +798,8 @@
     replica_count = lax.axis_size("dp")
     to_chip = [mask * CORES for mask in range(CHIPS)]
     second = exchanged(hidden_states, "tensor", to_chip[2])
+    first = exchanged(hidden_states, "tensor", to_chip[1])
+    beside = exchanged(hidden_states, "tensor", 1)
     staged = (
         segments,
         page_targets.reshape(1, -1),
@@ -792,37 +815,38 @@
     heads, upward, downward = weights
     destinations, own_joined, own_hidden = staged[12:]
 
-    first = exchanged(hidden, "tensor", to_chip[1])
-    beside = exchanged(hidden, "tensor", 1)
-    second, own_joined = lax.optimization_barrier((second, own_joined))
+    first, own_joined = lax.optimization_barrier((first, own_joined))
+    first_beside = exchanged(first, "tensor", 1)
+    second, first_beside, beside = lax.optimization_barrier((second, first_beside, beside))
     third = exchanged(second, "tensor", to_chip[1])
-    second_beside = exchanged(second, "tensor", 1)
-    first_beside = exchanged(first, "tensor", 1)
-    there_joined, there_hidden = middle_rows(
-        "there_rows", ((2, 0),), (second,), gains, (heads, upward), tables[1:]
-    )
-    third, there_joined = lax.optimization_barrier((third, there_joined))
-    third_beside = exchanged(third, "tensor", 1)
-    beside_joined, beside_hidden, output = middle_rows(
-        "beside_rows",
-        ((1, 0), (0, 1), (1, 1), (2, 1)),
-        (first, beside, first_beside, second_beside),
+    middle_joined, middle_hidden, output = middle_rows(
+        "middle_rows",
+        ((0, 1), (1, 0), (1, 1), (2, 0)),
+        (beside, first, first_beside, second),
         gains,
         (heads, upward),
         tables[1:],
         output_weight,
     )
-    joined, sibling, own = last_rows(
-        (third, third_beside),
+    second, middle_joined = lax.optimization_barrier((second, middle_joined))
+    second_beside = exchanged(second, "tensor", 1)
+    third, second_beside, middle_joined, middle_hidden = lax.optimization_barrier(
+        (third, second_beside, middle_joined, middle_hidden)
+    )
+    third_beside = exchanged(third, "tensor", 1)
+    fed = fed_rows(own_hidden, middle_hidden, downward)
+    third_beside, fed = lax.optimization_barrier((third_beside, fed))
+    joined, fed_beside, sibling, own = last_rows(
+        (second_beside, third, third_beside),
         gains,
         (heads, upward, downward, output),
         tables,
-        (own_joined, there_joined, beside_joined),
-    )
-
-    pieces = (own_hidden, there_hidden, beside_hidden)
+        own_joined,
+        middle_joined,
+    )
+
     received = exchanged(sibling, "tensor", 1)
-    partials = kind_rows("rest_rows", (0, 1, 2), joined, tables[0], (output, downward), pieces)
+    partials = rest_rows(joined, tables[0], output, fed, fed_beside)
     siblings, owns = partials[: CHIPS - 1], partials[CHIPS - 1 :]
     third_sum = added("third_added", own, received)
     third_sum, siblings, joined = lax.optimization_barrier((third_sum, siblings, joined))

time: 41.3 us -> 39.5 us (0.956)
  waiting for transfers between devices: 7.37 us -> 9.7 us
  starting transfers between devices: 17.6 us -> 15.4 us
  Pallas kernels: 15.4 us -> 13.6 us
    ppermute x17, waiting for transfers between devices: 7.37 us -> 9.7 us  [exchanged(): lax.ppermute(block, axis, [(member, member ^ mask) for member in range(co...]
    ppermute x17, starting transfers between devices: 17.6 us -> 15.4 us  [exchanged(): lax.ppermute(block, axis, [(member, member ^ mask) for member in range(co...]
    pallas_call x2 -> x1, Pallas kernels: 3.7 us -> 2.09 us  [middle_rows(): pl.pallas_call(functools.partial(middle_kernel, origins), out_shape=[pltp...]
    pallas_call x1 -> x2, Pallas kernels: 1.6 us -> 1.64 us  [the longest x1 0.85 us: fed_rows(): pl.pallas_call(fed_kernel, out_shape=pltpu.VMEM((rows, width), jnp.float3...]
  transfers between devices with their start and end apart: 17 -> 17, of which waited for: 3 -> 7; matrix products, arithmetic and copies ran while one was open for 0% -> 0% of each run, Pallas kernels for 28% -> 26%
where the time goes in v8:
time: 39.5 us; the launch traced here: 39.4 us
  starting transfers between devices  15.4 us (39%)
  Pallas kernels  13.6 us (34%)
  waiting for transfers between devices  9.7 us (25%)
  between operations  0.72 us (2%)
    ppermute x17, starting transfers between devices, exchanged(): lax.ppermute(block, axis, [(member, member ^ mask) for member in range(co...  15.4 us
    ppermute x17, waiting for transfers between devices, exchanged(): lax.ppermute(block, axis, [(member, member ^ mask) for member in range(co...  9.7 us
    pallas_call x1, Pallas kernels, own_rows(): pl.pallas_call(functools.partial(own_kernel, count, replica_count), out_s...  5.27 us
    pallas_call x1, Pallas kernels, last_rows(): pl.pallas_call(last_kernel, out_shape=[pltpu.VMEM((tokens, 3 * HD), jnp.b...  2.58 us
    pallas_call x1, Pallas kernels, middle_rows(): pl.pallas_call(functools.partial(middle_kernel, origins), out_shape=[pltp...  2.09 us
    pallas_call x1, Pallas kernels, fed_rows(): pl.pallas_call(fed_kernel, out_shape=pltpu.VMEM((rows, width), jnp.float3...  0.85 us
    pallas_call x1, Pallas kernels, finished(): pl.pallas_call(functools.partial(finish_kernel, masks), out_shape=[jax.Sh...  0.83 us
  transfers between devices with their start and end apart: 17, of which 7 were waited for; matrix products, arithmetic and copies ran while one was open for 0% of the time, Pallas kernels for 26%

profile of v8, /device:TPU:0, one launch (start us, length us, event | category | flops | bytes accessed | tf_op | source)
XLA Modules:
  0.0 39.4 jit_solution(8158194347728981382)
XLA Ops:
  0.6 3.1 %collective-permute-start.1 = (bf16[32,2048]{1,0:T(8,128)(2,1)}, bf16[32,2048]{1,0:T(8,128)(2,1)S(1)}, u32[]{:S(2)}, u32[]{:S(2)}) collective-permute-start(bf16[32,2048]{1,0:T(8,128)(2,1)} %refs_2_.1), channel_id=1, source_target_pairs={{0,2},{1,3},{2,0},{3,1},{4,6},{5,7},{6,4},{7,5},{8,10},{9,11},{10,... | collective-permute-start | bytes 393224 | tf_op jit(solution)/shard_map/ppermute | solution.py:235
  3.7 2.6 %collective-permute-start = (bf16[32,2048]{1,0:T(8,128)(2,1)}, bf16[32,2048]{1,0:T(8,128)(2,1)S(1)}, u32[]{:S(2)}, u32[]{:S(2)}) collective-permute-start(bf16[32,2048]{1,0:T(8,128)(2,1)} %refs_2_.1), channel_id=1, source_target_pairs={{0,4},{1,5},{2,6},{3,7},{4,0},{5,1},{6,2},{7,3},{8,12},{9,13},{10,... | collective-permute-start | bytes 393224 | tf_op jit(solution)/shard_map/ppermute | solution.py:235
  6.3 0.0 collective-permute-start.3
  6.3 5.3 %own_rows.1 = (s32[1,256]{1,0:T(1,128)}, s32[1,16]{1,0:T(1,128)}, bf16[32,2048]{1,0:T(8,128)(2,1)S(1)}, f32[1,2048]{1,0:T(1,128)S(1)}, f32[1,2048]{1,0:T(1,128)S...) custom-call(s32[1,256]{1,0:T(1,128)} %refs_0_.1, ...), custom_call_target="tpu_custom_call" | custom-call | flops 234881024 | bytes 11682880 | tf_op jit(solution)/shard_map/own_rows/pallas_call | solution.py:452
  11.6 0.6 %collective-permute-start.2 = (bf16[32,2048]{1,0:T(8,128)(2,1)S(1)}, bf16[32,2048]{1,0:T(8,128)(2,1)S(1)}, u32[]{:S(2)}, u32[]{:S(2)}) collective-permute-start(bf16[32,2048]{1,0:T(8,128)(2,1)S(1)} %collective-permute-done.1.refs_1_), channel_id=1, source_target_pairs={{0,1},{1,0},{2,3},{3,2},{4,5},{5,4},{6,7},{7,6},{8,9},{9,8},{10,11... | collective-permute-start | bytes 393224 | tf_op jit(solution)/shard_map/ppermute | solution.py:235
  12.2 0.5 %collective-permute-done.refs_3_ = bf16[32,2048]{1,0:T(8,128)(2,1)S(1)} collective-permute-done((bf16[32,2048]{1,0:T(8,128)(2,1)}, bf16[32,2048]{1,0:T(8,128)(2,1)S(1)}, u32[]{:S(2)}, u32[]{:S(2)}) %collective-permute-start) | collective-permute-done | bytes 131104 | tf_op jit(solution)/shard_map/ppermute | solution.py:235
  12.7 0.0 collective-permute-done.3.refs_0_
  12.7 0.5 %collective-permute-done.2.refs_2_ = bf16[32,2048]{1,0:T(8,128)(2,1)S(1)} collective-permute-done((bf16[32,2048]{1,0:T(8,128)(2,1)S(1)}, bf16[32,2048]{1,0:T(8,128)(2,1)S(1)}, u32[]{:S(2)}, u32[]{:S(2)}) %collective-permute-start.2) | collective-permute-done | bytes 131104 | tf_op jit(solution)/shard_map/ppermute | solution.py:235
  13.2 0.5 %collective-permute-start.4 = (bf16[32,2048]{1,0:T(8,128)(2,1)S(1)}, bf16[32,2048]{1,0:T(8,128)(2,1)S(1)}, u32[]{:S(2)}, u32[]{:S(2)}) collective-permute-start(bf16[32,2048]{1,0:T(8,128)(2,1)S(1)} %collective-permute-done.refs_3_), channel_id=1, source_target_pairs={{0,2},{1,3},{2,0},{3,1},{4,6},{5,7},{6,4},{7,5},{8,10},{9,11},{10,... | collective-permute-start | bytes 393224 | tf_op jit(solution)/shard_map/ppermute | solution.py:235
  13.6 2.1 %middle_rows.1 = (bf16[128,768]{1,0:T(8,128)(2,1)S(1)}, bf16[128,1024]{1,0:T(8,128)(2,1)S(1)}, bf16[256,2048]{1,0:T(8,128)(2,1)S(1)}) custom-call(bf16[32,2048]{1,0:T(8,128)(2,1)S(1)} %collective-permute-done.3.refs_0_, bf16[32,2048]{1,0:T(8,128)(2,1)S(1)} %collective-permute-done.1.refs_1_, bf16[32,2048]{1,0:T(8,128)(2,1)S(1)} %collective-permute-done.2.refs_2_, ...), custom_call_target="tpu_custom_call" | custom-call | flops 939524096 | bytes 1048576 | tf_op jit(solution)/shard_map/middle_rows/pallas_call | solution.py:492
  15.7 0.1 collective-permute-start.5
  15.9 3.1 %collective-permute-done.4.refs_1_ = bf16[32,2048]{1,0:T(8,128)(2,1)S(1)} collective-permute-done((bf16[32,2048]{1,0:T(8,128)(2,1)S(1)}, bf16[32,2048]{1,0:T(8,128)(2,1)S(1)}, u32[]{:S(2)}, u32[]{:S(2)}) %collective-permute-start.4) | collective-permute-done | bytes 131104 | tf_op jit(solution)/shard_map/ppermute | solution.py:235
  18.9 0.0 collective-permute-done.5.refs_0_
  18.9 0.8 %fed_rows.1.fed_ref = f32[160,2048]{1,0:T(8,128)S(1)} custom-call(bf16[32,1024]{1,0:T(8,128)(2,1)S(1)} %get-tuple-element.74.own_hidden_ref, bf16[128,1024]{1,0:T(8,128)(2,1)S(1)} %get-tuple-element.75.middle_hidden_ref, bf16[1024,2048]{1,0:T(8,128)(2,1)S(1)} %get-tuple-element.76.downward_ref.refs_7_), custom_call_target="tpu_custom_call" | custom-call | flops 671088640 | bytes 1048576 | tf_op jit(solution)/shard_map/fed_rows/pallas_call | solution.py:590
  19.8 0.5 %collective-permute-done.6.refs_2_ = bf16[32,2048]{1,0:T(8,128)(2,1)S(1)} collective-permute-done((bf16[32,2048]{1,0:T(8,128)(2,1)S(1)}, bf16[32,2048]{1,0:T(8,128)(2,1)S(1)}, u32[]{:S(2)}, u32[]{:S(2)}) %collective-permute-start.6) | collective-permute-done | bytes 131104 | tf_op jit(solution)/shard_map/ppermute | solution.py:235
  20.3 2.6 %last_rows.1 = (bf16[256,768]{1,0:T(8,128)(2,1)S(1)}, f32[32,2048]{1,0:T(8,128)S(1)}, bf16[32,2048]{1,0:T(8,128)(2,1)S(1)}, f32[32,2048]{1,0:T(8,128)S(1)}) custom-call(bf16[32,2048]{1,0:T(8,128)(2,1)S(1)} %collective-permute-done.5.refs_0_, bf16[32,2048]{1,0:T(8,128)(2,1)S(1)} %collective-permute-done.4.refs_1_, ...), custom_call_target="tpu_custom_call" | custom-call | flops 1207959552 | bytes 1048576 | tf_op jit(solution)/shard_map/last_rows/pallas_call | solution.py:552
  22.9 0.2 collective-permute-start.7
  23.1 0.8 %rest_rows.1 = (bf16[32,2048]{1,0:T(8,128)(2,1)S(1)}, bf16[32,2048]{1,0:T(8,128)(2,1)S(1)}, bf16[32,2048]{1,0:T(8,128)(2,1)S(1)}, f32[32,2048]{1,0:T(8,128)S(1)}...) custom-call(bf16[256,768]{1,0:T(8,128)(2,1)S(1)} %get-tuple-element.99.joined_ref, ...), custom_call_target="tpu_custom_call" | custom-call | flops 201326592 | bytes 1048576 | tf_op jit(solution)/shard_map/rest_rows/pallas_call | solution.py:629
  23.9 0.4 %collective-permute-done.7.refs_1_ = bf16[32,2048]{1,0:T(8,128)(2,1)S(1)} collective-permute-done((bf16[32,2048]{1,0:T(8,128)(2,1)S(1)}, bf16[32,2048]{1,0:T(8,128)(2,1)S(1)}, u32[]{:S(2)}, u32[]{:S(2)}) %collective-permute-start.7) | collective-permute-done | bytes 131104 | tf_op jit(solution)/shard_map/ppermute | solution.py:235
  24.3 0.5 %collective-permute-start.8 = (bf16[32,2048]{1,0:T(8,128)(2,1)S(1)}, bf16[32,2048]{1,0:T(8,128)(2,1)S(1)}, u32[]{:S(2)}, u32[]{:S(2)}) collective-permute-start(bf16[32,2048]{1,0:T(8,128)(2,1)S(1)} %third_added.1), channel_id=1, source_target_pairs={{0,2},{1,3},{2,0},{3,1},{4,6},{5,7},{6,4},{7,5},{8,10},{9,11},{10,... | collective-permute-start | bytes 393224 | tf_op jit(solution)/shard_map/ppermute | solution.py:235
  24.8 0.5 %collective-permute-start.10 = (bf16[32,2048]{1,0:T(8,128)(2,1)S(1)}, bf16[32,2048]{1,0:T(8,128)(2,1)S(1)}, u32[]{:S(2)}, u32[]{:S(2)}) collective-permute-start(bf16[32,2048]{1,0:T(8,128)(2,1)S(1)} %get-tuple-element.93), channel_id=1, source_target_pairs={{0,1},{1,0},{2,3},{3,2},{4,5},{5,4},{6,7},{7,6},{8,9},{9,8},{10,11... | collective-permute-start | bytes 393224 | tf_op jit(solution)/shard_map/ppermute | solution.py:235
  25.3 0.3 cached_pages.1
  25.6 2.5 %collective-permute-start.16 = (bf16[8,16,512]{2,1,0:T(8,128)(2,1)S(1)}, bf16[8,16,512]{2,1,0:T(8,128)(2,1)S(1)}, u32[]{:S(2)}, u32[]{:S(2)}) collective-permute-start(bf16[8,16,512]{2,1,0:T(8,128)(2,1)S(1)} %get-tuple-element.109), channel_id=1, source_target_pairs={{0,24},{8,16},{16,8},{24,0},{1,25},{9,17},{17,9},{25,1},{2,26},{10... | collective-permute-start | bytes 393224 | tf_op jit(solution)/shard_map/ppermute | solution.py:235
  28.2 1.8 %collective-permute-done.8.passing_ref = bf16[32,2048]{1,0:T(8,128)(2,1)S(1)} collective-permute-done((bf16[32,2048]{1,0:T(8,128)(2,1)S(1)}, bf16[32,2048]{1,0:T(8,128)(2,1)S(1)}, u32[]{:S(2)}, u32[]{:S(2)}) %collective-permute-start.8) | collective-permute-done | bytes 131104 | tf_op jit(solution)/shard_map/ppermute | solution.py:235
  29.9 0.1 remaining_sums.1
  30.0 0.4 %collective-permute-start.12 = (bf16[32,2048]{1,0:T(8,128)(2,1)S(1)}, bf16[32,2048]{1,0:T(8,128)(2,1)S(1)}, u32[]{:S(2)}, u32[]{:S(2)}) collective-permute-start(bf16[32,2048]{1,0:T(8,128)(2,1)S(1)} %get-tuple-element.104), channel_id=1, source_target_pairs={{0,4},{1,5},{2,6},{3,7},{4,0},{5,1},{6,2},{7,3},{8,12},{9,13},{10,... | collective-permute-start | bytes 393224 | tf_op jit(solution)/shard_map/ppermute | solution.py:235
  30.4 1.4 %collective-permute-start.13 = (bf16[32,2048]{1,0:T(8,128)(2,1)S(1)}, bf16[32,2048]{1,0:T(8,128)(2,1)S(1)}, u32[]{:S(2)}, u32[]{:S(2)}) collective-permute-start(bf16[32,2048]{1,0:T(8,128)(2,1)S(1)} %get-tuple-element.105), channel_id=1, source_target_pairs={{0,2},{1,3},{2,0},{3,1},{4,6},{5,7},{6,4},{7,5},{8,10},{9,11},{10,... | collective-permute-start | bytes 393224 | tf_op jit(solution)/shard_map/ppermute | solution.py:235
  31.8 1.5 %collective-permute-start.14 = (bf16[8,16,512]{2,1,0:T(8,128)(2,1)S(1)}, bf16[8,16,512]{2,1,0:T(8,128)(2,1)S(1)}, u32[]{:S(2)}, u32[]{:S(2)}) collective-permute-start(bf16[8,16,512]{2,1,0:T(8,128)(2,1)S(1)} %get-tuple-element.106), channel_id=1, source_target_pairs={{0,8},{8,0},{16,24},{24,16},{1,9},{9,1},{17,25},{25,17},{2,10},{10... | collective-permute-start | bytes 393224 | tf_op jit(solution)/shard_map/ppermute | solution.py:235
  33.3 1.5 %collective-permute-start.15 = (bf16[8,16,512]{2,1,0:T(8,128)(2,1)S(1)}, bf16[8,16,512]{2,1,0:T(8,128)(2,1)S(1)}, u32[]{:S(2)}, u32[]{:S(2)}) collective-permute-start(bf16[8,16,512]{2,1,0:T(8,128)(2,1)S(1)} %get-tuple-element.107), channel_id=1, source_target_pairs={{0,16},{8,24},{16,0},{24,8},{1,17},{9,25},{17,1},{25,9},{2,18},{10... | collective-permute-start | bytes 393224 | tf_op jit(solution)/shard_map/ppermute | solution.py:235
  34.8 0.7 %placed.1.refs_4_ = bf16[1,4,8,16,512]{4,3,2,1,0:T(8,128)(2,1)} custom-call(bf16[8,16,512]{2,1,0:T(8,128)(2,1)S(1)} %get-tuple-element.108.refs_0_, bf16[8,16,512]{2,1,0:T(8,128)(2,1)S(1)} %collective-permute-done.16.refs_1_), custom_call_target="tpu_custom_call" | custom-call | tf_op jit(solution)/shard_map/placed/pallas_call | solution.py:733
  35.6 3.0 %collective-permute-done.12.refs_0_ = bf16[32,2048]{1,0:T(8,128)(2,1)S(1)} collective-permute-done((bf16[32,2048]{1,0:T(8,128)(2,1)S(1)}, bf16[32,2048]{1,0:T(8,128)(2,1)S(1)}, u32[]{:S(2)}, u32[]{:S(2)}) %collective-permute-start.12) | collective-permute-done | bytes 131104 | tf_op jit(solution)/shard_map/ppermute | solution.py:235
  38.6 0.8 %finished.1 = (f32[32,2048]{1,0:T(8,128)}, bf16[1,4,8,16,512]{4,3,2,1,0:T(8,128)(2,1)}) custom-call(f32[32,2048]{1,0:T(8,128)S(1)} %get-tuple-element.103.base_ref, bf16[32,2048]{1,0:T(8,128)(2,1)S(1)} %collective-permute-done.12.refs_0_, bf16[32,2048]{1,0:T(8,128)(2,1)S(1)} %collective-permute-done.13.refs_1_, ...), custom_call_target="tpu_custom_call", output_to_operand_aliasing={{1}: (5, {})} | custom-call | tf_op jit(solution)/shard_map/finished/pallas_call | solution.py:767
  (12 shorter events, 0.1 us)
Async XLA Ops:
  0.6 11.0 %collective-permute-start.1 = (bf16[32,2048]{1,0:T(8,128)(2,1)}, bf16[32,2048]{1,0:T(8,128)(2,1)S(1)}, u32[]{:S(2)}, u32[]{:S(2)}) collective-permute-start(bf16[32,2048]{1,0:T(8,128)(2,1)} %refs_2_.1), channel_id=1, source_target_pairs={{0,2},{1,3},{2,0},{3,1},{4,6},{5,7},{6,4},{7,5},{8,10},{9,11},{10,... | collective-permute-start | bytes 393224 | tf_op jit(solution)/shard_map/ppermute | solution.py:235
  3.7 8.9 %collective-permute-start = (bf16[32,2048]{1,0:T(8,128)(2,1)}, bf16[32,2048]{1,0:T(8,128)(2,1)S(1)}, u32[]{:S(2)}, u32[]{:S(2)}) collective-permute-start(bf16[32,2048]{1,0:T(8,128)(2,1)} %refs_2_.1), channel_id=1, source_target_pairs={{0,4},{1,5},{2,6},{3,7},{4,0},{5,1},{6,2},{7,3},{8,12},{9,13},{10,... | collective-permute-start | bytes 393224 | tf_op jit(solution)/shard_map/ppermute | solution.py:235
  6.3 6.4 %collective-permute-start.3 = (bf16[32,2048]{1,0:T(8,128)(2,1)}, bf16[32,2048]{1,0:T(8,128)(2,1)S(1)}, u32[]{:S(2)}, u32[]{:S(2)}) collective-permute-start(bf16[32,2048]{1,0:T(8,128)(2,1)} %refs_2_.1), channel_id=1, source_target_pairs={{0,1},{1,0},{2,3},{3,2},{4,5},{5,4},{6,7},{7,6},{8,9},{9,8},{10,11... | collective-permute-start | bytes 393224 | tf_op jit(solution)/shard_map/ppermute | solution.py:235
  11.6 1.6 %collective-permute-start.2 = (bf16[32,2048]{1,0:T(8,128)(2,1)S(1)}, bf16[32,2048]{1,0:T(8,128)(2,1)S(1)}, u32[]{:S(2)}, u32[]{:S(2)}) collective-permute-start(bf16[32,2048]{1,0:T(8,128)(2,1)S(1)} %collective-permute-done.1.refs_1_), channel_id=1, source_target_pairs={{0,1},{1,0},{2,3},{3,2},{4,5},{5,4},{6,7},{7,6},{8,9},{9,8},{10,11... | collective-permute-start | bytes 393224 | tf_op jit(solution)/shard_map/ppermute | solution.py:235
  13.2 5.8 %collective-permute-start.4 = (bf16[32,2048]{1,0:T(8,128)(2,1)S(1)}, bf16[32,2048]{1,0:T(8,128)(2,1)S(1)}, u32[]{:S(2)}, u32[]{:S(2)}) collective-permute-start(bf16[32,2048]{1,0:T(8,128)(2,1)S(1)} %collective-permute-done.refs_3_), channel_id=1, source_target_pairs={{0,2},{1,3},{2,0},{3,1},{4,6},{5,7},{6,4},{7,5},{8,10},{9,11},{10,... | collective-permute-start | bytes 393224 | tf_op jit(solution)/shard_map/ppermute | solution.py:235
  15.7 3.2 %collective-permute-start.5 = (bf16[32,2048]{1,0:T(8,128)(2,1)S(1)}, bf16[32,2048]{1,0:T(8,128)(2,1)S(1)}, u32[]{:S(2)}, u32[]{:S(2)}) collective-permute-start(bf16[32,2048]{1,0:T(8,128)(2,1)S(1)} %collective-permute-done.refs_3_), channel_id=1, source_target_pairs={{0,1},{1,0},{2,3},{3,2},{4,5},{5,4},{6,7},{7,6},{8,9},{9,8},{10,11... | collective-permute-start | bytes 393224 | tf_op jit(solution)/shard_map/ppermute | solution.py:235
  18.9 1.3 %collective-permute-start.6 = (bf16[32,2048]{1,0:T(8,128)(2,1)S(1)}, bf16[32,2048]{1,0:T(8,128)(2,1)S(1)}, u32[]{:S(2)}, u32[]{:S(2)}) collective-permute-start(bf16[32,2048]{1,0:T(8,128)(2,1)S(1)} %collective-permute-done.4.refs_1_), channel_id=1, source_target_pairs={{0,1},{1,0},{2,3},{3,2},{4,5},{5,4},{6,7},{7,6},{8,9},{9,8},{10,11... | collective-permute-start | bytes 393224 | tf_op jit(solution)/shard_map/ppermute | solution.py:235
  22.9 1.4 %collective-permute-start.7 = (bf16[32,2048]{1,0:T(8,128)(2,1)S(1)}, bf16[32,2048]{1,0:T(8,128)(2,1)S(1)}, u32[]{:S(2)}, u32[]{:S(2)}) collective-permute-start(bf16[32,2048]{1,0:T(8,128)(2,1)S(1)} %get-tuple-element.83), channel_id=1, source_target_pairs={{0,1},{1,0},{2,3},{3,2},{4,5},{5,4},{6,7},{7,6},{8,9},{9,8},{10,11... | collective-permute-start | bytes 393224 | tf_op jit(solution)/shard_map/ppermute | solution.py:235
  24.3 5.6 %collective-permute-start.8 = (bf16[32,2048]{1,0:T(8,128)(2,1)S(1)}, bf16[32,2048]{1,0:T(8,128)(2,1)S(1)}, u32[]{:S(2)}, u32[]{:S(2)}) collective-permute-start(bf16[32,2048]{1,0:T(8,128)(2,1)S(1)} %third_added.1), channel_id=1, source_target_pairs={{0,2},{1,3},{2,0},{3,1},{4,6},{5,7},{6,4},{7,5},{8,10},{9,11},{10,... | collective-permute-start | bytes 393224 | tf_op jit(solution)/shard_map/ppermute | solution.py:235
  24.8 5.1 %collective-permute-start.9 = (bf16[32,2048]{1,0:T(8,128)(2,1)S(1)}, bf16[32,2048]{1,0:T(8,128)(2,1)S(1)}, u32[]{:S(2)}, u32[]{:S(2)}) collective-permute-start(bf16[32,2048]{1,0:T(8,128)(2,1)S(1)} %get-tuple-element.91), channel_id=1, source_target_pairs={{0,1},{1,0},{2,3},{3,2},{4,5},{5,4},{6,7},{7,6},{8,9},{9,8},{10,11... | collective-permute-start | bytes 393224 | tf_op jit(solution)/shard_map/ppermute | solution.py:235
  24.8 5.1 %collective-permute-start.10 = (bf16[32,2048]{1,0:T(8,128)(2,1)S(1)}, bf16[32,2048]{1,0:T(8,128)(2,1)S(1)}, u32[]{:S(2)}, u32[]{:S(2)}) collective-permute-start(bf16[32,2048]{1,0:T(8,128)(2,1)S(1)} %get-tuple-element.93), channel_id=1, source_target_pairs={{0,1},{1,0},{2,3},{3,2},{4,5},{5,4},{6,7},{7,6},{8,9},{9,8},{10,11... | collective-permute-start | bytes 393224 | tf_op jit(solution)/shard_map/ppermute | solution.py:235
  25.3 4.6 %collective-permute-start.11 = (bf16[32,2048]{1,0:T(8,128)(2,1)S(1)}, bf16[32,2048]{1,0:T(8,128)(2,1)S(1)}, u32[]{:S(2)}, u32[]{:S(2)}) collective-permute-start(bf16[32,2048]{1,0:T(8,128)(2,1)S(1)} %get-tuple-element.95), channel_id=1, source_target_pairs={{0,1},{1,0},{2,3},{3,2},{4,5},{5,4},{6,7},{7,6},{8,9},{9,8},{10,11... | collective-permute-start | bytes 393224 | tf_op jit(solution)/shard_map/ppermute | solution.py:235
  25.6 9.2 %collective-permute-start.16 = (bf16[8,16,512]{2,1,0:T(8,128)(2,1)S(1)}, bf16[8,16,512]{2,1,0:T(8,128)(2,1)S(1)}, u32[]{:S(2)}, u32[]{:S(2)}) collective-permute-start(bf16[8,16,512]{2,1,0:T(8,128)(2,1)S(1)} %get-tuple-element.109), channel_id=1, source_target_pairs={{0,24},{8,16},{16,8},{24,0},{1,25},{9,17},{17,9},{25,1},{2,26},{10... | collective-permute-start | bytes 393224 | tf_op jit(solution)/shard_map/ppermute | solution.py:235
  30.0 8.5 %collective-permute-start.12 = (bf16[32,2048]{1,0:T(8,128)(2,1)S(1)}, bf16[32,2048]{1,0:T(8,128)(2,1)S(1)}, u32[]{:S(2)}, u32[]{:S(2)}) collective-permute-start(bf16[32,2048]{1,0:T(8,128)(2,1)S(1)} %get-tuple-element.104), channel_id=1, source_target_pairs={{0,4},{1,5},{2,6},{3,7},{4,0},{5,1},{6,2},{7,3},{8,12},{9,13},{10,... | collective-permute-start | bytes 393224 | tf_op jit(solution)/shard_map/ppermute | solution.py:235
  30.4 8.1 %collective-permute-start.13 = (bf16[32,2048]{1,0:T(8,128)(2,1)S(1)}, bf16[32,2048]{1,0:T(8,128)(2,1)S(1)}, u32[]{:S(2)}, u32[]{:S(2)}) collective-permute-start(bf16[32,2048]{1,0:T(8,128)(2,1)S(1)} %get-tuple-element.105), channel_id=1, source_target_pairs={{0,2},{1,3},{2,0},{3,1},{4,6},{5,7},{6,4},{7,5},{8,10},{9,11},{10,... | collective-permute-start | bytes 393224 | tf_op jit(solution)/shard_map/ppermute | solution.py:235
  31.8 6.7 %collective-permute-start.14 = (bf16[8,16,512]{2,1,0:T(8,128)(2,1)S(1)}, bf16[8,16,512]{2,1,0:T(8,128)(2,1)S(1)}, u32[]{:S(2)}, u32[]{:S(2)}) collective-permute-start(bf16[8,16,512]{2,1,0:T(8,128)(2,1)S(1)} %get-tuple-element.106), channel_id=1, source_target_pairs={{0,8},{8,0},{16,24},{24,16},{1,9},{9,1},{17,25},{25,17},{2,10},{10... | collective-permute-start | bytes 393224 | tf_op jit(solution)/shard_map/ppermute | solution.py:235
  33.3 5.2 %collective-permute-start.15 = (bf16[8,16,512]{2,1,0:T(8,128)(2,1)S(1)}, bf16[8,16,512]{2,1,0:T(8,128)(2,1)S(1)}, u32[]{:S(2)}, u32[]{:S(2)}) collective-permute-start(bf16[8,16,512]{2,1,0:T(8,128)(2,1)S(1)} %get-tuple-element.107), channel_id=1, source_target_pairs={{0,16},{8,24},{16,0},{24,8},{1,17},{9,25},{17,1},{25,9},{2,18},{10... | collective-permute-start | bytes 393224 | tf_op jit(solution)/shard_map/ppermute | solution.py:235

commit v9 on v8

--- a/solution.py
+++ b/solution.py
@@ -233,6 +233,12 @@
 def exchanged(block, axis, mask):
     count = lax.axis_size(axis)
     return lax.ppermute(block, axis, [(member, member ^ mask) for member in range(count)])
+
+
+def exchanged_by(core, block, axis, mask):
+    count = lax.axis_size(axis)
+    members = [member for member in range(count) if member % CORES == core]
+    return lax.ppermute(block, axis, [(member, member ^ mask) for member in members])
 
 
 def vmem_specs(count):
@@ -417,10 +423,10 @@
 
 def own_kernel(count, replica_count, *refs):
     sources, targets = refs[:count], refs[count : 2 * count]
-    offsets_ref, *table_refs, destinations_ref, joined_ref, hidden_ref = refs[2 * count : -3]
-    attention_scr, feedforward_scr, sems = refs[-3:]
+    offsets_ref, *table_refs, destinations_ref, joined_ref, feedforward_ref = refs[2 * count : -2]
+    attention_scr, sems = refs[-2:]
     copies = copies_in(sources, targets, sems)
-    segments_ref, targets_ref, states_ref, *gain_refs, heads_ref, upward_ref, _ = targets
+    segments_ref, targets_ref, states_ref, *gain_refs, heads_ref = targets
     block_rows = states_ref.shape[0]
     wait_for(copies[0])
     make_tables(segments_ref, offsets_ref, *table_refs)
@@ -428,25 +434,21 @@
     make_destinations(targets_ref, destinations_ref, replica_count, block_rows)
     for number in (2, 3, 4):
         wait_for(copies[number])
-    normalize([states_ref], gain_refs, [attention_scr, feedforward_scr])
+    normalize([states_ref], gain_refs, [attention_scr, feedforward_ref])
     wait_for(copies[5])
     places = [position_of(0, 0, block_rows)]
     project(attention_scr, heads_ref, table_refs, places, joined_ref, 0)
-    wait_for(copies[6])
-    hide(feedforward_scr, upward_ref, hidden_ref, 0)
-    wait_for(copies[7])
 
 
 def own_rows(staged, replica_count):
     tokens = staged[0].shape[1]
     rows, width = staged[2].shape
-    hidden_width = staged[6].shape[1]
     shapes = [pltpu.VMEM(array.shape, array.dtype) for array in staged]
     shapes += [pltpu.VMEM((tokens, 128), jnp.float32)] * 4
     shapes += [
         pltpu.VMEM((1, tokens), jnp.int32),
         pltpu.VMEM((rows, 3 * HD), jnp.bfloat16),
-        pltpu.VMEM((rows, hidden_width), jnp.bfloat16),
+        pltpu.VMEM((rows, width), jnp.bfloat16),
     ]
     count = len(staged)
     return pl.pallas_call(
@@ -456,28 +458,55 @@
         out_specs=vmem_specs(len(shapes)),
         scratch_shapes=[
             pltpu.VMEM((rows, width), jnp.bfloat16),
-            pltpu.VMEM((rows, width), jnp.bfloat16),
             pltpu.SemaphoreType.DMA((count, 4)),
         ],
         compiler_params=parameters(12),
         cost_estimate=pl.CostEstimate(
-            flops=2 * rows * width * (3 * HD + hidden_width),
+            flops=2 * rows * width * 3 * HD,
             bytes_accessed=sum(array.nbytes for array in staged),
-            transcendentals=rows * hidden_width,
+            transcendentals=0,
         ),
         name="own_rows",
     )(*[in_hbm(array) for array in staged])
 
 
+def units_kernel(feedforward_ref, *refs):
+    sources, targets, hidden_ref, sems = refs[:2], refs[2:4], refs[4], refs[5]
+    copies = copies_in(sources, targets, sems)
+    wait_for(copies[0])
+    hide(feedforward_ref, targets[0], hidden_ref, 0)
+    wait_for(copies[1])
+
+
+def own_units(normed, upward_weight, downward_weight):
+    rows = normed.shape[0]
+    staged = (upward_weight, downward_weight)
+    hidden_width = upward_weight.shape[1]
+    return pl.pallas_call(
+        units_kernel,
+        out_shape=[pltpu.VMEM(array.shape, array.dtype) for array in staged]
+        + [pltpu.VMEM((rows, hidden_width), jnp.bfloat16)],
+        in_specs=vmem_specs(1) + [pl.BlockSpec(memory_space=pltpu.HBM)] * 2,
+        out_specs=vmem_specs(3),
+        scratch_shapes=[pltpu.SemaphoreType.DMA((2, 4))],
+        compiler_params=parameters(12),
+        cost_estimate=pl.CostEstimate(
+            flops=0, bytes_accessed=MIB, transcendentals=rows * hidden_width
+        ),
+        name="own_units",
+    )(normed, *[in_hbm(array) for array in staged])
+
+
 def middle_kernel(origins, *refs):
     count = len(origins)
-    blocks, (gain_a, gain_f, heads_ref, upward_ref) = refs[:count], refs[count : count + 4]
-    table_refs, refs = refs[count + 4 : count + 7], refs[count + 7 :]
-    staged = (len(refs) - 5) // 2
-    sources, (joined_ref, hidden_ref), refs = refs[:staged], refs[staged:][:2], refs[staged + 2 :]
-    targets, (attention_scr, feedforward_scr, sems) = refs[:staged], refs[staged:]
-    copies = copies_in(sources, targets, sems)
+    blocks, refs = refs[: count + 1], refs[count + 1 :]
+    gain_a, gain_f, heads_ref, upward_ref, *table_refs, source_ref = refs[:8]
+    joined_ref, hidden_ref, second_ref, target_ref = refs[8:12]
+    attention_scr, feedforward_scr, sems = refs[12:]
+    copies = copies_in([source_ref], [target_ref], sems)
     block_rows = blocks[0].shape[0]
+    second_ref[...] = blocks[-2][...] + blocks[-1][...]
+    blocks = (*blocks[:-2], second_ref)
     normalize(blocks, [gain_a, gain_f], [attention_scr, feedforward_scr])
     places = [position_of(kind, half, block_rows) for kind, half in origins]
     project(attention_scr, heads_ref, table_refs, places, joined_ref, 0)
@@ -485,24 +514,24 @@
     wait_for(sum(copies, []))
 
 
-def middle_rows(name, origins, blocks, gains, weights, tables, *staged):
+def middle_rows(origins, blocks, gains, weights, tables, staged):
     block_rows, width = blocks[0].shape
-    rows = len(blocks) * block_rows
+    rows = len(origins) * block_rows
     hidden_width = weights[1].shape[1]
     return pl.pallas_call(
         functools.partial(middle_kernel, origins),
         out_shape=[
             pltpu.VMEM((rows, 3 * HD), jnp.bfloat16),
             pltpu.VMEM((rows, hidden_width), jnp.bfloat16),
-        ]
-        + [pltpu.VMEM(array.shape, array.dtype) for array in staged],
-        in_specs=vmem_specs(len(blocks) + 2 + 2 + 3)
-        + [pl.BlockSpec(memory_space=pltpu.HBM)] * len(staged),
-        out_specs=vmem_specs(2 + len(staged)),
+            pltpu.VMEM((block_rows, width), jnp.bfloat16),
+            pltpu.VMEM(staged.shape, staged.dtype),
+        ],
+        in_specs=vmem_specs(len(blocks) + 2 + 2 + 3) + [pl.BlockSpec(memory_space=pltpu.HBM)],
+        out_specs=vmem_specs(4),
         scratch_shapes=[
             pltpu.VMEM((rows, width), jnp.bfloat16),
             pltpu.VMEM((rows, width), jnp.bfloat16),
-            pltpu.SemaphoreType.DMA((max(len(staged), 1), 4)),
+            pltpu.SemaphoreType.DMA((1, 4)),
         ],
         compiler_params=parameters(12),
         cost_estimate=pl.CostEstimate(
@@ -510,8 +539,8 @@
             bytes_accessed=MIB,
             transcendentals=rows * hidden_width,
         ),
-        name=name,
-    )(*blocks, *gains, *weights, *tables, *[in_hbm(array) for array in staged])
+        name="middle_rows",
+    )(*blocks, *gains, *weights, *tables, in_hbm(staged))
 
 
 def last_kernel(*refs):
@@ -797,7 +826,7 @@
 ):
     replica_count = lax.axis_size("dp")
     to_chip = [mask * CORES for mask in range(CHIPS)]
-    second = exchanged(hidden_states, "tensor", to_chip[2])
+    second_even = exchanged_by(0, hidden_states, "tensor", to_chip[2])
     first = exchanged(hidden_states, "tensor", to_chip[1])
     beside = exchanged(hidden_states, "tensor", 1)
     staged = (
@@ -807,32 +836,34 @@
         attention_gain[None],
         feedforward_gain[None],
         heads_weight,
-        upward_weight,
-        downward_weight,
     )
     staged = own_rows(staged, replica_count)
-    hidden, gains, weights, tables = staged[2], staged[3:5], staged[5:8], staged[8:12]
-    heads, upward, downward = weights
-    destinations, own_joined, own_hidden = staged[12:]
-
-    first, own_joined = lax.optimization_barrier((first, own_joined))
+    hidden, gains, heads, tables = staged[2], staged[3:5], staged[5], staged[6:10]
+    destinations, own_joined, own_feedforward = staged[10:]
+    second_odd = exchanged_by(1, hidden, "tensor", to_chip[2])
+    upward, downward, own_hidden = own_units(own_feedforward, upward_weight, downward_weight)
+
+    first, second_even, own_hidden = lax.optimization_barrier((first, second_even, own_hidden))
+    third_even = exchanged_by(0, second_even, "tensor", to_chip[1])
     first_beside = exchanged(first, "tensor", 1)
-    second, first_beside, beside = lax.optimization_barrier((second, first_beside, beside))
-    third = exchanged(second, "tensor", to_chip[1])
-    middle_joined, middle_hidden, output = middle_rows(
-        "middle_rows",
+    second_odd, first_beside, beside = lax.optimization_barrier(
+        (second_odd, first_beside, beside)
+    )
+    third_odd = exchanged_by(1, second_odd, "tensor", to_chip[1])
+    middle_joined, middle_hidden, second, output = middle_rows(
         ((0, 1), (1, 0), (1, 1), (2, 0)),
-        (beside, first, first_beside, second),
+        (beside, first, first_beside, second_even, second_odd),
         gains,
         (heads, upward),
         tables[1:],
         output_weight,
     )
-    second, middle_joined = lax.optimization_barrier((second, middle_joined))
     second_beside = exchanged(second, "tensor", 1)
-    third, second_beside, middle_joined, middle_hidden = lax.optimization_barrier(
-        (third, second_beside, middle_joined, middle_hidden)
-    )
+    third_even, third_odd, middle_joined, middle_hidden = lax.optimization_barrier(
+        (third_even, third_odd, middle_joined, middle_hidden)
+    )
+    third = added("third_block", third_even, third_odd)
+    third, second_beside = lax.optimization_barrier((third, second_beside))
     third_beside = exchanged(third, "tensor", 1)
     fed = fed_rows(own_hidden, middle_hidden, downward)
     third_beside, fed = lax.optimization_barrier((third_beside, fed))

time: 39.5 us -> 47 us (1.19)
  starting transfers between devices: 15.4 us -> 26.3 us
  waiting for transfers between devices: 9.7 us -> 4.98 us
  Pallas kernels: 13.6 us -> 14.8 us
    ppermute x0 -> x4, starting transfers between devices: none -> 9.58 us  [exchanged_by(): lax.ppermute(block, axis, [(member, member ^ mask) for member in members])]
    ppermute x17 -> x15, waiting for transfers between devices: 9.7 us -> 4.59 us  [exchanged(): lax.ppermute(block, axis, [(member, member ^ mask) for member in range(co...]
    pallas_call x0 -> x1, Pallas kernels: none -> 3.48 us  [own_units(): pl.pallas_call(units_kernel, out_shape=[pltpu.VMEM(array.shape, array.dty...]
    pallas_call x1, Pallas kernels: 5.27 us -> 2.91 us  [own_rows(): pl.pallas_call(functools.partial(own_kernel, count, replica_count), out_s...]
    ppermute x17 -> x15, starting transfers between devices: 15.4 us -> 16.7 us  [exchanged(): lax.ppermute(block, axis, [(member, member ^ mask) for member in range(co...]
  transfers between devices with their start and end apart: 17 -> 19, of which waited for: 7 -> 8; matrix products, arithmetic and copies ran while one was open for 0% -> 0% of each run, Pallas kernels for 26% -> 24%
where the time goes in v9:
time: 47 us; the launch traced here: 46.8 us
  starting transfers between devices  26.3 us (56%)
  Pallas kernels  14.8 us (31%)
  waiting for transfers between devices  4.98 us (11%)
  between operations  0.78 us (2%)
    ppermute x15, starting transfers between devices, exchanged(): lax.ppermute(block, axis, [(member, member ^ mask) for member in range(co...  16.7 us
    ppermute x4, starting transfers between devices, exchanged_by(): lax.ppermute(block, axis, [(member, member ^ mask) for member in members])  9.58 us
    ppermute x15, waiting for transfers between devices, exchanged(): lax.ppermute(block, axis, [(member, member ^ mask) for member in range(co...  4.59 us
    pallas_call x1, Pallas kernels, own_units(): pl.pallas_call(units_kernel, out_shape=[pltpu.VMEM(array.shape, array.dty...  3.48 us
    pallas_call x1, Pallas kernels, own_rows(): pl.pallas_call(functools.partial(own_kernel, count, replica_count), out_s...  2.91 us
    pallas_call x1, Pallas kernels, last_rows(): pl.pallas_call(last_kernel, out_shape=[pltpu.VMEM((tokens, 3 * HD), jnp.b...  2.58 us
    pallas_call x1, Pallas kernels, middle_rows(): pl.pallas_call(functools.partial(middle_kernel, origins), out_shape=[pltp...  2.12 us
  transfers between devices with their start and end apart: 19, of which 8 were waited for; matrix products, arithmetic and copies ran while one was open for 0% of the time, Pallas kernels for 24%

profile of v9, /device:TPU:0, one launch (start us, length us, event | category | flops | bytes accessed | tf_op | source)
XLA Modules:
  0.0 46.8 jit_solution(15515888713891611221)
XLA Ops:
  0.6 5.9 %collective-permute-start.1 = (bf16[32,2048]{1,0:T(8,128)(2,1)}, bf16[32,2048]{1,0:T(8,128)(2,1)S(1)}, u32[]{:S(2)}, u32[]{:S(2)}) collective-permute-start(bf16[32,2048]{1,0:T(8,128)(2,1)} %refs_2_.1), channel_id=1, source_target_pairs={{0,4},{2,6},{4,0},{6,2},{8,12},{10,14},{12,8},{14,10},{16,20},{18,... | collective-permute-start | bytes 393224 | tf_op jit(solution)/shard_map/ppermute | solution.py:241
  6.6 1.6 %collective-permute-start = (bf16[32,2048]{1,0:T(8,128)(2,1)}, bf16[32,2048]{1,0:T(8,128)(2,1)S(1)}, u32[]{:S(2)}, u32[]{:S(2)}) collective-permute-start(bf16[32,2048]{1,0:T(8,128)(2,1)} %refs_2_.1), channel_id=1, source_target_pairs={{0,2},{1,3},{2,0},{3,1},{4,6},{5,7},{6,4},{7,5},{8,10},{9,11},{10,... | collective-permute-start | bytes 393224 | tf_op jit(solution)/shard_map/ppermute | solution.py:235
  8.2 2.9 %own_rows.1 = (s32[1,256]{1,0:T(1,128)}, s32[1,16]{1,0:T(1,128)}, bf16[32,2048]{1,0:T(8,128)(2,1)S(1)}, f32[1,2048]{1,0:T(1,128)S(1)}, f32[1,2048]{1,0:T(1,128)S...) custom-call(s32[1,256]{1,0:T(1,128)} %refs_0_.2, ...), custom_call_target="tpu_custom_call" | custom-call | flops 100663296 | bytes 3294272 | tf_op jit(solution)/shard_map/own_rows/pallas_call | solution.py:454
  11.1 0.7 %collective-permute-start.3 = (bf16[32,2048]{1,0:T(8,128)(2,1)S(1)}, bf16[32,2048]{1,0:T(8,128)(2,1)S(1)}, u32[]{:S(2)}, u32[]{:S(2)}) collective-permute-start(bf16[32,2048]{1,0:T(8,128)(2,1)S(1)} %get-tuple-element.62.refs_6_), channel_id=1, source_target_pairs={{1,5},{3,7},{5,1},{7,3},{9,13},{11,15},{13,9},{15,11},{17,21},{19,... | collective-permute-start | bytes 393224 | tf_op jit(solution)/shard_map/ppermute | solution.py:241
  11.8 3.5 %own_units.1 = (bf16[2048,1024]{1,0:T(8,128)(2,1)S(1)}, bf16[1024,2048]{1,0:T(8,128)(2,1)S(1)}, bf16[32,1024]{1,0:T(8,128)(2,1)S(1)}) custom-call(bf16[32,2048]{1,0:T(8,128)(2,1)S(1)} %get-tuple-element.59.feedforward_ref, bf16[2048,1024]{1,0:T(8,128)(2,1)} %refs_0_.3, bf16[1024,2048]{1,0:T(8,128)(2,1)} %refs_1_.1), custom_call_target="tpu_custom_call" | custom-call | bytes 1048576 | tf_op jit(solution)/shard_map/own_units/pallas_call | solution.py:485
  15.3 1.9 %collective-permute-start.4 = (bf16[32,2048]{1,0:T(8,128)(2,1)S(1)}, bf16[32,2048]{1,0:T(8,128)(2,1)S(1)}, u32[]{:S(2)}, u32[]{:S(2)}) collective-permute-start(bf16[32,2048]{1,0:T(8,128)(2,1)S(1)} %collective-permute-done.refs_1_), channel_id=1, source_target_pairs={{0,1},{1,0},{2,3},{3,2},{4,5},{5,4},{6,7},{7,6},{8,9},{9,8},{10,11... | collective-permute-start | bytes 393224 | tf_op jit(solution)/shard_map/ppermute | solution.py:235
  17.2 2.3 %collective-permute-start.2 = (bf16[32,2048]{1,0:T(8,128)(2,1)S(1)}, bf16[32,2048]{1,0:T(8,128)(2,1)S(1)}, u32[]{:S(2)}, u32[]{:S(2)}) collective-permute-start(bf16[32,2048]{1,0:T(8,128)(2,1)S(1)} %collective-permute-done.1.refs_3_), channel_id=1, source_target_pairs={{0,2},{2,0},{4,6},{6,4},{8,10},{10,8},{12,14},{14,12},{16,18},{18,... | collective-permute-start | bytes 393224 | tf_op jit(solution)/shard_map/ppermute | solution.py:241
  19.5 0.7 %collective-permute-start.6 = (bf16[32,2048]{1,0:T(8,128)(2,1)S(1)}, bf16[32,2048]{1,0:T(8,128)(2,1)S(1)}, u32[]{:S(2)}, u32[]{:S(2)}) collective-permute-start(bf16[32,2048]{1,0:T(8,128)(2,1)S(1)} %collective-permute-done.3.refs_4_), channel_id=1, source_target_pairs={{1,3},{3,1},{5,7},{7,5},{9,11},{11,9},{13,15},{15,13},{17,19},{19,... | collective-permute-start | bytes 393224 | tf_op jit(solution)/shard_map/ppermute | solution.py:241
  20.2 2.1 %middle_rows.1 = (bf16[128,768]{1,0:T(8,128)(2,1)S(1)}, bf16[128,1024]{1,0:T(8,128)(2,1)S(1)}, bf16[32,2048]{1,0:T(8,128)(2,1)S(1)}, bf16[256,2048]{1,0:T(8,128)(2,1)S(1)}) custom-call(bf16[32,2048]{1,0:T(8,128)(2,1)S(1)} %collective-permute-done.5.refs_0_, bf16[32,2048]{1,0:T(8,128)(2,1)S(1)} %collective-permute-done.refs_1_, ...), custom_call_target="tpu_custom_call" | custom-call | flops 939524096 | bytes 1048576 | tf_op jit(solution)/shard_map/middle_rows/pallas_call | solution.py:521
  22.4 1.3 %collective-permute-start.7 = (bf16[32,2048]{1,0:T(8,128)(2,1)S(1)}, bf16[32,2048]{1,0:T(8,128)(2,1)S(1)}, u32[]{:S(2)}, u32[]{:S(2)}) collective-permute-start(bf16[32,2048]{1,0:T(8,128)(2,1)S(1)} %get-tuple-element.78), channel_id=1, source_target_pairs={{0,1},{1,0},{2,3},{3,2},{4,5},{5,4},{6,7},{7,6},{8,9},{9,8},{10,11... | collective-permute-start | bytes 393224 | tf_op jit(solution)/shard_map/ppermute | solution.py:235
  23.7 0.4 collective-permute-done.2.refs_0_
  24.1 0.6 %collective-permute-done.7.refs_0_ = bf16[32,2048]{1,0:T(8,128)(2,1)S(1)} collective-permute-done((bf16[32,2048]{1,0:T(8,128)(2,1)S(1)}, bf16[32,2048]{1,0:T(8,128)(2,1)S(1)}, u32[]{:S(2)}, u32[]{:S(2)}) %collective-permute-start.7) | collective-permute-done | bytes 131104 | tf_op jit(solution)/shard_map/ppermute | solution.py:235
  24.7 0.7 %collective-permute-start.8 = (bf16[32,2048]{1,0:T(8,128)(2,1)S(1)}, bf16[32,2048]{1,0:T(8,128)(2,1)S(1)}, u32[]{:S(2)}, u32[]{:S(2)}) collective-permute-start(bf16[32,2048]{1,0:T(8,128)(2,1)S(1)} %third_block.1.refs_1_), channel_id=1, source_target_pairs={{0,1},{1,0},{2,3},{3,2},{4,5},{5,4},{6,7},{7,6},{8,9},{9,8},{10,11... | collective-permute-start | bytes 393224 | tf_op jit(solution)/shard_map/ppermute | solution.py:235
  25.4 0.8 %fed_rows.1.fed_ref = f32[160,2048]{1,0:T(8,128)S(1)} custom-call(bf16[32,1024]{1,0:T(8,128)(2,1)S(1)} %get-tuple-element.81.own_hidden_ref, bf16[128,1024]{1,0:T(8,128)(2,1)S(1)} %get-tuple-element.82.middle_hidden_ref, bf16[1024,2048]{1,0:T(8,128)(2,1)S(1)} %get-tuple-element.83.downward_ref.refs_7_), custom_call_target="tpu_custom_call" | custom-call | flops 671088640 | bytes 1048576 | tf_op jit(solution)/shard_map/fed_rows/pallas_call | solution.py:619
  26.4 2.6 %last_rows.1 = (bf16[256,768]{1,0:T(8,128)(2,1)S(1)}, f32[32,2048]{1,0:T(8,128)S(1)}, bf16[32,2048]{1,0:T(8,128)(2,1)S(1)}, f32[32,2048]{1,0:T(8,128)S(1)}) custom-call(bf16[32,2048]{1,0:T(8,128)(2,1)S(1)} %collective-permute-done.7.refs_0_, bf16[32,2048]{1,0:T(8,128)(2,1)S(1)} %third_block.1.refs_1_, bf16[32,2048]{1,0:T(8,128)(2,1)S(1)} %collective-permute-done.8.refs_2_, ...), custom_call_target="tpu_custom_call" | custom-call | flops 1207959552 | bytes 1048576 | tf_op jit(solution)/shard_map/last_rows/pallas_call | solution.py:581
  29.0 0.4 collective-permute-start.9
  29.4 0.8 %rest_rows.1 = (bf16[32,2048]{1,0:T(8,128)(2,1)S(1)}, bf16[32,2048]{1,0:T(8,128)(2,1)S(1)}, bf16[32,2048]{1,0:T(8,128)(2,1)S(1)}, f32[32,2048]{1,0:T(8,128)S(1)}...) custom-call(bf16[256,768]{1,0:T(8,128)(2,1)S(1)} %get-tuple-element.105.joined_ref, ...), custom_call_target="tpu_custom_call" | custom-call | flops 201326592 | bytes 1048576 | tf_op jit(solution)/shard_map/rest_rows/pallas_call | solution.py:658
  30.2 0.2 collective-permute-done.9.refs_1_
  30.4 1.5 %collective-permute-start.10 = (bf16[32,2048]{1,0:T(8,128)(2,1)S(1)}, bf16[32,2048]{1,0:T(8,128)(2,1)S(1)}, u32[]{:S(2)}, u32[]{:S(2)}) collective-permute-start(bf16[32,2048]{1,0:T(8,128)(2,1)S(1)} %third_added.1), channel_id=1, source_target_pairs={{0,2},{1,3},{2,0},{3,1},{4,6},{5,7},{6,4},{7,5},{8,10},{9,11},{10,... | collective-permute-start | bytes 393224 | tf_op jit(solution)/shard_map/ppermute | solution.py:235
  31.9 0.4 collective-permute-start.12
  32.4 0.3 cached_pages.1
  32.7 2.5 %collective-permute-start.18 = (bf16[8,16,512]{2,1,0:T(8,128)(2,1)S(1)}, bf16[8,16,512]{2,1,0:T(8,128)(2,1)S(1)}, u32[]{:S(2)}, u32[]{:S(2)}) collective-permute-start(bf16[8,16,512]{2,1,0:T(8,128)(2,1)S(1)} %get-tuple-element.115), channel_id=1, source_target_pairs={{0,24},{8,16},{16,8},{24,0},{1,25},{9,17},{17,9},{25,1},{2,26},{10... | collective-permute-start | bytes 393224 | tf_op jit(solution)/shard_map/ppermute | solution.py:235
  35.2 1.0 %collective-permute-done.10.passing_ref = bf16[32,2048]{1,0:T(8,128)(2,1)S(1)} collective-permute-done((bf16[32,2048]{1,0:T(8,128)(2,1)S(1)}, bf16[32,2048]{1,0:T(8,128)(2,1)S(1)}, u32[]{:S(2)}, u32[]{:S(2)}) %collective-permute-start.10) | collective-permute-done | bytes 131104 | tf_op jit(solution)/shard_map/ppermute | solution.py:235
  36.4 2.7 %collective-permute-start.14 = (bf16[32,2048]{1,0:T(8,128)(2,1)S(1)}, bf16[32,2048]{1,0:T(8,128)(2,1)S(1)}, u32[]{:S(2)}, u32[]{:S(2)}) collective-permute-start(bf16[32,2048]{1,0:T(8,128)(2,1)S(1)} %get-tuple-element.110), channel_id=1, source_target_pairs={{0,4},{1,5},{2,6},{3,7},{4,0},{5,1},{6,2},{7,3},{8,12},{9,13},{10,... | collective-permute-start | bytes 393224 | tf_op jit(solution)/shard_map/ppermute | solution.py:235
  39.0 0.4 collective-permute-start.15
  39.5 1.5 %collective-permute-start.16 = (bf16[8,16,512]{2,1,0:T(8,128)(2,1)S(1)}, bf16[8,16,512]{2,1,0:T(8,128)(2,1)S(1)}, u32[]{:S(2)}, u32[]{:S(2)}) collective-permute-start(bf16[8,16,512]{2,1,0:T(8,128)(2,1)S(1)} %get-tuple-element.112), channel_id=1, source_target_pairs={{0,8},{8,0},{16,24},{24,16},{1,9},{9,1},{17,25},{25,17},{2,10},{10... | collective-permute-start | bytes 393224 | tf_op jit(solution)/shard_map/ppermute | solution.py:235
  41.0 1.5 %collective-permute-start.17 = (bf16[8,16,512]{2,1,0:T(8,128)(2,1)S(1)}, bf16[8,16,512]{2,1,0:T(8,128)(2,1)S(1)}, u32[]{:S(2)}, u32[]{:S(2)}) collective-permute-start(bf16[8,16,512]{2,1,0:T(8,128)(2,1)S(1)} %get-tuple-element.113), channel_id=1, source_target_pairs={{0,16},{8,24},{16,0},{24,8},{1,17},{9,25},{17,1},{25,9},{2,18},{10... | collective-permute-start | bytes 393224 | tf_op jit(solution)/shard_map/ppermute | solution.py:235
  42.5 0.7 %placed.1.refs_4_ = bf16[1,4,8,16,512]{4,3,2,1,0:T(8,128)(2,1)} custom-call(bf16[8,16,512]{2,1,0:T(8,128)(2,1)S(1)} %get-tuple-element.114.refs_0_, bf16[8,16,512]{2,1,0:T(8,128)(2,1)S(1)} %collective-permute-done.18.refs_1_), custom_call_target="tpu_custom_call" | custom-call | tf_op jit(solution)/shard_map/placed/pallas_call | solution.py:762
  43.2 1.9 %collective-permute-done.14.refs_0_ = bf16[32,2048]{1,0:T(8,128)(2,1)S(1)} collective-permute-done((bf16[32,2048]{1,0:T(8,128)(2,1)S(1)}, bf16[32,2048]{1,0:T(8,128)(2,1)S(1)}, u32[]{:S(2)}, u32[]{:S(2)}) %collective-permute-start.14) | collective-permute-done | bytes 131104 | tf_op jit(solution)/shard_map/ppermute | solution.py:235
  45.2 0.3 collective-permute-done.15.refs_1_
  45.5 0.4 collective-permute-done.17.refs_3_
  46.0 0.8 %finished.1 = (f32[32,2048]{1,0:T(8,128)}, bf16[1,4,8,16,512]{4,3,2,1,0:T(8,128)(2,1)}) custom-call(f32[32,2048]{1,0:T(8,128)S(1)} %get-tuple-element.109.base_ref, bf16[32,2048]{1,0:T(8,128)(2,1)S(1)} %collective-permute-done.14.refs_0_, bf16[32,2048]{1,0:T(8,128)(2,1)S(1)} %collective-permute-done.15.refs_1_, ...), custom_call_target="tpu_custom_call", output_to_operand_aliasing={{1}: (5, {})} | custom-call | tf_op jit(solution)/shard_map/finished/pallas_call | solution.py:796
  (18 shorter events, 0.5 us)
Async XLA Ops:
  0.6 14.7 %collective-permute-start.1 = (bf16[32,2048]{1,0:T(8,128)(2,1)}, bf16[32,2048]{1,0:T(8,128)(2,1)S(1)}, u32[]{:S(2)}, u32[]{:S(2)}) collective-permute-start(bf16[32,2048]{1,0:T(8,128)(2,1)} %refs_2_.1), channel_id=1, source_target_pairs={{0,4},{2,6},{4,0},{6,2},{8,12},{10,14},{12,8},{14,10},{16,20},{18,... | collective-permute-start | bytes 393224 | tf_op jit(solution)/shard_map/ppermute | solution.py:241
  6.6 8.7 %collective-permute-start = (bf16[32,2048]{1,0:T(8,128)(2,1)}, bf16[32,2048]{1,0:T(8,128)(2,1)S(1)}, u32[]{:S(2)}, u32[]{:S(2)}) collective-permute-start(bf16[32,2048]{1,0:T(8,128)(2,1)} %refs_2_.1), channel_id=1, source_target_pairs={{0,2},{1,3},{2,0},{3,1},{4,6},{5,7},{6,4},{7,5},{8,10},{9,11},{10,... | collective-permute-start | bytes 393224 | tf_op jit(solution)/shard_map/ppermute | solution.py:235
  8.2 11.3 %collective-permute-start.5 = (bf16[32,2048]{1,0:T(8,128)(2,1)}, bf16[32,2048]{1,0:T(8,128)(2,1)S(1)}, u32[]{:S(2)}, u32[]{:S(2)}) collective-permute-start(bf16[32,2048]{1,0:T(8,128)(2,1)} %refs_2_.1), channel_id=1, source_target_pairs={{0,1},{1,0},{2,3},{3,2},{4,5},{5,4},{6,7},{7,6},{8,9},{9,8},{10,11... | collective-permute-start | bytes 393224 | tf_op jit(solution)/shard_map/ppermute | solution.py:235
  11.1 8.4 %collective-permute-start.3 = (bf16[32,2048]{1,0:T(8,128)(2,1)S(1)}, bf16[32,2048]{1,0:T(8,128)(2,1)S(1)}, u32[]{:S(2)}, u32[]{:S(2)}) collective-permute-start(bf16[32,2048]{1,0:T(8,128)(2,1)S(1)} %get-tuple-element.62.refs_6_), channel_id=1, source_target_pairs={{1,5},{3,7},{5,1},{7,3},{9,13},{11,15},{13,9},{15,11},{17,21},{19,... | collective-permute-start | bytes 393224 | tf_op jit(solution)/shard_map/ppermute | solution.py:241
  15.3 4.2 %collective-permute-start.4 = (bf16[32,2048]{1,0:T(8,128)(2,1)S(1)}, bf16[32,2048]{1,0:T(8,128)(2,1)S(1)}, u32[]{:S(2)}, u32[]{:S(2)}) collective-permute-start(bf16[32,2048]{1,0:T(8,128)(2,1)S(1)} %collective-permute-done.refs_1_), channel_id=1, source_target_pairs={{0,1},{1,0},{2,3},{3,2},{4,5},{5,4},{6,7},{7,6},{8,9},{9,8},{10,11... | collective-permute-start | bytes 393224 | tf_op jit(solution)/shard_map/ppermute | solution.py:235
  17.2 6.8 %collective-permute-start.2 = (bf16[32,2048]{1,0:T(8,128)(2,1)S(1)}, bf16[32,2048]{1,0:T(8,128)(2,1)S(1)}, u32[]{:S(2)}, u32[]{:S(2)}) collective-permute-start(bf16[32,2048]{1,0:T(8,128)(2,1)S(1)} %collective-permute-done.1.refs_3_), channel_id=1, source_target_pairs={{0,2},{2,0},{4,6},{6,4},{8,10},{10,8},{12,14},{14,12},{16,18},{18,... | collective-permute-start | bytes 393224 | tf_op jit(solution)/shard_map/ppermute | solution.py:241
  19.5 4.5 %collective-permute-start.6 = (bf16[32,2048]{1,0:T(8,128)(2,1)S(1)}, bf16[32,2048]{1,0:T(8,128)(2,1)S(1)}, u32[]{:S(2)}, u32[]{:S(2)}) collective-permute-start(bf16[32,2048]{1,0:T(8,128)(2,1)S(1)} %collective-permute-done.3.refs_4_), channel_id=1, source_target_pairs={{1,3},{3,1},{5,7},{7,5},{9,11},{11,9},{13,15},{15,13},{17,19},{19,... | collective-permute-start | bytes 393224 | tf_op jit(solution)/shard_map/ppermute | solution.py:241
  22.4 2.3 %collective-permute-start.7 = (bf16[32,2048]{1,0:T(8,128)(2,1)S(1)}, bf16[32,2048]{1,0:T(8,128)(2,1)S(1)}, u32[]{:S(2)}, u32[]{:S(2)}) collective-permute-start(bf16[32,2048]{1,0:T(8,128)(2,1)S(1)} %get-tuple-element.78), channel_id=1, source_target_pairs={{0,1},{1,0},{2,3},{3,2},{4,5},{5,4},{6,7},{7,6},{8,9},{9,8},{10,11... | collective-permute-start | bytes 393224 | tf_op jit(solution)/shard_map/ppermute | solution.py:235
  24.7 1.7 %collective-permute-start.8 = (bf16[32,2048]{1,0:T(8,128)(2,1)S(1)}, bf16[32,2048]{1,0:T(8,128)(2,1)S(1)}, u32[]{:S(2)}, u32[]{:S(2)}) collective-permute-start(bf16[32,2048]{1,0:T(8,128)(2,1)S(1)} %third_block.1.refs_1_), channel_id=1, source_target_pairs={{0,1},{1,0},{2,3},{3,2},{4,5},{5,4},{6,7},{7,6},{8,9},{9,8},{10,11... | collective-permute-start | bytes 393224 | tf_op jit(solution)/shard_map/ppermute | solution.py:235
  29.0 1.4 %collective-permute-start.9 = (bf16[32,2048]{1,0:T(8,128)(2,1)S(1)}, bf16[32,2048]{1,0:T(8,128)(2,1)S(1)}, u32[]{:S(2)}, u32[]{:S(2)}) collective-permute-start(bf16[32,2048]{1,0:T(8,128)(2,1)S(1)} %get-tuple-element.90), channel_id=1, source_target_pairs={{0,1},{1,0},{2,3},{3,2},{4,5},{5,4},{6,7},{7,6},{8,9},{9,8},{10,11... | collective-permute-start | bytes 393224 | tf_op jit(solution)/shard_map/ppermute | solution.py:235
  30.4 5.8 %collective-permute-start.10 = (bf16[32,2048]{1,0:T(8,128)(2,1)S(1)}, bf16[32,2048]{1,0:T(8,128)(2,1)S(1)}, u32[]{:S(2)}, u32[]{:S(2)}) collective-permute-start(bf16[32,2048]{1,0:T(8,128)(2,1)S(1)} %third_added.1), channel_id=1, source_target_pairs={{0,2},{1,3},{2,0},{3,1},{4,6},{5,7},{6,4},{7,5},{8,10},{9,11},{10,... | collective-permute-start | bytes 393224 | tf_op jit(solution)/shard_map/ppermute | solution.py:235
  31.8 4.4 %collective-permute-start.11 = (bf16[32,2048]{1,0:T(8,128)(2,1)S(1)}, bf16[32,2048]{1,0:T(8,128)(2,1)S(1)}, u32[]{:S(2)}, u32[]{:S(2)}) collective-permute-start(bf16[32,2048]{1,0:T(8,128)(2,1)S(1)} %get-tuple-element.98), channel_id=1, source_target_pairs={{0,1},{1,0},{2,3},{3,2},{4,5},{5,4},{6,7},{7,6},{8,9},{9,8},{10,11... | collective-permute-start | bytes 393224 | tf_op jit(solution)/shard_map/ppermute | solution.py:235
  31.9 4.3 %collective-permute-start.12 = (bf16[32,2048]{1,0:T(8,128)(2,1)S(1)}, bf16[32,2048]{1,0:T(8,128)(2,1)S(1)}, u32[]{:S(2)}, u32[]{:S(2)}) collective-permute-start(bf16[32,2048]{1,0:T(8,128)(2,1)S(1)} %get-tuple-element.100), channel_id=1, source_target_pairs={{0,1},{1,0},{2,3},{3,2},{4,5},{5,4},{6,7},{7,6},{8,9},{9,8},{10,11... | collective-permute-start | bytes 393224 | tf_op jit(solution)/shard_map/ppermute | solution.py:235
  32.4 3.9 %collective-permute-start.13 = (bf16[32,2048]{1,0:T(8,128)(2,1)S(1)}, bf16[32,2048]{1,0:T(8,128)(2,1)S(1)}, u32[]{:S(2)}, u32[]{:S(2)}) collective-permute-start(bf16[32,2048]{1,0:T(8,128)(2,1)S(1)} %get-tuple-element.102), channel_id=1, source_target_pairs={{0,1},{1,0},{2,3},{3,2},{4,5},{5,4},{6,7},{7,6},{8,9},{9,8},{10,11... | collective-permute-start | bytes 393224 | tf_op jit(solution)/shard_map/ppermute | solution.py:235
  32.7 9.8 %collective-permute-start.18 = (bf16[8,16,512]{2,1,0:T(8,128)(2,1)S(1)}, bf16[8,16,512]{2,1,0:T(8,128)(2,1)S(1)}, u32[]{:S(2)}, u32[]{:S(2)}) collective-permute-start(bf16[8,16,512]{2,1,0:T(8,128)(2,1)S(1)} %get-tuple-element.115), channel_id=1, source_target_pairs={{0,24},{8,16},{16,8},{24,0},{1,25},{9,17},{17,9},{25,1},{2,26},{10... | collective-permute-start | bytes 393224 | tf_op jit(solution)/shard_map/ppermute | solution.py:235
  36.4 8.8 %collective-permute-start.14 = (bf16[32,2048]{1,0:T(8,128)(2,1)S(1)}, bf16[32,2048]{1,0:T(8,128)(2,1)S(1)}, u32[]{:S(2)}, u32[]{:S(2)}) collective-permute-start(bf16[32,2048]{1,0:T(8,128)(2,1)S(1)} %get-tuple-element.110), channel_id=1, source_target_pairs={{0,4},{1,5},{2,6},{3,7},{4,0},{5,1},{6,2},{7,3},{8,12},{9,13},{10,... | collective-permute-start | bytes 393224 | tf_op jit(solution)/shard_map/ppermute | solution.py:235
  39.0 6.5 %collective-permute-start.15 = (bf16[32,2048]{1,0:T(8,128)(2,1)S(1)}, bf16[32,2048]{1,0:T(8,128)(2,1)S(1)}, u32[]{:S(2)}, u32[]{:S(2)}) collective-permute-start(bf16[32,2048]{1,0:T(8,128)(2,1)S(1)} %get-tuple-element.111), channel_id=1, source_target_pairs={{0,2},{1,3},{2,0},{3,1},{4,6},{5,7},{6,4},{7,5},{8,10},{9,11},{10,... | collective-permute-start | bytes 393224 | tf_op jit(solution)/shard_map/ppermute | solution.py:235
  39.5 6.0 %collective-permute-start.16 = (bf16[8,16,512]{2,1,0:T(8,128)(2,1)S(1)}, bf16[8,16,512]{2,1,0:T(8,128)(2,1)S(1)}, u32[]{:S(2)}, u32[]{:S(2)}) collective-permute-start(bf16[8,16,512]{2,1,0:T(8,128)(2,1)S(1)} %get-tuple-element.112), channel_id=1, source_target_pairs={{0,8},{8,0},{16,24},{24,16},{1,9},{9,1},{17,25},{25,17},{2,10},{10... | collective-permute-start | bytes 393224 | tf_op jit(solution)/shard_map/ppermute | solution.py:235
  41.0 5.0 %collective-permute-start.17 = (bf16[8,16,512]{2,1,0:T(8,128)(2,1)S(1)}, bf16[8,16,512]{2,1,0:T(8,128)(2,1)S(1)}, u32[]{:S(2)}, u32[]{:S(2)}) collective-permute-start(bf16[8,16,512]{2,1,0:T(8,128)(2,1)S(1)} %get-tuple-element.113), channel_id=1, source_target_pairs={{0,16},{8,24},{16,0},{24,8},{1,17},{9,25},{17,1},{25,9},{2,18},{10... | collective-permute-start | bytes 393224 | tf_op jit(solution)/shard_map/ppermute | solution.py:235

commit v10 on v8

--- a/solution.py
+++ b/solution.py
@@ -420,7 +420,7 @@
     offsets_ref, *table_refs, destinations_ref, joined_ref, hidden_ref = refs[2 * count : -3]
     attention_scr, feedforward_scr, sems = refs[-3:]
     copies = copies_in(sources, targets, sems)
-    segments_ref, targets_ref, states_ref, *gain_refs, heads_ref, upward_ref, _ = targets
+    segments_ref, targets_ref, states_ref, *gain_refs, heads_ref, upward_ref = targets
     block_rows = states_ref.shape[0]
     wait_for(copies[0])
     make_tables(segments_ref, offsets_ref, *table_refs)
@@ -434,7 +434,6 @@
     project(attention_scr, heads_ref, table_refs, places, joined_ref, 0)
     wait_for(copies[6])
     hide(feedforward_scr, upward_ref, hidden_ref, 0)
-    wait_for(copies[7])
 
 
 def own_rows(staged, replica_count):
@@ -808,24 +807,22 @@
         feedforward_gain[None],
         heads_weight,
         upward_weight,
-        downward_weight,
     )
     staged = own_rows(staged, replica_count)
-    hidden, gains, weights, tables = staged[2], staged[3:5], staged[5:8], staged[8:12]
-    heads, upward, downward = weights
-    destinations, own_joined, own_hidden = staged[12:]
-
-    first, own_joined = lax.optimization_barrier((first, own_joined))
+    hidden, gains, (heads, upward), tables = staged[2], staged[3:5], staged[5:7], staged[7:11]
+    destinations, own_joined, own_hidden = staged[11:]
+
+    first, second, own_joined = lax.optimization_barrier((first, second, own_joined))
     first_beside = exchanged(first, "tensor", 1)
-    second, first_beside, beside = lax.optimization_barrier((second, first_beside, beside))
     third = exchanged(second, "tensor", to_chip[1])
-    middle_joined, middle_hidden, output = middle_rows(
+    middle_joined, middle_hidden, downward, output = middle_rows(
         "middle_rows",
         ((0, 1), (1, 0), (1, 1), (2, 0)),
         (beside, first, first_beside, second),
         gains,
         (heads, upward),
         tables[1:],
+        downward_weight,
         output_weight,
     )
     second, middle_joined = lax.optimization_barrier((second, middle_joined))

time: 39.5 us -> 40.1 us (1.015)
  starting transfers between devices: 15.4 us -> 19 us
  waiting for transfers between devices: 9.7 us -> 6.31 us
    ppermute x17, starting transfers between devices: 15.4 us -> 19 us  [exchanged(): lax.ppermute(block, axis, [(member, member ^ mask) for member in range(co...]
    ppermute x17, waiting for transfers between devices: 9.7 us -> 6.31 us  [exchanged(): lax.ppermute(block, axis, [(member, member ^ mask) for member in range(co...]
    pallas_call x1, Pallas kernels: 2.09 us -> 3.41 us  [middle_rows(): pl.pallas_call(functools.partial(middle_kernel, origins), out_shape=[pltp...]
    pallas_call x1, Pallas kernels: 5.27 us -> 4.33 us  [own_rows(): pl.pallas_call(functools.partial(own_kernel, count, replica_count), out_s...]
  transfers between devices with their start and end apart: 17 -> 17, of which waited for: 7 -> 10; matrix products, arithmetic and copies ran while one was open for 0% -> 0% of each run, Pallas kernels for 26% -> 26%
where the time goes in v10:
time: 40.1 us; the launch traced here: 40 us
  starting transfers between devices  19 us (47%)
  Pallas kernels  13.9 us (35%)
  waiting for transfers between devices  6.31 us (16%)
  between operations  0.7 us (2%)
    ppermute x17, starting transfers between devices, exchanged(): lax.ppermute(block, axis, [(member, member ^ mask) for member in range(co...  19 us
    ppermute x17, waiting for transfers between devices, exchanged(): lax.ppermute(block, axis, [(member, member ^ mask) for member in range(co...  6.31 us
    pallas_call x1, Pallas kernels, own_rows(): pl.pallas_call(functools.partial(own_kernel, count, replica_count), out_s...  4.33 us
    pallas_call x1, Pallas kernels, middle_rows(): pl.pallas_call(functools.partial(middle_kernel, origins), out_shape=[pltp...  3.41 us
    pallas_call x1, Pallas kernels, last_rows(): pl.pallas_call(last_kernel, out_shape=[pltpu.VMEM((tokens, 3 * HD), jnp.b...  2.58 us
    pallas_call x1, Pallas kernels, fed_rows(): pl.pallas_call(fed_kernel, out_shape=pltpu.VMEM((rows, width), jnp.float3...  0.84 us
    pallas_call x1, Pallas kernels, finished(): pl.pallas_call(functools.partial(finish_kernel, masks), out_shape=[jax.Sh...  0.82 us
  transfers between devices with their start and end apart: 17, of which 10 were waited for; matrix products, arithmetic and copies ran while one was open for 0% of the time, Pallas kernels for 26%

profile of v10, /device:TPU:0, one launch (start us, length us, event | category | flops | bytes accessed | tf_op | source)
XLA Modules:
  0.0 40.0 jit_solution(16989838421173693833)
XLA Ops:
  0.6 4.1 %collective-permute-start.1 = (bf16[32,2048]{1,0:T(8,128)(2,1)}, bf16[32,2048]{1,0:T(8,128)(2,1)S(1)}, u32[]{:S(2)}, u32[]{:S(2)}) collective-permute-start(bf16[32,2048]{1,0:T(8,128)(2,1)} %refs_2_.1), channel_id=1, source_target_pairs={{0,4},{1,5},{2,6},{3,7},{4,0},{5,1},{6,2},{7,3},{8,12},{9,13},{10,... | collective-permute-start | bytes 393224 | tf_op jit(solution)/shard_map/ppermute | solution.py:235
  4.7 1.6 %collective-permute-start = (bf16[32,2048]{1,0:T(8,128)(2,1)}, bf16[32,2048]{1,0:T(8,128)(2,1)S(1)}, u32[]{:S(2)}, u32[]{:S(2)}) collective-permute-start(bf16[32,2048]{1,0:T(8,128)(2,1)} %refs_2_.1), channel_id=1, source_target_pairs={{0,2},{1,3},{2,0},{3,1},{4,6},{5,7},{6,4},{7,5},{8,10},{9,11},{10,... | collective-permute-start | bytes 393224 | tf_op jit(solution)/shard_map/ppermute | solution.py:235
  6.3 4.3 %own_rows.1 = (s32[1,256]{1,0:T(1,128)}, s32[1,16]{1,0:T(1,128)}, bf16[32,2048]{1,0:T(8,128)(2,1)S(1)}, f32[1,2048]{1,0:T(1,128)S(1)}, f32[1,2048]{1,0:T(1,128)S...) custom-call(s32[1,256]{1,0:T(1,128)} %refs_0_.1, ...), custom_call_target="tpu_custom_call" | custom-call | flops 234881024 | bytes 7488576 | tf_op jit(solution)/shard_map/own_rows/pallas_call | solution.py:451
  10.6 0.7 %collective-permute-done.1.refs_3_ = bf16[32,2048]{1,0:T(8,128)(2,1)S(1)} collective-permute-done((bf16[32,2048]{1,0:T(8,128)(2,1)}, bf16[32,2048]{1,0:T(8,128)(2,1)S(1)}, u32[]{:S(2)}, u32[]{:S(2)}) %collective-permute-start.1) | collective-permute-done | bytes 131104 | tf_op jit(solution)/shard_map/ppermute | solution.py:235
  11.4 0.2 collective-permute-done.refs_1_
  11.6 1.4 %collective-permute-start.2 = (bf16[32,2048]{1,0:T(8,128)(2,1)S(1)}, bf16[32,2048]{1,0:T(8,128)(2,1)S(1)}, u32[]{:S(2)}, u32[]{:S(2)}) collective-permute-start(bf16[32,2048]{1,0:T(8,128)(2,1)S(1)} %collective-permute-done.1.refs_3_), channel_id=1, source_target_pairs={{0,2},{1,3},{2,0},{3,1},{4,6},{5,7},{6,4},{7,5},{8,10},{9,11},{10,... | collective-permute-start | bytes 393224 | tf_op jit(solution)/shard_map/ppermute | solution.py:235
  13.0 3.4 %middle_rows.1 = (bf16[128,768]{1,0:T(8,128)(2,1)S(1)}, bf16[128,1024]{1,0:T(8,128)(2,1)S(1)}, bf16[1024,2048]{1,0:T(8,128)(2,1)S(1)}, bf16[256,2048]{1,0:T(8,128)(2,1)S(1)}) custom-call(bf16[32,2048]{1,0:T(8,128)(2,1)S(1)} %collective-permute-done.3.refs_0_, bf16[32,2048]{1,0:T(8,128)(2,1)S(1)} %collective-permute-done.refs_1_, ...), custom_call_target="tpu_custom_call" | custom-call | flops 939524096 | bytes 1048576 | tf_op jit(solution)/shard_map/middle_rows/pallas_call | solution.py:491
  16.4 0.3 collective-permute-start.5
  16.7 0.8 %collective-permute-done.2.refs_1_ = bf16[32,2048]{1,0:T(8,128)(2,1)S(1)} collective-permute-done((bf16[32,2048]{1,0:T(8,128)(2,1)S(1)}, bf16[32,2048]{1,0:T(8,128)(2,1)S(1)}, u32[]{:S(2)}, u32[]{:S(2)}) %collective-permute-start.2) | collective-permute-done | bytes 131104 | tf_op jit(solution)/shard_map/ppermute | solution.py:235
  17.5 0.4 collective-permute-done.5.refs_0_
  17.8 0.2 collective-permute-start.6
  18.1 0.8 %fed_rows.1.fed_ref = f32[160,2048]{1,0:T(8,128)S(1)} custom-call(bf16[32,1024]{1,0:T(8,128)(2,1)S(1)} %get-tuple-element.70.own_hidden_ref, bf16[128,1024]{1,0:T(8,128)(2,1)S(1)} %get-tuple-element.71.middle_hidden_ref, bf16[1024,2048]{1,0:T(8,128)(2,1)S(1)} %get-tuple-element.72.downward_ref.refs_7_), custom_call_target="tpu_custom_call" | custom-call | flops 671088640 | bytes 1048576 | tf_op jit(solution)/shard_map/fed_rows/pallas_call | solution.py:589
  18.9 0.3 collective-permute-done.6.refs_2_
  19.2 2.6 %last_rows.1 = (bf16[256,768]{1,0:T(8,128)(2,1)S(1)}, f32[32,2048]{1,0:T(8,128)S(1)}, bf16[32,2048]{1,0:T(8,128)(2,1)S(1)}, f32[32,2048]{1,0:T(8,128)S(1)}) custom-call(bf16[32,2048]{1,0:T(8,128)(2,1)S(1)} %collective-permute-done.5.refs_0_, bf16[32,2048]{1,0:T(8,128)(2,1)S(1)} %collective-permute-done.2.refs_1_, ...), custom_call_target="tpu_custom_call" | custom-call | flops 1207959552 | bytes 1048576 | tf_op jit(solution)/shard_map/last_rows/pallas_call | solution.py:551
  21.8 0.3 collective-permute-start.7
  22.0 0.8 %rest_rows.1 = (bf16[32,2048]{1,0:T(8,128)(2,1)S(1)}, bf16[32,2048]{1,0:T(8,128)(2,1)S(1)}, bf16[32,2048]{1,0:T(8,128)(2,1)S(1)}, f32[32,2048]{1,0:T(8,128)S(1)}...) custom-call(bf16[256,768]{1,0:T(8,128)(2,1)S(1)} %get-tuple-element.95.joined_ref, ...), custom_call_target="tpu_custom_call" | custom-call | flops 201326592 | bytes 1048576 | tf_op jit(solution)/shard_map/rest_rows/pallas_call | solution.py:628
  22.8 0.3 collective-permute-done.7.refs_1_
  23.2 1.4 %collective-permute-start.8 = (bf16[32,2048]{1,0:T(8,128)(2,1)S(1)}, bf16[32,2048]{1,0:T(8,128)(2,1)S(1)}, u32[]{:S(2)}, u32[]{:S(2)}) collective-permute-start(bf16[32,2048]{1,0:T(8,128)(2,1)S(1)} %third_added.1), channel_id=1, source_target_pairs={{0,2},{1,3},{2,0},{3,1},{4,6},{5,7},{6,4},{7,5},{8,10},{9,11},{10,... | collective-permute-start | bytes 393224 | tf_op jit(solution)/shard_map/ppermute | solution.py:235
  24.6 0.5 %collective-permute-start.10 = (bf16[32,2048]{1,0:T(8,128)(2,1)S(1)}, bf16[32,2048]{1,0:T(8,128)(2,1)S(1)}, u32[]{:S(2)}, u32[]{:S(2)}) collective-permute-start(bf16[32,2048]{1,0:T(8,128)(2,1)S(1)} %get-tuple-element.89), channel_id=1, source_target_pairs={{0,1},{1,0},{2,3},{3,2},{4,5},{5,4},{6,7},{7,6},{8,9},{9,8},{10,11... | collective-permute-start | bytes 393224 | tf_op jit(solution)/shard_map/ppermute | solution.py:235
  25.1 0.3 cached_pages.1
  25.4 2.5 %collective-permute-start.16 = (bf16[8,16,512]{2,1,0:T(8,128)(2,1)S(1)}, bf16[8,16,512]{2,1,0:T(8,128)(2,1)S(1)}, u32[]{:S(2)}, u32[]{:S(2)}) collective-permute-start(bf16[8,16,512]{2,1,0:T(8,128)(2,1)S(1)} %get-tuple-element.105), channel_id=1, source_target_pairs={{0,24},{8,16},{16,8},{24,0},{1,25},{9,17},{17,9},{25,1},{2,26},{10... | collective-permute-start | bytes 393224 | tf_op jit(solution)/shard_map/ppermute | solution.py:235
  27.9 0.9 %collective-permute-done.8.passing_ref = bf16[32,2048]{1,0:T(8,128)(2,1)S(1)} collective-permute-done((bf16[32,2048]{1,0:T(8,128)(2,1)S(1)}, bf16[32,2048]{1,0:T(8,128)(2,1)S(1)}, u32[]{:S(2)}, u32[]{:S(2)}) %collective-permute-start.8) | collective-permute-done | bytes 131104 | tf_op jit(solution)/shard_map/ppermute | solution.py:235
  28.9 0.1 remaining_sums.1
  29.0 2.4 %collective-permute-start.12 = (bf16[32,2048]{1,0:T(8,128)(2,1)S(1)}, bf16[32,2048]{1,0:T(8,128)(2,1)S(1)}, u32[]{:S(2)}, u32[]{:S(2)}) collective-permute-start(bf16[32,2048]{1,0:T(8,128)(2,1)S(1)} %get-tuple-element.100), channel_id=1, source_target_pairs={{0,4},{1,5},{2,6},{3,7},{4,0},{5,1},{6,2},{7,3},{8,12},{9,13},{10,... | collective-permute-start | bytes 393224 | tf_op jit(solution)/shard_map/ppermute | solution.py:235
  31.5 1.3 %collective-permute-start.13 = (bf16[32,2048]{1,0:T(8,128)(2,1)S(1)}, bf16[32,2048]{1,0:T(8,128)(2,1)S(1)}, u32[]{:S(2)}, u32[]{:S(2)}) collective-permute-start(bf16[32,2048]{1,0:T(8,128)(2,1)S(1)} %get-tuple-element.101), channel_id=1, source_target_pairs={{0,2},{1,3},{2,0},{3,1},{4,6},{5,7},{6,4},{7,5},{8,10},{9,11},{10,... | collective-permute-start | bytes 393224 | tf_op jit(solution)/shard_map/ppermute | solution.py:235
  32.7 1.5 %collective-permute-start.14 = (bf16[8,16,512]{2,1,0:T(8,128)(2,1)S(1)}, bf16[8,16,512]{2,1,0:T(8,128)(2,1)S(1)}, u32[]{:S(2)}, u32[]{:S(2)}) collective-permute-start(bf16[8,16,512]{2,1,0:T(8,128)(2,1)S(1)} %get-tuple-element.102), channel_id=1, source_target_pairs={{0,8},{8,0},{16,24},{24,16},{1,9},{9,1},{17,25},{25,17},{2,10},{10... | collective-permute-start | bytes 393224 | tf_op jit(solution)/shard_map/ppermute | solution.py:235
  34.2 1.5 %collective-permute-start.15 = (bf16[8,16,512]{2,1,0:T(8,128)(2,1)S(1)}, bf16[8,16,512]{2,1,0:T(8,128)(2,1)S(1)}, u32[]{:S(2)}, u32[]{:S(2)}) collective-permute-start(bf16[8,16,512]{2,1,0:T(8,128)(2,1)S(1)} %get-tuple-element.103), channel_id=1, source_target_pairs={{0,16},{8,24},{16,0},{24,8},{1,17},{9,25},{17,1},{25,9},{2,18},{10... | collective-permute-start | bytes 393224 | tf_op jit(solution)/shard_map/ppermute | solution.py:235
  35.7 0.7 %placed.1.refs_4_ = bf16[1,4,8,16,512]{4,3,2,1,0:T(8,128)(2,1)} custom-call(bf16[8,16,512]{2,1,0:T(8,128)(2,1)S(1)} %get-tuple-element.104.refs_0_, bf16[8,16,512]{2,1,0:T(8,128)(2,1)S(1)} %collective-permute-done.16.refs_1_), custom_call_target="tpu_custom_call" | custom-call | tf_op jit(solution)/shard_map/placed/pallas_call | solution.py:732
  36.4 1.2 %collective-permute-done.12.refs_0_ = bf16[32,2048]{1,0:T(8,128)(2,1)S(1)} collective-permute-done((bf16[32,2048]{1,0:T(8,128)(2,1)S(1)}, bf16[32,2048]{1,0:T(8,128)(2,1)S(1)}, u32[]{:S(2)}, u32[]{:S(2)}) %collective-permute-start.12) | collective-permute-done | bytes 131104 | tf_op jit(solution)/shard_map/ppermute | solution.py:235
  37.7 0.4 %collective-permute-done.13.refs_1_ = bf16[32,2048]{1,0:T(8,128)(2,1)S(1)} collective-permute-done((bf16[32,2048]{1,0:T(8,128)(2,1)S(1)}, bf16[32,2048]{1,0:T(8,128)(2,1)S(1)}, u32[]{:S(2)}, u32[]{:S(2)}) %collective-permute-start.13) | collective-permute-done | bytes 131104 | tf_op jit(solution)/shard_map/ppermute | solution.py:235
  38.1 1.1 %collective-permute-done.15.refs_3_ = bf16[8,16,512]{2,1,0:T(8,128)(2,1)S(1)} collective-permute-done((bf16[8,16,512]{2,1,0:T(8,128)(2,1)S(1)}, bf16[8,16,512]{2,1,0:T(8,128)(2,1)S(1)}, u32[]{:S(2)}, u32[]{:S(2)}) %collective-permute-start.15) | collective-permute-done | bytes 131104 | tf_op jit(solution)/shard_map/ppermute | solution.py:235
  39.2 0.8 %finished.1 = (f32[32,2048]{1,0:T(8,128)}, bf16[1,4,8,16,512]{4,3,2,1,0:T(8,128)(2,1)}) custom-call(f32[32,2048]{1,0:T(8,128)S(1)} %get-tuple-element.99.base_ref, bf16[32,2048]{1,0:T(8,128)(2,1)S(1)} %collective-permute-done.12.refs_0_, bf16[32,2048]{1,0:T(8,128)(2,1)S(1)} %collective-permute-done.13.refs_1_, ...), custom_call_target="tpu_custom_call", output_to_operand_aliasing={{1}: (5, {})} | custom-call | tf_op jit(solution)/shard_map/finished/pallas_call | solution.py:766
  (12 shorter events, 0.1 us)
Async XLA Ops:
  0.6 10.7 %collective-permute-start.1 = (bf16[32,2048]{1,0:T(8,128)(2,1)}, bf16[32,2048]{1,0:T(8,128)(2,1)S(1)}, u32[]{:S(2)}, u32[]{:S(2)}) collective-permute-start(bf16[32,2048]{1,0:T(8,128)(2,1)} %refs_2_.1), channel_id=1, source_target_pairs={{0,4},{1,5},{2,6},{3,7},{4,0},{5,1},{6,2},{7,3},{8,12},{9,13},{10,... | collective-permute-start | bytes 393224 | tf_op jit(solution)/shard_map/ppermute | solution.py:235
  4.7 6.8 %collective-permute-start = (bf16[32,2048]{1,0:T(8,128)(2,1)}, bf16[32,2048]{1,0:T(8,128)(2,1)S(1)}, u32[]{:S(2)}, u32[]{:S(2)}) collective-permute-start(bf16[32,2048]{1,0:T(8,128)(2,1)} %refs_2_.1), channel_id=1, source_target_pairs={{0,2},{1,3},{2,0},{3,1},{4,6},{5,7},{6,4},{7,5},{8,10},{9,11},{10,... | collective-permute-start | bytes 393224 | tf_op jit(solution)/shard_map/ppermute | solution.py:235
  6.3 6.7 %collective-permute-start.3 = (bf16[32,2048]{1,0:T(8,128)(2,1)}, bf16[32,2048]{1,0:T(8,128)(2,1)S(1)}, u32[]{:S(2)}, u32[]{:S(2)}) collective-permute-start(bf16[32,2048]{1,0:T(8,128)(2,1)} %refs_2_.1), channel_id=1, source_target_pairs={{0,1},{1,0},{2,3},{3,2},{4,5},{5,4},{6,7},{7,6},{8,9},{9,8},{10,11... | collective-permute-start | bytes 393224 | tf_op jit(solution)/shard_map/ppermute | solution.py:235
  11.6 1.4 %collective-permute-start.4 = (bf16[32,2048]{1,0:T(8,128)(2,1)S(1)}, bf16[32,2048]{1,0:T(8,128)(2,1)S(1)}, u32[]{:S(2)}, u32[]{:S(2)}) collective-permute-start(bf16[32,2048]{1,0:T(8,128)(2,1)S(1)} %collective-permute-done.refs_1_), channel_id=1, source_target_pairs={{0,1},{1,0},{2,3},{3,2},{4,5},{5,4},{6,7},{7,6},{8,9},{9,8},{10,11... | collective-permute-start | bytes 393224 | tf_op jit(solution)/shard_map/ppermute | solution.py:235
  11.6 5.9 %collective-permute-start.2 = (bf16[32,2048]{1,0:T(8,128)(2,1)S(1)}, bf16[32,2048]{1,0:T(8,128)(2,1)S(1)}, u32[]{:S(2)}, u32[]{:S(2)}) collective-permute-start(bf16[32,2048]{1,0:T(8,128)(2,1)S(1)} %collective-permute-done.1.refs_3_), channel_id=1, source_target_pairs={{0,2},{1,3},{2,0},{3,1},{4,6},{5,7},{6,4},{7,5},{8,10},{9,11},{10,... | collective-permute-start | bytes 393224 | tf_op jit(solution)/shard_map/ppermute | solution.py:235
  16.4 1.4 %collective-permute-start.5 = (bf16[32,2048]{1,0:T(8,128)(2,1)S(1)}, bf16[32,2048]{1,0:T(8,128)(2,1)S(1)}, u32[]{:S(2)}, u32[]{:S(2)}) collective-permute-start(bf16[32,2048]{1,0:T(8,128)(2,1)S(1)} %collective-permute-done.1.refs_3_), channel_id=1, source_target_pairs={{0,1},{1,0},{2,3},{3,2},{4,5},{5,4},{6,7},{7,6},{8,9},{9,8},{10,11... | collective-permute-start | bytes 393224 | tf_op jit(solution)/shard_map/ppermute | solution.py:235
  17.8 1.3 %collective-permute-start.6 = (bf16[32,2048]{1,0:T(8,128)(2,1)S(1)}, bf16[32,2048]{1,0:T(8,128)(2,1)S(1)}, u32[]{:S(2)}, u32[]{:S(2)}) collective-permute-start(bf16[32,2048]{1,0:T(8,128)(2,1)S(1)} %collective-permute-done.2.refs_1_), channel_id=1, source_target_pairs={{0,1},{1,0},{2,3},{3,2},{4,5},{5,4},{6,7},{7,6},{8,9},{9,8},{10,11... | collective-permute-start | bytes 393224 | tf_op jit(solution)/shard_map/ppermute | solution.py:235
  21.8 1.4 %collective-permute-start.7 = (bf16[32,2048]{1,0:T(8,128)(2,1)S(1)}, bf16[32,2048]{1,0:T(8,128)(2,1)S(1)}, u32[]{:S(2)}, u32[]{:S(2)}) collective-permute-start(bf16[32,2048]{1,0:T(8,128)(2,1)S(1)} %get-tuple-element.79), channel_id=1, source_target_pairs={{0,1},{1,0},{2,3},{3,2},{4,5},{5,4},{6,7},{7,6},{8,9},{9,8},{10,11... | collective-permute-start | bytes 393224 | tf_op jit(solution)/shard_map/ppermute | solution.py:235
  23.2 5.7 %collective-permute-start.8 = (bf16[32,2048]{1,0:T(8,128)(2,1)S(1)}, bf16[32,2048]{1,0:T(8,128)(2,1)S(1)}, u32[]{:S(2)}, u32[]{:S(2)}) collective-permute-start(bf16[32,2048]{1,0:T(8,128)(2,1)S(1)} %third_added.1), channel_id=1, source_target_pairs={{0,2},{1,3},{2,0},{3,1},{4,6},{5,7},{6,4},{7,5},{8,10},{9,11},{10,... | collective-permute-start | bytes 393224 | tf_op jit(solution)/shard_map/ppermute | solution.py:235
  24.6 4.3 %collective-permute-start.9 = (bf16[32,2048]{1,0:T(8,128)(2,1)S(1)}, bf16[32,2048]{1,0:T(8,128)(2,1)S(1)}, u32[]{:S(2)}, u32[]{:S(2)}) collective-permute-start(bf16[32,2048]{1,0:T(8,128)(2,1)S(1)} %get-tuple-element.87), channel_id=1, source_target_pairs={{0,1},{1,0},{2,3},{3,2},{4,5},{5,4},{6,7},{7,6},{8,9},{9,8},{10,11... | collective-permute-start | bytes 393224 | tf_op jit(solution)/shard_map/ppermute | solution.py:235
  24.6 4.3 %collective-permute-start.10 = (bf16[32,2048]{1,0:T(8,128)(2,1)S(1)}, bf16[32,2048]{1,0:T(8,128)(2,1)S(1)}, u32[]{:S(2)}, u32[]{:S(2)}) collective-permute-start(bf16[32,2048]{1,0:T(8,128)(2,1)S(1)} %get-tuple-element.89), channel_id=1, source_target_pairs={{0,1},{1,0},{2,3},{3,2},{4,5},{5,4},{6,7},{7,6},{8,9},{9,8},{10,11... | collective-permute-start | bytes 393224 | tf_op jit(solution)/shard_map/ppermute | solution.py:235
  25.1 3.8 %collective-permute-start.11 = (bf16[32,2048]{1,0:T(8,128)(2,1)S(1)}, bf16[32,2048]{1,0:T(8,128)(2,1)S(1)}, u32[]{:S(2)}, u32[]{:S(2)}) collective-permute-start(bf16[32,2048]{1,0:T(8,128)(2,1)S(1)} %get-tuple-element.91), channel_id=1, source_target_pairs={{0,1},{1,0},{2,3},{3,2},{4,5},{5,4},{6,7},{7,6},{8,9},{9,8},{10,11... | collective-permute-start | bytes 393224 | tf_op jit(solution)/shard_map/ppermute | solution.py:235
  25.4 10.3 %collective-permute-start.16 = (bf16[8,16,512]{2,1,0:T(8,128)(2,1)S(1)}, bf16[8,16,512]{2,1,0:T(8,128)(2,1)S(1)}, u32[]{:S(2)}, u32[]{:S(2)}) collective-permute-start(bf16[8,16,512]{2,1,0:T(8,128)(2,1)S(1)} %get-tuple-element.105), channel_id=1, source_target_pairs={{0,24},{8,16},{16,8},{24,0},{1,25},{9,17},{17,9},{25,1},{2,26},{10... | collective-permute-start | bytes 393224 | tf_op jit(solution)/shard_map/ppermute | solution.py:235
  29.0 8.6 %collective-permute-start.12 = (bf16[32,2048]{1,0:T(8,128)(2,1)S(1)}, bf16[32,2048]{1,0:T(8,128)(2,1)S(1)}, u32[]{:S(2)}, u32[]{:S(2)}) collective-permute-start(bf16[32,2048]{1,0:T(8,128)(2,1)S(1)} %get-tuple-element.100), channel_id=1, source_target_pairs={{0,4},{1,5},{2,6},{3,7},{4,0},{5,1},{6,2},{7,3},{8,12},{9,13},{10,... | collective-permute-start | bytes 393224 | tf_op jit(solution)/shard_map/ppermute | solution.py:235
  31.5 6.6 %collective-permute-start.13 = (bf16[32,2048]{1,0:T(8,128)(2,1)S(1)}, bf16[32,2048]{1,0:T(8,128)(2,1)S(1)}, u32[]{:S(2)}, u32[]{:S(2)}) collective-permute-start(bf16[32,2048]{1,0:T(8,128)(2,1)S(1)} %get-tuple-element.101), channel_id=1, source_target_pairs={{0,2},{1,3},{2,0},{3,1},{4,6},{5,7},{6,4},{7,5},{8,10},{9,11},{10,... | collective-permute-start | bytes 393224 | tf_op jit(solution)/shard_map/ppermute | solution.py:235
  32.7 5.4 %collective-permute-start.14 = (bf16[8,16,512]{2,1,0:T(8,128)(2,1)S(1)}, bf16[8,16,512]{2,1,0:T(8,128)(2,1)S(1)}, u32[]{:S(2)}, u32[]{:S(2)}) collective-permute-start(bf16[8,16,512]{2,1,0:T(8,128)(2,1)S(1)} %get-tuple-element.102), channel_id=1, source_target_pairs={{0,8},{8,0},{16,24},{24,16},{1,9},{9,1},{17,25},{25,17},{2,10},{10... | collective-permute-start | bytes 393224 | tf_op jit(solution)/shard_map/ppermute | solution.py:235
  34.2 5.0 %collective-permute-start.15 = (bf16[8,16,512]{2,1,0:T(8,128)(2,1)S(1)}, bf16[8,16,512]{2,1,0:T(8,128)(2,1)S(1)}, u32[]{:S(2)}, u32[]{:S(2)}) collective-permute-start(bf16[8,16,512]{2,1,0:T(8,128)(2,1)S(1)} %get-tuple-element.103), channel_id=1, source_target_pairs={{0,16},{8,24},{16,0},{24,8},{1,17},{9,25},{17,1},{25,9},{2,18},{10... | collective-permute-start | bytes 393224 | tf_op jit(solution)/shard_map/ppermute | solution.py:235

commit v11 on v8

--- a/solution.py
+++ b/solution.py
@@ -529,9 +529,9 @@
     origins = ((CHIPS - 2, 1), (CHIPS - 1, 0), (CHIPS - 1, 1))
     places = [position_of(kind, half, block_rows) for kind, half in origins]
     project(attention_scr, heads_ref, table_refs, places, joined_ref, first)
-    hide(feedforward_scr, upward_ref, hidden_scr, 0)
     rows = CORES * block_rows
     attended = attend(joined_ref, offsets_ref, tokens - rows, rows, block_rows)
+    hide(feedforward_scr, upward_ref, hidden_scr, 0)
     chunk = 512
     for begin in range(0, downward_ref.shape[1], chunk):
         columns = slice(begin, begin + chunk)
@@ -815,9 +815,8 @@
     heads, upward, downward = weights
     destinations, own_joined, own_hidden = staged[12:]
 
-    first, own_joined = lax.optimization_barrier((first, own_joined))
+    first, second, own_joined = lax.optimization_barrier((first, second, own_joined))
     first_beside = exchanged(first, "tensor", 1)
-    second, first_beside, beside = lax.optimization_barrier((second, first_beside, beside))
     third = exchanged(second, "tensor", to_chip[1])
     middle_joined, middle_hidden, output = middle_rows(
         "middle_rows",

time: 39.5 us -> 40 us (1.013)
  starting transfers between devices: 15.4 us -> 18.7 us
  waiting for transfers between devices: 9.7 us -> 6.75 us
    ppermute x17, starting transfers between devices: 15.4 us -> 18.7 us  [exchanged(): lax.ppermute(block, axis, [(member, member ^ mask) for member in range(co...]
    ppermute x17, waiting for transfers between devices: 9.7 us -> 6.75 us  [exchanged(): lax.ppermute(block, axis, [(member, member ^ mask) for member in range(co...]
  transfers between devices with their start and end apart: 17 -> 17, of which waited for: 7 -> 8; matrix products, arithmetic and copies ran while one was open for 0% -> 0% of each run, Pallas kernels for 26% -> 25%
where the time goes in v11:
time: 40 us; the launch traced here: 39.8 us
  starting transfers between devices  18.7 us (47%)
  Pallas kernels  13.7 us (34%)
  waiting for transfers between devices  6.75 us (17%)
  between operations  0.72 us (2%)
    ppermute x17, starting transfers between devices, exchanged(): lax.ppermute(block, axis, [(member, member ^ mask) for member in range(co...  18.7 us
    ppermute x17, waiting for transfers between devices, exchanged(): lax.ppermute(block, axis, [(member, member ^ mask) for member in range(co...  6.75 us
    pallas_call x1, Pallas kernels, own_rows(): pl.pallas_call(functools.partial(own_kernel, count, replica_count), out_s...  5.27 us
    pallas_call x1, Pallas kernels, last_rows(): pl.pallas_call(last_kernel, out_shape=[pltpu.VMEM((tokens, 3 * HD), jnp.b...  2.68 us
    pallas_call x1, Pallas kernels, middle_rows(): pl.pallas_call(functools.partial(middle_kernel, origins), out_shape=[pltp...  2.09 us
    pallas_call x1, Pallas kernels, fed_rows(): pl.pallas_call(fed_kernel, out_shape=pltpu.VMEM((rows, width), jnp.float3...  0.85 us
    pallas_call x1, Pallas kernels, finished(): pl.pallas_call(functools.partial(finish_kernel, masks), out_shape=[jax.Sh...  0.82 us
  transfers between devices with their start and end apart: 17, of which 8 were waited for; matrix products, arithmetic and copies ran while one was open for 0% of the time, Pallas kernels for 25%

profile of v11, /device:TPU:0, one launch (start us, length us, event | category | flops | bytes accessed | tf_op | source)
XLA Modules:
  0.0 39.8 jit_solution(74495773596911634)
XLA Ops:
  0.6 4.1 %collective-permute-start.1 = (bf16[32,2048]{1,0:T(8,128)(2,1)}, bf16[32,2048]{1,0:T(8,128)(2,1)S(1)}, u32[]{:S(2)}, u32[]{:S(2)}) collective-permute-start(bf16[32,2048]{1,0:T(8,128)(2,1)} %refs_2_.1), channel_id=1, source_target_pairs={{0,4},{1,5},{2,6},{3,7},{4,0},{5,1},{6,2},{7,3},{8,12},{9,13},{10,... | collective-permute-start | bytes 393224 | tf_op jit(solution)/shard_map/ppermute | solution.py:235
  4.7 1.6 %collective-permute-start = (bf16[32,2048]{1,0:T(8,128)(2,1)}, bf16[32,2048]{1,0:T(8,128)(2,1)S(1)}, u32[]{:S(2)}, u32[]{:S(2)}) collective-permute-start(bf16[32,2048]{1,0:T(8,128)(2,1)} %refs_2_.1), channel_id=1, source_target_pairs={{0,2},{1,3},{2,0},{3,1},{4,6},{5,7},{6,4},{7,5},{8,10},{9,11},{10,... | collective-permute-start | bytes 393224 | tf_op jit(solution)/shard_map/ppermute | solution.py:235
  6.3 5.3 %own_rows.1 = (s32[1,256]{1,0:T(1,128)}, s32[1,16]{1,0:T(1,128)}, bf16[32,2048]{1,0:T(8,128)(2,1)S(1)}, f32[1,2048]{1,0:T(1,128)S(1)}, f32[1,2048]{1,0:T(1,128)S...) custom-call(s32[1,256]{1,0:T(1,128)} %refs_0_.1, ...), custom_call_target="tpu_custom_call" | custom-call | flops 234881024 | bytes 11682880 | tf_op jit(solution)/shard_map/own_rows/pallas_call | solution.py:452
  11.6 0.0 collective-permute-done.1.refs_3_
  11.6 0.6 %collective-permute-start.4 = (bf16[32,2048]{1,0:T(8,128)(2,1)S(1)}, bf16[32,2048]{1,0:T(8,128)(2,1)S(1)}, u32[]{:S(2)}, u32[]{:S(2)}) collective-permute-start(bf16[32,2048]{1,0:T(8,128)(2,1)S(1)} %collective-permute-done.refs_1_), channel_id=1, source_target_pairs={{0,1},{1,0},{2,3},{3,2},{4,5},{5,4},{6,7},{7,6},{8,9},{9,8},{10,11... | collective-permute-start | bytes 393224 | tf_op jit(solution)/shard_map/ppermute | solution.py:235
  12.2 0.8 %collective-permute-start.2 = (bf16[32,2048]{1,0:T(8,128)(2,1)S(1)}, bf16[32,2048]{1,0:T(8,128)(2,1)S(1)}, u32[]{:S(2)}, u32[]{:S(2)}) collective-permute-start(bf16[32,2048]{1,0:T(8,128)(2,1)S(1)} %collective-permute-done.1.refs_3_), channel_id=1, source_target_pairs={{0,2},{1,3},{2,0},{3,1},{4,6},{5,7},{6,4},{7,5},{8,10},{9,11},{10,... | collective-permute-start | bytes 393224 | tf_op jit(solution)/shard_map/ppermute | solution.py:235
  13.0 0.2 collective-permute-done.4.refs_2_
  13.2 2.1 %middle_rows.1 = (bf16[128,768]{1,0:T(8,128)(2,1)S(1)}, bf16[128,1024]{1,0:T(8,128)(2,1)S(1)}, bf16[256,2048]{1,0:T(8,128)(2,1)S(1)}) custom-call(bf16[32,2048]{1,0:T(8,128)(2,1)S(1)} %collective-permute-done.3.refs_0_, bf16[32,2048]{1,0:T(8,128)(2,1)S(1)} %collective-permute-done.refs_1_, bf16[32,2048]{1,0:T(8,128)(2,1)S(1)} %collective-permute-done.4.refs_2_, ...), custom_call_target="tpu_custom_call" | custom-call | flops 939524096 | bytes 1048576 | tf_op jit(solution)/shard_map/middle_rows/pallas_call | solution.py:492
  15.3 0.4 %collective-permute-start.5 = (bf16[32,2048]{1,0:T(8,128)(2,1)S(1)}, bf16[32,2048]{1,0:T(8,128)(2,1)S(1)}, u32[]{:S(2)}, u32[]{:S(2)}) collective-permute-start(bf16[32,2048]{1,0:T(8,128)(2,1)S(1)} %collective-permute-done.1.refs_3_), channel_id=1, source_target_pairs={{0,1},{1,0},{2,3},{3,2},{4,5},{5,4},{6,7},{7,6},{8,9},{9,8},{10,11... | collective-permute-start | bytes 393224 | tf_op jit(solution)/shard_map/ppermute | solution.py:235
  15.7 2.0 %collective-permute-done.2.refs_1_ = bf16[32,2048]{1,0:T(8,128)(2,1)S(1)} collective-permute-done((bf16[32,2048]{1,0:T(8,128)(2,1)S(1)}, bf16[32,2048]{1,0:T(8,128)(2,1)S(1)}, u32[]{:S(2)}, u32[]{:S(2)}) %collective-permute-start.2) | collective-permute-done | bytes 131104 | tf_op jit(solution)/shard_map/ppermute | solution.py:235
  17.7 0.0 collective-permute-done.5.refs_0_
  17.7 0.8 %fed_rows.1.fed_ref = f32[160,2048]{1,0:T(8,128)S(1)} custom-call(bf16[32,1024]{1,0:T(8,128)(2,1)S(1)} %get-tuple-element.70.own_hidden_ref, bf16[128,1024]{1,0:T(8,128)(2,1)S(1)} %get-tuple-element.71.middle_hidden_ref, bf16[1024,2048]{1,0:T(8,128)(2,1)S(1)} %get-tuple-element.72.downward_ref.refs_7_), custom_call_target="tpu_custom_call" | custom-call | flops 671088640 | bytes 1048576 | tf_op jit(solution)/shard_map/fed_rows/pallas_call | solution.py:590
  18.5 0.5 %collective-permute-done.6.refs_2_ = bf16[32,2048]{1,0:T(8,128)(2,1)S(1)} collective-permute-done((bf16[32,2048]{1,0:T(8,128)(2,1)S(1)}, bf16[32,2048]{1,0:T(8,128)(2,1)S(1)}, u32[]{:S(2)}, u32[]{:S(2)}) %collective-permute-start.6) | collective-permute-done | bytes 131104 | tf_op jit(solution)/shard_map/ppermute | solution.py:235
  19.0 2.7 %last_rows.1 = (bf16[256,768]{1,0:T(8,128)(2,1)S(1)}, f32[32,2048]{1,0:T(8,128)S(1)}, bf16[32,2048]{1,0:T(8,128)(2,1)S(1)}, f32[32,2048]{1,0:T(8,128)S(1)}) custom-call(bf16[32,2048]{1,0:T(8,128)(2,1)S(1)} %collective-permute-done.5.refs_0_, bf16[32,2048]{1,0:T(8,128)(2,1)S(1)} %collective-permute-done.2.refs_1_, ...), custom_call_target="tpu_custom_call" | custom-call | flops 1207959552 | bytes 1048576 | tf_op jit(solution)/shard_map/last_rows/pallas_call | solution.py:552
  21.7 0.2 collective-permute-start.7
  21.9 0.8 %rest_rows.1 = (bf16[32,2048]{1,0:T(8,128)(2,1)S(1)}, bf16[32,2048]{1,0:T(8,128)(2,1)S(1)}, bf16[32,2048]{1,0:T(8,128)(2,1)S(1)}, f32[32,2048]{1,0:T(8,128)S(1)}...) custom-call(bf16[256,768]{1,0:T(8,128)(2,1)S(1)} %get-tuple-element.95.joined_ref, ...), custom_call_target="tpu_custom_call" | custom-call | flops 201326592 | bytes 1048576 | tf_op jit(solution)/shard_map/rest_rows/pallas_call | solution.py:629
  22.7 0.4 %collective-permute-done.7.refs_1_ = bf16[32,2048]{1,0:T(8,128)(2,1)S(1)} collective-permute-done((bf16[32,2048]{1,0:T(8,128)(2,1)S(1)}, bf16[32,2048]{1,0:T(8,128)(2,1)S(1)}, u32[]{:S(2)}, u32[]{:S(2)}) %collective-permute-start.7) | collective-permute-done | bytes 131104 | tf_op jit(solution)/shard_map/ppermute | solution.py:235
  23.1 1.3 %collective-permute-start.8 = (bf16[32,2048]{1,0:T(8,128)(2,1)S(1)}, bf16[32,2048]{1,0:T(8,128)(2,1)S(1)}, u32[]{:S(2)}, u32[]{:S(2)}) collective-permute-start(bf16[32,2048]{1,0:T(8,128)(2,1)S(1)} %third_added.1), channel_id=1, source_target_pairs={{0,2},{1,3},{2,0},{3,1},{4,6},{5,7},{6,4},{7,5},{8,10},{9,11},{10,... | collective-permute-start | bytes 393224 | tf_op jit(solution)/shard_map/ppermute | solution.py:235
  24.4 0.5 %collective-permute-start.10 = (bf16[32,2048]{1,0:T(8,128)(2,1)S(1)}, bf16[32,2048]{1,0:T(8,128)(2,1)S(1)}, u32[]{:S(2)}, u32[]{:S(2)}) collective-permute-start(bf16[32,2048]{1,0:T(8,128)(2,1)S(1)} %get-tuple-element.89), channel_id=1, source_target_pairs={{0,1},{1,0},{2,3},{3,2},{4,5},{5,4},{6,7},{7,6},{8,9},{9,8},{10,11... | collective-permute-start | bytes 393224 | tf_op jit(solution)/shard_map/ppermute | solution.py:235
  25.0 0.3 cached_pages.1
  25.3 2.5 %collective-permute-start.16 = (bf16[8,16,512]{2,1,0:T(8,128)(2,1)S(1)}, bf16[8,16,512]{2,1,0:T(8,128)(2,1)S(1)}, u32[]{:S(2)}, u32[]{:S(2)}) collective-permute-start(bf16[8,16,512]{2,1,0:T(8,128)(2,1)S(1)} %get-tuple-element.105), channel_id=1, source_target_pairs={{0,24},{8,16},{16,8},{24,0},{1,25},{9,17},{17,9},{25,1},{2,26},{10... | collective-permute-start | bytes 393224 | tf_op jit(solution)/shard_map/ppermute | solution.py:235
  27.8 1.0 %collective-permute-done.8.passing_ref = bf16[32,2048]{1,0:T(8,128)(2,1)S(1)} collective-permute-done((bf16[32,2048]{1,0:T(8,128)(2,1)S(1)}, bf16[32,2048]{1,0:T(8,128)(2,1)S(1)}, u32[]{:S(2)}, u32[]{:S(2)}) %collective-permute-start.8) | collective-permute-done | bytes 131104 | tf_op jit(solution)/shard_map/ppermute | solution.py:235
  28.8 0.1 remaining_sums.1
  28.9 1.9 %collective-permute-start.12 = (bf16[32,2048]{1,0:T(8,128)(2,1)S(1)}, bf16[32,2048]{1,0:T(8,128)(2,1)S(1)}, u32[]{:S(2)}, u32[]{:S(2)}) collective-permute-start(bf16[32,2048]{1,0:T(8,128)(2,1)S(1)} %get-tuple-element.100), channel_id=1, source_target_pairs={{0,4},{1,5},{2,6},{3,7},{4,0},{5,1},{6,2},{7,3},{8,12},{9,13},{10,... | collective-permute-start | bytes 393224 | tf_op jit(solution)/shard_map/ppermute | solution.py:235
  30.8 1.7 %collective-permute-start.13 = (bf16[32,2048]{1,0:T(8,128)(2,1)S(1)}, bf16[32,2048]{1,0:T(8,128)(2,1)S(1)}, u32[]{:S(2)}, u32[]{:S(2)}) collective-permute-start(bf16[32,2048]{1,0:T(8,128)(2,1)S(1)} %get-tuple-element.101), channel_id=1, source_target_pairs={{0,2},{1,3},{2,0},{3,1},{4,6},{5,7},{6,4},{7,5},{8,10},{9,11},{10,... | collective-permute-start | bytes 393224 | tf_op jit(solution)/shard_map/ppermute | solution.py:235
  32.5 1.5 %collective-permute-start.14 = (bf16[8,16,512]{2,1,0:T(8,128)(2,1)S(1)}, bf16[8,16,512]{2,1,0:T(8,128)(2,1)S(1)}, u32[]{:S(2)}, u32[]{:S(2)}) collective-permute-start(bf16[8,16,512]{2,1,0:T(8,128)(2,1)S(1)} %get-tuple-element.102), channel_id=1, source_target_pairs={{0,8},{8,0},{16,24},{24,16},{1,9},{9,1},{17,25},{25,17},{2,10},{10... | collective-permute-start | bytes 393224 | tf_op jit(solution)/shard_map/ppermute | solution.py:235
  34.0 1.5 %collective-permute-start.15 = (bf16[8,16,512]{2,1,0:T(8,128)(2,1)S(1)}, bf16[8,16,512]{2,1,0:T(8,128)(2,1)S(1)}, u32[]{:S(2)}, u32[]{:S(2)}) collective-permute-start(bf16[8,16,512]{2,1,0:T(8,128)(2,1)S(1)} %get-tuple-element.103), channel_id=1, source_target_pairs={{0,16},{8,24},{16,0},{24,8},{1,17},{9,25},{17,1},{25,9},{2,18},{10... | collective-permute-start | bytes 393224 | tf_op jit(solution)/shard_map/ppermute | solution.py:235
  35.6 0.7 %placed.1.refs_4_ = bf16[1,4,8,16,512]{4,3,2,1,0:T(8,128)(2,1)} custom-call(bf16[8,16,512]{2,1,0:T(8,128)(2,1)S(1)} %get-tuple-element.104.refs_0_, bf16[8,16,512]{2,1,0:T(8,128)(2,1)S(1)} %collective-permute-done.16.refs_1_), custom_call_target="tpu_custom_call" | custom-call | tf_op jit(solution)/shard_map/placed/pallas_call | solution.py:733
  36.3 1.2 %collective-permute-done.12.refs_0_ = bf16[32,2048]{1,0:T(8,128)(2,1)S(1)} collective-permute-done((bf16[32,2048]{1,0:T(8,128)(2,1)S(1)}, bf16[32,2048]{1,0:T(8,128)(2,1)S(1)}, u32[]{:S(2)}, u32[]{:S(2)}) %collective-permute-start.12) | collective-permute-done | bytes 131104 | tf_op jit(solution)/shard_map/ppermute | solution.py:235
  37.4 0.3 collective-permute-done.13.refs_1_
  37.7 1.3 %collective-permute-done.15.refs_3_ = bf16[8,16,512]{2,1,0:T(8,128)(2,1)S(1)} collective-permute-done((bf16[8,16,512]{2,1,0:T(8,128)(2,1)S(1)}, bf16[8,16,512]{2,1,0:T(8,128)(2,1)S(1)}, u32[]{:S(2)}, u32[]{:S(2)}) %collective-permute-start.15) | collective-permute-done | bytes 131104 | tf_op jit(solution)/shard_map/ppermute | solution.py:235
  39.0 0.8 %finished.1 = (f32[32,2048]{1,0:T(8,128)}, bf16[1,4,8,16,512]{4,3,2,1,0:T(8,128)(2,1)}) custom-call(f32[32,2048]{1,0:T(8,128)S(1)} %get-tuple-element.99.base_ref, bf16[32,2048]{1,0:T(8,128)(2,1)S(1)} %collective-permute-done.12.refs_0_, bf16[32,2048]{1,0:T(8,128)(2,1)S(1)} %collective-permute-done.13.refs_1_, ...), custom_call_target="tpu_custom_call", output_to_operand_aliasing={{1}: (5, {})} | custom-call | tf_op jit(solution)/shard_map/finished/pallas_call | solution.py:767
  (12 shorter events, 0.1 us)
Async XLA Ops:
  0.6 11.0 %collective-permute-start.1 = (bf16[32,2048]{1,0:T(8,128)(2,1)}, bf16[32,2048]{1,0:T(8,128)(2,1)S(1)}, u32[]{:S(2)}, u32[]{:S(2)}) collective-permute-start(bf16[32,2048]{1,0:T(8,128)(2,1)} %refs_2_.1), channel_id=1, source_target_pairs={{0,4},{1,5},{2,6},{3,7},{4,0},{5,1},{6,2},{7,3},{8,12},{9,13},{10,... | collective-permute-start | bytes 393224 | tf_op jit(solution)/shard_map/ppermute | solution.py:235
  4.7 6.9 %collective-permute-start = (bf16[32,2048]{1,0:T(8,128)(2,1)}, bf16[32,2048]{1,0:T(8,128)(2,1)S(1)}, u32[]{:S(2)}, u32[]{:S(2)}) collective-permute-start(bf16[32,2048]{1,0:T(8,128)(2,1)} %refs_2_.1), channel_id=1, source_target_pairs={{0,2},{1,3},{2,0},{3,1},{4,6},{5,7},{6,4},{7,5},{8,10},{9,11},{10,... | collective-permute-start | bytes 393224 | tf_op jit(solution)/shard_map/ppermute | solution.py:235
  6.3 6.7 %collective-permute-start.3 = (bf16[32,2048]{1,0:T(8,128)(2,1)}, bf16[32,2048]{1,0:T(8,128)(2,1)S(1)}, u32[]{:S(2)}, u32[]{:S(2)}) collective-permute-start(bf16[32,2048]{1,0:T(8,128)(2,1)} %refs_2_.1), channel_id=1, source_target_pairs={{0,1},{1,0},{2,3},{3,2},{4,5},{5,4},{6,7},{7,6},{8,9},{9,8},{10,11... | collective-permute-start | bytes 393224 | tf_op jit(solution)/shard_map/ppermute | solution.py:235
  11.6 1.6 %collective-permute-start.4 = (bf16[32,2048]{1,0:T(8,128)(2,1)S(1)}, bf16[32,2048]{1,0:T(8,128)(2,1)S(1)}, u32[]{:S(2)}, u32[]{:S(2)}) collective-permute-start(bf16[32,2048]{1,0:T(8,128)(2,1)S(1)} %collective-permute-done.refs_1_), channel_id=1, source_target_pairs={{0,1},{1,0},{2,3},{3,2},{4,5},{5,4},{6,7},{7,6},{8,9},{9,8},{10,11... | collective-permute-start | bytes 393224 | tf_op jit(solution)/shard_map/ppermute | solution.py:235
  12.2 5.5 %collective-permute-start.2 = (bf16[32,2048]{1,0:T(8,128)(2,1)S(1)}, bf16[32,2048]{1,0:T(8,128)(2,1)S(1)}, u32[]{:S(2)}, u32[]{:S(2)}) collective-permute-start(bf16[32,2048]{1,0:T(8,128)(2,1)S(1)} %collective-permute-done.1.refs_3_), channel_id=1, source_target_pairs={{0,2},{1,3},{2,0},{3,1},{4,6},{5,7},{6,4},{7,5},{8,10},{9,11},{10,... | collective-permute-start | bytes 393224 | tf_op jit(solution)/shard_map/ppermute | solution.py:235
  15.3 2.4 %collective-permute-start.5 = (bf16[32,2048]{1,0:T(8,128)(2,1)S(1)}, bf16[32,2048]{1,0:T(8,128)(2,1)S(1)}, u32[]{:S(2)}, u32[]{:S(2)}) collective-permute-start(bf16[32,2048]{1,0:T(8,128)(2,1)S(1)} %collective-permute-done.1.refs_3_), channel_id=1, source_target_pairs={{0,1},{1,0},{2,3},{3,2},{4,5},{5,4},{6,7},{7,6},{8,9},{9,8},{10,11... | collective-permute-start | bytes 393224 | tf_op jit(solution)/shard_map/ppermute | solution.py:235
  17.7 1.3 %collective-permute-start.6 = (bf16[32,2048]{1,0:T(8,128)(2,1)S(1)}, bf16[32,2048]{1,0:T(8,128)(2,1)S(1)}, u32[]{:S(2)}, u32[]{:S(2)}) collective-permute-start(bf16[32,2048]{1,0:T(8,128)(2,1)S(1)} %collective-permute-done.2.refs_1_), channel_id=1, source_target_pairs={{0,1},{1,0},{2,3},{3,2},{4,5},{5,4},{6,7},{7,6},{8,9},{9,8},{10,11... | collective-permute-start | bytes 393224 | tf_op jit(solution)/shard_map/ppermute | solution.py:235
  21.7 1.4 %collective-permute-start.7 = (bf16[32,2048]{1,0:T(8,128)(2,1)S(1)}, bf16[32,2048]{1,0:T(8,128)(2,1)S(1)}, u32[]{:S(2)}, u32[]{:S(2)}) collective-permute-start(bf16[32,2048]{1,0:T(8,128)(2,1)S(1)} %get-tuple-element.79), channel_id=1, source_target_pairs={{0,1},{1,0},{2,3},{3,2},{4,5},{5,4},{6,7},{7,6},{8,9},{9,8},{10,11... | collective-permute-start | bytes 393224 | tf_op jit(solution)/shard_map/ppermute | solution.py:235
  23.1 5.6 %collective-permute-start.8 = (bf16[32,2048]{1,0:T(8,128)(2,1)S(1)}, bf16[32,2048]{1,0:T(8,128)(2,1)S(1)}, u32[]{:S(2)}, u32[]{:S(2)}) collective-permute-start(bf16[32,2048]{1,0:T(8,128)(2,1)S(1)} %third_added.1), channel_id=1, source_target_pairs={{0,2},{1,3},{2,0},{3,1},{4,6},{5,7},{6,4},{7,5},{8,10},{9,11},{10,... | collective-permute-start | bytes 393224 | tf_op jit(solution)/shard_map/ppermute | solution.py:235
  24.4 4.3 %collective-permute-start.9 = (bf16[32,2048]{1,0:T(8,128)(2,1)S(1)}, bf16[32,2048]{1,0:T(8,128)(2,1)S(1)}, u32[]{:S(2)}, u32[]{:S(2)}) collective-permute-start(bf16[32,2048]{1,0:T(8,128)(2,1)S(1)} %get-tuple-element.87), channel_id=1, source_target_pairs={{0,1},{1,0},{2,3},{3,2},{4,5},{5,4},{6,7},{7,6},{8,9},{9,8},{10,11... | collective-permute-start | bytes 393224 | tf_op jit(solution)/shard_map/ppermute | solution.py:235
  24.4 4.3 %collective-permute-start.10 = (bf16[32,2048]{1,0:T(8,128)(2,1)S(1)}, bf16[32,2048]{1,0:T(8,128)(2,1)S(1)}, u32[]{:S(2)}, u32[]{:S(2)}) collective-permute-start(bf16[32,2048]{1,0:T(8,128)(2,1)S(1)} %get-tuple-element.89), channel_id=1, source_target_pairs={{0,1},{1,0},{2,3},{3,2},{4,5},{5,4},{6,7},{7,6},{8,9},{9,8},{10,11... | collective-permute-start | bytes 393224 | tf_op jit(solution)/shard_map/ppermute | solution.py:235
  24.9 3.8 %collective-permute-start.11 = (bf16[32,2048]{1,0:T(8,128)(2,1)S(1)}, bf16[32,2048]{1,0:T(8,128)(2,1)S(1)}, u32[]{:S(2)}, u32[]{:S(2)}) collective-permute-start(bf16[32,2048]{1,0:T(8,128)(2,1)S(1)} %get-tuple-element.91), channel_id=1, source_target_pairs={{0,1},{1,0},{2,3},{3,2},{4,5},{5,4},{6,7},{7,6},{8,9},{9,8},{10,11... | collective-permute-start | bytes 393224 | tf_op jit(solution)/shard_map/ppermute | solution.py:235
  25.3 10.3 %collective-permute-start.16 = (bf16[8,16,512]{2,1,0:T(8,128)(2,1)S(1)}, bf16[8,16,512]{2,1,0:T(8,128)(2,1)S(1)}, u32[]{:S(2)}, u32[]{:S(2)}) collective-permute-start(bf16[8,16,512]{2,1,0:T(8,128)(2,1)S(1)} %get-tuple-element.105), channel_id=1, source_target_pairs={{0,24},{8,16},{16,8},{24,0},{1,25},{9,17},{17,9},{25,1},{2,26},{10... | collective-permute-start | bytes 393224 | tf_op jit(solution)/shard_map/ppermute | solution.py:235
  28.9 8.6 %collective-permute-start.12 = (bf16[32,2048]{1,0:T(8,128)(2,1)S(1)}, bf16[32,2048]{1,0:T(8,128)(2,1)S(1)}, u32[]{:S(2)}, u32[]{:S(2)}) collective-permute-start(bf16[32,2048]{1,0:T(8,128)(2,1)S(1)} %get-tuple-element.100), channel_id=1, source_target_pairs={{0,4},{1,5},{2,6},{3,7},{4,0},{5,1},{6,2},{7,3},{8,12},{9,13},{10,... | collective-permute-start | bytes 393224 | tf_op jit(solution)/shard_map/ppermute | solution.py:235
  30.8 6.9 %collective-permute-start.13 = (bf16[32,2048]{1,0:T(8,128)(2,1)S(1)}, bf16[32,2048]{1,0:T(8,128)(2,1)S(1)}, u32[]{:S(2)}, u32[]{:S(2)}) collective-permute-start(bf16[32,2048]{1,0:T(8,128)(2,1)S(1)} %get-tuple-element.101), channel_id=1, source_target_pairs={{0,2},{1,3},{2,0},{3,1},{4,6},{5,7},{6,4},{7,5},{8,10},{9,11},{10,... | collective-permute-start | bytes 393224 | tf_op jit(solution)/shard_map/ppermute | solution.py:235
  32.5 5.2 %collective-permute-start.14 = (bf16[8,16,512]{2,1,0:T(8,128)(2,1)S(1)}, bf16[8,16,512]{2,1,0:T(8,128)(2,1)S(1)}, u32[]{:S(2)}, u32[]{:S(2)}) collective-permute-start(bf16[8,16,512]{2,1,0:T(8,128)(2,1)S(1)} %get-tuple-element.102), channel_id=1, source_target_pairs={{0,8},{8,0},{16,24},{24,16},{1,9},{9,1},{17,25},{25,17},{2,10},{10... | collective-permute-start | bytes 393224 | tf_op jit(solution)/shard_map/ppermute | solution.py:235
  34.0 5.0 %collective-permute-start.15 = (bf16[8,16,512]{2,1,0:T(8,128)(2,1)S(1)}, bf16[8,16,512]{2,1,0:T(8,128)(2,1)S(1)}, u32[]{:S(2)}, u32[]{:S(2)}) collective-permute-start(bf16[8,16,512]{2,1,0:T(8,128)(2,1)S(1)} %get-tuple-element.103), channel_id=1, source_target_pairs={{0,16},{8,24},{16,0},{24,8},{1,17},{9,25},{17,1},{25,9},{2,18},{10... | collective-permute-start | bytes 393224 | tf_op jit(solution)/shard_map/ppermute | solution.py:235

commit v12 on v11

--- a/solution.py
+++ b/solution.py
@@ -262,7 +262,7 @@
     return ((((chip ^ kind) << 1) | (core ^ half)) << bits) | (place & (block_rows - 1))
 
 
-def normalize(blocks, gain_refs, normed_refs):
+def normalize(blocks, gain_refs, normed_refs, place=0):
     piece = 16
     gains = [gain_ref[...] for gain_ref in gain_refs]
     for number, block_ref in enumerate(blocks):
@@ -273,7 +273,7 @@
             shifted = floats - center
             spread = jnp.mean(shifted * shifted, axis=-1, keepdims=True)
             scaled = shifted * lax.rsqrt(spread + epsilon)
-            first = number * block_rows + part
+            first = place + number * block_rows + part
             for gain, normed_ref in zip(gains, normed_refs):
                 normed_ref[first : first + piece, :] = (scaled * gain).astype(jnp.bfloat16)
 
@@ -281,36 +281,32 @@
 def project(normed_ref, heads_ref, table_refs, places, joined_ref, first):
     rows = normed_ref.shape[0]
     block_rows = rows // len(places)
-    for component in range(3):
-        columns = slice(component * HD, (component + 1) * HD)
-        joined = jnp.dot(
-            normed_ref[...], heads_ref[:, columns], preferred_element_type=jnp.float32
-        ).astype(jnp.bfloat16)
-        joined_ref[first : first + rows, columns] = joined
-        if component < 2:
-            cosine, sine_down, sine_up = [
-                jnp.concatenate(
-                    [
-                        table_ref[pl.ds(pl.multiple_of(place, block_rows), block_rows), :]
-                        for place in places
-                    ],
-                    0,
-                )
-                for table_ref in table_refs
-            ]
-            turning = joined[:, :128].astype(jnp.float32)
-            turned = (
-                turning * cosine
-                + pltpu.roll(turning, 128 - ROT // 2, 1) * sine_down
-                + pltpu.roll(turning, ROT // 2, 1) * sine_up
-            )
-            joined_ref[first : first + rows, component * HD : component * HD + 128] = turned.astype(
-                jnp.bfloat16
-            )
-
-
-def hide(normed_ref, upward_ref, hidden_ref, place):
-    chunk = 256
+    own = slice(first, first + rows)
+    cosine, sine_down, sine_up = [
+        jnp.concatenate(
+            [
+                table_ref[pl.ds(pl.multiple_of(place, block_rows), block_rows), :]
+                for place in places
+            ],
+            0,
+        )
+        for table_ref in table_refs
+    ]
+    joined_ref[own, :] = jnp.dot(
+        normed_ref[...], heads_ref[...], preferred_element_type=jnp.float32
+    ).astype(jnp.bfloat16)
+    for begin in (0, HD):
+        columns = slice(begin, begin + 128)
+        turning = joined_ref[own, columns].astype(jnp.float32)
+        turned = (
+            turning * cosine
+            + pltpu.roll(turning, 128 - ROT // 2, 1) * sine_down
+            + pltpu.roll(turning, ROT // 2, 1) * sine_up
+        )
+        joined_ref[own, columns] = turned.astype(jnp.bfloat16)
+
+
+def hide(normed_ref, upward_ref, hidden_ref, place, chunk=256):
     rows = slice(place, place + normed_ref.shape[0])
     for first in range(0, upward_ref.shape[1], chunk):
         columns = slice(first, first + chunk)
@@ -515,24 +511,28 @@
 
 
 def last_kernel(*refs):
-    blocks, (gain_a, gain_f, heads_ref, upward_ref, downward_ref, output_ref) = refs[:3], refs[3:9]
+    block_ref, *normed_refs = refs[:3]
+    gain_a, gain_f, heads_ref, upward_ref, downward_ref, output_ref = refs[3:9]
     offsets_ref, *table_refs = refs[9:13]
     own_joined_ref, middle_joined_ref = refs[13:15]
     joined_ref, fed_ref, sibling_ref, own_ref = refs[15:19]
     attention_scr, feedforward_scr, hidden_scr = refs[19:]
-    block_rows = blocks[0].shape[0]
+    block_rows = block_ref.shape[0]
     tokens = joined_ref.shape[0]
-    first = tokens - len(blocks) * block_rows
-    normalize(blocks, [gain_a, gain_f], [attention_scr, feedforward_scr])
+    first = tokens - attention_scr.shape[0]
+    count = normed_refs[0].shape[0]
+    normalize([block_ref], [gain_a, gain_f], [attention_scr, feedforward_scr], count)
+    for normed_ref, normed_scr in zip(normed_refs, (attention_scr, feedforward_scr)):
+        normed_scr[:count, :] = normed_ref[...]
     joined_ref[:block_rows, :] = own_joined_ref[...]
     joined_ref[block_rows:first, :] = middle_joined_ref[...]
     origins = ((CHIPS - 2, 1), (CHIPS - 1, 0), (CHIPS - 1, 1))
     places = [position_of(kind, half, block_rows) for kind, half in origins]
     project(attention_scr, heads_ref, table_refs, places, joined_ref, first)
     rows = CORES * block_rows
+    hide(feedforward_scr, upward_ref, hidden_scr, 0, 512)
     attended = attend(joined_ref, offsets_ref, tokens - rows, rows, block_rows)
-    hide(feedforward_scr, upward_ref, hidden_scr, 0)
-    chunk = 512
+    chunk = 1024
     for begin in range(0, downward_ref.shape[1], chunk):
         columns = slice(begin, begin + chunk)
         fed = jnp.dot(hidden_scr[...], downward_ref[:, columns], preferred_element_type=jnp.float32)
@@ -544,9 +544,9 @@
         sibling_ref[:, columns] = partial[block_rows:].astype(jnp.bfloat16)
 
 
-def last_rows(blocks, gains, weights, tables, own_joined, middle_joined):
-    block_rows, width = blocks[0].shape
-    rows = len(blocks) * block_rows
+def last_rows(block, normed, gains, weights, tables, own_joined, middle_joined):
+    block_rows, width = block.shape
+    rows = normed[0].shape[0] + block_rows
     hidden_width = weights[1].shape[1]
     tokens = CHIPS * CORES * block_rows
     return pl.pallas_call(
@@ -557,7 +557,7 @@
             pltpu.VMEM((block_rows, width), jnp.bfloat16),
             pltpu.VMEM((block_rows, width), jnp.float32),
         ],
-        in_specs=vmem_specs(len(blocks) + 2 + 4 + 4 + 2),
+        in_specs=vmem_specs(1 + 2 + 2 + 4 + 4 + 2),
         out_specs=vmem_specs(4),
         scratch_shapes=[
             pltpu.VMEM((rows, width), jnp.bfloat16),
@@ -571,10 +571,12 @@
             transcendentals=rows * hidden_width,
         ),
         name="last_rows",
-    )(*blocks, *gains, *weights, *tables, own_joined, middle_joined)
-
-
-def fed_kernel(own_hidden_ref, middle_hidden_ref, downward_ref, fed_ref):
+    )(block, *normed, *gains, *weights, *tables, own_joined, middle_joined)
+
+
+def fed_kernel(own_hidden_ref, middle_hidden_ref, downward_ref, *refs):
+    blocks, gain_refs, (fed_ref, *normed_refs) = refs[:2], refs[2:4], refs[4:]
+    normalize(blocks, gain_refs, normed_refs)
     hidden = jnp.concatenate([own_hidden_ref[...], middle_hidden_ref[...]], 0)
     chunk = 512
     for begin in range(0, downward_ref.shape[1], chunk):
@@ -584,20 +586,21 @@
         )
 
 
-def fed_rows(own_hidden, middle_hidden, downward_weight):
+def fed_rows(own_hidden, middle_hidden, downward_weight, blocks, gains):
     rows = own_hidden.shape[0] + middle_hidden.shape[0]
     depth, width = downward_weight.shape
+    normed = pltpu.VMEM((len(blocks) * blocks[0].shape[0], width), jnp.bfloat16)
     return pl.pallas_call(
         fed_kernel,
-        out_shape=pltpu.VMEM((rows, width), jnp.float32),
-        in_specs=vmem_specs(3),
-        out_specs=pl.BlockSpec(memory_space=pltpu.VMEM),
+        out_shape=[pltpu.VMEM((rows, width), jnp.float32), normed, normed],
+        in_specs=vmem_specs(7),
+        out_specs=vmem_specs(3),
         compiler_params=parameters(12),
         cost_estimate=pl.CostEstimate(
             flops=2 * rows * depth * width, bytes_accessed=MIB, transcendentals=0
         ),
         name="fed_rows",
-    )(own_hidden, middle_hidden, downward_weight)
+    )(own_hidden, middle_hidden, downward_weight, *blocks, *gains)
 
 
 def rest_kernel(joined_ref, offsets_ref, output_ref, fed_ref, fed_beside_ref, *refs):
@@ -833,10 +836,10 @@
         (third, second_beside, middle_joined, middle_hidden)
     )
     third_beside = exchanged(third, "tensor", 1)
-    fed = fed_rows(own_hidden, middle_hidden, downward)
-    third_beside, fed = lax.optimization_barrier((third_beside, fed))
+    fed, *normed = fed_rows(own_hidden, middle_hidden, downward, (second_beside, third), gains)
     joined, fed_beside, sibling, own = last_rows(
-        (second_beside, third, third_beside),
+        third_beside,
+        normed,
         gains,
         (heads, upward, downward, output),
         tables,

time: 40 us -> 39.7 us (level)
  transfers between devices with their start and end apart: 17 -> 17, of which waited for: 8 -> 8; matrix products, arithmetic and copies ran while one was open for 0% -> 0% of each run, Pallas kernels for 25% -> 26%
where the time goes in v12:
time: 39.7 us; the launch traced here: 39.6 us
  starting transfers between devices  18.7 us (47%)
  Pallas kernels  13.5 us (34%)
  waiting for transfers between devices  6.68 us (17%)
  between operations  0.72 us (2%)
    ppermute x17, starting transfers between devices, exchanged(): lax.ppermute(block, axis, [(member, member ^ mask) for member in range(co...  18.7 us
    ppermute x17, waiting for transfers between devices, exchanged(): lax.ppermute(block, axis, [(member, member ^ mask) for member in range(co...  6.68 us
    pallas_call x1, Pallas kernels, own_rows(): pl.pallas_call(functools.partial(own_kernel, count, replica_count), out_s...  5.27 us
    pallas_call x1, Pallas kernels, last_rows(): pl.pallas_call(last_kernel, out_shape=[pltpu.VMEM((tokens, 3 * HD), jnp.b...  2.41 us
    pallas_call x1, Pallas kernels, middle_rows(): pl.pallas_call(functools.partial(middle_kernel, origins), out_shape=[pltp...  2.12 us
    pallas_call x1, Pallas kernels, fed_rows(): pl.pallas_call(fed_kernel, out_shape=[pltpu.VMEM((rows, width), jnp.float...  0.9 us
    pallas_call x1, Pallas kernels, finished(): pl.pallas_call(functools.partial(finish_kernel, masks), out_shape=[jax.Sh...  0.82 us
  transfers between devices with their start and end apart: 17, of which 8 were waited for; matrix products, arithmetic and copies ran while one was open for 0% of the time, Pallas kernels for 26%

profile of v12, /device:TPU:0, one launch (start us, length us, event | category | flops | bytes accessed | tf_op | source)
XLA Modules:
  0.0 39.6 jit_solution(3592304371072720370)
XLA Ops:
  0.6 4.1 %collective-permute-start.1 = (bf16[32,2048]{1,0:T(8,128)(2,1)}, bf16[32,2048]{1,0:T(8,128)(2,1)S(1)}, u32[]{:S(2)}, u32[]{:S(2)}) collective-permute-start(bf16[32,2048]{1,0:T(8,128)(2,1)} %refs_2_.1), channel_id=1, source_target_pairs={{0,4},{1,5},{2,6},{3,7},{4,0},{5,1},{6,2},{7,3},{8,12},{9,13},{10,... | collective-permute-start | bytes 393224 | tf_op jit(solution)/shard_map/ppermute | solution.py:235
  4.7 1.6 %collective-permute-start = (bf16[32,2048]{1,0:T(8,128)(2,1)}, bf16[32,2048]{1,0:T(8,128)(2,1)S(1)}, u32[]{:S(2)}, u32[]{:S(2)}) collective-permute-start(bf16[32,2048]{1,0:T(8,128)(2,1)} %refs_2_.1), channel_id=1, source_target_pairs={{0,2},{1,3},{2,0},{3,1},{4,6},{5,7},{6,4},{7,5},{8,10},{9,11},{10,... | collective-permute-start | bytes 393224 | tf_op jit(solution)/shard_map/ppermute | solution.py:235
  6.3 5.3 %own_rows.1 = (s32[1,256]{1,0:T(1,128)}, s32[1,16]{1,0:T(1,128)}, bf16[32,2048]{1,0:T(8,128)(2,1)S(1)}, f32[1,2048]{1,0:T(1,128)S(1)}, f32[1,2048]{1,0:T(1,128)S...) custom-call(s32[1,256]{1,0:T(1,128)} %refs_0_.1, ...), custom_call_target="tpu_custom_call" | custom-call | flops 234881024 | bytes 11682880 | tf_op jit(solution)/shard_map/own_rows/pallas_call | solution.py:448
  11.6 0.0 collective-permute-done.1.refs_3_
  11.6 0.6 %collective-permute-start.4 = (bf16[32,2048]{1,0:T(8,128)(2,1)S(1)}, bf16[32,2048]{1,0:T(8,128)(2,1)S(1)}, u32[]{:S(2)}, u32[]{:S(2)}) collective-permute-start(bf16[32,2048]{1,0:T(8,128)(2,1)S(1)} %collective-permute-done.refs_1_), channel_id=1, source_target_pairs={{0,1},{1,0},{2,3},{3,2},{4,5},{5,4},{6,7},{7,6},{8,9},{9,8},{10,11... | collective-permute-start | bytes 393224 | tf_op jit(solution)/shard_map/ppermute | solution.py:235
  12.2 0.8 %collective-permute-start.2 = (bf16[32,2048]{1,0:T(8,128)(2,1)S(1)}, bf16[32,2048]{1,0:T(8,128)(2,1)S(1)}, u32[]{:S(2)}, u32[]{:S(2)}) collective-permute-start(bf16[32,2048]{1,0:T(8,128)(2,1)S(1)} %collective-permute-done.1.refs_3_), channel_id=1, source_target_pairs={{0,2},{1,3},{2,0},{3,1},{4,6},{5,7},{6,4},{7,5},{8,10},{9,11},{10,... | collective-permute-start | bytes 393224 | tf_op jit(solution)/shard_map/ppermute | solution.py:235
  13.0 0.2 collective-permute-done.4.refs_2_
  13.2 2.1 %middle_rows.1 = (bf16[128,768]{1,0:T(8,128)(2,1)S(1)}, bf16[128,1024]{1,0:T(8,128)(2,1)S(1)}, bf16[256,2048]{1,0:T(8,128)(2,1)S(1)}) custom-call(bf16[32,2048]{1,0:T(8,128)(2,1)S(1)} %collective-permute-done.3.refs_0_, bf16[32,2048]{1,0:T(8,128)(2,1)S(1)} %collective-permute-done.refs_1_, bf16[32,2048]{1,0:T(8,128)(2,1)S(1)} %collective-permute-done.4.refs_2_, ...), custom_call_target="tpu_custom_call" | custom-call | flops 939524096 | bytes 1048576 | tf_op jit(solution)/shard_map/middle_rows/pallas_call | solution.py:488
  15.3 0.4 %collective-permute-start.5 = (bf16[32,2048]{1,0:T(8,128)(2,1)S(1)}, bf16[32,2048]{1,0:T(8,128)(2,1)S(1)}, u32[]{:S(2)}, u32[]{:S(2)}) collective-permute-start(bf16[32,2048]{1,0:T(8,128)(2,1)S(1)} %collective-permute-done.1.refs_3_), channel_id=1, source_target_pairs={{0,1},{1,0},{2,3},{3,2},{4,5},{5,4},{6,7},{7,6},{8,9},{9,8},{10,11... | collective-permute-start | bytes 393224 | tf_op jit(solution)/shard_map/ppermute | solution.py:235
  15.7 1.9 %collective-permute-done.2.refs_1_ = bf16[32,2048]{1,0:T(8,128)(2,1)S(1)} collective-permute-done((bf16[32,2048]{1,0:T(8,128)(2,1)S(1)}, bf16[32,2048]{1,0:T(8,128)(2,1)S(1)}, u32[]{:S(2)}, u32[]{:S(2)}) %collective-permute-start.2) | collective-permute-done | bytes 131104 | tf_op jit(solution)/shard_map/ppermute | solution.py:235
  17.7 0.0 collective-permute-done.5.refs_0_
  17.7 0.9 %fed_rows.1 = (f32[160,2048]{1,0:T(8,128)S(1)}, bf16[64,2048]{1,0:T(8,128)(2,1)S(1)}, bf16[64,2048]{1,0:T(8,128)(2,1)S(1)}) custom-call(bf16[32,1024]{1,0:T(8,128)(2,1)S(1)} %get-tuple-element.70.own_hidden_ref, bf16[128,1024]{1,0:T(8,128)(2,1)S(1)} %get-tuple-element.71.middle_hidden_ref, bf16[1024,2048]{1,0:T(8,128)(2,1)S(1)} %get-tuple-element.72.downward_ref.refs_7_, ...), custom_call_target="tpu_custom_call" | custom-call | flops 671088640 | bytes 1048576 | tf_op jit(solution)/shard_map/fed_rows/pallas_call | solution.py:593
  18.6 0.4 %collective-permute-done.6.refs_0_ = bf16[32,2048]{1,0:T(8,128)(2,1)S(1)} collective-permute-done((bf16[32,2048]{1,0:T(8,128)(2,1)S(1)}, bf16[32,2048]{1,0:T(8,128)(2,1)S(1)}, u32[]{:S(2)}, u32[]{:S(2)}) %collective-permute-start.6) | collective-permute-done | bytes 131104 | tf_op jit(solution)/shard_map/ppermute | solution.py:235
  19.0 2.4 %last_rows.1 = (bf16[256,768]{1,0:T(8,128)(2,1)S(1)}, f32[32,2048]{1,0:T(8,128)S(1)}, bf16[32,2048]{1,0:T(8,128)(2,1)S(1)}, f32[32,2048]{1,0:T(8,128)S(1)}) custom-call(bf16[32,2048]{1,0:T(8,128)(2,1)S(1)} %collective-permute-done.6.refs_0_, bf16[64,2048]{1,0:T(8,128)(2,1)S(1)} %get-tuple-element.74.refs_1_, bf16[64,2048]{1,0:T(8,128)(2,1)S(1)} %get-tuple-element.75.refs_2_, ...), custom_call_target="tpu_custom_call" | custom-call | flops 1207959552 | bytes 1048576 | tf_op jit(solution)/shard_map/last_rows/pallas_call | solution.py:552
  21.4 0.2 collective-permute-start.7
  21.6 0.8 %rest_rows.1 = (bf16[32,2048]{1,0:T(8,128)(2,1)S(1)}, bf16[32,2048]{1,0:T(8,128)(2,1)S(1)}, bf16[32,2048]{1,0:T(8,128)(2,1)S(1)}, f32[32,2048]{1,0:T(8,128)S(1)}...) custom-call(bf16[256,768]{1,0:T(8,128)(2,1)S(1)} %get-tuple-element.97.joined_ref, ...), custom_call_target="tpu_custom_call" | custom-call | flops 201326592 | bytes 1048576 | tf_op jit(solution)/shard_map/rest_rows/pallas_call | solution.py:632
  22.4 0.4 %collective-permute-done.7.refs_1_ = bf16[32,2048]{1,0:T(8,128)(2,1)S(1)} collective-permute-done((bf16[32,2048]{1,0:T(8,128)(2,1)S(1)}, bf16[32,2048]{1,0:T(8,128)(2,1)S(1)}, u32[]{:S(2)}, u32[]{:S(2)}) %collective-permute-start.7) | collective-permute-done | bytes 131104 | tf_op jit(solution)/shard_map/ppermute | solution.py:235
  22.9 1.3 %collective-permute-start.8 = (bf16[32,2048]{1,0:T(8,128)(2,1)S(1)}, bf16[32,2048]{1,0:T(8,128)(2,1)S(1)}, u32[]{:S(2)}, u32[]{:S(2)}) collective-permute-start(bf16[32,2048]{1,0:T(8,128)(2,1)S(1)} %third_added.1), channel_id=1, source_target_pairs={{0,2},{1,3},{2,0},{3,1},{4,6},{5,7},{6,4},{7,5},{8,10},{9,11},{10,... | collective-permute-start | bytes 393224 | tf_op jit(solution)/shard_map/ppermute | solution.py:235
  24.2 0.5 %collective-permute-start.10 = (bf16[32,2048]{1,0:T(8,128)(2,1)S(1)}, bf16[32,2048]{1,0:T(8,128)(2,1)S(1)}, u32[]{:S(2)}, u32[]{:S(2)}) collective-permute-start(bf16[32,2048]{1,0:T(8,128)(2,1)S(1)} %get-tuple-element.91), channel_id=1, source_target_pairs={{0,1},{1,0},{2,3},{3,2},{4,5},{5,4},{6,7},{7,6},{8,9},{9,8},{10,11... | collective-permute-start | bytes 393224 | tf_op jit(solution)/shard_map/ppermute | solution.py:235
  24.7 0.3 cached_pages.1
  25.0 2.5 %collective-permute-start.16 = (bf16[8,16,512]{2,1,0:T(8,128)(2,1)S(1)}, bf16[8,16,512]{2,1,0:T(8,128)(2,1)S(1)}, u32[]{:S(2)}, u32[]{:S(2)}) collective-permute-start(bf16[8,16,512]{2,1,0:T(8,128)(2,1)S(1)} %get-tuple-element.107), channel_id=1, source_target_pairs={{0,24},{8,16},{16,8},{24,0},{1,25},{9,17},{17,9},{25,1},{2,26},{10... | collective-permute-start | bytes 393224 | tf_op jit(solution)/shard_map/ppermute | solution.py:235
  27.5 1.0 %collective-permute-done.8.passing_ref = bf16[32,2048]{1,0:T(8,128)(2,1)S(1)} collective-permute-done((bf16[32,2048]{1,0:T(8,128)(2,1)S(1)}, bf16[32,2048]{1,0:T(8,128)(2,1)S(1)}, u32[]{:S(2)}, u32[]{:S(2)}) %collective-permute-start.8) | collective-permute-done | bytes 131104 | tf_op jit(solution)/shard_map/ppermute | solution.py:235
  28.5 0.1 remaining_sums.1
  28.6 1.9 %collective-permute-start.12 = (bf16[32,2048]{1,0:T(8,128)(2,1)S(1)}, bf16[32,2048]{1,0:T(8,128)(2,1)S(1)}, u32[]{:S(2)}, u32[]{:S(2)}) collective-permute-start(bf16[32,2048]{1,0:T(8,128)(2,1)S(1)} %get-tuple-element.102), channel_id=1, source_target_pairs={{0,4},{1,5},{2,6},{3,7},{4,0},{5,1},{6,2},{7,3},{8,12},{9,13},{10,... | collective-permute-start | bytes 393224 | tf_op jit(solution)/shard_map/ppermute | solution.py:235
  30.5 1.7 %collective-permute-start.13 = (bf16[32,2048]{1,0:T(8,128)(2,1)S(1)}, bf16[32,2048]{1,0:T(8,128)(2,1)S(1)}, u32[]{:S(2)}, u32[]{:S(2)}) collective-permute-start(bf16[32,2048]{1,0:T(8,128)(2,1)S(1)} %get-tuple-element.103), channel_id=1, source_target_pairs={{0,2},{1,3},{2,0},{3,1},{4,6},{5,7},{6,4},{7,5},{8,10},{9,11},{10,... | collective-permute-start | bytes 393224 | tf_op jit(solution)/shard_map/ppermute | solution.py:235
  32.3 1.5 %collective-permute-start.14 = (bf16[8,16,512]{2,1,0:T(8,128)(2,1)S(1)}, bf16[8,16,512]{2,1,0:T(8,128)(2,1)S(1)}, u32[]{:S(2)}, u32[]{:S(2)}) collective-permute-start(bf16[8,16,512]{2,1,0:T(8,128)(2,1)S(1)} %get-tuple-element.104), channel_id=1, source_target_pairs={{0,8},{8,0},{16,24},{24,16},{1,9},{9,1},{17,25},{25,17},{2,10},{10... | collective-permute-start | bytes 393224 | tf_op jit(solution)/shard_map/ppermute | solution.py:235
  33.8 1.5 %collective-permute-start.15 = (bf16[8,16,512]{2,1,0:T(8,128)(2,1)S(1)}, bf16[8,16,512]{2,1,0:T(8,128)(2,1)S(1)}, u32[]{:S(2)}, u32[]{:S(2)}) collective-permute-start(bf16[8,16,512]{2,1,0:T(8,128)(2,1)S(1)} %get-tuple-element.105), channel_id=1, source_target_pairs={{0,16},{8,24},{16,0},{24,8},{1,17},{9,25},{17,1},{25,9},{2,18},{10... | collective-permute-start | bytes 393224 | tf_op jit(solution)/shard_map/ppermute | solution.py:235
  35.3 0.7 %placed.1.refs_4_ = bf16[1,4,8,16,512]{4,3,2,1,0:T(8,128)(2,1)} custom-call(bf16[8,16,512]{2,1,0:T(8,128)(2,1)S(1)} %get-tuple-element.106.refs_0_, bf16[8,16,512]{2,1,0:T(8,128)(2,1)S(1)} %collective-permute-done.16.refs_1_), custom_call_target="tpu_custom_call" | custom-call | tf_op jit(solution)/shard_map/placed/pallas_call | solution.py:736
  36.0 1.2 %collective-permute-done.12.refs_0_ = bf16[32,2048]{1,0:T(8,128)(2,1)S(1)} collective-permute-done((bf16[32,2048]{1,0:T(8,128)(2,1)S(1)}, bf16[32,2048]{1,0:T(8,128)(2,1)S(1)}, u32[]{:S(2)}, u32[]{:S(2)}) %collective-permute-start.12) | collective-permute-done | bytes 131104 | tf_op jit(solution)/shard_map/ppermute | solution.py:235
  37.2 0.3 collective-permute-done.13.refs_1_
  37.5 1.3 %collective-permute-done.15.refs_3_ = bf16[8,16,512]{2,1,0:T(8,128)(2,1)S(1)} collective-permute-done((bf16[8,16,512]{2,1,0:T(8,128)(2,1)S(1)}, bf16[8,16,512]{2,1,0:T(8,128)(2,1)S(1)}, u32[]{:S(2)}, u32[]{:S(2)}) %collective-permute-start.15) | collective-permute-done | bytes 131104 | tf_op jit(solution)/shard_map/ppermute | solution.py:235
  38.7 0.8 %finished.1 = (f32[32,2048]{1,0:T(8,128)}, bf16[1,4,8,16,512]{4,3,2,1,0:T(8,128)(2,1)}) custom-call(f32[32,2048]{1,0:T(8,128)S(1)} %get-tuple-element.101.base_ref, bf16[32,2048]{1,0:T(8,128)(2,1)S(1)} %collective-permute-done.12.refs_0_, bf16[32,2048]{1,0:T(8,128)(2,1)S(1)} %collective-permute-done.13.refs_1_, ...), custom_call_target="tpu_custom_call", output_to_operand_aliasing={{1}: (5, {})} | custom-call | tf_op jit(solution)/shard_map/finished/pallas_call | solution.py:770
  (12 shorter events, 0.1 us)
Async XLA Ops:
  0.6 11.0 %collective-permute-start.1 = (bf16[32,2048]{1,0:T(8,128)(2,1)}, bf16[32,2048]{1,0:T(8,128)(2,1)S(1)}, u32[]{:S(2)}, u32[]{:S(2)}) collective-permute-start(bf16[32,2048]{1,0:T(8,128)(2,1)} %refs_2_.1), channel_id=1, source_target_pairs={{0,4},{1,5},{2,6},{3,7},{4,0},{5,1},{6,2},{7,3},{8,12},{9,13},{10,... | collective-permute-start | bytes 393224 | tf_op jit(solution)/shard_map/ppermute | solution.py:235
  4.7 6.9 %collective-permute-start = (bf16[32,2048]{1,0:T(8,128)(2,1)}, bf16[32,2048]{1,0:T(8,128)(2,1)S(1)}, u32[]{:S(2)}, u32[]{:S(2)}) collective-permute-start(bf16[32,2048]{1,0:T(8,128)(2,1)} %refs_2_.1), channel_id=1, source_target_pairs={{0,2},{1,3},{2,0},{3,1},{4,6},{5,7},{6,4},{7,5},{8,10},{9,11},{10,... | collective-permute-start | bytes 393224 | tf_op jit(solution)/shard_map/ppermute | solution.py:235
  6.3 6.7 %collective-permute-start.3 = (bf16[32,2048]{1,0:T(8,128)(2,1)}, bf16[32,2048]{1,0:T(8,128)(2,1)S(1)}, u32[]{:S(2)}, u32[]{:S(2)}) collective-permute-start(bf16[32,2048]{1,0:T(8,128)(2,1)} %refs_2_.1), channel_id=1, source_target_pairs={{0,1},{1,0},{2,3},{3,2},{4,5},{5,4},{6,7},{7,6},{8,9},{9,8},{10,11... | collective-permute-start | bytes 393224 | tf_op jit(solution)/shard_map/ppermute | solution.py:235
  11.6 1.6 %collective-permute-start.4 = (bf16[32,2048]{1,0:T(8,128)(2,1)S(1)}, bf16[32,2048]{1,0:T(8,128)(2,1)S(1)}, u32[]{:S(2)}, u32[]{:S(2)}) collective-permute-start(bf16[32,2048]{1,0:T(8,128)(2,1)S(1)} %collective-permute-done.refs_1_), channel_id=1, source_target_pairs={{0,1},{1,0},{2,3},{3,2},{4,5},{5,4},{6,7},{7,6},{8,9},{9,8},{10,11... | collective-permute-start | bytes 393224 | tf_op jit(solution)/shard_map/ppermute | solution.py:235
  12.2 5.5 %collective-permute-start.2 = (bf16[32,2048]{1,0:T(8,128)(2,1)S(1)}, bf16[32,2048]{1,0:T(8,128)(2,1)S(1)}, u32[]{:S(2)}, u32[]{:S(2)}) collective-permute-start(bf16[32,2048]{1,0:T(8,128)(2,1)S(1)} %collective-permute-done.1.refs_3_), channel_id=1, source_target_pairs={{0,2},{1,3},{2,0},{3,1},{4,6},{5,7},{6,4},{7,5},{8,10},{9,11},{10,... | collective-permute-start | bytes 393224 | tf_op jit(solution)/shard_map/ppermute | solution.py:235
  15.3 2.4 %collective-permute-start.5 = (bf16[32,2048]{1,0:T(8,128)(2,1)S(1)}, bf16[32,2048]{1,0:T(8,128)(2,1)S(1)}, u32[]{:S(2)}, u32[]{:S(2)}) collective-permute-start(bf16[32,2048]{1,0:T(8,128)(2,1)S(1)} %collective-permute-done.1.refs_3_), channel_id=1, source_target_pairs={{0,1},{1,0},{2,3},{3,2},{4,5},{5,4},{6,7},{7,6},{8,9},{9,8},{10,11... | collective-permute-start | bytes 393224 | tf_op jit(solution)/shard_map/ppermute | solution.py:235
  17.7 1.3 %collective-permute-start.6 = (bf16[32,2048]{1,0:T(8,128)(2,1)S(1)}, bf16[32,2048]{1,0:T(8,128)(2,1)S(1)}, u32[]{:S(2)}, u32[]{:S(2)}) collective-permute-start(bf16[32,2048]{1,0:T(8,128)(2,1)S(1)} %collective-permute-done.2.refs_1_), channel_id=1, source_target_pairs={{0,1},{1,0},{2,3},{3,2},{4,5},{5,4},{6,7},{7,6},{8,9},{9,8},{10,11... | collective-permute-start | bytes 393224 | tf_op jit(solution)/shard_map/ppermute | solution.py:235
  21.4 1.4 %collective-permute-start.7 = (bf16[32,2048]{1,0:T(8,128)(2,1)S(1)}, bf16[32,2048]{1,0:T(8,128)(2,1)S(1)}, u32[]{:S(2)}, u32[]{:S(2)}) collective-permute-start(bf16[32,2048]{1,0:T(8,128)(2,1)S(1)} %get-tuple-element.81), channel_id=1, source_target_pairs={{0,1},{1,0},{2,3},{3,2},{4,5},{5,4},{6,7},{7,6},{8,9},{9,8},{10,11... | collective-permute-start | bytes 393224 | tf_op jit(solution)/shard_map/ppermute | solution.py:235
  22.9 5.6 %collective-permute-start.8 = (bf16[32,2048]{1,0:T(8,128)(2,1)S(1)}, bf16[32,2048]{1,0:T(8,128)(2,1)S(1)}, u32[]{:S(2)}, u32[]{:S(2)}) collective-permute-start(bf16[32,2048]{1,0:T(8,128)(2,1)S(1)} %third_added.1), channel_id=1, source_target_pairs={{0,2},{1,3},{2,0},{3,1},{4,6},{5,7},{6,4},{7,5},{8,10},{9,11},{10,... | collective-permute-start | bytes 393224 | tf_op jit(solution)/shard_map/ppermute | solution.py:235
  24.2 4.3 %collective-permute-start.9 = (bf16[32,2048]{1,0:T(8,128)(2,1)S(1)}, bf16[32,2048]{1,0:T(8,128)(2,1)S(1)}, u32[]{:S(2)}, u32[]{:S(2)}) collective-permute-start(bf16[32,2048]{1,0:T(8,128)(2,1)S(1)} %get-tuple-element.89), channel_id=1, source_target_pairs={{0,1},{1,0},{2,3},{3,2},{4,5},{5,4},{6,7},{7,6},{8,9},{9,8},{10,11... | collective-permute-start | bytes 393224 | tf_op jit(solution)/shard_map/ppermute | solution.py:235
  24.2 4.3 %collective-permute-start.10 = (bf16[32,2048]{1,0:T(8,128)(2,1)S(1)}, bf16[32,2048]{1,0:T(8,128)(2,1)S(1)}, u32[]{:S(2)}, u32[]{:S(2)}) collective-permute-start(bf16[32,2048]{1,0:T(8,128)(2,1)S(1)} %get-tuple-element.91), channel_id=1, source_target_pairs={{0,1},{1,0},{2,3},{3,2},{4,5},{5,4},{6,7},{7,6},{8,9},{9,8},{10,11... | collective-permute-start | bytes 393224 | tf_op jit(solution)/shard_map/ppermute | solution.py:235
  24.7 3.8 %collective-permute-start.11 = (bf16[32,2048]{1,0:T(8,128)(2,1)S(1)}, bf16[32,2048]{1,0:T(8,128)(2,1)S(1)}, u32[]{:S(2)}, u32[]{:S(2)}) collective-permute-start(bf16[32,2048]{1,0:T(8,128)(2,1)S(1)} %get-tuple-element.93), channel_id=1, source_target_pairs={{0,1},{1,0},{2,3},{3,2},{4,5},{5,4},{6,7},{7,6},{8,9},{9,8},{10,11... | collective-permute-start | bytes 393224 | tf_op jit(solution)/shard_map/ppermute | solution.py:235
  25.0 10.3 %collective-permute-start.16 = (bf16[8,16,512]{2,1,0:T(8,128)(2,1)S(1)}, bf16[8,16,512]{2,1,0:T(8,128)(2,1)S(1)}, u32[]{:S(2)}, u32[]{:S(2)}) collective-permute-start(bf16[8,16,512]{2,1,0:T(8,128)(2,1)S(1)} %get-tuple-element.107), channel_id=1, source_target_pairs={{0,24},{8,16},{16,8},{24,0},{1,25},{9,17},{17,9},{25,1},{2,26},{10... | collective-permute-start | bytes 393224 | tf_op jit(solution)/shard_map/ppermute | solution.py:235
  28.6 8.6 %collective-permute-start.12 = (bf16[32,2048]{1,0:T(8,128)(2,1)S(1)}, bf16[32,2048]{1,0:T(8,128)(2,1)S(1)}, u32[]{:S(2)}, u32[]{:S(2)}) collective-permute-start(bf16[32,2048]{1,0:T(8,128)(2,1)S(1)} %get-tuple-element.102), channel_id=1, source_target_pairs={{0,4},{1,5},{2,6},{3,7},{4,0},{5,1},{6,2},{7,3},{8,12},{9,13},{10,... | collective-permute-start | bytes 393224 | tf_op jit(solution)/shard_map/ppermute | solution.py:235
  30.5 6.9 %collective-permute-start.13 = (bf16[32,2048]{1,0:T(8,128)(2,1)S(1)}, bf16[32,2048]{1,0:T(8,128)(2,1)S(1)}, u32[]{:S(2)}, u32[]{:S(2)}) collective-permute-start(bf16[32,2048]{1,0:T(8,128)(2,1)S(1)} %get-tuple-element.103), channel_id=1, source_target_pairs={{0,2},{1,3},{2,0},{3,1},{4,6},{5,7},{6,4},{7,5},{8,10},{9,11},{10,... | collective-permute-start | bytes 393224 | tf_op jit(solution)/shard_map/ppermute | solution.py:235
  32.3 5.2 %collective-permute-start.14 = (bf16[8,16,512]{2,1,0:T(8,128)(2,1)S(1)}, bf16[8,16,512]{2,1,0:T(8,128)(2,1)S(1)}, u32[]{:S(2)}, u32[]{:S(2)}) collective-permute-start(bf16[8,16,512]{2,1,0:T(8,128)(2,1)S(1)} %get-tuple-element.104), channel_id=1, source_target_pairs={{0,8},{8,0},{16,24},{24,16},{1,9},{9,1},{17,25},{25,17},{2,10},{10... | collective-permute-start | bytes 393224 | tf_op jit(solution)/shard_map/ppermute | solution.py:235
  33.8 5.0 %collective-permute-start.15 = (bf16[8,16,512]{2,1,0:T(8,128)(2,1)S(1)}, bf16[8,16,512]{2,1,0:T(8,128)(2,1)S(1)}, u32[]{:S(2)}, u32[]{:S(2)}) collective-permute-start(bf16[8,16,512]{2,1,0:T(8,128)(2,1)S(1)} %get-tuple-element.105), channel_id=1, source_target_pairs={{0,16},{8,24},{16,0},{24,8},{1,17},{9,25},{17,1},{25,9},{2,18},{10... | collective-permute-start | bytes 393224 | tf_op jit(solution)/shard_map/ppermute | solution.py:235

commit v13 on v12

--- a/solution.py
+++ b/solution.py
@@ -688,60 +688,59 @@
     )(*parts)
 
 
-def sums_kernel(passing_ref, *refs):
-    zeros, ones, twos = refs[0:2], refs[2:4], refs[4:6]
-    hidden_ref, second_ref, first_ref, base_ref = refs[6:]
-
-    def total(pair, extra=None):
+def near_kernel(*refs):
+    zeros, ones, hidden_ref, first_ref, base_ref = refs[0:2], refs[2:4], *refs[4:]
+
+    def total(pair):
         received_ref, own_ref = pair
-        value = own_ref[...] + received_ref[...].astype(jnp.float32)
-        return value if extra is None else value + extra[...].astype(jnp.float32)
-
-    second_ref[...] = total(twos, passing_ref).astype(jnp.bfloat16)
+        return own_ref[...] + received_ref[...].astype(jnp.float32)
+
     first_ref[...] = total(ones).astype(jnp.bfloat16)
-    base_ref[...] = total(zeros, hidden_ref)
-
-
-def remaining_sums(passing, pairs, hidden):
+    base_ref[...] = total(zeros) + hidden_ref[...].astype(jnp.float32)
+
+
+def near_sums(pairs, hidden):
     shape = hidden.shape
     return pl.pallas_call(
-        sums_kernel,
-        out_shape=[
-            pltpu.VMEM(shape, jnp.bfloat16),
-            pltpu.VMEM(shape, jnp.bfloat16),
-            pltpu.VMEM(shape, jnp.float32),
-        ],
-        in_specs=vmem_specs(8),
-        out_specs=vmem_specs(3),
+        near_kernel,
+        out_shape=[pltpu.VMEM(shape, jnp.bfloat16), pltpu.VMEM(shape, jnp.float32)],
+        in_specs=vmem_specs(5),
+        out_specs=vmem_specs(2),
         compiler_params=parameters(4),
-        name="remaining_sums",
-    )(passing, *[array for pair in pairs for array in pair], hidden)
+        name="near_sums",
+    )(*[array for pair in pairs for array in pair], hidden)
 
 
 def place_kernel(masks, *refs):
     group = lax.axis_index("dp")
-    pages, (cache_ref, sems) = refs[:-2], refs[-2:]
+    count = len(masks)
+    pages, (part_ref, base_ref) = refs[:count], refs[count : count + 2]
+    cache_ref, total_ref, sems = refs[count + 2 :]
     copies = [
         pltpu.make_async_copy(page_ref, cache_ref.at[0, group ^ mask], sems.at[number])
         for number, (mask, page_ref) in enumerate(zip(masks, pages))
     ]
     for copy in copies:
         copy.start()
+    total_ref[...] = base_ref[...] + part_ref[...].astype(jnp.float32)
     for copy in copies:
         copy.wait()
 
 
-def placed(masks, pages, replica_count):
+def placed(masks, pages, part, base, replica_count):
     count = len(pages)
     return pl.pallas_call(
         functools.partial(place_kernel, masks),
-        out_shape=jax.ShapeDtypeStruct((1, replica_count) + pages[0].shape, pages[0].dtype),
-        in_specs=[pl.BlockSpec(memory_space=pl.ANY)] * count,
-        out_specs=pl.BlockSpec(memory_space=pltpu.HBM),
+        out_shape=[
+            jax.ShapeDtypeStruct((1, replica_count) + pages[0].shape, pages[0].dtype),
+            pltpu.VMEM(base.shape, base.dtype),
+        ],
+        in_specs=[pl.BlockSpec(memory_space=pl.ANY)] * count + vmem_specs(2),
+        out_specs=[pl.BlockSpec(memory_space=pltpu.HBM)] + vmem_specs(1),
         scratch_shapes=[pltpu.SemaphoreType.DMA((count,))],
         compiler_params=parameters(4),
         name="placed",
-    )(*pages)
+    )(*pages, part, base)
 
 
 def finish_kernel(masks, base_ref, *refs):
@@ -849,21 +848,25 @@
 
     received = exchanged(sibling, "tensor", 1)
     partials = rest_rows(joined, tables[0], output, fed, fed_beside)
-    siblings, owns = partials[: CHIPS - 1], partials[CHIPS - 1 :]
+    siblings, owns = list(partials[: CHIPS - 1]), partials[CHIPS - 1 :]
     third_sum = added("third_added", own, received)
-    third_sum, siblings, joined = lax.optimization_barrier((third_sum, siblings, joined))
+    third_sum, siblings[2], joined = lax.optimization_barrier((third_sum, siblings[2], joined))
     passing = exchanged(third_sum, "tensor", to_chip[1])
     pairs = [(exchanged(sibling, "tensor", 1), own) for sibling, own in zip(siblings, owns)]
     pages = cached_pages(joined, destinations, replica_count)
     early, late = (3,), (1, 2)
     arriving = [exchanged(pages[mask], "dp", mask) for mask in early]
-    second_sum, first_sum, base = remaining_sums(passing, pairs, hidden)
+    first_sum, base = near_sums(pairs[:2], hidden)
+    from_first = exchanged(first_sum, "tensor", to_chip[1])
+    second_received, second_own = pairs[2]
+    second_sum = added("second_added", second_own, passing, second_received)
+    second_sum, late_pages = lax.optimization_barrier(
+        (second_sum, [pages[mask] for mask in late])
+    )
     from_second = exchanged(second_sum, "tensor", to_chip[2])
-    from_first = exchanged(first_sum, "tensor", to_chip[1])
-    base, late_pages = lax.optimization_barrier((base, [pages[mask] for mask in late]))
     late_pages = [exchanged(page, "dp", mask) for mask, page in zip(late, late_pages)]
-    cache_pages = placed((0,) + early, [pages[0]] + arriving, replica_count)
-    return tuple(finished(base, (from_second, from_first), late, late_pages, cache_pages))
+    cache_pages, base = placed((0,) + early, [pages[0]] + arriving, from_first, base, replica_count)
+    return tuple(finished(base, (from_second,), late, late_pages, cache_pages))
 
 
 def solution(mesh):

time: 39.7 us -> 38.7 us (0.975)
  starting transfers between devices: 18.7 us -> 18.1 us
  waiting for transfers between devices: 6.68 us -> 6.25 us
    ppermute x17, starting transfers between devices: 18.7 us -> 18.1 us  [exchanged(): lax.ppermute(block, axis, [(member, member ^ mask) for member in range(co...]
    ppermute x17, waiting for transfers between devices: 6.68 us -> 6.25 us  [exchanged(): lax.ppermute(block, axis, [(member, member ^ mask) for member in range(co...]
  transfers between devices with their start and end apart: 17 -> 17, of which waited for: 8 -> 6; matrix products, arithmetic and copies ran while one was open for 0% -> 0% of each run, Pallas kernels for 26% -> 27%
where the time goes in v13:
time: 38.7 us; the launch traced here: 38.5 us
  starting transfers between devices  18.1 us (47%)
  Pallas kernels  13.5 us (35%)
  waiting for transfers between devices  6.25 us (16%)
  between operations  0.72 us (2%)
    ppermute x17, starting transfers between devices, exchanged(): lax.ppermute(block, axis, [(member, member ^ mask) for member in range(co...  18.1 us
    ppermute x17, waiting for transfers between devices, exchanged(): lax.ppermute(block, axis, [(member, member ^ mask) for member in range(co...  6.25 us
    pallas_call x1, Pallas kernels, own_rows(): pl.pallas_call(functools.partial(own_kernel, count, replica_count), out_s...  5.27 us
    pallas_call x1, Pallas kernels, last_rows(): pl.pallas_call(last_kernel, out_shape=[pltpu.VMEM((tokens, 3 * HD), jnp.b...  2.41 us
    pallas_call x1, Pallas kernels, middle_rows(): pl.pallas_call(functools.partial(middle_kernel, origins), out_shape=[pltp...  2.12 us
    pallas_call x1, Pallas kernels, fed_rows(): pl.pallas_call(fed_kernel, out_shape=[pltpu.VMEM((rows, width), jnp.float...  0.9 us
    pallas_call x1, Pallas kernels, finished(): pl.pallas_call(functools.partial(finish_kernel, masks), out_shape=[jax.Sh...  0.83 us
    pallas_call x1, Pallas kernels, rest_rows(): pl.pallas_call(rest_kernel, out_shape=shapes, in_specs=vmem_specs(5), out...  0.79 us
  transfers between devices with their start and end apart: 17, of which 6 were waited for; matrix products, arithmetic and copies ran while one was open for 0% of the time, Pallas kernels for 27%

profile of v13, /device:TPU:0, one launch (start us, length us, event | category | flops | bytes accessed | tf_op | source)
XLA Modules:
  0.0 38.5 jit_solution(16666944482595883825)
XLA Ops:
  0.6 4.1 %collective-permute-start.1 = (bf16[32,2048]{1,0:T(8,128)(2,1)}, bf16[32,2048]{1,0:T(8,128)(2,1)S(1)}, u32[]{:S(2)}, u32[]{:S(2)}) collective-permute-start(bf16[32,2048]{1,0:T(8,128)(2,1)} %refs_2_.1), channel_id=1, source_target_pairs={{0,4},{1,5},{2,6},{3,7},{4,0},{5,1},{6,2},{7,3},{8,12},{9,13},{10,... | collective-permute-start | bytes 393224 | tf_op jit(solution)/shard_map/ppermute | solution.py:235
  4.7 1.6 %collective-permute-start = (bf16[32,2048]{1,0:T(8,128)(2,1)}, bf16[32,2048]{1,0:T(8,128)(2,1)S(1)}, u32[]{:S(2)}, u32[]{:S(2)}) collective-permute-start(bf16[32,2048]{1,0:T(8,128)(2,1)} %refs_2_.1), channel_id=1, source_target_pairs={{0,2},{1,3},{2,0},{3,1},{4,6},{5,7},{6,4},{7,5},{8,10},{9,11},{10,... | collective-permute-start | bytes 393224 | tf_op jit(solution)/shard_map/ppermute | solution.py:235
  6.3 5.3 %own_rows.1 = (s32[1,256]{1,0:T(1,128)}, s32[1,16]{1,0:T(1,128)}, bf16[32,2048]{1,0:T(8,128)(2,1)S(1)}, f32[1,2048]{1,0:T(1,128)S(1)}, f32[1,2048]{1,0:T(1,128)S...) custom-call(s32[1,256]{1,0:T(1,128)} %refs_0_.1, ...), custom_call_target="tpu_custom_call" | custom-call | flops 234881024 | bytes 11682880 | tf_op jit(solution)/shard_map/own_rows/pallas_call | solution.py:448
  11.6 0.0 collective-permute-done.1.refs_3_
  11.6 0.6 %collective-permute-start.4 = (bf16[32,2048]{1,0:T(8,128)(2,1)S(1)}, bf16[32,2048]{1,0:T(8,128)(2,1)S(1)}, u32[]{:S(2)}, u32[]{:S(2)}) collective-permute-start(bf16[32,2048]{1,0:T(8,128)(2,1)S(1)} %collective-permute-done.refs_1_), channel_id=1, source_target_pairs={{0,1},{1,0},{2,3},{3,2},{4,5},{5,4},{6,7},{7,6},{8,9},{9,8},{10,11... | collective-permute-start | bytes 393224 | tf_op jit(solution)/shard_map/ppermute | solution.py:235
  12.2 0.8 %collective-permute-start.2 = (bf16[32,2048]{1,0:T(8,128)(2,1)S(1)}, bf16[32,2048]{1,0:T(8,128)(2,1)S(1)}, u32[]{:S(2)}, u32[]{:S(2)}) collective-permute-start(bf16[32,2048]{1,0:T(8,128)(2,1)S(1)} %collective-permute-done.1.refs_3_), channel_id=1, source_target_pairs={{0,2},{1,3},{2,0},{3,1},{4,6},{5,7},{6,4},{7,5},{8,10},{9,11},{10,... | collective-permute-start | bytes 393224 | tf_op jit(solution)/shard_map/ppermute | solution.py:235
  13.0 0.2 collective-permute-done.4.refs_2_
  13.2 2.1 %middle_rows.1 = (bf16[128,768]{1,0:T(8,128)(2,1)S(1)}, bf16[128,1024]{1,0:T(8,128)(2,1)S(1)}, bf16[256,2048]{1,0:T(8,128)(2,1)S(1)}) custom-call(bf16[32,2048]{1,0:T(8,128)(2,1)S(1)} %collective-permute-done.3.refs_0_, bf16[32,2048]{1,0:T(8,128)(2,1)S(1)} %collective-permute-done.refs_1_, bf16[32,2048]{1,0:T(8,128)(2,1)S(1)} %collective-permute-done.4.refs_2_, ...), custom_call_target="tpu_custom_call" | custom-call | flops 939524096 | bytes 1048576 | tf_op jit(solution)/shard_map/middle_rows/pallas_call | solution.py:488
  15.3 0.4 %collective-permute-start.5 = (bf16[32,2048]{1,0:T(8,128)(2,1)S(1)}, bf16[32,2048]{1,0:T(8,128)(2,1)S(1)}, u32[]{:S(2)}, u32[]{:S(2)}) collective-permute-start(bf16[32,2048]{1,0:T(8,128)(2,1)S(1)} %collective-permute-done.1.refs_3_), channel_id=1, source_target_pairs={{0,1},{1,0},{2,3},{3,2},{4,5},{5,4},{6,7},{7,6},{8,9},{9,8},{10,11... | collective-permute-start | bytes 393224 | tf_op jit(solution)/shard_map/ppermute | solution.py:235
  15.7 1.9 %collective-permute-done.2.refs_1_ = bf16[32,2048]{1,0:T(8,128)(2,1)S(1)} collective-permute-done((bf16[32,2048]{1,0:T(8,128)(2,1)S(1)}, bf16[32,2048]{1,0:T(8,128)(2,1)S(1)}, u32[]{:S(2)}, u32[]{:S(2)}) %collective-permute-start.2) | collective-permute-done | bytes 131104 | tf_op jit(solution)/shard_map/ppermute | solution.py:235
  17.7 0.0 collective-permute-done.5.refs_0_
  17.7 0.9 %fed_rows.1 = (f32[160,2048]{1,0:T(8,128)S(1)}, bf16[64,2048]{1,0:T(8,128)(2,1)S(1)}, bf16[64,2048]{1,0:T(8,128)(2,1)S(1)}) custom-call(bf16[32,1024]{1,0:T(8,128)(2,1)S(1)} %get-tuple-element.69.own_hidden_ref, bf16[128,1024]{1,0:T(8,128)(2,1)S(1)} %get-tuple-element.70.middle_hidden_ref, bf16[1024,2048]{1,0:T(8,128)(2,1)S(1)} %get-tuple-element.71.downward_ref.refs_7_, ...), custom_call_target="tpu_custom_call" | custom-call | flops 671088640 | bytes 1048576 | tf_op jit(solution)/shard_map/fed_rows/pallas_call | solution.py:593
  18.6 0.4 %collective-permute-done.6.refs_0_ = bf16[32,2048]{1,0:T(8,128)(2,1)S(1)} collective-permute-done((bf16[32,2048]{1,0:T(8,128)(2,1)S(1)}, bf16[32,2048]{1,0:T(8,128)(2,1)S(1)}, u32[]{:S(2)}, u32[]{:S(2)}) %collective-permute-start.6) | collective-permute-done | bytes 131104 | tf_op jit(solution)/shard_map/ppermute | solution.py:235
  19.0 2.4 %last_rows.1 = (bf16[256,768]{1,0:T(8,128)(2,1)S(1)}, f32[32,2048]{1,0:T(8,128)S(1)}, bf16[32,2048]{1,0:T(8,128)(2,1)S(1)}, f32[32,2048]{1,0:T(8,128)S(1)}) custom-call(bf16[32,2048]{1,0:T(8,128)(2,1)S(1)} %collective-permute-done.6.refs_0_, bf16[64,2048]{1,0:T(8,128)(2,1)S(1)} %get-tuple-element.73.refs_1_, bf16[64,2048]{1,0:T(8,128)(2,1)S(1)} %get-tuple-element.74.refs_2_, ...), custom_call_target="tpu_custom_call" | custom-call | flops 1207959552 | bytes 1048576 | tf_op jit(solution)/shard_map/last_rows/pallas_call | solution.py:552
  21.4 0.2 collective-permute-start.7
  21.6 0.8 %rest_rows.1 = (bf16[32,2048]{1,0:T(8,128)(2,1)S(1)}, bf16[32,2048]{1,0:T(8,128)(2,1)S(1)}, bf16[32,2048]{1,0:T(8,128)(2,1)S(1)}, f32[32,2048]{1,0:T(8,128)S(1)}...) custom-call(bf16[256,768]{1,0:T(8,128)(2,1)S(1)} %get-tuple-element.85.joined_ref, ...), custom_call_target="tpu_custom_call" | custom-call | flops 201326592 | bytes 1048576 | tf_op jit(solution)/shard_map/rest_rows/pallas_call | solution.py:632
  22.4 0.4 %collective-permute-start.9 = (bf16[32,2048]{1,0:T(8,128)(2,1)S(1)}, bf16[32,2048]{1,0:T(8,128)(2,1)S(1)}, u32[]{:S(2)}, u32[]{:S(2)}) collective-permute-start(bf16[32,2048]{1,0:T(8,128)(2,1)S(1)} %get-tuple-element.89), channel_id=1, source_target_pairs={{0,1},{1,0},{2,3},{3,2},{4,5},{5,4},{6,7},{7,6},{8,9},{9,8},{10,11... | collective-permute-start | bytes 393224 | tf_op jit(solution)/shard_map/ppermute | solution.py:235
  22.9 0.1 collective-permute-start.10
  23.0 1.3 %collective-permute-start.12 = (bf16[32,2048]{1,0:T(8,128)(2,1)S(1)}, bf16[32,2048]{1,0:T(8,128)(2,1)S(1)}, u32[]{:S(2)}, u32[]{:S(2)}) collective-permute-start(bf16[32,2048]{1,0:T(8,128)(2,1)S(1)} %third_added.1), channel_id=1, source_target_pairs={{0,2},{1,3},{2,0},{3,1},{4,6},{5,7},{6,4},{7,5},{8,10},{9,11},{10,... | collective-permute-start | bytes 393224 | tf_op jit(solution)/shard_map/ppermute | solution.py:235
  24.4 0.1 collective-permute-start.13
  24.4 0.3 cached_pages.1
  24.7 2.5 %collective-permute-start.8 = (bf16[8,16,512]{2,1,0:T(8,128)(2,1)S(1)}, bf16[8,16,512]{2,1,0:T(8,128)(2,1)S(1)}, u32[]{:S(2)}, u32[]{:S(2)}) collective-permute-start(bf16[8,16,512]{2,1,0:T(8,128)(2,1)S(1)} %get-tuple-element.88), channel_id=1, source_target_pairs={{0,24},{8,16},{16,8},{24,0},{1,25},{9,17},{17,9},{25,1},{2,26},{10... | collective-permute-start | bytes 393224 | tf_op jit(solution)/shard_map/ppermute | solution.py:235
  27.3 0.1 near_sums.1
  27.3 0.9 %collective-permute-start.11 = (bf16[32,2048]{1,0:T(8,128)(2,1)S(1)}, bf16[32,2048]{1,0:T(8,128)(2,1)S(1)}, u32[]{:S(2)}, u32[]{:S(2)}) collective-permute-start(bf16[32,2048]{1,0:T(8,128)(2,1)S(1)} %get-tuple-element.94), channel_id=1, source_target_pairs={{0,2},{1,3},{2,0},{3,1},{4,6},{5,7},{6,4},{7,5},{8,10},{9,11},{10,... | collective-permute-start | bytes 393224 | tf_op jit(solution)/shard_map/ppermute | solution.py:235
  28.2 0.7 %collective-permute-done.12.refs_1_ = bf16[32,2048]{1,0:T(8,128)(2,1)S(1)} collective-permute-done((bf16[32,2048]{1,0:T(8,128)(2,1)S(1)}, bf16[32,2048]{1,0:T(8,128)(2,1)S(1)}, u32[]{:S(2)}, u32[]{:S(2)}) %collective-permute-start.12) | collective-permute-done | bytes 131104 | tf_op jit(solution)/shard_map/ppermute | solution.py:235
  28.9 1.9 %collective-permute-start.14 = (bf16[32,2048]{1,0:T(8,128)(2,1)S(1)}, bf16[32,2048]{1,0:T(8,128)(2,1)S(1)}, u32[]{:S(2)}, u32[]{:S(2)}) collective-permute-start(bf16[32,2048]{1,0:T(8,128)(2,1)S(1)} %second_added.1), channel_id=1, source_target_pairs={{0,4},{1,5},{2,6},{3,7},{4,0},{5,1},{6,2},{7,3},{8,12},{9,13},{10,... | collective-permute-start | bytes 393224 | tf_op jit(solution)/shard_map/ppermute | solution.py:235
  30.8 1.5 %collective-permute-start.15 = (bf16[8,16,512]{2,1,0:T(8,128)(2,1)S(1)}, bf16[8,16,512]{2,1,0:T(8,128)(2,1)S(1)}, u32[]{:S(2)}, u32[]{:S(2)}) collective-permute-start(bf16[8,16,512]{2,1,0:T(8,128)(2,1)S(1)} %get-tuple-element.103), channel_id=1, source_target_pairs={{0,8},{8,0},{16,24},{24,16},{1,9},{9,1},{17,25},{25,17},{2,10},{10... | collective-permute-start | bytes 393224 | tf_op jit(solution)/shard_map/ppermute | solution.py:235
  32.3 1.6 %collective-permute-start.16 = (bf16[8,16,512]{2,1,0:T(8,128)(2,1)S(1)}, bf16[8,16,512]{2,1,0:T(8,128)(2,1)S(1)}, u32[]{:S(2)}, u32[]{:S(2)}) collective-permute-start(bf16[8,16,512]{2,1,0:T(8,128)(2,1)S(1)} %get-tuple-element.104), channel_id=1, source_target_pairs={{0,16},{8,24},{16,0},{24,8},{1,17},{9,25},{17,1},{25,9},{2,18},{10... | collective-permute-start | bytes 393224 | tf_op jit(solution)/shard_map/ppermute | solution.py:235
  34.0 1.8 %collective-permute-done.11.refs_2_ = bf16[32,2048]{1,0:T(8,128)(2,1)S(1)} collective-permute-done((bf16[32,2048]{1,0:T(8,128)(2,1)S(1)}, bf16[32,2048]{1,0:T(8,128)(2,1)S(1)}, u32[]{:S(2)}, u32[]{:S(2)}) %collective-permute-start.11) | collective-permute-done | bytes 131104 | tf_op jit(solution)/shard_map/ppermute | solution.py:235
  35.7 0.7 %placed.1 = (bf16[1,4,8,16,512]{4,3,2,1,0:T(8,128)(2,1)}, f32[32,2048]{1,0:T(8,128)S(1)}) custom-call(bf16[8,16,512]{2,1,0:T(8,128)(2,1)S(1)} %get-tuple-element.87.refs_0_, bf16[8,16,512]{2,1,0:T(8,128)(2,1)S(1)} %collective-permute-done.8.refs_1_, bf16[32,2048]{1,0:T(8,128)(2,1)S(1)} %collective-permute-done.11.refs_2_, ...), custom_call_target="tpu_custom_call" | custom-call | tf_op jit(solution)/shard_map/placed/pallas_call | solution.py:732
  36.5 1.2 %collective-permute-done.14.refs_0_ = bf16[32,2048]{1,0:T(8,128)(2,1)S(1)} collective-permute-done((bf16[32,2048]{1,0:T(8,128)(2,1)S(1)}, bf16[32,2048]{1,0:T(8,128)(2,1)S(1)}, u32[]{:S(2)}, u32[]{:S(2)}) %collective-permute-start.14) | collective-permute-done | bytes 131104 | tf_op jit(solution)/shard_map/ppermute | solution.py:235
  37.7 0.8 %finished.1 = (f32[32,2048]{1,0:T(8,128)}, bf16[1,4,8,16,512]{4,3,2,1,0:T(8,128)(2,1)}) custom-call(f32[32,2048]{1,0:T(8,128)S(1)} %get-tuple-element.96.base_ref, bf16[32,2048]{1,0:T(8,128)(2,1)S(1)} %collective-permute-done.14.refs_0_, bf16[8,16,512]{2,1,0:T(8,128)(2,1)S(1)} %collective-permute-done.15.refs_1_, ...), custom_call_target="tpu_custom_call", output_to_operand_aliasing={{1}: (4, {})} | custom-call | tf_op jit(solution)/shard_map/finished/pallas_call | solution.py:769
  (13 shorter events, 0.1 us)
Async XLA Ops:
  0.6 11.0 %collective-permute-start.1 = (bf16[32,2048]{1,0:T(8,128)(2,1)}, bf16[32,2048]{1,0:T(8,128)(2,1)S(1)}, u32[]{:S(2)}, u32[]{:S(2)}) collective-permute-start(bf16[32,2048]{1,0:T(8,128)(2,1)} %refs_2_.1), channel_id=1, source_target_pairs={{0,4},{1,5},{2,6},{3,7},{4,0},{5,1},{6,2},{7,3},{8,12},{9,13},{10,... | collective-permute-start | bytes 393224 | tf_op jit(solution)/shard_map/ppermute | solution.py:235
  4.7 6.9 %collective-permute-start = (bf16[32,2048]{1,0:T(8,128)(2,1)}, bf16[32,2048]{1,0:T(8,128)(2,1)S(1)}, u32[]{:S(2)}, u32[]{:S(2)}) collective-permute-start(bf16[32,2048]{1,0:T(8,128)(2,1)} %refs_2_.1), channel_id=1, source_target_pairs={{0,2},{1,3},{2,0},{3,1},{4,6},{5,7},{6,4},{7,5},{8,10},{9,11},{10,... | collective-permute-start | bytes 393224 | tf_op jit(solution)/shard_map/ppermute | solution.py:235
  6.3 6.7 %collective-permute-start.3 = (bf16[32,2048]{1,0:T(8,128)(2,1)}, bf16[32,2048]{1,0:T(8,128)(2,1)S(1)}, u32[]{:S(2)}, u32[]{:S(2)}) collective-permute-start(bf16[32,2048]{1,0:T(8,128)(2,1)} %refs_2_.1), channel_id=1, source_target_pairs={{0,1},{1,0},{2,3},{3,2},{4,5},{5,4},{6,7},{7,6},{8,9},{9,8},{10,11... | collective-permute-start | bytes 393224 | tf_op jit(solution)/shard_map/ppermute | solution.py:235
  11.6 1.6 %collective-permute-start.4 = (bf16[32,2048]{1,0:T(8,128)(2,1)S(1)}, bf16[32,2048]{1,0:T(8,128)(2,1)S(1)}, u32[]{:S(2)}, u32[]{:S(2)}) collective-permute-start(bf16[32,2048]{1,0:T(8,128)(2,1)S(1)} %collective-permute-done.refs_1_), channel_id=1, source_target_pairs={{0,1},{1,0},{2,3},{3,2},{4,5},{5,4},{6,7},{7,6},{8,9},{9,8},{10,11... | collective-permute-start | bytes 393224 | tf_op jit(solution)/shard_map/ppermute | solution.py:235
  12.2 5.5 %collective-permute-start.2 = (bf16[32,2048]{1,0:T(8,128)(2,1)S(1)}, bf16[32,2048]{1,0:T(8,128)(2,1)S(1)}, u32[]{:S(2)}, u32[]{:S(2)}) collective-permute-start(bf16[32,2048]{1,0:T(8,128)(2,1)S(1)} %collective-permute-done.1.refs_3_), channel_id=1, source_target_pairs={{0,2},{1,3},{2,0},{3,1},{4,6},{5,7},{6,4},{7,5},{8,10},{9,11},{10,... | collective-permute-start | bytes 393224 | tf_op jit(solution)/shard_map/ppermute | solution.py:235
  15.3 2.4 %collective-permute-start.5 = (bf16[32,2048]{1,0:T(8,128)(2,1)S(1)}, bf16[32,2048]{1,0:T(8,128)(2,1)S(1)}, u32[]{:S(2)}, u32[]{:S(2)}) collective-permute-start(bf16[32,2048]{1,0:T(8,128)(2,1)S(1)} %collective-permute-done.1.refs_3_), channel_id=1, source_target_pairs={{0,1},{1,0},{2,3},{3,2},{4,5},{5,4},{6,7},{7,6},{8,9},{9,8},{10,11... | collective-permute-start | bytes 393224 | tf_op jit(solution)/shard_map/ppermute | solution.py:235
  17.7 1.3 %collective-permute-start.6 = (bf16[32,2048]{1,0:T(8,128)(2,1)S(1)}, bf16[32,2048]{1,0:T(8,128)(2,1)S(1)}, u32[]{:S(2)}, u32[]{:S(2)}) collective-permute-start(bf16[32,2048]{1,0:T(8,128)(2,1)S(1)} %collective-permute-done.2.refs_1_), channel_id=1, source_target_pairs={{0,1},{1,0},{2,3},{3,2},{4,5},{5,4},{6,7},{7,6},{8,9},{9,8},{10,11... | collective-permute-start | bytes 393224 | tf_op jit(solution)/shard_map/ppermute | solution.py:235
  21.4 1.6 %collective-permute-start.7 = (bf16[32,2048]{1,0:T(8,128)(2,1)S(1)}, bf16[32,2048]{1,0:T(8,128)(2,1)S(1)}, u32[]{:S(2)}, u32[]{:S(2)}) collective-permute-start(bf16[32,2048]{1,0:T(8,128)(2,1)S(1)} %get-tuple-element.80), channel_id=1, source_target_pairs={{0,1},{1,0},{2,3},{3,2},{4,5},{5,4},{6,7},{7,6},{8,9},{9,8},{10,11... | collective-permute-start | bytes 393224 | tf_op jit(solution)/shard_map/ppermute | solution.py:235
  22.4 4.8 %collective-permute-start.9 = (bf16[32,2048]{1,0:T(8,128)(2,1)S(1)}, bf16[32,2048]{1,0:T(8,128)(2,1)S(1)}, u32[]{:S(2)}, u32[]{:S(2)}) collective-permute-start(bf16[32,2048]{1,0:T(8,128)(2,1)S(1)} %get-tuple-element.89), channel_id=1, source_target_pairs={{0,1},{1,0},{2,3},{3,2},{4,5},{5,4},{6,7},{7,6},{8,9},{9,8},{10,11... | collective-permute-start | bytes 393224 | tf_op jit(solution)/shard_map/ppermute | solution.py:235
  22.9 4.4 %collective-permute-start.10 = (bf16[32,2048]{1,0:T(8,128)(2,1)S(1)}, bf16[32,2048]{1,0:T(8,128)(2,1)S(1)}, u32[]{:S(2)}, u32[]{:S(2)}) collective-permute-start(bf16[32,2048]{1,0:T(8,128)(2,1)S(1)} %get-tuple-element.91), channel_id=1, source_target_pairs={{0,1},{1,0},{2,3},{3,2},{4,5},{5,4},{6,7},{7,6},{8,9},{9,8},{10,11... | collective-permute-start | bytes 393224 | tf_op jit(solution)/shard_map/ppermute | solution.py:235
  23.0 5.8 %collective-permute-start.12 = (bf16[32,2048]{1,0:T(8,128)(2,1)S(1)}, bf16[32,2048]{1,0:T(8,128)(2,1)S(1)}, u32[]{:S(2)}, u32[]{:S(2)}) collective-permute-start(bf16[32,2048]{1,0:T(8,128)(2,1)S(1)} %third_added.1), channel_id=1, source_target_pairs={{0,2},{1,3},{2,0},{3,1},{4,6},{5,7},{6,4},{7,5},{8,10},{9,11},{10,... | collective-permute-start | bytes 393224 | tf_op jit(solution)/shard_map/ppermute | solution.py:235
  24.4 4.5 %collective-permute-start.13 = (bf16[32,2048]{1,0:T(8,128)(2,1)S(1)}, bf16[32,2048]{1,0:T(8,128)(2,1)S(1)}, u32[]{:S(2)}, u32[]{:S(2)}) collective-permute-start(bf16[32,2048]{1,0:T(8,128)(2,1)S(1)} %get-tuple-element.99), channel_id=1, source_target_pairs={{0,1},{1,0},{2,3},{3,2},{4,5},{5,4},{6,7},{7,6},{8,9},{9,8},{10,11... | collective-permute-start | bytes 393224 | tf_op jit(solution)/shard_map/ppermute | solution.py:235
  24.7 9.2 %collective-permute-start.8 = (bf16[8,16,512]{2,1,0:T(8,128)(2,1)S(1)}, bf16[8,16,512]{2,1,0:T(8,128)(2,1)S(1)}, u32[]{:S(2)}, u32[]{:S(2)}) collective-permute-start(bf16[8,16,512]{2,1,0:T(8,128)(2,1)S(1)} %get-tuple-element.88), channel_id=1, source_target_pairs={{0,24},{8,16},{16,8},{24,0},{1,25},{9,17},{17,9},{25,1},{2,26},{10... | collective-permute-start | bytes 393224 | tf_op jit(solution)/shard_map/ppermute | solution.py:235
  27.3 8.4 %collective-permute-start.11 = (bf16[32,2048]{1,0:T(8,128)(2,1)S(1)}, bf16[32,2048]{1,0:T(8,128)(2,1)S(1)}, u32[]{:S(2)}, u32[]{:S(2)}) collective-permute-start(bf16[32,2048]{1,0:T(8,128)(2,1)S(1)} %get-tuple-element.94), channel_id=1, source_target_pairs={{0,2},{1,3},{2,0},{3,1},{4,6},{5,7},{6,4},{7,5},{8,10},{9,11},{10,... | collective-permute-start | bytes 393224 | tf_op jit(solution)/shard_map/ppermute | solution.py:235
  28.9 8.8 %collective-permute-start.14 = (bf16[32,2048]{1,0:T(8,128)(2,1)S(1)}, bf16[32,2048]{1,0:T(8,128)(2,1)S(1)}, u32[]{:S(2)}, u32[]{:S(2)}) collective-permute-start(bf16[32,2048]{1,0:T(8,128)(2,1)S(1)} %second_added.1), channel_id=1, source_target_pairs={{0,4},{1,5},{2,6},{3,7},{4,0},{5,1},{6,2},{7,3},{8,12},{9,13},{10,... | collective-permute-start | bytes 393224 | tf_op jit(solution)/shard_map/ppermute | solution.py:235
  30.8 6.9 %collective-permute-start.15 = (bf16[8,16,512]{2,1,0:T(8,128)(2,1)S(1)}, bf16[8,16,512]{2,1,0:T(8,128)(2,1)S(1)}, u32[]{:S(2)}, u32[]{:S(2)}) collective-permute-start(bf16[8,16,512]{2,1,0:T(8,128)(2,1)S(1)} %get-tuple-element.103), channel_id=1, source_target_pairs={{0,8},{8,0},{16,24},{24,16},{1,9},{9,1},{17,25},{25,17},{2,10},{10... | collective-permute-start | bytes 393224 | tf_op jit(solution)/shard_map/ppermute | solution.py:235
  32.3 5.4 %collective-permute-start.16 = (bf16[8,16,512]{2,1,0:T(8,128)(2,1)S(1)}, bf16[8,16,512]{2,1,0:T(8,128)(2,1)S(1)}, u32[]{:S(2)}, u32[]{:S(2)}) collective-permute-start(bf16[8,16,512]{2,1,0:T(8,128)(2,1)S(1)} %get-tuple-element.104), channel_id=1, source_target_pairs={{0,16},{8,24},{16,0},{24,8},{1,17},{9,25},{17,1},{25,9},{2,18},{10... | collective-permute-start | bytes 393224 | tf_op jit(solution)/shard_map/ppermute | solution.py:235

commit v14 on v13

--- a/solution.py
+++ b/solution.py
@@ -604,9 +604,8 @@
 
 
 def rest_kernel(joined_ref, offsets_ref, output_ref, fed_ref, fed_beside_ref, *refs):
-    count = len(refs) // 2
-    siblings, owns = refs[:count], refs[count:]
-    block_rows = owns[0].shape[0]
+    near_ref, far_ref, *owns = refs
+    block_rows = far_ref.shape[0]
     rows = fed_ref.shape[0] + fed_beside_ref.shape[0]
     attended = attend(joined_ref, offsets_ref, 0, rows, block_rows)
     chunk = 512
@@ -616,11 +615,15 @@
         partial = fed + jnp.dot(
             attended, output_ref[:, columns], preferred_element_type=jnp.float32
         )
-        for number, (sibling_ref, own_ref) in enumerate(zip(siblings, owns)):
+        for number, own_ref in enumerate(owns):
             first = CORES * number * block_rows
             middle = first + block_rows
             own_ref[:, columns] = partial[first:middle]
-            sibling_ref[:, columns] = partial[middle : middle + block_rows].astype(jnp.bfloat16)
+            sibling = partial[middle : middle + block_rows].astype(jnp.bfloat16)
+            if number < near_ref.shape[0]:
+                near_ref[number, :, columns] = sibling
+            else:
+                far_ref[:, columns] = sibling
 
 
 def rest_rows(joined, offsets, output_weight, fed, fed_beside):
@@ -628,12 +631,13 @@
     rows = fed.shape[0] + fed_beside.shape[0]
     count = CHIPS - 1
     shape = (rows // (CORES * count), width)
-    shapes = [pltpu.VMEM(shape, dtype) for dtype in [jnp.bfloat16] * count + [jnp.float32] * count]
+    shapes = [pltpu.VMEM((count - 1, *shape), jnp.bfloat16), pltpu.VMEM(shape, jnp.bfloat16)]
+    shapes += [pltpu.VMEM(shape, jnp.float32)] * count
     return pl.pallas_call(
         rest_kernel,
         out_shape=shapes,
         in_specs=vmem_specs(5),
-        out_specs=vmem_specs(2 * count),
+        out_specs=vmem_specs(2 + count),
         compiler_params=parameters(12),
         cost_estimate=pl.CostEstimate(
             flops=2 * rows * width * HD,
@@ -688,27 +692,22 @@
     )(*parts)
 
 
-def near_kernel(*refs):
-    zeros, ones, hidden_ref, first_ref, base_ref = refs[0:2], refs[2:4], *refs[4:]
-
-    def total(pair):
-        received_ref, own_ref = pair
-        return own_ref[...] + received_ref[...].astype(jnp.float32)
-
-    first_ref[...] = total(ones).astype(jnp.bfloat16)
-    base_ref[...] = total(zeros) + hidden_ref[...].astype(jnp.float32)
-
-
-def near_sums(pairs, hidden):
+def near_kernel(received_ref, zero_ref, one_ref, hidden_ref, first_ref, base_ref):
+    first_ref[...] = (one_ref[...] + received_ref[1].astype(jnp.float32)).astype(jnp.bfloat16)
+    zero = zero_ref[...] + received_ref[0].astype(jnp.float32)
+    base_ref[...] = zero + hidden_ref[...].astype(jnp.float32)
+
+
+def near_sums(received, owns, hidden):
     shape = hidden.shape
     return pl.pallas_call(
         near_kernel,
         out_shape=[pltpu.VMEM(shape, jnp.bfloat16), pltpu.VMEM(shape, jnp.float32)],
-        in_specs=vmem_specs(5),
+        in_specs=vmem_specs(4),
         out_specs=vmem_specs(2),
         compiler_params=parameters(4),
         name="near_sums",
-    )(*[array for pair in pairs for array in pair], hidden)
+    )(received, *owns, hidden)
 
 
 def place_kernel(masks, *refs):
@@ -754,12 +753,18 @@
     ]
     for copy in copies:
         copy.start()
-    total = base_ref[...]
-    for part_ref in parts:
-        total = total + part_ref[...].astype(jnp.float32)
-    total_scr[...] = total
-    copies.append(pltpu.make_async_copy(total_scr, output_ref, sems.at[count]))
-    copies[-1].start()
+    rows = 8
+    for first in range(0, base_ref.shape[0], 2 * rows):
+        both = slice(first, first + 2 * rows)
+        total = base_ref[both, :]
+        for part_ref in parts:
+            total = total + part_ref[both, :].astype(jnp.float32)
+        total_scr[both, :] = total
+        for place in (first, first + rows):
+            piece = pl.ds(place, rows)
+            sem = sems.at[count + place // rows]
+            copies.append(pltpu.make_async_copy(total_scr.at[piece], output_ref.at[piece], sem))
+            copies[-1].start()
     for copy in copies:
         copy.wait()
 
@@ -778,7 +783,7 @@
         out_specs=[pl.BlockSpec(memory_space=pltpu.HBM)] * 2,
         scratch_shapes=[
             pltpu.VMEM(base.shape, base.dtype),
-            pltpu.SemaphoreType.DMA((count + 1,)),
+            pltpu.SemaphoreType.DMA((count + base.shape[0] // 8,)),
         ],
         input_output_aliases={1 + len(parts) + count: 1},
         compiler_params=parameters(4),
@@ -848,18 +853,18 @@
 
     received = exchanged(sibling, "tensor", 1)
     partials = rest_rows(joined, tables[0], output, fed, fed_beside)
-    siblings, owns = list(partials[: CHIPS - 1]), partials[CHIPS - 1 :]
+    near_sibling, far_sibling, *owns = partials
+    near_received = exchanged(near_sibling, "tensor", 1)
     third_sum = added("third_added", own, received)
-    third_sum, siblings[2], joined = lax.optimization_barrier((third_sum, siblings[2], joined))
+    third_sum, far_sibling, joined = lax.optimization_barrier((third_sum, far_sibling, joined))
     passing = exchanged(third_sum, "tensor", to_chip[1])
-    pairs = [(exchanged(sibling, "tensor", 1), own) for sibling, own in zip(siblings, owns)]
+    far_received = exchanged(far_sibling, "tensor", 1)
     pages = cached_pages(joined, destinations, replica_count)
     early, late = (3,), (1, 2)
     arriving = [exchanged(pages[mask], "dp", mask) for mask in early]
-    first_sum, base = near_sums(pairs[:2], hidden)
+    first_sum, base = near_sums(near_received, owns[:2], hidden)
     from_first = exchanged(first_sum, "tensor", to_chip[1])
-    second_received, second_own = pairs[2]
-    second_sum = added("second_added", second_own, passing, second_received)
+    second_sum = added("second_added", owns[2], passing, far_received)
     second_sum, late_pages = lax.optimization_barrier(
         (second_sum, [pages[mask] for mask in late])
     )

time: 38.7 us -> 37.9 us (0.979)
  waiting for transfers between devices: 6.25 us -> 5.77 us
    ppermute x17 -> x16, waiting for transfers between devices: 6.25 us -> 5.77 us  [exchanged(): lax.ppermute(block, axis, [(member, member ^ mask) for member in range(co...]
    ppermute x17 -> x16, starting transfers between devices: 18.1 us -> 17.8 us  [exchanged(): lax.ppermute(block, axis, [(member, member ^ mask) for member in range(co...]
  transfers between devices with their start and end apart: 17 -> 16, of which waited for: 6 -> 6; matrix products, arithmetic and copies ran while one was open for 0% -> 0% of each run, Pallas kernels for 27% -> 27%
where the time goes in v14:
time: 37.9 us; the launch traced here: 37.8 us
  starting transfers between devices  17.8 us (47%)
  Pallas kernels  13.5 us (36%)
  waiting for transfers between devices  5.77 us (15%)
  between operations  0.73 us (2%)
    ppermute x16, starting transfers between devices, exchanged(): lax.ppermute(block, axis, [(member, member ^ mask) for member in range(co...  17.8 us
    ppermute x16, waiting for transfers between devices, exchanged(): lax.ppermute(block, axis, [(member, member ^ mask) for member in range(co...  5.77 us
    pallas_call x1, Pallas kernels, own_rows(): pl.pallas_call(functools.partial(own_kernel, count, replica_count), out_s...  5.27 us
    pallas_call x1, Pallas kernels, last_rows(): pl.pallas_call(last_kernel, out_shape=[pltpu.VMEM((tokens, 3 * HD), jnp.b...  2.41 us
    pallas_call x1, Pallas kernels, middle_rows(): pl.pallas_call(functools.partial(middle_kernel, origins), out_shape=[pltp...  2.12 us
    pallas_call x1, Pallas kernels, fed_rows(): pl.pallas_call(fed_kernel, out_shape=[pltpu.VMEM((rows, width), jnp.float...  0.9 us
    pallas_call x1, Pallas kernels, finished(): pl.pallas_call(functools.partial(finish_kernel, masks), out_shape=[jax.Sh...  0.84 us
    pallas_call x1, Pallas kernels, rest_rows(): pl.pallas_call(rest_kernel, out_shape=shapes, in_specs=vmem_specs(5), out...  0.79 us
  transfers between devices with their start and end apart: 16, of which 6 were waited for; matrix products, arithmetic and copies ran while one was open for 0% of the time, Pallas kernels for 27%

profile of v14, /device:TPU:0, one launch (start us, length us, event | category | flops | bytes accessed | tf_op | source)
XLA Modules:
  0.0 37.8 jit_solution(12490695176572365035)
XLA Ops:
  0.6 4.1 %collective-permute-start.1 = (bf16[32,2048]{1,0:T(8,128)(2,1)}, bf16[32,2048]{1,0:T(8,128)(2,1)S(1)}, u32[]{:S(2)}, u32[]{:S(2)}) collective-permute-start(bf16[32,2048]{1,0:T(8,128)(2,1)} %refs_2_.1), channel_id=1, source_target_pairs={{0,4},{1,5},{2,6},{3,7},{4,0},{5,1},{6,2},{7,3},{8,12},{9,13},{10,... | collective-permute-start | bytes 393224 | tf_op jit(solution)/shard_map/ppermute | solution.py:235
  4.7 1.6 %collective-permute-start = (bf16[32,2048]{1,0:T(8,128)(2,1)}, bf16[32,2048]{1,0:T(8,128)(2,1)S(1)}, u32[]{:S(2)}, u32[]{:S(2)}) collective-permute-start(bf16[32,2048]{1,0:T(8,128)(2,1)} %refs_2_.1), channel_id=1, source_target_pairs={{0,2},{1,3},{2,0},{3,1},{4,6},{5,7},{6,4},{7,5},{8,10},{9,11},{10,... | collective-permute-start | bytes 393224 | tf_op jit(solution)/shard_map/ppermute | solution.py:235
  6.3 5.3 %own_rows.1 = (s32[1,256]{1,0:T(1,128)}, s32[1,16]{1,0:T(1,128)}, bf16[32,2048]{1,0:T(8,128)(2,1)S(1)}, f32[1,2048]{1,0:T(1,128)S(1)}, f32[1,2048]{1,0:T(1,128)S...) custom-call(s32[1,256]{1,0:T(1,128)} %refs_0_.1, ...), custom_call_target="tpu_custom_call" | custom-call | flops 234881024 | bytes 11682880 | tf_op jit(solution)/shard_map/own_rows/pallas_call | solution.py:448
  11.6 0.0 collective-permute-done.1.refs_3_
  11.6 0.6 %collective-permute-start.4 = (bf16[32,2048]{1,0:T(8,128)(2,1)S(1)}, bf16[32,2048]{1,0:T(8,128)(2,1)S(1)}, u32[]{:S(2)}, u32[]{:S(2)}) collective-permute-start(bf16[32,2048]{1,0:T(8,128)(2,1)S(1)} %collective-permute-done.refs_1_), channel_id=1, source_target_pairs={{0,1},{1,0},{2,3},{3,2},{4,5},{5,4},{6,7},{7,6},{8,9},{9,8},{10,11... | collective-permute-start | bytes 393224 | tf_op jit(solution)/shard_map/ppermute | solution.py:235
  12.2 0.8 %collective-permute-start.2 = (bf16[32,2048]{1,0:T(8,128)(2,1)S(1)}, bf16[32,2048]{1,0:T(8,128)(2,1)S(1)}, u32[]{:S(2)}, u32[]{:S(2)}) collective-permute-start(bf16[32,2048]{1,0:T(8,128)(2,1)S(1)} %collective-permute-done.1.refs_3_), channel_id=1, source_target_pairs={{0,2},{1,3},{2,0},{3,1},{4,6},{5,7},{6,4},{7,5},{8,10},{9,11},{10,... | collective-permute-start | bytes 393224 | tf_op jit(solution)/shard_map/ppermute | solution.py:235
  13.0 0.2 collective-permute-done.4.refs_2_
  13.2 2.1 %middle_rows.1 = (bf16[128,768]{1,0:T(8,128)(2,1)S(1)}, bf16[128,1024]{1,0:T(8,128)(2,1)S(1)}, bf16[256,2048]{1,0:T(8,128)(2,1)S(1)}) custom-call(bf16[32,2048]{1,0:T(8,128)(2,1)S(1)} %collective-permute-done.3.refs_0_, bf16[32,2048]{1,0:T(8,128)(2,1)S(1)} %collective-permute-done.refs_1_, bf16[32,2048]{1,0:T(8,128)(2,1)S(1)} %collective-permute-done.4.refs_2_, ...), custom_call_target="tpu_custom_call" | custom-call | flops 939524096 | bytes 1048576 | tf_op jit(solution)/shard_map/middle_rows/pallas_call | solution.py:488
  15.3 0.4 %collective-permute-start.5 = (bf16[32,2048]{1,0:T(8,128)(2,1)S(1)}, bf16[32,2048]{1,0:T(8,128)(2,1)S(1)}, u32[]{:S(2)}, u32[]{:S(2)}) collective-permute-start(bf16[32,2048]{1,0:T(8,128)(2,1)S(1)} %collective-permute-done.1.refs_3_), channel_id=1, source_target_pairs={{0,1},{1,0},{2,3},{3,2},{4,5},{5,4},{6,7},{7,6},{8,9},{9,8},{10,11... | collective-permute-start | bytes 393224 | tf_op jit(solution)/shard_map/ppermute | solution.py:235
  15.7 1.9 %collective-permute-done.2.refs_1_ = bf16[32,2048]{1,0:T(8,128)(2,1)S(1)} collective-permute-done((bf16[32,2048]{1,0:T(8,128)(2,1)S(1)}, bf16[32,2048]{1,0:T(8,128)(2,1)S(1)}, u32[]{:S(2)}, u32[]{:S(2)}) %collective-permute-start.2) | collective-permute-done | bytes 131104 | tf_op jit(solution)/shard_map/ppermute | solution.py:235
  17.7 0.0 collective-permute-done.5.refs_0_
  17.7 0.0 collective-permute-start.6
  17.7 0.9 %fed_rows.1 = (f32[160,2048]{1,0:T(8,128)S(1)}, bf16[64,2048]{1,0:T(8,128)(2,1)S(1)}, bf16[64,2048]{1,0:T(8,128)(2,1)S(1)}) custom-call(bf16[32,1024]{1,0:T(8,128)(2,1)S(1)} %get-tuple-element.68.own_hidden_ref, bf16[128,1024]{1,0:T(8,128)(2,1)S(1)} %get-tuple-element.69.middle_hidden_ref, bf16[1024,2048]{1,0:T(8,128)(2,1)S(1)} %get-tuple-element.70.downward_ref.refs_7_, ...), custom_call_target="tpu_custom_call" | custom-call | flops 671088640 | bytes 1048576 | tf_op jit(solution)/shard_map/fed_rows/pallas_call | solution.py:593
  18.6 0.4 %collective-permute-done.6.refs_0_ = bf16[32,2048]{1,0:T(8,128)(2,1)S(1)} collective-permute-done((bf16[32,2048]{1,0:T(8,128)(2,1)S(1)}, bf16[32,2048]{1,0:T(8,128)(2,1)S(1)}, u32[]{:S(2)}, u32[]{:S(2)}) %collective-permute-start.6) | collective-permute-done | bytes 131104 | tf_op jit(solution)/shard_map/ppermute | solution.py:235
  19.0 2.4 %last_rows.1 = (bf16[256,768]{1,0:T(8,128)(2,1)S(1)}, f32[32,2048]{1,0:T(8,128)S(1)}, bf16[32,2048]{1,0:T(8,128)(2,1)S(1)}, f32[32,2048]{1,0:T(8,128)S(1)}) custom-call(bf16[32,2048]{1,0:T(8,128)(2,1)S(1)} %collective-permute-done.6.refs_0_, bf16[64,2048]{1,0:T(8,128)(2,1)S(1)} %get-tuple-element.72.refs_1_, bf16[64,2048]{1,0:T(8,128)(2,1)S(1)} %get-tuple-element.73.refs_2_, ...), custom_call_target="tpu_custom_call" | custom-call | flops 1207959552 | bytes 1048576 | tf_op jit(solution)/shard_map/last_rows/pallas_call | solution.py:552
  21.4 0.2 collective-permute-start.7
  21.6 0.8 %rest_rows.1 = (bf16[2,32,2048]{2,1,0:T(8,128)(2,1)S(1)}, bf16[32,2048]{1,0:T(8,128)(2,1)S(1)}, f32[32,2048]{1,0:T(8,128)S(1)}, f32[32,2048]{1,0:T(8,128)S(1)}, f32[32,2048]{1,0:T(8,128)S(1)}) custom-call(bf16[256,768]{1,0:T(8,128)(2,1)S(1)} %get-tuple-element.84.joined_ref, f32[256,128]{1,0:T(8,128)S(1)} %get-tuple-element.75.refs_9_.offsets_ref, ...), custom_call_target="tpu_custom_call" | custom-call | flops 201326592 | bytes 1048576 | tf_op jit(solution)/shard_map/rest_rows/pallas_call | solution.py:636
  22.4 0.4 %collective-permute-start.9 = (bf16[2,32,2048]{2,1,0:T(8,128)(2,1)S(1)}, bf16[2,32,2048]{2,1,0:T(8,128)(2,1)S(1)}, u32[]{:S(2)}, u32[]{:S(2)}) collective-permute-start(bf16[2,32,2048]{2,1,0:T(8,128)(2,1)S(1)} %get-tuple-element.88), channel_id=1, source_target_pairs={{0,1},{1,0},{2,3},{3,2},{4,5},{5,4},{6,7},{7,6},{8,9},{9,8},{10,11... | collective-permute-start | bytes 786440 | tf_op jit(solution)/shard_map/ppermute | solution.py:235
  22.9 0.0 collective-permute-done.7.refs_1_
  22.9 1.3 %collective-permute-start.11 = (bf16[32,2048]{1,0:T(8,128)(2,1)S(1)}, bf16[32,2048]{1,0:T(8,128)(2,1)S(1)}, u32[]{:S(2)}, u32[]{:S(2)}) collective-permute-start(bf16[32,2048]{1,0:T(8,128)(2,1)S(1)} %third_added.1), channel_id=1, source_target_pairs={{0,2},{1,3},{2,0},{3,1},{4,6},{5,7},{6,4},{7,5},{8,10},{9,11},{10,... | collective-permute-start | bytes 393224 | tf_op jit(solution)/shard_map/ppermute | solution.py:235
  24.2 0.3 cached_pages.1
  24.5 2.5 %collective-permute-start.8 = (bf16[8,16,512]{2,1,0:T(8,128)(2,1)S(1)}, bf16[8,16,512]{2,1,0:T(8,128)(2,1)S(1)}, u32[]{:S(2)}, u32[]{:S(2)}) collective-permute-start(bf16[8,16,512]{2,1,0:T(8,128)(2,1)S(1)} %get-tuple-element.87), channel_id=1, source_target_pairs={{0,24},{8,16},{16,8},{24,0},{1,25},{9,17},{17,9},{25,1},{2,26},{10... | collective-permute-start | bytes 393224 | tf_op jit(solution)/shard_map/ppermute | solution.py:235
  27.0 0.1 near_sums.1
  27.1 0.9 %collective-permute-start.10 = (bf16[32,2048]{1,0:T(8,128)(2,1)S(1)}, bf16[32,2048]{1,0:T(8,128)(2,1)S(1)}, u32[]{:S(2)}, u32[]{:S(2)}) collective-permute-start(bf16[32,2048]{1,0:T(8,128)(2,1)S(1)} %get-tuple-element.92), channel_id=1, source_target_pairs={{0,2},{1,3},{2,0},{3,1},{4,6},{5,7},{6,4},{7,5},{8,10},{9,11},{10,... | collective-permute-start | bytes 393224 | tf_op jit(solution)/shard_map/ppermute | solution.py:235
  28.0 0.6 %collective-permute-done.11.refs_1_ = bf16[32,2048]{1,0:T(8,128)(2,1)S(1)} collective-permute-done((bf16[32,2048]{1,0:T(8,128)(2,1)S(1)}, bf16[32,2048]{1,0:T(8,128)(2,1)S(1)}, u32[]{:S(2)}, u32[]{:S(2)}) %collective-permute-start.11) | collective-permute-done | bytes 131104 | tf_op jit(solution)/shard_map/ppermute | solution.py:235
  28.6 1.9 %collective-permute-start.13 = (bf16[32,2048]{1,0:T(8,128)(2,1)S(1)}, bf16[32,2048]{1,0:T(8,128)(2,1)S(1)}, u32[]{:S(2)}, u32[]{:S(2)}) collective-permute-start(bf16[32,2048]{1,0:T(8,128)(2,1)S(1)} %second_added.1), channel_id=1, source_target_pairs={{0,4},{1,5},{2,6},{3,7},{4,0},{5,1},{6,2},{7,3},{8,12},{9,13},{10,... | collective-permute-start | bytes 393224 | tf_op jit(solution)/shard_map/ppermute | solution.py:235
  30.5 1.5 %collective-permute-start.14 = (bf16[8,16,512]{2,1,0:T(8,128)(2,1)S(1)}, bf16[8,16,512]{2,1,0:T(8,128)(2,1)S(1)}, u32[]{:S(2)}, u32[]{:S(2)}) collective-permute-start(bf16[8,16,512]{2,1,0:T(8,128)(2,1)S(1)} %get-tuple-element.101), channel_id=1, source_target_pairs={{0,8},{8,0},{16,24},{24,16},{1,9},{9,1},{17,25},{25,17},{2,10},{10... | collective-permute-start | bytes 393224 | tf_op jit(solution)/shard_map/ppermute | solution.py:235
  32.0 1.6 %collective-permute-start.15 = (bf16[8,16,512]{2,1,0:T(8,128)(2,1)S(1)}, bf16[8,16,512]{2,1,0:T(8,128)(2,1)S(1)}, u32[]{:S(2)}, u32[]{:S(2)}) collective-permute-start(bf16[8,16,512]{2,1,0:T(8,128)(2,1)S(1)} %get-tuple-element.102), channel_id=1, source_target_pairs={{0,16},{8,24},{16,0},{24,8},{1,17},{9,25},{17,1},{25,9},{2,18},{10... | collective-permute-start | bytes 393224 | tf_op jit(solution)/shard_map/ppermute | solution.py:235
  33.5 2.1 %collective-permute-done.10.refs_2_ = bf16[32,2048]{1,0:T(8,128)(2,1)S(1)} collective-permute-done((bf16[32,2048]{1,0:T(8,128)(2,1)S(1)}, bf16[32,2048]{1,0:T(8,128)(2,1)S(1)}, u32[]{:S(2)}, u32[]{:S(2)}) %collective-permute-start.10) | collective-permute-done | bytes 131104 | tf_op jit(solution)/shard_map/ppermute | solution.py:235
  35.6 0.7 %placed.1 = (bf16[1,4,8,16,512]{4,3,2,1,0:T(8,128)(2,1)}, f32[32,2048]{1,0:T(8,128)S(1)}) custom-call(bf16[8,16,512]{2,1,0:T(8,128)(2,1)S(1)} %get-tuple-element.86.refs_0_, bf16[8,16,512]{2,1,0:T(8,128)(2,1)S(1)} %collective-permute-done.8.refs_1_, bf16[32,2048]{1,0:T(8,128)(2,1)S(1)} %collective-permute-done.10.refs_2_, ...), custom_call_target="tpu_custom_call" | custom-call | tf_op jit(solution)/shard_map/placed/pallas_call | solution.py:731
  36.4 0.6 %collective-permute-done.15.refs_2_ = bf16[8,16,512]{2,1,0:T(8,128)(2,1)S(1)} collective-permute-done((bf16[8,16,512]{2,1,0:T(8,128)(2,1)S(1)}, bf16[8,16,512]{2,1,0:T(8,128)(2,1)S(1)}, u32[]{:S(2)}, u32[]{:S(2)}) %collective-permute-start.15) | collective-permute-done | bytes 131104 | tf_op jit(solution)/shard_map/ppermute | solution.py:235
  36.9 0.8 %finished.1 = (f32[32,2048]{1,0:T(8,128)}, bf16[1,4,8,16,512]{4,3,2,1,0:T(8,128)(2,1)}) custom-call(f32[32,2048]{1,0:T(8,128)S(1)} %get-tuple-element.94.base_ref, bf16[32,2048]{1,0:T(8,128)(2,1)S(1)} %collective-permute-done.13.refs_0_, bf16[8,16,512]{2,1,0:T(8,128)(2,1)S(1)} %collective-permute-done.14.refs_1_, ...), custom_call_target="tpu_custom_call", output_to_operand_aliasing={{1}: (4, {})} | custom-call | tf_op jit(solution)/shard_map/finished/pallas_call | solution.py:774
  (11 shorter events, 0.1 us)
Async XLA Ops:
  0.6 11.0 %collective-permute-start.1 = (bf16[32,2048]{1,0:T(8,128)(2,1)}, bf16[32,2048]{1,0:T(8,128)(2,1)S(1)}, u32[]{:S(2)}, u32[]{:S(2)}) collective-permute-start(bf16[32,2048]{1,0:T(8,128)(2,1)} %refs_2_.1), channel_id=1, source_target_pairs={{0,4},{1,5},{2,6},{3,7},{4,0},{5,1},{6,2},{7,3},{8,12},{9,13},{10,... | collective-permute-start | bytes 393224 | tf_op jit(solution)/shard_map/ppermute | solution.py:235
  4.7 6.9 %collective-permute-start = (bf16[32,2048]{1,0:T(8,128)(2,1)}, bf16[32,2048]{1,0:T(8,128)(2,1)S(1)}, u32[]{:S(2)}, u32[]{:S(2)}) collective-permute-start(bf16[32,2048]{1,0:T(8,128)(2,1)} %refs_2_.1), channel_id=1, source_target_pairs={{0,2},{1,3},{2,0},{3,1},{4,6},{5,7},{6,4},{7,5},{8,10},{9,11},{10,... | collective-permute-start | bytes 393224 | tf_op jit(solution)/shard_map/ppermute | solution.py:235
  6.3 6.7 %collective-permute-start.3 = (bf16[32,2048]{1,0:T(8,128)(2,1)}, bf16[32,2048]{1,0:T(8,128)(2,1)S(1)}, u32[]{:S(2)}, u32[]{:S(2)}) collective-permute-start(bf16[32,2048]{1,0:T(8,128)(2,1)} %refs_2_.1), channel_id=1, source_target_pairs={{0,1},{1,0},{2,3},{3,2},{4,5},{5,4},{6,7},{7,6},{8,9},{9,8},{10,11... | collective-permute-start | bytes 393224 | tf_op jit(solution)/shard_map/ppermute | solution.py:235
  11.6 1.6 %collective-permute-start.4 = (bf16[32,2048]{1,0:T(8,128)(2,1)S(1)}, bf16[32,2048]{1,0:T(8,128)(2,1)S(1)}, u32[]{:S(2)}, u32[]{:S(2)}) collective-permute-start(bf16[32,2048]{1,0:T(8,128)(2,1)S(1)} %collective-permute-done.refs_1_), channel_id=1, source_target_pairs={{0,1},{1,0},{2,3},{3,2},{4,5},{5,4},{6,7},{7,6},{8,9},{9,8},{10,11... | collective-permute-start | bytes 393224 | tf_op jit(solution)/shard_map/ppermute | solution.py:235
  12.2 5.5 %collective-permute-start.2 = (bf16[32,2048]{1,0:T(8,128)(2,1)S(1)}, bf16[32,2048]{1,0:T(8,128)(2,1)S(1)}, u32[]{:S(2)}, u32[]{:S(2)}) collective-permute-start(bf16[32,2048]{1,0:T(8,128)(2,1)S(1)} %collective-permute-done.1.refs_3_), channel_id=1, source_target_pairs={{0,2},{1,3},{2,0},{3,1},{4,6},{5,7},{6,4},{7,5},{8,10},{9,11},{10,... | collective-permute-start | bytes 393224 | tf_op jit(solution)/shard_map/ppermute | solution.py:235
  15.3 2.4 %collective-permute-start.5 = (bf16[32,2048]{1,0:T(8,128)(2,1)S(1)}, bf16[32,2048]{1,0:T(8,128)(2,1)S(1)}, u32[]{:S(2)}, u32[]{:S(2)}) collective-permute-start(bf16[32,2048]{1,0:T(8,128)(2,1)S(1)} %collective-permute-done.1.refs_3_), channel_id=1, source_target_pairs={{0,1},{1,0},{2,3},{3,2},{4,5},{5,4},{6,7},{7,6},{8,9},{9,8},{10,11... | collective-permute-start | bytes 393224 | tf_op jit(solution)/shard_map/ppermute | solution.py:235
  17.7 1.3 %collective-permute-start.6 = (bf16[32,2048]{1,0:T(8,128)(2,1)S(1)}, bf16[32,2048]{1,0:T(8,128)(2,1)S(1)}, u32[]{:S(2)}, u32[]{:S(2)}) collective-permute-start(bf16[32,2048]{1,0:T(8,128)(2,1)S(1)} %collective-permute-done.2.refs_1_), channel_id=1, source_target_pairs={{0,1},{1,0},{2,3},{3,2},{4,5},{5,4},{6,7},{7,6},{8,9},{9,8},{10,11... | collective-permute-start | bytes 393224 | tf_op jit(solution)/shard_map/ppermute | solution.py:235
  21.4 1.4 %collective-permute-start.7 = (bf16[32,2048]{1,0:T(8,128)(2,1)S(1)}, bf16[32,2048]{1,0:T(8,128)(2,1)S(1)}, u32[]{:S(2)}, u32[]{:S(2)}) collective-permute-start(bf16[32,2048]{1,0:T(8,128)(2,1)S(1)} %get-tuple-element.79), channel_id=1, source_target_pairs={{0,1},{1,0},{2,3},{3,2},{4,5},{5,4},{6,7},{7,6},{8,9},{9,8},{10,11... | collective-permute-start | bytes 393224 | tf_op jit(solution)/shard_map/ppermute | solution.py:235
  22.4 4.6 %collective-permute-start.9 = (bf16[2,32,2048]{2,1,0:T(8,128)(2,1)S(1)}, bf16[2,32,2048]{2,1,0:T(8,128)(2,1)S(1)}, u32[]{:S(2)}, u32[]{:S(2)}) collective-permute-start(bf16[2,32,2048]{2,1,0:T(8,128)(2,1)S(1)} %get-tuple-element.88), channel_id=1, source_target_pairs={{0,1},{1,0},{2,3},{3,2},{4,5},{5,4},{6,7},{7,6},{8,9},{9,8},{10,11... | collective-permute-start | bytes 786440 | tf_op jit(solution)/shard_map/ppermute | solution.py:235
  22.9 5.6 %collective-permute-start.11 = (bf16[32,2048]{1,0:T(8,128)(2,1)S(1)}, bf16[32,2048]{1,0:T(8,128)(2,1)S(1)}, u32[]{:S(2)}, u32[]{:S(2)}) collective-permute-start(bf16[32,2048]{1,0:T(8,128)(2,1)S(1)} %third_added.1), channel_id=1, source_target_pairs={{0,2},{1,3},{2,0},{3,1},{4,6},{5,7},{6,4},{7,5},{8,10},{9,11},{10,... | collective-permute-start | bytes 393224 | tf_op jit(solution)/shard_map/ppermute | solution.py:235
  24.2 4.3 %collective-permute-start.12 = (bf16[32,2048]{1,0:T(8,128)(2,1)S(1)}, bf16[32,2048]{1,0:T(8,128)(2,1)S(1)}, u32[]{:S(2)}, u32[]{:S(2)}) collective-permute-start(bf16[32,2048]{1,0:T(8,128)(2,1)S(1)} %get-tuple-element.97), channel_id=1, source_target_pairs={{0,1},{1,0},{2,3},{3,2},{4,5},{5,4},{6,7},{7,6},{8,9},{9,8},{10,11... | collective-permute-start | bytes 393224 | tf_op jit(solution)/shard_map/ppermute | solution.py:235
  24.5 9.0 %collective-permute-start.8 = (bf16[8,16,512]{2,1,0:T(8,128)(2,1)S(1)}, bf16[8,16,512]{2,1,0:T(8,128)(2,1)S(1)}, u32[]{:S(2)}, u32[]{:S(2)}) collective-permute-start(bf16[8,16,512]{2,1,0:T(8,128)(2,1)S(1)} %get-tuple-element.87), channel_id=1, source_target_pairs={{0,24},{8,16},{16,8},{24,0},{1,25},{9,17},{17,9},{25,1},{2,26},{10... | collective-permute-start | bytes 393224 | tf_op jit(solution)/shard_map/ppermute | solution.py:235
  27.1 8.5 %collective-permute-start.10 = (bf16[32,2048]{1,0:T(8,128)(2,1)S(1)}, bf16[32,2048]{1,0:T(8,128)(2,1)S(1)}, u32[]{:S(2)}, u32[]{:S(2)}) collective-permute-start(bf16[32,2048]{1,0:T(8,128)(2,1)S(1)} %get-tuple-element.92), channel_id=1, source_target_pairs={{0,2},{1,3},{2,0},{3,1},{4,6},{5,7},{6,4},{7,5},{8,10},{9,11},{10,... | collective-permute-start | bytes 393224 | tf_op jit(solution)/shard_map/ppermute | solution.py:235
  28.6 7.8 %collective-permute-start.13 = (bf16[32,2048]{1,0:T(8,128)(2,1)S(1)}, bf16[32,2048]{1,0:T(8,128)(2,1)S(1)}, u32[]{:S(2)}, u32[]{:S(2)}) collective-permute-start(bf16[32,2048]{1,0:T(8,128)(2,1)S(1)} %second_added.1), channel_id=1, source_target_pairs={{0,4},{1,5},{2,6},{3,7},{4,0},{5,1},{6,2},{7,3},{8,12},{9,13},{10,... | collective-permute-start | bytes 393224 | tf_op jit(solution)/shard_map/ppermute | solution.py:235
  30.5 5.9 %collective-permute-start.14 = (bf16[8,16,512]{2,1,0:T(8,128)(2,1)S(1)}, bf16[8,16,512]{2,1,0:T(8,128)(2,1)S(1)}, u32[]{:S(2)}, u32[]{:S(2)}) collective-permute-start(bf16[8,16,512]{2,1,0:T(8,128)(2,1)S(1)} %get-tuple-element.101), channel_id=1, source_target_pairs={{0,8},{8,0},{16,24},{24,16},{1,9},{9,1},{17,25},{25,17},{2,10},{10... | collective-permute-start | bytes 393224 | tf_op jit(solution)/shard_map/ppermute | solution.py:235
  32.0 5.0 %collective-permute-start.15 = (bf16[8,16,512]{2,1,0:T(8,128)(2,1)S(1)}, bf16[8,16,512]{2,1,0:T(8,128)(2,1)S(1)}, u32[]{:S(2)}, u32[]{:S(2)}) collective-permute-start(bf16[8,16,512]{2,1,0:T(8,128)(2,1)S(1)} %get-tuple-element.102), channel_id=1, source_target_pairs={{0,16},{8,24},{16,0},{24,8},{1,17},{9,25},{17,1},{25,9},{2,18},{10... | collective-permute-start | bytes 393224 | tf_op jit(solution)/shard_map/ppermute | solution.py:235

commit v15 on v14

--- a/solution.py
+++ b/solution.py
@@ -389,7 +389,7 @@
     destinations_ref[...] = slot * PAGE + (positions & (PAGE - 1))
 
 
-def copies_in(sources, targets, sems):
+def copies_in(sources, targets, sems, at_once=None):
     copies = []
     for number, (source, target) in enumerate(zip(sources, targets)):
         parts = 4 if source.shape[0] >= 256 else 1
@@ -401,7 +401,7 @@
                 for part, place in enumerate(places)
             ]
         )
-    for copy in sum(copies, []):
+    for copy in sum(copies[:at_once], []):
         copy.start()
     return copies
 
@@ -415,7 +415,7 @@
     sources, targets = refs[:count], refs[count : 2 * count]
     offsets_ref, *table_refs, destinations_ref, joined_ref, hidden_ref = refs[2 * count : -3]
     attention_scr, feedforward_scr, sems = refs[-3:]
-    copies = copies_in(sources, targets, sems)
+    copies = copies_in(sources, targets, sems, 7)
     segments_ref, targets_ref, states_ref, *gain_refs, heads_ref, upward_ref, _ = targets
     block_rows = states_ref.shape[0]
     wait_for(copies[0])
@@ -426,6 +426,8 @@
         wait_for(copies[number])
     normalize([states_ref], gain_refs, [attention_scr, feedforward_scr])
     wait_for(copies[5])
+    for copy in copies[7]:
+        copy.start()
     places = [position_of(0, 0, block_rows)]
     project(attention_scr, heads_ref, table_refs, places, joined_ref, 0)
     wait_for(copies[6])
@@ -753,18 +755,12 @@
     ]
     for copy in copies:
         copy.start()
-    rows = 8
-    for first in range(0, base_ref.shape[0], 2 * rows):
-        both = slice(first, first + 2 * rows)
-        total = base_ref[both, :]
-        for part_ref in parts:
-            total = total + part_ref[both, :].astype(jnp.float32)
-        total_scr[both, :] = total
-        for place in (first, first + rows):
-            piece = pl.ds(place, rows)
-            sem = sems.at[count + place // rows]
-            copies.append(pltpu.make_async_copy(total_scr.at[piece], output_ref.at[piece], sem))
-            copies[-1].start()
+    total = base_ref[...]
+    for part_ref in parts:
+        total = total + part_ref[...].astype(jnp.float32)
+    total_scr[...] = total
+    copies.append(pltpu.make_async_copy(total_scr, output_ref, sems.at[count]))
+    copies[-1].start()
     for copy in copies:
         copy.wait()
 
@@ -783,7 +779,7 @@
         out_specs=[pl.BlockSpec(memory_space=pltpu.HBM)] * 2,
         scratch_shapes=[
             pltpu.VMEM(base.shape, base.dtype),
-            pltpu.SemaphoreType.DMA((count + base.shape[0] // 8,)),
+            pltpu.SemaphoreType.DMA((count + 1,)),
         ],
         input_output_aliases={1 + len(parts) + count: 1},
         compiler_params=parameters(4),

time: 37.9 us -> 38.5 us (1.016)
  waiting for transfers between devices: 5.77 us -> 6.61 us
  starting transfers between devices: 17.8 us -> 17.3 us
    ppermute x16, waiting for transfers between devices: 5.77 us -> 6.61 us  [exchanged(): lax.ppermute(block, axis, [(member, member ^ mask) for member in range(co...]
    ppermute x16, starting transfers between devices: 17.8 us -> 17.3 us  [exchanged(): lax.ppermute(block, axis, [(member, member ^ mask) for member in range(co...]
where the time goes in v15:
time: 38.5 us; the launch traced here: 38.4 us
  starting transfers between devices  17.3 us (45%)
  Pallas kernels  13.7 us (36%)
  waiting for transfers between devices  6.61 us (17%)
  between operations  0.72 us (2%)
    ppermute x16, starting transfers between devices, exchanged(): lax.ppermute(block, axis, [(member, member ^ mask) for member in range(co...  17.3 us
    ppermute x16, waiting for transfers between devices, exchanged(): lax.ppermute(block, axis, [(member, member ^ mask) for member in range(co...  6.61 us
    pallas_call x1, Pallas kernels, own_rows(): pl.pallas_call(functools.partial(own_kernel, count, replica_count), out_s...  5.5 us
    pallas_call x1, Pallas kernels, last_rows(): pl.pallas_call(last_kernel, out_shape=[pltpu.VMEM((tokens, 3 * HD), jnp.b...  2.4 us
    pallas_call x1, Pallas kernels, middle_rows(): pl.pallas_call(functools.partial(middle_kernel, origins), out_shape=[pltp...  2.12 us
    pallas_call x1, Pallas kernels, fed_rows(): pl.pallas_call(fed_kernel, out_shape=[pltpu.VMEM((rows, width), jnp.float...  0.9 us
    pallas_call x1, Pallas kernels, finished(): pl.pallas_call(functools.partial(finish_kernel, masks), out_shape=[jax.Sh...  0.83 us
    pallas_call x1, Pallas kernels, rest_rows(): pl.pallas_call(rest_kernel, out_shape=shapes, in_specs=vmem_specs(5), out...  0.79 us
  transfers between devices with their start and end apart: 16, of which 6 were waited for; matrix products, arithmetic and copies ran while one was open for 0% of the time, Pallas kernels for 27%

profile of v15, /device:TPU:0, one launch (start us, length us, event | category | flops | bytes accessed | tf_op | source)
XLA Modules:
  0.0 38.4 jit_solution(1678604261680799146)
XLA Ops:
  0.6 4.1 %collective-permute-start.1 = (bf16[32,2048]{1,0:T(8,128)(2,1)}, bf16[32,2048]{1,0:T(8,128)(2,1)S(1)}, u32[]{:S(2)}, u32[]{:S(2)}) collective-permute-start(bf16[32,2048]{1,0:T(8,128)(2,1)} %refs_2_.1), channel_id=1, source_target_pairs={{0,4},{1,5},{2,6},{3,7},{4,0},{5,1},{6,2},{7,3},{8,12},{9,13},{10,... | collective-permute-start | bytes 393224 | tf_op jit(solution)/shard_map/ppermute | solution.py:235
  4.7 1.6 %collective-permute-start = (bf16[32,2048]{1,0:T(8,128)(2,1)}, bf16[32,2048]{1,0:T(8,128)(2,1)S(1)}, u32[]{:S(2)}, u32[]{:S(2)}) collective-permute-start(bf16[32,2048]{1,0:T(8,128)(2,1)} %refs_2_.1), channel_id=1, source_target_pairs={{0,2},{1,3},{2,0},{3,1},{4,6},{5,7},{6,4},{7,5},{8,10},{9,11},{10,... | collective-permute-start | bytes 393224 | tf_op jit(solution)/shard_map/ppermute | solution.py:235
  6.3 5.5 %own_rows.1 = (s32[1,256]{1,0:T(1,128)}, s32[1,16]{1,0:T(1,128)}, bf16[32,2048]{1,0:T(8,128)(2,1)S(1)}, f32[1,2048]{1,0:T(1,128)S(1)}, f32[1,2048]{1,0:T(1,128)S...) custom-call(s32[1,256]{1,0:T(1,128)} %refs_0_.1, ...), custom_call_target="tpu_custom_call" | custom-call | flops 234881024 | bytes 11682880 | tf_op jit(solution)/shard_map/own_rows/pallas_call | solution.py:450
  11.8 0.0 collective-permute-done.refs_1_
  11.8 0.6 %collective-permute-start.4 = (bf16[32,2048]{1,0:T(8,128)(2,1)S(1)}, bf16[32,2048]{1,0:T(8,128)(2,1)S(1)}, u32[]{:S(2)}, u32[]{:S(2)}) collective-permute-start(bf16[32,2048]{1,0:T(8,128)(2,1)S(1)} %collective-permute-done.refs_1_), channel_id=1, source_target_pairs={{0,1},{1,0},{2,3},{3,2},{4,5},{5,4},{6,7},{7,6},{8,9},{9,8},{10,11... | collective-permute-start | bytes 393224 | tf_op jit(solution)/shard_map/ppermute | solution.py:235
  12.4 0.6 %collective-permute-start.2 = (bf16[32,2048]{1,0:T(8,128)(2,1)S(1)}, bf16[32,2048]{1,0:T(8,128)(2,1)S(1)}, u32[]{:S(2)}, u32[]{:S(2)}) collective-permute-start(bf16[32,2048]{1,0:T(8,128)(2,1)S(1)} %collective-permute-done.1.refs_3_), channel_id=1, source_target_pairs={{0,2},{1,3},{2,0},{3,1},{4,6},{5,7},{6,4},{7,5},{8,10},{9,11},{10,... | collective-permute-start | bytes 393224 | tf_op jit(solution)/shard_map/ppermute | solution.py:235
  13.0 0.0 collective-permute-done.3.refs_0_
  13.0 0.4 %collective-permute-done.4.refs_2_ = bf16[32,2048]{1,0:T(8,128)(2,1)S(1)} collective-permute-done((bf16[32,2048]{1,0:T(8,128)(2,1)S(1)}, bf16[32,2048]{1,0:T(8,128)(2,1)S(1)}, u32[]{:S(2)}, u32[]{:S(2)}) %collective-permute-start.4) | collective-permute-done | bytes 131104 | tf_op jit(solution)/shard_map/ppermute | solution.py:235
  13.4 2.1 %middle_rows.1 = (bf16[128,768]{1,0:T(8,128)(2,1)S(1)}, bf16[128,1024]{1,0:T(8,128)(2,1)S(1)}, bf16[256,2048]{1,0:T(8,128)(2,1)S(1)}) custom-call(bf16[32,2048]{1,0:T(8,128)(2,1)S(1)} %collective-permute-done.3.refs_0_, bf16[32,2048]{1,0:T(8,128)(2,1)S(1)} %collective-permute-done.refs_1_, bf16[32,2048]{1,0:T(8,128)(2,1)S(1)} %collective-permute-done.4.refs_2_, ...), custom_call_target="tpu_custom_call" | custom-call | flops 939524096 | bytes 1048576 | tf_op jit(solution)/shard_map/middle_rows/pallas_call | solution.py:490
  15.5 0.4 %collective-permute-start.5 = (bf16[32,2048]{1,0:T(8,128)(2,1)S(1)}, bf16[32,2048]{1,0:T(8,128)(2,1)S(1)}, u32[]{:S(2)}, u32[]{:S(2)}) collective-permute-start(bf16[32,2048]{1,0:T(8,128)(2,1)S(1)} %collective-permute-done.1.refs_3_), channel_id=1, source_target_pairs={{0,1},{1,0},{2,3},{3,2},{4,5},{5,4},{6,7},{7,6},{8,9},{9,8},{10,11... | collective-permute-start | bytes 393224 | tf_op jit(solution)/shard_map/ppermute | solution.py:235
  16.0 1.9 %collective-permute-done.2.refs_1_ = bf16[32,2048]{1,0:T(8,128)(2,1)S(1)} collective-permute-done((bf16[32,2048]{1,0:T(8,128)(2,1)S(1)}, bf16[32,2048]{1,0:T(8,128)(2,1)S(1)}, u32[]{:S(2)}, u32[]{:S(2)}) %collective-permute-start.2) | collective-permute-done | bytes 131104 | tf_op jit(solution)/shard_map/ppermute | solution.py:235
  17.9 0.0 collective-permute-done.5.refs_0_
  17.9 0.9 %fed_rows.1 = (f32[160,2048]{1,0:T(8,128)S(1)}, bf16[64,2048]{1,0:T(8,128)(2,1)S(1)}, bf16[64,2048]{1,0:T(8,128)(2,1)S(1)}) custom-call(bf16[32,1024]{1,0:T(8,128)(2,1)S(1)} %get-tuple-element.68.own_hidden_ref, bf16[128,1024]{1,0:T(8,128)(2,1)S(1)} %get-tuple-element.69.middle_hidden_ref, bf16[1024,2048]{1,0:T(8,128)(2,1)S(1)} %get-tuple-element.70.downward_ref.refs_7_, ...), custom_call_target="tpu_custom_call" | custom-call | flops 671088640 | bytes 1048576 | tf_op jit(solution)/shard_map/fed_rows/pallas_call | solution.py:595
  18.8 0.4 %collective-permute-done.6.refs_0_ = bf16[32,2048]{1,0:T(8,128)(2,1)S(1)} collective-permute-done((bf16[32,2048]{1,0:T(8,128)(2,1)S(1)}, bf16[32,2048]{1,0:T(8,128)(2,1)S(1)}, u32[]{:S(2)}, u32[]{:S(2)}) %collective-permute-start.6) | collective-permute-done | bytes 131104 | tf_op jit(solution)/shard_map/ppermute | solution.py:235
  19.3 2.4 %last_rows.1 = (bf16[256,768]{1,0:T(8,128)(2,1)S(1)}, f32[32,2048]{1,0:T(8,128)S(1)}, bf16[32,2048]{1,0:T(8,128)(2,1)S(1)}, f32[32,2048]{1,0:T(8,128)S(1)}) custom-call(bf16[32,2048]{1,0:T(8,128)(2,1)S(1)} %collective-permute-done.6.refs_0_, bf16[64,2048]{1,0:T(8,128)(2,1)S(1)} %get-tuple-element.72.refs_1_, bf16[64,2048]{1,0:T(8,128)(2,1)S(1)} %get-tuple-element.73.refs_2_, ...), custom_call_target="tpu_custom_call" | custom-call | flops 1207959552 | bytes 1048576 | tf_op jit(solution)/shard_map/last_rows/pallas_call | solution.py:554
  21.7 0.2 collective-permute-start.7
  21.9 0.8 %rest_rows.1 = (bf16[2,32,2048]{2,1,0:T(8,128)(2,1)S(1)}, bf16[32,2048]{1,0:T(8,128)(2,1)S(1)}, f32[32,2048]{1,0:T(8,128)S(1)}, f32[32,2048]{1,0:T(8,128)S(1)}, f32[32,2048]{1,0:T(8,128)S(1)}) custom-call(bf16[256,768]{1,0:T(8,128)(2,1)S(1)} %get-tuple-element.84.joined_ref, f32[256,128]{1,0:T(8,128)S(1)} %get-tuple-element.75.refs_9_.offsets_ref, ...), custom_call_target="tpu_custom_call" | custom-call | flops 201326592 | bytes 1048576 | tf_op jit(solution)/shard_map/rest_rows/pallas_call | solution.py:638
  22.7 0.4 %collective-permute-start.9 = (bf16[2,32,2048]{2,1,0:T(8,128)(2,1)S(1)}, bf16[2,32,2048]{2,1,0:T(8,128)(2,1)S(1)}, u32[]{:S(2)}, u32[]{:S(2)}) collective-permute-start(bf16[2,32,2048]{2,1,0:T(8,128)(2,1)S(1)} %get-tuple-element.88), channel_id=1, source_target_pairs={{0,1},{1,0},{2,3},{3,2},{4,5},{5,4},{6,7},{7,6},{8,9},{9,8},{10,11... | collective-permute-start | bytes 786440 | tf_op jit(solution)/shard_map/ppermute | solution.py:235
  23.1 0.0 collective-permute-done.7.refs_1_
  23.1 1.1 %collective-permute-start.11 = (bf16[32,2048]{1,0:T(8,128)(2,1)S(1)}, bf16[32,2048]{1,0:T(8,128)(2,1)S(1)}, u32[]{:S(2)}, u32[]{:S(2)}) collective-permute-start(bf16[32,2048]{1,0:T(8,128)(2,1)S(1)} %third_added.1), channel_id=1, source_target_pairs={{0,2},{1,3},{2,0},{3,1},{4,6},{5,7},{6,4},{7,5},{8,10},{9,11},{10,... | collective-permute-start | bytes 393224 | tf_op jit(solution)/shard_map/ppermute | solution.py:235
  24.2 0.3 cached_pages.1
  24.5 2.5 %collective-permute-start.8 = (bf16[8,16,512]{2,1,0:T(8,128)(2,1)S(1)}, bf16[8,16,512]{2,1,0:T(8,128)(2,1)S(1)}, u32[]{:S(2)}, u32[]{:S(2)}) collective-permute-start(bf16[8,16,512]{2,1,0:T(8,128)(2,1)S(1)} %get-tuple-element.87), channel_id=1, source_target_pairs={{0,24},{8,16},{16,8},{24,0},{1,25},{9,17},{17,9},{25,1},{2,26},{10... | collective-permute-start | bytes 393224 | tf_op jit(solution)/shard_map/ppermute | solution.py:235
  27.0 0.1 near_sums.1
  27.1 1.1 %collective-permute-start.10 = (bf16[32,2048]{1,0:T(8,128)(2,1)S(1)}, bf16[32,2048]{1,0:T(8,128)(2,1)S(1)}, u32[]{:S(2)}, u32[]{:S(2)}) collective-permute-start(bf16[32,2048]{1,0:T(8,128)(2,1)S(1)} %get-tuple-element.92), channel_id=1, source_target_pairs={{0,2},{1,3},{2,0},{3,1},{4,6},{5,7},{6,4},{7,5},{8,10},{9,11},{10,... | collective-permute-start | bytes 393224 | tf_op jit(solution)/shard_map/ppermute | solution.py:235
  28.2 0.5 %collective-permute-done.11.refs_1_ = bf16[32,2048]{1,0:T(8,128)(2,1)S(1)} collective-permute-done((bf16[32,2048]{1,0:T(8,128)(2,1)S(1)}, bf16[32,2048]{1,0:T(8,128)(2,1)S(1)}, u32[]{:S(2)}, u32[]{:S(2)}) %collective-permute-start.11) | collective-permute-done | bytes 131104 | tf_op jit(solution)/shard_map/ppermute | solution.py:235
  28.8 1.7 %collective-permute-start.13 = (bf16[32,2048]{1,0:T(8,128)(2,1)S(1)}, bf16[32,2048]{1,0:T(8,128)(2,1)S(1)}, u32[]{:S(2)}, u32[]{:S(2)}) collective-permute-start(bf16[32,2048]{1,0:T(8,128)(2,1)S(1)} %second_added.1), channel_id=1, source_target_pairs={{0,4},{1,5},{2,6},{3,7},{4,0},{5,1},{6,2},{7,3},{8,12},{9,13},{10,... | collective-permute-start | bytes 393224 | tf_op jit(solution)/shard_map/ppermute | solution.py:235
  30.5 1.5 %collective-permute-start.14 = (bf16[8,16,512]{2,1,0:T(8,128)(2,1)S(1)}, bf16[8,16,512]{2,1,0:T(8,128)(2,1)S(1)}, u32[]{:S(2)}, u32[]{:S(2)}) collective-permute-start(bf16[8,16,512]{2,1,0:T(8,128)(2,1)S(1)} %get-tuple-element.101), channel_id=1, source_target_pairs={{0,8},{8,0},{16,24},{24,16},{1,9},{9,1},{17,25},{25,17},{2,10},{10... | collective-permute-start | bytes 393224 | tf_op jit(solution)/shard_map/ppermute | solution.py:235
  32.0 1.6 %collective-permute-start.15 = (bf16[8,16,512]{2,1,0:T(8,128)(2,1)S(1)}, bf16[8,16,512]{2,1,0:T(8,128)(2,1)S(1)}, u32[]{:S(2)}, u32[]{:S(2)}) collective-permute-start(bf16[8,16,512]{2,1,0:T(8,128)(2,1)S(1)} %get-tuple-element.102), channel_id=1, source_target_pairs={{0,16},{8,24},{16,0},{24,8},{1,17},{9,25},{17,1},{25,9},{2,18},{10... | collective-permute-start | bytes 393224 | tf_op jit(solution)/shard_map/ppermute | solution.py:235
  33.5 2.0 %collective-permute-done.10.refs_2_ = bf16[32,2048]{1,0:T(8,128)(2,1)S(1)} collective-permute-done((bf16[32,2048]{1,0:T(8,128)(2,1)S(1)}, bf16[32,2048]{1,0:T(8,128)(2,1)S(1)}, u32[]{:S(2)}, u32[]{:S(2)}) %collective-permute-start.10) | collective-permute-done | bytes 131104 | tf_op jit(solution)/shard_map/ppermute | solution.py:235
  35.6 0.7 %placed.1 = (bf16[1,4,8,16,512]{4,3,2,1,0:T(8,128)(2,1)}, f32[32,2048]{1,0:T(8,128)S(1)}) custom-call(bf16[8,16,512]{2,1,0:T(8,128)(2,1)S(1)} %get-tuple-element.86.refs_0_, bf16[8,16,512]{2,1,0:T(8,128)(2,1)S(1)} %collective-permute-done.8.refs_1_, bf16[32,2048]{1,0:T(8,128)(2,1)S(1)} %collective-permute-done.10.refs_2_, ...), custom_call_target="tpu_custom_call" | custom-call | tf_op jit(solution)/shard_map/placed/pallas_call | solution.py:733
  36.3 1.2 %collective-permute-done.13.refs_0_ = bf16[32,2048]{1,0:T(8,128)(2,1)S(1)} collective-permute-done((bf16[32,2048]{1,0:T(8,128)(2,1)S(1)}, bf16[32,2048]{1,0:T(8,128)(2,1)S(1)}, u32[]{:S(2)}, u32[]{:S(2)}) %collective-permute-start.13) | collective-permute-done | bytes 131104 | tf_op jit(solution)/shard_map/ppermute | solution.py:235
  37.5 0.8 %finished.1 = (f32[32,2048]{1,0:T(8,128)}, bf16[1,4,8,16,512]{4,3,2,1,0:T(8,128)(2,1)}) custom-call(f32[32,2048]{1,0:T(8,128)S(1)} %get-tuple-element.94.base_ref, bf16[32,2048]{1,0:T(8,128)(2,1)S(1)} %collective-permute-done.13.refs_0_, bf16[8,16,512]{2,1,0:T(8,128)(2,1)S(1)} %collective-permute-done.14.refs_1_, ...), custom_call_target="tpu_custom_call", output_to_operand_aliasing={{1}: (4, {})} | custom-call | tf_op jit(solution)/shard_map/finished/pallas_call | solution.py:770
  (11 shorter events, 0.1 us)
Async XLA Ops:
  0.6 11.2 %collective-permute-start.1 = (bf16[32,2048]{1,0:T(8,128)(2,1)}, bf16[32,2048]{1,0:T(8,128)(2,1)S(1)}, u32[]{:S(2)}, u32[]{:S(2)}) collective-permute-start(bf16[32,2048]{1,0:T(8,128)(2,1)} %refs_2_.1), channel_id=1, source_target_pairs={{0,4},{1,5},{2,6},{3,7},{4,0},{5,1},{6,2},{7,3},{8,12},{9,13},{10,... | collective-permute-start | bytes 393224 | tf_op jit(solution)/shard_map/ppermute | solution.py:235
  4.7 7.1 %collective-permute-start = (bf16[32,2048]{1,0:T(8,128)(2,1)}, bf16[32,2048]{1,0:T(8,128)(2,1)S(1)}, u32[]{:S(2)}, u32[]{:S(2)}) collective-permute-start(bf16[32,2048]{1,0:T(8,128)(2,1)} %refs_2_.1), channel_id=1, source_target_pairs={{0,2},{1,3},{2,0},{3,1},{4,6},{5,7},{6,4},{7,5},{8,10},{9,11},{10,... | collective-permute-start | bytes 393224 | tf_op jit(solution)/shard_map/ppermute | solution.py:235
  6.3 6.7 %collective-permute-start.3 = (bf16[32,2048]{1,0:T(8,128)(2,1)}, bf16[32,2048]{1,0:T(8,128)(2,1)S(1)}, u32[]{:S(2)}, u32[]{:S(2)}) collective-permute-start(bf16[32,2048]{1,0:T(8,128)(2,1)} %refs_2_.1), channel_id=1, source_target_pairs={{0,1},{1,0},{2,3},{3,2},{4,5},{5,4},{6,7},{7,6},{8,9},{9,8},{10,11... | collective-permute-start | bytes 393224 | tf_op jit(solution)/shard_map/ppermute | solution.py:235
  11.8 1.6 %collective-permute-start.4 = (bf16[32,2048]{1,0:T(8,128)(2,1)S(1)}, bf16[32,2048]{1,0:T(8,128)(2,1)S(1)}, u32[]{:S(2)}, u32[]{:S(2)}) collective-permute-start(bf16[32,2048]{1,0:T(8,128)(2,1)S(1)} %collective-permute-done.refs_1_), channel_id=1, source_target_pairs={{0,1},{1,0},{2,3},{3,2},{4,5},{5,4},{6,7},{7,6},{8,9},{9,8},{10,11... | collective-permute-start | bytes 393224 | tf_op jit(solution)/shard_map/ppermute | solution.py:235
  12.4 5.5 %collective-permute-start.2 = (bf16[32,2048]{1,0:T(8,128)(2,1)S(1)}, bf16[32,2048]{1,0:T(8,128)(2,1)S(1)}, u32[]{:S(2)}, u32[]{:S(2)}) collective-permute-start(bf16[32,2048]{1,0:T(8,128)(2,1)S(1)} %collective-permute-done.1.refs_3_), channel_id=1, source_target_pairs={{0,2},{1,3},{2,0},{3,1},{4,6},{5,7},{6,4},{7,5},{8,10},{9,11},{10,... | collective-permute-start | bytes 393224 | tf_op jit(solution)/shard_map/ppermute | solution.py:235
  15.5 2.4 %collective-permute-start.5 = (bf16[32,2048]{1,0:T(8,128)(2,1)S(1)}, bf16[32,2048]{1,0:T(8,128)(2,1)S(1)}, u32[]{:S(2)}, u32[]{:S(2)}) collective-permute-start(bf16[32,2048]{1,0:T(8,128)(2,1)S(1)} %collective-permute-done.1.refs_3_), channel_id=1, source_target_pairs={{0,1},{1,0},{2,3},{3,2},{4,5},{5,4},{6,7},{7,6},{8,9},{9,8},{10,11... | collective-permute-start | bytes 393224 | tf_op jit(solution)/shard_map/ppermute | solution.py:235
  17.9 1.3 %collective-permute-start.6 = (bf16[32,2048]{1,0:T(8,128)(2,1)S(1)}, bf16[32,2048]{1,0:T(8,128)(2,1)S(1)}, u32[]{:S(2)}, u32[]{:S(2)}) collective-permute-start(bf16[32,2048]{1,0:T(8,128)(2,1)S(1)} %collective-permute-done.2.refs_1_), channel_id=1, source_target_pairs={{0,1},{1,0},{2,3},{3,2},{4,5},{5,4},{6,7},{7,6},{8,9},{9,8},{10,11... | collective-permute-start | bytes 393224 | tf_op jit(solution)/shard_map/ppermute | solution.py:235
  21.7 1.4 %collective-permute-start.7 = (bf16[32,2048]{1,0:T(8,128)(2,1)S(1)}, bf16[32,2048]{1,0:T(8,128)(2,1)S(1)}, u32[]{:S(2)}, u32[]{:S(2)}) collective-permute-start(bf16[32,2048]{1,0:T(8,128)(2,1)S(1)} %get-tuple-element.79), channel_id=1, source_target_pairs={{0,1},{1,0},{2,3},{3,2},{4,5},{5,4},{6,7},{7,6},{8,9},{9,8},{10,11... | collective-permute-start | bytes 393224 | tf_op jit(solution)/shard_map/ppermute | solution.py:235
  22.7 4.4 %collective-permute-start.9 = (bf16[2,32,2048]{2,1,0:T(8,128)(2,1)S(1)}, bf16[2,32,2048]{2,1,0:T(8,128)(2,1)S(1)}, u32[]{:S(2)}, u32[]{:S(2)}) collective-permute-start(bf16[2,32,2048]{2,1,0:T(8,128)(2,1)S(1)} %get-tuple-element.88), channel_id=1, source_target_pairs={{0,1},{1,0},{2,3},{3,2},{4,5},{5,4},{6,7},{7,6},{8,9},{9,8},{10,11... | collective-permute-start | bytes 786440 | tf_op jit(solution)/shard_map/ppermute | solution.py:235
  23.1 5.6 %collective-permute-start.11 = (bf16[32,2048]{1,0:T(8,128)(2,1)S(1)}, bf16[32,2048]{1,0:T(8,128)(2,1)S(1)}, u32[]{:S(2)}, u32[]{:S(2)}) collective-permute-start(bf16[32,2048]{1,0:T(8,128)(2,1)S(1)} %third_added.1), channel_id=1, source_target_pairs={{0,2},{1,3},{2,0},{3,1},{4,6},{5,7},{6,4},{7,5},{8,10},{9,11},{10,... | collective-permute-start | bytes 393224 | tf_op jit(solution)/shard_map/ppermute | solution.py:235
  24.2 4.5 %collective-permute-start.12 = (bf16[32,2048]{1,0:T(8,128)(2,1)S(1)}, bf16[32,2048]{1,0:T(8,128)(2,1)S(1)}, u32[]{:S(2)}, u32[]{:S(2)}) collective-permute-start(bf16[32,2048]{1,0:T(8,128)(2,1)S(1)} %get-tuple-element.97), channel_id=1, source_target_pairs={{0,1},{1,0},{2,3},{3,2},{4,5},{5,4},{6,7},{7,6},{8,9},{9,8},{10,11... | collective-permute-start | bytes 393224 | tf_op jit(solution)/shard_map/ppermute | solution.py:235
  24.5 9.0 %collective-permute-start.8 = (bf16[8,16,512]{2,1,0:T(8,128)(2,1)S(1)}, bf16[8,16,512]{2,1,0:T(8,128)(2,1)S(1)}, u32[]{:S(2)}, u32[]{:S(2)}) collective-permute-start(bf16[8,16,512]{2,1,0:T(8,128)(2,1)S(1)} %get-tuple-element.87), channel_id=1, source_target_pairs={{0,24},{8,16},{16,8},{24,0},{1,25},{9,17},{17,9},{25,1},{2,26},{10... | collective-permute-start | bytes 393224 | tf_op jit(solution)/shard_map/ppermute | solution.py:235
  27.1 8.5 %collective-permute-start.10 = (bf16[32,2048]{1,0:T(8,128)(2,1)S(1)}, bf16[32,2048]{1,0:T(8,128)(2,1)S(1)}, u32[]{:S(2)}, u32[]{:S(2)}) collective-permute-start(bf16[32,2048]{1,0:T(8,128)(2,1)S(1)} %get-tuple-element.92), channel_id=1, source_target_pairs={{0,2},{1,3},{2,0},{3,1},{4,6},{5,7},{6,4},{7,5},{8,10},{9,11},{10,... | collective-permute-start | bytes 393224 | tf_op jit(solution)/shard_map/ppermute | solution.py:235
  28.8 8.7 %collective-permute-start.13 = (bf16[32,2048]{1,0:T(8,128)(2,1)S(1)}, bf16[32,2048]{1,0:T(8,128)(2,1)S(1)}, u32[]{:S(2)}, u32[]{:S(2)}) collective-permute-start(bf16[32,2048]{1,0:T(8,128)(2,1)S(1)} %second_added.1), channel_id=1, source_target_pairs={{0,4},{1,5},{2,6},{3,7},{4,0},{5,1},{6,2},{7,3},{8,12},{9,13},{10,... | collective-permute-start | bytes 393224 | tf_op jit(solution)/shard_map/ppermute | solution.py:235
  30.5 7.1 %collective-permute-start.14 = (bf16[8,16,512]{2,1,0:T(8,128)(2,1)S(1)}, bf16[8,16,512]{2,1,0:T(8,128)(2,1)S(1)}, u32[]{:S(2)}, u32[]{:S(2)}) collective-permute-start(bf16[8,16,512]{2,1,0:T(8,128)(2,1)S(1)} %get-tuple-element.101), channel_id=1, source_target_pairs={{0,8},{8,0},{16,24},{24,16},{1,9},{9,1},{17,25},{25,17},{2,10},{10... | collective-permute-start | bytes 393224 | tf_op jit(solution)/shard_map/ppermute | solution.py:235
  32.0 5.6 %collective-permute-start.15 = (bf16[8,16,512]{2,1,0:T(8,128)(2,1)S(1)}, bf16[8,16,512]{2,1,0:T(8,128)(2,1)S(1)}, u32[]{:S(2)}, u32[]{:S(2)}) collective-permute-start(bf16[8,16,512]{2,1,0:T(8,128)(2,1)S(1)} %get-tuple-element.102), channel_id=1, source_target_pairs={{0,16},{8,24},{16,0},{24,8},{1,17},{9,25},{17,1},{25,9},{2,18},{10... | collective-permute-start | bytes 393224 | tf_op jit(solution)/shard_map/ppermute | solution.py:235

commit v16 on v15

--- a/solution.py
+++ b/solution.py
@@ -389,7 +389,7 @@
     destinations_ref[...] = slot * PAGE + (positions & (PAGE - 1))
 
 
-def copies_in(sources, targets, sems, at_once=None):
+def copies_in(sources, targets, sems):
     copies = []
     for number, (source, target) in enumerate(zip(sources, targets)):
         parts = 4 if source.shape[0] >= 256 else 1
@@ -401,7 +401,7 @@
                 for part, place in enumerate(places)
             ]
         )
-    for copy in sum(copies[:at_once], []):
+    for copy in sum(copies, []):
         copy.start()
     return copies
 
@@ -415,7 +415,7 @@
     sources, targets = refs[:count], refs[count : 2 * count]
     offsets_ref, *table_refs, destinations_ref, joined_ref, hidden_ref = refs[2 * count : -3]
     attention_scr, feedforward_scr, sems = refs[-3:]
-    copies = copies_in(sources, targets, sems, 7)
+    copies = copies_in(sources, targets, sems)
     segments_ref, targets_ref, states_ref, *gain_refs, heads_ref, upward_ref, _ = targets
     block_rows = states_ref.shape[0]
     wait_for(copies[0])
@@ -426,8 +426,6 @@
         wait_for(copies[number])
     normalize([states_ref], gain_refs, [attention_scr, feedforward_scr])
     wait_for(copies[5])
-    for copy in copies[7]:
-        copy.start()
     places = [position_of(0, 0, block_rows)]
     project(attention_scr, heads_ref, table_refs, places, joined_ref, 0)
     wait_for(copies[6])
@@ -856,7 +854,7 @@
     passing = exchanged(third_sum, "tensor", to_chip[1])
     far_received = exchanged(far_sibling, "tensor", 1)
     pages = cached_pages(joined, destinations, replica_count)
-    early, late = (3,), (1, 2)
+    early, late = (3,), (2, 1)
     arriving = [exchanged(pages[mask], "dp", mask) for mask in early]
     first_sum, base = near_sums(near_received, owns[:2], hidden)
     from_first = exchanged(first_sum, "tensor", to_chip[1])

time: 38.5 us -> 37.9 us (0.984)
  waiting for transfers between devices: 6.61 us -> 5.8 us
  starting transfers between devices: 17.3 us -> 17.8 us
    ppermute x16, waiting for transfers between devices: 6.61 us -> 5.8 us  [exchanged(): lax.ppermute(block, axis, [(member, member ^ mask) for member in range(co...]
    ppermute x16, starting transfers between devices: 17.3 us -> 17.8 us  [exchanged(): lax.ppermute(block, axis, [(member, member ^ mask) for member in range(co...]
where the time goes in v16:
time: 37.9 us; the launch traced here: 37.8 us
  starting transfers between devices  17.8 us (47%)
  Pallas kernels  13.5 us (36%)
  waiting for transfers between devices  5.8 us (15%)
  between operations  0.73 us (2%)
    ppermute x16, starting transfers between devices, exchanged(): lax.ppermute(block, axis, [(member, member ^ mask) for member in range(co...  17.8 us
    ppermute x16, waiting for transfers between devices, exchanged(): lax.ppermute(block, axis, [(member, member ^ mask) for member in range(co...  5.8 us
    pallas_call x1, Pallas kernels, own_rows(): pl.pallas_call(functools.partial(own_kernel, count, replica_count), out_s...  5.27 us
    pallas_call x1, Pallas kernels, last_rows(): pl.pallas_call(last_kernel, out_shape=[pltpu.VMEM((tokens, 3 * HD), jnp.b...  2.41 us
    pallas_call x1, Pallas kernels, middle_rows(): pl.pallas_call(functools.partial(middle_kernel, origins), out_shape=[pltp...  2.12 us
    pallas_call x1, Pallas kernels, fed_rows(): pl.pallas_call(fed_kernel, out_shape=[pltpu.VMEM((rows, width), jnp.float...  0.9 us
    pallas_call x1, Pallas kernels, finished(): pl.pallas_call(functools.partial(finish_kernel, masks), out_shape=[jax.Sh...  0.82 us
    pallas_call x1, Pallas kernels, rest_rows(): pl.pallas_call(rest_kernel, out_shape=shapes, in_specs=vmem_specs(5), out...  0.79 us
  transfers between devices with their start and end apart: 16, of which 6 were waited for; matrix products, arithmetic and copies ran while one was open for 0% of the time, Pallas kernels for 27%

profile of v16, /device:TPU:0, one launch (start us, length us, event | category | flops | bytes accessed | tf_op | source)
XLA Modules:
  0.0 37.8 jit_solution(9533233201071144397)
XLA Ops:
  0.6 4.1 %collective-permute-start.1 = (bf16[32,2048]{1,0:T(8,128)(2,1)}, bf16[32,2048]{1,0:T(8,128)(2,1)S(1)}, u32[]{:S(2)}, u32[]{:S(2)}) collective-permute-start(bf16[32,2048]{1,0:T(8,128)(2,1)} %refs_2_.1), channel_id=1, source_target_pairs={{0,4},{1,5},{2,6},{3,7},{4,0},{5,1},{6,2},{7,3},{8,12},{9,13},{10,... | collective-permute-start | bytes 393224 | tf_op jit(solution)/shard_map/ppermute | solution.py:235
  4.7 1.6 %collective-permute-start = (bf16[32,2048]{1,0:T(8,128)(2,1)}, bf16[32,2048]{1,0:T(8,128)(2,1)S(1)}, u32[]{:S(2)}, u32[]{:S(2)}) collective-permute-start(bf16[32,2048]{1,0:T(8,128)(2,1)} %refs_2_.1), channel_id=1, source_target_pairs={{0,2},{1,3},{2,0},{3,1},{4,6},{5,7},{6,4},{7,5},{8,10},{9,11},{10,... | collective-permute-start | bytes 393224 | tf_op jit(solution)/shard_map/ppermute | solution.py:235
  6.3 0.0 collective-permute-start.3
  6.3 5.3 %own_rows.1 = (s32[1,256]{1,0:T(1,128)}, s32[1,16]{1,0:T(1,128)}, bf16[32,2048]{1,0:T(8,128)(2,1)S(1)}, f32[1,2048]{1,0:T(1,128)S(1)}, f32[1,2048]{1,0:T(1,128)S...) custom-call(s32[1,256]{1,0:T(1,128)} %refs_0_.1, ...), custom_call_target="tpu_custom_call" | custom-call | flops 234881024 | bytes 11682880 | tf_op jit(solution)/shard_map/own_rows/pallas_call | solution.py:448
  11.6 0.0 collective-permute-done.1.refs_3_
  11.6 0.0 collective-permute-done.refs_1_
  11.6 0.6 %collective-permute-start.4 = (bf16[32,2048]{1,0:T(8,128)(2,1)S(1)}, bf16[32,2048]{1,0:T(8,128)(2,1)S(1)}, u32[]{:S(2)}, u32[]{:S(2)}) collective-permute-start(bf16[32,2048]{1,0:T(8,128)(2,1)S(1)} %collective-permute-done.refs_1_), channel_id=1, source_target_pairs={{0,1},{1,0},{2,3},{3,2},{4,5},{5,4},{6,7},{7,6},{8,9},{9,8},{10,11... | collective-permute-start | bytes 393224 | tf_op jit(solution)/shard_map/ppermute | solution.py:235
  12.2 0.8 %collective-permute-start.2 = (bf16[32,2048]{1,0:T(8,128)(2,1)S(1)}, bf16[32,2048]{1,0:T(8,128)(2,1)S(1)}, u32[]{:S(2)}, u32[]{:S(2)}) collective-permute-start(bf16[32,2048]{1,0:T(8,128)(2,1)S(1)} %collective-permute-done.1.refs_3_), channel_id=1, source_target_pairs={{0,2},{1,3},{2,0},{3,1},{4,6},{5,7},{6,4},{7,5},{8,10},{9,11},{10,... | collective-permute-start | bytes 393224 | tf_op jit(solution)/shard_map/ppermute | solution.py:235
  13.0 0.2 collective-permute-done.4.refs_2_
  13.2 2.1 %middle_rows.1 = (bf16[128,768]{1,0:T(8,128)(2,1)S(1)}, bf16[128,1024]{1,0:T(8,128)(2,1)S(1)}, bf16[256,2048]{1,0:T(8,128)(2,1)S(1)}) custom-call(bf16[32,2048]{1,0:T(8,128)(2,1)S(1)} %collective-permute-done.3.refs_0_, bf16[32,2048]{1,0:T(8,128)(2,1)S(1)} %collective-permute-done.refs_1_, bf16[32,2048]{1,0:T(8,128)(2,1)S(1)} %collective-permute-done.4.refs_2_, ...), custom_call_target="tpu_custom_call" | custom-call | flops 939524096 | bytes 1048576 | tf_op jit(solution)/shard_map/middle_rows/pallas_call | solution.py:488
  15.3 0.4 %collective-permute-start.5 = (bf16[32,2048]{1,0:T(8,128)(2,1)S(1)}, bf16[32,2048]{1,0:T(8,128)(2,1)S(1)}, u32[]{:S(2)}, u32[]{:S(2)}) collective-permute-start(bf16[32,2048]{1,0:T(8,128)(2,1)S(1)} %collective-permute-done.1.refs_3_), channel_id=1, source_target_pairs={{0,1},{1,0},{2,3},{3,2},{4,5},{5,4},{6,7},{7,6},{8,9},{9,8},{10,11... | collective-permute-start | bytes 393224 | tf_op jit(solution)/shard_map/ppermute | solution.py:235
  15.7 1.9 %collective-permute-done.2.refs_1_ = bf16[32,2048]{1,0:T(8,128)(2,1)S(1)} collective-permute-done((bf16[32,2048]{1,0:T(8,128)(2,1)S(1)}, bf16[32,2048]{1,0:T(8,128)(2,1)S(1)}, u32[]{:S(2)}, u32[]{:S(2)}) %collective-permute-start.2) | collective-permute-done | bytes 131104 | tf_op jit(solution)/shard_map/ppermute | solution.py:235
  17.7 0.0 collective-permute-done.5.refs_0_
  17.7 0.9 %fed_rows.1 = (f32[160,2048]{1,0:T(8,128)S(1)}, bf16[64,2048]{1,0:T(8,128)(2,1)S(1)}, bf16[64,2048]{1,0:T(8,128)(2,1)S(1)}) custom-call(bf16[32,1024]{1,0:T(8,128)(2,1)S(1)} %get-tuple-element.68.own_hidden_ref, bf16[128,1024]{1,0:T(8,128)(2,1)S(1)} %get-tuple-element.69.middle_hidden_ref, bf16[1024,2048]{1,0:T(8,128)(2,1)S(1)} %get-tuple-element.70.downward_ref.refs_7_, ...), custom_call_target="tpu_custom_call" | custom-call | flops 671088640 | bytes 1048576 | tf_op jit(solution)/shard_map/fed_rows/pallas_call | solution.py:593
  18.6 0.4 %collective-permute-done.6.refs_0_ = bf16[32,2048]{1,0:T(8,128)(2,1)S(1)} collective-permute-done((bf16[32,2048]{1,0:T(8,128)(2,1)S(1)}, bf16[32,2048]{1,0:T(8,128)(2,1)S(1)}, u32[]{:S(2)}, u32[]{:S(2)}) %collective-permute-start.6) | collective-permute-done | bytes 131104 | tf_op jit(solution)/shard_map/ppermute | solution.py:235
  19.0 2.4 %last_rows.1 = (bf16[256,768]{1,0:T(8,128)(2,1)S(1)}, f32[32,2048]{1,0:T(8,128)S(1)}, bf16[32,2048]{1,0:T(8,128)(2,1)S(1)}, f32[32,2048]{1,0:T(8,128)S(1)}) custom-call(bf16[32,2048]{1,0:T(8,128)(2,1)S(1)} %collective-permute-done.6.refs_0_, bf16[64,2048]{1,0:T(8,128)(2,1)S(1)} %get-tuple-element.72.refs_1_, bf16[64,2048]{1,0:T(8,128)(2,1)S(1)} %get-tuple-element.73.refs_2_, ...), custom_call_target="tpu_custom_call" | custom-call | flops 1207959552 | bytes 1048576 | tf_op jit(solution)/shard_map/last_rows/pallas_call | solution.py:552
  21.4 0.2 collective-permute-start.7
  21.6 0.8 %rest_rows.1 = (bf16[2,32,2048]{2,1,0:T(8,128)(2,1)S(1)}, bf16[32,2048]{1,0:T(8,128)(2,1)S(1)}, f32[32,2048]{1,0:T(8,128)S(1)}, f32[32,2048]{1,0:T(8,128)S(1)}, f32[32,2048]{1,0:T(8,128)S(1)}) custom-call(bf16[256,768]{1,0:T(8,128)(2,1)S(1)} %get-tuple-element.84.joined_ref, f32[256,128]{1,0:T(8,128)S(1)} %get-tuple-element.75.refs_9_.offsets_ref, ...), custom_call_target="tpu_custom_call" | custom-call | flops 201326592 | bytes 1048576 | tf_op jit(solution)/shard_map/rest_rows/pallas_call | solution.py:636
  22.4 0.4 %collective-permute-start.9 = (bf16[2,32,2048]{2,1,0:T(8,128)(2,1)S(1)}, bf16[2,32,2048]{2,1,0:T(8,128)(2,1)S(1)}, u32[]{:S(2)}, u32[]{:S(2)}) collective-permute-start(bf16[2,32,2048]{2,1,0:T(8,128)(2,1)S(1)} %get-tuple-element.88), channel_id=1, source_target_pairs={{0,1},{1,0},{2,3},{3,2},{4,5},{5,4},{6,7},{7,6},{8,9},{9,8},{10,11... | collective-permute-start | bytes 786440 | tf_op jit(solution)/shard_map/ppermute | solution.py:235
  22.9 1.3 %collective-permute-start.11 = (bf16[32,2048]{1,0:T(8,128)(2,1)S(1)}, bf16[32,2048]{1,0:T(8,128)(2,1)S(1)}, u32[]{:S(2)}, u32[]{:S(2)}) collective-permute-start(bf16[32,2048]{1,0:T(8,128)(2,1)S(1)} %third_added.1), channel_id=1, source_target_pairs={{0,2},{1,3},{2,0},{3,1},{4,6},{5,7},{6,4},{7,5},{8,10},{9,11},{10,... | collective-permute-start | bytes 393224 | tf_op jit(solution)/shard_map/ppermute | solution.py:235
  24.2 0.3 cached_pages.1
  24.5 2.5 %collective-permute-start.8 = (bf16[8,16,512]{2,1,0:T(8,128)(2,1)S(1)}, bf16[8,16,512]{2,1,0:T(8,128)(2,1)S(1)}, u32[]{:S(2)}, u32[]{:S(2)}) collective-permute-start(bf16[8,16,512]{2,1,0:T(8,128)(2,1)S(1)} %get-tuple-element.87), channel_id=1, source_target_pairs={{0,24},{8,16},{16,8},{24,0},{1,25},{9,17},{17,9},{25,1},{2,26},{10... | collective-permute-start | bytes 393224 | tf_op jit(solution)/shard_map/ppermute | solution.py:235
  27.0 0.1 near_sums.1
  27.1 0.9 %collective-permute-start.10 = (bf16[32,2048]{1,0:T(8,128)(2,1)S(1)}, bf16[32,2048]{1,0:T(8,128)(2,1)S(1)}, u32[]{:S(2)}, u32[]{:S(2)}) collective-permute-start(bf16[32,2048]{1,0:T(8,128)(2,1)S(1)} %get-tuple-element.92), channel_id=1, source_target_pairs={{0,2},{1,3},{2,0},{3,1},{4,6},{5,7},{6,4},{7,5},{8,10},{9,11},{10,... | collective-permute-start | bytes 393224 | tf_op jit(solution)/shard_map/ppermute | solution.py:235
  28.0 0.6 %collective-permute-done.11.refs_1_ = bf16[32,2048]{1,0:T(8,128)(2,1)S(1)} collective-permute-done((bf16[32,2048]{1,0:T(8,128)(2,1)S(1)}, bf16[32,2048]{1,0:T(8,128)(2,1)S(1)}, u32[]{:S(2)}, u32[]{:S(2)}) %collective-permute-start.11) | collective-permute-done | bytes 131104 | tf_op jit(solution)/shard_map/ppermute | solution.py:235
  28.6 1.9 %collective-permute-start.13 = (bf16[32,2048]{1,0:T(8,128)(2,1)S(1)}, bf16[32,2048]{1,0:T(8,128)(2,1)S(1)}, u32[]{:S(2)}, u32[]{:S(2)}) collective-permute-start(bf16[32,2048]{1,0:T(8,128)(2,1)S(1)} %second_added.1), channel_id=1, source_target_pairs={{0,4},{1,5},{2,6},{3,7},{4,0},{5,1},{6,2},{7,3},{8,12},{9,13},{10,... | collective-permute-start | bytes 393224 | tf_op jit(solution)/shard_map/ppermute | solution.py:235
  30.5 1.5 %collective-permute-start.14 = (bf16[8,16,512]{2,1,0:T(8,128)(2,1)S(1)}, bf16[8,16,512]{2,1,0:T(8,128)(2,1)S(1)}, u32[]{:S(2)}, u32[]{:S(2)}) collective-permute-start(bf16[8,16,512]{2,1,0:T(8,128)(2,1)S(1)} %get-tuple-element.101), channel_id=1, source_target_pairs={{0,16},{8,24},{16,0},{24,8},{1,17},{9,25},{17,1},{25,9},{2,18},{10... | collective-permute-start | bytes 393224 | tf_op jit(solution)/shard_map/ppermute | solution.py:235
  32.0 1.5 %collective-permute-start.15 = (bf16[8,16,512]{2,1,0:T(8,128)(2,1)S(1)}, bf16[8,16,512]{2,1,0:T(8,128)(2,1)S(1)}, u32[]{:S(2)}, u32[]{:S(2)}) collective-permute-start(bf16[8,16,512]{2,1,0:T(8,128)(2,1)S(1)} %get-tuple-element.102), channel_id=1, source_target_pairs={{0,8},{8,0},{16,24},{24,16},{1,9},{9,1},{17,25},{25,17},{2,10},{10... | collective-permute-start | bytes 393224 | tf_op jit(solution)/shard_map/ppermute | solution.py:235
  33.5 2.1 %collective-permute-done.10.refs_2_ = bf16[32,2048]{1,0:T(8,128)(2,1)S(1)} collective-permute-done((bf16[32,2048]{1,0:T(8,128)(2,1)S(1)}, bf16[32,2048]{1,0:T(8,128)(2,1)S(1)}, u32[]{:S(2)}, u32[]{:S(2)}) %collective-permute-start.10) | collective-permute-done | bytes 131104 | tf_op jit(solution)/shard_map/ppermute | solution.py:235
  35.6 0.7 %placed.1 = (bf16[1,4,8,16,512]{4,3,2,1,0:T(8,128)(2,1)}, f32[32,2048]{1,0:T(8,128)S(1)}) custom-call(bf16[8,16,512]{2,1,0:T(8,128)(2,1)S(1)} %get-tuple-element.86.refs_0_, bf16[8,16,512]{2,1,0:T(8,128)(2,1)S(1)} %collective-permute-done.8.refs_1_, bf16[32,2048]{1,0:T(8,128)(2,1)S(1)} %collective-permute-done.10.refs_2_, ...), custom_call_target="tpu_custom_call" | custom-call | tf_op jit(solution)/shard_map/placed/pallas_call | solution.py:731
  36.4 0.6 %collective-permute-done.15.refs_2_ = bf16[8,16,512]{2,1,0:T(8,128)(2,1)S(1)} collective-permute-done((bf16[8,16,512]{2,1,0:T(8,128)(2,1)S(1)}, bf16[8,16,512]{2,1,0:T(8,128)(2,1)S(1)}, u32[]{:S(2)}, u32[]{:S(2)}) %collective-permute-start.15) | collective-permute-done | bytes 131104 | tf_op jit(solution)/shard_map/ppermute | solution.py:235
  37.0 0.8 %finished.1 = (f32[32,2048]{1,0:T(8,128)}, bf16[1,4,8,16,512]{4,3,2,1,0:T(8,128)(2,1)}) custom-call(f32[32,2048]{1,0:T(8,128)S(1)} %get-tuple-element.94.base_ref, bf16[32,2048]{1,0:T(8,128)(2,1)S(1)} %collective-permute-done.13.refs_0_, bf16[8,16,512]{2,1,0:T(8,128)(2,1)S(1)} %collective-permute-done.14.refs_1_, ...), custom_call_target="tpu_custom_call", output_to_operand_aliasing={{1}: (4, {})} | custom-call | tf_op jit(solution)/shard_map/finished/pallas_call | solution.py:768
  (11 shorter events, 0.1 us)
Async XLA Ops:
  0.6 11.0 %collective-permute-start.1 = (bf16[32,2048]{1,0:T(8,128)(2,1)}, bf16[32,2048]{1,0:T(8,128)(2,1)S(1)}, u32[]{:S(2)}, u32[]{:S(2)}) collective-permute-start(bf16[32,2048]{1,0:T(8,128)(2,1)} %refs_2_.1), channel_id=1, source_target_pairs={{0,4},{1,5},{2,6},{3,7},{4,0},{5,1},{6,2},{7,3},{8,12},{9,13},{10,... | collective-permute-start | bytes 393224 | tf_op jit(solution)/shard_map/ppermute | solution.py:235
  4.7 6.9 %collective-permute-start = (bf16[32,2048]{1,0:T(8,128)(2,1)}, bf16[32,2048]{1,0:T(8,128)(2,1)S(1)}, u32[]{:S(2)}, u32[]{:S(2)}) collective-permute-start(bf16[32,2048]{1,0:T(8,128)(2,1)} %refs_2_.1), channel_id=1, source_target_pairs={{0,2},{1,3},{2,0},{3,1},{4,6},{5,7},{6,4},{7,5},{8,10},{9,11},{10,... | collective-permute-start | bytes 393224 | tf_op jit(solution)/shard_map/ppermute | solution.py:235
  6.3 6.7 %collective-permute-start.3 = (bf16[32,2048]{1,0:T(8,128)(2,1)}, bf16[32,2048]{1,0:T(8,128)(2,1)S(1)}, u32[]{:S(2)}, u32[]{:S(2)}) collective-permute-start(bf16[32,2048]{1,0:T(8,128)(2,1)} %refs_2_.1), channel_id=1, source_target_pairs={{0,1},{1,0},{2,3},{3,2},{4,5},{5,4},{6,7},{7,6},{8,9},{9,8},{10,11... | collective-permute-start | bytes 393224 | tf_op jit(solution)/shard_map/ppermute | solution.py:235
  11.6 1.6 %collective-permute-start.4 = (bf16[32,2048]{1,0:T(8,128)(2,1)S(1)}, bf16[32,2048]{1,0:T(8,128)(2,1)S(1)}, u32[]{:S(2)}, u32[]{:S(2)}) collective-permute-start(bf16[32,2048]{1,0:T(8,128)(2,1)S(1)} %collective-permute-done.refs_1_), channel_id=1, source_target_pairs={{0,1},{1,0},{2,3},{3,2},{4,5},{5,4},{6,7},{7,6},{8,9},{9,8},{10,11... | collective-permute-start | bytes 393224 | tf_op jit(solution)/shard_map/ppermute | solution.py:235
  12.2 5.5 %collective-permute-start.2 = (bf16[32,2048]{1,0:T(8,128)(2,1)S(1)}, bf16[32,2048]{1,0:T(8,128)(2,1)S(1)}, u32[]{:S(2)}, u32[]{:S(2)}) collective-permute-start(bf16[32,2048]{1,0:T(8,128)(2,1)S(1)} %collective-permute-done.1.refs_3_), channel_id=1, source_target_pairs={{0,2},{1,3},{2,0},{3,1},{4,6},{5,7},{6,4},{7,5},{8,10},{9,11},{10,... | collective-permute-start | bytes 393224 | tf_op jit(solution)/shard_map/ppermute | solution.py:235
  15.3 2.4 %collective-permute-start.5 = (bf16[32,2048]{1,0:T(8,128)(2,1)S(1)}, bf16[32,2048]{1,0:T(8,128)(2,1)S(1)}, u32[]{:S(2)}, u32[]{:S(2)}) collective-permute-start(bf16[32,2048]{1,0:T(8,128)(2,1)S(1)} %collective-permute-done.1.refs_3_), channel_id=1, source_target_pairs={{0,1},{1,0},{2,3},{3,2},{4,5},{5,4},{6,7},{7,6},{8,9},{9,8},{10,11... | collective-permute-start | bytes 393224 | tf_op jit(solution)/shard_map/ppermute | solution.py:235
  17.7 1.3 %collective-permute-start.6 = (bf16[32,2048]{1,0:T(8,128)(2,1)S(1)}, bf16[32,2048]{1,0:T(8,128)(2,1)S(1)}, u32[]{:S(2)}, u32[]{:S(2)}) collective-permute-start(bf16[32,2048]{1,0:T(8,128)(2,1)S(1)} %collective-permute-done.2.refs_1_), channel_id=1, source_target_pairs={{0,1},{1,0},{2,3},{3,2},{4,5},{5,4},{6,7},{7,6},{8,9},{9,8},{10,11... | collective-permute-start | bytes 393224 | tf_op jit(solution)/shard_map/ppermute | solution.py:235
  21.4 1.4 %collective-permute-start.7 = (bf16[32,2048]{1,0:T(8,128)(2,1)S(1)}, bf16[32,2048]{1,0:T(8,128)(2,1)S(1)}, u32[]{:S(2)}, u32[]{:S(2)}) collective-permute-start(bf16[32,2048]{1,0:T(8,128)(2,1)S(1)} %get-tuple-element.79), channel_id=1, source_target_pairs={{0,1},{1,0},{2,3},{3,2},{4,5},{5,4},{6,7},{7,6},{8,9},{9,8},{10,11... | collective-permute-start | bytes 393224 | tf_op jit(solution)/shard_map/ppermute | solution.py:235
  22.4 4.6 %collective-permute-start.9 = (bf16[2,32,2048]{2,1,0:T(8,128)(2,1)S(1)}, bf16[2,32,2048]{2,1,0:T(8,128)(2,1)S(1)}, u32[]{:S(2)}, u32[]{:S(2)}) collective-permute-start(bf16[2,32,2048]{2,1,0:T(8,128)(2,1)S(1)} %get-tuple-element.88), channel_id=1, source_target_pairs={{0,1},{1,0},{2,3},{3,2},{4,5},{5,4},{6,7},{7,6},{8,9},{9,8},{10,11... | collective-permute-start | bytes 786440 | tf_op jit(solution)/shard_map/ppermute | solution.py:235
  22.9 5.6 %collective-permute-start.11 = (bf16[32,2048]{1,0:T(8,128)(2,1)S(1)}, bf16[32,2048]{1,0:T(8,128)(2,1)S(1)}, u32[]{:S(2)}, u32[]{:S(2)}) collective-permute-start(bf16[32,2048]{1,0:T(8,128)(2,1)S(1)} %third_added.1), channel_id=1, source_target_pairs={{0,2},{1,3},{2,0},{3,1},{4,6},{5,7},{6,4},{7,5},{8,10},{9,11},{10,... | collective-permute-start | bytes 393224 | tf_op jit(solution)/shard_map/ppermute | solution.py:235
  24.2 4.3 %collective-permute-start.12 = (bf16[32,2048]{1,0:T(8,128)(2,1)S(1)}, bf16[32,2048]{1,0:T(8,128)(2,1)S(1)}, u32[]{:S(2)}, u32[]{:S(2)}) collective-permute-start(bf16[32,2048]{1,0:T(8,128)(2,1)S(1)} %get-tuple-element.97), channel_id=1, source_target_pairs={{0,1},{1,0},{2,3},{3,2},{4,5},{5,4},{6,7},{7,6},{8,9},{9,8},{10,11... | collective-permute-start | bytes 393224 | tf_op jit(solution)/shard_map/ppermute | solution.py:235
  24.5 9.0 %collective-permute-start.8 = (bf16[8,16,512]{2,1,0:T(8,128)(2,1)S(1)}, bf16[8,16,512]{2,1,0:T(8,128)(2,1)S(1)}, u32[]{:S(2)}, u32[]{:S(2)}) collective-permute-start(bf16[8,16,512]{2,1,0:T(8,128)(2,1)S(1)} %get-tuple-element.87), channel_id=1, source_target_pairs={{0,24},{8,16},{16,8},{24,0},{1,25},{9,17},{17,9},{25,1},{2,26},{10... | collective-permute-start | bytes 393224 | tf_op jit(solution)/shard_map/ppermute | solution.py:235
  27.1 8.5 %collective-permute-start.10 = (bf16[32,2048]{1,0:T(8,128)(2,1)S(1)}, bf16[32,2048]{1,0:T(8,128)(2,1)S(1)}, u32[]{:S(2)}, u32[]{:S(2)}) collective-permute-start(bf16[32,2048]{1,0:T(8,128)(2,1)S(1)} %get-tuple-element.92), channel_id=1, source_target_pairs={{0,2},{1,3},{2,0},{3,1},{4,6},{5,7},{6,4},{7,5},{8,10},{9,11},{10,... | collective-permute-start | bytes 393224 | tf_op jit(solution)/shard_map/ppermute | solution.py:235
  28.6 7.8 %collective-permute-start.13 = (bf16[32,2048]{1,0:T(8,128)(2,1)S(1)}, bf16[32,2048]{1,0:T(8,128)(2,1)S(1)}, u32[]{:S(2)}, u32[]{:S(2)}) collective-permute-start(bf16[32,2048]{1,0:T(8,128)(2,1)S(1)} %second_added.1), channel_id=1, source_target_pairs={{0,4},{1,5},{2,6},{3,7},{4,0},{5,1},{6,2},{7,3},{8,12},{9,13},{10,... | collective-permute-start | bytes 393224 | tf_op jit(solution)/shard_map/ppermute | solution.py:235
  30.5 5.9 %collective-permute-start.14 = (bf16[8,16,512]{2,1,0:T(8,128)(2,1)S(1)}, bf16[8,16,512]{2,1,0:T(8,128)(2,1)S(1)}, u32[]{:S(2)}, u32[]{:S(2)}) collective-permute-start(bf16[8,16,512]{2,1,0:T(8,128)(2,1)S(1)} %get-tuple-element.101), channel_id=1, source_target_pairs={{0,16},{8,24},{16,0},{24,8},{1,17},{9,25},{17,1},{25,9},{2,18},{10... | collective-permute-start | bytes 393224 | tf_op jit(solution)/shard_map/ppermute | solution.py:235
  32.0 5.0 %collective-permute-start.15 = (bf16[8,16,512]{2,1,0:T(8,128)(2,1)S(1)}, bf16[8,16,512]{2,1,0:T(8,128)(2,1)S(1)}, u32[]{:S(2)}, u32[]{:S(2)}) collective-permute-start(bf16[8,16,512]{2,1,0:T(8,128)(2,1)S(1)} %get-tuple-element.102), channel_id=1, source_target_pairs={{0,8},{8,0},{16,24},{24,16},{1,9},{9,1},{17,25},{25,17},{2,10},{10... | collective-permute-start | bytes 393224 | tf_op jit(solution)/shard_map/ppermute | solution.py:235

commit v17 on v16

--- a/solution.py
+++ b/solution.py
@@ -248,6 +248,10 @@
     return member // CORES, member % CORES
 
 
+def kind_at(stand):
+    return stand ^ (stand >> 1)
+
+
 def position_of(kind, half, block_rows):
     chip, core = whereabouts()
     return ((chip ^ kind) * CORES + (core ^ half)) * block_rows
@@ -257,7 +261,7 @@
     chip, core = whereabouts()
     bits = block_rows.bit_length() - 1
     place = first + lax.broadcasted_iota(jnp.int32, shape, axis)
-    kind = place >> (bits + 1)
+    kind = kind_at(place >> (bits + 1))
     half = (place >> bits) & 1
     return ((((chip ^ kind) << 1) | (core ^ half)) << bits) | (place & (block_rows - 1))
 
@@ -320,7 +324,7 @@
 def attend(joined_ref, offsets_ref, first, rows, block_rows):
     tokens = joined_ref.shape[0]
     starts = [
-        position_of(place // (2 * block_rows), (place // block_rows) % 2, block_rows)
+        position_of(kind_at(place // (2 * block_rows)), (place // block_rows) % 2, block_rows)
         for place in range(first, first + rows, block_rows)
     ]
     reach = jnp.concatenate(
@@ -514,9 +518,9 @@
     block_ref, *normed_refs = refs[:3]
     gain_a, gain_f, heads_ref, upward_ref, downward_ref, output_ref = refs[3:9]
     offsets_ref, *table_refs = refs[9:13]
-    own_joined_ref, middle_joined_ref = refs[13:15]
-    joined_ref, fed_ref, sibling_ref, own_ref = refs[15:19]
-    attention_scr, feedforward_scr, hidden_scr = refs[19:]
+    own_joined_ref, middle_joined_ref, early_ref = refs[13:16]
+    joined_ref, fed_ref, sibling_ref, own_ref = refs[16:20]
+    attention_scr, feedforward_scr, hidden_scr = refs[20:]
     block_rows = block_ref.shape[0]
     tokens = joined_ref.shape[0]
     first = tokens - attention_scr.shape[0]
@@ -526,25 +530,24 @@
         normed_scr[:count, :] = normed_ref[...]
     joined_ref[:block_rows, :] = own_joined_ref[...]
     joined_ref[block_rows:first, :] = middle_joined_ref[...]
-    origins = ((CHIPS - 2, 1), (CHIPS - 1, 0), (CHIPS - 1, 1))
+    origins = ((3, 1), (2, 0), (2, 1))
     places = [position_of(kind, half, block_rows) for kind, half in origins]
     project(attention_scr, heads_ref, table_refs, places, joined_ref, first)
     rows = CORES * block_rows
     hide(feedforward_scr, upward_ref, hidden_scr, 0, 512)
-    attended = attend(joined_ref, offsets_ref, tokens - rows, rows, block_rows)
+    attended = attend(joined_ref, offsets_ref, first - block_rows, rows, block_rows)
     chunk = 1024
     for begin in range(0, downward_ref.shape[1], chunk):
         columns = slice(begin, begin + chunk)
         fed = jnp.dot(hidden_scr[...], downward_ref[:, columns], preferred_element_type=jnp.float32)
-        fed_ref[:, columns] = fed[:block_rows]
-        partial = fed[block_rows:] + jnp.dot(
-            attended, output_ref[:, columns], preferred_element_type=jnp.float32
-        )
-        own_ref[:, columns] = partial[:block_rows]
-        sibling_ref[:, columns] = partial[block_rows:].astype(jnp.bfloat16)
-
-
-def last_rows(block, normed, gains, weights, tables, own_joined, middle_joined):
+        fed_ref[:, columns] = fed[block_rows:]
+        product = jnp.dot(attended, output_ref[:, columns], preferred_element_type=jnp.float32)
+        own_ref[:, columns] = early_ref[first - block_rows :, columns] + product[:block_rows]
+        sibling = fed[:block_rows] + product[block_rows:]
+        sibling_ref[:, columns] = sibling.astype(jnp.bfloat16)
+
+
+def last_rows(block, normed, gains, weights, tables, own_joined, middle_joined, early):
     block_rows, width = block.shape
     rows = normed[0].shape[0] + block_rows
     hidden_width = weights[1].shape[1]
@@ -553,11 +556,11 @@
         last_kernel,
         out_shape=[
             pltpu.VMEM((tokens, 3 * HD), jnp.bfloat16),
-            pltpu.VMEM((block_rows, width), jnp.float32),
+            pltpu.VMEM((CORES * block_rows, width), jnp.float32),
             pltpu.VMEM((block_rows, width), jnp.bfloat16),
             pltpu.VMEM((block_rows, width), jnp.float32),
         ],
-        in_specs=vmem_specs(1 + 2 + 2 + 4 + 4 + 2),
+        in_specs=vmem_specs(1 + 2 + 2 + 4 + 4 + 3),
         out_specs=vmem_specs(4),
         scratch_shapes=[
             pltpu.VMEM((rows, width), jnp.bfloat16),
@@ -571,7 +574,7 @@
             transcendentals=rows * hidden_width,
         ),
         name="last_rows",
-    )(block, *normed, *gains, *weights, *tables, own_joined, middle_joined)
+    )(block, *normed, *gains, *weights, *tables, own_joined, middle_joined, early)
 
 
 def fed_kernel(own_hidden_ref, middle_hidden_ref, downward_ref, *refs):
@@ -603,15 +606,23 @@
     )(own_hidden, middle_hidden, downward_weight, *blocks, *gains)
 
 
-def rest_kernel(joined_ref, offsets_ref, output_ref, fed_ref, fed_beside_ref, *refs):
+def rest_kernel(joined_ref, offsets_ref, output_ref, early_ref, late_ref, *refs):
     near_ref, far_ref, *owns = refs
     block_rows = far_ref.shape[0]
-    rows = fed_ref.shape[0] + fed_beside_ref.shape[0]
-    attended = attend(joined_ref, offsets_ref, 0, rows, block_rows)
+    late = CORES * block_rows
+    early = late * near_ref.shape[0]
+    tokens = joined_ref.shape[0]
+    attended = jnp.concatenate(
+        [
+            attend(joined_ref, offsets_ref, 0, early, block_rows),
+            attend(joined_ref, offsets_ref, tokens - late, late, block_rows),
+        ],
+        0,
+    )
     chunk = 512
     for begin in range(0, output_ref.shape[1], chunk):
         columns = slice(begin, begin + chunk)
-        fed = jnp.concatenate([fed_ref[:, columns], fed_beside_ref[:, columns]], 0)
+        fed = jnp.concatenate([early_ref[:early, columns], late_ref[:, columns]], 0)
         partial = fed + jnp.dot(
             attended, output_ref[:, columns], preferred_element_type=jnp.float32
         )
@@ -626,10 +637,10 @@
                 far_ref[:, columns] = sibling
 
 
-def rest_rows(joined, offsets, output_weight, fed, fed_beside):
-    width = fed.shape[1]
-    rows = fed.shape[0] + fed_beside.shape[0]
+def rest_rows(joined, offsets, output_weight, early, late):
+    width = early.shape[1]
     count = CHIPS - 1
+    rows = late.shape[0] * count
     shape = (rows // (CORES * count), width)
     shapes = [pltpu.VMEM((count - 1, *shape), jnp.bfloat16), pltpu.VMEM(shape, jnp.bfloat16)]
     shapes += [pltpu.VMEM(shape, jnp.float32)] * count
@@ -645,7 +656,7 @@
             transcendentals=rows * joined.shape[0],
         ),
         name="rest_rows",
-    )(joined, offsets, output_weight, fed, fed_beside)
+    )(joined, offsets, output_weight, early, late)
 
 
 def pages_kernel(joined_ref, destinations_ref, *page_refs):
@@ -798,7 +809,7 @@
 ):
     replica_count = lax.axis_size("dp")
     to_chip = [mask * CORES for mask in range(CHIPS)]
-    second = exchanged(hidden_states, "tensor", to_chip[2])
+    third = exchanged(hidden_states, "tensor", to_chip[3])
     first = exchanged(hidden_states, "tensor", to_chip[1])
     beside = exchanged(hidden_states, "tensor", 1)
     staged = (
@@ -816,37 +827,38 @@
     heads, upward, downward = weights
     destinations, own_joined, own_hidden = staged[12:]
 
-    first, second, own_joined = lax.optimization_barrier((first, second, own_joined))
+    first, third, own_joined = lax.optimization_barrier((first, third, own_joined))
     first_beside = exchanged(first, "tensor", 1)
-    third = exchanged(second, "tensor", to_chip[1])
+    second = exchanged(third, "tensor", to_chip[1])
     middle_joined, middle_hidden, output = middle_rows(
         "middle_rows",
-        ((0, 1), (1, 0), (1, 1), (2, 0)),
-        (beside, first, first_beside, second),
+        ((0, 1), (1, 0), (1, 1), (3, 0)),
+        (beside, first, first_beside, third),
         gains,
         (heads, upward),
         tables[1:],
         output_weight,
     )
-    second, middle_joined = lax.optimization_barrier((second, middle_joined))
+    third, middle_joined = lax.optimization_barrier((third, middle_joined))
+    third_beside = exchanged(third, "tensor", 1)
+    second, third_beside, middle_joined, middle_hidden = lax.optimization_barrier(
+        (second, third_beside, middle_joined, middle_hidden)
+    )
     second_beside = exchanged(second, "tensor", 1)
-    third, second_beside, middle_joined, middle_hidden = lax.optimization_barrier(
-        (third, second_beside, middle_joined, middle_hidden)
-    )
-    third_beside = exchanged(third, "tensor", 1)
-    fed, *normed = fed_rows(own_hidden, middle_hidden, downward, (second_beside, third), gains)
-    joined, fed_beside, sibling, own = last_rows(
-        third_beside,
+    fed, *normed = fed_rows(own_hidden, middle_hidden, downward, (third_beside, second), gains)
+    joined, fed_late, sibling, own = last_rows(
+        second_beside,
         normed,
         gains,
         (heads, upward, downward, output),
         tables,
         own_joined,
         middle_joined,
+        fed,
     )
 
     received = exchanged(sibling, "tensor", 1)
-    partials = rest_rows(joined, tables[0], output, fed, fed_beside)
+    partials = rest_rows(joined, tables[0], output, fed, fed_late)
     near_sibling, far_sibling, *owns = partials
     near_received = exchanged(near_sibling, "tensor", 1)
     third_sum = added("third_added", own, received)

time: 37.9 us -> 39 us (1.029)
  waiting for transfers between devices: 5.8 us -> 8.29 us
  starting transfers between devices: 17.8 us -> 16.1 us
    ppermute x16, waiting for transfers between devices: 5.8 us -> 8.29 us  [exchanged(): lax.ppermute(block, axis, [(member, member ^ mask) for member in range(co...]
    ppermute x16, starting transfers between devices: 17.8 us -> 16.1 us  [exchanged(): lax.ppermute(block, axis, [(member, member ^ mask) for member in range(co...]
where the time goes in v17:
time: 39 us; the launch traced here: 38.8 us
  starting transfers between devices  16.1 us (41%)
  Pallas kernels  13.7 us (35%)
  waiting for transfers between devices  8.29 us (21%)
  between operations  0.71 us (2%)
    ppermute x16, starting transfers between devices, exchanged(): lax.ppermute(block, axis, [(member, member ^ mask) for member in range(co...  16.1 us
    ppermute x16, waiting for transfers between devices, exchanged(): lax.ppermute(block, axis, [(member, member ^ mask) for member in range(co...  8.29 us
    pallas_call x1, Pallas kernels, own_rows(): pl.pallas_call(functools.partial(own_kernel, count, replica_count), out_s...  5.27 us
    pallas_call x1, Pallas kernels, last_rows(): pl.pallas_call(last_kernel, out_shape=[pltpu.VMEM((tokens, 3 * HD), jnp.b...  2.4 us
    pallas_call x1, Pallas kernels, middle_rows(): pl.pallas_call(functools.partial(middle_kernel, origins), out_shape=[pltp...  2.12 us
    pallas_call x1, Pallas kernels, rest_rows(): pl.pallas_call(rest_kernel, out_shape=shapes, in_specs=vmem_specs(5), out...  1 us
    pallas_call x1, Pallas kernels, fed_rows(): pl.pallas_call(fed_kernel, out_shape=[pltpu.VMEM((rows, width), jnp.float...  0.9 us
    pallas_call x1, Pallas kernels, finished(): pl.pallas_call(functools.partial(finish_kernel, masks), out_shape=[jax.Sh...  0.83 us
  transfers between devices with their start and end apart: 16, of which 6 were waited for; matrix products, arithmetic and copies ran while one was open for 0% of the time, Pallas kernels for 27%

profile of v17, /device:TPU:0, one launch (start us, length us, event | category | flops | bytes accessed | tf_op | source)
XLA Modules:
  0.0 38.8 jit_solution(10306294773418084863)
XLA Ops:
  0.6 5.1 %collective-permute-start.1 = (bf16[32,2048]{1,0:T(8,128)(2,1)}, bf16[32,2048]{1,0:T(8,128)(2,1)S(1)}, u32[]{:S(2)}, u32[]{:S(2)}) collective-permute-start(bf16[32,2048]{1,0:T(8,128)(2,1)} %refs_2_.1), channel_id=1, source_target_pairs={{0,6},{1,7},{2,4},{3,5},{4,2},{5,3},{6,0},{7,1},{8,14},{9,15},{10,... | collective-permute-start | bytes 393224 | tf_op jit(solution)/shard_map/ppermute | solution.py:235
  5.7 0.0 collective-permute-start
  5.8 0.0 collective-permute-start.3
  5.8 5.3 %own_rows.1 = (s32[1,256]{1,0:T(1,128)}, s32[1,16]{1,0:T(1,128)}, bf16[32,2048]{1,0:T(8,128)(2,1)S(1)}, f32[1,2048]{1,0:T(1,128)S(1)}, f32[1,2048]{1,0:T(1,128)S...) custom-call(s32[1,256]{1,0:T(1,128)} %refs_0_.1, ...), custom_call_target="tpu_custom_call" | custom-call | flops 234881024 | bytes 11682880 | tf_op jit(solution)/shard_map/own_rows/pallas_call | solution.py:452
  11.0 0.0 collective-permute-done.1.refs_3_
  11.0 1.3 %collective-permute-done.refs_1_ = bf16[32,2048]{1,0:T(8,128)(2,1)S(1)} collective-permute-done((bf16[32,2048]{1,0:T(8,128)(2,1)}, bf16[32,2048]{1,0:T(8,128)(2,1)S(1)}, u32[]{:S(2)}, u32[]{:S(2)}) %collective-permute-start) | collective-permute-done | bytes 131104 | tf_op jit(solution)/shard_map/ppermute | solution.py:235
  12.4 1.7 %collective-permute-start.2 = (bf16[32,2048]{1,0:T(8,128)(2,1)S(1)}, bf16[32,2048]{1,0:T(8,128)(2,1)S(1)}, u32[]{:S(2)}, u32[]{:S(2)}) collective-permute-start(bf16[32,2048]{1,0:T(8,128)(2,1)S(1)} %collective-permute-done.1.refs_3_), channel_id=1, source_target_pairs={{0,2},{1,3},{2,0},{3,1},{4,6},{5,7},{6,4},{7,5},{8,10},{9,11},{10,... | collective-permute-start | bytes 393224 | tf_op jit(solution)/shard_map/ppermute | solution.py:235
  14.1 0.0 collective-permute-done.3.refs_0_
  14.1 0.0 collective-permute-done.4.refs_2_
  14.1 2.1 %middle_rows.1 = (bf16[128,768]{1,0:T(8,128)(2,1)S(1)}, bf16[128,1024]{1,0:T(8,128)(2,1)S(1)}, bf16[256,2048]{1,0:T(8,128)(2,1)S(1)}) custom-call(bf16[32,2048]{1,0:T(8,128)(2,1)S(1)} %collective-permute-done.3.refs_0_, bf16[32,2048]{1,0:T(8,128)(2,1)S(1)} %collective-permute-done.refs_1_, bf16[32,2048]{1,0:T(8,128)(2,1)S(1)} %collective-permute-done.4.refs_2_, ...), custom_call_target="tpu_custom_call" | custom-call | flops 939524096 | bytes 1048576 | tf_op jit(solution)/shard_map/middle_rows/pallas_call | solution.py:492
  16.2 0.3 collective-permute-start.5
  16.5 1.8 %collective-permute-done.2.refs_1_ = bf16[32,2048]{1,0:T(8,128)(2,1)S(1)} collective-permute-done((bf16[32,2048]{1,0:T(8,128)(2,1)S(1)}, bf16[32,2048]{1,0:T(8,128)(2,1)S(1)}, u32[]{:S(2)}, u32[]{:S(2)}) %collective-permute-start.2) | collective-permute-done | bytes 131104 | tf_op jit(solution)/shard_map/ppermute | solution.py:235
  18.3 0.9 %fed_rows.1 = (f32[160,2048]{1,0:T(8,128)S(1)}, bf16[64,2048]{1,0:T(8,128)(2,1)S(1)}, bf16[64,2048]{1,0:T(8,128)(2,1)S(1)}) custom-call(bf16[32,1024]{1,0:T(8,128)(2,1)S(1)} %get-tuple-element.68.own_hidden_ref, bf16[128,1024]{1,0:T(8,128)(2,1)S(1)} %get-tuple-element.69.middle_hidden_ref, bf16[1024,2048]{1,0:T(8,128)(2,1)S(1)} %get-tuple-element.70.downward_ref.refs_7_, ...), custom_call_target="tpu_custom_call" | custom-call | flops 671088640 | bytes 1048576 | tf_op jit(solution)/shard_map/fed_rows/pallas_call | solution.py:596
  19.2 0.4 %collective-permute-done.6.refs_0_ = bf16[32,2048]{1,0:T(8,128)(2,1)S(1)} collective-permute-done((bf16[32,2048]{1,0:T(8,128)(2,1)S(1)}, bf16[32,2048]{1,0:T(8,128)(2,1)S(1)}, u32[]{:S(2)}, u32[]{:S(2)}) %collective-permute-start.6) | collective-permute-done | bytes 131104 | tf_op jit(solution)/shard_map/ppermute | solution.py:235
  19.6 2.4 %last_rows.1 = (bf16[256,768]{1,0:T(8,128)(2,1)S(1)}, f32[64,2048]{1,0:T(8,128)S(1)}, bf16[32,2048]{1,0:T(8,128)(2,1)S(1)}, f32[32,2048]{1,0:T(8,128)S(1)}) custom-call(bf16[32,2048]{1,0:T(8,128)(2,1)S(1)} %collective-permute-done.6.refs_0_, bf16[64,2048]{1,0:T(8,128)(2,1)S(1)} %get-tuple-element.72.refs_1_, bf16[64,2048]{1,0:T(8,128)(2,1)S(1)} %get-tuple-element.73.refs_2_, ...), custom_call_target="tpu_custom_call" | custom-call | flops 1207959552 | bytes 1048576 | tf_op jit(solution)/shard_map/last_rows/pallas_call | solution.py:555
  22.0 0.2 collective-permute-start.7
  22.2 1.0 %rest_rows.1 = (bf16[2,32,2048]{2,1,0:T(8,128)(2,1)S(1)}, bf16[32,2048]{1,0:T(8,128)(2,1)S(1)}, f32[32,2048]{1,0:T(8,128)S(1)}, f32[32,2048]{1,0:T(8,128)S(1)}, f32[32,2048]{1,0:T(8,128)S(1)}) custom-call(bf16[256,768]{1,0:T(8,128)(2,1)S(1)} %get-tuple-element.84.joined_ref, f32[256,128]{1,0:T(8,128)S(1)} %get-tuple-element.75.refs_9_.offsets_ref, ...), custom_call_target="tpu_custom_call" | custom-call | flops 201326592 | bytes 1048576 | tf_op jit(solution)/shard_map/rest_rows/pallas_call | solution.py:647
  23.2 0.4 %collective-permute-start.9 = (bf16[2,32,2048]{2,1,0:T(8,128)(2,1)S(1)}, bf16[2,32,2048]{2,1,0:T(8,128)(2,1)S(1)}, u32[]{:S(2)}, u32[]{:S(2)}) collective-permute-start(bf16[2,32,2048]{2,1,0:T(8,128)(2,1)S(1)} %get-tuple-element.88), channel_id=1, source_target_pairs={{0,1},{1,0},{2,3},{3,2},{4,5},{5,4},{6,7},{7,6},{8,9},{9,8},{10,11... | collective-permute-start | bytes 786440 | tf_op jit(solution)/shard_map/ppermute | solution.py:235
  23.7 1.7 %collective-permute-start.11 = (bf16[32,2048]{1,0:T(8,128)(2,1)S(1)}, bf16[32,2048]{1,0:T(8,128)(2,1)S(1)}, u32[]{:S(2)}, u32[]{:S(2)}) collective-permute-start(bf16[32,2048]{1,0:T(8,128)(2,1)S(1)} %third_added.1), channel_id=1, source_target_pairs={{0,2},{1,3},{2,0},{3,1},{4,6},{5,7},{6,4},{7,5},{8,10},{9,11},{10,... | collective-permute-start | bytes 393224 | tf_op jit(solution)/shard_map/ppermute | solution.py:235
  25.4 0.0 collective-permute-start.12
  25.5 0.3 cached_pages.1
  25.8 2.5 %collective-permute-start.8 = (bf16[8,16,512]{2,1,0:T(8,128)(2,1)S(1)}, bf16[8,16,512]{2,1,0:T(8,128)(2,1)S(1)}, u32[]{:S(2)}, u32[]{:S(2)}) collective-permute-start(bf16[8,16,512]{2,1,0:T(8,128)(2,1)S(1)} %get-tuple-element.87), channel_id=1, source_target_pairs={{0,24},{8,16},{16,8},{24,0},{1,25},{9,17},{17,9},{25,1},{2,26},{10... | collective-permute-start | bytes 393224 | tf_op jit(solution)/shard_map/ppermute | solution.py:235
  28.3 0.1 near_sums.1
  28.3 0.4 %collective-permute-start.10 = (bf16[32,2048]{1,0:T(8,128)(2,1)S(1)}, bf16[32,2048]{1,0:T(8,128)(2,1)S(1)}, u32[]{:S(2)}, u32[]{:S(2)}) collective-permute-start(bf16[32,2048]{1,0:T(8,128)(2,1)S(1)} %get-tuple-element.92), channel_id=1, source_target_pairs={{0,2},{1,3},{2,0},{3,1},{4,6},{5,7},{6,4},{7,5},{8,10},{9,11},{10,... | collective-permute-start | bytes 393224 | tf_op jit(solution)/shard_map/ppermute | solution.py:235
  28.8 0.6 %collective-permute-done.11.refs_1_ = bf16[32,2048]{1,0:T(8,128)(2,1)S(1)} collective-permute-done((bf16[32,2048]{1,0:T(8,128)(2,1)S(1)}, bf16[32,2048]{1,0:T(8,128)(2,1)S(1)}, u32[]{:S(2)}, u32[]{:S(2)}) %collective-permute-start.11) | collective-permute-done | bytes 131104 | tf_op jit(solution)/shard_map/ppermute | solution.py:235
  29.4 0.7 %collective-permute-start.13 = (bf16[32,2048]{1,0:T(8,128)(2,1)S(1)}, bf16[32,2048]{1,0:T(8,128)(2,1)S(1)}, u32[]{:S(2)}, u32[]{:S(2)}) collective-permute-start(bf16[32,2048]{1,0:T(8,128)(2,1)S(1)} %second_added.1), channel_id=1, source_target_pairs={{0,4},{1,5},{2,6},{3,7},{4,0},{5,1},{6,2},{7,3},{8,12},{9,13},{10,... | collective-permute-start | bytes 393224 | tf_op jit(solution)/shard_map/ppermute | solution.py:235
  30.0 1.5 %collective-permute-start.14 = (bf16[8,16,512]{2,1,0:T(8,128)(2,1)S(1)}, bf16[8,16,512]{2,1,0:T(8,128)(2,1)S(1)}, u32[]{:S(2)}, u32[]{:S(2)}) collective-permute-start(bf16[8,16,512]{2,1,0:T(8,128)(2,1)S(1)} %get-tuple-element.101), channel_id=1, source_target_pairs={{0,16},{8,24},{16,0},{24,8},{1,17},{9,25},{17,1},{25,9},{2,18},{10... | collective-permute-start | bytes 393224 | tf_op jit(solution)/shard_map/ppermute | solution.py:235
  31.6 1.5 %collective-permute-start.15 = (bf16[8,16,512]{2,1,0:T(8,128)(2,1)S(1)}, bf16[8,16,512]{2,1,0:T(8,128)(2,1)S(1)}, u32[]{:S(2)}, u32[]{:S(2)}) collective-permute-start(bf16[8,16,512]{2,1,0:T(8,128)(2,1)S(1)} %get-tuple-element.102), channel_id=1, source_target_pairs={{0,8},{8,0},{16,24},{24,16},{1,9},{9,1},{17,25},{25,17},{2,10},{10... | collective-permute-start | bytes 393224 | tf_op jit(solution)/shard_map/ppermute | solution.py:235
  33.1 2.8 %collective-permute-done.10.refs_2_ = bf16[32,2048]{1,0:T(8,128)(2,1)S(1)} collective-permute-done((bf16[32,2048]{1,0:T(8,128)(2,1)S(1)}, bf16[32,2048]{1,0:T(8,128)(2,1)S(1)}, u32[]{:S(2)}, u32[]{:S(2)}) %collective-permute-start.10) | collective-permute-done | bytes 131104 | tf_op jit(solution)/shard_map/ppermute | solution.py:235
  35.9 0.7 %placed.1 = (bf16[1,4,8,16,512]{4,3,2,1,0:T(8,128)(2,1)}, f32[32,2048]{1,0:T(8,128)S(1)}) custom-call(bf16[8,16,512]{2,1,0:T(8,128)(2,1)S(1)} %get-tuple-element.86.refs_0_, bf16[8,16,512]{2,1,0:T(8,128)(2,1)S(1)} %collective-permute-done.8.refs_1_, bf16[32,2048]{1,0:T(8,128)(2,1)S(1)} %collective-permute-done.10.refs_2_, ...), custom_call_target="tpu_custom_call" | custom-call | tf_op jit(solution)/shard_map/placed/pallas_call | solution.py:742
  36.7 1.3 %collective-permute-done.13.refs_0_ = bf16[32,2048]{1,0:T(8,128)(2,1)S(1)} collective-permute-done((bf16[32,2048]{1,0:T(8,128)(2,1)S(1)}, bf16[32,2048]{1,0:T(8,128)(2,1)S(1)}, u32[]{:S(2)}, u32[]{:S(2)}) %collective-permute-start.13) | collective-permute-done | bytes 131104 | tf_op jit(solution)/shard_map/ppermute | solution.py:235
  38.0 0.8 %finished.1 = (f32[32,2048]{1,0:T(8,128)}, bf16[1,4,8,16,512]{4,3,2,1,0:T(8,128)(2,1)}) custom-call(f32[32,2048]{1,0:T(8,128)S(1)} %get-tuple-element.94.base_ref, bf16[32,2048]{1,0:T(8,128)(2,1)S(1)} %collective-permute-done.13.refs_0_, bf16[8,16,512]{2,1,0:T(8,128)(2,1)S(1)} %collective-permute-done.14.refs_1_, ...), custom_call_target="tpu_custom_call", output_to_operand_aliasing={{1}: (4, {})} | custom-call | tf_op jit(solution)/shard_map/finished/pallas_call | solution.py:779
  (11 shorter events, 0.1 us)
Async XLA Ops:
  0.6 10.4 %collective-permute-start.1 = (bf16[32,2048]{1,0:T(8,128)(2,1)}, bf16[32,2048]{1,0:T(8,128)(2,1)S(1)}, u32[]{:S(2)}, u32[]{:S(2)}) collective-permute-start(bf16[32,2048]{1,0:T(8,128)(2,1)} %refs_2_.1), channel_id=1, source_target_pairs={{0,6},{1,7},{2,4},{3,5},{4,2},{5,3},{6,0},{7,1},{8,14},{9,15},{10,... | collective-permute-start | bytes 393224 | tf_op jit(solution)/shard_map/ppermute | solution.py:235
  5.7 6.6 %collective-permute-start = (bf16[32,2048]{1,0:T(8,128)(2,1)}, bf16[32,2048]{1,0:T(8,128)(2,1)S(1)}, u32[]{:S(2)}, u32[]{:S(2)}) collective-permute-start(bf16[32,2048]{1,0:T(8,128)(2,1)} %refs_2_.1), channel_id=1, source_target_pairs={{0,2},{1,3},{2,0},{3,1},{4,6},{5,7},{6,4},{7,5},{8,10},{9,11},{10,... | collective-permute-start | bytes 393224 | tf_op jit(solution)/shard_map/ppermute | solution.py:235
  5.8 8.3 %collective-permute-start.3 = (bf16[32,2048]{1,0:T(8,128)(2,1)}, bf16[32,2048]{1,0:T(8,128)(2,1)S(1)}, u32[]{:S(2)}, u32[]{:S(2)}) collective-permute-start(bf16[32,2048]{1,0:T(8,128)(2,1)} %refs_2_.1), channel_id=1, source_target_pairs={{0,1},{1,0},{2,3},{3,2},{4,5},{5,4},{6,7},{7,6},{8,9},{9,8},{10,11... | collective-permute-start | bytes 393224 | tf_op jit(solution)/shard_map/ppermute | solution.py:235
  12.4 1.7 %collective-permute-start.4 = (bf16[32,2048]{1,0:T(8,128)(2,1)S(1)}, bf16[32,2048]{1,0:T(8,128)(2,1)S(1)}, u32[]{:S(2)}, u32[]{:S(2)}) collective-permute-start(bf16[32,2048]{1,0:T(8,128)(2,1)S(1)} %collective-permute-done.refs_1_), channel_id=1, source_target_pairs={{0,1},{1,0},{2,3},{3,2},{4,5},{5,4},{6,7},{7,6},{8,9},{9,8},{10,11... | collective-permute-start | bytes 393224 | tf_op jit(solution)/shard_map/ppermute | solution.py:235
  12.4 5.9 %collective-permute-start.2 = (bf16[32,2048]{1,0:T(8,128)(2,1)S(1)}, bf16[32,2048]{1,0:T(8,128)(2,1)S(1)}, u32[]{:S(2)}, u32[]{:S(2)}) collective-permute-start(bf16[32,2048]{1,0:T(8,128)(2,1)S(1)} %collective-permute-done.1.refs_3_), channel_id=1, source_target_pairs={{0,2},{1,3},{2,0},{3,1},{4,6},{5,7},{6,4},{7,5},{8,10},{9,11},{10,... | collective-permute-start | bytes 393224 | tf_op jit(solution)/shard_map/ppermute | solution.py:235
  16.2 2.1 %collective-permute-start.5 = (bf16[32,2048]{1,0:T(8,128)(2,1)S(1)}, bf16[32,2048]{1,0:T(8,128)(2,1)S(1)}, u32[]{:S(2)}, u32[]{:S(2)}) collective-permute-start(bf16[32,2048]{1,0:T(8,128)(2,1)S(1)} %collective-permute-done.1.refs_3_), channel_id=1, source_target_pairs={{0,1},{1,0},{2,3},{3,2},{4,5},{5,4},{6,7},{7,6},{8,9},{9,8},{10,11... | collective-permute-start | bytes 393224 | tf_op jit(solution)/shard_map/ppermute | solution.py:235
  18.3 1.3 %collective-permute-start.6 = (bf16[32,2048]{1,0:T(8,128)(2,1)S(1)}, bf16[32,2048]{1,0:T(8,128)(2,1)S(1)}, u32[]{:S(2)}, u32[]{:S(2)}) collective-permute-start(bf16[32,2048]{1,0:T(8,128)(2,1)S(1)} %collective-permute-done.2.refs_1_), channel_id=1, source_target_pairs={{0,1},{1,0},{2,3},{3,2},{4,5},{5,4},{6,7},{7,6},{8,9},{9,8},{10,11... | collective-permute-start | bytes 393224 | tf_op jit(solution)/shard_map/ppermute | solution.py:235
  22.0 1.6 %collective-permute-start.7 = (bf16[32,2048]{1,0:T(8,128)(2,1)S(1)}, bf16[32,2048]{1,0:T(8,128)(2,1)S(1)}, u32[]{:S(2)}, u32[]{:S(2)}) collective-permute-start(bf16[32,2048]{1,0:T(8,128)(2,1)S(1)} %get-tuple-element.80), channel_id=1, source_target_pairs={{0,1},{1,0},{2,3},{3,2},{4,5},{5,4},{6,7},{7,6},{8,9},{9,8},{10,11... | collective-permute-start | bytes 393224 | tf_op jit(solution)/shard_map/ppermute | solution.py:235
  23.2 5.0 %collective-permute-start.9 = (bf16[2,32,2048]{2,1,0:T(8,128)(2,1)S(1)}, bf16[2,32,2048]{2,1,0:T(8,128)(2,1)S(1)}, u32[]{:S(2)}, u32[]{:S(2)}) collective-permute-start(bf16[2,32,2048]{2,1,0:T(8,128)(2,1)S(1)} %get-tuple-element.88), channel_id=1, source_target_pairs={{0,1},{1,0},{2,3},{3,2},{4,5},{5,4},{6,7},{7,6},{8,9},{9,8},{10,11... | collective-permute-start | bytes 786440 | tf_op jit(solution)/shard_map/ppermute | solution.py:235
  23.7 5.6 %collective-permute-start.11 = (bf16[32,2048]{1,0:T(8,128)(2,1)S(1)}, bf16[32,2048]{1,0:T(8,128)(2,1)S(1)}, u32[]{:S(2)}, u32[]{:S(2)}) collective-permute-start(bf16[32,2048]{1,0:T(8,128)(2,1)S(1)} %third_added.1), channel_id=1, source_target_pairs={{0,2},{1,3},{2,0},{3,1},{4,6},{5,7},{6,4},{7,5},{8,10},{9,11},{10,... | collective-permute-start | bytes 393224 | tf_op jit(solution)/shard_map/ppermute | solution.py:235
  25.4 3.9 %collective-permute-start.12 = (bf16[32,2048]{1,0:T(8,128)(2,1)S(1)}, bf16[32,2048]{1,0:T(8,128)(2,1)S(1)}, u32[]{:S(2)}, u32[]{:S(2)}) collective-permute-start(bf16[32,2048]{1,0:T(8,128)(2,1)S(1)} %get-tuple-element.97), channel_id=1, source_target_pairs={{0,1},{1,0},{2,3},{3,2},{4,5},{5,4},{6,7},{7,6},{8,9},{9,8},{10,11... | collective-permute-start | bytes 393224 | tf_op jit(solution)/shard_map/ppermute | solution.py:235
  25.8 7.3 %collective-permute-start.8 = (bf16[8,16,512]{2,1,0:T(8,128)(2,1)S(1)}, bf16[8,16,512]{2,1,0:T(8,128)(2,1)S(1)}, u32[]{:S(2)}, u32[]{:S(2)}) collective-permute-start(bf16[8,16,512]{2,1,0:T(8,128)(2,1)S(1)} %get-tuple-element.87), channel_id=1, source_target_pairs={{0,24},{8,16},{16,8},{24,0},{1,25},{9,17},{17,9},{25,1},{2,26},{10... | collective-permute-start | bytes 393224 | tf_op jit(solution)/shard_map/ppermute | solution.py:235
  28.3 7.6 %collective-permute-start.10 = (bf16[32,2048]{1,0:T(8,128)(2,1)S(1)}, bf16[32,2048]{1,0:T(8,128)(2,1)S(1)}, u32[]{:S(2)}, u32[]{:S(2)}) collective-permute-start(bf16[32,2048]{1,0:T(8,128)(2,1)S(1)} %get-tuple-element.92), channel_id=1, source_target_pairs={{0,2},{1,3},{2,0},{3,1},{4,6},{5,7},{6,4},{7,5},{8,10},{9,11},{10,... | collective-permute-start | bytes 393224 | tf_op jit(solution)/shard_map/ppermute | solution.py:235
  29.4 8.6 %collective-permute-start.13 = (bf16[32,2048]{1,0:T(8,128)(2,1)S(1)}, bf16[32,2048]{1,0:T(8,128)(2,1)S(1)}, u32[]{:S(2)}, u32[]{:S(2)}) collective-permute-start(bf16[32,2048]{1,0:T(8,128)(2,1)S(1)} %second_added.1), channel_id=1, source_target_pairs={{0,4},{1,5},{2,6},{3,7},{4,0},{5,1},{6,2},{7,3},{8,12},{9,13},{10,... | collective-permute-start | bytes 393224 | tf_op jit(solution)/shard_map/ppermute | solution.py:235
  30.0 7.9 %collective-permute-start.14 = (bf16[8,16,512]{2,1,0:T(8,128)(2,1)S(1)}, bf16[8,16,512]{2,1,0:T(8,128)(2,1)S(1)}, u32[]{:S(2)}, u32[]{:S(2)}) collective-permute-start(bf16[8,16,512]{2,1,0:T(8,128)(2,1)S(1)} %get-tuple-element.101), channel_id=1, source_target_pairs={{0,16},{8,24},{16,0},{24,8},{1,17},{9,25},{17,1},{25,9},{2,18},{10... | collective-permute-start | bytes 393224 | tf_op jit(solution)/shard_map/ppermute | solution.py:235
  31.6 6.4 %collective-permute-start.15 = (bf16[8,16,512]{2,1,0:T(8,128)(2,1)S(1)}, bf16[8,16,512]{2,1,0:T(8,128)(2,1)S(1)}, u32[]{:S(2)}, u32[]{:S(2)}) collective-permute-start(bf16[8,16,512]{2,1,0:T(8,128)(2,1)S(1)} %get-tuple-element.102), channel_id=1, source_target_pairs={{0,8},{8,0},{16,24},{24,16},{1,9},{9,1},{17,25},{25,17},{2,10},{10... | collective-permute-start | bytes 393224 | tf_op jit(solution)/shard_map/ppermute | solution.py:235

commit v18 on v17

--- a/solution.py
+++ b/solution.py
@@ -248,8 +248,7 @@
     return member // CORES, member % CORES
 
 
-def kind_at(stand):
-    return stand ^ (stand >> 1)
+ORDER = (0, 3, 1, 2)
 
 
 def position_of(kind, half, block_rows):
@@ -261,7 +260,8 @@
     chip, core = whereabouts()
     bits = block_rows.bit_length() - 1
     place = first + lax.broadcasted_iota(jnp.int32, shape, axis)
-    kind = kind_at(place >> (bits + 1))
+    stand = place >> (bits + 1)
+    kind = jnp.where(stand == 1, ORDER[1], jnp.maximum(stand - 1, 0))
     half = (place >> bits) & 1
     return ((((chip ^ kind) << 1) | (core ^ half)) << bits) | (place & (block_rows - 1))
 
@@ -324,7 +324,7 @@
 def attend(joined_ref, offsets_ref, first, rows, block_rows):
     tokens = joined_ref.shape[0]
     starts = [
-        position_of(kind_at(place // (2 * block_rows)), (place // block_rows) % 2, block_rows)
+        position_of(ORDER[place // (2 * block_rows)], (place // block_rows) % 2, block_rows)
         for place in range(first, first + rows, block_rows)
     ]
     reach = jnp.concatenate(
@@ -530,7 +530,7 @@
         normed_scr[:count, :] = normed_ref[...]
     joined_ref[:block_rows, :] = own_joined_ref[...]
     joined_ref[block_rows:first, :] = middle_joined_ref[...]
-    origins = ((3, 1), (2, 0), (2, 1))
+    origins = ((3, 1), (1, 0), (1, 1), (2, 0), (2, 1))
     places = [position_of(kind, half, block_rows) for kind, half in origins]
     project(attention_scr, heads_ref, table_refs, places, joined_ref, first)
     rows = CORES * block_rows
@@ -556,7 +556,7 @@
         last_kernel,
         out_shape=[
             pltpu.VMEM((tokens, 3 * HD), jnp.bfloat16),
-            pltpu.VMEM((CORES * block_rows, width), jnp.float32),
+            pltpu.VMEM((rows - block_rows, width), jnp.float32),
             pltpu.VMEM((block_rows, width), jnp.bfloat16),
             pltpu.VMEM((block_rows, width), jnp.float32),
         ],
@@ -578,7 +578,7 @@
 
 
 def fed_kernel(own_hidden_ref, middle_hidden_ref, downward_ref, *refs):
-    blocks, gain_refs, (fed_ref, *normed_refs) = refs[:2], refs[2:4], refs[4:]
+    blocks, gain_refs, (fed_ref, *normed_refs) = refs[:-5], refs[-5:-3], refs[-3:]
     normalize(blocks, gain_refs, normed_refs)
     hidden = jnp.concatenate([own_hidden_ref[...], middle_hidden_ref[...]], 0)
     chunk = 512
@@ -596,7 +596,7 @@
     return pl.pallas_call(
         fed_kernel,
         out_shape=[pltpu.VMEM((rows, width), jnp.float32), normed, normed],
-        in_specs=vmem_specs(7),
+        in_specs=vmem_specs(5 + len(blocks)),
         out_specs=vmem_specs(3),
         compiler_params=parameters(12),
         cost_estimate=pl.CostEstimate(
@@ -609,16 +609,10 @@
 def rest_kernel(joined_ref, offsets_ref, output_ref, early_ref, late_ref, *refs):
     near_ref, far_ref, *owns = refs
     block_rows = far_ref.shape[0]
-    late = CORES * block_rows
-    early = late * near_ref.shape[0]
     tokens = joined_ref.shape[0]
-    attended = jnp.concatenate(
-        [
-            attend(joined_ref, offsets_ref, 0, early, block_rows),
-            attend(joined_ref, offsets_ref, tokens - late, late, block_rows),
-        ],
-        0,
-    )
+    early = CORES * block_rows
+    attended = attend(joined_ref, offsets_ref, 0, tokens, block_rows)
+    attended = jnp.concatenate([attended[:early], attended[2 * early :]], 0)
     chunk = 512
     for begin in range(0, output_ref.shape[1], chunk):
         columns = slice(begin, begin + chunk)
@@ -640,7 +634,7 @@
 def rest_rows(joined, offsets, output_weight, early, late):
     width = early.shape[1]
     count = CHIPS - 1
-    rows = late.shape[0] * count
+    rows = late.shape[0] * count // (count - 1)
     shape = (rows // (CORES * count), width)
     shapes = [pltpu.VMEM((count - 1, *shape), jnp.bfloat16), pltpu.VMEM(shape, jnp.bfloat16)]
     shapes += [pltpu.VMEM(shape, jnp.float32)] * count
@@ -827,25 +821,27 @@
     heads, upward, downward = weights
     destinations, own_joined, own_hidden = staged[12:]
 
-    first, third, own_joined = lax.optimization_barrier((first, third, own_joined))
-    first_beside = exchanged(first, "tensor", 1)
+    third, own_joined = lax.optimization_barrier((third, own_joined))
     second = exchanged(third, "tensor", to_chip[1])
     middle_joined, middle_hidden, output = middle_rows(
         "middle_rows",
-        ((0, 1), (1, 0), (1, 1), (3, 0)),
-        (beside, first, first_beside, third),
+        ((0, 1), (3, 0)),
+        (beside, third),
         gains,
         (heads, upward),
         tables[1:],
         output_weight,
     )
-    third, middle_joined = lax.optimization_barrier((third, middle_joined))
+    third, first, middle_joined = lax.optimization_barrier((third, first, middle_joined))
+    first_beside = exchanged(first, "tensor", 1)
     third_beside = exchanged(third, "tensor", 1)
-    second, third_beside, middle_joined, middle_hidden = lax.optimization_barrier(
-        (second, third_beside, middle_joined, middle_hidden)
+    second, first_beside, third_beside, middle_joined, middle_hidden = lax.optimization_barrier(
+        (second, first_beside, third_beside, middle_joined, middle_hidden)
     )
     second_beside = exchanged(second, "tensor", 1)
-    fed, *normed = fed_rows(own_hidden, middle_hidden, downward, (third_beside, second), gains)
+    fed, *normed = fed_rows(
+        own_hidden, middle_hidden, downward, (third_beside, first, first_beside, second), gains
+    )
     joined, fed_late, sibling, own = last_rows(
         second_beside,
         normed,

time: 39 us -> 39.6 us (1.015)
  waiting for transfers between devices: 8.29 us -> 5.76 us
  starting transfers between devices: 16.1 us -> 18.6 us
  Pallas kernels: 13.7 us -> 14.3 us
    ppermute x16, waiting for transfers between devices: 8.29 us -> 5.76 us  [exchanged(): lax.ppermute(block, axis, [(member, member ^ mask) for member in range(co...]
    ppermute x16, starting transfers between devices: 16.1 us -> 18.6 us  [exchanged(): lax.ppermute(block, axis, [(member, member ^ mask) for member in range(co...]
    pallas_call x1, Pallas kernels: 2.4 us -> 2.99 us  [last_rows(): pl.pallas_call(last_kernel, out_shape=[pltpu.VMEM((tokens, 3 * HD), jnp.b...]
  transfers between devices with their start and end apart: 16 -> 16, of which waited for: 6 -> 5; matrix products, arithmetic and copies ran while one was open for 0% -> 0% of each run, Pallas kernels for 27% -> 27%
where the time goes in v18:
time: 39.6 us; the launch traced here: 39.4 us
  starting transfers between devices  18.6 us (47%)
  Pallas kernels  14.3 us (36%)
  waiting for transfers between devices  5.76 us (15%)
  between operations  0.74 us (2%)
    ppermute x16, starting transfers between devices, exchanged(): lax.ppermute(block, axis, [(member, member ^ mask) for member in range(co...  18.6 us
    ppermute x16, waiting for transfers between devices, exchanged(): lax.ppermute(block, axis, [(member, member ^ mask) for member in range(co...  5.76 us
    pallas_call x1, Pallas kernels, own_rows(): pl.pallas_call(functools.partial(own_kernel, count, replica_count), out_s...  5.27 us
    pallas_call x1, Pallas kernels, last_rows(): pl.pallas_call(last_kernel, out_shape=[pltpu.VMEM((tokens, 3 * HD), jnp.b...  2.99 us
    pallas_call x1, Pallas kernels, middle_rows(): pl.pallas_call(functools.partial(middle_kernel, origins), out_shape=[pltp...  2.26 us
    pallas_call x1, Pallas kernels, fed_rows(): pl.pallas_call(fed_kernel, out_shape=[pltpu.VMEM((rows, width), jnp.float...  0.97 us
    pallas_call x1, Pallas kernels, rest_rows(): pl.pallas_call(rest_kernel, out_shape=shapes, in_specs=vmem_specs(5), out...  0.83 us
    pallas_call x1, Pallas kernels, finished(): pl.pallas_call(functools.partial(finish_kernel, masks), out_shape=[jax.Sh...  0.83 us
  transfers between devices with their start and end apart: 16, of which 5 were waited for; matrix products, arithmetic and copies ran while one was open for 0% of the time, Pallas kernels for 27%

profile of v18, /device:TPU:0, one launch (start us, length us, event | category | flops | bytes accessed | tf_op | source)
XLA Modules:
  0.0 39.4 jit_solution(18216066099238256599)
XLA Ops:
  0.6 5.1 %collective-permute-start = (bf16[32,2048]{1,0:T(8,128)(2,1)}, bf16[32,2048]{1,0:T(8,128)(2,1)S(1)}, u32[]{:S(2)}, u32[]{:S(2)}) collective-permute-start(bf16[32,2048]{1,0:T(8,128)(2,1)} %refs_2_.1), channel_id=1, source_target_pairs={{0,6},{1,7},{2,4},{3,5},{4,2},{5,3},{6,0},{7,1},{8,14},{9,15},{10,... | collective-permute-start | bytes 393224 | tf_op jit(solution)/shard_map/ppermute | solution.py:235
  5.7 0.0 collective-permute-start.3
  5.8 0.0 collective-permute-start.2
  5.8 5.3 %own_rows.1 = (s32[1,256]{1,0:T(1,128)}, s32[1,16]{1,0:T(1,128)}, bf16[32,2048]{1,0:T(8,128)(2,1)S(1)}, f32[1,2048]{1,0:T(1,128)S(1)}, f32[1,2048]{1,0:T(1,128)S...) custom-call(s32[1,256]{1,0:T(1,128)} %refs_0_.1, ...), custom_call_target="tpu_custom_call" | custom-call | flops 234881024 | bytes 11682880 | tf_op jit(solution)/shard_map/own_rows/pallas_call | solution.py:452
  11.0 2.1 %collective-permute-start.1 = (bf16[32,2048]{1,0:T(8,128)(2,1)S(1)}, bf16[32,2048]{1,0:T(8,128)(2,1)S(1)}, u32[]{:S(2)}, u32[]{:S(2)}) collective-permute-start(bf16[32,2048]{1,0:T(8,128)(2,1)S(1)} %collective-permute-done.refs_1_), channel_id=1, source_target_pairs={{0,2},{1,3},{2,0},{3,1},{4,6},{5,7},{6,4},{7,5},{8,10},{9,11},{10,... | collective-permute-start | bytes 393224 | tf_op jit(solution)/shard_map/ppermute | solution.py:235
  13.1 0.0 collective-permute-done.3.refs_0_
  13.1 2.3 %middle_rows.1 = (bf16[64,768]{1,0:T(8,128)(2,1)S(1)}, bf16[64,1024]{1,0:T(8,128)(2,1)S(1)}, bf16[256,2048]{1,0:T(8,128)(2,1)S(1)}) custom-call(bf16[32,2048]{1,0:T(8,128)(2,1)S(1)} %collective-permute-done.3.refs_0_, bf16[32,2048]{1,0:T(8,128)(2,1)S(1)} %collective-permute-done.refs_1_, f32[1,2048]{1,0:T(1,128)S(1)} %get-tuple-element.56.refs_2_.refs_4_.refs_3_, ...), custom_call_target="tpu_custom_call" | custom-call | flops 469762048 | bytes 1048576 | tf_op jit(solution)/shard_map/middle_rows/pallas_call | solution.py:492
  15.4 0.0 collective-permute-done.2.refs_1_
  15.4 0.1 collective-permute-start.5
  15.5 0.5 %collective-permute-start.4 = (bf16[32,2048]{1,0:T(8,128)(2,1)S(1)}, bf16[32,2048]{1,0:T(8,128)(2,1)S(1)}, u32[]{:S(2)}, u32[]{:S(2)}) collective-permute-start(bf16[32,2048]{1,0:T(8,128)(2,1)S(1)} %collective-permute-done.2.refs_1_), channel_id=1, source_target_pairs={{0,1},{1,0},{2,3},{3,2},{4,5},{5,4},{6,7},{7,6},{8,9},{9,8},{10,11... | collective-permute-start | bytes 393224 | tf_op jit(solution)/shard_map/ppermute | solution.py:235
  16.0 1.0 %collective-permute-done.1.refs_3_ = bf16[32,2048]{1,0:T(8,128)(2,1)S(1)} collective-permute-done((bf16[32,2048]{1,0:T(8,128)(2,1)S(1)}, bf16[32,2048]{1,0:T(8,128)(2,1)S(1)}, u32[]{:S(2)}, u32[]{:S(2)}) %collective-permute-start.1) | collective-permute-done | bytes 131104 | tf_op jit(solution)/shard_map/ppermute | solution.py:235
  17.0 0.3 collective-permute-start.6
  17.3 1.0 %fed_rows.1 = (f32[96,2048]{1,0:T(8,128)S(1)}, bf16[128,2048]{1,0:T(8,128)(2,1)S(1)}, bf16[128,2048]{1,0:T(8,128)(2,1)S(1)}) custom-call(bf16[32,1024]{1,0:T(8,128)(2,1)S(1)} %get-tuple-element.69.own_hidden_ref, bf16[64,1024]{1,0:T(8,128)(2,1)S(1)} %get-tuple-element.70.middle_hidden_ref, bf16[1024,2048]{1,0:T(8,128)(2,1)S(1)} %get-tuple-element.71.downward_ref.refs_7_, ...), custom_call_target="tpu_custom_call" | custom-call | flops 402653184 | bytes 1048576 | tf_op jit(solution)/shard_map/fed_rows/pallas_call | solution.py:596
  18.3 0.1 collective-permute-done.6.refs_0_
  18.4 3.0 %last_rows.1 = (bf16[256,768]{1,0:T(8,128)(2,1)S(1)}, f32[128,2048]{1,0:T(8,128)S(1)}, bf16[32,2048]{1,0:T(8,128)(2,1)S(1)}, f32[32,2048]{1,0:T(8,128)S(1)}) custom-call(bf16[32,2048]{1,0:T(8,128)(2,1)S(1)} %collective-permute-done.6.refs_0_, bf16[128,2048]{1,0:T(8,128)(2,1)S(1)} %get-tuple-element.74.refs_1_, ...), custom_call_target="tpu_custom_call" | custom-call | flops 2013265920 | bytes 1048576 | tf_op jit(solution)/shard_map/last_rows/pallas_call | solution.py:555
  21.4 0.4 collective-permute-start.7
  21.7 0.8 %rest_rows.1 = (bf16[2,32,2048]{2,1,0:T(8,128)(2,1)S(1)}, bf16[32,2048]{1,0:T(8,128)(2,1)S(1)}, f32[32,2048]{1,0:T(8,128)S(1)}, f32[32,2048]{1,0:T(8,128)S(1)}, f32[32,2048]{1,0:T(8,128)S(1)}) custom-call(bf16[256,768]{1,0:T(8,128)(2,1)S(1)} %get-tuple-element.86.joined_ref, f32[256,128]{1,0:T(8,128)S(1)} %get-tuple-element.77.refs_9_.offsets_ref, ...), custom_call_target="tpu_custom_call" | custom-call | flops 201326592 | bytes 1048576 | tf_op jit(solution)/shard_map/rest_rows/pallas_call | solution.py:641
  22.6 0.3 collective-permute-start.9
  22.8 0.0 collective-permute-done.7.refs_1_
  22.9 1.8 %collective-permute-start.11 = (bf16[32,2048]{1,0:T(8,128)(2,1)S(1)}, bf16[32,2048]{1,0:T(8,128)(2,1)S(1)}, u32[]{:S(2)}, u32[]{:S(2)}) collective-permute-start(bf16[32,2048]{1,0:T(8,128)(2,1)S(1)} %third_added.1), channel_id=1, source_target_pairs={{0,2},{1,3},{2,0},{3,1},{4,6},{5,7},{6,4},{7,5},{8,10},{9,11},{10,... | collective-permute-start | bytes 393224 | tf_op jit(solution)/shard_map/ppermute | solution.py:235
  24.7 0.3 cached_pages.1
  25.0 2.5 %collective-permute-start.8 = (bf16[8,16,512]{2,1,0:T(8,128)(2,1)S(1)}, bf16[8,16,512]{2,1,0:T(8,128)(2,1)S(1)}, u32[]{:S(2)}, u32[]{:S(2)}) collective-permute-start(bf16[8,16,512]{2,1,0:T(8,128)(2,1)S(1)} %get-tuple-element.89), channel_id=1, source_target_pairs={{0,24},{8,16},{16,8},{24,0},{1,25},{9,17},{17,9},{25,1},{2,26},{10... | collective-permute-start | bytes 393224 | tf_op jit(solution)/shard_map/ppermute | solution.py:235
  27.5 1.1 %collective-permute-done.11.refs_1_ = bf16[32,2048]{1,0:T(8,128)(2,1)S(1)} collective-permute-done((bf16[32,2048]{1,0:T(8,128)(2,1)S(1)}, bf16[32,2048]{1,0:T(8,128)(2,1)S(1)}, u32[]{:S(2)}, u32[]{:S(2)}) %collective-permute-start.11) | collective-permute-done | bytes 131104 | tf_op jit(solution)/shard_map/ppermute | solution.py:235
  28.7 0.1 near_sums.1
  28.8 1.7 %collective-permute-start.10 = (bf16[32,2048]{1,0:T(8,128)(2,1)S(1)}, bf16[32,2048]{1,0:T(8,128)(2,1)S(1)}, u32[]{:S(2)}, u32[]{:S(2)}) collective-permute-start(bf16[32,2048]{1,0:T(8,128)(2,1)S(1)} %get-tuple-element.94), channel_id=1, source_target_pairs={{0,2},{1,3},{2,0},{3,1},{4,6},{5,7},{6,4},{7,5},{8,10},{9,11},{10,... | collective-permute-start | bytes 393224 | tf_op jit(solution)/shard_map/ppermute | solution.py:235
  30.4 0.9 %collective-permute-start.13 = (bf16[32,2048]{1,0:T(8,128)(2,1)S(1)}, bf16[32,2048]{1,0:T(8,128)(2,1)S(1)}, u32[]{:S(2)}, u32[]{:S(2)}) collective-permute-start(bf16[32,2048]{1,0:T(8,128)(2,1)S(1)} %second_added.1), channel_id=1, source_target_pairs={{0,4},{1,5},{2,6},{3,7},{4,0},{5,1},{6,2},{7,3},{8,12},{9,13},{10,... | collective-permute-start | bytes 393224 | tf_op jit(solution)/shard_map/ppermute | solution.py:235
  31.3 1.5 %collective-permute-start.14 = (bf16[8,16,512]{2,1,0:T(8,128)(2,1)S(1)}, bf16[8,16,512]{2,1,0:T(8,128)(2,1)S(1)}, u32[]{:S(2)}, u32[]{:S(2)}) collective-permute-start(bf16[8,16,512]{2,1,0:T(8,128)(2,1)S(1)} %get-tuple-element.103), channel_id=1, source_target_pairs={{0,16},{8,24},{16,0},{24,8},{1,17},{9,25},{17,1},{25,9},{2,18},{10... | collective-permute-start | bytes 393224 | tf_op jit(solution)/shard_map/ppermute | solution.py:235
  32.9 1.5 %collective-permute-start.15 = (bf16[8,16,512]{2,1,0:T(8,128)(2,1)S(1)}, bf16[8,16,512]{2,1,0:T(8,128)(2,1)S(1)}, u32[]{:S(2)}, u32[]{:S(2)}) collective-permute-start(bf16[8,16,512]{2,1,0:T(8,128)(2,1)S(1)} %get-tuple-element.104), channel_id=1, source_target_pairs={{0,8},{8,0},{16,24},{24,16},{1,9},{9,1},{17,25},{25,17},{2,10},{10... | collective-permute-start | bytes 393224 | tf_op jit(solution)/shard_map/ppermute | solution.py:235
  34.4 0.6 %collective-permute-done.10.refs_2_ = bf16[32,2048]{1,0:T(8,128)(2,1)S(1)} collective-permute-done((bf16[32,2048]{1,0:T(8,128)(2,1)S(1)}, bf16[32,2048]{1,0:T(8,128)(2,1)S(1)}, u32[]{:S(2)}, u32[]{:S(2)}) %collective-permute-start.10) | collective-permute-done | bytes 131104 | tf_op jit(solution)/shard_map/ppermute | solution.py:235
  34.9 0.7 %placed.1 = (bf16[1,4,8,16,512]{4,3,2,1,0:T(8,128)(2,1)}, f32[32,2048]{1,0:T(8,128)S(1)}) custom-call(bf16[8,16,512]{2,1,0:T(8,128)(2,1)S(1)} %get-tuple-element.88.refs_0_, bf16[8,16,512]{2,1,0:T(8,128)(2,1)S(1)} %collective-permute-done.8.refs_1_, bf16[32,2048]{1,0:T(8,128)(2,1)S(1)} %collective-permute-done.10.refs_2_, ...), custom_call_target="tpu_custom_call" | custom-call | tf_op jit(solution)/shard_map/placed/pallas_call | solution.py:736
  35.7 2.9 %collective-permute-done.13.refs_0_ = bf16[32,2048]{1,0:T(8,128)(2,1)S(1)} collective-permute-done((bf16[32,2048]{1,0:T(8,128)(2,1)S(1)}, bf16[32,2048]{1,0:T(8,128)(2,1)S(1)}, u32[]{:S(2)}, u32[]{:S(2)}) %collective-permute-start.13) | collective-permute-done | bytes 131104 | tf_op jit(solution)/shard_map/ppermute | solution.py:235
  38.6 0.8 %finished.1 = (f32[32,2048]{1,0:T(8,128)}, bf16[1,4,8,16,512]{4,3,2,1,0:T(8,128)(2,1)}) custom-call(f32[32,2048]{1,0:T(8,128)S(1)} %get-tuple-element.96.base_ref, bf16[32,2048]{1,0:T(8,128)(2,1)S(1)} %collective-permute-done.13.refs_0_, bf16[8,16,512]{2,1,0:T(8,128)(2,1)S(1)} %collective-permute-done.14.refs_1_, ...), custom_call_target="tpu_custom_call", output_to_operand_aliasing={{1}: (4, {})} | custom-call | tf_op jit(solution)/shard_map/finished/pallas_call | solution.py:773
  (11 shorter events, 0.1 us)
Async XLA Ops:
  0.6 10.4 %collective-permute-start = (bf16[32,2048]{1,0:T(8,128)(2,1)}, bf16[32,2048]{1,0:T(8,128)(2,1)S(1)}, u32[]{:S(2)}, u32[]{:S(2)}) collective-permute-start(bf16[32,2048]{1,0:T(8,128)(2,1)} %refs_2_.1), channel_id=1, source_target_pairs={{0,6},{1,7},{2,4},{3,5},{4,2},{5,3},{6,0},{7,1},{8,14},{9,15},{10,... | collective-permute-start | bytes 393224 | tf_op jit(solution)/shard_map/ppermute | solution.py:235
  5.7 7.4 %collective-permute-start.3 = (bf16[32,2048]{1,0:T(8,128)(2,1)}, bf16[32,2048]{1,0:T(8,128)(2,1)S(1)}, u32[]{:S(2)}, u32[]{:S(2)}) collective-permute-start(bf16[32,2048]{1,0:T(8,128)(2,1)} %refs_2_.1), channel_id=1, source_target_pairs={{0,1},{1,0},{2,3},{3,2},{4,5},{5,4},{6,7},{7,6},{8,9},{9,8},{10,11... | collective-permute-start | bytes 393224 | tf_op jit(solution)/shard_map/ppermute | solution.py:235
  5.8 9.7 %collective-permute-start.2 = (bf16[32,2048]{1,0:T(8,128)(2,1)}, bf16[32,2048]{1,0:T(8,128)(2,1)S(1)}, u32[]{:S(2)}, u32[]{:S(2)}) collective-permute-start(bf16[32,2048]{1,0:T(8,128)(2,1)} %refs_2_.1), channel_id=1, source_target_pairs={{0,2},{1,3},{2,0},{3,1},{4,6},{5,7},{6,4},{7,5},{8,10},{9,11},{10,... | collective-permute-start | bytes 393224 | tf_op jit(solution)/shard_map/ppermute | solution.py:235
  11.0 6.0 %collective-permute-start.1 = (bf16[32,2048]{1,0:T(8,128)(2,1)S(1)}, bf16[32,2048]{1,0:T(8,128)(2,1)S(1)}, u32[]{:S(2)}, u32[]{:S(2)}) collective-permute-start(bf16[32,2048]{1,0:T(8,128)(2,1)S(1)} %collective-permute-done.refs_1_), channel_id=1, source_target_pairs={{0,2},{1,3},{2,0},{3,1},{4,6},{5,7},{6,4},{7,5},{8,10},{9,11},{10,... | collective-permute-start | bytes 393224 | tf_op jit(solution)/shard_map/ppermute | solution.py:235
  15.4 1.6 %collective-permute-start.5 = (bf16[32,2048]{1,0:T(8,128)(2,1)S(1)}, bf16[32,2048]{1,0:T(8,128)(2,1)S(1)}, u32[]{:S(2)}, u32[]{:S(2)}) collective-permute-start(bf16[32,2048]{1,0:T(8,128)(2,1)S(1)} %collective-permute-done.refs_1_), channel_id=1, source_target_pairs={{0,1},{1,0},{2,3},{3,2},{4,5},{5,4},{6,7},{7,6},{8,9},{9,8},{10,11... | collective-permute-start | bytes 393224 | tf_op jit(solution)/shard_map/ppermute | solution.py:235
  15.5 1.5 %collective-permute-start.4 = (bf16[32,2048]{1,0:T(8,128)(2,1)S(1)}, bf16[32,2048]{1,0:T(8,128)(2,1)S(1)}, u32[]{:S(2)}, u32[]{:S(2)}) collective-permute-start(bf16[32,2048]{1,0:T(8,128)(2,1)S(1)} %collective-permute-done.2.refs_1_), channel_id=1, source_target_pairs={{0,1},{1,0},{2,3},{3,2},{4,5},{5,4},{6,7},{7,6},{8,9},{9,8},{10,11... | collective-permute-start | bytes 393224 | tf_op jit(solution)/shard_map/ppermute | solution.py:235
  17.0 1.4 %collective-permute-start.6 = (bf16[32,2048]{1,0:T(8,128)(2,1)S(1)}, bf16[32,2048]{1,0:T(8,128)(2,1)S(1)}, u32[]{:S(2)}, u32[]{:S(2)}) collective-permute-start(bf16[32,2048]{1,0:T(8,128)(2,1)S(1)} %collective-permute-done.1.refs_3_), channel_id=1, source_target_pairs={{0,1},{1,0},{2,3},{3,2},{4,5},{5,4},{6,7},{7,6},{8,9},{9,8},{10,11... | collective-permute-start | bytes 393224 | tf_op jit(solution)/shard_map/ppermute | solution.py:235
  21.4 1.5 %collective-permute-start.7 = (bf16[32,2048]{1,0:T(8,128)(2,1)S(1)}, bf16[32,2048]{1,0:T(8,128)(2,1)S(1)}, u32[]{:S(2)}, u32[]{:S(2)}) collective-permute-start(bf16[32,2048]{1,0:T(8,128)(2,1)S(1)} %get-tuple-element.82), channel_id=1, source_target_pairs={{0,1},{1,0},{2,3},{3,2},{4,5},{5,4},{6,7},{7,6},{8,9},{9,8},{10,11... | collective-permute-start | bytes 393224 | tf_op jit(solution)/shard_map/ppermute | solution.py:235
  22.6 6.1 %collective-permute-start.9 = (bf16[2,32,2048]{2,1,0:T(8,128)(2,1)S(1)}, bf16[2,32,2048]{2,1,0:T(8,128)(2,1)S(1)}, u32[]{:S(2)}, u32[]{:S(2)}) collective-permute-start(bf16[2,32,2048]{2,1,0:T(8,128)(2,1)S(1)} %get-tuple-element.90), channel_id=1, source_target_pairs={{0,1},{1,0},{2,3},{3,2},{4,5},{5,4},{6,7},{7,6},{8,9},{9,8},{10,11... | collective-permute-start | bytes 786440 | tf_op jit(solution)/shard_map/ppermute | solution.py:235
  22.9 5.8 %collective-permute-start.11 = (bf16[32,2048]{1,0:T(8,128)(2,1)S(1)}, bf16[32,2048]{1,0:T(8,128)(2,1)S(1)}, u32[]{:S(2)}, u32[]{:S(2)}) collective-permute-start(bf16[32,2048]{1,0:T(8,128)(2,1)S(1)} %third_added.1), channel_id=1, source_target_pairs={{0,2},{1,3},{2,0},{3,1},{4,6},{5,7},{6,4},{7,5},{8,10},{9,11},{10,... | collective-permute-start | bytes 393224 | tf_op jit(solution)/shard_map/ppermute | solution.py:235
  24.7 4.0 %collective-permute-start.12 = (bf16[32,2048]{1,0:T(8,128)(2,1)S(1)}, bf16[32,2048]{1,0:T(8,128)(2,1)S(1)}, u32[]{:S(2)}, u32[]{:S(2)}) collective-permute-start(bf16[32,2048]{1,0:T(8,128)(2,1)S(1)} %get-tuple-element.99), channel_id=1, source_target_pairs={{0,1},{1,0},{2,3},{3,2},{4,5},{5,4},{6,7},{7,6},{8,9},{9,8},{10,11... | collective-permute-start | bytes 393224 | tf_op jit(solution)/shard_map/ppermute | solution.py:235
  25.0 9.4 %collective-permute-start.8 = (bf16[8,16,512]{2,1,0:T(8,128)(2,1)S(1)}, bf16[8,16,512]{2,1,0:T(8,128)(2,1)S(1)}, u32[]{:S(2)}, u32[]{:S(2)}) collective-permute-start(bf16[8,16,512]{2,1,0:T(8,128)(2,1)S(1)} %get-tuple-element.89), channel_id=1, source_target_pairs={{0,24},{8,16},{16,8},{24,0},{1,25},{9,17},{17,9},{25,1},{2,26},{10... | collective-permute-start | bytes 393224 | tf_op jit(solution)/shard_map/ppermute | solution.py:235
  28.8 6.2 %collective-permute-start.10 = (bf16[32,2048]{1,0:T(8,128)(2,1)S(1)}, bf16[32,2048]{1,0:T(8,128)(2,1)S(1)}, u32[]{:S(2)}, u32[]{:S(2)}) collective-permute-start(bf16[32,2048]{1,0:T(8,128)(2,1)S(1)} %get-tuple-element.94), channel_id=1, source_target_pairs={{0,2},{1,3},{2,0},{3,1},{4,6},{5,7},{6,4},{7,5},{8,10},{9,11},{10,... | collective-permute-start | bytes 393224 | tf_op jit(solution)/shard_map/ppermute | solution.py:235
  30.4 8.2 %collective-permute-start.13 = (bf16[32,2048]{1,0:T(8,128)(2,1)S(1)}, bf16[32,2048]{1,0:T(8,128)(2,1)S(1)}, u32[]{:S(2)}, u32[]{:S(2)}) collective-permute-start(bf16[32,2048]{1,0:T(8,128)(2,1)S(1)} %second_added.1), channel_id=1, source_target_pairs={{0,4},{1,5},{2,6},{3,7},{4,0},{5,1},{6,2},{7,3},{8,12},{9,13},{10,... | collective-permute-start | bytes 393224 | tf_op jit(solution)/shard_map/ppermute | solution.py:235
  31.3 7.2 %collective-permute-start.14 = (bf16[8,16,512]{2,1,0:T(8,128)(2,1)S(1)}, bf16[8,16,512]{2,1,0:T(8,128)(2,1)S(1)}, u32[]{:S(2)}, u32[]{:S(2)}) collective-permute-start(bf16[8,16,512]{2,1,0:T(8,128)(2,1)S(1)} %get-tuple-element.103), channel_id=1, source_target_pairs={{0,16},{8,24},{16,0},{24,8},{1,17},{9,25},{17,1},{25,9},{2,18},{10... | collective-permute-start | bytes 393224 | tf_op jit(solution)/shard_map/ppermute | solution.py:235
  32.9 5.7 %collective-permute-start.15 = (bf16[8,16,512]{2,1,0:T(8,128)(2,1)S(1)}, bf16[8,16,512]{2,1,0:T(8,128)(2,1)S(1)}, u32[]{:S(2)}, u32[]{:S(2)}) collective-permute-start(bf16[8,16,512]{2,1,0:T(8,128)(2,1)S(1)} %get-tuple-element.104), channel_id=1, source_target_pairs={{0,8},{8,0},{16,24},{24,16},{1,9},{9,1},{17,25},{25,17},{2,10},{10... | collective-permute-start | bytes 393224 | tf_op jit(solution)/shard_map/ppermute | solution.py:235

commit v19 on v18

--- a/solution.py
+++ b/solution.py
@@ -296,9 +296,11 @@
         )
         for table_ref in table_refs
     ]
-    joined_ref[own, :] = jnp.dot(
-        normed_ref[...], heads_ref[...], preferred_element_type=jnp.float32
-    ).astype(jnp.bfloat16)
+    for begin in range(0, heads_ref.shape[1], HD):
+        columns = slice(begin, begin + HD)
+        joined_ref[own, columns] = jnp.dot(
+            normed_ref[...], heads_ref[:, columns], preferred_element_type=jnp.float32
+        ).astype(jnp.bfloat16)
     for begin in (0, HD):
         columns = slice(begin, begin + 128)
         turning = joined_ref[own, columns].astype(jnp.float32)
@@ -534,9 +536,9 @@
     places = [position_of(kind, half, block_rows) for kind, half in origins]
     project(attention_scr, heads_ref, table_refs, places, joined_ref, first)
     rows = CORES * block_rows
-    hide(feedforward_scr, upward_ref, hidden_scr, 0, 512)
+    hide(feedforward_scr, upward_ref, hidden_scr, 0)
     attended = attend(joined_ref, offsets_ref, first - block_rows, rows, block_rows)
-    chunk = 1024
+    chunk = 512
     for begin in range(0, downward_ref.shape[1], chunk):
         columns = slice(begin, begin + chunk)
         fed = jnp.dot(hidden_scr[...], downward_ref[:, columns], preferred_element_type=jnp.float32)
@@ -860,8 +862,9 @@
     third_sum = added("third_added", own, received)
     third_sum, far_sibling, joined = lax.optimization_barrier((third_sum, far_sibling, joined))
     passing = exchanged(third_sum, "tensor", to_chip[1])
+    pages = cached_pages(joined, destinations, replica_count)
+    far_sibling, pages = lax.optimization_barrier((far_sibling, pages))
     far_received = exchanged(far_sibling, "tensor", 1)
-    pages = cached_pages(joined, destinations, replica_count)
     early, late = (3,), (2, 1)
     arriving = [exchanged(pages[mask], "dp", mask) for mask in early]
     first_sum, base = near_sums(near_received, owns[:2], hidden)

time: 39.6 us -> 38.4 us (0.970)
  waiting for transfers between devices: 5.76 us -> 4.51 us
    ppermute x16, waiting for transfers between devices: 5.76 us -> 4.51 us  [exchanged(): lax.ppermute(block, axis, [(member, member ^ mask) for member in range(co...]
where the time goes in v19:
time: 38.4 us; the launch traced here: 38.3 us
  starting transfers between devices  18.7 us (49%)
  Pallas kernels  14.3 us (37%)
  waiting for transfers between devices  4.51 us (12%)
  between operations  0.74 us (2%)
    ppermute x16, starting transfers between devices, exchanged(): lax.ppermute(block, axis, [(member, member ^ mask) for member in range(co...  18.7 us
    pallas_call x1, Pallas kernels, own_rows(): pl.pallas_call(functools.partial(own_kernel, count, replica_count), out_s...  5.27 us
    ppermute x16, waiting for transfers between devices, exchanged(): lax.ppermute(block, axis, [(member, member ^ mask) for member in range(co...  4.51 us
    pallas_call x1, Pallas kernels, last_rows(): pl.pallas_call(last_kernel, out_shape=[pltpu.VMEM((tokens, 3 * HD), jnp.b...  3 us
    pallas_call x1, Pallas kernels, middle_rows(): pl.pallas_call(functools.partial(middle_kernel, origins), out_shape=[pltp...  2.26 us
    pallas_call x1, Pallas kernels, fed_rows(): pl.pallas_call(fed_kernel, out_shape=[pltpu.VMEM((rows, width), jnp.float...  0.97 us
    pallas_call x1, Pallas kernels, rest_rows(): pl.pallas_call(rest_kernel, out_shape=shapes, in_specs=vmem_specs(5), out...  0.83 us
    pallas_call x1, Pallas kernels, finished(): pl.pallas_call(functools.partial(finish_kernel, masks), out_shape=[jax.Sh...  0.83 us
  transfers between devices with their start and end apart: 16, of which 5 were waited for; matrix products, arithmetic and copies ran while one was open for 0% of the time, Pallas kernels for 27%

profile of v19, /device:TPU:0, one launch (start us, length us, event | category | flops | bytes accessed | tf_op | source)
XLA Modules:
  0.0 38.3 jit_solution(4710160010210498433)
XLA Ops:
  0.6 5.1 %collective-permute-start = (bf16[32,2048]{1,0:T(8,128)(2,1)}, bf16[32,2048]{1,0:T(8,128)(2,1)S(1)}, u32[]{:S(2)}, u32[]{:S(2)}) collective-permute-start(bf16[32,2048]{1,0:T(8,128)(2,1)} %refs_2_.1), channel_id=1, source_target_pairs={{0,6},{1,7},{2,4},{3,5},{4,2},{5,3},{6,0},{7,1},{8,14},{9,15},{10,... | collective-permute-start | bytes 393224 | tf_op jit(solution)/shard_map/ppermute | solution.py:235
  5.8 5.3 %own_rows.1 = (s32[1,256]{1,0:T(1,128)}, s32[1,16]{1,0:T(1,128)}, bf16[32,2048]{1,0:T(8,128)(2,1)S(1)}, f32[1,2048]{1,0:T(1,128)S(1)}, f32[1,2048]{1,0:T(1,128)S...) custom-call(s32[1,256]{1,0:T(1,128)} %refs_0_.1, ...), custom_call_target="tpu_custom_call" | custom-call | flops 234881024 | bytes 11682880 | tf_op jit(solution)/shard_map/own_rows/pallas_call | solution.py:454
  11.0 2.1 %collective-permute-start.1 = (bf16[32,2048]{1,0:T(8,128)(2,1)S(1)}, bf16[32,2048]{1,0:T(8,128)(2,1)S(1)}, u32[]{:S(2)}, u32[]{:S(2)}) collective-permute-start(bf16[32,2048]{1,0:T(8,128)(2,1)S(1)} %collective-permute-done.refs_1_), channel_id=1, source_target_pairs={{0,2},{1,3},{2,0},{3,1},{4,6},{5,7},{6,4},{7,5},{8,10},{9,11},{10,... | collective-permute-start | bytes 393224 | tf_op jit(solution)/shard_map/ppermute | solution.py:235
  13.1 0.0 collective-permute-done.3.refs_0_
  13.1 2.3 %middle_rows.1 = (bf16[64,768]{1,0:T(8,128)(2,1)S(1)}, bf16[64,1024]{1,0:T(8,128)(2,1)S(1)}, bf16[256,2048]{1,0:T(8,128)(2,1)S(1)}) custom-call(bf16[32,2048]{1,0:T(8,128)(2,1)S(1)} %collective-permute-done.3.refs_0_, bf16[32,2048]{1,0:T(8,128)(2,1)S(1)} %collective-permute-done.refs_1_, f32[1,2048]{1,0:T(1,128)S(1)} %get-tuple-element.61.refs_2_.refs_4_.refs_3_, ...), custom_call_target="tpu_custom_call" | custom-call | flops 469762048 | bytes 1048576 | tf_op jit(solution)/shard_map/middle_rows/pallas_call | solution.py:494
  15.4 0.1 collective-permute-start.5
  15.5 0.5 %collective-permute-start.4 = (bf16[32,2048]{1,0:T(8,128)(2,1)S(1)}, bf16[32,2048]{1,0:T(8,128)(2,1)S(1)}, u32[]{:S(2)}, u32[]{:S(2)}) collective-permute-start(bf16[32,2048]{1,0:T(8,128)(2,1)S(1)} %collective-permute-done.2.refs_1_), channel_id=1, source_target_pairs={{0,1},{1,0},{2,3},{3,2},{4,5},{5,4},{6,7},{7,6},{8,9},{9,8},{10,11... | collective-permute-start | bytes 393224 | tf_op jit(solution)/shard_map/ppermute | solution.py:235
  16.0 1.0 %collective-permute-done.1.refs_3_ = bf16[32,2048]{1,0:T(8,128)(2,1)S(1)} collective-permute-done((bf16[32,2048]{1,0:T(8,128)(2,1)S(1)}, bf16[32,2048]{1,0:T(8,128)(2,1)S(1)}, u32[]{:S(2)}, u32[]{:S(2)}) %collective-permute-start.1) | collective-permute-done | bytes 131104 | tf_op jit(solution)/shard_map/ppermute | solution.py:235
  17.0 0.0 collective-permute-done.5.refs_0_
  17.0 0.0 collective-permute-done.4.refs_2_
  17.0 0.3 collective-permute-start.6
  17.3 1.0 %fed_rows.1 = (f32[96,2048]{1,0:T(8,128)S(1)}, bf16[128,2048]{1,0:T(8,128)(2,1)S(1)}, bf16[128,2048]{1,0:T(8,128)(2,1)S(1)}) custom-call(bf16[32,1024]{1,0:T(8,128)(2,1)S(1)} %get-tuple-element.74.own_hidden_ref, bf16[64,1024]{1,0:T(8,128)(2,1)S(1)} %get-tuple-element.75.middle_hidden_ref, bf16[1024,2048]{1,0:T(8,128)(2,1)S(1)} %get-tuple-element.76.downward_ref.refs_7_, ...), custom_call_target="tpu_custom_call" | custom-call | flops 402653184 | bytes 1048576 | tf_op jit(solution)/shard_map/fed_rows/pallas_call | solution.py:598
  18.3 0.1 collective-permute-done.6.refs_0_
  18.4 3.0 %last_rows.1 = (bf16[256,768]{1,0:T(8,128)(2,1)S(1)}, f32[128,2048]{1,0:T(8,128)S(1)}, bf16[32,2048]{1,0:T(8,128)(2,1)S(1)}, f32[32,2048]{1,0:T(8,128)S(1)}) custom-call(bf16[32,2048]{1,0:T(8,128)(2,1)S(1)} %collective-permute-done.6.refs_0_, bf16[128,2048]{1,0:T(8,128)(2,1)S(1)} %get-tuple-element.79.refs_1_, ...), custom_call_target="tpu_custom_call" | custom-call | flops 2013265920 | bytes 1048576 | tf_op jit(solution)/shard_map/last_rows/pallas_call | solution.py:557
  21.4 0.4 collective-permute-start.7
  21.8 0.8 %rest_rows.1 = (bf16[2,32,2048]{2,1,0:T(8,128)(2,1)S(1)}, bf16[32,2048]{1,0:T(8,128)(2,1)S(1)}, f32[32,2048]{1,0:T(8,128)S(1)}, f32[32,2048]{1,0:T(8,128)S(1)}, f32[32,2048]{1,0:T(8,128)S(1)}) custom-call(bf16[256,768]{1,0:T(8,128)(2,1)S(1)} %get-tuple-element.92.joined_ref, f32[256,128]{1,0:T(8,128)S(1)} %get-tuple-element.82.refs_9_.offsets_ref, ...), custom_call_target="tpu_custom_call" | custom-call | flops 201326592 | bytes 1048576 | tf_op jit(solution)/shard_map/rest_rows/pallas_call | solution.py:643
  22.6 0.3 collective-permute-start.9
  22.9 1.8 %collective-permute-start.11 = (bf16[32,2048]{1,0:T(8,128)(2,1)S(1)}, bf16[32,2048]{1,0:T(8,128)(2,1)S(1)}, u32[]{:S(2)}, u32[]{:S(2)}) collective-permute-start(bf16[32,2048]{1,0:T(8,128)(2,1)S(1)} %third_added.1), channel_id=1, source_target_pairs={{0,2},{1,3},{2,0},{3,1},{4,6},{5,7},{6,4},{7,5},{8,10},{9,11},{10,... | collective-permute-start | bytes 393224 | tf_op jit(solution)/shard_map/ppermute | solution.py:235
  24.7 0.3 cached_pages.1
  25.0 0.1 collective-permute-start.12
  25.1 2.5 %collective-permute-start.8 = (bf16[8,16,512]{2,1,0:T(8,128)(2,1)S(1)}, bf16[8,16,512]{2,1,0:T(8,128)(2,1)S(1)}, u32[]{:S(2)}, u32[]{:S(2)}) collective-permute-start(bf16[8,16,512]{2,1,0:T(8,128)(2,1)S(1)} %get-tuple-element.99), channel_id=1, source_target_pairs={{0,24},{8,16},{16,8},{24,0},{1,25},{9,17},{17,9},{25,1},{2,26},{10... | collective-permute-start | bytes 393224 | tf_op jit(solution)/shard_map/ppermute | solution.py:235
  27.6 0.1 near_sums.1
  27.7 0.3 collective-permute-start.10
  28.0 0.6 %collective-permute-done.11.refs_1_ = bf16[32,2048]{1,0:T(8,128)(2,1)S(1)} collective-permute-done((bf16[32,2048]{1,0:T(8,128)(2,1)S(1)}, bf16[32,2048]{1,0:T(8,128)(2,1)S(1)}, u32[]{:S(2)}, u32[]{:S(2)}) %collective-permute-start.11) | collective-permute-done | bytes 131104 | tf_op jit(solution)/shard_map/ppermute | solution.py:235
  28.7 0.0 collective-permute-done.12.refs_2_
  28.7 1.6 %collective-permute-start.13 = (bf16[32,2048]{1,0:T(8,128)(2,1)S(1)}, bf16[32,2048]{1,0:T(8,128)(2,1)S(1)}, u32[]{:S(2)}, u32[]{:S(2)}) collective-permute-start(bf16[32,2048]{1,0:T(8,128)(2,1)S(1)} %second_added.1), channel_id=1, source_target_pairs={{0,4},{1,5},{2,6},{3,7},{4,0},{5,1},{6,2},{7,3},{8,12},{9,13},{10,... | collective-permute-start | bytes 393224 | tf_op jit(solution)/shard_map/ppermute | solution.py:235
  30.4 1.5 %collective-permute-start.14 = (bf16[8,16,512]{2,1,0:T(8,128)(2,1)S(1)}, bf16[8,16,512]{2,1,0:T(8,128)(2,1)S(1)}, u32[]{:S(2)}, u32[]{:S(2)}) collective-permute-start(bf16[8,16,512]{2,1,0:T(8,128)(2,1)S(1)} %get-tuple-element.113), channel_id=1, source_target_pairs={{0,16},{8,24},{16,0},{24,8},{1,17},{9,25},{17,1},{25,9},{2,18},{10... | collective-permute-start | bytes 393224 | tf_op jit(solution)/shard_map/ppermute | solution.py:235
  31.9 2.1 %collective-permute-start.15 = (bf16[8,16,512]{2,1,0:T(8,128)(2,1)S(1)}, bf16[8,16,512]{2,1,0:T(8,128)(2,1)S(1)}, u32[]{:S(2)}, u32[]{:S(2)}) collective-permute-start(bf16[8,16,512]{2,1,0:T(8,128)(2,1)S(1)} %get-tuple-element.114), channel_id=1, source_target_pairs={{0,8},{8,0},{16,24},{24,16},{1,9},{9,1},{17,25},{25,17},{2,10},{10... | collective-permute-start | bytes 393224 | tf_op jit(solution)/shard_map/ppermute | solution.py:235
  34.0 1.3 %collective-permute-done.10.refs_2_ = bf16[32,2048]{1,0:T(8,128)(2,1)S(1)} collective-permute-done((bf16[32,2048]{1,0:T(8,128)(2,1)S(1)}, bf16[32,2048]{1,0:T(8,128)(2,1)S(1)}, u32[]{:S(2)}, u32[]{:S(2)}) %collective-permute-start.10) | collective-permute-done | bytes 131104 | tf_op jit(solution)/shard_map/ppermute | solution.py:235
  35.3 0.7 %placed.1 = (bf16[1,4,8,16,512]{4,3,2,1,0:T(8,128)(2,1)}, f32[32,2048]{1,0:T(8,128)S(1)}) custom-call(bf16[8,16,512]{2,1,0:T(8,128)(2,1)S(1)} %get-tuple-element.98.refs_0_, bf16[8,16,512]{2,1,0:T(8,128)(2,1)S(1)} %collective-permute-done.8.refs_1_, bf16[32,2048]{1,0:T(8,128)(2,1)S(1)} %collective-permute-done.10.refs_2_, ...), custom_call_target="tpu_custom_call" | custom-call | tf_op jit(solution)/shard_map/placed/pallas_call | solution.py:738
  36.0 1.5 %collective-permute-done.13.refs_0_ = bf16[32,2048]{1,0:T(8,128)(2,1)S(1)} collective-permute-done((bf16[32,2048]{1,0:T(8,128)(2,1)S(1)}, bf16[32,2048]{1,0:T(8,128)(2,1)S(1)}, u32[]{:S(2)}, u32[]{:S(2)}) %collective-permute-start.13) | collective-permute-done | bytes 131104 | tf_op jit(solution)/shard_map/ppermute | solution.py:235
  37.5 0.8 %finished.1 = (f32[32,2048]{1,0:T(8,128)}, bf16[1,4,8,16,512]{4,3,2,1,0:T(8,128)(2,1)}) custom-call(f32[32,2048]{1,0:T(8,128)S(1)} %get-tuple-element.106.base_ref, bf16[32,2048]{1,0:T(8,128)(2,1)S(1)} %collective-permute-done.13.refs_0_, bf16[8,16,512]{2,1,0:T(8,128)(2,1)S(1)} %collective-permute-done.14.refs_1_, ...), custom_call_target="tpu_custom_call", output_to_operand_aliasing={{1}: (4, {})} | custom-call | tf_op jit(solution)/shard_map/finished/pallas_call | solution.py:775
  (11 shorter events, 0.1 us)
Async XLA Ops:
  0.6 10.4 %collective-permute-start = (bf16[32,2048]{1,0:T(8,128)(2,1)}, bf16[32,2048]{1,0:T(8,128)(2,1)S(1)}, u32[]{:S(2)}, u32[]{:S(2)}) collective-permute-start(bf16[32,2048]{1,0:T(8,128)(2,1)} %refs_2_.1), channel_id=1, source_target_pairs={{0,6},{1,7},{2,4},{3,5},{4,2},{5,3},{6,0},{7,1},{8,14},{9,15},{10,... | collective-permute-start | bytes 393224 | tf_op jit(solution)/shard_map/ppermute | solution.py:235
  5.7 7.4 %collective-permute-start.3 = (bf16[32,2048]{1,0:T(8,128)(2,1)}, bf16[32,2048]{1,0:T(8,128)(2,1)S(1)}, u32[]{:S(2)}, u32[]{:S(2)}) collective-permute-start(bf16[32,2048]{1,0:T(8,128)(2,1)} %refs_2_.1), channel_id=1, source_target_pairs={{0,1},{1,0},{2,3},{3,2},{4,5},{5,4},{6,7},{7,6},{8,9},{9,8},{10,11... | collective-permute-start | bytes 393224 | tf_op jit(solution)/shard_map/ppermute | solution.py:235
  5.8 9.7 %collective-permute-start.2 = (bf16[32,2048]{1,0:T(8,128)(2,1)}, bf16[32,2048]{1,0:T(8,128)(2,1)S(1)}, u32[]{:S(2)}, u32[]{:S(2)}) collective-permute-start(bf16[32,2048]{1,0:T(8,128)(2,1)} %refs_2_.1), channel_id=1, source_target_pairs={{0,2},{1,3},{2,0},{3,1},{4,6},{5,7},{6,4},{7,5},{8,10},{9,11},{10,... | collective-permute-start | bytes 393224 | tf_op jit(solution)/shard_map/ppermute | solution.py:235
  11.0 6.0 %collective-permute-start.1 = (bf16[32,2048]{1,0:T(8,128)(2,1)S(1)}, bf16[32,2048]{1,0:T(8,128)(2,1)S(1)}, u32[]{:S(2)}, u32[]{:S(2)}) collective-permute-start(bf16[32,2048]{1,0:T(8,128)(2,1)S(1)} %collective-permute-done.refs_1_), channel_id=1, source_target_pairs={{0,2},{1,3},{2,0},{3,1},{4,6},{5,7},{6,4},{7,5},{8,10},{9,11},{10,... | collective-permute-start | bytes 393224 | tf_op jit(solution)/shard_map/ppermute | solution.py:235
  15.4 1.6 %collective-permute-start.5 = (bf16[32,2048]{1,0:T(8,128)(2,1)S(1)}, bf16[32,2048]{1,0:T(8,128)(2,1)S(1)}, u32[]{:S(2)}, u32[]{:S(2)}) collective-permute-start(bf16[32,2048]{1,0:T(8,128)(2,1)S(1)} %collective-permute-done.refs_1_), channel_id=1, source_target_pairs={{0,1},{1,0},{2,3},{3,2},{4,5},{5,4},{6,7},{7,6},{8,9},{9,8},{10,11... | collective-permute-start | bytes 393224 | tf_op jit(solution)/shard_map/ppermute | solution.py:235
  15.5 1.5 %collective-permute-start.4 = (bf16[32,2048]{1,0:T(8,128)(2,1)S(1)}, bf16[32,2048]{1,0:T(8,128)(2,1)S(1)}, u32[]{:S(2)}, u32[]{:S(2)}) collective-permute-start(bf16[32,2048]{1,0:T(8,128)(2,1)S(1)} %collective-permute-done.2.refs_1_), channel_id=1, source_target_pairs={{0,1},{1,0},{2,3},{3,2},{4,5},{5,4},{6,7},{7,6},{8,9},{9,8},{10,11... | collective-permute-start | bytes 393224 | tf_op jit(solution)/shard_map/ppermute | solution.py:235
  17.0 1.4 %collective-permute-start.6 = (bf16[32,2048]{1,0:T(8,128)(2,1)S(1)}, bf16[32,2048]{1,0:T(8,128)(2,1)S(1)}, u32[]{:S(2)}, u32[]{:S(2)}) collective-permute-start(bf16[32,2048]{1,0:T(8,128)(2,1)S(1)} %collective-permute-done.1.refs_3_), channel_id=1, source_target_pairs={{0,1},{1,0},{2,3},{3,2},{4,5},{5,4},{6,7},{7,6},{8,9},{9,8},{10,11... | collective-permute-start | bytes 393224 | tf_op jit(solution)/shard_map/ppermute | solution.py:235
  21.4 1.5 %collective-permute-start.7 = (bf16[32,2048]{1,0:T(8,128)(2,1)S(1)}, bf16[32,2048]{1,0:T(8,128)(2,1)S(1)}, u32[]{:S(2)}, u32[]{:S(2)}) collective-permute-start(bf16[32,2048]{1,0:T(8,128)(2,1)S(1)} %get-tuple-element.87), channel_id=1, source_target_pairs={{0,1},{1,0},{2,3},{3,2},{4,5},{5,4},{6,7},{7,6},{8,9},{9,8},{10,11... | collective-permute-start | bytes 393224 | tf_op jit(solution)/shard_map/ppermute | solution.py:235
  22.6 5.0 %collective-permute-start.9 = (bf16[2,32,2048]{2,1,0:T(8,128)(2,1)S(1)}, bf16[2,32,2048]{2,1,0:T(8,128)(2,1)S(1)}, u32[]{:S(2)}, u32[]{:S(2)}) collective-permute-start(bf16[2,32,2048]{2,1,0:T(8,128)(2,1)S(1)} %get-tuple-element.100), channel_id=1, source_target_pairs={{0,1},{1,0},{2,3},{3,2},{4,5},{5,4},{6,7},{7,6},{8,9},{9,8},{10,11... | collective-permute-start | bytes 786440 | tf_op jit(solution)/shard_map/ppermute | solution.py:235
  22.9 5.8 %collective-permute-start.11 = (bf16[32,2048]{1,0:T(8,128)(2,1)S(1)}, bf16[32,2048]{1,0:T(8,128)(2,1)S(1)}, u32[]{:S(2)}, u32[]{:S(2)}) collective-permute-start(bf16[32,2048]{1,0:T(8,128)(2,1)S(1)} %third_added.1), channel_id=1, source_target_pairs={{0,2},{1,3},{2,0},{3,1},{4,6},{5,7},{6,4},{7,5},{8,10},{9,11},{10,... | collective-permute-start | bytes 393224 | tf_op jit(solution)/shard_map/ppermute | solution.py:235
  25.0 3.7 %collective-permute-start.12 = (bf16[32,2048]{1,0:T(8,128)(2,1)S(1)}, bf16[32,2048]{1,0:T(8,128)(2,1)S(1)}, u32[]{:S(2)}, u32[]{:S(2)}) collective-permute-start(bf16[32,2048]{1,0:T(8,128)(2,1)S(1)} %get-tuple-element.109), channel_id=1, source_target_pairs={{0,1},{1,0},{2,3},{3,2},{4,5},{5,4},{6,7},{7,6},{8,9},{9,8},{10,11... | collective-permute-start | bytes 393224 | tf_op jit(solution)/shard_map/ppermute | solution.py:235
  25.1 8.9 %collective-permute-start.8 = (bf16[8,16,512]{2,1,0:T(8,128)(2,1)S(1)}, bf16[8,16,512]{2,1,0:T(8,128)(2,1)S(1)}, u32[]{:S(2)}, u32[]{:S(2)}) collective-permute-start(bf16[8,16,512]{2,1,0:T(8,128)(2,1)S(1)} %get-tuple-element.99), channel_id=1, source_target_pairs={{0,24},{8,16},{16,8},{24,0},{1,25},{9,17},{17,9},{25,1},{2,26},{10... | collective-permute-start | bytes 393224 | tf_op jit(solution)/shard_map/ppermute | solution.py:235
  27.7 7.6 %collective-permute-start.10 = (bf16[32,2048]{1,0:T(8,128)(2,1)S(1)}, bf16[32,2048]{1,0:T(8,128)(2,1)S(1)}, u32[]{:S(2)}, u32[]{:S(2)}) collective-permute-start(bf16[32,2048]{1,0:T(8,128)(2,1)S(1)} %get-tuple-element.104), channel_id=1, source_target_pairs={{0,2},{1,3},{2,0},{3,1},{4,6},{5,7},{6,4},{7,5},{8,10},{9,11},{10,... | collective-permute-start | bytes 393224 | tf_op jit(solution)/shard_map/ppermute | solution.py:235
  28.7 8.7 %collective-permute-start.13 = (bf16[32,2048]{1,0:T(8,128)(2,1)S(1)}, bf16[32,2048]{1,0:T(8,128)(2,1)S(1)}, u32[]{:S(2)}, u32[]{:S(2)}) collective-permute-start(bf16[32,2048]{1,0:T(8,128)(2,1)S(1)} %second_added.1), channel_id=1, source_target_pairs={{0,4},{1,5},{2,6},{3,7},{4,0},{5,1},{6,2},{7,3},{8,12},{9,13},{10,... | collective-permute-start | bytes 393224 | tf_op jit(solution)/shard_map/ppermute | solution.py:235
  30.4 7.1 %collective-permute-start.14 = (bf16[8,16,512]{2,1,0:T(8,128)(2,1)S(1)}, bf16[8,16,512]{2,1,0:T(8,128)(2,1)S(1)}, u32[]{:S(2)}, u32[]{:S(2)}) collective-permute-start(bf16[8,16,512]{2,1,0:T(8,128)(2,1)S(1)} %get-tuple-element.113), channel_id=1, source_target_pairs={{0,16},{8,24},{16,0},{24,8},{1,17},{9,25},{17,1},{25,9},{2,18},{10... | collective-permute-start | bytes 393224 | tf_op jit(solution)/shard_map/ppermute | solution.py:235
  31.9 5.6 %collective-permute-start.15 = (bf16[8,16,512]{2,1,0:T(8,128)(2,1)S(1)}, bf16[8,16,512]{2,1,0:T(8,128)(2,1)S(1)}, u32[]{:S(2)}, u32[]{:S(2)}) collective-permute-start(bf16[8,16,512]{2,1,0:T(8,128)(2,1)S(1)} %get-tuple-element.114), channel_id=1, source_target_pairs={{0,8},{8,0},{16,24},{24,16},{1,9},{9,1},{17,25},{25,17},{2,10},{10... | collective-permute-start | bytes 393224 | tf_op jit(solution)/shard_map/ppermute | solution.py:235

commit v20 on v19

--- a/solution.py
+++ b/solution.py
@@ -530,21 +530,25 @@
     normalize([block_ref], [gain_a, gain_f], [attention_scr, feedforward_scr], count)
     for normed_ref, normed_scr in zip(normed_refs, (attention_scr, feedforward_scr)):
         normed_scr[:count, :] = normed_ref[...]
+    early = 3 * block_rows
+    middle = early + block_rows
     joined_ref[:block_rows, :] = own_joined_ref[...]
-    joined_ref[block_rows:first, :] = middle_joined_ref[...]
-    origins = ((3, 1), (1, 0), (1, 1), (2, 0), (2, 1))
+    joined_ref[block_rows:early, :] = middle_joined_ref[: 2 * block_rows, :]
+    origins = ((3, 1), (1, 1), (2, 0), (2, 1))
     places = [position_of(kind, half, block_rows) for kind, half in origins]
     project(attention_scr, heads_ref, table_refs, places, joined_ref, first)
+    joined_ref[early:middle, :] = joined_ref[first : first + block_rows, :]
+    joined_ref[middle : middle + block_rows, :] = middle_joined_ref[2 * block_rows :, :]
     rows = CORES * block_rows
     hide(feedforward_scr, upward_ref, hidden_scr, 0)
-    attended = attend(joined_ref, offsets_ref, first - block_rows, rows, block_rows)
+    attended = attend(joined_ref, offsets_ref, early - block_rows, rows, block_rows)
     chunk = 512
     for begin in range(0, downward_ref.shape[1], chunk):
         columns = slice(begin, begin + chunk)
         fed = jnp.dot(hidden_scr[...], downward_ref[:, columns], preferred_element_type=jnp.float32)
         fed_ref[:, columns] = fed[block_rows:]
         product = jnp.dot(attended, output_ref[:, columns], preferred_element_type=jnp.float32)
-        own_ref[:, columns] = early_ref[first - block_rows :, columns] + product[:block_rows]
+        own_ref[:, columns] = early_ref[early - block_rows : early, columns] + product[:block_rows]
         sibling = fed[:block_rows] + product[block_rows:]
         sibling_ref[:, columns] = sibling.astype(jnp.bfloat16)
 
@@ -618,7 +622,14 @@
     chunk = 512
     for begin in range(0, output_ref.shape[1], chunk):
         columns = slice(begin, begin + chunk)
-        fed = jnp.concatenate([early_ref[:early, columns], late_ref[:, columns]], 0)
+        fed = jnp.concatenate(
+            [
+                early_ref[:early, columns],
+                early_ref[early + block_rows :, columns],
+                late_ref[:, columns],
+            ],
+            0,
+        )
         partial = fed + jnp.dot(
             attended, output_ref[:, columns], preferred_element_type=jnp.float32
         )
@@ -636,8 +647,8 @@
 def rest_rows(joined, offsets, output_weight, early, late):
     width = early.shape[1]
     count = CHIPS - 1
-    rows = late.shape[0] * count // (count - 1)
-    shape = (rows // (CORES * count), width)
+    shape = (joined.shape[0] // (CORES * CHIPS), width)
+    rows = CORES * count * shape[0]
     shapes = [pltpu.VMEM((count - 1, *shape), jnp.bfloat16), pltpu.VMEM(shape, jnp.bfloat16)]
     shapes += [pltpu.VMEM(shape, jnp.float32)] * count
     return pl.pallas_call(
@@ -827,8 +838,8 @@
     second = exchanged(third, "tensor", to_chip[1])
     middle_joined, middle_hidden, output = middle_rows(
         "middle_rows",
-        ((0, 1), (3, 0)),
-        (beside, third),
+        ((0, 1), (3, 0), (1, 0)),
+        (beside, third, first),
         gains,
         (heads, upward),
         tables[1:],
@@ -842,7 +853,7 @@
     )
     second_beside = exchanged(second, "tensor", 1)
     fed, *normed = fed_rows(
-        own_hidden, middle_hidden, downward, (third_beside, first, first_beside, second), gains
+        own_hidden, middle_hidden, downward, (third_beside, first_beside, second), gains
     )
     joined, fed_late, sibling, own = last_rows(
         second_beside,

time: 38.4 us -> 37.6 us (0.979)
  Pallas kernels: 14.3 us -> 13.4 us
    pallas_call x1, Pallas kernels: 3 us -> 2.25 us  [last_rows(): pl.pallas_call(last_kernel, out_shape=[pltpu.VMEM((tokens, 3 * HD), jnp.b...]
  transfers between devices with their start and end apart: 16 -> 16, of which waited for: 5 -> 5; matrix products, arithmetic and copies ran while one was open for 0% -> 0% of each run, Pallas kernels for 27% -> 28%
where the time goes in v20:
time: 37.6 us; the launch traced here: 37.5 us
  starting transfers between devices  18.7 us (50%)
  Pallas kernels  13.4 us (36%)
  waiting for transfers between devices  4.63 us (12%)
  between operations  0.72 us (2%)
    ppermute x16, starting transfers between devices, exchanged(): lax.ppermute(block, axis, [(member, member ^ mask) for member in range(co...  18.7 us
    pallas_call x1, Pallas kernels, own_rows(): pl.pallas_call(functools.partial(own_kernel, count, replica_count), out_s...  5.27 us
    ppermute x16, waiting for transfers between devices, exchanged(): lax.ppermute(block, axis, [(member, member ^ mask) for member in range(co...  4.63 us
    pallas_call x1, Pallas kernels, last_rows(): pl.pallas_call(last_kernel, out_shape=[pltpu.VMEM((tokens, 3 * HD), jnp.b...  2.25 us
    pallas_call x1, Pallas kernels, middle_rows(): pl.pallas_call(functools.partial(middle_kernel, origins), out_shape=[pltp...  2.23 us
    pallas_call x1, Pallas kernels, fed_rows(): pl.pallas_call(fed_kernel, out_shape=[pltpu.VMEM((rows, width), jnp.float...  0.84 us
    pallas_call x1, Pallas kernels, rest_rows(): pl.pallas_call(rest_kernel, out_shape=shapes, in_specs=vmem_specs(5), out...  0.83 us
    pallas_call x1, Pallas kernels, finished(): pl.pallas_call(functools.partial(finish_kernel, masks), out_shape=[jax.Sh...  0.83 us
  transfers between devices with their start and end apart: 16, of which 5 were waited for; matrix products, arithmetic and copies ran while one was open for 0% of the time, Pallas kernels for 28%

profile of v20, /device:TPU:0, one launch (start us, length us, event | category | flops | bytes accessed | tf_op | source)
XLA Modules:
  0.0 37.5 jit_solution(11736471037209413143)
XLA Ops:
  0.6 5.1 %collective-permute-start = (bf16[32,2048]{1,0:T(8,128)(2,1)}, bf16[32,2048]{1,0:T(8,128)(2,1)S(1)}, u32[]{:S(2)}, u32[]{:S(2)}) collective-permute-start(bf16[32,2048]{1,0:T(8,128)(2,1)} %refs_2_.1), channel_id=1, source_target_pairs={{0,6},{1,7},{2,4},{3,5},{4,2},{5,3},{6,0},{7,1},{8,14},{9,15},{10,... | collective-permute-start | bytes 393224 | tf_op jit(solution)/shard_map/ppermute | solution.py:235
  5.7 0.0 collective-permute-start.3
  5.8 0.0 collective-permute-start.2
  5.8 5.3 %own_rows.1 = (s32[1,256]{1,0:T(1,128)}, s32[1,16]{1,0:T(1,128)}, bf16[32,2048]{1,0:T(8,128)(2,1)S(1)}, f32[1,2048]{1,0:T(1,128)S(1)}, f32[1,2048]{1,0:T(1,128)S...) custom-call(s32[1,256]{1,0:T(1,128)} %refs_0_.1, ...), custom_call_target="tpu_custom_call" | custom-call | flops 234881024 | bytes 11682880 | tf_op jit(solution)/shard_map/own_rows/pallas_call | solution.py:454
  11.0 2.1 %collective-permute-start.1 = (bf16[32,2048]{1,0:T(8,128)(2,1)S(1)}, bf16[32,2048]{1,0:T(8,128)(2,1)S(1)}, u32[]{:S(2)}, u32[]{:S(2)}) collective-permute-start(bf16[32,2048]{1,0:T(8,128)(2,1)S(1)} %collective-permute-done.refs_1_), channel_id=1, source_target_pairs={{0,2},{1,3},{2,0},{3,1},{4,6},{5,7},{6,4},{7,5},{8,10},{9,11},{10,... | collective-permute-start | bytes 393224 | tf_op jit(solution)/shard_map/ppermute | solution.py:235
  13.1 0.0 collective-permute-done.3.refs_0_
  13.1 0.0 collective-permute-done.2.refs_2_
  13.1 2.2 %middle_rows.1 = (bf16[96,768]{1,0:T(8,128)(2,1)S(1)}, bf16[96,1024]{1,0:T(8,128)(2,1)S(1)}, bf16[256,2048]{1,0:T(8,128)(2,1)S(1)}) custom-call(bf16[32,2048]{1,0:T(8,128)(2,1)S(1)} %collective-permute-done.3.refs_0_, bf16[32,2048]{1,0:T(8,128)(2,1)S(1)} %collective-permute-done.refs_1_, bf16[32,2048]{1,0:T(8,128)(2,1)S(1)} %collective-permute-done.2.refs_2_, ...), custom_call_target="tpu_custom_call" | custom-call | flops 704643072 | bytes 1048576 | tf_op jit(solution)/shard_map/middle_rows/pallas_call | solution.py:494
  15.4 0.1 collective-permute-start.4
  15.5 0.5 %collective-permute-start.5 = (bf16[32,2048]{1,0:T(8,128)(2,1)S(1)}, bf16[32,2048]{1,0:T(8,128)(2,1)S(1)}, u32[]{:S(2)}, u32[]{:S(2)}) collective-permute-start(bf16[32,2048]{1,0:T(8,128)(2,1)S(1)} %collective-permute-done.refs_1_), channel_id=1, source_target_pairs={{0,1},{1,0},{2,3},{3,2},{4,5},{5,4},{6,7},{7,6},{8,9},{9,8},{10,11... | collective-permute-start | bytes 393224 | tf_op jit(solution)/shard_map/ppermute | solution.py:235
  16.0 1.1 %collective-permute-done.1.refs_2_ = bf16[32,2048]{1,0:T(8,128)(2,1)S(1)} collective-permute-done((bf16[32,2048]{1,0:T(8,128)(2,1)S(1)}, bf16[32,2048]{1,0:T(8,128)(2,1)S(1)}, u32[]{:S(2)}, u32[]{:S(2)}) %collective-permute-start.1) | collective-permute-done | bytes 131104 | tf_op jit(solution)/shard_map/ppermute | solution.py:235
  17.0 0.3 collective-permute-start.6
  17.3 0.8 %fed_rows.1 = (f32[128,2048]{1,0:T(8,128)S(1)}, bf16[96,2048]{1,0:T(8,128)(2,1)S(1)}, bf16[96,2048]{1,0:T(8,128)(2,1)S(1)}) custom-call(bf16[32,1024]{1,0:T(8,128)(2,1)S(1)} %get-tuple-element.74.own_hidden_ref, bf16[96,1024]{1,0:T(8,128)(2,1)S(1)} %get-tuple-element.75.middle_hidden_ref, bf16[1024,2048]{1,0:T(8,128)(2,1)S(1)} %get-tuple-element.76.downward_ref.refs_7_, ...), custom_call_target="tpu_custom_call" | custom-call | flops 536870912 | bytes 1048576 | tf_op jit(solution)/shard_map/fed_rows/pallas_call | solution.py:602
  18.2 0.2 collective-permute-done.6.refs_0_
  18.4 2.3 %last_rows.1 = (bf16[256,768]{1,0:T(8,128)(2,1)S(1)}, f32[96,2048]{1,0:T(8,128)S(1)}, bf16[32,2048]{1,0:T(8,128)(2,1)S(1)}, f32[32,2048]{1,0:T(8,128)S(1)}) custom-call(bf16[32,2048]{1,0:T(8,128)(2,1)S(1)} %collective-permute-done.6.refs_0_, bf16[96,2048]{1,0:T(8,128)(2,1)S(1)} %get-tuple-element.79.refs_1_, bf16[96,2048]{1,0:T(8,128)(2,1)S(1)} %get-tuple-element.80.refs_2_, ...), custom_call_target="tpu_custom_call" | custom-call | flops 1610612736 | bytes 1048576 | tf_op jit(solution)/shard_map/last_rows/pallas_call | solution.py:561
  20.6 0.3 collective-permute-start.7
  21.0 0.8 %rest_rows.1 = (bf16[2,32,2048]{2,1,0:T(8,128)(2,1)S(1)}, bf16[32,2048]{1,0:T(8,128)(2,1)S(1)}, f32[32,2048]{1,0:T(8,128)S(1)}, f32[32,2048]{1,0:T(8,128)S(1)}, f32[32,2048]{1,0:T(8,128)S(1)}) custom-call(bf16[256,768]{1,0:T(8,128)(2,1)S(1)} %get-tuple-element.92.joined_ref, f32[256,128]{1,0:T(8,128)S(1)} %get-tuple-element.82.refs_9_.offsets_ref, ...), custom_call_target="tpu_custom_call" | custom-call | flops 201326592 | bytes 1048576 | tf_op jit(solution)/shard_map/rest_rows/pallas_call | solution.py:654
  21.8 0.3 collective-permute-start.9
  22.1 1.8 %collective-permute-start.11 = (bf16[32,2048]{1,0:T(8,128)(2,1)S(1)}, bf16[32,2048]{1,0:T(8,128)(2,1)S(1)}, u32[]{:S(2)}, u32[]{:S(2)}) collective-permute-start(bf16[32,2048]{1,0:T(8,128)(2,1)S(1)} %third_added.1), channel_id=1, source_target_pairs={{0,2},{1,3},{2,0},{3,1},{4,6},{5,7},{6,4},{7,5},{8,10},{9,11},{10,... | collective-permute-start | bytes 393224 | tf_op jit(solution)/shard_map/ppermute | solution.py:235
  24.0 0.3 cached_pages.1
  24.3 0.1 collective-permute-start.12
  24.3 2.5 %collective-permute-start.8 = (bf16[8,16,512]{2,1,0:T(8,128)(2,1)S(1)}, bf16[8,16,512]{2,1,0:T(8,128)(2,1)S(1)}, u32[]{:S(2)}, u32[]{:S(2)}) collective-permute-start(bf16[8,16,512]{2,1,0:T(8,128)(2,1)S(1)} %get-tuple-element.99), channel_id=1, source_target_pairs={{0,24},{8,16},{16,8},{24,0},{1,25},{9,17},{17,9},{25,1},{2,26},{10... | collective-permute-start | bytes 393224 | tf_op jit(solution)/shard_map/ppermute | solution.py:235
  26.9 0.1 near_sums.1
  26.9 0.3 collective-permute-start.10
  27.3 0.6 %collective-permute-done.11.refs_1_ = bf16[32,2048]{1,0:T(8,128)(2,1)S(1)} collective-permute-done((bf16[32,2048]{1,0:T(8,128)(2,1)S(1)}, bf16[32,2048]{1,0:T(8,128)(2,1)S(1)}, u32[]{:S(2)}, u32[]{:S(2)}) %collective-permute-start.11) | collective-permute-done | bytes 131104 | tf_op jit(solution)/shard_map/ppermute | solution.py:235
  27.9 1.6 %collective-permute-start.13 = (bf16[32,2048]{1,0:T(8,128)(2,1)S(1)}, bf16[32,2048]{1,0:T(8,128)(2,1)S(1)}, u32[]{:S(2)}, u32[]{:S(2)}) collective-permute-start(bf16[32,2048]{1,0:T(8,128)(2,1)S(1)} %second_added.1), channel_id=1, source_target_pairs={{0,4},{1,5},{2,6},{3,7},{4,0},{5,1},{6,2},{7,3},{8,12},{9,13},{10,... | collective-permute-start | bytes 393224 | tf_op jit(solution)/shard_map/ppermute | solution.py:235
  29.6 1.5 %collective-permute-start.14 = (bf16[8,16,512]{2,1,0:T(8,128)(2,1)S(1)}, bf16[8,16,512]{2,1,0:T(8,128)(2,1)S(1)}, u32[]{:S(2)}, u32[]{:S(2)}) collective-permute-start(bf16[8,16,512]{2,1,0:T(8,128)(2,1)S(1)} %get-tuple-element.113), channel_id=1, source_target_pairs={{0,16},{8,24},{16,0},{24,8},{1,17},{9,25},{17,1},{25,9},{2,18},{10... | collective-permute-start | bytes 393224 | tf_op jit(solution)/shard_map/ppermute | solution.py:235
  31.1 2.1 %collective-permute-start.15 = (bf16[8,16,512]{2,1,0:T(8,128)(2,1)S(1)}, bf16[8,16,512]{2,1,0:T(8,128)(2,1)S(1)}, u32[]{:S(2)}, u32[]{:S(2)}) collective-permute-start(bf16[8,16,512]{2,1,0:T(8,128)(2,1)S(1)} %get-tuple-element.114), channel_id=1, source_target_pairs={{0,8},{8,0},{16,24},{24,16},{1,9},{9,1},{17,25},{25,17},{2,10},{10... | collective-permute-start | bytes 393224 | tf_op jit(solution)/shard_map/ppermute | solution.py:235
  33.2 1.4 %collective-permute-done.10.refs_2_ = bf16[32,2048]{1,0:T(8,128)(2,1)S(1)} collective-permute-done((bf16[32,2048]{1,0:T(8,128)(2,1)S(1)}, bf16[32,2048]{1,0:T(8,128)(2,1)S(1)}, u32[]{:S(2)}, u32[]{:S(2)}) %collective-permute-start.10) | collective-permute-done | bytes 131104 | tf_op jit(solution)/shard_map/ppermute | solution.py:235
  34.6 0.7 %placed.1 = (bf16[1,4,8,16,512]{4,3,2,1,0:T(8,128)(2,1)}, f32[32,2048]{1,0:T(8,128)S(1)}) custom-call(bf16[8,16,512]{2,1,0:T(8,128)(2,1)S(1)} %get-tuple-element.98.refs_0_, bf16[8,16,512]{2,1,0:T(8,128)(2,1)S(1)} %collective-permute-done.8.refs_1_, bf16[32,2048]{1,0:T(8,128)(2,1)S(1)} %collective-permute-done.10.refs_2_, ...), custom_call_target="tpu_custom_call" | custom-call | tf_op jit(solution)/shard_map/placed/pallas_call | solution.py:749
  35.3 1.3 %collective-permute-done.13.refs_0_ = bf16[32,2048]{1,0:T(8,128)(2,1)S(1)} collective-permute-done((bf16[32,2048]{1,0:T(8,128)(2,1)S(1)}, bf16[32,2048]{1,0:T(8,128)(2,1)S(1)}, u32[]{:S(2)}, u32[]{:S(2)}) %collective-permute-start.13) | collective-permute-done | bytes 131104 | tf_op jit(solution)/shard_map/ppermute | solution.py:235
  36.6 0.8 %finished.1 = (f32[32,2048]{1,0:T(8,128)}, bf16[1,4,8,16,512]{4,3,2,1,0:T(8,128)(2,1)}) custom-call(f32[32,2048]{1,0:T(8,128)S(1)} %get-tuple-element.106.base_ref, bf16[32,2048]{1,0:T(8,128)(2,1)S(1)} %collective-permute-done.13.refs_0_, bf16[8,16,512]{2,1,0:T(8,128)(2,1)S(1)} %collective-permute-done.14.refs_1_, ...), custom_call_target="tpu_custom_call", output_to_operand_aliasing={{1}: (4, {})} | custom-call | tf_op jit(solution)/shard_map/finished/pallas_call | solution.py:786
  (11 shorter events, 0.1 us)
Async XLA Ops:
  0.6 10.4 %collective-permute-start = (bf16[32,2048]{1,0:T(8,128)(2,1)}, bf16[32,2048]{1,0:T(8,128)(2,1)S(1)}, u32[]{:S(2)}, u32[]{:S(2)}) collective-permute-start(bf16[32,2048]{1,0:T(8,128)(2,1)} %refs_2_.1), channel_id=1, source_target_pairs={{0,6},{1,7},{2,4},{3,5},{4,2},{5,3},{6,0},{7,1},{8,14},{9,15},{10,... | collective-permute-start | bytes 393224 | tf_op jit(solution)/shard_map/ppermute | solution.py:235
  5.7 7.4 %collective-permute-start.3 = (bf16[32,2048]{1,0:T(8,128)(2,1)}, bf16[32,2048]{1,0:T(8,128)(2,1)S(1)}, u32[]{:S(2)}, u32[]{:S(2)}) collective-permute-start(bf16[32,2048]{1,0:T(8,128)(2,1)} %refs_2_.1), channel_id=1, source_target_pairs={{0,1},{1,0},{2,3},{3,2},{4,5},{5,4},{6,7},{7,6},{8,9},{9,8},{10,11... | collective-permute-start | bytes 393224 | tf_op jit(solution)/shard_map/ppermute | solution.py:235
  5.8 7.4 %collective-permute-start.2 = (bf16[32,2048]{1,0:T(8,128)(2,1)}, bf16[32,2048]{1,0:T(8,128)(2,1)S(1)}, u32[]{:S(2)}, u32[]{:S(2)}) collective-permute-start(bf16[32,2048]{1,0:T(8,128)(2,1)} %refs_2_.1), channel_id=1, source_target_pairs={{0,2},{1,3},{2,0},{3,1},{4,6},{5,7},{6,4},{7,5},{8,10},{9,11},{10,... | collective-permute-start | bytes 393224 | tf_op jit(solution)/shard_map/ppermute | solution.py:235
  11.0 6.0 %collective-permute-start.1 = (bf16[32,2048]{1,0:T(8,128)(2,1)S(1)}, bf16[32,2048]{1,0:T(8,128)(2,1)S(1)}, u32[]{:S(2)}, u32[]{:S(2)}) collective-permute-start(bf16[32,2048]{1,0:T(8,128)(2,1)S(1)} %collective-permute-done.refs_1_), channel_id=1, source_target_pairs={{0,2},{1,3},{2,0},{3,1},{4,6},{5,7},{6,4},{7,5},{8,10},{9,11},{10,... | collective-permute-start | bytes 393224 | tf_op jit(solution)/shard_map/ppermute | solution.py:235
  15.4 1.6 %collective-permute-start.4 = (bf16[32,2048]{1,0:T(8,128)(2,1)S(1)}, bf16[32,2048]{1,0:T(8,128)(2,1)S(1)}, u32[]{:S(2)}, u32[]{:S(2)}) collective-permute-start(bf16[32,2048]{1,0:T(8,128)(2,1)S(1)} %collective-permute-done.2.refs_2_), channel_id=1, source_target_pairs={{0,1},{1,0},{2,3},{3,2},{4,5},{5,4},{6,7},{7,6},{8,9},{9,8},{10,11... | collective-permute-start | bytes 393224 | tf_op jit(solution)/shard_map/ppermute | solution.py:235
  15.5 1.6 %collective-permute-start.5 = (bf16[32,2048]{1,0:T(8,128)(2,1)S(1)}, bf16[32,2048]{1,0:T(8,128)(2,1)S(1)}, u32[]{:S(2)}, u32[]{:S(2)}) collective-permute-start(bf16[32,2048]{1,0:T(8,128)(2,1)S(1)} %collective-permute-done.refs_1_), channel_id=1, source_target_pairs={{0,1},{1,0},{2,3},{3,2},{4,5},{5,4},{6,7},{7,6},{8,9},{9,8},{10,11... | collective-permute-start | bytes 393224 | tf_op jit(solution)/shard_map/ppermute | solution.py:235
  17.0 1.4 %collective-permute-start.6 = (bf16[32,2048]{1,0:T(8,128)(2,1)S(1)}, bf16[32,2048]{1,0:T(8,128)(2,1)S(1)}, u32[]{:S(2)}, u32[]{:S(2)}) collective-permute-start(bf16[32,2048]{1,0:T(8,128)(2,1)S(1)} %collective-permute-done.1.refs_2_), channel_id=1, source_target_pairs={{0,1},{1,0},{2,3},{3,2},{4,5},{5,4},{6,7},{7,6},{8,9},{9,8},{10,11... | collective-permute-start | bytes 393224 | tf_op jit(solution)/shard_map/ppermute | solution.py:235
  20.6 1.5 %collective-permute-start.7 = (bf16[32,2048]{1,0:T(8,128)(2,1)S(1)}, bf16[32,2048]{1,0:T(8,128)(2,1)S(1)}, u32[]{:S(2)}, u32[]{:S(2)}) collective-permute-start(bf16[32,2048]{1,0:T(8,128)(2,1)S(1)} %get-tuple-element.87), channel_id=1, source_target_pairs={{0,1},{1,0},{2,3},{3,2},{4,5},{5,4},{6,7},{7,6},{8,9},{9,8},{10,11... | collective-permute-start | bytes 393224 | tf_op jit(solution)/shard_map/ppermute | solution.py:235
  21.8 5.1 %collective-permute-start.9 = (bf16[2,32,2048]{2,1,0:T(8,128)(2,1)S(1)}, bf16[2,32,2048]{2,1,0:T(8,128)(2,1)S(1)}, u32[]{:S(2)}, u32[]{:S(2)}) collective-permute-start(bf16[2,32,2048]{2,1,0:T(8,128)(2,1)S(1)} %get-tuple-element.100), channel_id=1, source_target_pairs={{0,1},{1,0},{2,3},{3,2},{4,5},{5,4},{6,7},{7,6},{8,9},{9,8},{10,11... | collective-permute-start | bytes 786440 | tf_op jit(solution)/shard_map/ppermute | solution.py:235
  22.1 5.8 %collective-permute-start.11 = (bf16[32,2048]{1,0:T(8,128)(2,1)S(1)}, bf16[32,2048]{1,0:T(8,128)(2,1)S(1)}, u32[]{:S(2)}, u32[]{:S(2)}) collective-permute-start(bf16[32,2048]{1,0:T(8,128)(2,1)S(1)} %third_added.1), channel_id=1, source_target_pairs={{0,2},{1,3},{2,0},{3,1},{4,6},{5,7},{6,4},{7,5},{8,10},{9,11},{10,... | collective-permute-start | bytes 393224 | tf_op jit(solution)/shard_map/ppermute | solution.py:235
  24.3 3.6 %collective-permute-start.12 = (bf16[32,2048]{1,0:T(8,128)(2,1)S(1)}, bf16[32,2048]{1,0:T(8,128)(2,1)S(1)}, u32[]{:S(2)}, u32[]{:S(2)}) collective-permute-start(bf16[32,2048]{1,0:T(8,128)(2,1)S(1)} %get-tuple-element.109), channel_id=1, source_target_pairs={{0,1},{1,0},{2,3},{3,2},{4,5},{5,4},{6,7},{7,6},{8,9},{9,8},{10,11... | collective-permute-start | bytes 393224 | tf_op jit(solution)/shard_map/ppermute | solution.py:235
  24.3 8.8 %collective-permute-start.8 = (bf16[8,16,512]{2,1,0:T(8,128)(2,1)S(1)}, bf16[8,16,512]{2,1,0:T(8,128)(2,1)S(1)}, u32[]{:S(2)}, u32[]{:S(2)}) collective-permute-start(bf16[8,16,512]{2,1,0:T(8,128)(2,1)S(1)} %get-tuple-element.99), channel_id=1, source_target_pairs={{0,24},{8,16},{16,8},{24,0},{1,25},{9,17},{17,9},{25,1},{2,26},{10... | collective-permute-start | bytes 393224 | tf_op jit(solution)/shard_map/ppermute | solution.py:235
  26.9 7.6 %collective-permute-start.10 = (bf16[32,2048]{1,0:T(8,128)(2,1)S(1)}, bf16[32,2048]{1,0:T(8,128)(2,1)S(1)}, u32[]{:S(2)}, u32[]{:S(2)}) collective-permute-start(bf16[32,2048]{1,0:T(8,128)(2,1)S(1)} %get-tuple-element.104), channel_id=1, source_target_pairs={{0,2},{1,3},{2,0},{3,1},{4,6},{5,7},{6,4},{7,5},{8,10},{9,11},{10,... | collective-permute-start | bytes 393224 | tf_op jit(solution)/shard_map/ppermute | solution.py:235
  27.9 8.7 %collective-permute-start.13 = (bf16[32,2048]{1,0:T(8,128)(2,1)S(1)}, bf16[32,2048]{1,0:T(8,128)(2,1)S(1)}, u32[]{:S(2)}, u32[]{:S(2)}) collective-permute-start(bf16[32,2048]{1,0:T(8,128)(2,1)S(1)} %second_added.1), channel_id=1, source_target_pairs={{0,4},{1,5},{2,6},{3,7},{4,0},{5,1},{6,2},{7,3},{8,12},{9,13},{10,... | collective-permute-start | bytes 393224 | tf_op jit(solution)/shard_map/ppermute | solution.py:235
  29.6 7.1 %collective-permute-start.14 = (bf16[8,16,512]{2,1,0:T(8,128)(2,1)S(1)}, bf16[8,16,512]{2,1,0:T(8,128)(2,1)S(1)}, u32[]{:S(2)}, u32[]{:S(2)}) collective-permute-start(bf16[8,16,512]{2,1,0:T(8,128)(2,1)S(1)} %get-tuple-element.113), channel_id=1, source_target_pairs={{0,16},{8,24},{16,0},{24,8},{1,17},{9,25},{17,1},{25,9},{2,18},{10... | collective-permute-start | bytes 393224 | tf_op jit(solution)/shard_map/ppermute | solution.py:235
  31.1 5.5 %collective-permute-start.15 = (bf16[8,16,512]{2,1,0:T(8,128)(2,1)S(1)}, bf16[8,16,512]{2,1,0:T(8,128)(2,1)S(1)}, u32[]{:S(2)}, u32[]{:S(2)}) collective-permute-start(bf16[8,16,512]{2,1,0:T(8,128)(2,1)S(1)} %get-tuple-element.114), channel_id=1, source_target_pairs={{0,8},{8,0},{16,24},{24,16},{1,9},{9,1},{17,25},{25,17},{2,10},{10... | collective-permute-start | bytes 393224 | tf_op jit(solution)/shard_map/ppermute | solution.py:235

commit v21 on v20

--- a/solution.py
+++ b/solution.py
@@ -395,16 +395,20 @@
     destinations_ref[...] = slot * PAGE + (positions & (PAGE - 1))
 
 
-def copies_in(sources, targets, sems):
+def copies_in(sources, targets, sems, tails=False):
     copies = []
     for number, (source, target) in enumerate(zip(sources, targets)):
-        parts = 4 if source.shape[0] >= 256 else 1
-        rows = source.shape[0] // parts
-        places = [pl.ds(part * rows, rows) for part in range(parts)]
+        parts = 4 if target.shape[0] >= 256 else 1
+        rows = target.shape[0] // parts
+        skipped = source.shape[0] - target.shape[0] if tails else 0
         copies.append(
             [
-                pltpu.make_async_copy(source.at[place], target.at[place], sems.at[number, part])
-                for part, place in enumerate(places)
+                pltpu.make_async_copy(
+                    source.at[pl.ds(skipped + part * rows, rows)],
+                    target.at[pl.ds(part * rows, rows)],
+                    sems.at[number, part],
+                )
+                for part in range(parts)
             ]
         )
     for copy in sum(copies, []):
@@ -443,7 +447,9 @@
     tokens = staged[0].shape[1]
     rows, width = staged[2].shape
     hidden_width = staged[6].shape[1]
-    shapes = [pltpu.VMEM(array.shape, array.dtype) for array in staged]
+    shapes = [pltpu.VMEM(array.shape, array.dtype) for array in staged[:-1]]
+    depth = staged[-1].shape[0] // 2
+    shapes += [pltpu.VMEM((depth, width), staged[-1].dtype)]
     shapes += [pltpu.VMEM((tokens, 128), jnp.float32)] * 4
     shapes += [
         pltpu.VMEM((1, tokens), jnp.int32),
@@ -478,7 +484,7 @@
     staged = (len(refs) - 5) // 2
     sources, (joined_ref, hidden_ref), refs = refs[:staged], refs[staged:][:2], refs[staged + 2 :]
     targets, (attention_scr, feedforward_scr, sems) = refs[:staged], refs[staged:]
-    copies = copies_in(sources, targets, sems)
+    copies = copies_in(sources, targets, sems, True)
     block_rows = blocks[0].shape[0]
     normalize(blocks, [gain_a, gain_f], [attention_scr, feedforward_scr])
     places = [position_of(kind, half, block_rows) for kind, half in origins]
@@ -497,7 +503,7 @@
             pltpu.VMEM((rows, 3 * HD), jnp.bfloat16),
             pltpu.VMEM((rows, hidden_width), jnp.bfloat16),
         ]
-        + [pltpu.VMEM(array.shape, array.dtype) for array in staged],
+        + [pltpu.VMEM((count, array.shape[1]), array.dtype) for count, array in staged],
         in_specs=vmem_specs(len(blocks) + 2 + 2 + 3)
         + [pl.BlockSpec(memory_space=pltpu.HBM)] * len(staged),
         out_specs=vmem_specs(2 + len(staged)),
@@ -513,16 +519,16 @@
             transcendentals=rows * hidden_width,
         ),
         name=name,
-    )(*blocks, *gains, *weights, *tables, *[in_hbm(array) for array in staged])
+    )(*blocks, *gains, *weights, *tables, *[in_hbm(array) for _, array in staged])
 
 
 def last_kernel(*refs):
     block_ref, *normed_refs = refs[:3]
-    gain_a, gain_f, heads_ref, upward_ref, downward_ref, output_ref = refs[3:9]
-    offsets_ref, *table_refs = refs[9:13]
-    own_joined_ref, middle_joined_ref, early_ref = refs[13:16]
-    joined_ref, fed_ref, sibling_ref, own_ref = refs[16:20]
-    attention_scr, feedforward_scr, hidden_scr = refs[20:]
+    gain_a, gain_f, heads_ref, upward_ref, *downward_refs, output_ref = refs[3:10]
+    offsets_ref, *table_refs = refs[10:14]
+    own_joined_ref, middle_joined_ref, early_ref = refs[14:17]
+    joined_ref, fed_ref, sibling_ref, own_ref = refs[17:21]
+    attention_scr, feedforward_scr, hidden_scr = refs[21:]
     block_rows = block_ref.shape[0]
     tokens = joined_ref.shape[0]
     first = tokens - attention_scr.shape[0]
@@ -543,9 +549,9 @@
     hide(feedforward_scr, upward_ref, hidden_scr, 0)
     attended = attend(joined_ref, offsets_ref, early - block_rows, rows, block_rows)
     chunk = 512
-    for begin in range(0, downward_ref.shape[1], chunk):
+    for begin in range(0, output_ref.shape[1], chunk):
         columns = slice(begin, begin + chunk)
-        fed = jnp.dot(hidden_scr[...], downward_ref[:, columns], preferred_element_type=jnp.float32)
+        fed = down(hidden_scr[...], downward_refs, columns)
         fed_ref[:, columns] = fed[block_rows:]
         product = jnp.dot(attended, output_ref[:, columns], preferred_element_type=jnp.float32)
         own_ref[:, columns] = early_ref[early - block_rows : early, columns] + product[:block_rows]
@@ -566,7 +572,7 @@
             pltpu.VMEM((block_rows, width), jnp.bfloat16),
             pltpu.VMEM((block_rows, width), jnp.float32),
         ],
-        in_specs=vmem_specs(1 + 2 + 2 + 4 + 4 + 3),
+        in_specs=vmem_specs(1 + 2 + 2 + 5 + 4 + 3),
         out_specs=vmem_specs(4),
         scratch_shapes=[
             pltpu.VMEM((rows, width), jnp.bfloat16),
@@ -583,33 +589,44 @@
     )(block, *normed, *gains, *weights, *tables, own_joined, middle_joined, early)
 
 
-def fed_kernel(own_hidden_ref, middle_hidden_ref, downward_ref, *refs):
+def down(hidden, downward_refs, columns):
+    depth = downward_refs[0].shape[0]
+    upper, lower = [
+        jnp.dot(
+            hidden[:, number * depth : (number + 1) * depth],
+            downward_ref[:, columns],
+            preferred_element_type=jnp.float32,
+        )
+        for number, downward_ref in enumerate(downward_refs)
+    ]
+    return upper + lower
+
+
+def fed_kernel(own_hidden_ref, middle_hidden_ref, upper_ref, lower_ref, *refs):
     blocks, gain_refs, (fed_ref, *normed_refs) = refs[:-5], refs[-5:-3], refs[-3:]
     normalize(blocks, gain_refs, normed_refs)
     hidden = jnp.concatenate([own_hidden_ref[...], middle_hidden_ref[...]], 0)
     chunk = 512
-    for begin in range(0, downward_ref.shape[1], chunk):
+    for begin in range(0, upper_ref.shape[1], chunk):
         columns = slice(begin, begin + chunk)
-        fed_ref[:, columns] = jnp.dot(
-            hidden, downward_ref[:, columns], preferred_element_type=jnp.float32
-        )
-
-
-def fed_rows(own_hidden, middle_hidden, downward_weight, blocks, gains):
+        fed_ref[:, columns] = down(hidden, (upper_ref, lower_ref), columns)
+
+
+def fed_rows(own_hidden, middle_hidden, downward_weights, blocks, gains):
     rows = own_hidden.shape[0] + middle_hidden.shape[0]
-    depth, width = downward_weight.shape
+    depth, width = own_hidden.shape[1], downward_weights[0].shape[1]
     normed = pltpu.VMEM((len(blocks) * blocks[0].shape[0], width), jnp.bfloat16)
     return pl.pallas_call(
         fed_kernel,
         out_shape=[pltpu.VMEM((rows, width), jnp.float32), normed, normed],
-        in_specs=vmem_specs(5 + len(blocks)),
+        in_specs=vmem_specs(6 + len(blocks)),
         out_specs=vmem_specs(3),
         compiler_params=parameters(12),
         cost_estimate=pl.CostEstimate(
             flops=2 * rows * depth * width, bytes_accessed=MIB, transcendentals=0
         ),
         name="fed_rows",
-    )(own_hidden, middle_hidden, downward_weight, *blocks, *gains)
+    )(own_hidden, middle_hidden, *downward_weights, *blocks, *gains)
 
 
 def rest_kernel(joined_ref, offsets_ref, output_ref, early_ref, late_ref, *refs):
@@ -836,14 +853,15 @@
 
     third, own_joined = lax.optimization_barrier((third, own_joined))
     second = exchanged(third, "tensor", to_chip[1])
-    middle_joined, middle_hidden, output = middle_rows(
+    middle_joined, middle_hidden, lower, output = middle_rows(
         "middle_rows",
         ((0, 1), (3, 0), (1, 0)),
         (beside, third, first),
         gains,
         (heads, upward),
         tables[1:],
-        output_weight,
+        (downward_weight.shape[0] // 2, downward_weight),
+        (output_weight.shape[0], output_weight),
     )
     third, first, middle_joined = lax.optimization_barrier((third, first, middle_joined))
     first_beside = exchanged(first, "tensor", 1)
@@ -853,13 +871,13 @@
     )
     second_beside = exchanged(second, "tensor", 1)
     fed, *normed = fed_rows(
-        own_hidden, middle_hidden, downward, (third_beside, first_beside, second), gains
+        own_hidden, middle_hidden, (downward, lower), (third_beside, first_beside, second), gains
     )
     joined, fed_late, sibling, own = last_rows(
         second_beside,
         normed,
         gains,
-        (heads, upward, downward, output),
+        (heads, upward, downward, lower, output),
         tables,
         own_joined,
         middle_joined,

time: 37.6 us -> 38 us (1.011)
  Pallas kernels: 13.4 us -> 13.8 us
    pallas_call x1, Pallas kernels: 2.23 us -> 2.91 us  [middle_rows(): pl.pallas_call(functools.partial(middle_kernel, origins), out_shape=[pltp...]
  transfers between devices with their start and end apart: 16 -> 16, of which waited for: 5 -> 7; matrix products, arithmetic and copies ran while one was open for 0% -> 0% of each run, Pallas kernels for 28% -> 28%
where the time goes in v21:
time: 38 us; the launch traced here: 37.8 us
  starting transfers between devices  19 us (50%)
  Pallas kernels  13.8 us (36%)
  waiting for transfers between devices  4.31 us (11%)
  between operations  0.72 us (2%)
    ppermute x16, starting transfers between devices, exchanged(): lax.ppermute(block, axis, [(member, member ^ mask) for member in range(co...  19 us
    pallas_call x1, Pallas kernels, own_rows(): pl.pallas_call(functools.partial(own_kernel, count, replica_count), out_s...  4.93 us
    ppermute x16, waiting for transfers between devices, exchanged(): lax.ppermute(block, axis, [(member, member ^ mask) for member in range(co...  4.31 us
    pallas_call x1, Pallas kernels, middle_rows(): pl.pallas_call(functools.partial(middle_kernel, origins), out_shape=[pltp...  2.91 us
    pallas_call x1, Pallas kernels, last_rows(): pl.pallas_call(last_kernel, out_shape=[pltpu.VMEM((tokens, 3 * HD), jnp.b...  2.25 us
    pallas_call x1, Pallas kernels, fed_rows(): pl.pallas_call(fed_kernel, out_shape=[pltpu.VMEM((rows, width), jnp.float...  0.84 us
    pallas_call x1, Pallas kernels, rest_rows(): pl.pallas_call(rest_kernel, out_shape=shapes, in_specs=vmem_specs(5), out...  0.83 us
    pallas_call x1, Pallas kernels, finished(): pl.pallas_call(functools.partial(finish_kernel, masks), out_shape=[jax.Sh...  0.83 us
  transfers between devices with their start and end apart: 16, of which 7 were waited for; matrix products, arithmetic and copies ran while one was open for 0% of the time, Pallas kernels for 28%

profile of v21, /device:TPU:0, one launch (start us, length us, event | category | flops | bytes accessed | tf_op | source)
XLA Modules:
  0.0 37.8 jit_solution(3515390698056205367)
XLA Ops:
  0.6 5.1 %collective-permute-start = (bf16[32,2048]{1,0:T(8,128)(2,1)}, bf16[32,2048]{1,0:T(8,128)(2,1)S(1)}, u32[]{:S(2)}, u32[]{:S(2)}) collective-permute-start(bf16[32,2048]{1,0:T(8,128)(2,1)} %refs_2_.1), channel_id=1, source_target_pairs={{0,6},{1,7},{2,4},{3,5},{4,2},{5,3},{6,0},{7,1},{8,14},{9,15},{10,... | collective-permute-start | bytes 393224 | tf_op jit(solution)/shard_map/ppermute | solution.py:235
  5.7 0.0 collective-permute-start.3
  5.7 0.0 collective-permute-start.2
  5.8 4.9 %own_rows.1 = (s32[1,256]{1,0:T(1,128)}, s32[1,16]{1,0:T(1,128)}, bf16[32,2048]{1,0:T(8,128)(2,1)S(1)}, f32[1,2048]{1,0:T(1,128)S(1)}, f32[1,2048]{1,0:T(1,128)S...) custom-call(s32[1,256]{1,0:T(1,128)} %refs_0_.1, ...), custom_call_target="tpu_custom_call" | custom-call | flops 234881024 | bytes 11682880 | tf_op jit(solution)/shard_map/own_rows/pallas_call | solution.py:460
  10.7 2.1 %collective-permute-start.1 = (bf16[32,2048]{1,0:T(8,128)(2,1)S(1)}, bf16[32,2048]{1,0:T(8,128)(2,1)S(1)}, u32[]{:S(2)}, u32[]{:S(2)}) collective-permute-start(bf16[32,2048]{1,0:T(8,128)(2,1)S(1)} %collective-permute-done.refs_1_), channel_id=1, source_target_pairs={{0,2},{1,3},{2,0},{3,1},{4,6},{5,7},{6,4},{7,5},{8,10},{9,11},{10,... | collective-permute-start | bytes 393224 | tf_op jit(solution)/shard_map/ppermute | solution.py:235
  12.8 2.9 %middle_rows.1 = (bf16[96,768]{1,0:T(8,128)(2,1)S(1)}, bf16[96,1024]{1,0:T(8,128)(2,1)S(1)}, bf16[512,2048]{1,0:T(8,128)(2,1)S(1)}, bf16[256,2048]{1,0:T(8,128)(2,1)S(1)}) custom-call(bf16[32,2048]{1,0:T(8,128)(2,1)S(1)} %collective-permute-done.3.refs_0_, bf16[32,2048]{1,0:T(8,128)(2,1)S(1)} %collective-permute-done.refs_1_, ...), custom_call_target="tpu_custom_call" | custom-call | flops 704643072 | bytes 1048576 | tf_op jit(solution)/shard_map/middle_rows/pallas_call | solution.py:500
  15.7 0.1 collective-permute-start.4
  15.8 0.5 %collective-permute-start.5 = (bf16[32,2048]{1,0:T(8,128)(2,1)S(1)}, bf16[32,2048]{1,0:T(8,128)(2,1)S(1)}, u32[]{:S(2)}, u32[]{:S(2)}) collective-permute-start(bf16[32,2048]{1,0:T(8,128)(2,1)S(1)} %collective-permute-done.refs_1_), channel_id=1, source_target_pairs={{0,1},{1,0},{2,3},{3,2},{4,5},{5,4},{6,7},{7,6},{8,9},{9,8},{10,11... | collective-permute-start | bytes 393224 | tf_op jit(solution)/shard_map/ppermute | solution.py:235
  16.3 0.4 %collective-permute-done.1.refs_2_ = bf16[32,2048]{1,0:T(8,128)(2,1)S(1)} collective-permute-done((bf16[32,2048]{1,0:T(8,128)(2,1)S(1)}, bf16[32,2048]{1,0:T(8,128)(2,1)S(1)}, u32[]{:S(2)}, u32[]{:S(2)}) %collective-permute-start.1) | collective-permute-done | bytes 131104 | tf_op jit(solution)/shard_map/ppermute | solution.py:235
  16.7 0.4 %collective-permute-done.4.refs_1_ = bf16[32,2048]{1,0:T(8,128)(2,1)S(1)} collective-permute-done((bf16[32,2048]{1,0:T(8,128)(2,1)S(1)}, bf16[32,2048]{1,0:T(8,128)(2,1)S(1)}, u32[]{:S(2)}, u32[]{:S(2)}) %collective-permute-start.4) | collective-permute-done | bytes 131104 | tf_op jit(solution)/shard_map/ppermute | solution.py:235
  17.1 0.2 collective-permute-done.5.refs_0_
  17.3 0.3 collective-permute-start.6
  17.6 0.8 %fed_rows.1 = (f32[128,2048]{1,0:T(8,128)S(1)}, bf16[96,2048]{1,0:T(8,128)(2,1)S(1)}, bf16[96,2048]{1,0:T(8,128)(2,1)S(1)}) custom-call(bf16[32,1024]{1,0:T(8,128)(2,1)S(1)} %get-tuple-element.75.own_hidden_ref, bf16[96,1024]{1,0:T(8,128)(2,1)S(1)} %get-tuple-element.76.middle_hidden_ref, bf16[512,2048]{1,0:T(8,128)(2,1)S(1)} %get-tuple-element.77.upper_ref.refs_7_, ...), custom_call_target="tpu_custom_call" | custom-call | flops 536870912 | bytes 1048576 | tf_op jit(solution)/shard_map/fed_rows/pallas_call | solution.py:619
  18.5 0.2 collective-permute-done.6.refs_0_
  18.7 2.2 %last_rows.1 = (bf16[256,768]{1,0:T(8,128)(2,1)S(1)}, f32[96,2048]{1,0:T(8,128)S(1)}, bf16[32,2048]{1,0:T(8,128)(2,1)S(1)}, f32[32,2048]{1,0:T(8,128)S(1)}) custom-call(bf16[32,2048]{1,0:T(8,128)(2,1)S(1)} %collective-permute-done.6.refs_0_, bf16[96,2048]{1,0:T(8,128)(2,1)S(1)} %get-tuple-element.81.refs_1_, bf16[96,2048]{1,0:T(8,128)(2,1)S(1)} %get-tuple-element.82.refs_2_, ...), custom_call_target="tpu_custom_call" | custom-call | flops 1610612736 | bytes 1048576 | tf_op jit(solution)/shard_map/last_rows/pallas_call | solution.py:567
  20.9 0.4 collective-permute-start.7
  21.3 0.8 %rest_rows.1 = (bf16[2,32,2048]{2,1,0:T(8,128)(2,1)S(1)}, bf16[32,2048]{1,0:T(8,128)(2,1)S(1)}, f32[32,2048]{1,0:T(8,128)S(1)}, f32[32,2048]{1,0:T(8,128)S(1)}, f32[32,2048]{1,0:T(8,128)S(1)}) custom-call(bf16[256,768]{1,0:T(8,128)(2,1)S(1)} %get-tuple-element.94.joined_ref, f32[256,128]{1,0:T(8,128)S(1)} %get-tuple-element.84.refs_10_.offsets_ref, ...), custom_call_target="tpu_custom_call" | custom-call | flops 201326592 | bytes 1048576 | tf_op jit(solution)/shard_map/rest_rows/pallas_call | solution.py:671
  22.1 0.2 collective-permute-start.9
  22.4 1.3 %collective-permute-start.11 = (bf16[32,2048]{1,0:T(8,128)(2,1)S(1)}, bf16[32,2048]{1,0:T(8,128)(2,1)S(1)}, u32[]{:S(2)}, u32[]{:S(2)}) collective-permute-start(bf16[32,2048]{1,0:T(8,128)(2,1)S(1)} %third_added.1), channel_id=1, source_target_pairs={{0,2},{1,3},{2,0},{3,1},{4,6},{5,7},{6,4},{7,5},{8,10},{9,11},{10,... | collective-permute-start | bytes 393224 | tf_op jit(solution)/shard_map/ppermute | solution.py:235
  23.7 0.3 cached_pages.1
  24.0 0.1 collective-permute-start.12
  24.1 2.5 %collective-permute-start.8 = (bf16[8,16,512]{2,1,0:T(8,128)(2,1)S(1)}, bf16[8,16,512]{2,1,0:T(8,128)(2,1)S(1)}, u32[]{:S(2)}, u32[]{:S(2)}) collective-permute-start(bf16[8,16,512]{2,1,0:T(8,128)(2,1)S(1)} %get-tuple-element.101), channel_id=1, source_target_pairs={{0,24},{8,16},{16,8},{24,0},{1,25},{9,17},{17,9},{25,1},{2,26},{10... | collective-permute-start | bytes 393224 | tf_op jit(solution)/shard_map/ppermute | solution.py:235
  26.6 0.1 near_sums.1
  26.7 0.8 %collective-permute-start.10 = (bf16[32,2048]{1,0:T(8,128)(2,1)S(1)}, bf16[32,2048]{1,0:T(8,128)(2,1)S(1)}, u32[]{:S(2)}, u32[]{:S(2)}) collective-permute-start(bf16[32,2048]{1,0:T(8,128)(2,1)S(1)} %get-tuple-element.106), channel_id=1, source_target_pairs={{0,2},{1,3},{2,0},{3,1},{4,6},{5,7},{6,4},{7,5},{8,10},{9,11},{10,... | collective-permute-start | bytes 393224 | tf_op jit(solution)/shard_map/ppermute | solution.py:235
  27.5 0.7 %collective-permute-done.11.refs_1_ = bf16[32,2048]{1,0:T(8,128)(2,1)S(1)} collective-permute-done((bf16[32,2048]{1,0:T(8,128)(2,1)S(1)}, bf16[32,2048]{1,0:T(8,128)(2,1)S(1)}, u32[]{:S(2)}, u32[]{:S(2)}) %collective-permute-start.11) | collective-permute-done | bytes 131104 | tf_op jit(solution)/shard_map/ppermute | solution.py:235
  28.2 2.0 %collective-permute-start.13 = (bf16[32,2048]{1,0:T(8,128)(2,1)S(1)}, bf16[32,2048]{1,0:T(8,128)(2,1)S(1)}, u32[]{:S(2)}, u32[]{:S(2)}) collective-permute-start(bf16[32,2048]{1,0:T(8,128)(2,1)S(1)} %second_added.1), channel_id=1, source_target_pairs={{0,4},{1,5},{2,6},{3,7},{4,0},{5,1},{6,2},{7,3},{8,12},{9,13},{10,... | collective-permute-start | bytes 393224 | tf_op jit(solution)/shard_map/ppermute | solution.py:235
  30.2 1.5 %collective-permute-start.14 = (bf16[8,16,512]{2,1,0:T(8,128)(2,1)S(1)}, bf16[8,16,512]{2,1,0:T(8,128)(2,1)S(1)}, u32[]{:S(2)}, u32[]{:S(2)}) collective-permute-start(bf16[8,16,512]{2,1,0:T(8,128)(2,1)S(1)} %get-tuple-element.115), channel_id=1, source_target_pairs={{0,16},{8,24},{16,0},{24,8},{1,17},{9,25},{17,1},{25,9},{2,18},{10... | collective-permute-start | bytes 393224 | tf_op jit(solution)/shard_map/ppermute | solution.py:235
  31.7 2.1 %collective-permute-start.15 = (bf16[8,16,512]{2,1,0:T(8,128)(2,1)S(1)}, bf16[8,16,512]{2,1,0:T(8,128)(2,1)S(1)}, u32[]{:S(2)}, u32[]{:S(2)}) collective-permute-start(bf16[8,16,512]{2,1,0:T(8,128)(2,1)S(1)} %get-tuple-element.116), channel_id=1, source_target_pairs={{0,8},{8,0},{16,24},{24,16},{1,9},{9,1},{17,25},{25,17},{2,10},{10... | collective-permute-start | bytes 393224 | tf_op jit(solution)/shard_map/ppermute | solution.py:235
  33.8 0.6 %collective-permute-done.10.refs_2_ = bf16[32,2048]{1,0:T(8,128)(2,1)S(1)} collective-permute-done((bf16[32,2048]{1,0:T(8,128)(2,1)S(1)}, bf16[32,2048]{1,0:T(8,128)(2,1)S(1)}, u32[]{:S(2)}, u32[]{:S(2)}) %collective-permute-start.10) | collective-permute-done | bytes 131104 | tf_op jit(solution)/shard_map/ppermute | solution.py:235
  34.4 0.7 %placed.1 = (bf16[1,4,8,16,512]{4,3,2,1,0:T(8,128)(2,1)}, f32[32,2048]{1,0:T(8,128)S(1)}) custom-call(bf16[8,16,512]{2,1,0:T(8,128)(2,1)S(1)} %get-tuple-element.100.refs_0_, bf16[8,16,512]{2,1,0:T(8,128)(2,1)S(1)} %collective-permute-done.8.refs_1_, bf16[32,2048]{1,0:T(8,128)(2,1)S(1)} %collective-permute-done.10.refs_2_, ...), custom_call_target="tpu_custom_call" | custom-call | tf_op jit(solution)/shard_map/placed/pallas_call | solution.py:766
  35.2 1.8 %collective-permute-done.13.refs_0_ = bf16[32,2048]{1,0:T(8,128)(2,1)S(1)} collective-permute-done((bf16[32,2048]{1,0:T(8,128)(2,1)S(1)}, bf16[32,2048]{1,0:T(8,128)(2,1)S(1)}, u32[]{:S(2)}, u32[]{:S(2)}) %collective-permute-start.13) | collective-permute-done | bytes 131104 | tf_op jit(solution)/shard_map/ppermute | solution.py:235
  37.0 0.8 %finished.1 = (f32[32,2048]{1,0:T(8,128)}, bf16[1,4,8,16,512]{4,3,2,1,0:T(8,128)(2,1)}) custom-call(f32[32,2048]{1,0:T(8,128)S(1)} %get-tuple-element.108.base_ref, bf16[32,2048]{1,0:T(8,128)(2,1)S(1)} %collective-permute-done.13.refs_0_, bf16[8,16,512]{2,1,0:T(8,128)(2,1)S(1)} %collective-permute-done.14.refs_1_, ...), custom_call_target="tpu_custom_call", output_to_operand_aliasing={{1}: (4, {})} | custom-call | tf_op jit(solution)/shard_map/finished/pallas_call | solution.py:803
  (11 shorter events, 0.1 us)
Async XLA Ops:
  0.6 10.1 %collective-permute-start = (bf16[32,2048]{1,0:T(8,128)(2,1)}, bf16[32,2048]{1,0:T(8,128)(2,1)S(1)}, u32[]{:S(2)}, u32[]{:S(2)}) collective-permute-start(bf16[32,2048]{1,0:T(8,128)(2,1)} %refs_2_.1), channel_id=1, source_target_pairs={{0,6},{1,7},{2,4},{3,5},{4,2},{5,3},{6,0},{7,1},{8,14},{9,15},{10,... | collective-permute-start | bytes 393224 | tf_op jit(solution)/shard_map/ppermute | solution.py:235
  5.7 7.0 %collective-permute-start.3 = (bf16[32,2048]{1,0:T(8,128)(2,1)}, bf16[32,2048]{1,0:T(8,128)(2,1)S(1)}, u32[]{:S(2)}, u32[]{:S(2)}) collective-permute-start(bf16[32,2048]{1,0:T(8,128)(2,1)} %refs_2_.1), channel_id=1, source_target_pairs={{0,1},{1,0},{2,3},{3,2},{4,5},{5,4},{6,7},{7,6},{8,9},{9,8},{10,11... | collective-permute-start | bytes 393224 | tf_op jit(solution)/shard_map/ppermute | solution.py:235
  5.7 7.0 %collective-permute-start.2 = (bf16[32,2048]{1,0:T(8,128)(2,1)}, bf16[32,2048]{1,0:T(8,128)(2,1)S(1)}, u32[]{:S(2)}, u32[]{:S(2)}) collective-permute-start(bf16[32,2048]{1,0:T(8,128)(2,1)} %refs_2_.1), channel_id=1, source_target_pairs={{0,2},{1,3},{2,0},{3,1},{4,6},{5,7},{6,4},{7,5},{8,10},{9,11},{10,... | collective-permute-start | bytes 393224 | tf_op jit(solution)/shard_map/ppermute | solution.py:235
  10.7 6.0 %collective-permute-start.1 = (bf16[32,2048]{1,0:T(8,128)(2,1)S(1)}, bf16[32,2048]{1,0:T(8,128)(2,1)S(1)}, u32[]{:S(2)}, u32[]{:S(2)}) collective-permute-start(bf16[32,2048]{1,0:T(8,128)(2,1)S(1)} %collective-permute-done.refs_1_), channel_id=1, source_target_pairs={{0,2},{1,3},{2,0},{3,1},{4,6},{5,7},{6,4},{7,5},{8,10},{9,11},{10,... | collective-permute-start | bytes 393224 | tf_op jit(solution)/shard_map/ppermute | solution.py:235
  15.7 1.4 %collective-permute-start.4 = (bf16[32,2048]{1,0:T(8,128)(2,1)S(1)}, bf16[32,2048]{1,0:T(8,128)(2,1)S(1)}, u32[]{:S(2)}, u32[]{:S(2)}) collective-permute-start(bf16[32,2048]{1,0:T(8,128)(2,1)S(1)} %collective-permute-done.2.refs_2_), channel_id=1, source_target_pairs={{0,1},{1,0},{2,3},{3,2},{4,5},{5,4},{6,7},{7,6},{8,9},{9,8},{10,11... | collective-permute-start | bytes 393224 | tf_op jit(solution)/shard_map/ppermute | solution.py:235
  15.8 1.5 %collective-permute-start.5 = (bf16[32,2048]{1,0:T(8,128)(2,1)S(1)}, bf16[32,2048]{1,0:T(8,128)(2,1)S(1)}, u32[]{:S(2)}, u32[]{:S(2)}) collective-permute-start(bf16[32,2048]{1,0:T(8,128)(2,1)S(1)} %collective-permute-done.refs_1_), channel_id=1, source_target_pairs={{0,1},{1,0},{2,3},{3,2},{4,5},{5,4},{6,7},{7,6},{8,9},{9,8},{10,11... | collective-permute-start | bytes 393224 | tf_op jit(solution)/shard_map/ppermute | solution.py:235
  17.3 1.3 %collective-permute-start.6 = (bf16[32,2048]{1,0:T(8,128)(2,1)S(1)}, bf16[32,2048]{1,0:T(8,128)(2,1)S(1)}, u32[]{:S(2)}, u32[]{:S(2)}) collective-permute-start(bf16[32,2048]{1,0:T(8,128)(2,1)S(1)} %collective-permute-done.1.refs_2_), channel_id=1, source_target_pairs={{0,1},{1,0},{2,3},{3,2},{4,5},{5,4},{6,7},{7,6},{8,9},{9,8},{10,11... | collective-permute-start | bytes 393224 | tf_op jit(solution)/shard_map/ppermute | solution.py:235
  20.9 1.5 %collective-permute-start.7 = (bf16[32,2048]{1,0:T(8,128)(2,1)S(1)}, bf16[32,2048]{1,0:T(8,128)(2,1)S(1)}, u32[]{:S(2)}, u32[]{:S(2)}) collective-permute-start(bf16[32,2048]{1,0:T(8,128)(2,1)S(1)} %get-tuple-element.89), channel_id=1, source_target_pairs={{0,1},{1,0},{2,3},{3,2},{4,5},{5,4},{6,7},{7,6},{8,9},{9,8},{10,11... | collective-permute-start | bytes 393224 | tf_op jit(solution)/shard_map/ppermute | solution.py:235
  22.1 4.5 %collective-permute-start.9 = (bf16[2,32,2048]{2,1,0:T(8,128)(2,1)S(1)}, bf16[2,32,2048]{2,1,0:T(8,128)(2,1)S(1)}, u32[]{:S(2)}, u32[]{:S(2)}) collective-permute-start(bf16[2,32,2048]{2,1,0:T(8,128)(2,1)S(1)} %get-tuple-element.102), channel_id=1, source_target_pairs={{0,1},{1,0},{2,3},{3,2},{4,5},{5,4},{6,7},{7,6},{8,9},{9,8},{10,11... | collective-permute-start | bytes 786440 | tf_op jit(solution)/shard_map/ppermute | solution.py:235
  22.4 5.8 %collective-permute-start.11 = (bf16[32,2048]{1,0:T(8,128)(2,1)S(1)}, bf16[32,2048]{1,0:T(8,128)(2,1)S(1)}, u32[]{:S(2)}, u32[]{:S(2)}) collective-permute-start(bf16[32,2048]{1,0:T(8,128)(2,1)S(1)} %third_added.1), channel_id=1, source_target_pairs={{0,2},{1,3},{2,0},{3,1},{4,6},{5,7},{6,4},{7,5},{8,10},{9,11},{10,... | collective-permute-start | bytes 393224 | tf_op jit(solution)/shard_map/ppermute | solution.py:235
  24.0 4.2 %collective-permute-start.12 = (bf16[32,2048]{1,0:T(8,128)(2,1)S(1)}, bf16[32,2048]{1,0:T(8,128)(2,1)S(1)}, u32[]{:S(2)}, u32[]{:S(2)}) collective-permute-start(bf16[32,2048]{1,0:T(8,128)(2,1)S(1)} %get-tuple-element.111), channel_id=1, source_target_pairs={{0,1},{1,0},{2,3},{3,2},{4,5},{5,4},{6,7},{7,6},{8,9},{9,8},{10,11... | collective-permute-start | bytes 393224 | tf_op jit(solution)/shard_map/ppermute | solution.py:235
  24.1 9.7 %collective-permute-start.8 = (bf16[8,16,512]{2,1,0:T(8,128)(2,1)S(1)}, bf16[8,16,512]{2,1,0:T(8,128)(2,1)S(1)}, u32[]{:S(2)}, u32[]{:S(2)}) collective-permute-start(bf16[8,16,512]{2,1,0:T(8,128)(2,1)S(1)} %get-tuple-element.101), channel_id=1, source_target_pairs={{0,24},{8,16},{16,8},{24,0},{1,25},{9,17},{17,9},{25,1},{2,26},{10... | collective-permute-start | bytes 393224 | tf_op jit(solution)/shard_map/ppermute | solution.py:235
  26.7 7.7 %collective-permute-start.10 = (bf16[32,2048]{1,0:T(8,128)(2,1)S(1)}, bf16[32,2048]{1,0:T(8,128)(2,1)S(1)}, u32[]{:S(2)}, u32[]{:S(2)}) collective-permute-start(bf16[32,2048]{1,0:T(8,128)(2,1)S(1)} %get-tuple-element.106), channel_id=1, source_target_pairs={{0,2},{1,3},{2,0},{3,1},{4,6},{5,7},{6,4},{7,5},{8,10},{9,11},{10,... | collective-permute-start | bytes 393224 | tf_op jit(solution)/shard_map/ppermute | solution.py:235
  28.2 8.7 %collective-permute-start.13 = (bf16[32,2048]{1,0:T(8,128)(2,1)S(1)}, bf16[32,2048]{1,0:T(8,128)(2,1)S(1)}, u32[]{:S(2)}, u32[]{:S(2)}) collective-permute-start(bf16[32,2048]{1,0:T(8,128)(2,1)S(1)} %second_added.1), channel_id=1, source_target_pairs={{0,4},{1,5},{2,6},{3,7},{4,0},{5,1},{6,2},{7,3},{8,12},{9,13},{10,... | collective-permute-start | bytes 393224 | tf_op jit(solution)/shard_map/ppermute | solution.py:235
  30.2 6.8 %collective-permute-start.14 = (bf16[8,16,512]{2,1,0:T(8,128)(2,1)S(1)}, bf16[8,16,512]{2,1,0:T(8,128)(2,1)S(1)}, u32[]{:S(2)}, u32[]{:S(2)}) collective-permute-start(bf16[8,16,512]{2,1,0:T(8,128)(2,1)S(1)} %get-tuple-element.115), channel_id=1, source_target_pairs={{0,16},{8,24},{16,0},{24,8},{1,17},{9,25},{17,1},{25,9},{2,18},{10... | collective-permute-start | bytes 393224 | tf_op jit(solution)/shard_map/ppermute | solution.py:235
  31.7 5.3 %collective-permute-start.15 = (bf16[8,16,512]{2,1,0:T(8,128)(2,1)S(1)}, bf16[8,16,512]{2,1,0:T(8,128)(2,1)S(1)}, u32[]{:S(2)}, u32[]{:S(2)}) collective-permute-start(bf16[8,16,512]{2,1,0:T(8,128)(2,1)S(1)} %get-tuple-element.116), channel_id=1, source_target_pairs={{0,8},{8,0},{16,24},{24,16},{1,9},{9,1},{17,25},{25,17},{2,10},{10... | collective-permute-start | bytes 393224 | tf_op jit(solution)/shard_map/ppermute | solution.py:235

commit v22 on v20

--- a/solution.py
+++ b/solution.py
@@ -283,8 +283,8 @@
 
 
 def project(normed_ref, heads_ref, table_refs, places, joined_ref, first):
-    rows = normed_ref.shape[0]
-    block_rows = rows // len(places)
+    block_rows = normed_ref.shape[0] // (4 if len(places) == 3 else len(places))
+    rows = block_rows * len(places)
     own = slice(first, first + rows)
     cosine, sine_down, sine_up = [
         jnp.concatenate(
@@ -298,9 +298,10 @@
     ]
     for begin in range(0, heads_ref.shape[1], HD):
         columns = slice(begin, begin + HD)
-        joined_ref[own, columns] = jnp.dot(
+        joined = jnp.dot(
             normed_ref[...], heads_ref[:, columns], preferred_element_type=jnp.float32
-        ).astype(jnp.bfloat16)
+        )
+        joined_ref[own, columns] = joined[:rows].astype(jnp.bfloat16)
     for begin in (0, HD):
         columns = slice(begin, begin + 128)
         turning = joined_ref[own, columns].astype(jnp.float32)
@@ -313,14 +314,15 @@
 
 
 def hide(normed_ref, upward_ref, hidden_ref, place, chunk=256):
-    rows = slice(place, place + normed_ref.shape[0])
+    count = min(normed_ref.shape[0], hidden_ref.shape[0] - place)
+    rows = slice(place, place + count)
     for first in range(0, upward_ref.shape[1], chunk):
         columns = slice(first, first + chunk)
         upward = jnp.dot(
             normed_ref[...], upward_ref[:, columns], preferred_element_type=jnp.float32
         )
         hidden = 0.5 * upward * (1.0 + lax.erf(upward * (0.5**0.5)))
-        hidden_ref[rows, columns] = hidden.astype(jnp.bfloat16)
+        hidden_ref[rows, columns] = hidden[:count].astype(jnp.bfloat16)
 
 
 def attend(joined_ref, offsets_ref, first, rows, block_rows):
@@ -481,6 +483,8 @@
     copies = copies_in(sources, targets, sems)
     block_rows = blocks[0].shape[0]
     normalize(blocks, [gain_a, gain_f], [attention_scr, feedforward_scr])
+    for normed_scr in (attention_scr, feedforward_scr):
+        normed_scr[count * block_rows :, :] = jnp.zeros((block_rows, normed_scr.shape[1]), jnp.bfloat16)
     places = [position_of(kind, half, block_rows) for kind, half in origins]
     project(attention_scr, heads_ref, table_refs, places, joined_ref, 0)
     hide(feedforward_scr, upward_ref, hidden_ref, 0)
@@ -502,8 +506,8 @@
         + [pl.BlockSpec(memory_space=pltpu.HBM)] * len(staged),
         out_specs=vmem_specs(2 + len(staged)),
         scratch_shapes=[
-            pltpu.VMEM((rows, width), jnp.bfloat16),
-            pltpu.VMEM((rows, width), jnp.bfloat16),
+            pltpu.VMEM((rows + block_rows, width), jnp.bfloat16),
+            pltpu.VMEM((rows + block_rows, width), jnp.bfloat16),
             pltpu.SemaphoreType.DMA((max(len(staged), 1), 4)),
         ],
         compiler_params=parameters(12),

time: 37.6 us -> 37.5 us (level)
  transfers between devices with their start and end apart: 16 -> 16, of which waited for: 5 -> 5; matrix products, arithmetic and copies ran while one was open for 0% -> 0% of each run, Pallas kernels for 28% -> 27%
where the time goes in v22:
time: 37.5 us; the launch traced here: 37.3 us
  starting transfers between devices  18.4 us (49%)
  Pallas kernels  13.2 us (35%)
  waiting for transfers between devices  4.94 us (13%)
  between operations  0.72 us (2%)
    ppermute x16, starting transfers between devices, exchanged(): lax.ppermute(block, axis, [(member, member ^ mask) for member in range(co...  18.4 us
    pallas_call x1, Pallas kernels, own_rows(): pl.pallas_call(functools.partial(own_kernel, count, replica_count), out_s...  5.27 us
    ppermute x16, waiting for transfers between devices, exchanged(): lax.ppermute(block, axis, [(member, member ^ mask) for member in range(co...  4.94 us
    pallas_call x1, Pallas kernels, last_rows(): pl.pallas_call(last_kernel, out_shape=[pltpu.VMEM((tokens, 3 * HD), jnp.b...  2.25 us
    pallas_call x1, Pallas kernels, middle_rows(): pl.pallas_call(functools.partial(middle_kernel, origins), out_shape=[pltp...  2.06 us
    pallas_call x1, Pallas kernels, fed_rows(): pl.pallas_call(fed_kernel, out_shape=[pltpu.VMEM((rows, width), jnp.float...  0.83 us
    pallas_call x1, Pallas kernels, rest_rows(): pl.pallas_call(rest_kernel, out_shape=shapes, in_specs=vmem_specs(5), out...  0.83 us
    pallas_call x1, Pallas kernels, finished(): pl.pallas_call(functools.partial(finish_kernel, masks), out_shape=[jax.Sh...  0.83 us
  transfers between devices with their start and end apart: 16, of which 5 were waited for; matrix products, arithmetic and copies ran while one was open for 0% of the time, Pallas kernels for 27%

profile of v22, /device:TPU:0, one launch (start us, length us, event | category | flops | bytes accessed | tf_op | source)
XLA Modules:
  0.0 37.3 jit_solution(11481698734024223481)
XLA Ops:
  0.6 5.1 %collective-permute-start = (bf16[32,2048]{1,0:T(8,128)(2,1)}, bf16[32,2048]{1,0:T(8,128)(2,1)S(1)}, u32[]{:S(2)}, u32[]{:S(2)}) collective-permute-start(bf16[32,2048]{1,0:T(8,128)(2,1)} %refs_2_.1), channel_id=1, source_target_pairs={{0,6},{1,7},{2,4},{3,5},{4,2},{5,3},{6,0},{7,1},{8,14},{9,15},{10,... | collective-permute-start | bytes 393224 | tf_op jit(solution)/shard_map/ppermute | solution.py:235
  5.8 5.3 %own_rows.1 = (s32[1,256]{1,0:T(1,128)}, s32[1,16]{1,0:T(1,128)}, bf16[32,2048]{1,0:T(8,128)(2,1)S(1)}, f32[1,2048]{1,0:T(1,128)S(1)}, f32[1,2048]{1,0:T(1,128)S...) custom-call(s32[1,256]{1,0:T(1,128)} %refs_0_.1, ...), custom_call_target="tpu_custom_call" | custom-call | flops 234881024 | bytes 11682880 | tf_op jit(solution)/shard_map/own_rows/pallas_call | solution.py:456
  11.0 2.1 %collective-permute-start.1 = (bf16[32,2048]{1,0:T(8,128)(2,1)S(1)}, bf16[32,2048]{1,0:T(8,128)(2,1)S(1)}, u32[]{:S(2)}, u32[]{:S(2)}) collective-permute-start(bf16[32,2048]{1,0:T(8,128)(2,1)S(1)} %collective-permute-done.refs_1_), channel_id=1, source_target_pairs={{0,2},{1,3},{2,0},{3,1},{4,6},{5,7},{6,4},{7,5},{8,10},{9,11},{10,... | collective-permute-start | bytes 393224 | tf_op jit(solution)/shard_map/ppermute | solution.py:235
  13.1 0.0 collective-permute-done.3.refs_0_
  13.1 0.0 collective-permute-done.2.refs_2_
  13.1 2.1 %middle_rows.1 = (bf16[96,768]{1,0:T(8,128)(2,1)S(1)}, bf16[96,1024]{1,0:T(8,128)(2,1)S(1)}, bf16[256,2048]{1,0:T(8,128)(2,1)S(1)}) custom-call(bf16[32,2048]{1,0:T(8,128)(2,1)S(1)} %collective-permute-done.3.refs_0_, bf16[32,2048]{1,0:T(8,128)(2,1)S(1)} %collective-permute-done.refs_1_, bf16[32,2048]{1,0:T(8,128)(2,1)S(1)} %collective-permute-done.2.refs_2_, ...), custom_call_target="tpu_custom_call" | custom-call | flops 704643072 | bytes 1048576 | tf_op jit(solution)/shard_map/middle_rows/pallas_call | solution.py:498
  15.2 0.1 collective-permute-start.4
  15.3 0.5 %collective-permute-start.5 = (bf16[32,2048]{1,0:T(8,128)(2,1)S(1)}, bf16[32,2048]{1,0:T(8,128)(2,1)S(1)}, u32[]{:S(2)}, u32[]{:S(2)}) collective-permute-start(bf16[32,2048]{1,0:T(8,128)(2,1)S(1)} %collective-permute-done.refs_1_), channel_id=1, source_target_pairs={{0,1},{1,0},{2,3},{3,2},{4,5},{5,4},{6,7},{7,6},{8,9},{9,8},{10,11... | collective-permute-start | bytes 393224 | tf_op jit(solution)/shard_map/ppermute | solution.py:235
  15.8 1.2 %collective-permute-done.1.refs_2_ = bf16[32,2048]{1,0:T(8,128)(2,1)S(1)} collective-permute-done((bf16[32,2048]{1,0:T(8,128)(2,1)S(1)}, bf16[32,2048]{1,0:T(8,128)(2,1)S(1)}, u32[]{:S(2)}, u32[]{:S(2)}) %collective-permute-start.1) | collective-permute-done | bytes 131104 | tf_op jit(solution)/shard_map/ppermute | solution.py:235
  17.0 0.0 collective-permute-done.4.refs_1_
  17.0 0.1 collective-permute-start.6
  17.1 0.8 %fed_rows.1 = (f32[128,2048]{1,0:T(8,128)S(1)}, bf16[96,2048]{1,0:T(8,128)(2,1)S(1)}, bf16[96,2048]{1,0:T(8,128)(2,1)S(1)}) custom-call(bf16[32,1024]{1,0:T(8,128)(2,1)S(1)} %get-tuple-element.74.own_hidden_ref, bf16[96,1024]{1,0:T(8,128)(2,1)S(1)} %get-tuple-element.75.middle_hidden_ref, bf16[1024,2048]{1,0:T(8,128)(2,1)S(1)} %get-tuple-element.76.downward_ref.refs_7_, ...), custom_call_target="tpu_custom_call" | custom-call | flops 536870912 | bytes 1048576 | tf_op jit(solution)/shard_map/fed_rows/pallas_call | solution.py:606
  18.0 0.4 %collective-permute-done.6.refs_0_ = bf16[32,2048]{1,0:T(8,128)(2,1)S(1)} collective-permute-done((bf16[32,2048]{1,0:T(8,128)(2,1)S(1)}, bf16[32,2048]{1,0:T(8,128)(2,1)S(1)}, u32[]{:S(2)}, u32[]{:S(2)}) %collective-permute-start.6) | collective-permute-done | bytes 131104 | tf_op jit(solution)/shard_map/ppermute | solution.py:235
  18.4 2.3 %last_rows.1 = (bf16[256,768]{1,0:T(8,128)(2,1)S(1)}, f32[96,2048]{1,0:T(8,128)S(1)}, bf16[32,2048]{1,0:T(8,128)(2,1)S(1)}, f32[32,2048]{1,0:T(8,128)S(1)}) custom-call(bf16[32,2048]{1,0:T(8,128)(2,1)S(1)} %collective-permute-done.6.refs_0_, bf16[96,2048]{1,0:T(8,128)(2,1)S(1)} %get-tuple-element.79.refs_1_, bf16[96,2048]{1,0:T(8,128)(2,1)S(1)} %get-tuple-element.80.refs_2_, ...), custom_call_target="tpu_custom_call" | custom-call | flops 1610612736 | bytes 1048576 | tf_op jit(solution)/shard_map/last_rows/pallas_call | solution.py:565
  20.6 0.2 collective-permute-start.7
  20.8 0.8 %rest_rows.1 = (bf16[2,32,2048]{2,1,0:T(8,128)(2,1)S(1)}, bf16[32,2048]{1,0:T(8,128)(2,1)S(1)}, f32[32,2048]{1,0:T(8,128)S(1)}, f32[32,2048]{1,0:T(8,128)S(1)}, f32[32,2048]{1,0:T(8,128)S(1)}) custom-call(bf16[256,768]{1,0:T(8,128)(2,1)S(1)} %get-tuple-element.92.joined_ref, f32[256,128]{1,0:T(8,128)S(1)} %get-tuple-element.82.refs_9_.offsets_ref, ...), custom_call_target="tpu_custom_call" | custom-call | flops 201326592 | bytes 1048576 | tf_op jit(solution)/shard_map/rest_rows/pallas_call | solution.py:658
  21.7 0.4 %collective-permute-start.9 = (bf16[2,32,2048]{2,1,0:T(8,128)(2,1)S(1)}, bf16[2,32,2048]{2,1,0:T(8,128)(2,1)S(1)}, u32[]{:S(2)}, u32[]{:S(2)}) collective-permute-start(bf16[2,32,2048]{2,1,0:T(8,128)(2,1)S(1)} %get-tuple-element.100), channel_id=1, source_target_pairs={{0,1},{1,0},{2,3},{3,2},{4,5},{5,4},{6,7},{7,6},{8,9},{9,8},{10,11... | collective-permute-start | bytes 786440 | tf_op jit(solution)/shard_map/ppermute | solution.py:235
  22.1 1.8 %collective-permute-start.11 = (bf16[32,2048]{1,0:T(8,128)(2,1)S(1)}, bf16[32,2048]{1,0:T(8,128)(2,1)S(1)}, u32[]{:S(2)}, u32[]{:S(2)}) collective-permute-start(bf16[32,2048]{1,0:T(8,128)(2,1)S(1)} %third_added.1), channel_id=1, source_target_pairs={{0,2},{1,3},{2,0},{3,1},{4,6},{5,7},{6,4},{7,5},{8,10},{9,11},{10,... | collective-permute-start | bytes 393224 | tf_op jit(solution)/shard_map/ppermute | solution.py:235
  24.0 0.3 cached_pages.1
  24.3 0.1 collective-permute-start.12
  24.3 2.5 %collective-permute-start.8 = (bf16[8,16,512]{2,1,0:T(8,128)(2,1)S(1)}, bf16[8,16,512]{2,1,0:T(8,128)(2,1)S(1)}, u32[]{:S(2)}, u32[]{:S(2)}) collective-permute-start(bf16[8,16,512]{2,1,0:T(8,128)(2,1)S(1)} %get-tuple-element.99), channel_id=1, source_target_pairs={{0,24},{8,16},{16,8},{24,0},{1,25},{9,17},{17,9},{25,1},{2,26},{10... | collective-permute-start | bytes 393224 | tf_op jit(solution)/shard_map/ppermute | solution.py:235
  26.9 0.0 collective-permute-done.9.received_ref
  26.9 0.1 near_sums.1
  26.9 0.3 collective-permute-start.10
  27.3 0.5 %collective-permute-done.11.refs_1_ = bf16[32,2048]{1,0:T(8,128)(2,1)S(1)} collective-permute-done((bf16[32,2048]{1,0:T(8,128)(2,1)S(1)}, bf16[32,2048]{1,0:T(8,128)(2,1)S(1)}, u32[]{:S(2)}, u32[]{:S(2)}) %collective-permute-start.11) | collective-permute-done | bytes 131104 | tf_op jit(solution)/shard_map/ppermute | solution.py:235
  27.8 1.6 %collective-permute-start.13 = (bf16[32,2048]{1,0:T(8,128)(2,1)S(1)}, bf16[32,2048]{1,0:T(8,128)(2,1)S(1)}, u32[]{:S(2)}, u32[]{:S(2)}) collective-permute-start(bf16[32,2048]{1,0:T(8,128)(2,1)S(1)} %second_added.1), channel_id=1, source_target_pairs={{0,4},{1,5},{2,6},{3,7},{4,0},{5,1},{6,2},{7,3},{8,12},{9,13},{10,... | collective-permute-start | bytes 393224 | tf_op jit(solution)/shard_map/ppermute | solution.py:235
  29.4 1.5 %collective-permute-start.14 = (bf16[8,16,512]{2,1,0:T(8,128)(2,1)S(1)}, bf16[8,16,512]{2,1,0:T(8,128)(2,1)S(1)}, u32[]{:S(2)}, u32[]{:S(2)}) collective-permute-start(bf16[8,16,512]{2,1,0:T(8,128)(2,1)S(1)} %get-tuple-element.113), channel_id=1, source_target_pairs={{0,16},{8,24},{16,0},{24,8},{1,17},{9,25},{17,1},{25,9},{2,18},{10... | collective-permute-start | bytes 393224 | tf_op jit(solution)/shard_map/ppermute | solution.py:235
  30.9 2.0 %collective-permute-start.15 = (bf16[8,16,512]{2,1,0:T(8,128)(2,1)S(1)}, bf16[8,16,512]{2,1,0:T(8,128)(2,1)S(1)}, u32[]{:S(2)}, u32[]{:S(2)}) collective-permute-start(bf16[8,16,512]{2,1,0:T(8,128)(2,1)S(1)} %get-tuple-element.114), channel_id=1, source_target_pairs={{0,8},{8,0},{16,24},{24,16},{1,9},{9,1},{17,25},{25,17},{2,10},{10... | collective-permute-start | bytes 393224 | tf_op jit(solution)/shard_map/ppermute | solution.py:235
  33.0 1.8 %collective-permute-done.10.refs_2_ = bf16[32,2048]{1,0:T(8,128)(2,1)S(1)} collective-permute-done((bf16[32,2048]{1,0:T(8,128)(2,1)S(1)}, bf16[32,2048]{1,0:T(8,128)(2,1)S(1)}, u32[]{:S(2)}, u32[]{:S(2)}) %collective-permute-start.10) | collective-permute-done | bytes 131104 | tf_op jit(solution)/shard_map/ppermute | solution.py:235
  34.7 0.7 %placed.1 = (bf16[1,4,8,16,512]{4,3,2,1,0:T(8,128)(2,1)}, f32[32,2048]{1,0:T(8,128)S(1)}) custom-call(bf16[8,16,512]{2,1,0:T(8,128)(2,1)S(1)} %get-tuple-element.98.refs_0_, bf16[8,16,512]{2,1,0:T(8,128)(2,1)S(1)} %collective-permute-done.8.refs_1_, bf16[32,2048]{1,0:T(8,128)(2,1)S(1)} %collective-permute-done.10.refs_2_, ...), custom_call_target="tpu_custom_call" | custom-call | tf_op jit(solution)/shard_map/placed/pallas_call | solution.py:753
  35.4 1.0 %collective-permute-done.13.refs_0_ = bf16[32,2048]{1,0:T(8,128)(2,1)S(1)} collective-permute-done((bf16[32,2048]{1,0:T(8,128)(2,1)S(1)}, bf16[32,2048]{1,0:T(8,128)(2,1)S(1)}, u32[]{:S(2)}, u32[]{:S(2)}) %collective-permute-start.13) | collective-permute-done | bytes 131104 | tf_op jit(solution)/shard_map/ppermute | solution.py:235
  36.5 0.8 %finished.1 = (f32[32,2048]{1,0:T(8,128)}, bf16[1,4,8,16,512]{4,3,2,1,0:T(8,128)(2,1)}) custom-call(f32[32,2048]{1,0:T(8,128)S(1)} %get-tuple-element.106.base_ref, bf16[32,2048]{1,0:T(8,128)(2,1)S(1)} %collective-permute-done.13.refs_0_, bf16[8,16,512]{2,1,0:T(8,128)(2,1)S(1)} %collective-permute-done.14.refs_1_, ...), custom_call_target="tpu_custom_call", output_to_operand_aliasing={{1}: (4, {})} | custom-call | tf_op jit(solution)/shard_map/finished/pallas_call | solution.py:790
  (11 shorter events, 0.1 us)
Async XLA Ops:
  0.6 10.4 %collective-permute-start = (bf16[32,2048]{1,0:T(8,128)(2,1)}, bf16[32,2048]{1,0:T(8,128)(2,1)S(1)}, u32[]{:S(2)}, u32[]{:S(2)}) collective-permute-start(bf16[32,2048]{1,0:T(8,128)(2,1)} %refs_2_.1), channel_id=1, source_target_pairs={{0,6},{1,7},{2,4},{3,5},{4,2},{5,3},{6,0},{7,1},{8,14},{9,15},{10,... | collective-permute-start | bytes 393224 | tf_op jit(solution)/shard_map/ppermute | solution.py:235
  5.7 7.4 %collective-permute-start.3 = (bf16[32,2048]{1,0:T(8,128)(2,1)}, bf16[32,2048]{1,0:T(8,128)(2,1)S(1)}, u32[]{:S(2)}, u32[]{:S(2)}) collective-permute-start(bf16[32,2048]{1,0:T(8,128)(2,1)} %refs_2_.1), channel_id=1, source_target_pairs={{0,1},{1,0},{2,3},{3,2},{4,5},{5,4},{6,7},{7,6},{8,9},{9,8},{10,11... | collective-permute-start | bytes 393224 | tf_op jit(solution)/shard_map/ppermute | solution.py:235
  5.8 7.4 %collective-permute-start.2 = (bf16[32,2048]{1,0:T(8,128)(2,1)}, bf16[32,2048]{1,0:T(8,128)(2,1)S(1)}, u32[]{:S(2)}, u32[]{:S(2)}) collective-permute-start(bf16[32,2048]{1,0:T(8,128)(2,1)} %refs_2_.1), channel_id=1, source_target_pairs={{0,2},{1,3},{2,0},{3,1},{4,6},{5,7},{6,4},{7,5},{8,10},{9,11},{10,... | collective-permute-start | bytes 393224 | tf_op jit(solution)/shard_map/ppermute | solution.py:235
  11.0 6.0 %collective-permute-start.1 = (bf16[32,2048]{1,0:T(8,128)(2,1)S(1)}, bf16[32,2048]{1,0:T(8,128)(2,1)S(1)}, u32[]{:S(2)}, u32[]{:S(2)}) collective-permute-start(bf16[32,2048]{1,0:T(8,128)(2,1)S(1)} %collective-permute-done.refs_1_), channel_id=1, source_target_pairs={{0,2},{1,3},{2,0},{3,1},{4,6},{5,7},{6,4},{7,5},{8,10},{9,11},{10,... | collective-permute-start | bytes 393224 | tf_op jit(solution)/shard_map/ppermute | solution.py:235
  15.2 1.8 %collective-permute-start.4 = (bf16[32,2048]{1,0:T(8,128)(2,1)S(1)}, bf16[32,2048]{1,0:T(8,128)(2,1)S(1)}, u32[]{:S(2)}, u32[]{:S(2)}) collective-permute-start(bf16[32,2048]{1,0:T(8,128)(2,1)S(1)} %collective-permute-done.2.refs_2_), channel_id=1, source_target_pairs={{0,1},{1,0},{2,3},{3,2},{4,5},{5,4},{6,7},{7,6},{8,9},{9,8},{10,11... | collective-permute-start | bytes 393224 | tf_op jit(solution)/shard_map/ppermute | solution.py:235
  15.3 1.7 %collective-permute-start.5 = (bf16[32,2048]{1,0:T(8,128)(2,1)S(1)}, bf16[32,2048]{1,0:T(8,128)(2,1)S(1)}, u32[]{:S(2)}, u32[]{:S(2)}) collective-permute-start(bf16[32,2048]{1,0:T(8,128)(2,1)S(1)} %collective-permute-done.refs_1_), channel_id=1, source_target_pairs={{0,1},{1,0},{2,3},{3,2},{4,5},{5,4},{6,7},{7,6},{8,9},{9,8},{10,11... | collective-permute-start | bytes 393224 | tf_op jit(solution)/shard_map/ppermute | solution.py:235
  17.0 1.4 %collective-permute-start.6 = (bf16[32,2048]{1,0:T(8,128)(2,1)S(1)}, bf16[32,2048]{1,0:T(8,128)(2,1)S(1)}, u32[]{:S(2)}, u32[]{:S(2)}) collective-permute-start(bf16[32,2048]{1,0:T(8,128)(2,1)S(1)} %collective-permute-done.1.refs_2_), channel_id=1, source_target_pairs={{0,1},{1,0},{2,3},{3,2},{4,5},{5,4},{6,7},{7,6},{8,9},{9,8},{10,11... | collective-permute-start | bytes 393224 | tf_op jit(solution)/shard_map/ppermute | solution.py:235
  20.6 1.5 %collective-permute-start.7 = (bf16[32,2048]{1,0:T(8,128)(2,1)S(1)}, bf16[32,2048]{1,0:T(8,128)(2,1)S(1)}, u32[]{:S(2)}, u32[]{:S(2)}) collective-permute-start(bf16[32,2048]{1,0:T(8,128)(2,1)S(1)} %get-tuple-element.87), channel_id=1, source_target_pairs={{0,1},{1,0},{2,3},{3,2},{4,5},{5,4},{6,7},{7,6},{8,9},{9,8},{10,11... | collective-permute-start | bytes 393224 | tf_op jit(solution)/shard_map/ppermute | solution.py:235
  21.7 5.2 %collective-permute-start.9 = (bf16[2,32,2048]{2,1,0:T(8,128)(2,1)S(1)}, bf16[2,32,2048]{2,1,0:T(8,128)(2,1)S(1)}, u32[]{:S(2)}, u32[]{:S(2)}) collective-permute-start(bf16[2,32,2048]{2,1,0:T(8,128)(2,1)S(1)} %get-tuple-element.100), channel_id=1, source_target_pairs={{0,1},{1,0},{2,3},{3,2},{4,5},{5,4},{6,7},{7,6},{8,9},{9,8},{10,11... | collective-permute-start | bytes 786440 | tf_op jit(solution)/shard_map/ppermute | solution.py:235
  22.1 5.6 %collective-permute-start.11 = (bf16[32,2048]{1,0:T(8,128)(2,1)S(1)}, bf16[32,2048]{1,0:T(8,128)(2,1)S(1)}, u32[]{:S(2)}, u32[]{:S(2)}) collective-permute-start(bf16[32,2048]{1,0:T(8,128)(2,1)S(1)} %third_added.1), channel_id=1, source_target_pairs={{0,2},{1,3},{2,0},{3,1},{4,6},{5,7},{6,4},{7,5},{8,10},{9,11},{10,... | collective-permute-start | bytes 393224 | tf_op jit(solution)/shard_map/ppermute | solution.py:235
  24.3 3.5 %collective-permute-start.12 = (bf16[32,2048]{1,0:T(8,128)(2,1)S(1)}, bf16[32,2048]{1,0:T(8,128)(2,1)S(1)}, u32[]{:S(2)}, u32[]{:S(2)}) collective-permute-start(bf16[32,2048]{1,0:T(8,128)(2,1)S(1)} %get-tuple-element.109), channel_id=1, source_target_pairs={{0,1},{1,0},{2,3},{3,2},{4,5},{5,4},{6,7},{7,6},{8,9},{9,8},{10,11... | collective-permute-start | bytes 393224 | tf_op jit(solution)/shard_map/ppermute | solution.py:235
  24.3 8.6 %collective-permute-start.8 = (bf16[8,16,512]{2,1,0:T(8,128)(2,1)S(1)}, bf16[8,16,512]{2,1,0:T(8,128)(2,1)S(1)}, u32[]{:S(2)}, u32[]{:S(2)}) collective-permute-start(bf16[8,16,512]{2,1,0:T(8,128)(2,1)S(1)} %get-tuple-element.99), channel_id=1, source_target_pairs={{0,24},{8,16},{16,8},{24,0},{1,25},{9,17},{17,9},{25,1},{2,26},{10... | collective-permute-start | bytes 393224 | tf_op jit(solution)/shard_map/ppermute | solution.py:235
  26.9 7.8 %collective-permute-start.10 = (bf16[32,2048]{1,0:T(8,128)(2,1)S(1)}, bf16[32,2048]{1,0:T(8,128)(2,1)S(1)}, u32[]{:S(2)}, u32[]{:S(2)}) collective-permute-start(bf16[32,2048]{1,0:T(8,128)(2,1)S(1)} %get-tuple-element.104), channel_id=1, source_target_pairs={{0,2},{1,3},{2,0},{3,1},{4,6},{5,7},{6,4},{7,5},{8,10},{9,11},{10,... | collective-permute-start | bytes 393224 | tf_op jit(solution)/shard_map/ppermute | solution.py:235
  27.8 8.7 %collective-permute-start.13 = (bf16[32,2048]{1,0:T(8,128)(2,1)S(1)}, bf16[32,2048]{1,0:T(8,128)(2,1)S(1)}, u32[]{:S(2)}, u32[]{:S(2)}) collective-permute-start(bf16[32,2048]{1,0:T(8,128)(2,1)S(1)} %second_added.1), channel_id=1, source_target_pairs={{0,4},{1,5},{2,6},{3,7},{4,0},{5,1},{6,2},{7,3},{8,12},{9,13},{10,... | collective-permute-start | bytes 393224 | tf_op jit(solution)/shard_map/ppermute | solution.py:235
  29.4 7.1 %collective-permute-start.14 = (bf16[8,16,512]{2,1,0:T(8,128)(2,1)S(1)}, bf16[8,16,512]{2,1,0:T(8,128)(2,1)S(1)}, u32[]{:S(2)}, u32[]{:S(2)}) collective-permute-start(bf16[8,16,512]{2,1,0:T(8,128)(2,1)S(1)} %get-tuple-element.113), channel_id=1, source_target_pairs={{0,16},{8,24},{16,0},{24,8},{1,17},{9,25},{17,1},{25,9},{2,18},{10... | collective-permute-start | bytes 393224 | tf_op jit(solution)/shard_map/ppermute | solution.py:235
  30.9 5.6 %collective-permute-start.15 = (bf16[8,16,512]{2,1,0:T(8,128)(2,1)S(1)}, bf16[8,16,512]{2,1,0:T(8,128)(2,1)S(1)}, u32[]{:S(2)}, u32[]{:S(2)}) collective-permute-start(bf16[8,16,512]{2,1,0:T(8,128)(2,1)S(1)} %get-tuple-element.114), channel_id=1, source_target_pairs={{0,8},{8,0},{16,24},{24,16},{1,9},{9,1},{17,25},{25,17},{2,10},{10... | collective-permute-start | bytes 393224 | tf_op jit(solution)/shard_map/ppermute | solution.py:235

commit v23 on v22

--- a/solution.py
+++ b/solution.py
@@ -546,7 +546,7 @@
     rows = CORES * block_rows
     hide(feedforward_scr, upward_ref, hidden_scr, 0)
     attended = attend(joined_ref, offsets_ref, early - block_rows, rows, block_rows)
-    chunk = 512
+    chunk = 256
     for begin in range(0, downward_ref.shape[1], chunk):
         columns = slice(begin, begin + chunk)
         fed = jnp.dot(hidden_scr[...], downward_ref[:, columns], preferred_element_type=jnp.float32)
@@ -591,7 +591,7 @@
     blocks, gain_refs, (fed_ref, *normed_refs) = refs[:-5], refs[-5:-3], refs[-3:]
     normalize(blocks, gain_refs, normed_refs)
     hidden = jnp.concatenate([own_hidden_ref[...], middle_hidden_ref[...]], 0)
-    chunk = 512
+    chunk = 256
     for begin in range(0, downward_ref.shape[1], chunk):
         columns = slice(begin, begin + chunk)
         fed_ref[:, columns] = jnp.dot(

time: 37.5 us -> 37.4 us (level)
  no operation moved by 1% of the time
where the time goes in v23:
time: 37.4 us; the launch traced here: 37.3 us
  starting transfers between devices  18.4 us (49%)
  Pallas kernels  13.2 us (35%)
  waiting for transfers between devices  4.94 us (13%)
  between operations  0.72 us (2%)
    ppermute x16, starting transfers between devices, exchanged(): lax.ppermute(block, axis, [(member, member ^ mask) for member in range(co...  18.4 us
    pallas_call x1, Pallas kernels, own_rows(): pl.pallas_call(functools.partial(own_kernel, count, replica_count), out_s...  5.27 us
    ppermute x16, waiting for transfers between devices, exchanged(): lax.ppermute(block, axis, [(member, member ^ mask) for member in range(co...  4.94 us
    pallas_call x1, Pallas kernels, last_rows(): pl.pallas_call(last_kernel, out_shape=[pltpu.VMEM((tokens, 3 * HD), jnp.b...  2.24 us
    pallas_call x1, Pallas kernels, middle_rows(): pl.pallas_call(functools.partial(middle_kernel, origins), out_shape=[pltp...  2.06 us
    pallas_call x1, Pallas kernels, fed_rows(): pl.pallas_call(fed_kernel, out_shape=[pltpu.VMEM((rows, width), jnp.float...  0.83 us
    pallas_call x1, Pallas kernels, rest_rows(): pl.pallas_call(rest_kernel, out_shape=shapes, in_specs=vmem_specs(5), out...  0.83 us
    pallas_call x1, Pallas kernels, finished(): pl.pallas_call(functools.partial(finish_kernel, masks), out_shape=[jax.Sh...  0.83 us
  transfers between devices with their start and end apart: 16, of which 5 were waited for; matrix products, arithmetic and copies ran while one was open for 0% of the time, Pallas kernels for 27%

profile of v23, /device:TPU:0, one launch (start us, length us, event | category | flops | bytes accessed | tf_op | source)
XLA Modules:
  0.0 37.3 jit_solution(13611879397841345663)
XLA Ops:
  0.6 5.1 %collective-permute-start = (bf16[32,2048]{1,0:T(8,128)(2,1)}, bf16[32,2048]{1,0:T(8,128)(2,1)S(1)}, u32[]{:S(2)}, u32[]{:S(2)}) collective-permute-start(bf16[32,2048]{1,0:T(8,128)(2,1)} %refs_2_.1), channel_id=1, source_target_pairs={{0,6},{1,7},{2,4},{3,5},{4,2},{5,3},{6,0},{7,1},{8,14},{9,15},{10,... | collective-permute-start | bytes 393224 | tf_op jit(solution)/shard_map/ppermute | solution.py:235
  5.7 0.0 collective-permute-start.3
  5.8 5.3 %own_rows.1 = (s32[1,256]{1,0:T(1,128)}, s32[1,16]{1,0:T(1,128)}, bf16[32,2048]{1,0:T(8,128)(2,1)S(1)}, f32[1,2048]{1,0:T(1,128)S(1)}, f32[1,2048]{1,0:T(1,128)S...) custom-call(s32[1,256]{1,0:T(1,128)} %refs_0_.1, ...), custom_call_target="tpu_custom_call" | custom-call | flops 234881024 | bytes 11682880 | tf_op jit(solution)/shard_map/own_rows/pallas_call | solution.py:456
  11.0 0.0 collective-permute-done.refs_1_
  11.0 2.1 %collective-permute-start.1 = (bf16[32,2048]{1,0:T(8,128)(2,1)S(1)}, bf16[32,2048]{1,0:T(8,128)(2,1)S(1)}, u32[]{:S(2)}, u32[]{:S(2)}) collective-permute-start(bf16[32,2048]{1,0:T(8,128)(2,1)S(1)} %collective-permute-done.refs_1_), channel_id=1, source_target_pairs={{0,2},{1,3},{2,0},{3,1},{4,6},{5,7},{6,4},{7,5},{8,10},{9,11},{10,... | collective-permute-start | bytes 393224 | tf_op jit(solution)/shard_map/ppermute | solution.py:235
  13.1 0.0 collective-permute-done.2.refs_2_
  13.1 2.1 %middle_rows.1 = (bf16[96,768]{1,0:T(8,128)(2,1)S(1)}, bf16[96,1024]{1,0:T(8,128)(2,1)S(1)}, bf16[256,2048]{1,0:T(8,128)(2,1)S(1)}) custom-call(bf16[32,2048]{1,0:T(8,128)(2,1)S(1)} %collective-permute-done.3.refs_0_, bf16[32,2048]{1,0:T(8,128)(2,1)S(1)} %collective-permute-done.refs_1_, bf16[32,2048]{1,0:T(8,128)(2,1)S(1)} %collective-permute-done.2.refs_2_, ...), custom_call_target="tpu_custom_call" | custom-call | flops 704643072 | bytes 1048576 | tf_op jit(solution)/shard_map/middle_rows/pallas_call | solution.py:498
  15.2 0.1 collective-permute-start.4
  15.3 0.5 %collective-permute-start.5 = (bf16[32,2048]{1,0:T(8,128)(2,1)S(1)}, bf16[32,2048]{1,0:T(8,128)(2,1)S(1)}, u32[]{:S(2)}, u32[]{:S(2)}) collective-permute-start(bf16[32,2048]{1,0:T(8,128)(2,1)S(1)} %collective-permute-done.refs_1_), channel_id=1, source_target_pairs={{0,1},{1,0},{2,3},{3,2},{4,5},{5,4},{6,7},{7,6},{8,9},{9,8},{10,11... | collective-permute-start | bytes 393224 | tf_op jit(solution)/shard_map/ppermute | solution.py:235
  15.8 1.2 %collective-permute-done.1.refs_2_ = bf16[32,2048]{1,0:T(8,128)(2,1)S(1)} collective-permute-done((bf16[32,2048]{1,0:T(8,128)(2,1)S(1)}, bf16[32,2048]{1,0:T(8,128)(2,1)S(1)}, u32[]{:S(2)}, u32[]{:S(2)}) %collective-permute-start.1) | collective-permute-done | bytes 131104 | tf_op jit(solution)/shard_map/ppermute | solution.py:235
  17.0 0.0 collective-permute-done.4.refs_1_
  17.0 0.1 collective-permute-start.6
  17.1 0.8 %fed_rows.1 = (f32[128,2048]{1,0:T(8,128)S(1)}, bf16[96,2048]{1,0:T(8,128)(2,1)S(1)}, bf16[96,2048]{1,0:T(8,128)(2,1)S(1)}) custom-call(bf16[32,1024]{1,0:T(8,128)(2,1)S(1)} %get-tuple-element.74.own_hidden_ref, bf16[96,1024]{1,0:T(8,128)(2,1)S(1)} %get-tuple-element.75.middle_hidden_ref, bf16[1024,2048]{1,0:T(8,128)(2,1)S(1)} %get-tuple-element.76.downward_ref.refs_7_, ...), custom_call_target="tpu_custom_call" | custom-call | flops 536870912 | bytes 1048576 | tf_op jit(solution)/shard_map/fed_rows/pallas_call | solution.py:606
  18.0 0.4 %collective-permute-done.6.refs_0_ = bf16[32,2048]{1,0:T(8,128)(2,1)S(1)} collective-permute-done((bf16[32,2048]{1,0:T(8,128)(2,1)S(1)}, bf16[32,2048]{1,0:T(8,128)(2,1)S(1)}, u32[]{:S(2)}, u32[]{:S(2)}) %collective-permute-start.6) | collective-permute-done | bytes 131104 | tf_op jit(solution)/shard_map/ppermute | solution.py:235
  18.4 2.2 %last_rows.1 = (bf16[256,768]{1,0:T(8,128)(2,1)S(1)}, f32[96,2048]{1,0:T(8,128)S(1)}, bf16[32,2048]{1,0:T(8,128)(2,1)S(1)}, f32[32,2048]{1,0:T(8,128)S(1)}) custom-call(bf16[32,2048]{1,0:T(8,128)(2,1)S(1)} %collective-permute-done.6.refs_0_, bf16[96,2048]{1,0:T(8,128)(2,1)S(1)} %get-tuple-element.79.refs_1_, bf16[96,2048]{1,0:T(8,128)(2,1)S(1)} %get-tuple-element.80.refs_2_, ...), custom_call_target="tpu_custom_call" | custom-call | flops 1610612736 | bytes 1048576 | tf_op jit(solution)/shard_map/last_rows/pallas_call | solution.py:565
  20.6 0.2 collective-permute-start.7
  20.8 0.8 %rest_rows.1 = (bf16[2,32,2048]{2,1,0:T(8,128)(2,1)S(1)}, bf16[32,2048]{1,0:T(8,128)(2,1)S(1)}, f32[32,2048]{1,0:T(8,128)S(1)}, f32[32,2048]{1,0:T(8,128)S(1)}, f32[32,2048]{1,0:T(8,128)S(1)}) custom-call(bf16[256,768]{1,0:T(8,128)(2,1)S(1)} %get-tuple-element.92.joined_ref, f32[256,128]{1,0:T(8,128)S(1)} %get-tuple-element.82.refs_9_.offsets_ref, ...), custom_call_target="tpu_custom_call" | custom-call | flops 201326592 | bytes 1048576 | tf_op jit(solution)/shard_map/rest_rows/pallas_call | solution.py:658
  21.7 0.4 %collective-permute-start.9 = (bf16[2,32,2048]{2,1,0:T(8,128)(2,1)S(1)}, bf16[2,32,2048]{2,1,0:T(8,128)(2,1)S(1)}, u32[]{:S(2)}, u32[]{:S(2)}) collective-permute-start(bf16[2,32,2048]{2,1,0:T(8,128)(2,1)S(1)} %get-tuple-element.100), channel_id=1, source_target_pairs={{0,1},{1,0},{2,3},{3,2},{4,5},{5,4},{6,7},{7,6},{8,9},{9,8},{10,11... | collective-permute-start | bytes 786440 | tf_op jit(solution)/shard_map/ppermute | solution.py:235
  22.1 1.8 %collective-permute-start.11 = (bf16[32,2048]{1,0:T(8,128)(2,1)S(1)}, bf16[32,2048]{1,0:T(8,128)(2,1)S(1)}, u32[]{:S(2)}, u32[]{:S(2)}) collective-permute-start(bf16[32,2048]{1,0:T(8,128)(2,1)S(1)} %third_added.1), channel_id=1, source_target_pairs={{0,2},{1,3},{2,0},{3,1},{4,6},{5,7},{6,4},{7,5},{8,10},{9,11},{10,... | collective-permute-start | bytes 393224 | tf_op jit(solution)/shard_map/ppermute | solution.py:235
  23.9 0.3 cached_pages.1
  24.2 0.1 collective-permute-start.12
  24.3 2.5 %collective-permute-start.8 = (bf16[8,16,512]{2,1,0:T(8,128)(2,1)S(1)}, bf16[8,16,512]{2,1,0:T(8,128)(2,1)S(1)}, u32[]{:S(2)}, u32[]{:S(2)}) collective-permute-start(bf16[8,16,512]{2,1,0:T(8,128)(2,1)S(1)} %get-tuple-element.99), channel_id=1, source_target_pairs={{0,24},{8,16},{16,8},{24,0},{1,25},{9,17},{17,9},{25,1},{2,26},{10... | collective-permute-start | bytes 393224 | tf_op jit(solution)/shard_map/ppermute | solution.py:235
  26.8 0.1 near_sums.1
  26.9 0.3 collective-permute-start.10
  27.3 0.5 %collective-permute-done.11.refs_1_ = bf16[32,2048]{1,0:T(8,128)(2,1)S(1)} collective-permute-done((bf16[32,2048]{1,0:T(8,128)(2,1)S(1)}, bf16[32,2048]{1,0:T(8,128)(2,1)S(1)}, u32[]{:S(2)}, u32[]{:S(2)}) %collective-permute-start.11) | collective-permute-done | bytes 131104 | tf_op jit(solution)/shard_map/ppermute | solution.py:235
  27.8 1.6 %collective-permute-start.13 = (bf16[32,2048]{1,0:T(8,128)(2,1)S(1)}, bf16[32,2048]{1,0:T(8,128)(2,1)S(1)}, u32[]{:S(2)}, u32[]{:S(2)}) collective-permute-start(bf16[32,2048]{1,0:T(8,128)(2,1)S(1)} %second_added.1), channel_id=1, source_target_pairs={{0,4},{1,5},{2,6},{3,7},{4,0},{5,1},{6,2},{7,3},{8,12},{9,13},{10,... | collective-permute-start | bytes 393224 | tf_op jit(solution)/shard_map/ppermute | solution.py:235
  29.4 1.5 %collective-permute-start.14 = (bf16[8,16,512]{2,1,0:T(8,128)(2,1)S(1)}, bf16[8,16,512]{2,1,0:T(8,128)(2,1)S(1)}, u32[]{:S(2)}, u32[]{:S(2)}) collective-permute-start(bf16[8,16,512]{2,1,0:T(8,128)(2,1)S(1)} %get-tuple-element.113), channel_id=1, source_target_pairs={{0,16},{8,24},{16,0},{24,8},{1,17},{9,25},{17,1},{25,9},{2,18},{10... | collective-permute-start | bytes 393224 | tf_op jit(solution)/shard_map/ppermute | solution.py:235
  30.9 2.0 %collective-permute-start.15 = (bf16[8,16,512]{2,1,0:T(8,128)(2,1)S(1)}, bf16[8,16,512]{2,1,0:T(8,128)(2,1)S(1)}, u32[]{:S(2)}, u32[]{:S(2)}) collective-permute-start(bf16[8,16,512]{2,1,0:T(8,128)(2,1)S(1)} %get-tuple-element.114), channel_id=1, source_target_pairs={{0,8},{8,0},{16,24},{24,16},{1,9},{9,1},{17,25},{25,17},{2,10},{10... | collective-permute-start | bytes 393224 | tf_op jit(solution)/shard_map/ppermute | solution.py:235
  32.9 1.8 %collective-permute-done.10.refs_2_ = bf16[32,2048]{1,0:T(8,128)(2,1)S(1)} collective-permute-done((bf16[32,2048]{1,0:T(8,128)(2,1)S(1)}, bf16[32,2048]{1,0:T(8,128)(2,1)S(1)}, u32[]{:S(2)}, u32[]{:S(2)}) %collective-permute-start.10) | collective-permute-done | bytes 131104 | tf_op jit(solution)/shard_map/ppermute | solution.py:235
  34.7 0.7 %placed.1 = (bf16[1,4,8,16,512]{4,3,2,1,0:T(8,128)(2,1)}, f32[32,2048]{1,0:T(8,128)S(1)}) custom-call(bf16[8,16,512]{2,1,0:T(8,128)(2,1)S(1)} %get-tuple-element.98.refs_0_, bf16[8,16,512]{2,1,0:T(8,128)(2,1)S(1)} %collective-permute-done.8.refs_1_, bf16[32,2048]{1,0:T(8,128)(2,1)S(1)} %collective-permute-done.10.refs_2_, ...), custom_call_target="tpu_custom_call" | custom-call | tf_op jit(solution)/shard_map/placed/pallas_call | solution.py:753
  35.4 1.0 %collective-permute-done.13.refs_0_ = bf16[32,2048]{1,0:T(8,128)(2,1)S(1)} collective-permute-done((bf16[32,2048]{1,0:T(8,128)(2,1)S(1)}, bf16[32,2048]{1,0:T(8,128)(2,1)S(1)}, u32[]{:S(2)}, u32[]{:S(2)}) %collective-permute-start.13) | collective-permute-done | bytes 131104 | tf_op jit(solution)/shard_map/ppermute | solution.py:235
  36.4 0.8 %finished.1 = (f32[32,2048]{1,0:T(8,128)}, bf16[1,4,8,16,512]{4,3,2,1,0:T(8,128)(2,1)}) custom-call(f32[32,2048]{1,0:T(8,128)S(1)} %get-tuple-element.106.base_ref, bf16[32,2048]{1,0:T(8,128)(2,1)S(1)} %collective-permute-done.13.refs_0_, bf16[8,16,512]{2,1,0:T(8,128)(2,1)S(1)} %collective-permute-done.14.refs_1_, ...), custom_call_target="tpu_custom_call", output_to_operand_aliasing={{1}: (4, {})} | custom-call | tf_op jit(solution)/shard_map/finished/pallas_call | solution.py:790
  (11 shorter events, 0.1 us)
Async XLA Ops:
  0.6 10.4 %collective-permute-start = (bf16[32,2048]{1,0:T(8,128)(2,1)}, bf16[32,2048]{1,0:T(8,128)(2,1)S(1)}, u32[]{:S(2)}, u32[]{:S(2)}) collective-permute-start(bf16[32,2048]{1,0:T(8,128)(2,1)} %refs_2_.1), channel_id=1, source_target_pairs={{0,6},{1,7},{2,4},{3,5},{4,2},{5,3},{6,0},{7,1},{8,14},{9,15},{10,... | collective-permute-start | bytes 393224 | tf_op jit(solution)/shard_map/ppermute | solution.py:235
  5.7 7.4 %collective-permute-start.3 = (bf16[32,2048]{1,0:T(8,128)(2,1)}, bf16[32,2048]{1,0:T(8,128)(2,1)S(1)}, u32[]{:S(2)}, u32[]{:S(2)}) collective-permute-start(bf16[32,2048]{1,0:T(8,128)(2,1)} %refs_2_.1), channel_id=1, source_target_pairs={{0,1},{1,0},{2,3},{3,2},{4,5},{5,4},{6,7},{7,6},{8,9},{9,8},{10,11... | collective-permute-start | bytes 393224 | tf_op jit(solution)/shard_map/ppermute | solution.py:235
  5.8 7.4 %collective-permute-start.2 = (bf16[32,2048]{1,0:T(8,128)(2,1)}, bf16[32,2048]{1,0:T(8,128)(2,1)S(1)}, u32[]{:S(2)}, u32[]{:S(2)}) collective-permute-start(bf16[32,2048]{1,0:T(8,128)(2,1)} %refs_2_.1), channel_id=1, source_target_pairs={{0,2},{1,3},{2,0},{3,1},{4,6},{5,7},{6,4},{7,5},{8,10},{9,11},{10,... | collective-permute-start | bytes 393224 | tf_op jit(solution)/shard_map/ppermute | solution.py:235
  11.0 6.0 %collective-permute-start.1 = (bf16[32,2048]{1,0:T(8,128)(2,1)S(1)}, bf16[32,2048]{1,0:T(8,128)(2,1)S(1)}, u32[]{:S(2)}, u32[]{:S(2)}) collective-permute-start(bf16[32,2048]{1,0:T(8,128)(2,1)S(1)} %collective-permute-done.refs_1_), channel_id=1, source_target_pairs={{0,2},{1,3},{2,0},{3,1},{4,6},{5,7},{6,4},{7,5},{8,10},{9,11},{10,... | collective-permute-start | bytes 393224 | tf_op jit(solution)/shard_map/ppermute | solution.py:235
  15.2 1.8 %collective-permute-start.4 = (bf16[32,2048]{1,0:T(8,128)(2,1)S(1)}, bf16[32,2048]{1,0:T(8,128)(2,1)S(1)}, u32[]{:S(2)}, u32[]{:S(2)}) collective-permute-start(bf16[32,2048]{1,0:T(8,128)(2,1)S(1)} %collective-permute-done.2.refs_2_), channel_id=1, source_target_pairs={{0,1},{1,0},{2,3},{3,2},{4,5},{5,4},{6,7},{7,6},{8,9},{9,8},{10,11... | collective-permute-start | bytes 393224 | tf_op jit(solution)/shard_map/ppermute | solution.py:235
  15.3 1.7 %collective-permute-start.5 = (bf16[32,2048]{1,0:T(8,128)(2,1)S(1)}, bf16[32,2048]{1,0:T(8,128)(2,1)S(1)}, u32[]{:S(2)}, u32[]{:S(2)}) collective-permute-start(bf16[32,2048]{1,0:T(8,128)(2,1)S(1)} %collective-permute-done.refs_1_), channel_id=1, source_target_pairs={{0,1},{1,0},{2,3},{3,2},{4,5},{5,4},{6,7},{7,6},{8,9},{9,8},{10,11... | collective-permute-start | bytes 393224 | tf_op jit(solution)/shard_map/ppermute | solution.py:235
  17.0 1.4 %collective-permute-start.6 = (bf16[32,2048]{1,0:T(8,128)(2,1)S(1)}, bf16[32,2048]{1,0:T(8,128)(2,1)S(1)}, u32[]{:S(2)}, u32[]{:S(2)}) collective-permute-start(bf16[32,2048]{1,0:T(8,128)(2,1)S(1)} %collective-permute-done.1.refs_2_), channel_id=1, source_target_pairs={{0,1},{1,0},{2,3},{3,2},{4,5},{5,4},{6,7},{7,6},{8,9},{9,8},{10,11... | collective-permute-start | bytes 393224 | tf_op jit(solution)/shard_map/ppermute | solution.py:235
  20.6 1.5 %collective-permute-start.7 = (bf16[32,2048]{1,0:T(8,128)(2,1)S(1)}, bf16[32,2048]{1,0:T(8,128)(2,1)S(1)}, u32[]{:S(2)}, u32[]{:S(2)}) collective-permute-start(bf16[32,2048]{1,0:T(8,128)(2,1)S(1)} %get-tuple-element.87), channel_id=1, source_target_pairs={{0,1},{1,0},{2,3},{3,2},{4,5},{5,4},{6,7},{7,6},{8,9},{9,8},{10,11... | collective-permute-start | bytes 393224 | tf_op jit(solution)/shard_map/ppermute | solution.py:235
  21.7 5.2 %collective-permute-start.9 = (bf16[2,32,2048]{2,1,0:T(8,128)(2,1)S(1)}, bf16[2,32,2048]{2,1,0:T(8,128)(2,1)S(1)}, u32[]{:S(2)}, u32[]{:S(2)}) collective-permute-start(bf16[2,32,2048]{2,1,0:T(8,128)(2,1)S(1)} %get-tuple-element.100), channel_id=1, source_target_pairs={{0,1},{1,0},{2,3},{3,2},{4,5},{5,4},{6,7},{7,6},{8,9},{9,8},{10,11... | collective-permute-start | bytes 786440 | tf_op jit(solution)/shard_map/ppermute | solution.py:235
  22.1 5.6 %collective-permute-start.11 = (bf16[32,2048]{1,0:T(8,128)(2,1)S(1)}, bf16[32,2048]{1,0:T(8,128)(2,1)S(1)}, u32[]{:S(2)}, u32[]{:S(2)}) collective-permute-start(bf16[32,2048]{1,0:T(8,128)(2,1)S(1)} %third_added.1), channel_id=1, source_target_pairs={{0,2},{1,3},{2,0},{3,1},{4,6},{5,7},{6,4},{7,5},{8,10},{9,11},{10,... | collective-permute-start | bytes 393224 | tf_op jit(solution)/shard_map/ppermute | solution.py:235
  24.2 3.5 %collective-permute-start.12 = (bf16[32,2048]{1,0:T(8,128)(2,1)S(1)}, bf16[32,2048]{1,0:T(8,128)(2,1)S(1)}, u32[]{:S(2)}, u32[]{:S(2)}) collective-permute-start(bf16[32,2048]{1,0:T(8,128)(2,1)S(1)} %get-tuple-element.109), channel_id=1, source_target_pairs={{0,1},{1,0},{2,3},{3,2},{4,5},{5,4},{6,7},{7,6},{8,9},{9,8},{10,11... | collective-permute-start | bytes 393224 | tf_op jit(solution)/shard_map/ppermute | solution.py:235
  24.3 8.6 %collective-permute-start.8 = (bf16[8,16,512]{2,1,0:T(8,128)(2,1)S(1)}, bf16[8,16,512]{2,1,0:T(8,128)(2,1)S(1)}, u32[]{:S(2)}, u32[]{:S(2)}) collective-permute-start(bf16[8,16,512]{2,1,0:T(8,128)(2,1)S(1)} %get-tuple-element.99), channel_id=1, source_target_pairs={{0,24},{8,16},{16,8},{24,0},{1,25},{9,17},{17,9},{25,1},{2,26},{10... | collective-permute-start | bytes 393224 | tf_op jit(solution)/shard_map/ppermute | solution.py:235
  26.9 7.8 %collective-permute-start.10 = (bf16[32,2048]{1,0:T(8,128)(2,1)S(1)}, bf16[32,2048]{1,0:T(8,128)(2,1)S(1)}, u32[]{:S(2)}, u32[]{:S(2)}) collective-permute-start(bf16[32,2048]{1,0:T(8,128)(2,1)S(1)} %get-tuple-element.104), channel_id=1, source_target_pairs={{0,2},{1,3},{2,0},{3,1},{4,6},{5,7},{6,4},{7,5},{8,10},{9,11},{10,... | collective-permute-start | bytes 393224 | tf_op jit(solution)/shard_map/ppermute | solution.py:235
  27.8 8.7 %collective-permute-start.13 = (bf16[32,2048]{1,0:T(8,128)(2,1)S(1)}, bf16[32,2048]{1,0:T(8,128)(2,1)S(1)}, u32[]{:S(2)}, u32[]{:S(2)}) collective-permute-start(bf16[32,2048]{1,0:T(8,128)(2,1)S(1)} %second_added.1), channel_id=1, source_target_pairs={{0,4},{1,5},{2,6},{3,7},{4,0},{5,1},{6,2},{7,3},{8,12},{9,13},{10,... | collective-permute-start | bytes 393224 | tf_op jit(solution)/shard_map/ppermute | solution.py:235
  29.4 7.1 %collective-permute-start.14 = (bf16[8,16,512]{2,1,0:T(8,128)(2,1)S(1)}, bf16[8,16,512]{2,1,0:T(8,128)(2,1)S(1)}, u32[]{:S(2)}, u32[]{:S(2)}) collective-permute-start(bf16[8,16,512]{2,1,0:T(8,128)(2,1)S(1)} %get-tuple-element.113), channel_id=1, source_target_pairs={{0,16},{8,24},{16,0},{24,8},{1,17},{9,25},{17,1},{25,9},{2,18},{10... | collective-permute-start | bytes 393224 | tf_op jit(solution)/shard_map/ppermute | solution.py:235
  30.9 5.6 %collective-permute-start.15 = (bf16[8,16,512]{2,1,0:T(8,128)(2,1)S(1)}, bf16[8,16,512]{2,1,0:T(8,128)(2,1)S(1)}, u32[]{:S(2)}, u32[]{:S(2)}) collective-permute-start(bf16[8,16,512]{2,1,0:T(8,128)(2,1)S(1)} %get-tuple-element.114), channel_id=1, source_target_pairs={{0,8},{8,0},{16,24},{24,16},{1,9},{9,1},{17,25},{25,17},{2,10},{10... | collective-permute-start | bytes 393224 | tf_op jit(solution)/shard_map/ppermute | solution.py:235

commit v24 on v22

--- a/solution.py
+++ b/solution.py
@@ -544,7 +544,7 @@
     joined_ref[early:middle, :] = joined_ref[first : first + block_rows, :]
     joined_ref[middle : middle + block_rows, :] = middle_joined_ref[2 * block_rows :, :]
     rows = CORES * block_rows
-    hide(feedforward_scr, upward_ref, hidden_scr, 0)
+    hide(feedforward_scr, upward_ref, hidden_scr, 0, 512)
     attended = attend(joined_ref, offsets_ref, early - block_rows, rows, block_rows)
     chunk = 512
     for begin in range(0, downward_ref.shape[1], chunk):

time: 37.5 us -> 37.5 us (level)
  no operation moved by 1% of the time
where the time goes in v24:
time: 37.5 us; the launch traced here: 37.3 us
  starting transfers between devices  18.4 us (49%)
  Pallas kernels  13.2 us (35%)
  waiting for transfers between devices  4.94 us (13%)
  between operations  0.72 us (2%)
    ppermute x16, starting transfers between devices, exchanged(): lax.ppermute(block, axis, [(member, member ^ mask) for member in range(co...  18.4 us
    pallas_call x1, Pallas kernels, own_rows(): pl.pallas_call(functools.partial(own_kernel, count, replica_count), out_s...  5.27 us
    ppermute x16, waiting for transfers between devices, exchanged(): lax.ppermute(block, axis, [(member, member ^ mask) for member in range(co...  4.94 us
    pallas_call x1, Pallas kernels, last_rows(): pl.pallas_call(last_kernel, out_shape=[pltpu.VMEM((tokens, 3 * HD), jnp.b...  2.25 us
    pallas_call x1, Pallas kernels, middle_rows(): pl.pallas_call(functools.partial(middle_kernel, origins), out_shape=[pltp...  2.06 us
    pallas_call x1, Pallas kernels, fed_rows(): pl.pallas_call(fed_kernel, out_shape=[pltpu.VMEM((rows, width), jnp.float...  0.83 us
    pallas_call x1, Pallas kernels, rest_rows(): pl.pallas_call(rest_kernel, out_shape=shapes, in_specs=vmem_specs(5), out...  0.83 us
    pallas_call x1, Pallas kernels, finished(): pl.pallas_call(functools.partial(finish_kernel, masks), out_shape=[jax.Sh...  0.83 us
  transfers between devices with their start and end apart: 16, of which 5 were waited for; matrix products, arithmetic and copies ran while one was open for 0% of the time, Pallas kernels for 27%

profile of v24, /device:TPU:0, one launch (start us, length us, event | category | flops | bytes accessed | tf_op | source)
XLA Modules:
  0.0 37.3 jit_solution(11481698734024223481)
XLA Ops:
  0.6 5.1 %collective-permute-start = (bf16[32,2048]{1,0:T(8,128)(2,1)}, bf16[32,2048]{1,0:T(8,128)(2,1)S(1)}, u32[]{:S(2)}, u32[]{:S(2)}) collective-permute-start(bf16[32,2048]{1,0:T(8,128)(2,1)} %refs_2_.1), channel_id=1, source_target_pairs={{0,6},{1,7},{2,4},{3,5},{4,2},{5,3},{6,0},{7,1},{8,14},{9,15},{10,... | collective-permute-start | bytes 393224 | tf_op jit(solution)/shard_map/ppermute | solution.py:235
  5.8 5.3 %own_rows.1 = (s32[1,256]{1,0:T(1,128)}, s32[1,16]{1,0:T(1,128)}, bf16[32,2048]{1,0:T(8,128)(2,1)S(1)}, f32[1,2048]{1,0:T(1,128)S(1)}, f32[1,2048]{1,0:T(1,128)S...) custom-call(s32[1,256]{1,0:T(1,128)} %refs_0_.1, ...), custom_call_target="tpu_custom_call" | custom-call | flops 234881024 | bytes 11682880 | tf_op jit(solution)/shard_map/own_rows/pallas_call | solution.py:456
  11.0 2.1 %collective-permute-start.1 = (bf16[32,2048]{1,0:T(8,128)(2,1)S(1)}, bf16[32,2048]{1,0:T(8,128)(2,1)S(1)}, u32[]{:S(2)}, u32[]{:S(2)}) collective-permute-start(bf16[32,2048]{1,0:T(8,128)(2,1)S(1)} %collective-permute-done.refs_1_), channel_id=1, source_target_pairs={{0,2},{1,3},{2,0},{3,1},{4,6},{5,7},{6,4},{7,5},{8,10},{9,11},{10,... | collective-permute-start | bytes 393224 | tf_op jit(solution)/shard_map/ppermute | solution.py:235
  13.1 0.0 collective-permute-done.3.refs_0_
  13.1 0.0 collective-permute-done.2.refs_2_
  13.1 2.1 %middle_rows.1 = (bf16[96,768]{1,0:T(8,128)(2,1)S(1)}, bf16[96,1024]{1,0:T(8,128)(2,1)S(1)}, bf16[256,2048]{1,0:T(8,128)(2,1)S(1)}) custom-call(bf16[32,2048]{1,0:T(8,128)(2,1)S(1)} %collective-permute-done.3.refs_0_, bf16[32,2048]{1,0:T(8,128)(2,1)S(1)} %collective-permute-done.refs_1_, bf16[32,2048]{1,0:T(8,128)(2,1)S(1)} %collective-permute-done.2.refs_2_, ...), custom_call_target="tpu_custom_call" | custom-call | flops 704643072 | bytes 1048576 | tf_op jit(solution)/shard_map/middle_rows/pallas_call | solution.py:498
  15.2 0.1 collective-permute-start.4
  15.3 0.5 %collective-permute-start.5 = (bf16[32,2048]{1,0:T(8,128)(2,1)S(1)}, bf16[32,2048]{1,0:T(8,128)(2,1)S(1)}, u32[]{:S(2)}, u32[]{:S(2)}) collective-permute-start(bf16[32,2048]{1,0:T(8,128)(2,1)S(1)} %collective-permute-done.refs_1_), channel_id=1, source_target_pairs={{0,1},{1,0},{2,3},{3,2},{4,5},{5,4},{6,7},{7,6},{8,9},{9,8},{10,11... | collective-permute-start | bytes 393224 | tf_op jit(solution)/shard_map/ppermute | solution.py:235
  15.8 1.2 %collective-permute-done.1.refs_2_ = bf16[32,2048]{1,0:T(8,128)(2,1)S(1)} collective-permute-done((bf16[32,2048]{1,0:T(8,128)(2,1)S(1)}, bf16[32,2048]{1,0:T(8,128)(2,1)S(1)}, u32[]{:S(2)}, u32[]{:S(2)}) %collective-permute-start.1) | collective-permute-done | bytes 131104 | tf_op jit(solution)/shard_map/ppermute | solution.py:235
  17.0 0.0 collective-permute-done.4.refs_1_
  17.0 0.1 collective-permute-start.6
  17.1 0.8 %fed_rows.1 = (f32[128,2048]{1,0:T(8,128)S(1)}, bf16[96,2048]{1,0:T(8,128)(2,1)S(1)}, bf16[96,2048]{1,0:T(8,128)(2,1)S(1)}) custom-call(bf16[32,1024]{1,0:T(8,128)(2,1)S(1)} %get-tuple-element.74.own_hidden_ref, bf16[96,1024]{1,0:T(8,128)(2,1)S(1)} %get-tuple-element.75.middle_hidden_ref, bf16[1024,2048]{1,0:T(8,128)(2,1)S(1)} %get-tuple-element.76.downward_ref.refs_7_, ...), custom_call_target="tpu_custom_call" | custom-call | flops 536870912 | bytes 1048576 | tf_op jit(solution)/shard_map/fed_rows/pallas_call | solution.py:606
  18.0 0.4 %collective-permute-done.6.refs_0_ = bf16[32,2048]{1,0:T(8,128)(2,1)S(1)} collective-permute-done((bf16[32,2048]{1,0:T(8,128)(2,1)S(1)}, bf16[32,2048]{1,0:T(8,128)(2,1)S(1)}, u32[]{:S(2)}, u32[]{:S(2)}) %collective-permute-start.6) | collective-permute-done | bytes 131104 | tf_op jit(solution)/shard_map/ppermute | solution.py:235
  18.4 2.3 %last_rows.1 = (bf16[256,768]{1,0:T(8,128)(2,1)S(1)}, f32[96,2048]{1,0:T(8,128)S(1)}, bf16[32,2048]{1,0:T(8,128)(2,1)S(1)}, f32[32,2048]{1,0:T(8,128)S(1)}) custom-call(bf16[32,2048]{1,0:T(8,128)(2,1)S(1)} %collective-permute-done.6.refs_0_, bf16[96,2048]{1,0:T(8,128)(2,1)S(1)} %get-tuple-element.79.refs_1_, bf16[96,2048]{1,0:T(8,128)(2,1)S(1)} %get-tuple-element.80.refs_2_, ...), custom_call_target="tpu_custom_call" | custom-call | flops 1610612736 | bytes 1048576 | tf_op jit(solution)/shard_map/last_rows/pallas_call | solution.py:565
  20.6 0.2 collective-permute-start.7
  20.8 0.8 %rest_rows.1 = (bf16[2,32,2048]{2,1,0:T(8,128)(2,1)S(1)}, bf16[32,2048]{1,0:T(8,128)(2,1)S(1)}, f32[32,2048]{1,0:T(8,128)S(1)}, f32[32,2048]{1,0:T(8,128)S(1)}, f32[32,2048]{1,0:T(8,128)S(1)}) custom-call(bf16[256,768]{1,0:T(8,128)(2,1)S(1)} %get-tuple-element.92.joined_ref, f32[256,128]{1,0:T(8,128)S(1)} %get-tuple-element.82.refs_9_.offsets_ref, ...), custom_call_target="tpu_custom_call" | custom-call | flops 201326592 | bytes 1048576 | tf_op jit(solution)/shard_map/rest_rows/pallas_call | solution.py:658
  21.7 0.4 %collective-permute-start.9 = (bf16[2,32,2048]{2,1,0:T(8,128)(2,1)S(1)}, bf16[2,32,2048]{2,1,0:T(8,128)(2,1)S(1)}, u32[]{:S(2)}, u32[]{:S(2)}) collective-permute-start(bf16[2,32,2048]{2,1,0:T(8,128)(2,1)S(1)} %get-tuple-element.100), channel_id=1, source_target_pairs={{0,1},{1,0},{2,3},{3,2},{4,5},{5,4},{6,7},{7,6},{8,9},{9,8},{10,11... | collective-permute-start | bytes 786440 | tf_op jit(solution)/shard_map/ppermute | solution.py:235
  22.1 1.8 %collective-permute-start.11 = (bf16[32,2048]{1,0:T(8,128)(2,1)S(1)}, bf16[32,2048]{1,0:T(8,128)(2,1)S(1)}, u32[]{:S(2)}, u32[]{:S(2)}) collective-permute-start(bf16[32,2048]{1,0:T(8,128)(2,1)S(1)} %third_added.1), channel_id=1, source_target_pairs={{0,2},{1,3},{2,0},{3,1},{4,6},{5,7},{6,4},{7,5},{8,10},{9,11},{10,... | collective-permute-start | bytes 393224 | tf_op jit(solution)/shard_map/ppermute | solution.py:235
  24.0 0.3 cached_pages.1
  24.3 0.1 collective-permute-start.12
  24.3 2.5 %collective-permute-start.8 = (bf16[8,16,512]{2,1,0:T(8,128)(2,1)S(1)}, bf16[8,16,512]{2,1,0:T(8,128)(2,1)S(1)}, u32[]{:S(2)}, u32[]{:S(2)}) collective-permute-start(bf16[8,16,512]{2,1,0:T(8,128)(2,1)S(1)} %get-tuple-element.99), channel_id=1, source_target_pairs={{0,24},{8,16},{16,8},{24,0},{1,25},{9,17},{17,9},{25,1},{2,26},{10... | collective-permute-start | bytes 393224 | tf_op jit(solution)/shard_map/ppermute | solution.py:235
  26.9 0.0 collective-permute-done.9.received_ref
  26.9 0.1 near_sums.1
  26.9 0.3 collective-permute-start.10
  27.3 0.5 %collective-permute-done.11.refs_1_ = bf16[32,2048]{1,0:T(8,128)(2,1)S(1)} collective-permute-done((bf16[32,2048]{1,0:T(8,128)(2,1)S(1)}, bf16[32,2048]{1,0:T(8,128)(2,1)S(1)}, u32[]{:S(2)}, u32[]{:S(2)}) %collective-permute-start.11) | collective-permute-done | bytes 131104 | tf_op jit(solution)/shard_map/ppermute | solution.py:235
  27.8 1.6 %collective-permute-start.13 = (bf16[32,2048]{1,0:T(8,128)(2,1)S(1)}, bf16[32,2048]{1,0:T(8,128)(2,1)S(1)}, u32[]{:S(2)}, u32[]{:S(2)}) collective-permute-start(bf16[32,2048]{1,0:T(8,128)(2,1)S(1)} %second_added.1), channel_id=1, source_target_pairs={{0,4},{1,5},{2,6},{3,7},{4,0},{5,1},{6,2},{7,3},{8,12},{9,13},{10,... | collective-permute-start | bytes 393224 | tf_op jit(solution)/shard_map/ppermute | solution.py:235
  29.4 1.5 %collective-permute-start.14 = (bf16[8,16,512]{2,1,0:T(8,128)(2,1)S(1)}, bf16[8,16,512]{2,1,0:T(8,128)(2,1)S(1)}, u32[]{:S(2)}, u32[]{:S(2)}) collective-permute-start(bf16[8,16,512]{2,1,0:T(8,128)(2,1)S(1)} %get-tuple-element.113), channel_id=1, source_target_pairs={{0,16},{8,24},{16,0},{24,8},{1,17},{9,25},{17,1},{25,9},{2,18},{10... | collective-permute-start | bytes 393224 | tf_op jit(solution)/shard_map/ppermute | solution.py:235
  30.9 2.0 %collective-permute-start.15 = (bf16[8,16,512]{2,1,0:T(8,128)(2,1)S(1)}, bf16[8,16,512]{2,1,0:T(8,128)(2,1)S(1)}, u32[]{:S(2)}, u32[]{:S(2)}) collective-permute-start(bf16[8,16,512]{2,1,0:T(8,128)(2,1)S(1)} %get-tuple-element.114), channel_id=1, source_target_pairs={{0,8},{8,0},{16,24},{24,16},{1,9},{9,1},{17,25},{25,17},{2,10},{10... | collective-permute-start | bytes 393224 | tf_op jit(solution)/shard_map/ppermute | solution.py:235
  33.0 1.8 %collective-permute-done.10.refs_2_ = bf16[32,2048]{1,0:T(8,128)(2,1)S(1)} collective-permute-done((bf16[32,2048]{1,0:T(8,128)(2,1)S(1)}, bf16[32,2048]{1,0:T(8,128)(2,1)S(1)}, u32[]{:S(2)}, u32[]{:S(2)}) %collective-permute-start.10) | collective-permute-done | bytes 131104 | tf_op jit(solution)/shard_map/ppermute | solution.py:235
  34.7 0.7 %placed.1 = (bf16[1,4,8,16,512]{4,3,2,1,0:T(8,128)(2,1)}, f32[32,2048]{1,0:T(8,128)S(1)}) custom-call(bf16[8,16,512]{2,1,0:T(8,128)(2,1)S(1)} %get-tuple-element.98.refs_0_, bf16[8,16,512]{2,1,0:T(8,128)(2,1)S(1)} %collective-permute-done.8.refs_1_, bf16[32,2048]{1,0:T(8,128)(2,1)S(1)} %collective-permute-done.10.refs_2_, ...), custom_call_target="tpu_custom_call" | custom-call | tf_op jit(solution)/shard_map/placed/pallas_call | solution.py:753
  35.4 1.0 %collective-permute-done.13.refs_0_ = bf16[32,2048]{1,0:T(8,128)(2,1)S(1)} collective-permute-done((bf16[32,2048]{1,0:T(8,128)(2,1)S(1)}, bf16[32,2048]{1,0:T(8,128)(2,1)S(1)}, u32[]{:S(2)}, u32[]{:S(2)}) %collective-permute-start.13) | collective-permute-done | bytes 131104 | tf_op jit(solution)/shard_map/ppermute | solution.py:235
  36.5 0.8 %finished.1 = (f32[32,2048]{1,0:T(8,128)}, bf16[1,4,8,16,512]{4,3,2,1,0:T(8,128)(2,1)}) custom-call(f32[32,2048]{1,0:T(8,128)S(1)} %get-tuple-element.106.base_ref, bf16[32,2048]{1,0:T(8,128)(2,1)S(1)} %collective-permute-done.13.refs_0_, bf16[8,16,512]{2,1,0:T(8,128)(2,1)S(1)} %collective-permute-done.14.refs_1_, ...), custom_call_target="tpu_custom_call", output_to_operand_aliasing={{1}: (4, {})} | custom-call | tf_op jit(solution)/shard_map/finished/pallas_call | solution.py:790
  (11 shorter events, 0.1 us)
Async XLA Ops:
  0.6 10.4 %collective-permute-start = (bf16[32,2048]{1,0:T(8,128)(2,1)}, bf16[32,2048]{1,0:T(8,128)(2,1)S(1)}, u32[]{:S(2)}, u32[]{:S(2)}) collective-permute-start(bf16[32,2048]{1,0:T(8,128)(2,1)} %refs_2_.1), channel_id=1, source_target_pairs={{0,6},{1,7},{2,4},{3,5},{4,2},{5,3},{6,0},{7,1},{8,14},{9,15},{10,... | collective-permute-start | bytes 393224 | tf_op jit(solution)/shard_map/ppermute | solution.py:235
  5.7 7.4 %collective-permute-start.3 = (bf16[32,2048]{1,0:T(8,128)(2,1)}, bf16[32,2048]{1,0:T(8,128)(2,1)S(1)}, u32[]{:S(2)}, u32[]{:S(2)}) collective-permute-start(bf16[32,2048]{1,0:T(8,128)(2,1)} %refs_2_.1), channel_id=1, source_target_pairs={{0,1},{1,0},{2,3},{3,2},{4,5},{5,4},{6,7},{7,6},{8,9},{9,8},{10,11... | collective-permute-start | bytes 393224 | tf_op jit(solution)/shard_map/ppermute | solution.py:235
  5.8 7.4 %collective-permute-start.2 = (bf16[32,2048]{1,0:T(8,128)(2,1)}, bf16[32,2048]{1,0:T(8,128)(2,1)S(1)}, u32[]{:S(2)}, u32[]{:S(2)}) collective-permute-start(bf16[32,2048]{1,0:T(8,128)(2,1)} %refs_2_.1), channel_id=1, source_target_pairs={{0,2},{1,3},{2,0},{3,1},{4,6},{5,7},{6,4},{7,5},{8,10},{9,11},{10,... | collective-permute-start | bytes 393224 | tf_op jit(solution)/shard_map/ppermute | solution.py:235
  11.0 6.0 %collective-permute-start.1 = (bf16[32,2048]{1,0:T(8,128)(2,1)S(1)}, bf16[32,2048]{1,0:T(8,128)(2,1)S(1)}, u32[]{:S(2)}, u32[]{:S(2)}) collective-permute-start(bf16[32,2048]{1,0:T(8,128)(2,1)S(1)} %collective-permute-done.refs_1_), channel_id=1, source_target_pairs={{0,2},{1,3},{2,0},{3,1},{4,6},{5,7},{6,4},{7,5},{8,10},{9,11},{10,... | collective-permute-start | bytes 393224 | tf_op jit(solution)/shard_map/ppermute | solution.py:235
  15.2 1.8 %collective-permute-start.4 = (bf16[32,2048]{1,0:T(8,128)(2,1)S(1)}, bf16[32,2048]{1,0:T(8,128)(2,1)S(1)}, u32[]{:S(2)}, u32[]{:S(2)}) collective-permute-start(bf16[32,2048]{1,0:T(8,128)(2,1)S(1)} %collective-permute-done.2.refs_2_), channel_id=1, source_target_pairs={{0,1},{1,0},{2,3},{3,2},{4,5},{5,4},{6,7},{7,6},{8,9},{9,8},{10,11... | collective-permute-start | bytes 393224 | tf_op jit(solution)/shard_map/ppermute | solution.py:235
  15.3 1.7 %collective-permute-start.5 = (bf16[32,2048]{1,0:T(8,128)(2,1)S(1)}, bf16[32,2048]{1,0:T(8,128)(2,1)S(1)}, u32[]{:S(2)}, u32[]{:S(2)}) collective-permute-start(bf16[32,2048]{1,0:T(8,128)(2,1)S(1)} %collective-permute-done.refs_1_), channel_id=1, source_target_pairs={{0,1},{1,0},{2,3},{3,2},{4,5},{5,4},{6,7},{7,6},{8,9},{9,8},{10,11... | collective-permute-start | bytes 393224 | tf_op jit(solution)/shard_map/ppermute | solution.py:235
  17.0 1.4 %collective-permute-start.6 = (bf16[32,2048]{1,0:T(8,128)(2,1)S(1)}, bf16[32,2048]{1,0:T(8,128)(2,1)S(1)}, u32[]{:S(2)}, u32[]{:S(2)}) collective-permute-start(bf16[32,2048]{1,0:T(8,128)(2,1)S(1)} %collective-permute-done.1.refs_2_), channel_id=1, source_target_pairs={{0,1},{1,0},{2,3},{3,2},{4,5},{5,4},{6,7},{7,6},{8,9},{9,8},{10,11... | collective-permute-start | bytes 393224 | tf_op jit(solution)/shard_map/ppermute | solution.py:235
  20.6 1.5 %collective-permute-start.7 = (bf16[32,2048]{1,0:T(8,128)(2,1)S(1)}, bf16[32,2048]{1,0:T(8,128)(2,1)S(1)}, u32[]{:S(2)}, u32[]{:S(2)}) collective-permute-start(bf16[32,2048]{1,0:T(8,128)(2,1)S(1)} %get-tuple-element.87), channel_id=1, source_target_pairs={{0,1},{1,0},{2,3},{3,2},{4,5},{5,4},{6,7},{7,6},{8,9},{9,8},{10,11... | collective-permute-start | bytes 393224 | tf_op jit(solution)/shard_map/ppermute | solution.py:235
  21.7 5.2 %collective-permute-start.9 = (bf16[2,32,2048]{2,1,0:T(8,128)(2,1)S(1)}, bf16[2,32,2048]{2,1,0:T(8,128)(2,1)S(1)}, u32[]{:S(2)}, u32[]{:S(2)}) collective-permute-start(bf16[2,32,2048]{2,1,0:T(8,128)(2,1)S(1)} %get-tuple-element.100), channel_id=1, source_target_pairs={{0,1},{1,0},{2,3},{3,2},{4,5},{5,4},{6,7},{7,6},{8,9},{9,8},{10,11... | collective-permute-start | bytes 786440 | tf_op jit(solution)/shard_map/ppermute | solution.py:235
  22.1 5.6 %collective-permute-start.11 = (bf16[32,2048]{1,0:T(8,128)(2,1)S(1)}, bf16[32,2048]{1,0:T(8,128)(2,1)S(1)}, u32[]{:S(2)}, u32[]{:S(2)}) collective-permute-start(bf16[32,2048]{1,0:T(8,128)(2,1)S(1)} %third_added.1), channel_id=1, source_target_pairs={{0,2},{1,3},{2,0},{3,1},{4,6},{5,7},{6,4},{7,5},{8,10},{9,11},{10,... | collective-permute-start | bytes 393224 | tf_op jit(solution)/shard_map/ppermute | solution.py:235
  24.3 3.5 %collective-permute-start.12 = (bf16[32,2048]{1,0:T(8,128)(2,1)S(1)}, bf16[32,2048]{1,0:T(8,128)(2,1)S(1)}, u32[]{:S(2)}, u32[]{:S(2)}) collective-permute-start(bf16[32,2048]{1,0:T(8,128)(2,1)S(1)} %get-tuple-element.109), channel_id=1, source_target_pairs={{0,1},{1,0},{2,3},{3,2},{4,5},{5,4},{6,7},{7,6},{8,9},{9,8},{10,11... | collective-permute-start | bytes 393224 | tf_op jit(solution)/shard_map/ppermute | solution.py:235
  24.3 8.6 %collective-permute-start.8 = (bf16[8,16,512]{2,1,0:T(8,128)(2,1)S(1)}, bf16[8,16,512]{2,1,0:T(8,128)(2,1)S(1)}, u32[]{:S(2)}, u32[]{:S(2)}) collective-permute-start(bf16[8,16,512]{2,1,0:T(8,128)(2,1)S(1)} %get-tuple-element.99), channel_id=1, source_target_pairs={{0,24},{8,16},{16,8},{24,0},{1,25},{9,17},{17,9},{25,1},{2,26},{10... | collective-permute-start | bytes 393224 | tf_op jit(solution)/shard_map/ppermute | solution.py:235
  26.9 7.8 %collective-permute-start.10 = (bf16[32,2048]{1,0:T(8,128)(2,1)S(1)}, bf16[32,2048]{1,0:T(8,128)(2,1)S(1)}, u32[]{:S(2)}, u32[]{:S(2)}) collective-permute-start(bf16[32,2048]{1,0:T(8,128)(2,1)S(1)} %get-tuple-element.104), channel_id=1, source_target_pairs={{0,2},{1,3},{2,0},{3,1},{4,6},{5,7},{6,4},{7,5},{8,10},{9,11},{10,... | collective-permute-start | bytes 393224 | tf_op jit(solution)/shard_map/ppermute | solution.py:235
  27.8 8.7 %collective-permute-start.13 = (bf16[32,2048]{1,0:T(8,128)(2,1)S(1)}, bf16[32,2048]{1,0:T(8,128)(2,1)S(1)}, u32[]{:S(2)}, u32[]{:S(2)}) collective-permute-start(bf16[32,2048]{1,0:T(8,128)(2,1)S(1)} %second_added.1), channel_id=1, source_target_pairs={{0,4},{1,5},{2,6},{3,7},{4,0},{5,1},{6,2},{7,3},{8,12},{9,13},{10,... | collective-permute-start | bytes 393224 | tf_op jit(solution)/shard_map/ppermute | solution.py:235
  29.4 7.1 %collective-permute-start.14 = (bf16[8,16,512]{2,1,0:T(8,128)(2,1)S(1)}, bf16[8,16,512]{2,1,0:T(8,128)(2,1)S(1)}, u32[]{:S(2)}, u32[]{:S(2)}) collective-permute-start(bf16[8,16,512]{2,1,0:T(8,128)(2,1)S(1)} %get-tuple-element.113), channel_id=1, source_target_pairs={{0,16},{8,24},{16,0},{24,8},{1,17},{9,25},{17,1},{25,9},{2,18},{10... | collective-permute-start | bytes 393224 | tf_op jit(solution)/shard_map/ppermute | solution.py:235
  30.9 5.6 %collective-permute-start.15 = (bf16[8,16,512]{2,1,0:T(8,128)(2,1)S(1)}, bf16[8,16,512]{2,1,0:T(8,128)(2,1)S(1)}, u32[]{:S(2)}, u32[]{:S(2)}) collective-permute-start(bf16[8,16,512]{2,1,0:T(8,128)(2,1)S(1)} %get-tuple-element.114), channel_id=1, source_target_pairs={{0,8},{8,0},{16,24},{24,16},{1,9},{9,1},{17,25},{25,17},{2,10},{10... | collective-permute-start | bytes 393224 | tf_op jit(solution)/shard_map/ppermute | solution.py:235
